TPU v7x, 32 devices: a whole 2x2x4 slice. The times are simulated.
32 devices in a mesh: req: 16 (over z, y, x), tp: 2 (over core).
Axes of the slice: x: 2, y: 2, z: 4, core: 2. Of those that a mesh axis runs over, the one named last changes fastest.
Arguments:
- patches: bfloat16 [7168, 1664], P('req', 'tp'), may hold values from -48 to 48
- ln_gain: bfloat16 [1664], P('tp'), may hold values from 0.099609375 to 1.8984375
- ln_bias: bfloat16 [1664], P('tp'), may hold values from -3 to 3
- merge_weight: bfloat16 [4, 1664, 1664], P(None, 'tp'), may hold values from -0.078125 to 0.078125
- text_rows: bfloat16 [8192, 1664], P('req', 'tp'), may hold values from -48 to 48
- norm_gain: bfloat16 [1664], replicated, may hold values from 0.099609375 to 1.8984375
- qkv_weight: bfloat16 [1664, 4992], P('req', 'tp'), may hold values from -0.15625 to 0.15625
- token_pos: int32 [1792], P('req'), may hold values from 0 to 8191, as said below
- text_len: int32 [2], replicated, may hold values from 1 to 4096, as said below
Outputs:
- qkv_rows: bfloat16 [8192, 4992], P('req', 'tp')
Inputs may be any that keep to these rules, and one draw needn't show every extreme that they name: `token_pos`: all distinct. A device's merged tokens form 8 images of consecutive rows, each a multiple of 2 and at most 16 tokens, each written to consecutive positions that one device holds; a device's images go to 8 different devices and every device receives exactly 8 images. In every draw some image has 16 tokens. `text_len`: every image position of a request lies below its length.
All inputs are finite; a program needn't handle non-finite values.
Results may differ from a plain program's by a relative error of at most 0.0063.
Values may be sent and summed in bfloat16 or wider, within the bound.
No kernel may reach another device: no remote copies, remote signals or barrier semaphores. Data moves between devices by JAX's collectives and lax.ppermute only.
A program may use at most 128 MiB of HBM per device.

v0:
```python
import jax
import jax.numpy as jnp
from jax import lax
from jax.sharding import PartitionSpec as P

DV = 1664
SEQ = 4096


EPSILON = 1e-06


def shards(
    patches, ln_gain, ln_bias, merge_weight, text_rows, norm_gain, qkv_weight, token_pos, text_len
):
    values = patches.astype(jnp.float32)
    sum_part = jnp.sum(values, axis=1)
    square_part = jnp.sum(values * values, axis=1)
    sum_total, square_total = lax.psum((sum_part, square_part), "tp")
    row_mean = (sum_total / DV)[:, None]
    second = (square_total / DV)[:, None]
    normed = (
        (values - row_mean)
        * lax.rsqrt(second - row_mean * row_mean + EPSILON)
        * ln_gain.astype(jnp.float32)
        + ln_bias.astype(jnp.float32)
    ).astype(jnp.bfloat16)
    width_part = patches.shape[1]
    grouped = normed.reshape(patches.shape[0] // 4, 4, width_part)
    partial_value = jnp.einsum(
        "mkf,kfd->md", grouped, merge_weight, preferred_element_type=jnp.float32
    )
    merged = lax.psum_scatter(partial_value, "tp", scatter_dimension=1, tiled=True).astype(
        jnp.bfloat16
    )
    row_count = text_rows.shape[0]
    base_row = lax.axis_index("req") * row_count
    piece_rows = lax.all_gather(merged, "req", axis=0, tiled=True)
    piece_pos = lax.all_gather(token_pos, "req", axis=0, tiled=True)
    local_pos = piece_pos - base_row
    inside = (local_pos >= 0) & (local_pos < row_count)
    combined = text_rows.at[jnp.where(inside, local_pos, row_count)].set(piece_rows, mode="drop")
    full_rows = lax.all_gather(combined, "tp", axis=1, tiled=True).astype(jnp.float32)
    scaled = (
        full_rows
        * lax.rsqrt(jnp.mean(full_rows * full_rows, axis=1, keepdims=True) + EPSILON)
        * norm_gain.astype(jnp.float32)
    ).astype(jnp.bfloat16)
    whole_weight = lax.all_gather(qkv_weight, "req", axis=0, tiled=True)
    projected = jnp.dot(scaled, whole_weight, preferred_element_type=jnp.float32)
    position = base_row + jnp.arange(row_count, dtype=jnp.int32)
    request = position // SEQ
    request_ids = jnp.arange(text_len.shape[0], dtype=jnp.int32)
    limits = jnp.sum(
        jnp.where(request[:, None] == request_ids[None, :], text_len[None, :], 0), axis=1
    )
    keep_row = position % SEQ < limits
    return jnp.where(keep_row[:, None], projected, 0.0).astype(jnp.bfloat16)


def solution(mesh):
    placed = (
        P("req", "tp"),
        P("tp"),
        P("tp"),
        P(None, "tp", None),
        P("req", "tp"),
        P(),
        P("req", "tp"),
        P("req"),
        P(),
    )
    return jax.shard_map(
        shards, mesh=mesh, in_specs=placed, out_specs=P("req", "tp"), check_vma=False
    )
```

profile of v0, /device:TPU:0, one launch (start us, length us, event | category | flops | bytes accessed | tf_op | source)
XLA Modules:
  0.0 262.9 jit_solution(15138895932402181689)
XLA Ops:
  6.5 0.0 reduce-scatter.4.cloned.1.call-start
  6.5 1.5 convert_reduce_fusion
  8.0 0.7 convert_element_type.28
  8.7 0.7 convert_element_type.29
  9.4 2.6 all-reduce.1
  12.0 1.5 fusion.9
  13.5 0.2 reshape.56
  13.7 0.0 copy-start
  13.7 8.4 %convolution_bitcast_fusion = f32[1664,112]{1,0:T(8,128)} fusion(bf16[4,832,1664]{2,1,0:T(8,128)(2,1)} %param.12, bf16[112,4,832]{2,1,0:T(4,128)(2,1)S(1)} %reshape.56), kind=kOutput, calls=%fused_computation.7 | convolution fusion | flops 1240465408 | bytes 12566528 | tf_op jit(solution)/shard_map/mkf,kfd->md/dot_general | solution.py:30
  22.1 0.0 copy-start.4
  22.1 0.0 copy-start.3
  22.1 0.0 reduce-scatter.4.cloned.1.call-update
  22.2 0.0 all-gather.4.cloned.1.call-start
  22.2 11.0 %reduce-scatter.4.cloned.1.call-done = f32[832,112]{1,0:T(8,128)} async-done(((f32[1664,112]{1,0:T(8,128)}), f32[832,112]{1,0:T(8,128)}) %reduce-scatter.4.cloned.1.call-update) | async-done | bytes 372752
  33.2 1.8 copy.20
  35.0 0.0 all-gather.4.cloned.1.call-update
  35.1 0.0 all-gather.6.cloned.1.call-start
  35.1 0.0 copy-done
  35.1 0.6 copy.17
  35.7 0.0 copy-done.4
  35.8 0.6 dynamic-slice
  36.9 0.0 copy-done.3
  36.9 0.3 dynamic-update-slice
  37.2 14.9 %all-reduce = s32[1792]{0:T(1024)S(1)} all-reduce(s32[1792]{0:T(1024)S(1)} %dynamic-update-slice), channel_id=1, replica_groups=mesh['req'=16,'tp'=2] {'req'}, use_global_device_ids=true, to_apply=%add | all-reduce | flops 1792 | bytes 14336
  52.1 0.0 copy-start.1
  52.1 0.0 copy-start.2
  52.1 54.0 %all-gather.4.cloned.1.call-done = bf16[1792,832]{1,0:T(8,128)(2,1)} async-done(((bf16[112,832]{1,0:T(8,128)(2,1)}), bf16[1792,832]{1,0:T(8,128)(2,1)}) %all-gather.4.cloned.1.call-update) | async-done | bytes 2981904 | tf_op jit(solution)/shard_map/all_gather | solution.py:38
  106.1 11.9 %scatter_fusion = bf16[512,832]{1,0:T(8,128)(2,1)S(1)} fusion(bf16[512,832]{1,0:T(8,128)(2,1)S(1)} %copy.17, s32[1792]{0:T(1024)S(1)} %compare_select_fusion, bf16[1792,832]{1,0:T(8,128)(2,1)} %all-gather.4.cloned.1.call-done), kind=kCustom, calls=%fused_computation | custom fusion | bytes 8952832 | tf_op jit(solution)/shard_map/scatter | solution.py:42
  118.0 1.2 copy.18
  119.2 0.0 all-gather.6.cloned.1.call-update
  119.3 0.2 all-gather.8.cloned.1.call-start
  119.5 0.3 all-gather.8.cloned.1.call-update
  119.8 0.0 copy-done.1
  119.9 0.0 copy-done.2
  119.9 0.1 fusion.12
  120.0 7.9 %all-gather.6.cloned.1.call-done = bf16[512,1664]{0,1:T(8,128)(2,1)} async-done(((bf16[512,832]{0,1:T(8,128)(2,1)}), bf16[512,1664]{0,1:T(8,128)(2,1)}) %all-gather.6.cloned.1.call-update) | async-done | bytes 1703952 | tf_op jit(solution)/shard_map/all_gather | solution.py:43
  127.9 1.9 fusion
  129.8 116.2 %all-gather.8.cloned.1.call-done = bf16[1664,2496]{1,0:T(8,128)(2,1)} async-done(((bf16[104,2496]{1,0:T(8,128)(2,1)}), bf16[1664,2496]{1,0:T(8,128)(2,1)}) %all-gather.8.cloned.1.call-update) | async-done | bytes 8306704 | tf_op jit(solution)/shard_map/all_gather | solution.py:49
  246.0 10.4 %select_convert_fusion = bf16[512,2496]{0,1:T(8,128)(2,1)} fusion(bf16[1664,2496]{1,0:T(8,128)(2,1)} %all-gather.8.cloned.1.call-done, pred[512]{0:T(512)(128)(4,1)S(1)} %fusion.13, bf16[512,1664]{0,1:T(8,128)(2,1)} %all-gather.6.cloned.1.call-done, f32[1664]{0:T(1024)S(1)} %convert_element_type.33, f32[512]{0:T(512)S(1)} %add_rsqrt_fusion), kind=kOutput, calls=%fused_computation.1 | convolution fusion | flops 4258988032 | bytes 12575744 | tf_op jit(solution)/shard_map/dot_general | solution.py:50
  (7 shorter events, 0.1 us)
Async XLA Ops:
  6.5 26.7 %reduce-scatter.4.cloned.1.call-start = ((), (), s32[]{:S(2)}) async-start(), calls=%async_computation.4 | async-start | bytes 1277952
  13.7 21.5 %copy-start = (bf16[512,832]{0,1:T(8,128)(2,1)S(1)}, bf16[512,832]{0,1:T(8,128)(2,1)}, u32[]{:S(2)}) copy-start(bf16[512,832]{0,1:T(8,128)(2,1)} %param.13) | copy-start | bytes 2555908
  22.1 13.6 %copy-start.4 = (u32[32]{0:T(128)S(1)}, u32[32]{0:T(128)}, u32[]{:S(2)}) copy-start(u32[32]{0:T(128)} %constant.53) | copy-start | bytes 388
  22.1 14.7 %copy-start.3 = (s32[112]{0:T(128)S(1)}, s32[112]{0:T(128)}, u32[]{:S(2)}) copy-start(s32[112]{0:T(128)} %param.16) | copy-start | bytes 1348
  22.2 83.9 %all-gather.4.cloned.1.call-start = ((), (), s32[]{:S(2)}) async-start(), calls=%async_computation.1 | async-start | bytes 3411968 | tf_op jit(solution)/shard_map/all_gather | solution.py:38
  35.1 92.8 %all-gather.6.cloned.1.call-start = ((), (), s32[]{:S(2)}) async-start(), calls=%async_computation.2 | async-start | bytes 2555904 | tf_op jit(solution)/shard_map/all_gather | solution.py:43
  52.1 67.8 %copy-start.1 = (bf16[1664]{0:T(1024)(128)(2,1)S(1)}, bf16[1664]{0:T(1024)(128)(2,1)}, u32[]{:S(2)}) copy-start(bf16[1664]{0:T(1024)(128)(2,1)} %param.14) | copy-start | bytes 9988
  52.1 67.8 %copy-start.2 = (s32[2]{0:T(128)S(1)}, s32[2]{0:T(128)}, u32[]{:S(2)}) copy-start(s32[2]{0:T(128)} %param.17) | copy-start | bytes 28
  119.3 126.7 %all-gather.8.cloned.1.call-start = ((), (), s32[]{:S(2)}) async-start(), calls=%async_computation.3 | async-start | bytes 9052160 | tf_op jit(solution)/shard_map/all_gather | solution.py:49
Sparse Core Ops, SparseCore 0:
  22.3 10.8 reduce-scatter.3
  36.3 69.7 all-gather.3
  119.4 8.4 all-gather.5
  130.8 115.1 all-gather.7
where the time goes:
time: 263 us
  waiting for transfers between devices  190 us (72%)
  matrix products  18.9 us (7%)
  blocking collectives  17.5 us (7%)
  local copies, waits for them, and re-layouts  16.6 us (6%)
  between operations  13.8 us (5%)
  other arithmetic  6.37 us (2%)
    all_gather x1, waiting for transfers between devices, shards(): whole_weight = lax.all_gather(qkv_weight, 'req', axis=0, tiled=True)  116 us
    all_gather x1, waiting for transfers between devices, shards(): piece_rows = lax.all_gather(merged, 'req', axis=0, tiled=True)  54 us
    unnamed x1, blocking collectives  14.9 us
    scatter x2, local copies, waits for them, and re-layouts, shards(): text_rows.at[jnp.where(inside, local_pos, row_count)]  13.1 us
    unnamed x5, waiting for transfers between devices  11.4 us
    dot_general x1, matrix products, shards(): jnp.dot(scaled, whole_weight, preferred_element_type=jnp.float32)  10.4 us
    dot_general x1, matrix products, shards(): jnp.einsum('mkf,kfd->md', grouped, merge_weight, preferred_element_type=j...  8.45 us
    all_gather x1, waiting for transfers between devices, shards(): lax.all_gather(combined, 'tp', axis=1, tiled=True).astype(jnp.float32)  7.92 us
  transfers between devices with their start and end apart: 4, of which 4 were waited for; matrix products, arithmetic and copies ran while one was open for 1% of the time, Pallas kernels for 0%

commit v1 on v0

v1 whole, which is shorter than its diff:
```python
import functools

import jax
import jax.numpy as jnp
from jax import lax
from jax.sharding import PartitionSpec as P

DV = 1664
SEQ = 4096
IMG_CAP = 16
EPSILON = 1e-06


def folded_ring(count):
    odd = list(range(1, count, 2))
    even = list(range(0, count, 2))
    return even[:1] + odd + even[:0:-1]


def tp_shift(value, n_tp, distance):
    return lax.ppermute(value, "tp", [(i, (i + distance) % n_tp) for i in range(n_tp)])


def tp_gather(value, n_tp, axis):
    me = lax.axis_index("tp")
    width = value.shape[axis]
    if n_tp == 2:
        other = tp_shift(value, 2, 1)
        first = jnp.where(me == 0, value, other)
        second = jnp.where(me == 0, other, value)
        return jnp.concatenate([first, second], axis=axis)
    shape = list(value.shape)
    shape[axis] = width * n_tp
    whole = jnp.zeros(shape, value.dtype)
    for distance in range(n_tp):
        block = value if distance == 0 else tp_shift(value, n_tp, distance)
        whole = lax.dynamic_update_slice_in_dim(
            whole, block, (me - distance) % n_tp * width, axis
        )
    return whole


def tp_scatter_sum(value, n_tp, axis):
    me = lax.axis_index("tp")
    width = value.shape[axis] // n_tp
    total = lax.dynamic_slice_in_dim(value, me * width, width, axis)
    for distance in range(1, n_tp):
        block = lax.dynamic_slice_in_dim(value, (me + distance) % n_tp * width, width, axis)
        total = total + tp_shift(block, n_tp, distance)
    return total


def weight_groups(weight, n_req):
    lines = n_req // 4
    order = folded_ring(lines)
    following = {order[i]: order[(i + 1) % lines] for i in range(lines)}
    line_perm = [(z * 4 + p, following[z] * 4 + p) for z in range(lines) for p in range(4)]
    x_perm = [(i, i ^ 1) for i in range(n_req)]
    y_perm = [(i, i ^ 2) for i in range(n_req)]
    preceding = jnp.array([order[order.index(z) - 1] for z in range(lines)], jnp.int32)
    plane = lax.axis_index("req") // 4
    rows = weight.shape[0]
    cut = rows // 16 * 8
    held = weight
    groups = []
    for step in range(lines):
        by_x = lax.ppermute(held, "req", x_perm)
        by_y = lax.ppermute(held, "req", y_perm)
        upper = lax.ppermute(by_y[:cut], "req", x_perm)
        lower = lax.ppermute(by_x[cut:], "req", y_perm)
        groups.append((plane, [(0, held), (1, by_x), (2, by_y), (3, upper, lower)]))
        if step < lines - 1:
            held = lax.ppermute(held, "req", line_perm)
            plane = preceding[plane]
    return groups


def shards(
    n_req, n_tp,
    patches, ln_gain, ln_bias, merge_weight, text_rows, norm_gain, qkv_weight, token_pos, text_len,
):
    row_count, width = text_rows.shape
    me = lax.axis_index("req")
    groups = weight_groups(qkv_weight, n_req)
    text_full = tp_gather(text_rows.T, n_tp, 0)

    values = patches.astype(jnp.float32)
    sum_part = jnp.sum(values, axis=1)
    square_part = jnp.sum(values * values, axis=1)
    sum_total, square_total = lax.psum((sum_part, square_part), "tp")
    row_mean = (sum_total / DV)[:, None]
    second = (square_total / DV)[:, None]
    normed = (
        (values - row_mean)
        * lax.rsqrt(second - row_mean * row_mean + EPSILON)
        * ln_gain.astype(jnp.float32)
        + ln_bias.astype(jnp.float32)
    ).astype(jnp.bfloat16)
    grouped = normed.reshape(patches.shape[0] // 4, 4, patches.shape[1])
    partial_value = jnp.einsum(
        "mkf,kfd->md", grouped, merge_weight, preferred_element_type=jnp.float32
    )
    merged = tp_scatter_sum(partial_value, n_tp, 1).astype(jnp.bfloat16)

    token_count = token_pos.shape[0]
    target = token_pos // row_count
    same = target[:, None] == target[None, :]
    ids = jnp.arange(token_count, dtype=jnp.int32)
    before = jnp.sum((same & (ids[None, :] < ids[:, None])).astype(jnp.int32), axis=1)
    slot = target * IMG_CAP + before
    slot_count = n_req * IMG_CAP
    place = (
        jnp.arange(slot_count, dtype=jnp.int32)[:, None] == slot[None, :]
    ).astype(jnp.bfloat16)
    code = token_pos % row_count + 1
    code_cols = jnp.stack([code // 256, code % 256], axis=1).astype(jnp.bfloat16)
    padding = (-width - 2) % 128
    payload = jnp.concatenate(
        [merged, code_cols, jnp.zeros((token_count, padding), jnp.bfloat16)], axis=1
    )
    outgoing = jnp.dot(place, payload, preferred_element_type=jnp.float32).astype(jnp.bfloat16)
    arrived = lax.all_to_all(
        outgoing.reshape(n_req, IMG_CAP, -1), "req", split_axis=0, concat_axis=0
    ).reshape(slot_count, -1)
    local = (
        arrived[:, width].astype(jnp.int32) * 256 + arrived[:, width + 1].astype(jnp.int32) - 1
    )
    hit = local[:, None] == jnp.arange(row_count, dtype=jnp.int32)[None, :]
    image_rows = tp_gather(arrived[:, :width], n_tp, 1)
    image_part = lax.dot_general(
        image_rows,
        hit.astype(jnp.bfloat16),
        (((0,), (0,)), ((), ())),
        preferred_element_type=jnp.float32,
    )
    full = jnp.where(jnp.any(hit, axis=0)[None, :], image_part, text_full.astype(jnp.float32))
    scaled = (
        full
        * lax.rsqrt(jnp.mean(full * full, axis=0, keepdims=True) + EPSILON)
        * norm_gain.astype(jnp.float32)[:, None]
    ).astype(jnp.bfloat16)

    rows = qkv_weight.shape[0]
    corner = me % 4
    total = None
    for plane, pieces in groups:
        lefts, rights = [], []
        for flip, *blocks in pieces:
            start = (plane * 4 + (corner ^ flip)) * rows
            rights.append(lax.dynamic_slice_in_dim(scaled, start, rows, 0))
            lefts.extend(blocks)
        part = lax.dot_general(
            jnp.concatenate(lefts, axis=0),
            jnp.concatenate(rights, axis=0),
            (((0,), (0,)), ((), ())),
            preferred_element_type=jnp.float32,
        )
        total = part if total is None else total + part

    position = me * row_count + jnp.arange(row_count, dtype=jnp.int32)
    request_ids = jnp.arange(text_len.shape[0], dtype=jnp.int32)
    limits = jnp.sum(
        jnp.where((position // SEQ)[:, None] == request_ids[None, :], text_len[None, :], 0), axis=1
    )
    keep_row = position % SEQ < limits
    return jnp.where(keep_row[None, :], total, 0.0).astype(jnp.bfloat16).T


def solution(mesh):
    placed = (
        P("req", "tp"),
        P("tp"),
        P("tp"),
        P(None, "tp", None),
        P("req", "tp"),
        P(),
        P("req", "tp"),
        P("req"),
        P(),
    )
    body = functools.partial(shards, mesh.shape["req"], mesh.shape["tp"])
    return jax.shard_map(
        body, mesh=mesh, in_specs=placed, out_specs=P("req", "tp"), check_vma=False
    )
```

time: 263 us -> 118 us (0.45)
  waiting for transfers between devices: 190 us -> 31.5 us
  starting transfers between devices: 0.31 us -> 29.3 us
  blocking collectives: 17.5 us -> 2.47 us
  between operations: 13.8 us -> 6.24 us
  local copies, waits for them, and re-layouts: 16.6 us -> 20.2 us
  other arithmetic: 6.37 us -> 9.21 us
    all_gather x3 -> x0, waiting for transfers between devices: 178 us -> none  [the longest x1 116 us: shards(): whole_weight = lax.all_gather(qkv_weight, 'req', axis=0, tiled=True)]
    ppermute x0 -> x22, waiting for transfers between devices: none -> 31.5 us  [the longest x4 20.8 us: weight_groups(): by_y = lax.ppermute(held, 'req', y_perm)]
    ppermute x0 -> x22, starting transfers between devices: none -> 25.4 us  [the longest x4 5.67 us: weight_groups(): by_y = lax.ppermute(held, 'req', y_perm)]
    unnamed x1 -> x0, blocking collectives: 14.9 us -> none
    scatter x2 -> x0, local copies, waits for them, and re-layouts: 13.1 us -> none  [shards(): text_rows.at[jnp.where(inside, local_pos, row_count)]]
    unnamed x5 -> x0, waiting for transfers between devices: 11.4 us -> none
    unnamed x15 -> x32, local copies, waits for them, and re-layouts: 3.28 us -> 12.4 us
    all_to_all x0 -> x1, starting transfers between devices: none -> 3.97 us  [shards(): lax.all_to_all(outgoing.reshape(n_req, IMG_CAP, -1), 'req', split_axis=0,...]
  transfers between devices with their start and end apart: 4 -> 23, of which waited for: 4 -> 7; matrix products, arithmetic and copies ran while one was open for 1% -> 37% of each run, Pallas kernels for 0% -> 0%
where the time goes in v1:
time: 118 us; the launch traced here: 117 us
  waiting for transfers between devices  31.5 us (27%)
  starting transfers between devices  29.3 us (25%)
  local copies, waits for them, and re-layouts  20.2 us (17%)
  matrix products  17.7 us (15%)
  other arithmetic  9.21 us (8%)
  between operations  6.24 us (5%)
  blocking collectives  2.47 us (2%)
    ppermute x4, waiting for transfers between devices, weight_groups(): by_y = lax.ppermute(held, 'req', y_perm)  20.8 us
    unnamed x32, local copies, waits for them, and re-layouts  12.4 us
    dot_general x4, matrix products, shards(): lax.dot_general(jnp.concatenate(lefts, axis=0), jnp.concatenate(rights, a...  9.72 us
    ppermute x4, waiting for transfers between devices, weight_groups(): upper = lax.ppermute(by_y[:cut], 'req', x_perm)  6.92 us
    dot_general x1, matrix products, shards(): jnp.einsum('mkf,kfd->md', grouped, merge_weight, preferred_element_type=j...  5.95 us
    ppermute x4, starting transfers between devices, weight_groups(): by_y = lax.ppermute(held, 'req', y_perm)  5.67 us
    ppermute x4, starting transfers between devices, weight_groups(): by_x = lax.ppermute(held, 'req', x_perm)  5.28 us
    ppermute x4, starting transfers between devices, weight_groups(): upper = lax.ppermute(by_y[:cut], 'req', x_perm)  5.19 us
  transfers between devices with their start and end apart: 23, of which 7 were waited for; matrix products, arithmetic and copies ran while one was open for 37% of the time, Pallas kernels for 0%

profile of v1, /device:TPU:0, one launch (start us, length us, event | category | flops | bytes accessed | tf_op | source)
XLA Modules:
  0.0 116.6 jit_solution(1936109345010202454)
XLA Ops:
  0.0 3.0 %collective-permute-start.4 = (bf16[104,2496]{1,0:T(8,128)(2,1)}, bf16[104,2496]{1,0:T(8,128)(2,1)}, u32[]{:S(2)}, u32[]{:S(2)}) collective-permute-start(bf16[104,2496]{1,0:T(8,128)(2,1)} %param.16), channel_id=1, source_target_pairs={{0,4},{2,6},{4,0},{6,2},{8,12},{10,14},{12,8},{14,10},{16,20},{18,... | collective-permute-start | bytes 1557512 | tf_op jit(solution)/shard_map/ppermute | solution.py:68
  3.0 1.5 %collective-permute-start.3 = (bf16[104,2496]{1,0:T(8,128)(2,1)}, bf16[104,2496]{1,0:T(8,128)(2,1)S(1)}, u32[]{:S(2)}, u32[]{:S(2)}) collective-permute-start(bf16[104,2496]{1,0:T(8,128)(2,1)} %param.16), channel_id=1, source_target_pairs={{0,2},{2,0},{4,6},{6,4},{8,10},{10,8},{12,14},{14,12},{16,18},{18,... | collective-permute-start | bytes 1557512 | tf_op jit(solution)/shard_map/ppermute | solution.py:67
  4.5 1.6 %collective-permute-start.7 = (bf16[104,2496]{1,0:T(8,128)(2,1)}, bf16[104,2496]{1,0:T(8,128)(2,1)}, u32[]{:S(2)}, u32[]{:S(2)}) collective-permute-start(bf16[104,2496]{1,0:T(8,128)(2,1)} %param.16), channel_id=1, source_target_pairs={{0,8},{2,10},{4,12},{6,14},{8,24},{10,26},{12,28},{14,30},{16,0},{... | collective-permute-start | bytes 1557512 | tf_op jit(solution)/shard_map/ppermute | solution.py:73
  6.0 0.7 convert_element_type.47
  6.7 0.7 convert_element_type.48
  7.4 1.5 %convert_reduce_fusion = (f32[448]{0:T(512)S(1)}, f32[448]{0:T(512)S(1)}) fusion(bf16[448,832]{1,0:T(8,128)(2,1)} %param.10), kind=kLoop, calls=%fused_computation.7 | loop fusion | flops 1490048 | bytes 749056 | tf_op jit(solution)/shard_map/reduce_sum | solution.py:88
  8.9 2.5 %all-reduce = (f32[448]{0:T(512)S(1)}, f32[448]{0:T(512)S(1)}) all-reduce(f32[448]{0:T(512)S(1)} %get-tuple-element.6, f32[448]{0:T(512)S(1)} %get-tuple-element.5), channel_id=1, replica_groups=mesh['req'=16,'tp'=2] {'tp'}, use_global_device_ids=true, to_apply=%region_5.6 | all-reduce | flops 896 | bytes 7168 | tf_op jit(solution)/shard_map/psum | solution.py:90
  11.4 1.5 %fusion.3 = bf16[448,832]{1,0:T(8,128)(2,1)S(1)} fusion(bf16[448,832]{1,0:T(8,128)(2,1)} %param.10, f32[832]{0:T(1024)S(1)} %convert_element_type.48, f32[832]{0:T(1024)S(1)} %convert_element_type.47, f32[448]{0:T(512)S(1)} %get-tuple-element.34, f32[448]{0:T(512)S(1)} %get-tuple-element.33), kind=kLoop, calls=%fused_computation.11 | loop fusion | flops 2236416 | bytes 1501184 | tf_op jit(solution)/shard_map/convert_element_type | solution.py:98
  12.9 0.2 reshape.70
  13.1 5.9 %convolution_bitcast_fusion = f32[112,1664]{1,0:T(8,128)S(1)} fusion(bf16[4,832,1664]{2,1,0:T(8,128)(2,1)} %param.13, bf16[112,4,832]{2,1,0:T(4,128)(2,1)S(1)} %reshape.70), kind=kOutput, calls=%fused_computation.4 | convolution fusion | flops 1240465408 | bytes 12566528 | tf_op jit(solution)/shard_map/mkf,kfd->md/dot_general | solution.py:100
  19.1 0.9 constant_dynamic-slice_fusion.16
  20.2 0.3 collective-permute-start.2
  20.5 1.1 constant_dynamic-update-slice_fusion.4
  22.0 0.6 dynamic_slice.69
  24.3 0.7 dynamic_slice.74
  27.0 0.6 dynamic_slice.79
  30.0 1.2 %add_convert_fusion = bf16[112,832]{1,0:T(8,128)(2,1)S(1)} fusion(f32[112,832]{1,0:T(8,128)} %collective-permute-done, f32[112,1664]{1,0:T(8,128)S(1)} %convolution_bitcast_fusion, s32[]{:T(128)S(6)} %select_n.156), kind=kLoop, calls=%fused_computation.56 | loop fusion | flops 186368 | bytes 931844 | tf_op jit(solution)/shard_map/convert_element_type | solution.py:103
  31.2 1.1 convolution_convert_fusion
  32.2 4.0 %all-to-all-start = ((bf16[16,16,896]{2,1,0:T(8,128)(2,1)}), bf16[16,16,896]{2,1,0:T(8,128)(2,1)S(1)}, u32[]{:S(2)}, u32[]{:S(2)}) async-start(bf16[16,16,896]{2,1,0:T(8,128)(2,1)} %bitcast.3), calls=%async_computation | async-start | bytes 917504 | tf_op jit(solution)/shard_map/all_to_all | solution.py:122
  36.2 1.0 slice.47
  37.2 2.0 %collective-permute-start.5 = (bf16[48,2496]{1,0:T(8,128)(2,1)S(1)}, bf16[48,2496]{1,0:T(8,128)(2,1)S(1)}, u32[]{:S(2)}, u32[]{:S(2)}) collective-permute-start(bf16[48,2496]{1,0:T(8,128)(2,1)S(1)} %slice.47), channel_id=1, source_target_pairs={{0,2},{2,0},{4,6},{6,4},{8,10},{10,8},{12,14},{14,12},{16,18},{18,... | collective-permute-start | bytes 718856 | tf_op jit(solution)/shard_map/ppermute | solution.py:69
  39.2 1.5 %collective-permute-start.6 = (bf16[56,2496]{1,0:T(8,128)(2,1)S(1)}, bf16[56,2496]{1,0:T(8,128)(2,1)S(1)}, u32[]{:S(2)}, u32[]{:S(2)}) collective-permute-start(bf16[56,2496]{1,0:T(8,128)(2,1)S(1)} %slice.48), channel_id=1, source_target_pairs={{0,4},{2,6},{4,0},{6,2},{8,12},{10,14},{12,8},{14,10},{16,20},{18,... | collective-permute-start | bytes 838664 | tf_op jit(solution)/shard_map/ppermute | solution.py:70
  40.7 1.5 %collective-permute-start.12 = (bf16[104,2496]{1,0:T(8,128)(2,1)}, bf16[104,2496]{1,0:T(8,128)(2,1)}, u32[]{:S(2)}, u32[]{:S(2)}) collective-permute-start(bf16[104,2496]{1,0:T(8,128)(2,1)} %collective-permute-done.7), channel_id=1, source_target_pairs={{0,8},{2,10},{4,12},{6,14},{8,24},{10,26},{12,28},{14,30},{16,0},{... | collective-permute-start | bytes 1557512 | tf_op jit(solution)/shard_map/ppermute | solution.py:73
  42.2 0.6 collective-permute-start.9
  42.8 1.9 %constant_dynamic-update-slice_fusion.9 = bf16[416,2496]{1,0:T(8,128)(2,1)} fusion(bf16[104,2496]{1,0:T(8,128)(2,1)} %collective-permute-done.7), kind=kLoop, calls=%fused_computation.79 | loop fusion | bytes 1051648
  44.7 1.1 constant_dynamic-update-slice_fusion.2
  45.8 2.9 %collective-permute-done.5 = bf16[48,2496]{1,0:T(8,128)(2,1)S(1)} collective-permute-done((bf16[48,2496]{1,0:T(8,128)(2,1)S(1)}, bf16[48,2496]{1,0:T(8,128)(2,1)S(1)}, u32[]{:S(2)}, u32[]{:S(2)}) %collective-permute-start.5) | collective-permute-done | bytes 239648 | tf_op jit(solution)/shard_map/ppermute | solution.py:69
  48.7 1.2 %collective-permute-start.8 = (bf16[104,2496]{1,0:T(8,128)(2,1)}, bf16[104,2496]{1,0:T(8,128)(2,1)S(1)}, u32[]{:S(2)}, u32[]{:S(2)}) collective-permute-start(bf16[104,2496]{1,0:T(8,128)(2,1)} %collective-permute-done.7), channel_id=1, source_target_pairs={{0,2},{2,0},{4,6},{6,4},{8,10},{10,8},{12,14},{14,12},{16,18},{18,... | collective-permute-start | bytes 1557512 | tf_op jit(solution)/shard_map/ppermute | solution.py:67
  49.9 1.5 %collective-permute-done.6 = bf16[56,2496]{1,0:T(8,128)(2,1)S(1)} collective-permute-done((bf16[56,2496]{1,0:T(8,128)(2,1)S(1)}, bf16[56,2496]{1,0:T(8,128)(2,1)S(1)}, u32[]{:S(2)}, u32[]{:S(2)}) %collective-permute-start.6) | collective-permute-done | bytes 279584 | tf_op jit(solution)/shard_map/ppermute | solution.py:70
  51.5 2.7 %broadcast_select_fusion.1 = (bf16[832,512]{1,0:T(8,128)(2,1)}, bf16[832,512]{1,0:T(8,128)(2,1)}) fusion(bf16[832,512]{1,0:T(8,128)(2,1)} %collective-permute-done.2, pred[]{:T(512)S(6)} %eq.81, bf16[512,832]{0,1:T(8,128)(2,1)} %param.14), kind=kLoop, calls=%fused_computation.18 | loop fusion | flops 851968 | bytes 3407873 | tf_op jit(solution)/shard_map/jit(_where)/select_n | solution.py:29
  54.2 7.8 %collective-permute-done.9 = bf16[104,2496]{1,0:T(8,128)(2,1)S(1)} collective-permute-done((bf16[104,2496]{1,0:T(8,128)(2,1)}, bf16[104,2496]{1,0:T(8,128)(2,1)S(1)}, u32[]{:S(2)}, u32[]{:S(2)}) %collective-permute-start.9) | collective-permute-done | bytes 519200 | tf_op jit(solution)/shard_map/ppermute | solution.py:68
  62.0 0.7 slice.49
  62.7 1.1 collective-permute-start.10
  63.7 0.7 slice.50
  64.5 1.0 collective-permute-start.11
  65.4 1.3 %collective-permute-start.17 = (bf16[104,2496]{1,0:T(8,128)(2,1)}, bf16[104,2496]{1,0:T(8,128)(2,1)}, u32[]{:S(2)}, u32[]{:S(2)}) collective-permute-start(bf16[104,2496]{1,0:T(8,128)(2,1)} %collective-permute-done.12), channel_id=1, source_target_pairs={{0,8},{2,10},{4,12},{6,14},{8,24},{10,26},{12,28},{14,30},{16,0},{... | collective-permute-start | bytes 1557512 | tf_op jit(solution)/shard_map/ppermute | solution.py:73
  66.7 1.6 %collective-permute-start.14 = (bf16[104,2496]{1,0:T(8,128)(2,1)}, bf16[104,2496]{1,0:T(8,128)(2,1)}, u32[]{:S(2)}, u32[]{:S(2)}) collective-permute-start(bf16[104,2496]{1,0:T(8,128)(2,1)} %collective-permute-done.12), channel_id=1, source_target_pairs={{0,4},{2,6},{4,0},{6,2},{8,12},{10,14},{12,8},{14,10},{16,20},{18,... | collective-permute-start | bytes 1557512 | tf_op jit(solution)/shard_map/ppermute | solution.py:68
  68.2 0.9 collective-permute-start.13
  69.1 1.9 %constant_dynamic-update-slice_fusion.14 = bf16[416,2496]{1,0:T(8,128)(2,1)} fusion(bf16[104,2496]{1,0:T(8,128)(2,1)} %collective-permute-done.12), kind=kLoop, calls=%fused_computation.84 | loop fusion | bytes 1051648
  71.0 0.8 constant_dynamic-update-slice_fusion.8
  71.8 0.8 constant_dynamic-update-slice_fusion.7
  73.3 1.8 %constant_dynamic-update-slice_fusion.6 = bf16[416,2496]{1,0:T(8,128)(2,1)} fusion(bf16[416,2496]{1,0:T(8,128)(2,1)} %constant_dynamic-update-slice_fusion.7, bf16[48,2496]{1,0:T(8,128)(2,1)} %collective-permute-done.10), kind=kLoop, calls=%fused_computation.76 | loop fusion | bytes 491520
  75.1 0.7 constant_dynamic-update-slice_fusion.5
  75.8 8.8 %collective-permute-done.14 = bf16[104,2496]{1,0:T(8,128)(2,1)} collective-permute-done((bf16[104,2496]{1,0:T(8,128)(2,1)}, bf16[104,2496]{1,0:T(8,128)(2,1)}, u32[]{:S(2)}, u32[]{:S(2)}) %collective-permute-start.14) | collective-permute-done | bytes 519200 | tf_op jit(solution)/shard_map/ppermute | solution.py:68
  84.6 1.0 slice.51
  85.5 0.3 collective-permute-start.15
  85.9 1.5 %collective-permute-start.16 = (bf16[56,2496]{1,0:T(8,128)(2,1)S(1)}, bf16[56,2496]{1,0:T(8,128)(2,1)S(1)}, u32[]{:S(2)}, u32[]{:S(2)}) collective-permute-start(bf16[56,2496]{1,0:T(8,128)(2,1)S(1)} %slice.52), channel_id=1, source_target_pairs={{0,4},{2,6},{4,0},{6,2},{8,12},{10,14},{12,8},{14,10},{16,20},{18,... | collective-permute-start | bytes 838664 | tf_op jit(solution)/shard_map/ppermute | solution.py:70
  87.4 0.6 collective-permute-start.19
  88.0 1.7 %collective-permute-start.18 = (bf16[104,2496]{1,0:T(8,128)(2,1)}, bf16[104,2496]{1,0:T(8,128)(2,1)S(1)}, u32[]{:S(2)}, u32[]{:S(2)}) collective-permute-start(bf16[104,2496]{1,0:T(8,128)(2,1)} %collective-permute-done.17), channel_id=1, source_target_pairs={{0,2},{2,0},{4,6},{6,4},{8,10},{10,8},{12,14},{14,12},{16,18},{18,... | collective-permute-start | bytes 1557512 | tf_op jit(solution)/shard_map/ppermute | solution.py:67
  89.8 1.1 constant_dynamic-update-slice_fusion.19
  90.9 1.2 %constant_dynamic-update-slice_fusion.12 = bf16[416,2496]{1,0:T(8,128)(2,1)S(1)} fusion(bf16[416,2496]{1,0:T(8,128)(2,1)S(1)} %constant_dynamic-update-slice_fusion.13, bf16[104,2496]{1,0:T(8,128)(2,1)} %collective-permute-done.14), kind=kLoop, calls=%fused_computation.82 | loop fusion | bytes 1051648
  92.3 0.2 copy-done.2
  92.5 1.0 multiply_reduce_fusion
  93.5 0.4 multiply_convert_fusion
  93.8 0.2 constant_dynamic-slice_fusion.3
  94.1 1.6 %fusion.10 = f32[512,2496]{0,1:T(8,128)S(1)} fusion(bf16[416,2496]{1,0:T(8,128)(2,1)S(1)} %constant_dynamic-update-slice_fusion, bf16[104,512]{1,0:T(8,128)(2,1)S(1)} %get-tuple-element.23, bf16[104,512]{1,0:T(8,128)(2,1)S(1)} %get-tuple-element.24, bf16[104,512]{1,0:T(8,128)(2,1)S(1)} %get-tuple-element.25, bf16[104,512]{1,0:T(8,128)(2,1)S(1)} %get-tuple-element.26), kind=kOutput, calls=%fused_computation.24 | convolution fusion | flops 1064960000 | bytes 7614464 | tf_op jit(solution)/shard_map/dot_general | solution.py:152
  95.6 3.1 %fusion.18 = f32[512,2496]{0,1:T(8,128)S(1)} fusion(bf16[416,2496]{1,0:T(8,128)(2,1)} %constant_dynamic-update-slice_fusion.5, bf16[104,512]{1,0:T(8,128)(2,1)S(1)} %get-tuple-element.19, bf16[104,512]{1,0:T(8,128)(2,1)S(1)} %get-tuple-element.20, bf16[104,512]{1,0:T(8,128)(2,1)S(1)} %get-tuple-element.21, bf16[104,512]{1,0:T(8,128)(2,1)S(1)} %get-tuple-element.22), kind=kOutput, calls=%fused_computation.32 | convolution fusion | flops 1064960000 | bytes 7614464 | tf_op jit(solution)/shard_map/dot_general | solution.py:152
  98.9 1.5 %fusion.26 = f32[512,2496]{0,1:T(8,128)S(1)} fusion(bf16[416,2496]{1,0:T(8,128)(2,1)S(1)} %constant_dynamic-update-slice_fusion.10, bf16[104,512]{1,0:T(8,128)(2,1)S(1)} %get-tuple-element.15, bf16[104,512]{1,0:T(8,128)(2,1)S(1)} %get-tuple-element.16, bf16[104,512]{1,0:T(8,128)(2,1)S(1)} %get-tuple-element.17, bf16[104,512]{1,0:T(8,128)(2,1)S(1)} %get-tuple-element.18), kind=kOutput, calls=%fused_computation.40 | convolution fusion | flops 1064960000 | bytes 7614464 | tf_op jit(solution)/shard_map/dot_general | solution.py:152
  100.4 4.2 %collective-permute-done.19 = bf16[104,2496]{1,0:T(8,128)(2,1)S(1)} collective-permute-done((bf16[104,2496]{1,0:T(8,128)(2,1)}, bf16[104,2496]{1,0:T(8,128)(2,1)S(1)}, u32[]{:S(2)}, u32[]{:S(2)}) %collective-permute-start.19) | collective-permute-done | bytes 519200 | tf_op jit(solution)/shard_map/ppermute | solution.py:68
  104.6 1.8 %collective-permute-start.20 = (bf16[48,2496]{1,0:T(8,128)(2,1)S(1)}, bf16[48,2496]{1,0:T(8,128)(2,1)S(1)}, u32[]{:S(2)}, u32[]{:S(2)}) collective-permute-start(bf16[48,2496]{1,0:T(8,128)(2,1)S(1)} %slice.53), channel_id=1, source_target_pairs={{0,2},{2,0},{4,6},{6,4},{8,10},{10,8},{12,14},{14,12},{16,18},{18,... | collective-permute-start | bytes 718856 | tf_op jit(solution)/shard_map/ppermute | solution.py:69
  106.4 0.4 collective-permute-start.21
  106.9 4.0 %collective-permute-done.20 = bf16[48,2496]{1,0:T(8,128)(2,1)S(1)} collective-permute-done((bf16[48,2496]{1,0:T(8,128)(2,1)S(1)}, bf16[48,2496]{1,0:T(8,128)(2,1)S(1)}, u32[]{:S(2)}, u32[]{:S(2)}) %collective-permute-start.20) | collective-permute-done | bytes 239648 | tf_op jit(solution)/shard_map/ppermute | solution.py:69
  110.9 2.2 %collective-permute-done.21 = bf16[56,2496]{1,0:T(8,128)(2,1)S(1)} collective-permute-done((bf16[56,2496]{1,0:T(8,128)(2,1)S(1)}, bf16[56,2496]{1,0:T(8,128)(2,1)S(1)}, u32[]{:S(2)}, u32[]{:S(2)}) %collective-permute-start.21) | collective-permute-done | bytes 279584 | tf_op jit(solution)/shard_map/ppermute | solution.py:70
  113.2 3.5 %select_convert_fusion = bf16[512,2496]{0,1:T(8,128)(2,1)} fusion(f32[512,2496]{0,1:T(8,128)S(1)} %fusion.26, f32[512,2496]{0,1:T(8,128)S(1)} %fusion.10, f32[512,2496]{0,1:T(8,128)S(1)} %fusion.18, pred[512]{0:T(512)(128)(4,1)S(1)} %fusion.55, bf16[416,2496]{1,0:T(8,128)(2,1)S(1)} %constant_dynamic-update-slice_fusion.15, ...), kind=kOutput, calls=%fused_computation | convolution fusion | flops 1071349760 | bytes 20394496 | tf_op jit(solution)/shard_map/dot_general | solution.py:152
  (65 shorter events, 1.9 us)
Async XLA Ops:
  0.0 36.2 %collective-permute-start.4 = (bf16[104,2496]{1,0:T(8,128)(2,1)}, bf16[104,2496]{1,0:T(8,128)(2,1)}, u32[]{:S(2)}, u32[]{:S(2)}) collective-permute-start(bf16[104,2496]{1,0:T(8,128)(2,1)} %param.16), channel_id=1, source_target_pairs={{0,4},{2,6},{4,0},{6,2},{8,12},{10,14},{12,8},{14,10},{16,20},{18,... | collective-permute-start | bytes 1557512 | tf_op jit(solution)/shard_map/ppermute | solution.py:68
  3.0 36.2 %collective-permute-start.3 = (bf16[104,2496]{1,0:T(8,128)(2,1)}, bf16[104,2496]{1,0:T(8,128)(2,1)S(1)}, u32[]{:S(2)}, u32[]{:S(2)}) collective-permute-start(bf16[104,2496]{1,0:T(8,128)(2,1)} %param.16), channel_id=1, source_target_pairs={{0,2},{2,0},{4,6},{6,4},{8,10},{10,8},{12,14},{14,12},{16,18},{18,... | collective-permute-start | bytes 1557512 | tf_op jit(solution)/shard_map/ppermute | solution.py:67
  4.5 36.3 %collective-permute-start.7 = (bf16[104,2496]{1,0:T(8,128)(2,1)}, bf16[104,2496]{1,0:T(8,128)(2,1)}, u32[]{:S(2)}, u32[]{:S(2)}) collective-permute-start(bf16[104,2496]{1,0:T(8,128)(2,1)} %param.16), channel_id=1, source_target_pairs={{0,8},{2,10},{4,12},{6,14},{8,24},{10,26},{12,28},{14,30},{16,0},{... | collective-permute-start | bytes 1557512 | tf_op jit(solution)/shard_map/ppermute | solution.py:73
  13.1 8.5 %copy-start.5 = (s32[112]{0:T(128)S(1)}, s32[112]{0:T(128)}, u32[]{:S(2)}) copy-start(s32[112]{0:T(128)} %param.17) | copy-start | bytes 1348
  13.1 8.7 %copy-start.4 = (s32[2]{0:T(128)S(1)}, s32[2]{0:T(128)}, u32[]{:S(2)}) copy-start(s32[2]{0:T(128)} %param.18) | copy-start | bytes 28
  13.1 8.9 %copy-start.6 = (s32[4]{0:T(128)S(1)}, s32[4]{0:T(128)}, u32[]{:S(2)}) copy-start(s32[4]{0:T(128)} %constant.146.clone) | copy-start | bytes 52
  13.1 16.4 %copy-start.3 = (bf16[1664]{0:T(1024)(128)(2,1)S(1)}, bf16[1664]{0:T(1024)(128)(2,1)}, u32[]{:S(2)}) copy-start(bf16[1664]{0:T(1024)(128)(2,1)} %param.15) | copy-start | bytes 9988
  20.0 10.0 %collective-permute-start = (f32[112,832]{1,0:T(8,128)}, f32[112,832]{1,0:T(8,128)}, u32[]{:S(2)}, u32[]{:S(2)}) collective-permute-start(f32[112,832]{1,0:T(8,128)} %constant_dynamic-slice_fusion.16), channel_id=1, source_target_pairs={{0,1},{1,0},{2,3},{3,2},{4,5},{5,4},{6,7},{7,6},{8,9},{9,8},{10,11... | collective-permute-start | bytes 1118216 | tf_op jit(solution)/shard_map/ppermute | solution.py:21
  20.2 31.3 %collective-permute-start.2 = (bf16[832,512]{1,0:T(8,128)(2,1)}, bf16[832,512]{1,0:T(8,128)(2,1)}, u32[]{:S(2)}, u32[]{:S(2)}) collective-permute-start(bf16[832,512]{1,0:T(8,128)(2,1)} %bitcast.6), channel_id=1, source_target_pairs={{0,1},{1,0},{2,3},{3,2},{4,5},{5,4},{6,7},{7,6},{8,9},{9,8},{10,11... | collective-permute-start | bytes 2555912 | tf_op jit(solution)/shard_map/ppermute | solution.py:21
  32.2 40.5 %all-to-all-start = ((bf16[16,16,896]{2,1,0:T(8,128)(2,1)}), bf16[16,16,896]{2,1,0:T(8,128)(2,1)S(1)}, u32[]{:S(2)}, u32[]{:S(2)}) async-start(bf16[16,16,896]{2,1,0:T(8,128)(2,1)} %bitcast.3), calls=%async_computation | async-start | bytes 917504 | tf_op jit(solution)/shard_map/all_to_all | solution.py:122
  37.2 11.5 %collective-permute-start.5 = (bf16[48,2496]{1,0:T(8,128)(2,1)S(1)}, bf16[48,2496]{1,0:T(8,128)(2,1)S(1)}, u32[]{:S(2)}, u32[]{:S(2)}) collective-permute-start(bf16[48,2496]{1,0:T(8,128)(2,1)S(1)} %slice.47), channel_id=1, source_target_pairs={{0,2},{2,0},{4,6},{6,4},{8,10},{10,8},{12,14},{14,12},{16,18},{18,... | collective-permute-start | bytes 718856 | tf_op jit(solution)/shard_map/ppermute | solution.py:69
  39.2 12.2 %collective-permute-start.6 = (bf16[56,2496]{1,0:T(8,128)(2,1)S(1)}, bf16[56,2496]{1,0:T(8,128)(2,1)S(1)}, u32[]{:S(2)}, u32[]{:S(2)}) collective-permute-start(bf16[56,2496]{1,0:T(8,128)(2,1)S(1)} %slice.48), channel_id=1, source_target_pairs={{0,4},{2,6},{4,0},{6,2},{8,12},{10,14},{12,8},{14,10},{16,20},{18,... | collective-permute-start | bytes 838664 | tf_op jit(solution)/shard_map/ppermute | solution.py:70
  40.7 24.7 %collective-permute-start.12 = (bf16[104,2496]{1,0:T(8,128)(2,1)}, bf16[104,2496]{1,0:T(8,128)(2,1)}, u32[]{:S(2)}, u32[]{:S(2)}) collective-permute-start(bf16[104,2496]{1,0:T(8,128)(2,1)} %collective-permute-done.7), channel_id=1, source_target_pairs={{0,8},{2,10},{4,12},{6,14},{8,24},{10,26},{12,28},{14,30},{16,0},{... | collective-permute-start | bytes 1557512 | tf_op jit(solution)/shard_map/ppermute | solution.py:73
  42.2 19.7 %collective-permute-start.9 = (bf16[104,2496]{1,0:T(8,128)(2,1)}, bf16[104,2496]{1,0:T(8,128)(2,1)S(1)}, u32[]{:S(2)}, u32[]{:S(2)}) collective-permute-start(bf16[104,2496]{1,0:T(8,128)(2,1)} %collective-permute-done.7), channel_id=1, source_target_pairs={{0,4},{2,6},{4,0},{6,2},{8,12},{10,14},{12,8},{14,10},{16,20},{18,... | collective-permute-start | bytes 1557512 | tf_op jit(solution)/shard_map/ppermute | solution.py:68
  48.7 15.0 %collective-permute-start.8 = (bf16[104,2496]{1,0:T(8,128)(2,1)}, bf16[104,2496]{1,0:T(8,128)(2,1)S(1)}, u32[]{:S(2)}, u32[]{:S(2)}) collective-permute-start(bf16[104,2496]{1,0:T(8,128)(2,1)} %collective-permute-done.7), channel_id=1, source_target_pairs={{0,2},{2,0},{4,6},{6,4},{8,10},{10,8},{12,14},{14,12},{16,18},{18,... | collective-permute-start | bytes 1557512 | tf_op jit(solution)/shard_map/ppermute | solution.py:67
  62.7 10.5 %collective-permute-start.10 = (bf16[48,2496]{1,0:T(8,128)(2,1)}, bf16[48,2496]{1,0:T(8,128)(2,1)}, u32[]{:S(2)}, u32[]{:S(2)}) collective-permute-start(bf16[48,2496]{1,0:T(8,128)(2,1)} %slice.49), channel_id=1, source_target_pairs={{0,2},{2,0},{4,6},{6,4},{8,10},{10,8},{12,14},{14,12},{16,18},{18,... | collective-permute-start | bytes 718856 | tf_op jit(solution)/shard_map/ppermute | solution.py:69
  64.5 10.6 %collective-permute-start.11 = (bf16[56,2496]{1,0:T(8,128)(2,1)}, bf16[56,2496]{1,0:T(8,128)(2,1)S(1)}, u32[]{:S(2)}, u32[]{:S(2)}) collective-permute-start(bf16[56,2496]{1,0:T(8,128)(2,1)} %slice.50), channel_id=1, source_target_pairs={{0,4},{2,6},{4,0},{6,2},{8,12},{10,14},{12,8},{14,10},{16,20},{18,... | collective-permute-start | bytes 838664 | tf_op jit(solution)/shard_map/ppermute | solution.py:70
  65.4 22.0 %collective-permute-start.17 = (bf16[104,2496]{1,0:T(8,128)(2,1)}, bf16[104,2496]{1,0:T(8,128)(2,1)}, u32[]{:S(2)}, u32[]{:S(2)}) collective-permute-start(bf16[104,2496]{1,0:T(8,128)(2,1)} %collective-permute-done.12), channel_id=1, source_target_pairs={{0,8},{2,10},{4,12},{6,14},{8,24},{10,26},{12,28},{14,30},{16,0},{... | collective-permute-start | bytes 1557512 | tf_op jit(solution)/shard_map/ppermute | solution.py:73
  66.7 17.9 %collective-permute-start.14 = (bf16[104,2496]{1,0:T(8,128)(2,1)}, bf16[104,2496]{1,0:T(8,128)(2,1)}, u32[]{:S(2)}, u32[]{:S(2)}) collective-permute-start(bf16[104,2496]{1,0:T(8,128)(2,1)} %collective-permute-done.12), channel_id=1, source_target_pairs={{0,4},{2,6},{4,0},{6,2},{8,12},{10,14},{12,8},{14,10},{16,20},{18,... | collective-permute-start | bytes 1557512 | tf_op jit(solution)/shard_map/ppermute | solution.py:68
  68.2 17.6 %collective-permute-start.13 = (bf16[104,2496]{1,0:T(8,128)(2,1)}, bf16[104,2496]{1,0:T(8,128)(2,1)S(1)}, u32[]{:S(2)}, u32[]{:S(2)}) collective-permute-start(bf16[104,2496]{1,0:T(8,128)(2,1)} %collective-permute-done.12), channel_id=1, source_target_pairs={{0,2},{2,0},{4,6},{6,4},{8,10},{10,8},{12,14},{14,12},{16,18},{18,... | collective-permute-start | bytes 1557512 | tf_op jit(solution)/shard_map/ppermute | solution.py:67
  73.0 17.9 %copy-start = (bf16[416,2496]{1,0:T(8,128)(2,1)S(1)}, bf16[416,2496]{1,0:T(8,128)(2,1)}, u32[]{:S(2)}) copy-start(bf16[416,2496]{1,0:T(8,128)(2,1)} %constant_dynamic-update-slice_fusion.14) | copy-start | bytes 6230020
  73.2 19.0 %collective-permute-start.1 = (bf16[256,832]{1,0:T(8,128)(2,1)S(1)}, bf16[256,832]{1,0:T(8,128)(2,1)S(1)}, u32[]{:S(2)}, u32[]{:S(2)}) collective-permute-start(bf16[256,832]{1,0:T(8,128)(2,1)S(1)} %bitcast.22), channel_id=1, source_target_pairs={{0,1},{1,0},{2,3},{3,2},{4,5},{5,4},{6,7},{7,6},{8,9},{9,8},{10,11... | collective-permute-start | bytes 1277960 | tf_op jit(solution)/shard_map/ppermute | solution.py:21
  85.5 13.2 %collective-permute-start.15 = (bf16[48,2496]{1,0:T(8,128)(2,1)S(1)}, bf16[48,2496]{1,0:T(8,128)(2,1)S(1)}, u32[]{:S(2)}, u32[]{:S(2)}) collective-permute-start(bf16[48,2496]{1,0:T(8,128)(2,1)S(1)} %slice.51), channel_id=1, source_target_pairs={{0,2},{2,0},{4,6},{6,4},{8,10},{10,8},{12,14},{14,12},{16,18},{18,... | collective-permute-start | bytes 718856 | tf_op jit(solution)/shard_map/ppermute | solution.py:69
  85.9 12.9 %collective-permute-start.16 = (bf16[56,2496]{1,0:T(8,128)(2,1)S(1)}, bf16[56,2496]{1,0:T(8,128)(2,1)S(1)}, u32[]{:S(2)}, u32[]{:S(2)}) collective-permute-start(bf16[56,2496]{1,0:T(8,128)(2,1)S(1)} %slice.52), channel_id=1, source_target_pairs={{0,4},{2,6},{4,0},{6,2},{8,12},{10,14},{12,8},{14,10},{16,20},{18,... | collective-permute-start | bytes 838664 | tf_op jit(solution)/shard_map/ppermute | solution.py:70
  87.4 17.2 %collective-permute-start.19 = (bf16[104,2496]{1,0:T(8,128)(2,1)}, bf16[104,2496]{1,0:T(8,128)(2,1)S(1)}, u32[]{:S(2)}, u32[]{:S(2)}) collective-permute-start(bf16[104,2496]{1,0:T(8,128)(2,1)} %collective-permute-done.17), channel_id=1, source_target_pairs={{0,4},{2,6},{4,0},{6,2},{8,12},{10,14},{12,8},{14,10},{16,20},{18,... | collective-permute-start | bytes 1557512 | tf_op jit(solution)/shard_map/ppermute | solution.py:68
  88.0 18.4 %collective-permute-start.18 = (bf16[104,2496]{1,0:T(8,128)(2,1)}, bf16[104,2496]{1,0:T(8,128)(2,1)S(1)}, u32[]{:S(2)}, u32[]{:S(2)}) collective-permute-start(bf16[104,2496]{1,0:T(8,128)(2,1)} %collective-permute-done.17), channel_id=1, source_target_pairs={{0,2},{2,0},{4,6},{6,4},{8,10},{10,8},{12,14},{14,12},{16,18},{18,... | collective-permute-start | bytes 1557512 | tf_op jit(solution)/shard_map/ppermute | solution.py:67
  90.9 1.4 %copy-start.1 = (bf16[832,512]{1,0:T(8,128)(2,1)S(1)}, bf16[832,512]{1,0:T(8,128)(2,1)}, u32[]{:S(2)}) copy-start(bf16[832,512]{1,0:T(8,128)(2,1)} %get-tuple-element.27) | copy-start | bytes 2555908
  90.9 1.6 %copy-start.2 = (bf16[832,512]{1,0:T(8,128)(2,1)S(1)}, bf16[832,512]{1,0:T(8,128)(2,1)}, u32[]{:S(2)}) copy-start(bf16[832,512]{1,0:T(8,128)(2,1)} %get-tuple-element.28) | copy-start | bytes 2555908
  104.6 6.3 %collective-permute-start.20 = (bf16[48,2496]{1,0:T(8,128)(2,1)S(1)}, bf16[48,2496]{1,0:T(8,128)(2,1)S(1)}, u32[]{:S(2)}, u32[]{:S(2)}) collective-permute-start(bf16[48,2496]{1,0:T(8,128)(2,1)S(1)} %slice.53), channel_id=1, source_target_pairs={{0,2},{2,0},{4,6},{6,4},{8,10},{10,8},{12,14},{14,12},{16,18},{18,... | collective-permute-start | bytes 718856 | tf_op jit(solution)/shard_map/ppermute | solution.py:69
  106.4 6.7 %collective-permute-start.21 = (bf16[56,2496]{1,0:T(8,128)(2,1)S(1)}, bf16[56,2496]{1,0:T(8,128)(2,1)S(1)}, u32[]{:S(2)}, u32[]{:S(2)}) collective-permute-start(bf16[56,2496]{1,0:T(8,128)(2,1)S(1)} %slice.54), channel_id=1, source_target_pairs={{0,4},{2,6},{4,0},{6,2},{8,12},{10,14},{12,8},{14,10},{16,20},{18,... | collective-permute-start | bytes 838664 | tf_op jit(solution)/shard_map/ppermute | solution.py:70

commit v2 on v1

--- a/solution.py
+++ b/solution.py
@@ -50,29 +50,32 @@
     return total
 
 
-def weight_groups(weight, n_req):
-    lines = n_req // 4
-    order = folded_ring(lines)
-    following = {order[i]: order[(i + 1) % lines] for i in range(lines)}
-    line_perm = [(z * 4 + p, following[z] * 4 + p) for z in range(lines) for p in range(4)]
-    x_perm = [(i, i ^ 1) for i in range(n_req)]
-    y_perm = [(i, i ^ 2) for i in range(n_req)]
-    preceding = jnp.array([order[order.index(z) - 1] for z in range(lines)], jnp.int32)
-    plane = lax.axis_index("req") // 4
-    rows = weight.shape[0]
-    cut = rows // 16 * 8
-    held = weight
-    groups = []
-    for step in range(lines):
-        by_x = lax.ppermute(held, "req", x_perm)
-        by_y = lax.ppermute(held, "req", y_perm)
-        upper = lax.ppermute(by_y[:cut], "req", x_perm)
-        lower = lax.ppermute(by_x[cut:], "req", y_perm)
-        groups.append((plane, [(0, held), (1, by_x), (2, by_y), (3, upper, lower)]))
-        if step < lines - 1:
-            held = lax.ppermute(held, "req", line_perm)
-            plane = preceding[plane]
-    return groups
+def tie(*values):
+    return lax.optimization_barrier(values)
+
+
+class WeightRing:
+    def __init__(self, weight, n_req):
+        lines = n_req // 4
+        order = folded_ring(lines)
+        following = {order[i]: order[(i + 1) % lines] for i in range(lines)}
+        self.line_perm = [(z * 4 + p, following[z] * 4 + p) for z in range(lines) for p in range(4)]
+        self.x_perm = [(i, i ^ 1) for i in range(n_req)]
+        self.y_perm = [(i, i ^ 2) for i in range(n_req)]
+        self.preceding = jnp.array([order[order.index(z) - 1] for z in range(lines)], jnp.int32)
+        self.lines = lines
+        self.cut = weight.shape[0] // 16 * 8
+
+    def along_line(self, block):
+        return lax.ppermute(block, "req", self.line_perm)
+
+    def to_sides(self, block):
+        return lax.ppermute(block, "req", self.x_perm), lax.ppermute(block, "req", self.y_perm)
+
+    def to_corner(self, by_x, by_y):
+        upper = lax.ppermute(by_y[: self.cut], "req", self.x_perm)
+        lower = lax.ppermute(by_x[self.cut :], "req", self.y_perm)
+        return upper, lower
 
 
 def shards(
@@ -81,8 +84,28 @@
 ):
     row_count, width = text_rows.shape
     me = lax.axis_index("req")
-    groups = weight_groups(qkv_weight, n_req)
-    text_full = tp_gather(text_rows.T, n_tp, 0)
+    ring = WeightRing(qkv_weight, n_req)
+    lines = ring.lines
+    held = [qkv_weight]
+    sides = []
+    corners = []
+
+    def next_line(deps=()):
+        if len(held) < lines:
+            held.append(ring.along_line(held[-1]))
+
+    def next_sides():
+        if len(sides) < lines:
+            sides.append(ring.to_sides(held[len(sides)]))
+
+    def next_corner():
+        if len(corners) < lines:
+            corners.append(ring.to_corner(*sides[len(corners)]))
+
+    next_line()
+    next_sides()
+    text_other = text_rows.T
+    text_full = tp_gather(text_other, n_tp, 0)
 
     values = patches.astype(jnp.float32)
     sum_part = jnp.sum(values, axis=1)
@@ -96,10 +119,20 @@
         * ln_gain.astype(jnp.float32)
         + ln_bias.astype(jnp.float32)
     ).astype(jnp.bfloat16)
+
+    normed, held[-1], sides[0] = tie(normed, held[-1], sides[0])
+    next_line()
+    next_sides()
+    next_corner()
+
     grouped = normed.reshape(patches.shape[0] // 4, 4, patches.shape[1])
     partial_value = jnp.einsum(
         "mkf,kfd->md", grouped, merge_weight, preferred_element_type=jnp.float32
     )
+
+    partial_value, held[-1] = tie(partial_value, held[-1])
+    next_line()
+    next_sides()
     merged = tp_scatter_sum(partial_value, n_tp, 1).astype(jnp.bfloat16)
 
     token_count = token_pos.shape[0]
@@ -122,6 +155,10 @@
     arrived = lax.all_to_all(
         outgoing.reshape(n_req, IMG_CAP, -1), "req", split_axis=0, concat_axis=0
     ).reshape(slot_count, -1)
+
+    arrived, held[-1], sides[1] = tie(arrived, held[-1], sides[1])
+    next_corner()
+    next_sides()
     local = (
         arrived[:, width].astype(jnp.int32) * 256 + arrived[:, width + 1].astype(jnp.int32) - 1
     )
@@ -134,28 +171,58 @@
         preferred_element_type=jnp.float32,
     )
     full = jnp.where(jnp.any(hit, axis=0)[None, :], image_part, text_full.astype(jnp.float32))
+    full, sides[2 % lines] = tie(full, sides[2 % lines])
+    next_corner()
     scaled = (
         full
         * lax.rsqrt(jnp.mean(full * full, axis=0, keepdims=True) + EPSILON)
         * norm_gain.astype(jnp.float32)[:, None]
     ).astype(jnp.bfloat16)
 
+    while len(corners) < lines:
+        next_line()
+        next_sides()
+        next_corner()
+
     rows = qkv_weight.shape[0]
     corner = me % 4
-    total = None
-    for plane, pieces in groups:
-        lefts, rights = [], []
-        for flip, *blocks in pieces:
-            start = (plane * 4 + (corner ^ flip)) * rows
-            rights.append(lax.dynamic_slice_in_dim(scaled, start, rows, 0))
-            lefts.extend(blocks)
-        part = lax.dot_general(
+
+    def product(plane, flip, blocks, first=0):
+        count = sum(block.shape[0] for block in blocks)
+        start = (plane * 4 + (corner ^ flip)) * rows + first
+        return lax.dot_general(
+            blocks[0] if len(blocks) == 1 else jnp.concatenate(blocks, axis=0),
+            lax.dynamic_slice_in_dim(scaled, start, count, 0),
+            (((0,), (0,)), ((), ())),
+            preferred_element_type=jnp.float32,
+        )
+
+    def product_of(pieces):
+        lefts = [block for _, _, _, block in pieces]
+        rights = [
+            lax.dynamic_slice_in_dim(
+                scaled, (plane * 4 + (corner ^ flip)) * rows + first, block.shape[0], 0
+            )
+            for plane, flip, first, block in pieces
+        ]
+        return lax.dot_general(
             jnp.concatenate(lefts, axis=0),
             jnp.concatenate(rights, axis=0),
             (((0,), (0,)), ((), ())),
             preferred_element_type=jnp.float32,
         )
-        total = part if total is None else total + part
+
+    plane = me // 4
+    total = jnp.zeros((qkv_weight.shape[1], row_count), jnp.float32)
+    cut = ring.cut
+    for step in range(lines):
+        by_x, by_y = sides[step]
+        upper, lower = corners[step]
+        total = total + product_of(
+            [(plane, 0, 0, held[step]), (plane, 1, 0, by_x), (plane, 2, 0, by_y)]
+        )
+        total = total + product_of([(plane, 3, 0, upper), (plane, 3, cut, lower)])
+        plane = ring.preceding[plane]
 
     position = me * row_count + jnp.arange(row_count, dtype=jnp.int32)
     request_ids = jnp.arange(text_len.shape[0], dtype=jnp.int32)

time: 118 us -> 138 us (1.17)
  matrix products: 17.7 us -> 45 us
  local copies, waits for them, and re-layouts: 20.2 us -> 9.81 us
  starting transfers between devices: 29.3 us -> 32.1 us
    dot_general x4 -> x8, matrix products: 9.72 us -> 37.3 us  [product_of(): lax.dot_general(jnp.concatenate(lefts, axis=0), jnp.concatenate(rights, a...]
    unnamed x32 -> x22, local copies, waits for them, and re-layouts: 12.4 us -> 0.05 us
    slice x9 -> x8, local copies, waits for them, and re-layouts: 3.54 us -> 5.59 us  [the longest x4 2.9 us: to_corner(): upper = lax.ppermute(by_y[:self.cut], 'req', self.x_perm)]
    all_to_all x1, starting transfers between devices: 3.97 us -> 5.84 us  [shards(): lax.all_to_all(outgoing.reshape(n_req, IMG_CAP, -1), 'req', split_axis=0,...]
    dynamic_slice x4 -> x6, local copies, waits for them, and re-layouts: 2.07 us -> 3.24 us  [the longest x3 1.87 us: shards(): plane = ring.preceding[plane]]
  transfers between devices with their start and end apart: 23 -> 23, of which waited for: 7 -> 9; matrix products, arithmetic and copies ran while one was open for 37% -> 37% of each run, Pallas kernels for 0% -> 0%
where the time goes in v2:
time: 138 us; the launch traced here: 137 us
  matrix products  45 us (33%)
  waiting for transfers between devices  32.7 us (24%)
  starting transfers between devices  32.1 us (23%)
  local copies, waits for them, and re-layouts  9.81 us (7%)
  other arithmetic  9.08 us (7%)
  between operations  6.18 us (4%)
  blocking collectives  2.44 us (2%)
    dot_general x8, matrix products, product_of(): lax.dot_general(jnp.concatenate(lefts, axis=0), jnp.concatenate(rights, a...  37.3 us
    ppermute x3, waiting for transfers between devices, along_line(): return lax.ppermute(block, 'req', self.line_perm)  12.4 us
    ppermute x4, waiting for transfers between devices, to_sides(): lax.ppermute(block, 'req', self.y_perm)  11.3 us
    ppermute x4, starting transfers between devices, to_sides(): lax.ppermute(block, 'req', self.x_perm)  6.49 us
    ppermute x4, waiting for transfers between devices, to_corner(): upper = lax.ppermute(by_y[:self.cut], 'req', self.x_perm)  6 us
    dot_general x1, matrix products, shards(): jnp.einsum('mkf,kfd->md', grouped, merge_weight, preferred_element_type=j...  5.88 us
    all_to_all x1, starting transfers between devices, shards(): lax.all_to_all(outgoing.reshape(n_req, IMG_CAP, -1), 'req', split_axis=0,...  5.84 us
    ppermute x3, starting transfers between devices, along_line(): return lax.ppermute(block, 'req', self.line_perm)  5.68 us
  transfers between devices with their start and end apart: 23, of which 9 were waited for; matrix products, arithmetic and copies ran while one was open for 37% of the time, Pallas kernels for 0%

profile of v2, /device:TPU:0, one launch (start us, length us, event | category | flops | bytes accessed | tf_op | source)
XLA Modules:
  0.0 137.3 jit_solution(17536521141065963247)
XLA Ops:
  0.0 2.9 %collective-permute-start.1 = (bf16[104,2496]{1,0:T(8,128)(2,1)}, bf16[104,2496]{1,0:T(8,128)(2,1)S(1)}, u32[]{:S(2)}, u32[]{:S(2)}) collective-permute-start(bf16[104,2496]{1,0:T(8,128)(2,1)} %param.16), channel_id=1, source_target_pairs={{0,2},{2,0},{4,6},{6,4},{8,10},{10,8},{12,14},{14,12},{16,18},{18,... | collective-permute-start | bytes 1557512 | tf_op jit(solution)/shard_map/ppermute | solution.py:73
  2.9 1.6 %collective-permute-start = (bf16[104,2496]{1,0:T(8,128)(2,1)}, bf16[104,2496]{1,0:T(8,128)(2,1)}, u32[]{:S(2)}, u32[]{:S(2)}) collective-permute-start(bf16[104,2496]{1,0:T(8,128)(2,1)} %param.16), channel_id=1, source_target_pairs={{0,8},{2,10},{4,12},{6,14},{8,24},{10,26},{12,28},{14,30},{16,0},{... | collective-permute-start | bytes 1557512 | tf_op jit(solution)/shard_map/ppermute | solution.py:70
  4.5 1.5 %collective-permute-start.2 = (bf16[104,2496]{1,0:T(8,128)(2,1)}, bf16[104,2496]{1,0:T(8,128)(2,1)}, u32[]{:S(2)}, u32[]{:S(2)}) collective-permute-start(bf16[104,2496]{1,0:T(8,128)(2,1)} %param.16), channel_id=1, source_target_pairs={{0,4},{2,6},{4,0},{6,2},{8,12},{10,14},{12,8},{14,10},{16,20},{18,... | collective-permute-start | bytes 1557512 | tf_op jit(solution)/shard_map/ppermute | solution.py:73
  6.0 0.7 convert_bitcast_fusion
  6.7 1.5 %convert_reduce_fusion = (f32[448]{0:T(512)S(1)}, f32[448]{0:T(512)S(1)}) fusion(bf16[448,832]{1,0:T(8,128)(2,1)} %param.10), kind=kLoop, calls=%fused_computation.7 | loop fusion | flops 1490048 | bytes 749056 | tf_op jit(solution)/shard_map/reduce_sum | solution.py:111
  8.2 0.7 convert_element_type.47
  8.9 0.7 convert_element_type.48
  9.6 2.4 %all-reduce = (f32[448]{0:T(512)S(1)}, f32[448]{0:T(512)S(1)}) all-reduce(f32[448]{0:T(512)S(1)} %get-tuple-element.32, f32[448]{0:T(512)S(1)} %get-tuple-element.31), channel_id=1, replica_groups=mesh['req'=16,'tp'=2] {'tp'}, use_global_device_ids=true, to_apply=%region_5.6 | all-reduce | flops 896 | bytes 7168 | tf_op jit(solution)/shard_map/psum | solution.py:113
  12.0 1.5 %fusion.3 = bf16[448,832]{1,0:T(8,128)(2,1)S(1)} fusion(bf16[448,832]{1,0:T(8,128)(2,1)} %param.10, f32[832]{0:T(1024)S(1)} %convert_element_type.48, f32[832]{0:T(1024)S(1)} %convert_element_type.47, f32[448]{0:T(512)S(1)} %get-tuple-element.62, f32[448]{0:T(512)S(1)} %get-tuple-element.61), kind=kLoop, calls=%fused_computation.11 | loop fusion | flops 2236416 | bytes 1501184 | tf_op jit(solution)/shard_map/convert_element_type | solution.py:121
  13.5 1.7 %collective-permute-done.1 = bf16[104,2496]{1,0:T(8,128)(2,1)S(1)} collective-permute-done((bf16[104,2496]{1,0:T(8,128)(2,1)}, bf16[104,2496]{1,0:T(8,128)(2,1)S(1)}, u32[]{:S(2)}, u32[]{:S(2)}) %collective-permute-start.1) | collective-permute-done | bytes 519200 | tf_op jit(solution)/shard_map/ppermute | solution.py:73
  15.2 2.5 %collective-permute-done = bf16[104,2496]{1,0:T(8,128)(2,1)} collective-permute-done((bf16[104,2496]{1,0:T(8,128)(2,1)}, bf16[104,2496]{1,0:T(8,128)(2,1)}, u32[]{:S(2)}, u32[]{:S(2)}) %collective-permute-start) | collective-permute-done | bytes 519200 | tf_op jit(solution)/shard_map/ppermute | solution.py:70
  17.7 0.4 collective-permute-done.2
  18.1 0.2 reshape.70
  18.3 2.6 %collective-permute-start.3 = (bf16[104,2496]{1,0:T(8,128)(2,1)}, bf16[104,2496]{1,0:T(8,128)(2,1)}, u32[]{:S(2)}, u32[]{:S(2)}) collective-permute-start(bf16[104,2496]{1,0:T(8,128)(2,1)} %collective-permute-done), channel_id=1, source_target_pairs={{0,8},{2,10},{4,12},{6,14},{8,24},{10,26},{12,28},{14,30},{16,0},{... | collective-permute-start | bytes 1557512 | tf_op jit(solution)/shard_map/ppermute | solution.py:70
  21.0 5.9 %convolution_bitcast_fusion = f32[112,1664]{1,0:T(8,128)S(1)} fusion(bf16[4,832,1664]{2,1,0:T(8,128)(2,1)} %param.13, bf16[112,4,832]{2,1,0:T(4,128)(2,1)S(1)} %reshape.70), kind=kOutput, calls=%fused_computation.4 | convolution fusion | flops 1240465408 | bytes 12566528 | tf_op jit(solution)/shard_map/mkf,kfd->md/dot_general | solution.py:129
  26.9 5.0 %collective-permute-done.3 = bf16[104,2496]{1,0:T(8,128)(2,1)} collective-permute-done((bf16[104,2496]{1,0:T(8,128)(2,1)}, bf16[104,2496]{1,0:T(8,128)(2,1)}, u32[]{:S(2)}, u32[]{:S(2)}) %collective-permute-start.3) | collective-permute-done | bytes 519200 | tf_op jit(solution)/shard_map/ppermute | solution.py:70
  32.7 1.2 collective-permute-done.4
  34.1 1.1 convolution_convert_fusion
  35.1 5.8 %all-to-all-start = ((bf16[16,16,896]{2,1,0:T(8,128)(2,1)}), bf16[16,16,896]{2,1,0:T(8,128)(2,1)S(1)}, u32[]{:S(2)}, u32[]{:S(2)}) async-start(bf16[16,16,896]{2,1,0:T(8,128)(2,1)} %bitcast.3), calls=%async_computation | async-start | bytes 917504 | tf_op jit(solution)/shard_map/all_to_all | solution.py:155
  41.1 2.0 %collective-permute-start.7 = (bf16[104,2496]{1,0:T(8,128)(2,1)}, bf16[104,2496]{1,0:T(8,128)(2,1)}, u32[]{:S(2)}, u32[]{:S(2)}) collective-permute-start(bf16[104,2496]{1,0:T(8,128)(2,1)} %collective-permute-done), channel_id=1, source_target_pairs={{0,4},{2,6},{4,0},{6,2},{8,12},{10,14},{12,8},{14,10},{16,20},{18,... | collective-permute-start | bytes 1557512 | tf_op jit(solution)/shard_map/ppermute | solution.py:73
  43.1 1.5 %collective-permute-start.6 = (bf16[104,2496]{1,0:T(8,128)(2,1)}, bf16[104,2496]{1,0:T(8,128)(2,1)}, u32[]{:S(2)}, u32[]{:S(2)}) collective-permute-start(bf16[104,2496]{1,0:T(8,128)(2,1)} %collective-permute-done), channel_id=1, source_target_pairs={{0,2},{2,0},{4,6},{6,4},{8,10},{10,8},{12,14},{14,12},{16,18},{18,... | collective-permute-start | bytes 1557512 | tf_op jit(solution)/shard_map/ppermute | solution.py:73
  44.5 1.5 %collective-permute-start.5 = (bf16[104,2496]{1,0:T(8,128)(2,1)}, bf16[104,2496]{1,0:T(8,128)(2,1)}, u32[]{:S(2)}, u32[]{:S(2)}) collective-permute-start(bf16[104,2496]{1,0:T(8,128)(2,1)} %collective-permute-done.3), channel_id=1, source_target_pairs={{0,8},{2,10},{4,12},{6,14},{8,24},{10,26},{12,28},{14,30},{16,0},{... | collective-permute-start | bytes 1557512 | tf_op jit(solution)/shard_map/ppermute | solution.py:70
  46.0 0.7 dynamic_slice.82
  48.7 0.6 dynamic_slice.88
  50.9 0.7 dynamic_slice.94
  53.8 0.6 fusion.95
  54.5 1.0 slice.36
  55.4 0.7 slice.37
  56.1 0.6 collective-permute-start.13
  56.7 4.2 %collective-permute-done.7 = bf16[104,2496]{1,0:T(8,128)(2,1)} collective-permute-done((bf16[104,2496]{1,0:T(8,128)(2,1)}, bf16[104,2496]{1,0:T(8,128)(2,1)}, u32[]{:S(2)}, u32[]{:S(2)}) %collective-permute-start.7) | collective-permute-done | bytes 519200 | tf_op jit(solution)/shard_map/ppermute | solution.py:73
  60.9 4.9 %collective-permute-done.5 = bf16[104,2496]{1,0:T(8,128)(2,1)} collective-permute-done((bf16[104,2496]{1,0:T(8,128)(2,1)}, bf16[104,2496]{1,0:T(8,128)(2,1)}, u32[]{:S(2)}, u32[]{:S(2)}) %collective-permute-start.5) | collective-permute-done | bytes 519200 | tf_op jit(solution)/shard_map/ppermute | solution.py:70
  65.8 1.0 broadcast_select_fusion.1
  66.8 1.5 %collective-permute-start.11 = (bf16[104,2496]{1,0:T(8,128)(2,1)}, bf16[104,2496]{1,0:T(8,128)(2,1)}, u32[]{:S(2)}, u32[]{:S(2)}) collective-permute-start(bf16[104,2496]{1,0:T(8,128)(2,1)} %collective-permute-done.3), channel_id=1, source_target_pairs={{0,4},{2,6},{4,0},{6,2},{8,12},{10,14},{12,8},{14,10},{16,20},{18,... | collective-permute-start | bytes 1557512 | tf_op jit(solution)/shard_map/ppermute | solution.py:73
  68.3 1.5 %collective-permute-start.10 = (bf16[104,2496]{1,0:T(8,128)(2,1)}, bf16[104,2496]{1,0:T(8,128)(2,1)}, u32[]{:S(2)}, u32[]{:S(2)}) collective-permute-start(bf16[104,2496]{1,0:T(8,128)(2,1)} %collective-permute-done.3), channel_id=1, source_target_pairs={{0,2},{2,0},{4,6},{6,4},{8,10},{10,8},{12,14},{14,12},{16,18},{18,... | collective-permute-start | bytes 1557512 | tf_op jit(solution)/shard_map/ppermute | solution.py:73
  69.8 0.2 copy.27
  70.0 1.0 slice.38
  70.9 1.0 slice.39
  71.9 0.6 collective-permute-start.19
  72.7 0.6 collective-permute-start.18
  73.4 1.1 broadcast_select_fusion.3
  74.5 0.8 convert_select_fusion
  75.3 6.7 %collective-permute-done.11 = bf16[104,2496]{1,0:T(8,128)(2,1)} collective-permute-done((bf16[104,2496]{1,0:T(8,128)(2,1)}, bf16[104,2496]{1,0:T(8,128)(2,1)}, u32[]{:S(2)}, u32[]{:S(2)}) %collective-permute-start.11) | collective-permute-done | bytes 519200 | tf_op jit(solution)/shard_map/ppermute | solution.py:73
  82.0 1.5 %collective-permute-start.14 = (bf16[48,2496]{1,0:T(8,128)(2,1)S(1)}, bf16[48,2496]{1,0:T(8,128)(2,1)S(1)}, u32[]{:S(2)}, u32[]{:S(2)}) collective-permute-start(bf16[48,2496]{1,0:T(8,128)(2,1)S(1)} %slice.38), channel_id=1, source_target_pairs={{0,2},{2,0},{4,6},{6,4},{8,10},{10,8},{12,14},{14,12},{16,18},{18,... | collective-permute-start | bytes 718856 | tf_op jit(solution)/shard_map/ppermute | solution.py:76
  83.5 1.4 %collective-permute-start.15 = (bf16[56,2496]{1,0:T(8,128)(2,1)S(1)}, bf16[56,2496]{1,0:T(8,128)(2,1)S(1)}, u32[]{:S(2)}, u32[]{:S(2)}) collective-permute-start(bf16[56,2496]{1,0:T(8,128)(2,1)S(1)} %slice.39), channel_id=1, source_target_pairs={{0,4},{2,6},{4,0},{6,2},{8,12},{10,14},{12,8},{14,10},{16,20},{18,... | collective-permute-start | bytes 838664 | tf_op jit(solution)/shard_map/ppermute | solution.py:77
  85.0 0.3 multiply_reduce_fusion
  85.3 0.4 multiply_convert_fusion
  85.8 5.3 %fusion.11 = f32[512,2496]{0,1:T(8,128)} fusion(bf16[104,2496]{1,0:T(8,128)(2,1)} %collective-permute-done.7, bf16[104,2496]{1,0:T(8,128)(2,1)} %collective-permute-done.6, bf16[104,2496]{1,0:T(8,128)(2,1)} %collective-permute-done, bf16[104,512]{1,0:T(8,128)(2,1)S(1)} %get-tuple-element.52, bf16[104,512]{1,0:T(8,128)(2,1)S(1)} %get-tuple-element.53, ...), kind=kOutput, calls=%fused_computation.19 | convolution fusion | flops 803073024 | bytes 6988800 | tf_op jit(solution)/shard_map/dot_general | solution.py:208
  91.1 4.9 %fusion.5 = f32[512,2496]{0,1:T(8,128)} fusion(bf16[104,2496]{1,0:T(8,128)(2,1)} %collective-permute-done.2, bf16[104,2496]{1,0:T(8,128)(2,1)S(1)} %copy-done.5, bf16[104,2496]{1,0:T(8,128)(2,1)S(1)} %copy-done.9, bf16[104,512]{1,0:T(8,128)(2,1)S(1)} %get-tuple-element.55, bf16[104,512]{1,0:T(8,128)(2,1)S(1)} %get-tuple-element.56, ...), kind=kOutput, calls=%fused_computation.13 | convolution fusion | flops 803073024 | bytes 6988800 | tf_op jit(solution)/shard_map/dot_general | solution.py:208
  95.9 5.2 %fusion.17 = f32[512,2496]{0,1:T(8,128)} fusion(bf16[104,2496]{1,0:T(8,128)(2,1)} %collective-permute-done.11, bf16[104,2496]{1,0:T(8,128)(2,1)} %collective-permute-done.10, bf16[104,2496]{1,0:T(8,128)(2,1)} %collective-permute-done.3, bf16[104,512]{1,0:T(8,128)(2,1)S(1)} %get-tuple-element.49, bf16[104,512]{1,0:T(8,128)(2,1)S(1)} %get-tuple-element.50, ...), kind=kOutput, calls=%fused_computation.25 | convolution fusion | flops 803073024 | bytes 6988800 | tf_op jit(solution)/shard_map/dot_general | solution.py:208
  101.2 0.6 constant_dynamic-slice_fusion
  101.8 0.6 constant_dynamic-slice_fusion.1
  102.4 1.0 slice.40
  103.4 1.0 slice.41
  104.4 0.7 collective-permute-start.12
  105.1 1.4 %collective-permute-start.16 = (bf16[48,2496]{1,0:T(8,128)(2,1)S(1)}, bf16[48,2496]{1,0:T(8,128)(2,1)S(1)}, u32[]{:S(2)}, u32[]{:S(2)}) collective-permute-start(bf16[48,2496]{1,0:T(8,128)(2,1)S(1)} %slice.40), channel_id=1, source_target_pairs={{0,2},{2,0},{4,6},{6,4},{8,10},{10,8},{12,14},{14,12},{16,18},{18,... | collective-permute-start | bytes 718856 | tf_op jit(solution)/shard_map/ppermute | solution.py:76
  106.5 0.9 fusion.37
  107.4 6.0 %collective-permute-done.12 = bf16[48,2496]{1,0:T(8,128)(2,1)S(1)} collective-permute-done((bf16[48,2496]{1,0:T(8,128)(2,1)S(1)}, bf16[48,2496]{1,0:T(8,128)(2,1)S(1)}, u32[]{:S(2)}, u32[]{:S(2)}) %collective-permute-start.12) | collective-permute-done | bytes 239648 | tf_op jit(solution)/shard_map/ppermute | solution.py:76
  113.4 0.6 collective-permute-start.17
  114.0 1.8 %fusion.33 = f32[512,2496]{0,1:T(8,128)S(1)} fusion(bf16[56,2496]{1,0:T(8,128)(2,1)} %collective-permute-done.13, bf16[48,2496]{1,0:T(8,128)(2,1)S(1)} %collective-permute-done.12, bf16[56,512]{1,0:T(8,128)(2,1)S(1)} %get-tuple-element.44, bf16[48,512]{1,0:T(8,128)(2,1)S(1)} %get-tuple-element.40), kind=kOutput, calls=%fused_computation.44 | convolution fusion | flops 267065344 | bytes 5737472 | tf_op jit(solution)/shard_map/dot_general | solution.py:208
  115.8 1.5 %collective-permute-start.20 = (bf16[48,2496]{1,0:T(8,128)(2,1)S(1)}, bf16[48,2496]{1,0:T(8,128)(2,1)S(1)}, u32[]{:S(2)}, u32[]{:S(2)}) collective-permute-start(bf16[48,2496]{1,0:T(8,128)(2,1)S(1)} %slice.46), channel_id=1, source_target_pairs={{0,2},{2,0},{4,6},{6,4},{8,10},{10,8},{12,14},{14,12},{16,18},{18,... | collective-permute-start | bytes 718856 | tf_op jit(solution)/shard_map/ppermute | solution.py:76
  117.4 0.6 collective-permute-start.21
  118.0 4.8 %fusion.23 = f32[512,2496]{0,1:T(8,128)} fusion(bf16[104,2496]{1,0:T(8,128)(2,1)S(1)} %collective-permute-done.19, bf16[104,2496]{1,0:T(8,128)(2,1)S(1)} %collective-permute-done.18, bf16[104,2496]{1,0:T(8,128)(2,1)} %collective-permute-done.5, bf16[104,512]{1,0:T(8,128)(2,1)S(1)} %get-tuple-element.46, bf16[104,512]{1,0:T(8,128)(2,1)S(1)} %get-tuple-element.47, ...), kind=kOutput, calls=%fused_computation.31 | convolution fusion | flops 803073024 | bytes 6988800 | tf_op jit(solution)/shard_map/dot_general | solution.py:208
  122.8 3.2 %fusion.41 = f32[512,2496]{0,1:T(8,128)} fusion(bf16[56,2496]{1,0:T(8,128)(2,1)S(1)} %collective-permute-done.17, bf16[48,2496]{1,0:T(8,128)(2,1)S(1)} %collective-permute-done.16, bf16[56,512]{1,0:T(8,128)(2,1)S(1)} %get-tuple-element.42, bf16[48,512]{1,0:T(8,128)(2,1)S(1)} %get-tuple-element.38), kind=kOutput, calls=%fused_computation.52 | convolution fusion | flops 267065344 | bytes 5737472 | tf_op jit(solution)/shard_map/dot_general | solution.py:208
  126.0 11.2 %select_convert_fusion = bf16[512,2496]{0,1:T(8,128)(2,1)} fusion(f32[512,2496]{0,1:T(8,128)} %fusion.23, f32[512,2496]{0,1:T(8,128)} %fusion.41, f32[512,2496]{0,1:T(8,128)} %fusion.17, f32[512,2496]{0,1:T(8,128)S(1)} %fusion.37, f32[512,2496]{0,1:T(8,128)} %fusion.11, f32[512,2496]{0,1:T(8,128)} %fusion.5, f32[512,2496]{0,1:T(8,128)S(1)} %fusion.33, ...), kind=kOutput, calls=%fused_computation | convolution fusion | flops 278566912 | bytes 38964736 | tf_op jit(solution)/shard_map/dot_general | solution.py:208
  (58 shorter events, 1.6 us)
Async XLA Ops:
  0.0 15.2 %collective-permute-start.1 = (bf16[104,2496]{1,0:T(8,128)(2,1)}, bf16[104,2496]{1,0:T(8,128)(2,1)S(1)}, u32[]{:S(2)}, u32[]{:S(2)}) collective-permute-start(bf16[104,2496]{1,0:T(8,128)(2,1)} %param.16), channel_id=1, source_target_pairs={{0,2},{2,0},{4,6},{6,4},{8,10},{10,8},{12,14},{14,12},{16,18},{18,... | collective-permute-start | bytes 1557512 | tf_op jit(solution)/shard_map/ppermute | solution.py:73
  2.9 14.8 %collective-permute-start = (bf16[104,2496]{1,0:T(8,128)(2,1)}, bf16[104,2496]{1,0:T(8,128)(2,1)}, u32[]{:S(2)}, u32[]{:S(2)}) collective-permute-start(bf16[104,2496]{1,0:T(8,128)(2,1)} %param.16), channel_id=1, source_target_pairs={{0,8},{2,10},{4,12},{6,14},{8,24},{10,26},{12,28},{14,30},{16,0},{... | collective-permute-start | bytes 1557512 | tf_op jit(solution)/shard_map/ppermute | solution.py:70
  4.5 13.6 %collective-permute-start.2 = (bf16[104,2496]{1,0:T(8,128)(2,1)}, bf16[104,2496]{1,0:T(8,128)(2,1)}, u32[]{:S(2)}, u32[]{:S(2)}) collective-permute-start(bf16[104,2496]{1,0:T(8,128)(2,1)} %param.16), channel_id=1, source_target_pairs={{0,4},{2,6},{4,0},{6,2},{8,12},{10,14},{12,8},{14,10},{16,20},{18,... | collective-permute-start | bytes 1557512 | tf_op jit(solution)/shard_map/ppermute | solution.py:73
  15.2 40.2 %copy-start.4 = (bf16[104,2496]{1,0:T(8,128)(2,1)}, bf16[104,2496]{1,0:T(8,128)(2,1)S(1)}, u32[]{:S(2)}) copy-start(bf16[104,2496]{1,0:T(8,128)(2,1)S(1)} %collective-permute-done.1) | copy-start | bytes 1557508
  18.3 13.6 %collective-permute-start.3 = (bf16[104,2496]{1,0:T(8,128)(2,1)}, bf16[104,2496]{1,0:T(8,128)(2,1)}, u32[]{:S(2)}, u32[]{:S(2)}) collective-permute-start(bf16[104,2496]{1,0:T(8,128)(2,1)} %collective-permute-done), channel_id=1, source_target_pairs={{0,8},{2,10},{4,12},{6,14},{8,24},{10,26},{12,28},{14,30},{16,0},{... | collective-permute-start | bytes 1557512 | tf_op jit(solution)/shard_map/ppermute | solution.py:70
  26.8 14.2 %copy-start = (bf16[512,832]{0,1:T(8,128)(2,1)S(1)}, bf16[512,832]{0,1:T(8,128)(2,1)}, u32[]{:S(2)}) copy-start(bf16[512,832]{0,1:T(8,128)(2,1)} %param.14) | copy-start | bytes 2555908
  26.9 19.1 %copy-start.10 = (s32[4]{0:T(128)S(1)}, s32[4]{0:T(128)}, u32[]{:S(2)}) copy-start(s32[4]{0:T(128)} %constant.153.clone) | copy-start | bytes 52
  26.9 26.7 %copy-start.6 = (bf16[1664]{0:T(1024)(128)(2,1)S(1)}, bf16[1664]{0:T(1024)(128)(2,1)}, u32[]{:S(2)}) copy-start(bf16[1664]{0:T(1024)(128)(2,1)} %param.15) | copy-start | bytes 9988
  26.9 26.9 %copy-start.8 = (s32[2]{0:T(128)S(1)}, s32[2]{0:T(128)}, u32[]{:S(2)}) copy-start(s32[2]{0:T(128)} %param.18) | copy-start | bytes 28
  32.1 1.8 %collective-permute-start.4 = (f32[112,832]{1,0:T(8,128)S(1)}, f32[112,832]{1,0:T(8,128)S(1)}, u32[]{:S(2)}, u32[]{:S(2)}) collective-permute-start(f32[112,832]{1,0:T(8,128)S(1)} %constant_dynamic-slice_fusion.20), channel_id=1, source_target_pairs={{0,1},{1,0},{2,3},{3,2},{4,5},{5,4},{6,7},{7,6},{8,9},{9,8},{10,11... | collective-permute-start | bytes 1118216 | tf_op jit(solution)/shard_map/ppermute | solution.py:21
  35.1 30.7 %all-to-all-start = ((bf16[16,16,896]{2,1,0:T(8,128)(2,1)}), bf16[16,16,896]{2,1,0:T(8,128)(2,1)S(1)}, u32[]{:S(2)}, u32[]{:S(2)}) async-start(bf16[16,16,896]{2,1,0:T(8,128)(2,1)} %bitcast.3), calls=%async_computation | async-start | bytes 917504 | tf_op jit(solution)/shard_map/all_to_all | solution.py:155
  41.0 24.8 %collective-permute-start.9 = (bf16[832,512]{1,0:T(8,128)(2,1)S(1)}, bf16[832,512]{1,0:T(8,128)(2,1)S(1)}, u32[]{:S(2)}, u32[]{:S(2)}) collective-permute-start(bf16[832,512]{1,0:T(8,128)(2,1)S(1)} %bitcast.20), channel_id=1, source_target_pairs={{0,1},{1,0},{2,3},{3,2},{4,5},{5,4},{6,7},{7,6},{8,9},{9,8},{10,11... | collective-permute-start | bytes 2555912 | tf_op jit(solution)/shard_map/ppermute | solution.py:21
  41.1 19.8 %collective-permute-start.7 = (bf16[104,2496]{1,0:T(8,128)(2,1)}, bf16[104,2496]{1,0:T(8,128)(2,1)}, u32[]{:S(2)}, u32[]{:S(2)}) collective-permute-start(bf16[104,2496]{1,0:T(8,128)(2,1)} %collective-permute-done), channel_id=1, source_target_pairs={{0,4},{2,6},{4,0},{6,2},{8,12},{10,14},{12,8},{14,10},{16,20},{18,... | collective-permute-start | bytes 1557512 | tf_op jit(solution)/shard_map/ppermute | solution.py:73
  43.1 17.8 %collective-permute-start.6 = (bf16[104,2496]{1,0:T(8,128)(2,1)}, bf16[104,2496]{1,0:T(8,128)(2,1)}, u32[]{:S(2)}, u32[]{:S(2)}) collective-permute-start(bf16[104,2496]{1,0:T(8,128)(2,1)} %collective-permute-done), channel_id=1, source_target_pairs={{0,2},{2,0},{4,6},{6,4},{8,10},{10,8},{12,14},{14,12},{16,18},{18,... | collective-permute-start | bytes 1557512 | tf_op jit(solution)/shard_map/ppermute | solution.py:73
  44.5 21.3 %collective-permute-start.5 = (bf16[104,2496]{1,0:T(8,128)(2,1)}, bf16[104,2496]{1,0:T(8,128)(2,1)}, u32[]{:S(2)}, u32[]{:S(2)}) collective-permute-start(bf16[104,2496]{1,0:T(8,128)(2,1)} %collective-permute-done.3), channel_id=1, source_target_pairs={{0,8},{2,10},{4,12},{6,14},{8,24},{10,26},{12,28},{14,30},{16,0},{... | collective-permute-start | bytes 1557512 | tf_op jit(solution)/shard_map/ppermute | solution.py:70
  56.1 57.8 %collective-permute-start.13 = (bf16[56,2496]{1,0:T(8,128)(2,1)}, bf16[56,2496]{1,0:T(8,128)(2,1)}, u32[]{:S(2)}, u32[]{:S(2)}) collective-permute-start(bf16[56,2496]{1,0:T(8,128)(2,1)} %slice.37), channel_id=1, source_target_pairs={{0,4},{2,6},{4,0},{6,2},{8,12},{10,14},{12,8},{14,10},{16,20},{18,... | collective-permute-start | bytes 838664 | tf_op jit(solution)/shard_map/ppermute | solution.py:77
  65.8 6.9 %collective-permute-start.8 = (bf16[256,832]{1,0:T(8,128)(2,1)S(1)}, bf16[256,832]{1,0:T(8,128)(2,1)}, u32[]{:S(2)}, u32[]{:S(2)}) collective-permute-start(bf16[256,832]{1,0:T(8,128)(2,1)S(1)} %bitcast.17), channel_id=1, source_target_pairs={{0,1},{1,0},{2,3},{3,2},{4,5},{5,4},{6,7},{7,6},{8,9},{9,8},{10,11... | collective-permute-start | bytes 1277960 | tf_op jit(solution)/shard_map/ppermute | solution.py:21
  66.8 7.6 %copy-start.1 = (bf16[832,512]{1,0:T(8,128)(2,1)S(1)}, bf16[832,512]{1,0:T(8,128)(2,1)}, u32[]{:S(2)}) copy-start(bf16[832,512]{1,0:T(8,128)(2,1)} %get-tuple-element.58) | copy-start | bytes 2555908
  66.8 15.2 %collective-permute-start.11 = (bf16[104,2496]{1,0:T(8,128)(2,1)}, bf16[104,2496]{1,0:T(8,128)(2,1)}, u32[]{:S(2)}, u32[]{:S(2)}) collective-permute-start(bf16[104,2496]{1,0:T(8,128)(2,1)} %collective-permute-done.3), channel_id=1, source_target_pairs={{0,4},{2,6},{4,0},{6,2},{8,12},{10,14},{12,8},{14,10},{16,20},{18,... | collective-permute-start | bytes 1557512 | tf_op jit(solution)/shard_map/ppermute | solution.py:73
  68.3 15.3 %collective-permute-start.10 = (bf16[104,2496]{1,0:T(8,128)(2,1)}, bf16[104,2496]{1,0:T(8,128)(2,1)}, u32[]{:S(2)}, u32[]{:S(2)}) collective-permute-start(bf16[104,2496]{1,0:T(8,128)(2,1)} %collective-permute-done.3), channel_id=1, source_target_pairs={{0,2},{2,0},{4,6},{6,4},{8,10},{10,8},{12,14},{14,12},{16,18},{18,... | collective-permute-start | bytes 1557512 | tf_op jit(solution)/shard_map/ppermute | solution.py:73
  71.9 43.9 %collective-permute-start.19 = (bf16[104,2496]{1,0:T(8,128)(2,1)}, bf16[104,2496]{1,0:T(8,128)(2,1)S(1)}, u32[]{:S(2)}, u32[]{:S(2)}) collective-permute-start(bf16[104,2496]{1,0:T(8,128)(2,1)} %collective-permute-done.5), channel_id=1, source_target_pairs={{0,4},{2,6},{4,0},{6,2},{8,12},{10,14},{12,8},{14,10},{16,20},{18,... | collective-permute-start | bytes 1557512 | tf_op jit(solution)/shard_map/ppermute | solution.py:73
  72.7 44.6 %collective-permute-start.18 = (bf16[104,2496]{1,0:T(8,128)(2,1)}, bf16[104,2496]{1,0:T(8,128)(2,1)S(1)}, u32[]{:S(2)}, u32[]{:S(2)}) collective-permute-start(bf16[104,2496]{1,0:T(8,128)(2,1)} %collective-permute-done.5), channel_id=1, source_target_pairs={{0,2},{2,0},{4,6},{6,4},{8,10},{10,8},{12,14},{14,12},{16,18},{18,... | collective-permute-start | bytes 1557512 | tf_op jit(solution)/shard_map/ppermute | solution.py:73
  82.0 22.3 %collective-permute-start.14 = (bf16[48,2496]{1,0:T(8,128)(2,1)S(1)}, bf16[48,2496]{1,0:T(8,128)(2,1)S(1)}, u32[]{:S(2)}, u32[]{:S(2)}) collective-permute-start(bf16[48,2496]{1,0:T(8,128)(2,1)S(1)} %slice.38), channel_id=1, source_target_pairs={{0,2},{2,0},{4,6},{6,4},{8,10},{10,8},{12,14},{14,12},{16,18},{18,... | collective-permute-start | bytes 718856 | tf_op jit(solution)/shard_map/ppermute | solution.py:76
  83.5 21.5 %collective-permute-start.15 = (bf16[56,2496]{1,0:T(8,128)(2,1)S(1)}, bf16[56,2496]{1,0:T(8,128)(2,1)S(1)}, u32[]{:S(2)}, u32[]{:S(2)}) collective-permute-start(bf16[56,2496]{1,0:T(8,128)(2,1)S(1)} %slice.39), channel_id=1, source_target_pairs={{0,4},{2,6},{4,0},{6,2},{8,12},{10,14},{12,8},{14,10},{16,20},{18,... | collective-permute-start | bytes 838664 | tf_op jit(solution)/shard_map/ppermute | solution.py:77
  85.8 5.3 %copy-start.5 = (bf16[104,2496]{1,0:T(8,128)(2,1)S(1)}, bf16[104,2496]{1,0:T(8,128)(2,1)}, u32[]{:S(2)}) copy-start(bf16[104,2496]{1,0:T(8,128)(2,1)} %copy-done.4) | copy-start | bytes 1557508
  85.8 5.3 %copy-start.9 = (bf16[104,2496]{1,0:T(8,128)(2,1)S(1)}, bf16[104,2496]{1,0:T(8,128)(2,1)}, u32[]{:S(2)}) copy-start(bf16[104,2496]{1,0:T(8,128)(2,1)} %param.16) | copy-start | bytes 1557508
  104.4 9.0 %collective-permute-start.12 = (bf16[48,2496]{1,0:T(8,128)(2,1)S(1)}, bf16[48,2496]{1,0:T(8,128)(2,1)S(1)}, u32[]{:S(2)}, u32[]{:S(2)}) collective-permute-start(bf16[48,2496]{1,0:T(8,128)(2,1)S(1)} %slice.36), channel_id=1, source_target_pairs={{0,2},{2,0},{4,6},{6,4},{8,10},{10,8},{12,14},{14,12},{16,18},{18,... | collective-permute-start | bytes 718856 | tf_op jit(solution)/shard_map/ppermute | solution.py:76
  105.1 17.8 %collective-permute-start.16 = (bf16[48,2496]{1,0:T(8,128)(2,1)S(1)}, bf16[48,2496]{1,0:T(8,128)(2,1)S(1)}, u32[]{:S(2)}, u32[]{:S(2)}) collective-permute-start(bf16[48,2496]{1,0:T(8,128)(2,1)S(1)} %slice.40), channel_id=1, source_target_pairs={{0,2},{2,0},{4,6},{6,4},{8,10},{10,8},{12,14},{14,12},{16,18},{18,... | collective-permute-start | bytes 718856 | tf_op jit(solution)/shard_map/ppermute | solution.py:76
  113.4 9.5 %collective-permute-start.17 = (bf16[56,2496]{1,0:T(8,128)(2,1)S(1)}, bf16[56,2496]{1,0:T(8,128)(2,1)S(1)}, u32[]{:S(2)}, u32[]{:S(2)}) collective-permute-start(bf16[56,2496]{1,0:T(8,128)(2,1)S(1)} %slice.41), channel_id=1, source_target_pairs={{0,4},{2,6},{4,0},{6,2},{8,12},{10,14},{12,8},{14,10},{16,20},{18,... | collective-permute-start | bytes 838664 | tf_op jit(solution)/shard_map/ppermute | solution.py:77
  115.8 10.2 %collective-permute-start.20 = (bf16[48,2496]{1,0:T(8,128)(2,1)S(1)}, bf16[48,2496]{1,0:T(8,128)(2,1)S(1)}, u32[]{:S(2)}, u32[]{:S(2)}) collective-permute-start(bf16[48,2496]{1,0:T(8,128)(2,1)S(1)} %slice.46), channel_id=1, source_target_pairs={{0,2},{2,0},{4,6},{6,4},{8,10},{10,8},{12,14},{14,12},{16,18},{18,... | collective-permute-start | bytes 718856 | tf_op jit(solution)/shard_map/ppermute | solution.py:76
  117.4 8.6 %collective-permute-start.21 = (bf16[56,2496]{1,0:T(8,128)(2,1)S(1)}, bf16[56,2496]{1,0:T(8,128)(2,1)S(1)}, u32[]{:S(2)}, u32[]{:S(2)}) collective-permute-start(bf16[56,2496]{1,0:T(8,128)(2,1)S(1)} %slice.47), channel_id=1, source_target_pairs={{0,4},{2,6},{4,0},{6,2},{8,12},{10,14},{12,8},{14,10},{16,20},{18,... | collective-permute-start | bytes 838664 | tf_op jit(solution)/shard_map/ppermute | solution.py:77
  122.8 3.2 %copy-start.2 = (bf16[56,512]{1,0:T(8,128)(2,1)S(1)}, bf16[56,512]{1,0:T(8,128)(2,1)}, u32[]{:S(2)}) copy-start(bf16[56,512]{1,0:T(8,128)(2,1)} %get-tuple-element.41) | copy-start | bytes 172036
  122.8 3.2 %copy-start.3 = (bf16[48,512]{1,0:T(8,128)(2,1)S(1)}, bf16[48,512]{1,0:T(8,128)(2,1)}, u32[]{:S(2)}) copy-start(bf16[48,512]{1,0:T(8,128)(2,1)} %get-tuple-element.37) | copy-start | bytes 147460
  122.8 3.2 %copy-start.7 = (pred[512]{0:T(512)(128)(4,1)S(1)}, pred[512]{0:T(512)(128)(4,1)}, u32[]{:S(2)}) copy-start(pred[512]{0:T(512)(128)(4,1)} %fusion.95) | copy-start | bytes 1540

commit v3 on v1

--- a/solution.py
+++ b/solution.py
@@ -2,7 +2,10 @@
 
 import jax
 import jax.numpy as jnp
+import numpy as np
 from jax import lax
+from jax.experimental import pallas as pl
+from jax.experimental.pallas import tpu as pltpu
 from jax.sharding import PartitionSpec as P
 
 DV = 1664
@@ -50,29 +53,92 @@
     return total
 
 
-def weight_groups(weight, n_req):
+def tie(*values):
+    return lax.optimization_barrier(values)
+
+
+def ring_tables(n_req):
     lines = n_req // 4
     order = folded_ring(lines)
     following = {order[i]: order[(i + 1) % lines] for i in range(lines)}
     line_perm = [(z * 4 + p, following[z] * 4 + p) for z in range(lines) for p in range(4)]
-    x_perm = [(i, i ^ 1) for i in range(n_req)]
-    y_perm = [(i, i ^ 2) for i in range(n_req)]
-    preceding = jnp.array([order[order.index(z) - 1] for z in range(lines)], jnp.int32)
-    plane = lax.axis_index("req") // 4
-    rows = weight.shape[0]
-    cut = rows // 16 * 8
-    held = weight
-    groups = []
-    for step in range(lines):
-        by_x = lax.ppermute(held, "req", x_perm)
-        by_y = lax.ppermute(held, "req", y_perm)
-        upper = lax.ppermute(by_y[:cut], "req", x_perm)
-        lower = lax.ppermute(by_x[cut:], "req", y_perm)
-        groups.append((plane, [(0, held), (1, by_x), (2, by_y), (3, upper, lower)]))
-        if step < lines - 1:
-            held = lax.ppermute(held, "req", line_perm)
-            plane = preceding[plane]
-    return groups
+    table = np.zeros((n_req, n_req), np.int32)
+    for index in range(n_req):
+        for step in range(lines):
+            z = order[(order.index(index // 4) - step) % lines]
+            for flip in range(4):
+                table[index, step * 4 + flip] = z * 4 + ((index % 4) ^ flip)
+    return lines, line_perm, table
+
+
+def multiply(order, scaled, pieces, extra=None, total=None, keep=None):
+    columns = pieces[0][2].shape[1]
+    positions = scaled.shape[2]
+    tile = 640 if columns > 640 else columns
+    spec = [(slot, first, block.shape[0]) for slot, first, block in pieces]
+
+    def body(order_ref, scaled_ref, *refs):
+        refs = list(refs)
+        out_ref = refs.pop()
+        value = None
+        if total is not None:
+            value = refs.pop(0)[...]
+        if keep is not None:
+            keep_ref = refs.pop(0)
+        if extra is not None:
+            value_part = lax.dot_general(
+                refs.pop(0)[...],
+                refs.pop(0)[...],
+                (((0,), (0,)), ((), ())),
+                preferred_element_type=jnp.float32,
+            )
+            value = value_part if value is None else value + value_part
+        for (slot, first, count), ref in zip(spec, refs):
+            value_part = lax.dot_general(
+                ref[...],
+                scaled_ref[order_ref[slot], pl.ds(first, count), :],
+                (((0,), (0,)), ((), ())),
+                preferred_element_type=jnp.float32,
+            )
+            value = value_part if value is None else value + value_part
+        if keep is not None:
+            value = jnp.where(keep_ref[...] > 0, value, 0.0)
+        out_ref[...] = value.astype(out_ref.dtype)
+
+    operands = [scaled]
+    specs = [pl.BlockSpec(scaled.shape, lambda i, order_ref: (0, 0, 0))]
+    if total is not None:
+        operands.append(total)
+        specs.append(pl.BlockSpec((tile, positions), lambda i, order_ref: (i, 0)))
+    if keep is not None:
+        operands.append(keep)
+        specs.append(pl.BlockSpec(keep.shape, lambda i, order_ref: (0, 0)))
+    if extra is not None:
+        operands.extend(extra)
+        specs.append(pl.BlockSpec((extra[0].shape[0], tile), lambda i, order_ref: (0, i)))
+        specs.append(pl.BlockSpec(extra[1].shape, lambda i, order_ref: (0, 0)))
+    for _, _, block in pieces:
+        operands.append(block)
+        specs.append(pl.BlockSpec((block.shape[0], tile), lambda i, order_ref: (0, i)))
+    depth = sum(count for _, _, count in spec) + (extra[0].shape[0] if extra is not None else 0)
+    return pl.pallas_call(
+        body,
+        out_shape=jax.ShapeDtypeStruct(
+            (columns, positions), jnp.float32 if keep is None else jnp.bfloat16
+        ),
+        grid_spec=pltpu.PrefetchScalarGridSpec(
+            num_scalar_prefetch=1,
+            grid=(pl.cdiv(columns, tile),),
+            in_specs=specs,
+            out_specs=pl.BlockSpec((tile, positions), lambda i, order_ref: (i, 0)),
+        ),
+        compiler_params=pltpu.CompilerParams(vmem_limit_bytes=40 << 20),
+        cost_estimate=pl.CostEstimate(
+            flops=2 * depth * columns * positions,
+            bytes_accessed=2 * depth * (columns + positions) + 8 * columns * positions,
+            transcendentals=0,
+        ),
+    )(order, *operands)
 
 
 def shards(
@@ -81,8 +147,45 @@
 ):
     row_count, width = text_rows.shape
     me = lax.axis_index("req")
-    groups = weight_groups(qkv_weight, n_req)
+    lines, line_perm, table = ring_tables(n_req)
+    x_perm = [(i, i ^ 1) for i in range(n_req)]
+    y_perm = [(i, i ^ 2) for i in range(n_req)]
+    rows = qkv_weight.shape[0]
+    direct = rows * 4 // 5 // 16 * 16
+    cut = direct // 32 * 16 or direct // 2
+    order = lax.dynamic_slice_in_dim(jnp.asarray(table), me, 1, 0).reshape(-1)
+
+    def along_line(block):
+        return lax.ppermute(block, "req", line_perm)
+
+    def to_sides(block):
+        return lax.ppermute(block, "req", x_perm), lax.ppermute(block, "req", y_perm)
+
+    def to_corner(by_x, by_y):
+        upper = lax.ppermute(by_y[:cut], "req", x_perm)
+        lower = lax.ppermute(by_x[cut:], "req", y_perm)
+        return upper, lower
+
+    held = [qkv_weight[:direct]]
+    sides = []
+    corners = []
+    held.append(along_line(held[0]))
+    sides.append(to_sides(held[0]))
+    gathered = lax.all_gather(qkv_weight[direct:], "req", axis=0, tiled=True)
     text_full = tp_gather(text_rows.T, n_tp, 0)
+
+    token_count = token_pos.shape[0]
+    target = lax.div(token_pos, row_count)
+    same = target[:, None] == target[None, :]
+    ids = jnp.arange(token_count, dtype=jnp.int32)
+    before = jnp.sum((same & (ids[None, :] < ids[:, None])).astype(jnp.int32), axis=1)
+    slot = target * IMG_CAP + before
+    slot_count = n_req * IMG_CAP
+    place = (
+        jnp.arange(slot_count, dtype=jnp.int32)[:, None] == slot[None, :]
+    ).astype(jnp.bfloat16)
+    code = lax.rem(token_pos, row_count) + 1
+    code_cols = jnp.stack([lax.div(code, 256), lax.rem(code, 256)], axis=1).astype(jnp.bfloat16)
 
     values = patches.astype(jnp.float32)
     sum_part = jnp.sum(values, axis=1)
@@ -96,29 +199,30 @@
         * ln_gain.astype(jnp.float32)
         + ln_bias.astype(jnp.float32)
     ).astype(jnp.bfloat16)
+
+    normed, held[1], sides[0], place, code_cols, order = tie(
+        normed, held[1], sides[0], place, code_cols, order
+    )
+    held.append(along_line(held[1]))
+    sides.append(to_sides(held[1]))
+    corners.append(to_corner(*sides[0]))
+
     grouped = normed.reshape(patches.shape[0] // 4, 4, patches.shape[1])
     partial_value = jnp.einsum(
         "mkf,kfd->md", grouped, merge_weight, preferred_element_type=jnp.float32
     )
     merged = tp_scatter_sum(partial_value, n_tp, 1).astype(jnp.bfloat16)
-
-    token_count = token_pos.shape[0]
-    target = token_pos // row_count
-    same = target[:, None] == target[None, :]
-    ids = jnp.arange(token_count, dtype=jnp.int32)
-    before = jnp.sum((same & (ids[None, :] < ids[:, None])).astype(jnp.int32), axis=1)
-    slot = target * IMG_CAP + before
-    slot_count = n_req * IMG_CAP
-    place = (
-        jnp.arange(slot_count, dtype=jnp.int32)[:, None] == slot[None, :]
-    ).astype(jnp.bfloat16)
-    code = token_pos % row_count + 1
-    code_cols = jnp.stack([code // 256, code % 256], axis=1).astype(jnp.bfloat16)
     padding = (-width - 2) % 128
     payload = jnp.concatenate(
         [merged, code_cols, jnp.zeros((token_count, padding), jnp.bfloat16)], axis=1
     )
     outgoing = jnp.dot(place, payload, preferred_element_type=jnp.float32).astype(jnp.bfloat16)
+
+    outgoing, held[2], sides[1], corners[0] = tie(outgoing, held[2], sides[1], corners[0])
+    held.append(along_line(held[2]))
+    sides.append(to_sides(held[2]))
+    corners.append(to_corner(*sides[1]))
+
     arrived = lax.all_to_all(
         outgoing.reshape(n_req, IMG_CAP, -1), "req", split_axis=0, concat_axis=0
     ).reshape(slot_count, -1)
@@ -140,30 +244,48 @@
         * norm_gain.astype(jnp.float32)[:, None]
     ).astype(jnp.bfloat16)
 
-    rows = qkv_weight.shape[0]
-    corner = me % 4
-    total = None
-    for plane, pieces in groups:
-        lefts, rights = [], []
-        for flip, *blocks in pieces:
-            start = (plane * 4 + (corner ^ flip)) * rows
-            rights.append(lax.dynamic_slice_in_dim(scaled, start, rows, 0))
-            lefts.extend(blocks)
-        part = lax.dot_general(
-            jnp.concatenate(lefts, axis=0),
-            jnp.concatenate(rights, axis=0),
-            (((0,), (0,)), ((), ())),
-            preferred_element_type=jnp.float32,
-        )
-        total = part if total is None else total + part
+    scaled, held[3], sides[2], corners[1], gathered = tie(
+        scaled, held[3], sides[2], corners[1], gathered
+    )
+    for step in range(3, lines):
+        if step < lines - 1:
+            held.append(along_line(held[step]))
+        sides.append(to_sides(held[step]))
+        corners.append(to_corner(*sides[step - 1]))
+    blocks = scaled.reshape(n_req, rows, row_count)
+    rest = blocks[:, direct:].reshape(-1, row_count)
+
+    def pieces_of(step):
+        by_x, by_y = sides[step]
+        return [(step * 4, 0, held[step]), (step * 4 + 1, 0, by_x), (step * 4 + 2, 0, by_y)]
+
+    def corner_of(step):
+        upper, lower = corners[step]
+        return [(step * 4 + 3, 0, upper), (step * 4 + 3, cut, lower)]
+
+    total = multiply(
+        order, blocks,
+        pieces_of(0) + corner_of(0) + pieces_of(1) + corner_of(1),
+        extra=(gathered, rest),
+    )
+    total, sides[-1], corners[-1] = tie(total, sides[-1], corners[-1])
+    corners.append(to_corner(*sides[-1]))
+    late = []
+    for step in range(2, lines - 1):
+        late += pieces_of(step) + corner_of(step)
+    total = multiply(order, blocks, late + pieces_of(lines - 1), total=total)
 
     position = me * row_count + jnp.arange(row_count, dtype=jnp.int32)
     request_ids = jnp.arange(text_len.shape[0], dtype=jnp.int32)
     limits = jnp.sum(
-        jnp.where((position // SEQ)[:, None] == request_ids[None, :], text_len[None, :], 0), axis=1
-    )
-    keep_row = position % SEQ < limits
-    return jnp.where(keep_row[None, :], total, 0.0).astype(jnp.bfloat16).T
+        jnp.where(
+            lax.div(position, SEQ)[None, :] == request_ids[:, None], text_len[:, None], 0
+        ),
+        axis=0,
+        keepdims=True,
+    )
+    keep = (lax.rem(position, SEQ)[None, :] < limits).astype(jnp.int32)
+    return multiply(order, blocks, corner_of(lines - 1), total=total, keep=keep).T
 
 
 def solution(mesh):

time: 118 us -> 145 us (1.23)
  Pallas kernels: 0 us -> 23.8 us
  matrix products: 17.7 us -> 9.38 us
  between operations: 6.24 us -> 13.7 us
  waiting for transfers between devices: 31.5 us -> 38.1 us
  local copies, waits for them, and re-layouts: 20.2 us -> 15.9 us
  starting transfers between devices: 29.3 us -> 31.2 us
    pallas_call x0 -> x3, Pallas kernels: none -> 23.8 us  [multiply(): pl.pallas_call(body, out_shape=jax.ShapeDtypeStruct((columns, positions),...]
    dot_general x4 -> x0, matrix products: 9.72 us -> none  [shards(): lax.dot_general(jnp.concatenate(lefts, axis=0), jnp.concatenate(rights, a...]
    ppermute x19, waiting for transfers between devices: 31.5 us -> 22.8 us  [the longest x4 12.7 us: to_corner(): lower = lax.ppermute(by_x[cut:], 'req', y_perm)]
    all_gather x0 -> x1, waiting for transfers between devices: none -> 7.37 us  [shards(): gathered = lax.all_gather(qkv_weight[direct:], 'req', axis=0, tiled=True)]
    all_to_all x1, waiting for transfers between devices: 0.01 us -> 6.51 us  [shards(): lax.all_to_all(outgoing.reshape(n_req, IMG_CAP, -1), 'req', split_axis=0,...]
    unnamed x32 -> x30, local copies, waits for them, and re-layouts: 12.4 us -> 9.56 us
    dynamic_slice x4 -> x0, local copies, waits for them, and re-layouts: 2.07 us -> none  [the longest x3 1.83 us: weight_groups(): plane = preceding[plane]]
    slice x8 -> x11, local copies, waits for them, and re-layouts: 3.44 us -> 4.99 us  [the longest x4 1.62 us: to_corner(): upper = lax.ppermute(by_y[:cut], 'req', x_perm)]
  transfers between devices with their start and end apart: 23 -> 24, of which waited for: 7 -> 8; matrix products, arithmetic and copies ran while one was open for 37% -> 13% of each run, Pallas kernels for 0% -> 14%
where the time goes in v3:
time: 145 us
  waiting for transfers between devices  38.1 us (26%)
  starting transfers between devices  31.2 us (22%)
  Pallas kernels  23.8 us (16%)
  local copies, waits for them, and re-layouts  15.9 us (11%)
  between operations  13.7 us (9%)
  other arithmetic  9.92 us (7%)
  matrix products  9.38 us (6%)
  blocking collectives  2.47 us (2%)
    pallas_call x3, Pallas kernels, multiply(): pl.pallas_call(body, out_shape=jax.ShapeDtypeStruct((columns, positions),...  23.8 us
    ppermute x4, waiting for transfers between devices, to_corner(): lower = lax.ppermute(by_x[cut:], 'req', y_perm)  12.7 us
    unnamed x30, local copies, waits for them, and re-layouts  9.56 us
    ppermute x4, waiting for transfers between devices, to_corner(): upper = lax.ppermute(by_y[:cut], 'req', x_perm)  8.5 us
    ppermute x3, starting transfers between devices, along_line(): return lax.ppermute(block, 'req', line_perm)  7.63 us
    all_gather x1, waiting for transfers between devices, shards(): gathered = lax.all_gather(qkv_weight[direct:], 'req', axis=0, tiled=True)  7.37 us
    all_to_all x1, waiting for transfers between devices, shards(): lax.all_to_all(outgoing.reshape(n_req, IMG_CAP, -1), 'req', split_axis=0,...  6.51 us
    ppermute x4, starting transfers between devices, to_sides(): lax.ppermute(block, 'req', y_perm)  5.98 us
  transfers between devices with their start and end apart: 24, of which 8 were waited for; matrix products, arithmetic and copies ran while one was open for 13% of the time, Pallas kernels for 14%

profile of v3, /device:TPU:0, one launch (start us, length us, event | category | flops | bytes accessed | tf_op | source)
XLA Modules:
  0.0 144.6 jit_solution(7075832918373224008)
XLA Ops:
  6.5 1.0 slice.42.refs_2_
  7.6 3.1 %collective-permute-start = (bf16[80,2496]{1,0:T(8,128)(2,1)S(1)}, bf16[80,2496]{1,0:T(8,128)(2,1)S(1)}, u32[]{:S(2)}, u32[]{:S(2)}) collective-permute-start(bf16[80,2496]{1,0:T(8,128)(2,1)S(1)} %slice.42.refs_2_), channel_id=1, source_target_pairs={{0,8},{2,10},{4,12},{6,14},{8,24},{10,26},{12,28},{14,30},{16,0},{... | collective-permute-start | bytes 1198088 | tf_op jit(solution)/shard_map/ppermute | solution.py:159
  10.6 1.5 %collective-permute-start.1 = (bf16[80,2496]{1,0:T(8,128)(2,1)S(1)}, bf16[80,2496]{1,0:T(8,128)(2,1)S(1)}, u32[]{:S(2)}, u32[]{:S(2)}) collective-permute-start(bf16[80,2496]{1,0:T(8,128)(2,1)S(1)} %slice.42.refs_2_), channel_id=1, source_target_pairs={{0,2},{2,0},{4,6},{6,4},{8,10},{10,8},{12,14},{14,12},{16,18},{18,... | collective-permute-start | bytes 1198088 | tf_op jit(solution)/shard_map/ppermute | solution.py:162
  12.1 1.5 %collective-permute-start.2 = (bf16[80,2496]{1,0:T(8,128)(2,1)S(1)}, bf16[80,2496]{1,0:T(8,128)(2,1)S(1)}, u32[]{:S(2)}, u32[]{:S(2)}) collective-permute-start(bf16[80,2496]{1,0:T(8,128)(2,1)S(1)} %slice.42.refs_2_), channel_id=1, source_target_pairs={{0,4},{2,6},{4,0},{6,2},{8,12},{10,14},{12,8},{14,10},{16,20},{18,... | collective-permute-start | bytes 1198088 | tf_op jit(solution)/shard_map/ppermute | solution.py:162
  13.7 1.5 %convert_reduce_fusion = (f32[448]{0:T(512)S(1)}, f32[448]{0:T(512)S(1)}) fusion(bf16[448,832]{1,0:T(8,128)(2,1)} %param.10), kind=kLoop, calls=%fused_computation.6 | loop fusion | flops 1490048 | bytes 749056 | tf_op jit(solution)/shard_map/reduce_sum | solution.py:191
  15.1 0.7 convert_bitcast_fusion.1
  15.8 0.2 convert_reduce_fusion.1
  16.0 2.5 %all-reduce = (f32[448]{0:T(512)S(1)}, f32[448]{0:T(512)S(1)}) all-reduce(f32[448]{0:T(512)S(1)} %get-tuple-element.56, f32[448]{0:T(512)S(1)} %get-tuple-element.55), channel_id=1, replica_groups=mesh['req'=16,'tp'=2] {'tp'}, use_global_device_ids=true, to_apply=%region_3.4 | all-reduce | flops 896 | bytes 7168 | tf_op jit(solution)/shard_map/psum | solution.py:193
  18.5 0.7 fusion.21.order_ref
  19.2 0.7 convert_element_type.47
  19.9 0.7 convert_element_type.48
  20.6 1.5 %fusion.3 = bf16[448,832]{1,0:T(8,128)(2,1)S(1)} fusion(bf16[448,832]{1,0:T(8,128)(2,1)} %param.10, f32[832]{0:T(1024)S(1)} %convert_element_type.48, f32[832]{0:T(1024)S(1)} %convert_element_type.47, f32[448]{0:T(512)S(1)} %get-tuple-element.68, f32[448]{0:T(512)S(1)} %get-tuple-element.67), kind=kLoop, calls=%fused_computation.10 | loop fusion | flops 2236416 | bytes 1501184 | tf_op jit(solution)/shard_map/convert_element_type | solution.py:201
  22.1 0.6 collective-permute-done.2.refs_4_
  22.8 0.2 reshape.83
  23.0 5.9 %convolution_bitcast_fusion = f32[112,1664]{1,0:T(8,128)S(1)} fusion(bf16[4,832,1664]{2,1,0:T(8,128)(2,1)} %param.13, bf16[112,4,832]{2,1,0:T(4,128)(2,1)S(1)} %reshape.83), kind=kOutput, calls=%fused_computation.3 | convolution fusion | flops 1240465408 | bytes 12566528 | tf_op jit(solution)/shard_map/mkf,kfd->md/dot_general | solution.py:211
  28.9 0.2 constant_dynamic-slice_fusion
  29.2 1.6 %slice.50 = bf16[24,2496]{1,0:T(8,128)(2,1)} slice(bf16[104,2496]{1,0:T(8,128)(2,1)} %param.16), slice={[80:104], [0:2496]} | slice | bytes 239616 | tf_op jit(solution)/shard_map/slice | solution.py:174
  30.8 0.6 collective-permute-start.7
  31.4 0.2 collective-permute-start.10
  31.7 2.6 %collective-permute-start.4 = (bf16[80,2496]{1,0:T(8,128)(2,1)S(1)}, bf16[80,2496]{1,0:T(8,128)(2,1)}, u32[]{:S(2)}, u32[]{:S(2)}) collective-permute-start(bf16[80,2496]{1,0:T(8,128)(2,1)S(1)} %collective-permute-done.refs_7_), channel_id=1, source_target_pairs={{0,8},{2,10},{4,12},{6,14},{8,24},{10,26},{12,28},{14,30},{16,0},{... | collective-permute-start | bytes 1198088 | tf_op jit(solution)/shard_map/ppermute | solution.py:159
  34.3 1.5 %collective-permute-start.5 = (bf16[80,2496]{1,0:T(8,128)(2,1)S(1)}, bf16[80,2496]{1,0:T(8,128)(2,1)S(1)}, u32[]{:S(2)}, u32[]{:S(2)}) collective-permute-start(bf16[80,2496]{1,0:T(8,128)(2,1)S(1)} %collective-permute-done.refs_7_), channel_id=1, source_target_pairs={{0,2},{2,0},{4,6},{6,4},{8,10},{10,8},{12,14},{14,12},{16,18},{18,... | collective-permute-start | bytes 1198088 | tf_op jit(solution)/shard_map/ppermute | solution.py:162
  35.8 0.1 copy.26
  36.0 1.9 %collective-permute-done.7.refs_5_ = bf16[32,2496]{1,0:T(8,128)(2,1)S(1)} collective-permute-done((bf16[32,2496]{1,0:T(8,128)(2,1)S(1)}, bf16[32,2496]{1,0:T(8,128)(2,1)S(1)}, u32[]{:S(2)}, u32[]{:S(2)}) %collective-permute-start.7) | collective-permute-done | bytes 159776 | tf_op jit(solution)/shard_map/ppermute | solution.py:165
  37.9 1.5 %collective-permute-start.6 = (bf16[80,2496]{1,0:T(8,128)(2,1)S(1)}, bf16[80,2496]{1,0:T(8,128)(2,1)S(1)}, u32[]{:S(2)}, u32[]{:S(2)}) collective-permute-start(bf16[80,2496]{1,0:T(8,128)(2,1)S(1)} %collective-permute-done.refs_7_), channel_id=1, source_target_pairs={{0,4},{2,6},{4,0},{6,2},{8,12},{10,14},{12,8},{14,10},{16,20},{18,... | collective-permute-start | bytes 1198088 | tf_op jit(solution)/shard_map/ppermute | solution.py:162
  39.4 0.5 collective-permute-start.8
  39.9 1.2 add_convert_fusion
  41.1 1.0 convolution_convert_fusion
  42.2 12.7 %collective-permute-done.8.refs_6_ = bf16[48,2496]{1,0:T(8,128)(2,1)S(1)} collective-permute-done((bf16[48,2496]{1,0:T(8,128)(2,1)S(1)}, bf16[48,2496]{1,0:T(8,128)(2,1)S(1)}, u32[]{:S(2)}, u32[]{:S(2)}) %collective-permute-start.8) | collective-permute-done | bytes 239648 | tf_op jit(solution)/shard_map/ppermute | solution.py:166
  54.9 5.4 %all-to-all-start = ((bf16[16,16,896]{2,1,0:T(8,128)(2,1)}), bf16[16,16,896]{2,1,0:T(8,128)(2,1)S(1)}, u32[]{:S(2)}, u32[]{:S(2)}) async-start(bf16[16,16,896]{2,1,0:T(8,128)(2,1)} %bitcast.29), calls=%async_computation | async-start | bytes 917504 | tf_op jit(solution)/shard_map/all_to_all | solution.py:226
  60.3 2.0 %collective-permute-start.11 = (bf16[80,2496]{1,0:T(8,128)(2,1)}, bf16[80,2496]{1,0:T(8,128)(2,1)}, u32[]{:S(2)}, u32[]{:S(2)}) collective-permute-start(bf16[80,2496]{1,0:T(8,128)(2,1)} %collective-permute-done.4.refs_1_), channel_id=1, source_target_pairs={{0,8},{2,10},{4,12},{6,14},{8,24},{10,26},{12,28},{14,30},{16,0},{... | collective-permute-start | bytes 1198088 | tf_op jit(solution)/shard_map/ppermute | solution.py:159
  62.2 1.5 %collective-permute-start.12 = (bf16[80,2496]{1,0:T(8,128)(2,1)}, bf16[80,2496]{1,0:T(8,128)(2,1)S(1)}, u32[]{:S(2)}, u32[]{:S(2)}) collective-permute-start(bf16[80,2496]{1,0:T(8,128)(2,1)} %collective-permute-done.4.refs_1_), channel_id=1, source_target_pairs={{0,2},{2,0},{4,6},{6,4},{8,10},{10,8},{12,14},{14,12},{16,18},{18,... | collective-permute-start | bytes 1198088 | tf_op jit(solution)/shard_map/ppermute | solution.py:162
  63.7 1.5 %collective-permute-start.13 = (bf16[80,2496]{1,0:T(8,128)(2,1)}, bf16[80,2496]{1,0:T(8,128)(2,1)}, u32[]{:S(2)}, u32[]{:S(2)}) collective-permute-start(bf16[80,2496]{1,0:T(8,128)(2,1)} %collective-permute-done.4.refs_1_), channel_id=1, source_target_pairs={{0,4},{2,6},{4,0},{6,2},{8,12},{10,14},{12,8},{14,10},{16,20},{18,... | collective-permute-start | bytes 1198088 | tf_op jit(solution)/shard_map/ppermute | solution.py:162
  65.2 0.7 slice.49
  65.8 0.6 collective-permute-start.15
  66.4 0.7 slice.48
  67.1 2.7 %broadcast_select_fusion.1 = (bf16[832,512]{1,0:T(8,128)(2,1)}, bf16[832,512]{1,0:T(8,128)(2,1)}) fusion(bf16[832,512]{1,0:T(8,128)(2,1)} %collective-permute-done.10, pred[]{:T(512)S(6)} %eq.72, bf16[512,832]{0,1:T(8,128)(2,1)} %param.14), kind=kLoop, calls=%fused_computation.17 | loop fusion | flops 851968 | bytes 3407873 | tf_op jit(solution)/shard_map/jit(_where)/select_n | solution.py:32
  69.8 6.5 %all-to-all-done = bf16[16,16,896]{2,1,0:T(8,128)(2,1)S(1)} async-done(((bf16[16,16,896]{2,1,0:T(8,128)(2,1)}), bf16[16,16,896]{2,1,0:T(8,128)(2,1)S(1)}, u32[]{:S(2)}, u32[]{:S(2)}) %all-to-all-start) | async-done | bytes 458784 | tf_op jit(solution)/shard_map/all_to_all | solution.py:226
  76.5 0.1 copy.30
  76.6 0.2 fusion.9
  76.8 1.3 collective-permute-done.9
  78.1 1.0 collective-permute-start.14
  79.2 2.4 %multiply_reduce_fusion = (f32[512]{0:T(512)S(1)}, f32[1664,512]{1,0:T(8,128)S(1)}) fusion(bf16[832,512]{1,0:T(8,128)(2,1)} %get-tuple-element.62, bf16[832,512]{1,0:T(8,128)(2,1)} %get-tuple-element.61, s32[256]{0:T(256)S(1)} %bitcast.33, bf16[256,832]{1,0:T(8,128)(2,1)S(1)} %get-tuple-element.64, bf16[256,832]{1,0:T(8,128)(2,1)S(1)} %get-tuple-element.63, ...), kind=kOutput, calls=%fused_computation.1 | convolution fusion | flops 444005888 | bytes 5967360 | tf_op jit(solution)/shard_map/dot_general | solution.py:234
  81.6 0.4 multiply_convert_fusion
  82.0 6.6 %collective-permute-done.14.refs_10_ = bf16[32,2496]{1,0:T(8,128)(2,1)S(1)} collective-permute-done((bf16[32,2496]{1,0:T(8,128)(2,1)}, bf16[32,2496]{1,0:T(8,128)(2,1)S(1)}, u32[]{:S(2)}, u32[]{:S(2)}) %collective-permute-start.14) | collective-permute-done | bytes 159776 | tf_op jit(solution)/shard_map/ppermute | solution.py:165
  88.6 0.7 copy-done.10
  89.3 1.0 collective-permute-done.11.refs_6_
  90.2 7.4 %all-gather.2.cloned.1.call-done.refs_0_ = bf16[384,2496]{1,0:T(8,128)(2,1)} async-done(((bf16[24,2496]{1,0:T(8,128)(2,1)}), bf16[384,2496]{1,0:T(8,128)(2,1)}) %all-gather.2.cloned.1.call-update) | async-done | bytes 1916944 | tf_op jit(solution)/shard_map/all_gather | solution.py:174
  97.6 0.6 collective-permute-start.16
  98.2 1.5 %collective-permute-start.17 = (bf16[80,2496]{1,0:T(8,128)(2,1)}, bf16[80,2496]{1,0:T(8,128)(2,1)S(1)}, u32[]{:S(2)}, u32[]{:S(2)}) collective-permute-start(bf16[80,2496]{1,0:T(8,128)(2,1)} %collective-permute-done.11.refs_6_), channel_id=1, source_target_pairs={{0,4},{2,6},{4,0},{6,2},{8,12},{10,14},{12,8},{14,10},{16,20},{18,... | collective-permute-start | bytes 1198088 | tf_op jit(solution)/shard_map/ppermute | solution.py:162
  99.8 0.6 collective-permute-start.19
  100.4 0.9 slice.52
  101.4 1.5 %collective-permute-start.18 = (bf16[32,2496]{1,0:T(8,128)(2,1)S(1)}, bf16[32,2496]{1,0:T(8,128)(2,1)S(1)}, u32[]{:S(2)}, u32[]{:S(2)}) collective-permute-start(bf16[32,2496]{1,0:T(8,128)(2,1)S(1)} %slice.52), channel_id=1, source_target_pairs={{0,2},{2,0},{4,6},{6,4},{8,10},{10,8},{12,14},{14,12},{16,18},{18,... | collective-permute-start | bytes 479240 | tf_op jit(solution)/shard_map/ppermute | solution.py:165
  102.9 1.5 %copy-done.1 = bf16[384,2496]{1,0:T(8,128)(2,1)S(1)} copy-done((bf16[384,2496]{1,0:T(8,128)(2,1)S(1)}, bf16[384,2496]{1,0:T(8,128)(2,1)}, u32[]{:S(2)}) %copy-start.1) | copy-done | bytes 1916952
  104.4 1.0 copy-done.3
  105.4 1.0 copy-done.5
  106.4 1.0 copy-done.7
  107.4 0.9 copy-done.9
  108.4 0.9 copy-done.11
  109.3 11.2 %shard_map.118.refs_0_ = f32[2496,512]{1,0:T(8,128)S(1)} custom-call(s32[16]{0:T(128)S(1)} %fusion.21.order_ref, bf16[16,104,512]{2,1,0:T(8,128)(2,1)S(1)} %bitcast.22, bf16[384,2496]{1,0:T(8,128)(2,1)S(1)} %copy-done.1, bf16[384,512]{1,0:T(8,128)(2,1)S(1)} %bitcast.25, bf16[80,2496]{1,0:T(8,128)(2,1)S(1)} %slice.42.refs_2_, ...), custom_call_target="tpu_custom_call" | custom-call | flops 2617245696 | bytes 16384000 | tf_op jit(solution)/shard_map/pallas_call | solution.py:124
  120.5 2.3 %copy-done = f32[2496,512]{1,0:T(8,128)} copy-done((f32[2496,512]{1,0:T(8,128)}, f32[2496,512]{1,0:T(8,128)S(1)}, u32[]{:S(2)}) %copy-start) | copy-done | bytes 5111832
  122.8 1.6 %collective-permute-start.21 = (bf16[48,2496]{1,0:T(8,128)(2,1)S(1)}, bf16[48,2496]{1,0:T(8,128)(2,1)S(1)}, u32[]{:S(2)}, u32[]{:S(2)}) collective-permute-start(bf16[48,2496]{1,0:T(8,128)(2,1)S(1)} %slice.55), channel_id=1, source_target_pairs={{0,4},{2,6},{4,0},{6,2},{8,12},{10,14},{12,8},{14,10},{16,20},{18,... | collective-permute-start | bytes 718856 | tf_op jit(solution)/shard_map/ppermute | solution.py:166
  124.4 0.6 collective-permute-start.20
  125.0 8.7 %shard_map.119.refs_0_ = f32[2496,512]{1,0:T(8,128)S(1)} custom-call(s32[16]{0:T(128)S(1)} %fusion.21.order_ref, bf16[16,104,512]{2,1,0:T(8,128)(2,1)S(1)} %bitcast.23, f32[2496,512]{1,0:T(8,128)} %copy-done, bf16[80,2496]{1,0:T(8,128)(2,1)} %collective-permute-done.4.refs_1_, bf16[80,2496]{1,0:T(8,128)(2,1)S(1)} %collective-permute-done.12.refs_2_, ...), custom_call_target="tpu_custom_call" | custom-call | flops 1431306240 | bytes 13592576 | tf_op jit(solution)/shard_map/pallas_call | solution.py:124
  133.8 3.9 %shard_map.120 = bf16[2496,512]{1,0:T(8,128)(2,1)} custom-call(s32[16]{0:T(128)S(1)} %fusion.21.order_ref, bf16[16,104,512]{2,1,0:T(8,128)(2,1)S(1)} %bitcast.24, f32[2496,512]{1,0:T(8,128)S(1)} %shard_map.119.refs_0_, s32[1,512]{1,0:T(1,128)S(1)} %compare_convert_fusion.refs_1_, bf16[32,2496]{1,0:T(8,128)(2,1)S(1)} %collective-permute-done.20.refs_2_, ...), custom_call_target="tpu_custom_call" | custom-call | flops 204472320 | bytes 10704896 | tf_op jit(solution)/shard_map/pallas_call | solution.py:124
  (62 shorter events, 0.8 us)
Async XLA Ops:
  6.5 91.1 %all-gather.2.cloned.1.call-start = ((), (), s32[]{:S(2)}) async-start(), calls=%async_computation.1 | async-start | bytes 2088960 | tf_op jit(solution)/shard_map/all_gather | solution.py:174
  7.6 14.5 %collective-permute-start = (bf16[80,2496]{1,0:T(8,128)(2,1)S(1)}, bf16[80,2496]{1,0:T(8,128)(2,1)S(1)}, u32[]{:S(2)}, u32[]{:S(2)}) collective-permute-start(bf16[80,2496]{1,0:T(8,128)(2,1)S(1)} %slice.42.refs_2_), channel_id=1, source_target_pairs={{0,8},{2,10},{4,12},{6,14},{8,24},{10,26},{12,28},{14,30},{16,0},{... | collective-permute-start | bytes 1198088 | tf_op jit(solution)/shard_map/ppermute | solution.py:159
  10.6 11.5 %collective-permute-start.1 = (bf16[80,2496]{1,0:T(8,128)(2,1)S(1)}, bf16[80,2496]{1,0:T(8,128)(2,1)S(1)}, u32[]{:S(2)}, u32[]{:S(2)}) collective-permute-start(bf16[80,2496]{1,0:T(8,128)(2,1)S(1)} %slice.42.refs_2_), channel_id=1, source_target_pairs={{0,2},{2,0},{4,6},{6,4},{8,10},{10,8},{12,14},{14,12},{16,18},{18,... | collective-permute-start | bytes 1198088 | tf_op jit(solution)/shard_map/ppermute | solution.py:162
  12.1 10.6 %collective-permute-start.2 = (bf16[80,2496]{1,0:T(8,128)(2,1)S(1)}, bf16[80,2496]{1,0:T(8,128)(2,1)S(1)}, u32[]{:S(2)}, u32[]{:S(2)}) collective-permute-start(bf16[80,2496]{1,0:T(8,128)(2,1)S(1)} %slice.42.refs_2_), channel_id=1, source_target_pairs={{0,4},{2,6},{4,0},{6,2},{8,12},{10,14},{12,8},{14,10},{16,20},{18,... | collective-permute-start | bytes 1198088 | tf_op jit(solution)/shard_map/ppermute | solution.py:162
  22.1 15.8 %copy-start.6 = (bf16[80,2496]{1,0:T(8,128)(2,1)}, bf16[80,2496]{1,0:T(8,128)(2,1)S(1)}, u32[]{:S(2)}) copy-start(bf16[80,2496]{1,0:T(8,128)(2,1)S(1)} %collective-permute-done.refs_7_) | copy-start | bytes 1198084
  22.8 8.0 %copy-start.2 = (bf16[80,2496]{1,0:T(8,128)(2,1)}, bf16[80,2496]{1,0:T(8,128)(2,1)S(1)}, u32[]{:S(2)}) copy-start(bf16[80,2496]{1,0:T(8,128)(2,1)S(1)} %collective-permute-done.2.refs_4_) | copy-start | bytes 1198084
  28.9 31.3 %copy-start.12 = (bf16[1664]{0:T(1024)(128)(2,1)S(1)}, bf16[1664]{0:T(1024)(128)(2,1)}, u32[]{:S(2)}) copy-start(bf16[1664]{0:T(1024)(128)(2,1)} %param.15) | copy-start | bytes 9988
  29.1 10.3 %collective-permute-start.3 = (f32[112,832]{1,0:T(8,128)S(1)}, f32[112,832]{1,0:T(8,128)}, u32[]{:S(2)}, u32[]{:S(2)}) collective-permute-start(f32[112,832]{1,0:T(8,128)S(1)} %constant_dynamic-slice_fusion), channel_id=1, source_target_pairs={{0,1},{1,0},{2,3},{3,2},{4,5},{5,4},{6,7},{7,6},{8,9},{9,8},{10,11... | collective-permute-start | bytes 1118216 | tf_op jit(solution)/shard_map/ppermute | solution.py:24
  30.8 7.1 %collective-permute-start.7 = (bf16[32,2496]{1,0:T(8,128)(2,1)S(1)}, bf16[32,2496]{1,0:T(8,128)(2,1)S(1)}, u32[]{:S(2)}, u32[]{:S(2)}) collective-permute-start(bf16[32,2496]{1,0:T(8,128)(2,1)S(1)} %slice.43), channel_id=1, source_target_pairs={{0,2},{2,0},{4,6},{6,4},{8,10},{10,8},{12,14},{14,12},{16,18},{18,... | collective-permute-start | bytes 479240 | tf_op jit(solution)/shard_map/ppermute | solution.py:165
  31.4 35.7 %collective-permute-start.10 = (bf16[832,512]{1,0:T(8,128)(2,1)}, bf16[832,512]{1,0:T(8,128)(2,1)}, u32[]{:S(2)}, u32[]{:S(2)}) collective-permute-start(bf16[832,512]{1,0:T(8,128)(2,1)} %bitcast.30), channel_id=1, source_target_pairs={{0,1},{1,0},{2,3},{3,2},{4,5},{5,4},{6,7},{7,6},{8,9},{9,8},{10,11... | collective-permute-start | bytes 2555912 | tf_op jit(solution)/shard_map/ppermute | solution.py:24
  31.7 23.1 %collective-permute-start.4 = (bf16[80,2496]{1,0:T(8,128)(2,1)S(1)}, bf16[80,2496]{1,0:T(8,128)(2,1)}, u32[]{:S(2)}, u32[]{:S(2)}) collective-permute-start(bf16[80,2496]{1,0:T(8,128)(2,1)S(1)} %collective-permute-done.refs_7_), channel_id=1, source_target_pairs={{0,8},{2,10},{4,12},{6,14},{8,24},{10,26},{12,28},{14,30},{16,0},{... | collective-permute-start | bytes 1198088 | tf_op jit(solution)/shard_map/ppermute | solution.py:159
  34.3 20.5 %collective-permute-start.5 = (bf16[80,2496]{1,0:T(8,128)(2,1)S(1)}, bf16[80,2496]{1,0:T(8,128)(2,1)S(1)}, u32[]{:S(2)}, u32[]{:S(2)}) collective-permute-start(bf16[80,2496]{1,0:T(8,128)(2,1)S(1)} %collective-permute-done.refs_7_), channel_id=1, source_target_pairs={{0,2},{2,0},{4,6},{6,4},{8,10},{10,8},{12,14},{14,12},{16,18},{18,... | collective-permute-start | bytes 1198088 | tf_op jit(solution)/shard_map/ppermute | solution.py:162
  37.9 16.9 %collective-permute-start.6 = (bf16[80,2496]{1,0:T(8,128)(2,1)S(1)}, bf16[80,2496]{1,0:T(8,128)(2,1)S(1)}, u32[]{:S(2)}, u32[]{:S(2)}) collective-permute-start(bf16[80,2496]{1,0:T(8,128)(2,1)S(1)} %collective-permute-done.refs_7_), channel_id=1, source_target_pairs={{0,4},{2,6},{4,0},{6,2},{8,12},{10,14},{12,8},{14,10},{16,20},{18,... | collective-permute-start | bytes 1198088 | tf_op jit(solution)/shard_map/ppermute | solution.py:162
  39.4 15.4 %collective-permute-start.8 = (bf16[48,2496]{1,0:T(8,128)(2,1)S(1)}, bf16[48,2496]{1,0:T(8,128)(2,1)S(1)}, u32[]{:S(2)}, u32[]{:S(2)}) collective-permute-start(bf16[48,2496]{1,0:T(8,128)(2,1)S(1)} %slice.44), channel_id=1, source_target_pairs={{0,4},{2,6},{4,0},{6,2},{8,12},{10,14},{12,8},{14,10},{16,20},{18,... | collective-permute-start | bytes 718856 | tf_op jit(solution)/shard_map/ppermute | solution.py:166
  54.8 5.4 %copy-start.8 = (bf16[48,2496]{1,0:T(8,128)(2,1)}, bf16[48,2496]{1,0:T(8,128)(2,1)S(1)}, u32[]{:S(2)}) copy-start(bf16[48,2496]{1,0:T(8,128)(2,1)S(1)} %collective-permute-done.8.refs_6_) | copy-start | bytes 718852
  54.8 15.0 %copy-start.4 = (bf16[80,2496]{1,0:T(8,128)(2,1)}, bf16[80,2496]{1,0:T(8,128)(2,1)S(1)}, u32[]{:S(2)}) copy-start(bf16[80,2496]{1,0:T(8,128)(2,1)S(1)} %collective-permute-done.6.refs_9_) | copy-start | bytes 1198084
  54.9 21.5 %all-to-all-start = ((bf16[16,16,896]{2,1,0:T(8,128)(2,1)}), bf16[16,16,896]{2,1,0:T(8,128)(2,1)S(1)}, u32[]{:S(2)}, u32[]{:S(2)}) async-start(bf16[16,16,896]{2,1,0:T(8,128)(2,1)} %bitcast.29), calls=%async_computation | async-start | bytes 917504 | tf_op jit(solution)/shard_map/all_to_all | solution.py:226
  60.3 30.0 %collective-permute-start.11 = (bf16[80,2496]{1,0:T(8,128)(2,1)}, bf16[80,2496]{1,0:T(8,128)(2,1)}, u32[]{:S(2)}, u32[]{:S(2)}) collective-permute-start(bf16[80,2496]{1,0:T(8,128)(2,1)} %collective-permute-done.4.refs_1_), channel_id=1, source_target_pairs={{0,8},{2,10},{4,12},{6,14},{8,24},{10,26},{12,28},{14,30},{16,0},{... | collective-permute-start | bytes 1198088 | tf_op jit(solution)/shard_map/ppermute | solution.py:159
  62.2 28.0 %collective-permute-start.12 = (bf16[80,2496]{1,0:T(8,128)(2,1)}, bf16[80,2496]{1,0:T(8,128)(2,1)S(1)}, u32[]{:S(2)}, u32[]{:S(2)}) collective-permute-start(bf16[80,2496]{1,0:T(8,128)(2,1)} %collective-permute-done.4.refs_1_), channel_id=1, source_target_pairs={{0,2},{2,0},{4,6},{6,4},{8,10},{10,8},{12,14},{14,12},{16,18},{18,... | collective-permute-start | bytes 1198088 | tf_op jit(solution)/shard_map/ppermute | solution.py:162
  63.7 26.6 %collective-permute-start.13 = (bf16[80,2496]{1,0:T(8,128)(2,1)}, bf16[80,2496]{1,0:T(8,128)(2,1)}, u32[]{:S(2)}, u32[]{:S(2)}) collective-permute-start(bf16[80,2496]{1,0:T(8,128)(2,1)} %collective-permute-done.4.refs_1_), channel_id=1, source_target_pairs={{0,4},{2,6},{4,0},{6,2},{8,12},{10,14},{12,8},{14,10},{16,20},{18,... | collective-permute-start | bytes 1198088 | tf_op jit(solution)/shard_map/ppermute | solution.py:162
  65.8 23.4 %collective-permute-start.15 = (bf16[48,2496]{1,0:T(8,128)(2,1)}, bf16[48,2496]{1,0:T(8,128)(2,1)}, u32[]{:S(2)}, u32[]{:S(2)}) collective-permute-start(bf16[48,2496]{1,0:T(8,128)(2,1)} %slice.49), channel_id=1, source_target_pairs={{0,4},{2,6},{4,0},{6,2},{8,12},{10,14},{12,8},{14,10},{16,20},{18,... | collective-permute-start | bytes 718856 | tf_op jit(solution)/shard_map/ppermute | solution.py:166
  76.3 1.8 %collective-permute-start.9 = (bf16[256,832]{1,0:T(8,128)(2,1)S(1)}, bf16[256,832]{1,0:T(8,128)(2,1)S(1)}, u32[]{:S(2)}, u32[]{:S(2)}) collective-permute-start(bf16[256,832]{1,0:T(8,128)(2,1)S(1)} %bitcast.26), channel_id=1, source_target_pairs={{0,1},{1,0},{2,3},{3,2},{4,5},{5,4},{6,7},{7,6},{8,9},{9,8},{10,11... | collective-permute-start | bytes 1277960 | tf_op jit(solution)/shard_map/ppermute | solution.py:24
  78.1 10.5 %collective-permute-start.14 = (bf16[32,2496]{1,0:T(8,128)(2,1)}, bf16[32,2496]{1,0:T(8,128)(2,1)S(1)}, u32[]{:S(2)}, u32[]{:S(2)}) collective-permute-start(bf16[32,2496]{1,0:T(8,128)(2,1)} %slice.48), channel_id=1, source_target_pairs={{0,2},{2,0},{4,6},{6,4},{8,10},{10,8},{12,14},{14,12},{16,18},{18,... | collective-permute-start | bytes 479240 | tf_op jit(solution)/shard_map/ppermute | solution.py:165
  81.6 18.0 %copy-start.13 = (s32[2]{0:T(128)S(1)}, s32[2]{0:T(128)}, u32[]{:S(2)}) copy-start(s32[2]{0:T(128)} %param.18) | copy-start | bytes 28
  88.6 0.7 copy-start.10
  97.6 25.2 %collective-permute-start.16 = (bf16[80,2496]{1,0:T(8,128)(2,1)}, bf16[80,2496]{1,0:T(8,128)(2,1)S(1)}, u32[]{:S(2)}, u32[]{:S(2)}) collective-permute-start(bf16[80,2496]{1,0:T(8,128)(2,1)} %collective-permute-done.11.refs_6_), channel_id=1, source_target_pairs={{0,2},{2,0},{4,6},{6,4},{8,10},{10,8},{12,14},{14,12},{16,18},{18,... | collective-permute-start | bytes 1198088 | tf_op jit(solution)/shard_map/ppermute | solution.py:162
  98.2 24.6 %collective-permute-start.17 = (bf16[80,2496]{1,0:T(8,128)(2,1)}, bf16[80,2496]{1,0:T(8,128)(2,1)S(1)}, u32[]{:S(2)}, u32[]{:S(2)}) collective-permute-start(bf16[80,2496]{1,0:T(8,128)(2,1)} %collective-permute-done.11.refs_6_), channel_id=1, source_target_pairs={{0,4},{2,6},{4,0},{6,2},{8,12},{10,14},{12,8},{14,10},{16,20},{18,... | collective-permute-start | bytes 1198088 | tf_op jit(solution)/shard_map/ppermute | solution.py:162
  99.8 23.0 %collective-permute-start.19 = (bf16[48,2496]{1,0:T(8,128)(2,1)S(1)}, bf16[48,2496]{1,0:T(8,128)(2,1)S(1)}, u32[]{:S(2)}, u32[]{:S(2)}) collective-permute-start(bf16[48,2496]{1,0:T(8,128)(2,1)S(1)} %slice.53), channel_id=1, source_target_pairs={{0,4},{2,6},{4,0},{6,2},{8,12},{10,14},{12,8},{14,10},{16,20},{18,... | collective-permute-start | bytes 718856 | tf_op jit(solution)/shard_map/ppermute | solution.py:166
  101.4 21.4 %collective-permute-start.18 = (bf16[32,2496]{1,0:T(8,128)(2,1)S(1)}, bf16[32,2496]{1,0:T(8,128)(2,1)S(1)}, u32[]{:S(2)}, u32[]{:S(2)}) collective-permute-start(bf16[32,2496]{1,0:T(8,128)(2,1)S(1)} %slice.52), channel_id=1, source_target_pairs={{0,2},{2,0},{4,6},{6,4},{8,10},{10,8},{12,14},{14,12},{16,18},{18,... | collective-permute-start | bytes 479240 | tf_op jit(solution)/shard_map/ppermute | solution.py:165
  102.9 1.5 %copy-start.1 = (bf16[384,2496]{1,0:T(8,128)(2,1)S(1)}, bf16[384,2496]{1,0:T(8,128)(2,1)}, u32[]{:S(2)}) copy-start(bf16[384,2496]{1,0:T(8,128)(2,1)} %all-gather.2.cloned.1.call-done.refs_0_) | copy-start | bytes 5750788
  104.4 1.0 copy-start.3
  105.4 1.0 copy-start.5
  106.4 1.0 copy-start.7
  107.4 0.9 copy-start.9
  108.4 0.9 copy-start.11
  120.5 2.3 %copy-start = (f32[2496,512]{1,0:T(8,128)}, f32[2496,512]{1,0:T(8,128)S(1)}, u32[]{:S(2)}) copy-start(f32[2496,512]{1,0:T(8,128)S(1)} %shard_map.118.refs_0_) | copy-start | bytes 15335428
  122.8 11.0 %collective-permute-start.21 = (bf16[48,2496]{1,0:T(8,128)(2,1)S(1)}, bf16[48,2496]{1,0:T(8,128)(2,1)S(1)}, u32[]{:S(2)}, u32[]{:S(2)}) collective-permute-start(bf16[48,2496]{1,0:T(8,128)(2,1)S(1)} %slice.55), channel_id=1, source_target_pairs={{0,4},{2,6},{4,0},{6,2},{8,12},{10,14},{12,8},{14,10},{16,20},{18,... | collective-permute-start | bytes 718856 | tf_op jit(solution)/shard_map/ppermute | solution.py:166
  124.4 9.3 %collective-permute-start.20 = (bf16[32,2496]{1,0:T(8,128)(2,1)S(1)}, bf16[32,2496]{1,0:T(8,128)(2,1)S(1)}, u32[]{:S(2)}, u32[]{:S(2)}) collective-permute-start(bf16[32,2496]{1,0:T(8,128)(2,1)S(1)} %slice.54), channel_id=1, source_target_pairs={{0,2},{2,0},{4,6},{6,4},{8,10},{10,8},{12,14},{14,12},{16,18},{18,... | collective-permute-start | bytes 479240 | tf_op jit(solution)/shard_map/ppermute | solution.py:165
Sparse Core Ops, SparseCore 0:
  30.9 66.6 all-gather.1

commit v4 on v3

--- a/solution.py
+++ b/solution.py
@@ -12,6 +12,8 @@
 SEQ = 4096
 IMG_CAP = 16
 EPSILON = 1e-06
+VMEM = 56 << 20
+LIGHT = pl.CostEstimate(flops=1000, bytes_accessed=1000, transcendentals=0)
 
 
 def folded_ring(count):
@@ -22,25 +24,6 @@
 
 def tp_shift(value, n_tp, distance):
     return lax.ppermute(value, "tp", [(i, (i + distance) % n_tp) for i in range(n_tp)])
-
-
-def tp_gather(value, n_tp, axis):
-    me = lax.axis_index("tp")
-    width = value.shape[axis]
-    if n_tp == 2:
-        other = tp_shift(value, 2, 1)
-        first = jnp.where(me == 0, value, other)
-        second = jnp.where(me == 0, other, value)
-        return jnp.concatenate([first, second], axis=axis)
-    shape = list(value.shape)
-    shape[axis] = width * n_tp
-    whole = jnp.zeros(shape, value.dtype)
-    for distance in range(n_tp):
-        block = value if distance == 0 else tp_shift(value, n_tp, distance)
-        whole = lax.dynamic_update_slice_in_dim(
-            whole, block, (me - distance) % n_tp * width, axis
-        )
-    return whole
 
 
 def tp_scatter_sum(value, n_tp, axis):
@@ -51,10 +34,6 @@
         block = lax.dynamic_slice_in_dim(value, (me + distance) % n_tp * width, width, axis)
         total = total + tp_shift(block, n_tp, distance)
     return total
-
-
-def tie(*values):
-    return lax.optimization_barrier(values)
 
 
 def ring_tables(n_req):
@@ -120,7 +99,6 @@
     for _, _, block in pieces:
         operands.append(block)
         specs.append(pl.BlockSpec((block.shape[0], tile), lambda i, order_ref: (0, i)))
-    depth = sum(count for _, _, count in spec) + (extra[0].shape[0] if extra is not None else 0)
     return pl.pallas_call(
         body,
         out_shape=jax.ShapeDtypeStruct(
@@ -132,13 +110,101 @@
             in_specs=specs,
             out_specs=pl.BlockSpec((tile, positions), lambda i, order_ref: (i, 0)),
         ),
-        compiler_params=pltpu.CompilerParams(vmem_limit_bytes=40 << 20),
-        cost_estimate=pl.CostEstimate(
-            flops=2 * depth * columns * positions,
-            bytes_accessed=2 * depth * (columns + positions) + 8 * columns * positions,
-            transcendentals=0,
-        ),
+        compiler_params=pltpu.CompilerParams(vmem_limit_bytes=VMEM),
+        cost_estimate=LIGHT,
     )(order, *operands)
+
+
+def merge(patches, row_mean, row_scale, ln_gain, ln_bias, merge_weight):
+    rows, width = patches.shape
+    window, _, features = merge_weight.shape
+    tokens = rows // window
+
+    def body(patches_ref, mean_ref, scale_ref, gain_ref, bias_ref, weight_ref, out_ref, normed_ref):
+        step = pl.program_id(0)
+
+        @pl.when(step == 0)
+        def _():
+            normed = (patches_ref[...].astype(jnp.float32) - mean_ref[...]) * scale_ref[
+                ...
+            ] * gain_ref[...].astype(jnp.float32) + bias_ref[...].astype(jnp.float32)
+            normed_ref[...] = normed.astype(jnp.bfloat16)
+            out_ref[...] = jnp.zeros_like(out_ref)
+
+        wanted = lax.broadcasted_iota(jnp.int32, (tokens, rows), 0) * window + step
+        chosen = (lax.broadcasted_iota(jnp.int32, (tokens, rows), 1) == wanted).astype(jnp.bfloat16)
+        part = jnp.dot(chosen, normed_ref[...], preferred_element_type=jnp.float32)
+        out_ref[...] += jnp.dot(
+            part.astype(jnp.bfloat16), weight_ref[0], preferred_element_type=jnp.float32
+        )
+
+    def whole(shape):
+        return pl.BlockSpec(shape, lambda i: (0, 0))
+
+    return pl.pallas_call(
+        body,
+        out_shape=jax.ShapeDtypeStruct((tokens, features), jnp.float32),
+        grid=(window,),
+        in_specs=[
+            whole((rows, width)),
+            whole((rows, 1)),
+            whole((rows, 1)),
+            whole((1, width)),
+            whole((1, width)),
+            pl.BlockSpec((1, width, features), lambda i: (i, 0, 0)),
+        ],
+        out_specs=whole((tokens, features)),
+        scratch_shapes=[pltpu.VMEM((rows, width), jnp.bfloat16)],
+        compiler_params=pltpu.CompilerParams(vmem_limit_bytes=VMEM),
+        cost_estimate=LIGHT,
+    )(patches, row_mean, row_scale, ln_gain[None, :], ln_bias[None, :], merge_weight)
+
+
+def combine(tp_index, texts, images, norm_gain):
+    n_tp = len(texts)
+    width, positions = texts[0].shape
+    slots = images[0].shape[0]
+
+    def body(index_ref, gain_ref, *refs):
+        text_refs, image_refs = refs[:n_tp], refs[n_tp : 2 * n_tp]
+        out_ref, value_ref = refs[2 * n_tp :]
+        code = image_refs[0][:, width : width + 2].astype(jnp.float32)
+        local = code[:, 0:1] * 256.0 + code[:, 1:2] - 1.0
+        place = lax.broadcasted_iota(jnp.int32, (slots, positions), 1).astype(jnp.float32)
+        hit = jnp.where(local == place, 1.0, 0.0)
+        covered = jnp.max(hit, axis=0, keepdims=True)
+        hit = hit.astype(jnp.bfloat16)
+        squares = jnp.zeros((1, positions), jnp.float32)
+        starts = []
+        for distance in range(n_tp):
+            start = pl.multiple_of(
+                lax.rem(index_ref[0] + n_tp - distance, n_tp) * width, 16
+            )
+            starts.append(start)
+            image = lax.dot_general(
+                image_refs[distance][...],
+                hit,
+                (((0,), (0,)), ((), ())),
+                preferred_element_type=jnp.float32,
+            )[:width]
+            value = jnp.where(covered > 0.0, image, text_refs[distance][...].astype(jnp.float32))
+            squares += jnp.sum(value * value, axis=0, keepdims=True)
+            value_ref[pl.ds(start, width), :] = value
+        scale = lax.rsqrt(squares / (width * n_tp) + EPSILON)
+        out_ref[...] = (
+            value_ref[...] * scale * gain_ref[...].astype(jnp.float32)
+        ).astype(out_ref.dtype)
+
+    vmem = pl.BlockSpec(memory_space=pltpu.VMEM)
+    return pl.pallas_call(
+        body,
+        out_shape=jax.ShapeDtypeStruct((width * n_tp, positions), jnp.bfloat16),
+        in_specs=[pl.BlockSpec(memory_space=pltpu.SMEM)] + [vmem] * (1 + 2 * n_tp),
+        out_specs=vmem,
+        scratch_shapes=[pltpu.VMEM((width * n_tp, positions), jnp.float32)],
+        compiler_params=pltpu.CompilerParams(vmem_limit_bytes=VMEM),
+        cost_estimate=LIGHT,
+    )(tp_index, norm_gain[:, None], *texts, *images)
 
 
 def shards(
@@ -151,28 +217,21 @@
     x_perm = [(i, i ^ 1) for i in range(n_req)]
     y_perm = [(i, i ^ 2) for i in range(n_req)]
     rows = qkv_weight.shape[0]
-    direct = rows * 4 // 5 // 16 * 16
-    cut = direct // 32 * 16 or direct // 2
+    cut = rows // 32 * 16 or rows // 2
     order = lax.dynamic_slice_in_dim(jnp.asarray(table), me, 1, 0).reshape(-1)
 
-    def along_line(block):
-        return lax.ppermute(block, "req", line_perm)
-
-    def to_sides(block):
-        return lax.ppermute(block, "req", x_perm), lax.ppermute(block, "req", y_perm)
-
-    def to_corner(by_x, by_y):
-        upper = lax.ppermute(by_y[:cut], "req", x_perm)
-        lower = lax.ppermute(by_x[cut:], "req", y_perm)
-        return upper, lower
-
-    held = [qkv_weight[:direct]]
-    sides = []
-    corners = []
-    held.append(along_line(held[0]))
-    sides.append(to_sides(held[0]))
-    gathered = lax.all_gather(qkv_weight[direct:], "req", axis=0, tiled=True)
-    text_full = tp_gather(text_rows.T, n_tp, 0)
+    held, sides, corners = [qkv_weight], [], []
+    for step in range(lines):
+        if step < lines - 1:
+            held.append(lax.ppermute(held[step], "req", line_perm))
+        by_x = lax.ppermute(held[step], "req", x_perm)
+        by_y = lax.ppermute(held[step], "req", y_perm)
+        sides.append((by_x, by_y))
+        corners.append(
+            (lax.ppermute(by_y[:cut], "req", x_perm), lax.ppermute(by_x[cut:], "req", y_perm))
+        )
+    text_turned = text_rows.T
+    texts = [text_turned] + [tp_shift(text_turned, n_tp, d) for d in range(1, n_tp)]
 
     token_count = token_pos.shape[0]
     target = lax.div(token_pos, row_count)
@@ -193,67 +252,21 @@
     sum_total, square_total = lax.psum((sum_part, square_part), "tp")
     row_mean = (sum_total / DV)[:, None]
     second = (square_total / DV)[:, None]
-    normed = (
-        (values - row_mean)
-        * lax.rsqrt(second - row_mean * row_mean + EPSILON)
-        * ln_gain.astype(jnp.float32)
-        + ln_bias.astype(jnp.float32)
-    ).astype(jnp.bfloat16)
-
-    normed, held[1], sides[0], place, code_cols, order = tie(
-        normed, held[1], sides[0], place, code_cols, order
-    )
-    held.append(along_line(held[1]))
-    sides.append(to_sides(held[1]))
-    corners.append(to_corner(*sides[0]))
-
-    grouped = normed.reshape(patches.shape[0] // 4, 4, patches.shape[1])
-    partial_value = jnp.einsum(
-        "mkf,kfd->md", grouped, merge_weight, preferred_element_type=jnp.float32
-    )
+    row_scale = lax.rsqrt(second - row_mean * row_mean + EPSILON)
+    partial_value = merge(patches, row_mean, row_scale, ln_gain, ln_bias, merge_weight)
     merged = tp_scatter_sum(partial_value, n_tp, 1).astype(jnp.bfloat16)
     padding = (-width - 2) % 128
     payload = jnp.concatenate(
         [merged, code_cols, jnp.zeros((token_count, padding), jnp.bfloat16)], axis=1
     )
     outgoing = jnp.dot(place, payload, preferred_element_type=jnp.float32).astype(jnp.bfloat16)
-
-    outgoing, held[2], sides[1], corners[0] = tie(outgoing, held[2], sides[1], corners[0])
-    held.append(along_line(held[2]))
-    sides.append(to_sides(held[2]))
-    corners.append(to_corner(*sides[1]))
-
     arrived = lax.all_to_all(
         outgoing.reshape(n_req, IMG_CAP, -1), "req", split_axis=0, concat_axis=0
     ).reshape(slot_count, -1)
-    local = (
-        arrived[:, width].astype(jnp.int32) * 256 + arrived[:, width + 1].astype(jnp.int32) - 1
-    )
-    hit = local[:, None] == jnp.arange(row_count, dtype=jnp.int32)[None, :]
-    image_rows = tp_gather(arrived[:, :width], n_tp, 1)
-    image_part = lax.dot_general(
-        image_rows,
-        hit.astype(jnp.bfloat16),
-        (((0,), (0,)), ((), ())),
-        preferred_element_type=jnp.float32,
-    )
-    full = jnp.where(jnp.any(hit, axis=0)[None, :], image_part, text_full.astype(jnp.float32))
-    scaled = (
-        full
-        * lax.rsqrt(jnp.mean(full * full, axis=0, keepdims=True) + EPSILON)
-        * norm_gain.astype(jnp.float32)[:, None]
-    ).astype(jnp.bfloat16)
-
-    scaled, held[3], sides[2], corners[1], gathered = tie(
-        scaled, held[3], sides[2], corners[1], gathered
-    )
-    for step in range(3, lines):
-        if step < lines - 1:
-            held.append(along_line(held[step]))
-        sides.append(to_sides(held[step]))
-        corners.append(to_corner(*sides[step - 1]))
+    images = [arrived] + [tp_shift(arrived, n_tp, d) for d in range(1, n_tp)]
+    tp_index = lax.axis_index("tp").reshape(1)
+    scaled = combine(tp_index, texts, images, norm_gain)
     blocks = scaled.reshape(n_req, rows, row_count)
-    rest = blocks[:, direct:].reshape(-1, row_count)
 
     def pieces_of(step):
         by_x, by_y = sides[step]
@@ -263,16 +276,12 @@
         upper, lower = corners[step]
         return [(step * 4 + 3, 0, upper), (step * 4 + 3, cut, lower)]
 
-    total = multiply(
-        order, blocks,
-        pieces_of(0) + corner_of(0) + pieces_of(1) + corner_of(1),
-        extra=(gathered, rest),
-    )
-    total, sides[-1], corners[-1] = tie(total, sides[-1], corners[-1])
-    corners.append(to_corner(*sides[-1]))
-    late = []
-    for step in range(2, lines - 1):
+    early, late = [], []
+    for step in range(lines - 2):
+        early += pieces_of(step) + corner_of(step)
+    for step in range(lines - 2, lines - 1):
         late += pieces_of(step) + corner_of(step)
+    total = multiply(order, blocks, early)
     total = multiply(order, blocks, late + pieces_of(lines - 1), total=total)
 
     position = me * row_count + jnp.arange(row_count, dtype=jnp.int32)

time: 145 us -> 133 us (0.917)
  Pallas kernels: 23.8 us -> 41.7 us
  between operations: 13.7 us -> 0.21 us
  matrix products: 9.38 us -> 1.09 us
  other arithmetic: 9.92 us -> 3.53 us
  starting transfers between devices: 31.2 us -> 25.6 us
  local copies, waits for them, and re-layouts: 15.9 us -> 17.6 us
  waiting for transfers between devices: 38.1 us -> 39.6 us
    ppermute x19, waiting for transfers between devices: 22.8 us -> 39.6 us  [the longest x3 14.5 us: shards(): held.append(lax.ppermute(held[step], 'req', line_perm))]
    pallas_call x0 -> x2, Pallas kernels: none -> 12.7 us  [the longest x1 7.82 us: merge(): pl.pallas_call(body, out_shape=jax.ShapeDtypeStruct((tokens, features), j...]
    dot_general x2 -> x0, matrix products: 8.33 us -> none  [the longest x1 5.94 us: shards(): jnp.einsum('mkf,kfd->md', grouped, merge_weight, preferred_element_type=j...]
    all_gather x1 -> x0, waiting for transfers between devices: 7.37 us -> none  [shards(): gathered = lax.all_gather(qkv_weight[direct:], 'req', axis=0, tiled=True)]
    all_to_all x1, waiting for transfers between devices: 6.51 us -> 0.01 us  [shards(): lax.all_to_all(outgoing.reshape(n_req, IMG_CAP, -1), 'req', split_axis=0,...]
    pallas_call x3, Pallas kernels: 23.8 us -> 29 us  [multiply(): pl.pallas_call(body, out_shape=jax.ShapeDtypeStruct((columns, positions),...]
    broadcast_in_dim x0 -> x4, local copies, waits for them, and re-layouts: none -> 4.46 us  [the longest x1 1.27 us: merge(): ln_gain[None, :]]
    unnamed x30 -> x32, local copies, waits for them, and re-layouts: 9.56 us -> 5.15 us
  transfers between devices with their start and end apart: 24 -> 23, of which waited for: 8 -> 8; matrix products, arithmetic and copies ran while one was open for 13% -> 13% of each run, Pallas kernels for 14% -> 26%
where the time goes in v4:
time: 133 us; the launch traced here: 132 us
  Pallas kernels  41.7 us (31%)
  waiting for transfers between devices  39.6 us (30%)
  starting transfers between devices  25.6 us (19%)
  local copies, waits for them, and re-layouts  17.6 us (13%)
  other arithmetic  3.53 us (3%)
  blocking collectives  2.47 us (2%)
    pallas_call x3, Pallas kernels, multiply(): pl.pallas_call(body, out_shape=jax.ShapeDtypeStruct((columns, positions),...  29 us
    ppermute x3, waiting for transfers between devices, shards(): held.append(lax.ppermute(held[step], 'req', line_perm))  14.5 us
    ppermute x4, waiting for transfers between devices, shards(): by_x = lax.ppermute(held[step], 'req', x_perm)  11.6 us
    ppermute x4, waiting for transfers between devices, shards(): by_y = lax.ppermute(held[step], 'req', y_perm)  11.2 us
    pallas_call x1, Pallas kernels, merge(): pl.pallas_call(body, out_shape=jax.ShapeDtypeStruct((tokens, features), j...  7.82 us
    ppermute x3, starting transfers between devices, shards(): held.append(lax.ppermute(held[step], 'req', line_perm))  5.67 us
    unnamed x32, local copies, waits for them, and re-layouts  5.15 us
    ppermute x4, starting transfers between devices, shards(): lax.ppermute(by_x[cut:], 'req', y_perm)  5.01 us
  transfers between devices with their start and end apart: 23, of which 8 were waited for; matrix products, arithmetic and copies ran while one was open for 13% of the time, Pallas kernels for 26%

profile of v4, /device:TPU:0, one launch (start us, length us, event | category | flops | bytes accessed | tf_op | source)
XLA Modules:
  0.0 131.8 jit_solution(8244651612866478402)
XLA Ops:
  0.0 3.0 %collective-permute-start.7 = (bf16[104,2496]{1,0:T(8,128)(2,1)}, bf16[104,2496]{1,0:T(8,128)(2,1)}, u32[]{:S(2)}, u32[]{:S(2)}) collective-permute-start(bf16[104,2496]{1,0:T(8,128)(2,1)} %refs_0_.1), channel_id=1, source_target_pairs={{0,8},{2,10},{4,12},{6,14},{8,24},{10,26},{12,28},{14,30},{16,0},{... | collective-permute-start | bytes 1557512 | tf_op jit(solution)/shard_map/ppermute | solution.py:226
  3.0 1.5 %collective-permute-start.3 = (bf16[104,2496]{1,0:T(8,128)(2,1)}, bf16[104,2496]{1,0:T(8,128)(2,1)S(1)}, u32[]{:S(2)}, u32[]{:S(2)}) collective-permute-start(bf16[104,2496]{1,0:T(8,128)(2,1)} %refs_0_.1), channel_id=1, source_target_pairs={{0,2},{2,0},{4,6},{6,4},{8,10},{10,8},{12,14},{14,12},{16,18},{18,... | collective-permute-start | bytes 1557512 | tf_op jit(solution)/shard_map/ppermute | solution.py:227
  4.5 1.5 %collective-permute-start.4 = (bf16[104,2496]{1,0:T(8,128)(2,1)}, bf16[104,2496]{1,0:T(8,128)(2,1)S(1)}, u32[]{:S(2)}, u32[]{:S(2)}) collective-permute-start(bf16[104,2496]{1,0:T(8,128)(2,1)} %refs_0_.1), channel_id=1, source_target_pairs={{0,4},{2,6},{4,0},{6,2},{8,12},{10,14},{12,8},{14,10},{16,20},{18,... | collective-permute-start | bytes 1557512 | tf_op jit(solution)/shard_map/ppermute | solution.py:228
  6.0 1.5 %fusion = (f32[448]{0:T(512)S(1)}, f32[448]{0:T(512)S(1)}) fusion(bf16[448,832]{1,0:T(8,128)(2,1)} %patches_ref.1), kind=kLoop, calls=%fused_computation.2 | loop fusion | flops 1490048 | bytes 749056 | tf_op jit(solution)/shard_map/reduce_sum | solution.py:251
  7.5 2.5 %all-reduce = (f32[448]{0:T(512)S(1)}, f32[448]{0:T(512)S(1)}) all-reduce(f32[448]{0:T(512)S(1)} %get-tuple-element.6, f32[448]{0:T(512)S(1)} %get-tuple-element.5), channel_id=1, replica_groups=mesh['req'=16,'tp'=2] {'tp'}, use_global_device_ids=true, to_apply=%region_2.0 | all-reduce | flops 896 | bytes 7168 | tf_op jit(solution)/shard_map/psum | solution.py:252
  10.0 0.8 copy.18.mean_ref
  10.8 0.8 copy.19.scale_ref
  11.7 1.3 broadcast_in_dim.24.gain_ref
  12.9 1.3 broadcast_in_dim.42.bias_ref
  14.2 7.8 %shard_map.118 = f32[112,1664]{1,0:T(8,128)} custom-call(bf16[448,832]{1,0:T(8,128)(2,1)} %patches_ref.1, f32[448,1]{1,0:T(8,128)} %copy.18.mean_ref, f32[448,1]{1,0:T(8,128)} %copy.19.scale_ref, bf16[1,832]{1,0:T(2,128)(2,1)} %broadcast_in_dim.24.gain_ref, bf16[1,832]{1,0:T(2,128)(2,1)} %broadcast_in_dim.42.bias_ref, bf16[4,832,1664]{2,1,0:T(8,128)(2,1)} %weight_ref.1), custom_call_target="tpu_custom_call" | custom-call | flops 1000 | bytes 1000 | tf_op jit(solution)/shard_map/pallas_call | solution.py:144
  22.0 1.2 constant_dynamic-slice_fusion
  23.2 0.3 collective-permute-start.1
  23.5 0.2 convert_reduce_fusion.1
  23.7 2.6 %collective-permute-start.12 = (bf16[104,2496]{1,0:T(8,128)(2,1)}, bf16[104,2496]{1,0:T(8,128)(2,1)}, u32[]{:S(2)}, u32[]{:S(2)}) collective-permute-start(bf16[104,2496]{1,0:T(8,128)(2,1)} %collective-permute-done.7.refs_5_), channel_id=1, source_target_pairs={{0,8},{2,10},{4,12},{6,14},{8,24},{10,26},{12,28},{14,30},{16,0},{... | collective-permute-start | bytes 1557512 | tf_op jit(solution)/shard_map/ppermute | solution.py:226
  26.3 0.1 copy.21
  26.5 0.1 copy.20
  26.6 0.1 pad.3.clone
  26.7 1.2 add_convert_fusion
  27.9 1.1 convolution_convert_fusion
  29.0 3.7 %all-to-all-start = ((bf16[16,16,896]{2,1,0:T(8,128)(2,1)}), bf16[16,16,896]{2,1,0:T(8,128)(2,1)S(1)}, u32[]{:S(2)}, u32[]{:S(2)}) async-start(bf16[16,16,896]{2,1,0:T(8,128)(2,1)} %bitcast.7), calls=%async_computation | async-start | bytes 917504 | tf_op jit(solution)/shard_map/all_to_all | solution.py:263
  32.7 1.8 %collective-permute-start.8 = (bf16[104,2496]{1,0:T(8,128)(2,1)}, bf16[104,2496]{1,0:T(8,128)(2,1)S(1)}, u32[]{:S(2)}, u32[]{:S(2)}) collective-permute-start(bf16[104,2496]{1,0:T(8,128)(2,1)} %collective-permute-done.7.refs_5_), channel_id=1, source_target_pairs={{0,2},{2,0},{4,6},{6,4},{8,10},{10,8},{12,14},{14,12},{16,18},{18,... | collective-permute-start | bytes 1557512 | tf_op jit(solution)/shard_map/ppermute | solution.py:227
  34.5 7.9 %collective-permute-done.12.refs_1_ = bf16[104,2496]{1,0:T(8,128)(2,1)} collective-permute-done((bf16[104,2496]{1,0:T(8,128)(2,1)}, bf16[104,2496]{1,0:T(8,128)(2,1)}, u32[]{:S(2)}, u32[]{:S(2)}) %collective-permute-start.12) | collective-permute-done | bytes 519200 | tf_op jit(solution)/shard_map/ppermute | solution.py:226
  42.4 0.0 collective-permute-start.17
  42.4 0.0 collective-permute-start.9
  42.4 0.0 collective-permute-done.3.refs_1_
  42.4 0.0 copy-start.3
  42.5 0.8 collective-permute-start.13
  43.2 0.8 copy-done.6
  44.0 8.5 %collective-permute-done.8.refs_6_ = bf16[104,2496]{1,0:T(8,128)(2,1)S(1)} collective-permute-done((bf16[104,2496]{1,0:T(8,128)(2,1)}, bf16[104,2496]{1,0:T(8,128)(2,1)S(1)}, u32[]{:S(2)}, u32[]{:S(2)}) %collective-permute-start.8) | collective-permute-done | bytes 519200 | tf_op jit(solution)/shard_map/ppermute | solution.py:227
  52.5 1.5 %collective-permute-start.14 = (bf16[104,2496]{1,0:T(8,128)(2,1)}, bf16[104,2496]{1,0:T(8,128)(2,1)S(1)}, u32[]{:S(2)}, u32[]{:S(2)}) collective-permute-start(bf16[104,2496]{1,0:T(8,128)(2,1)} %collective-permute-done.12.refs_1_), channel_id=1, source_target_pairs={{0,4},{2,6},{4,0},{6,2},{8,12},{10,14},{12,8},{14,10},{16,20},{18,... | collective-permute-start | bytes 1557512 | tf_op jit(solution)/shard_map/ppermute | solution.py:228
  54.0 6.5 %collective-permute-done.17.refs_6_ = bf16[104,2496]{1,0:T(8,128)(2,1)} collective-permute-done((bf16[104,2496]{1,0:T(8,128)(2,1)}, bf16[104,2496]{1,0:T(8,128)(2,1)}, u32[]{:S(2)}, u32[]{:S(2)}) %collective-permute-start.17) | collective-permute-done | bytes 519200 | tf_op jit(solution)/shard_map/ppermute | solution.py:226
  60.6 0.5 collective-permute-start.18
  61.1 0.8 copy-done.7
  61.9 0.5 collective-permute-start.19
  62.4 0.7 collective-permute-done.13.refs_2_
  63.1 6.6 %collective-permute-done.14.refs_3_ = bf16[104,2496]{1,0:T(8,128)(2,1)S(1)} collective-permute-done((bf16[104,2496]{1,0:T(8,128)(2,1)}, bf16[104,2496]{1,0:T(8,128)(2,1)S(1)}, u32[]{:S(2)}, u32[]{:S(2)}) %collective-permute-start.14) | collective-permute-done | bytes 519200 | tf_op jit(solution)/shard_map/ppermute | solution.py:228
  69.7 0.6 collective-permute-start.6
  70.3 1.7 %slice.32 = bf16[48,2496]{1,0:T(8,128)(2,1)} slice(bf16[104,2496]{1,0:T(8,128)(2,1)} %copy-done.6), slice={[0:48], [0:2496]} | slice | bytes 479232 | tf_op jit(solution)/shard_map/slice | solution.py:231
  72.0 2.4 %collective-permute-done.18.refs_7_ = bf16[104,2496]{1,0:T(8,128)(2,1)S(1)} collective-permute-done((bf16[104,2496]{1,0:T(8,128)(2,1)}, bf16[104,2496]{1,0:T(8,128)(2,1)S(1)}, u32[]{:S(2)}, u32[]{:S(2)}) %collective-permute-start.18) | collective-permute-done | bytes 519200 | tf_op jit(solution)/shard_map/ppermute | solution.py:227
  74.4 0.5 collective-permute-start.5
  74.9 1.7 %slice.34 = bf16[48,2496]{1,0:T(8,128)(2,1)} slice(bf16[104,2496]{1,0:T(8,128)(2,1)} %copy-done.7), slice={[0:48], [0:2496]} | slice | bytes 479232 | tf_op jit(solution)/shard_map/slice | solution.py:231
  76.6 4.6 %collective-permute-done.19.refs_8_ = bf16[104,2496]{1,0:T(8,128)(2,1)} collective-permute-done((bf16[104,2496]{1,0:T(8,128)(2,1)}, bf16[104,2496]{1,0:T(8,128)(2,1)}, u32[]{:S(2)}, u32[]{:S(2)}) %collective-permute-start.19) | collective-permute-done | bytes 519200 | tf_op jit(solution)/shard_map/ppermute | solution.py:228
  81.2 0.8 collective-permute-start.10
  82.1 0.1 fusion.10
  82.3 1.0 slice.38
  83.3 1.9 %collective-permute-start.11 = (bf16[56,2496]{1,0:T(8,128)(2,1)S(1)}, bf16[56,2496]{1,0:T(8,128)(2,1)S(1)}, u32[]{:S(2)}, u32[]{:S(2)}) collective-permute-start(bf16[56,2496]{1,0:T(8,128)(2,1)S(1)} %slice.35), channel_id=1, source_target_pairs={{0,4},{2,6},{4,0},{6,2},{8,12},{10,14},{12,8},{14,10},{16,20},{18,... | collective-permute-start | bytes 838664 | tf_op jit(solution)/shard_map/ppermute | solution.py:231
  85.1 2.3 %collective-permute-done.6.refs_4_ = bf16[56,2496]{1,0:T(8,128)(2,1)} collective-permute-done((bf16[56,2496]{1,0:T(8,128)(2,1)S(1)}, bf16[56,2496]{1,0:T(8,128)(2,1)}, u32[]{:S(2)}, u32[]{:S(2)}) %collective-permute-start.6) | collective-permute-done | bytes 279584 | tf_op jit(solution)/shard_map/ppermute | solution.py:231
  87.4 0.6 collective-permute-start.16
  88.0 0.3 collective-permute-start.15
  88.2 0.0 collective-permute-done.10.refs_8_
  88.3 2.0 %collective-permute-start.21 = (bf16[56,2496]{1,0:T(8,128)(2,1)S(1)}, bf16[56,2496]{1,0:T(8,128)(2,1)S(1)}, u32[]{:S(2)}, u32[]{:S(2)}) collective-permute-start(bf16[56,2496]{1,0:T(8,128)(2,1)S(1)} %slice.39), channel_id=1, source_target_pairs={{0,4},{2,6},{4,0},{6,2},{8,12},{10,14},{12,8},{14,10},{16,20},{18,... | collective-permute-start | bytes 838664 | tf_op jit(solution)/shard_map/ppermute | solution.py:231
  90.3 1.2 collective-permute-start.20
  91.4 1.2 fusion.13.order_ref
  92.7 1.1 broadcast_in_dim.46.gain_ref
  93.7 0.6 compare_convert_fusion.refs_1_
  94.3 4.8 %shard_map.119 = bf16[1664,512]{1,0:T(8,128)(2,1)} custom-call(s32[1]{0:T(128)} %bitcast.1.index_ref, bf16[1664,1]{1,0:T(8,128)(2,1)} %broadcast_in_dim.46.gain_ref, bf16[832,512]{1,0:T(8,128)(2,1)} %bitcast.2.refs_0_, bf16[832,512]{1,0:T(8,128)(2,1)} %collective-permute-done.refs_1_, bf16[256,896]{1,0:T(8,128)(2,1)} %bitcast.19, ...), custom_call_target="tpu_custom_call" | custom-call | flops 1000 | bytes 1000 | tf_op jit(solution)/shard_map/pallas_call | solution.py:199
  99.2 0.7 copy-done.10
  99.9 11.5 %shard_map.120.refs_0_ = f32[2496,512]{1,0:T(8,128)} custom-call(s32[16]{0:T(128)} %fusion.13.order_ref, bf16[16,104,512]{2,1,0:T(8,128)(2,1)} %bitcast.15, bf16[104,2496]{1,0:T(8,128)(2,1)} %refs_0_.1, bf16[104,2496]{1,0:T(8,128)(2,1)} %copy-done.3, bf16[104,2496]{1,0:T(8,128)(2,1)} %copy-done.6, bf16[48,2496]{1,0:T(8,128)(2,1)} %collective-permute-done.5.refs_3_, ...), custom_call_target="tpu_custom_call" | custom-call | flops 1000 | bytes 1000 | tf_op jit(solution)/shard_map/pallas_call | solution.py:102
  111.5 0.7 copy-done.11
  112.1 0.7 copy-done.8
  112.8 10.7 %shard_map.121.refs_0_ = f32[2496,512]{1,0:T(8,128)} custom-call(s32[16]{0:T(128)} %fusion.13.order_ref, bf16[16,104,512]{2,1,0:T(8,128)(2,1)} %bitcast.16, f32[2496,512]{1,0:T(8,128)} %shard_map.120.refs_0_, bf16[104,2496]{1,0:T(8,128)(2,1)} %collective-permute-done.12.refs_1_, bf16[104,2496]{1,0:T(8,128)(2,1)} %copy-done.1, bf16[104,2496]{1,0:T(8,128)(2,1)} %copy-done.5, ...), custom_call_target="tpu_custom_call" | custom-call | flops 1000 | bytes 1000 | tf_op jit(solution)/shard_map/pallas_call | solution.py:102
  123.5 0.7 copy-done.12
  124.2 0.7 copy-done.9
  124.9 6.8 %shard_map.122 = bf16[2496,512]{1,0:T(8,128)(2,1)} custom-call(s32[16]{0:T(128)} %fusion.13.order_ref, bf16[16,104,512]{2,1,0:T(8,128)(2,1)} %bitcast.17, f32[2496,512]{1,0:T(8,128)} %shard_map.121.refs_0_, s32[1,512]{1,0:T(1,128)} %compare_convert_fusion.refs_1_, bf16[48,2496]{1,0:T(8,128)(2,1)} %copy-done.12, bf16[56,2496]{1,0:T(8,128)(2,1)} %copy-done.9), custom_call_target="tpu_custom_call" | custom-call | flops 1000 | bytes 1000 | tf_op jit(solution)/shard_map/pallas_call | solution.py:102
  (50 shorter events, 0.2 us)
Async XLA Ops:
  0.0 23.7 %collective-permute-start.7 = (bf16[104,2496]{1,0:T(8,128)(2,1)}, bf16[104,2496]{1,0:T(8,128)(2,1)}, u32[]{:S(2)}, u32[]{:S(2)}) collective-permute-start(bf16[104,2496]{1,0:T(8,128)(2,1)} %refs_0_.1), channel_id=1, source_target_pairs={{0,8},{2,10},{4,12},{6,14},{8,24},{10,26},{12,28},{14,30},{16,0},{... | collective-permute-start | bytes 1557512 | tf_op jit(solution)/shard_map/ppermute | solution.py:226
  3.0 39.4 %collective-permute-start.3 = (bf16[104,2496]{1,0:T(8,128)(2,1)}, bf16[104,2496]{1,0:T(8,128)(2,1)S(1)}, u32[]{:S(2)}, u32[]{:S(2)}) collective-permute-start(bf16[104,2496]{1,0:T(8,128)(2,1)} %refs_0_.1), channel_id=1, source_target_pairs={{0,2},{2,0},{4,6},{6,4},{8,10},{10,8},{12,14},{14,12},{16,18},{18,... | collective-permute-start | bytes 1557512 | tf_op jit(solution)/shard_map/ppermute | solution.py:227
  4.5 38.7 %collective-permute-start.4 = (bf16[104,2496]{1,0:T(8,128)(2,1)}, bf16[104,2496]{1,0:T(8,128)(2,1)S(1)}, u32[]{:S(2)}, u32[]{:S(2)}) collective-permute-start(bf16[104,2496]{1,0:T(8,128)(2,1)} %refs_0_.1), channel_id=1, source_target_pairs={{0,4},{2,6},{4,0},{6,2},{8,12},{10,14},{12,8},{14,10},{16,20},{18,... | collective-permute-start | bytes 1557512 | tf_op jit(solution)/shard_map/ppermute | solution.py:228
  14.2 9.3 %copy-start.15 = (s32[112]{0:T(128)S(1)}, s32[112]{0:T(128)}, u32[]{:S(2)}) copy-start(s32[112]{0:T(128)} %param.17) | copy-start | bytes 1348
  22.0 60.1 %copy-start.14 = (s32[2]{0:T(128)S(1)}, s32[2]{0:T(128)}, u32[]{:S(2)}) copy-start(s32[2]{0:T(128)} %param.18) | copy-start | bytes 28
  23.2 3.5 %collective-permute-start.1 = (f32[112,832]{1,0:T(8,128)S(1)}, f32[112,832]{1,0:T(8,128)S(1)}, u32[]{:S(2)}, u32[]{:S(2)}) collective-permute-start(f32[112,832]{1,0:T(8,128)S(1)} %constant_dynamic-slice_fusion), channel_id=1, source_target_pairs={{0,1},{1,0},{2,3},{3,2},{4,5},{5,4},{6,7},{7,6},{8,9},{9,8},{10,11... | collective-permute-start | bytes 1118216 | tf_op jit(solution)/shard_map/ppermute | solution.py:26
  23.7 18.7 %collective-permute-start.12 = (bf16[104,2496]{1,0:T(8,128)(2,1)}, bf16[104,2496]{1,0:T(8,128)(2,1)}, u32[]{:S(2)}, u32[]{:S(2)}) collective-permute-start(bf16[104,2496]{1,0:T(8,128)(2,1)} %collective-permute-done.7.refs_5_), channel_id=1, source_target_pairs={{0,8},{2,10},{4,12},{6,14},{8,24},{10,26},{12,28},{14,30},{16,0},{... | collective-permute-start | bytes 1557512 | tf_op jit(solution)/shard_map/ppermute | solution.py:226
  29.0 63.7 %copy-start.13 = (bf16[1664]{0:T(1024)(128)(2,1)S(1)}, bf16[1664]{0:T(1024)(128)(2,1)}, u32[]{:S(2)}) copy-start(bf16[1664]{0:T(1024)(128)(2,1)} %param.15) | copy-start | bytes 9988
  29.0 33.4 %all-to-all-start = ((bf16[16,16,896]{2,1,0:T(8,128)(2,1)}), bf16[16,16,896]{2,1,0:T(8,128)(2,1)S(1)}, u32[]{:S(2)}, u32[]{:S(2)}) async-start(bf16[16,16,896]{2,1,0:T(8,128)(2,1)} %bitcast.7), calls=%async_computation | async-start | bytes 917504 | tf_op jit(solution)/shard_map/all_to_all | solution.py:263
  32.7 19.9 %collective-permute-start.8 = (bf16[104,2496]{1,0:T(8,128)(2,1)}, bf16[104,2496]{1,0:T(8,128)(2,1)S(1)}, u32[]{:S(2)}, u32[]{:S(2)}) collective-permute-start(bf16[104,2496]{1,0:T(8,128)(2,1)} %collective-permute-done.7.refs_5_), channel_id=1, source_target_pairs={{0,2},{2,0},{4,6},{6,4},{8,10},{10,8},{12,14},{14,12},{16,18},{18,... | collective-permute-start | bytes 1557512 | tf_op jit(solution)/shard_map/ppermute | solution.py:227
  42.4 18.1 %collective-permute-start.17 = (bf16[104,2496]{1,0:T(8,128)(2,1)}, bf16[104,2496]{1,0:T(8,128)(2,1)}, u32[]{:S(2)}, u32[]{:S(2)}) collective-permute-start(bf16[104,2496]{1,0:T(8,128)(2,1)} %collective-permute-done.12.refs_1_), channel_id=1, source_target_pairs={{0,8},{2,10},{4,12},{6,14},{8,24},{10,26},{12,28},{14,30},{16,0},{... | collective-permute-start | bytes 1557512 | tf_op jit(solution)/shard_map/ppermute | solution.py:226
  42.4 18.7 %collective-permute-start.9 = (bf16[104,2496]{1,0:T(8,128)(2,1)}, bf16[104,2496]{1,0:T(8,128)(2,1)S(1)}, u32[]{:S(2)}, u32[]{:S(2)}) collective-permute-start(bf16[104,2496]{1,0:T(8,128)(2,1)} %collective-permute-done.7.refs_5_), channel_id=1, source_target_pairs={{0,4},{2,6},{4,0},{6,2},{8,12},{10,14},{12,8},{14,10},{16,20},{18,... | collective-permute-start | bytes 1557512 | tf_op jit(solution)/shard_map/ppermute | solution.py:228
  42.4 56.7 %copy-start.3 = (bf16[104,2496]{1,0:T(8,128)(2,1)}, bf16[104,2496]{1,0:T(8,128)(2,1)S(1)}, u32[]{:S(2)}) copy-start(bf16[104,2496]{1,0:T(8,128)(2,1)S(1)} %collective-permute-done.3.refs_1_) | copy-start | bytes 1557508
  42.5 20.6 %collective-permute-start.13 = (bf16[104,2496]{1,0:T(8,128)(2,1)}, bf16[104,2496]{1,0:T(8,128)(2,1)S(1)}, u32[]{:S(2)}, u32[]{:S(2)}) collective-permute-start(bf16[104,2496]{1,0:T(8,128)(2,1)} %collective-permute-done.12.refs_1_), channel_id=1, source_target_pairs={{0,2},{2,0},{4,6},{6,4},{8,10},{10,8},{12,14},{14,12},{16,18},{18,... | collective-permute-start | bytes 1557512 | tf_op jit(solution)/shard_map/ppermute | solution.py:227
  43.2 0.8 copy-start.6
  43.2 44.7 %collective-permute-start = (bf16[832,512]{1,0:T(8,128)(2,1)}, bf16[832,512]{1,0:T(8,128)(2,1)}, u32[]{:S(2)}, u32[]{:S(2)}) collective-permute-start(bf16[832,512]{1,0:T(8,128)(2,1)} %bitcast.2.refs_0_), channel_id=1, source_target_pairs={{0,1},{1,0},{2,3},{3,2},{4,5},{5,4},{6,7},{7,6},{8,9},{9,8},{10,11... | collective-permute-start | bytes 2555912 | tf_op jit(solution)/shard_map/ppermute | solution.py:26
  52.5 46.6 %copy-start.4 = (bf16[104,2496]{1,0:T(8,128)(2,1)}, bf16[104,2496]{1,0:T(8,128)(2,1)S(1)}, u32[]{:S(2)}) copy-start(bf16[104,2496]{1,0:T(8,128)(2,1)S(1)} %collective-permute-done.8.refs_6_) | copy-start | bytes 1557508
  52.5 17.2 %collective-permute-start.14 = (bf16[104,2496]{1,0:T(8,128)(2,1)}, bf16[104,2496]{1,0:T(8,128)(2,1)S(1)}, u32[]{:S(2)}, u32[]{:S(2)}) collective-permute-start(bf16[104,2496]{1,0:T(8,128)(2,1)} %collective-permute-done.12.refs_1_), channel_id=1, source_target_pairs={{0,4},{2,6},{4,0},{6,2},{8,12},{10,14},{12,8},{14,10},{16,20},{18,... | collective-permute-start | bytes 1557512 | tf_op jit(solution)/shard_map/ppermute | solution.py:228
  60.6 13.9 %collective-permute-start.18 = (bf16[104,2496]{1,0:T(8,128)(2,1)}, bf16[104,2496]{1,0:T(8,128)(2,1)S(1)}, u32[]{:S(2)}, u32[]{:S(2)}) collective-permute-start(bf16[104,2496]{1,0:T(8,128)(2,1)} %collective-permute-done.17.refs_6_), channel_id=1, source_target_pairs={{0,2},{2,0},{4,6},{6,4},{8,10},{10,8},{12,14},{14,12},{16,18},{18,... | collective-permute-start | bytes 1557512 | tf_op jit(solution)/shard_map/ppermute | solution.py:227
  61.1 0.8 copy-start.7
  61.9 19.3 %collective-permute-start.19 = (bf16[104,2496]{1,0:T(8,128)(2,1)}, bf16[104,2496]{1,0:T(8,128)(2,1)}, u32[]{:S(2)}, u32[]{:S(2)}) collective-permute-start(bf16[104,2496]{1,0:T(8,128)(2,1)} %collective-permute-done.17.refs_6_), channel_id=1, source_target_pairs={{0,4},{2,6},{4,0},{6,2},{8,12},{10,14},{12,8},{14,10},{16,20},{18,... | collective-permute-start | bytes 1557512 | tf_op jit(solution)/shard_map/ppermute | solution.py:228
  62.4 31.9 %copy-start = (bf16[16,16,896]{2,1,0:T(8,128)(2,1)}, bf16[16,16,896]{2,1,0:T(8,128)(2,1)S(1)}, u32[]{:S(2)}) copy-start(bf16[16,16,896]{2,1,0:T(8,128)(2,1)S(1)} %all-to-all-done) | copy-start | bytes 1376260
  63.1 36.1 %copy-start.1 = (bf16[104,2496]{1,0:T(8,128)(2,1)}, bf16[104,2496]{1,0:T(8,128)(2,1)S(1)}, u32[]{:S(2)}) copy-start(bf16[104,2496]{1,0:T(8,128)(2,1)S(1)} %collective-permute-done.13.refs_2_) | copy-start | bytes 1557508
  63.1 27.2 %collective-permute-start.2 = (bf16[256,896]{1,0:T(8,128)(2,1)S(1)}, bf16[256,896]{1,0:T(8,128)(2,1)}, u32[]{:S(2)}, u32[]{:S(2)}) collective-permute-start(bf16[256,896]{1,0:T(8,128)(2,1)S(1)} %bitcast.18), channel_id=1, source_target_pairs={{0,1},{1,0},{2,3},{3,2},{4,5},{5,4},{6,7},{7,6},{8,9},{9,8},{10,11... | collective-permute-start | bytes 1376264 | tf_op jit(solution)/shard_map/ppermute | solution.py:26
  69.7 29.4 %copy-start.5 = (bf16[104,2496]{1,0:T(8,128)(2,1)}, bf16[104,2496]{1,0:T(8,128)(2,1)S(1)}, u32[]{:S(2)}) copy-start(bf16[104,2496]{1,0:T(8,128)(2,1)S(1)} %collective-permute-done.14.refs_3_) | copy-start | bytes 1557508
  69.7 17.7 %collective-permute-start.6 = (bf16[56,2496]{1,0:T(8,128)(2,1)S(1)}, bf16[56,2496]{1,0:T(8,128)(2,1)}, u32[]{:S(2)}, u32[]{:S(2)}) collective-permute-start(bf16[56,2496]{1,0:T(8,128)(2,1)S(1)} %slice.33), channel_id=1, source_target_pairs={{0,4},{2,6},{4,0},{6,2},{8,12},{10,14},{12,8},{14,10},{16,20},{18,... | collective-permute-start | bytes 838664 | tf_op jit(solution)/shard_map/ppermute | solution.py:231
  74.4 24.8 %copy-start.2 = (bf16[104,2496]{1,0:T(8,128)(2,1)}, bf16[104,2496]{1,0:T(8,128)(2,1)S(1)}, u32[]{:S(2)}) copy-start(bf16[104,2496]{1,0:T(8,128)(2,1)S(1)} %collective-permute-done.18.refs_7_) | copy-start | bytes 1557508
  74.4 8.8 %collective-permute-start.5 = (bf16[48,2496]{1,0:T(8,128)(2,1)}, bf16[48,2496]{1,0:T(8,128)(2,1)}, u32[]{:S(2)}, u32[]{:S(2)}) collective-permute-start(bf16[48,2496]{1,0:T(8,128)(2,1)} %slice.32), channel_id=1, source_target_pairs={{0,2},{2,0},{4,6},{6,4},{8,10},{10,8},{12,14},{14,12},{16,18},{18,... | collective-permute-start | bytes 718856 | tf_op jit(solution)/shard_map/ppermute | solution.py:231
  81.2 7.0 %collective-permute-start.10 = (bf16[48,2496]{1,0:T(8,128)(2,1)}, bf16[48,2496]{1,0:T(8,128)(2,1)}, u32[]{:S(2)}, u32[]{:S(2)}) collective-permute-start(bf16[48,2496]{1,0:T(8,128)(2,1)} %slice.34), channel_id=1, source_target_pairs={{0,2},{2,0},{4,6},{6,4},{8,10},{10,8},{12,14},{14,12},{16,18},{18,... | collective-permute-start | bytes 718856 | tf_op jit(solution)/shard_map/ppermute | solution.py:231
  83.3 15.9 %collective-permute-start.11 = (bf16[56,2496]{1,0:T(8,128)(2,1)S(1)}, bf16[56,2496]{1,0:T(8,128)(2,1)S(1)}, u32[]{:S(2)}, u32[]{:S(2)}) collective-permute-start(bf16[56,2496]{1,0:T(8,128)(2,1)S(1)} %slice.35), channel_id=1, source_target_pairs={{0,4},{2,6},{4,0},{6,2},{8,12},{10,14},{12,8},{14,10},{16,20},{18,... | collective-permute-start | bytes 838664 | tf_op jit(solution)/shard_map/ppermute | solution.py:231
  87.4 24.1 %collective-permute-start.16 = (bf16[56,2496]{1,0:T(8,128)(2,1)S(1)}, bf16[56,2496]{1,0:T(8,128)(2,1)S(1)}, u32[]{:S(2)}, u32[]{:S(2)}) collective-permute-start(bf16[56,2496]{1,0:T(8,128)(2,1)S(1)} %slice.37), channel_id=1, source_target_pairs={{0,4},{2,6},{4,0},{6,2},{8,12},{10,14},{12,8},{14,10},{16,20},{18,... | collective-permute-start | bytes 838664 | tf_op jit(solution)/shard_map/ppermute | solution.py:231
  88.0 23.5 %collective-permute-start.15 = (bf16[48,2496]{1,0:T(8,128)(2,1)S(1)}, bf16[48,2496]{1,0:T(8,128)(2,1)S(1)}, u32[]{:S(2)}, u32[]{:S(2)}) collective-permute-start(bf16[48,2496]{1,0:T(8,128)(2,1)S(1)} %slice.36), channel_id=1, source_target_pairs={{0,2},{2,0},{4,6},{6,4},{8,10},{10,8},{12,14},{14,12},{16,18},{18,... | collective-permute-start | bytes 718856 | tf_op jit(solution)/shard_map/ppermute | solution.py:231
  88.3 35.2 %collective-permute-start.21 = (bf16[56,2496]{1,0:T(8,128)(2,1)S(1)}, bf16[56,2496]{1,0:T(8,128)(2,1)S(1)}, u32[]{:S(2)}, u32[]{:S(2)}) collective-permute-start(bf16[56,2496]{1,0:T(8,128)(2,1)S(1)} %slice.39), channel_id=1, source_target_pairs={{0,4},{2,6},{4,0},{6,2},{8,12},{10,14},{12,8},{14,10},{16,20},{18,... | collective-permute-start | bytes 838664 | tf_op jit(solution)/shard_map/ppermute | solution.py:231
  90.3 33.2 %collective-permute-start.20 = (bf16[48,2496]{1,0:T(8,128)(2,1)S(1)}, bf16[48,2496]{1,0:T(8,128)(2,1)S(1)}, u32[]{:S(2)}, u32[]{:S(2)}) collective-permute-start(bf16[48,2496]{1,0:T(8,128)(2,1)S(1)} %slice.38), channel_id=1, source_target_pairs={{0,2},{2,0},{4,6},{6,4},{8,10},{10,8},{12,14},{14,12},{16,18},{18,... | collective-permute-start | bytes 718856 | tf_op jit(solution)/shard_map/ppermute | solution.py:231
  99.2 0.7 copy-start.10
  111.4 0.7 copy-start.11
  112.1 0.7 copy-start.8
  123.5 0.7 copy-start.12
  124.2 0.7 copy-start.9

commit v5 on v0

v5 whole, which is shorter than its diff:
```python
import functools

import jax
import jax.numpy as jnp
import numpy as np
from jax import lax
from jax.experimental import pallas as pl
from jax.experimental.pallas import tpu as pltpu
from jax.sharding import PartitionSpec as P

DV = 1664
SEQ = 4096
IMG_CAP = 16
EPSILON = 1e-06
VMEM = 56 << 20
LIGHT = pl.CostEstimate(flops=1000, bytes_accessed=1000, transcendentals=0)


def folded_ring(count):
    odd = list(range(1, count, 2))
    even = list(range(0, count, 2))
    return even[:1] + odd + even[:0:-1]


def tp_shift(value, n_tp, distance):
    return lax.ppermute(value, "tp", [(i, (i + distance) % n_tp) for i in range(n_tp)])


def tp_scatter_sum(value, n_tp, axis):
    me = lax.axis_index("tp")
    width = value.shape[axis] // n_tp
    total = lax.dynamic_slice_in_dim(value, me * width, width, axis)
    for distance in range(1, n_tp):
        block = lax.dynamic_slice_in_dim(value, (me + distance) % n_tp * width, width, axis)
        total = total + tp_shift(block, n_tp, distance)
    return total


def ring_tables(n_req):
    lines = n_req // 4
    order = folded_ring(lines)
    following = {order[i]: order[(i + 1) % lines] for i in range(lines)}
    line_perm = [(z * 4 + p, following[z] * 4 + p) for z in range(lines) for p in range(4)]
    table = np.zeros((n_req, n_req), np.int32)
    for index in range(n_req):
        for step in range(lines):
            z = order[(order.index(index // 4) - step) % lines]
            for flip in range(4):
                table[index, step * 4 + flip] = z * 4 + ((index % 4) ^ flip)
    return lines, line_perm, table


def tie(*values):
    return lax.optimization_barrier(values)


def column_tile(columns):
    return 640 if columns > 640 else columns


def column_cut(columns):
    tile = column_tile(columns)
    return pl.cdiv(columns, tile) // 2 * tile


def place_rows(scratch_ref, order_ref, step, rows, pieces):
    for flip, piece in enumerate(pieces):
        start = pl.multiple_of(lax.rem(order_ref[step * 4 + flip], 4) * rows, 8)
        if piece is None:
            piece = jnp.zeros((rows, scratch_ref.shape[1]), jnp.float32)
        scratch_ref[pl.ds(start, rows), :] = piece.astype(jnp.float32)


def piece_specs(blocks, rows, tile):
    if len(blocks) == 1:
        return [pl.BlockSpec((rows, tile), lambda i, order_ref: (0, i))]
    first = blocks[0].shape[1] // tile
    return [
        pl.BlockSpec((rows, tile), lambda i, order_ref: (0, jnp.minimum(i, first - 1))),
        pl.BlockSpec((rows, tile), lambda i, order_ref: (0, jnp.maximum(i - first, 0))),
    ]


def project(order, scaled, planes, last, columns, total=None, base=None, text_len=None):
    _, positions, depth = scaled.shape
    rows = depth // 4
    tile = column_tile(columns)
    operands = [scaled]
    specs = [pl.BlockSpec(scaled.shape, lambda i, order_ref: (0, 0, 0))]
    if last:
        operands += [base, text_len, total]
        specs += [
            pl.BlockSpec(memory_space=pltpu.SMEM),
            pl.BlockSpec(memory_space=pltpu.SMEM),
            pl.BlockSpec((positions, tile), lambda i, order_ref: (0, i)),
        ]
    for _, pieces in planes:
        for piece in pieces:
            if piece is not None:
                operands += list(piece)
                specs += piece_specs(piece, rows, tile)

    def body(order_ref, scaled_ref, *refs):
        refs, out_ref, scratch_ref = list(refs[:-2]), refs[-2], refs[-1]
        column = pl.program_id(0) * tile
        if last:
            base_ref, length_ref, total_ref = refs[:3]
            refs = refs[3:]
            value = total_ref[...]
        else:
            value = jnp.zeros((positions, tile), jnp.float32)
        for step, pieces in planes:
            taken = []
            for piece in pieces:
                if piece is None:
                    taken.append(None)
                    continue
                weight = refs.pop(0)[...]
                if len(piece) == 2:
                    weight = jnp.where(column < piece[0].shape[1], weight, refs.pop(0)[...])
                taken.append(weight)
            place_rows(scratch_ref, order_ref, step, rows, taken)
            value += jnp.dot(
                scaled_ref[lax.div(order_ref[step * 4], 4)],
                scratch_ref[...].astype(jnp.bfloat16),
                preferred_element_type=jnp.float32,
            )
        if not last:
            out_ref[...] = value
            return
        position = base_ref[0] + lax.broadcasted_iota(jnp.int32, (positions, tile), 0)
        limit = jnp.zeros((positions, tile), jnp.int32)
        for request in range(text_len.shape[0]):
            limit = jnp.where(lax.div(position, SEQ) == request, length_ref[request], limit)
        there = column + lax.broadcasted_iota(jnp.int32, (positions, tile), 1) < columns
        keep = (lax.rem(position, SEQ) < limit) & there
        value = jnp.where(keep, value, 0.0).astype(jnp.bfloat16)
        for first in range(0, tile, 128):
            side = min(128, tile - first)
            identity = (
                lax.broadcasted_iota(jnp.int32, (side, side), 0)
                == lax.broadcasted_iota(jnp.int32, (side, side), 1)
            ).astype(jnp.bfloat16)
            out_ref[pl.ds(first, side), :] = lax.dot_general(
                identity,
                value[:, first : first + side],
                (((1,), (1,)), ((), ())),
                preferred_element_type=jnp.float32,
            ).astype(jnp.bfloat16)

    if last:
        out_shape = jax.ShapeDtypeStruct((columns, positions), jnp.bfloat16)
        out_spec = pl.BlockSpec((tile, positions), lambda i, order_ref: (i, 0))
    else:
        out_shape = jax.ShapeDtypeStruct((positions, columns), jnp.float32)
        out_spec = pl.BlockSpec((positions, tile), lambda i, order_ref: (0, i))
    return pl.pallas_call(
        body,
        out_shape=out_shape,
        grid_spec=pltpu.PrefetchScalarGridSpec(
            num_scalar_prefetch=1,
            grid=(pl.cdiv(columns, tile),),
            in_specs=specs,
            out_specs=out_spec,
            scratch_shapes=[pltpu.VMEM((depth, tile), jnp.float32)],
        ),
        compiler_params=pltpu.CompilerParams(vmem_limit_bytes=VMEM),
        cost_estimate=pl.CostEstimate(
            flops=2 * len(planes) * depth * columns * positions,
            bytes_accessed=2 * len(planes) * depth * columns + 6 * columns * positions,
            transcendentals=0,
        ),
    )(order, *operands)


def project_plain(order, scaled, planes, last, columns, total=None, base=None, text_len=None):
    _, positions, depth = scaled.shape
    rows = depth // 4
    if total is None:
        total = jnp.zeros((positions, columns), jnp.float32)
    for step, pieces in planes:
        source = lax.dynamic_index_in_dim(scaled, lax.div(order[step * 4], 4), 0, keepdims=False)
        for flip, piece in enumerate(pieces):
            if piece is None:
                continue
            start = lax.rem(order[step * 4 + flip], 4) * rows
            total += jnp.dot(
                lax.dynamic_slice_in_dim(source, start, rows, 1),
                jnp.concatenate(piece, axis=1),
                preferred_element_type=jnp.float32,
            )
    if not last:
        return total
    position = base[0] + jnp.arange(positions, dtype=jnp.int32)
    limit = text_len[lax.div(position, SEQ)]
    keep = lax.rem(position, SEQ) < limit
    return jnp.where(keep[:, None], total, 0.0).astype(jnp.bfloat16).T


def row_stats(patches):
    rows, _ = patches.shape

    def body(patches_ref, out_ref):
        values = patches_ref[...].astype(jnp.float32)
        sums = jnp.sum(values, axis=1, keepdims=True)
        squares = jnp.sum(values * values, axis=1, keepdims=True)
        out_ref[:, :128] = jnp.broadcast_to(sums, (rows, 128))
        out_ref[:, 128:] = jnp.broadcast_to(squares, (rows, 128))

    vmem = pl.BlockSpec(memory_space=pltpu.VMEM)
    return pl.pallas_call(
        body,
        out_shape=jax.ShapeDtypeStruct((rows, 256), jnp.float32),
        in_specs=[vmem],
        out_specs=vmem,
        compiler_params=pltpu.CompilerParams(vmem_limit_bytes=VMEM),
        cost_estimate=LIGHT,
    )(patches)


def merge(patches, stats, gain_bias, merge_weight):
    rows, width = patches.shape
    window, _, features = merge_weight.shape
    tokens = rows // window
    tile = min(features, 256)
    count = len(stats)

    def body(patches_ref, gain_bias_ref, *refs):
        stats_refs, weight_ref, out_ref, parts_ref = refs[:count], *refs[count:]

        @pl.when(pl.program_id(0) == 0)
        def _():
            sums = sum(ref[...] for ref in stats_refs) / DV
            row_mean = sums[:, 0:1]
            row_scale = lax.rsqrt(sums[:, 128:129] - row_mean * row_mean + EPSILON)
            gain_bias = gain_bias_ref[...].astype(jnp.float32)
            normed = (
                (patches_ref[...].astype(jnp.float32) - row_mean) * row_scale * gain_bias[0:1]
                + gain_bias[1:2]
            ).astype(jnp.bfloat16)
            taken = lax.broadcasted_iota(jnp.int32, (tokens, rows), 1)
            first = lax.broadcasted_iota(jnp.int32, (tokens, rows), 0) * window
            for slot in range(window):
                chosen = (taken == first + slot).astype(jnp.bfloat16)
                parts_ref[slot] = jnp.dot(
                    chosen, normed, preferred_element_type=jnp.float32
                ).astype(jnp.bfloat16)

        value = jnp.zeros((tokens, tile), jnp.float32)
        for slot in range(window):
            value += jnp.dot(
                parts_ref[slot], weight_ref[slot], preferred_element_type=jnp.float32
            )
        out_ref[...] = value

    def whole(shape):
        return pl.BlockSpec(shape, lambda i: (0, 0))

    return pl.pallas_call(
        body,
        out_shape=jax.ShapeDtypeStruct((tokens, features), jnp.float32),
        grid=(pl.cdiv(features, tile),),
        in_specs=[whole((rows, width)), whole((2, width))]
        + [whole((rows, 256))] * count
        + [pl.BlockSpec((window, width, tile), lambda i: (0, 0, i))],
        out_specs=pl.BlockSpec((tokens, tile), lambda i: (0, i)),
        scratch_shapes=[pltpu.VMEM((window, tokens, width), jnp.bfloat16)],
        compiler_params=pltpu.CompilerParams(vmem_limit_bytes=VMEM),
        cost_estimate=LIGHT,
    )(patches, gain_bias, *stats, merge_weight)


def combine(tp_index, texts, images, gain_planes):
    n_tp = len(texts)
    positions, width = texts[0].shape
    slots = images[0].shape[0]
    lines, _, depth = gain_planes.shape
    share = lines // n_tp
    corner = width // 128 * 128

    def body(index_ref, gain_ref, *refs):
        text_refs, image_refs = refs[:n_tp], refs[n_tp : 2 * n_tp]
        out_ref, value_ref = refs[2 * n_tp :]
        code = image_refs[0][:, corner : corner + 128].astype(jnp.float32).T
        high = code[width - corner : width - corner + 1]
        low = code[width - corner + 1 : width - corner + 2]
        local = high * 256.0 + low - 1.0
        place = lax.broadcasted_iota(jnp.int32, (positions, slots), 0).astype(jnp.float32)
        hit = jnp.where(local == place, 1.0, 0.0)
        covered = jnp.max(hit, axis=1, keepdims=True)
        hit = hit.astype(jnp.bfloat16)
        squares = jnp.zeros((positions, 1), jnp.float32)
        for distance in range(n_tp):
            first = lax.rem(index_ref[0] + n_tp - distance, n_tp) * share
            image = jnp.dot(hit, image_refs[distance][...], preferred_element_type=jnp.float32)
            value = jnp.where(
                covered > 0.0, image[:, :width], text_refs[distance][...].astype(jnp.float32)
            )
            squares += jnp.sum(value * value, axis=1, keepdims=True)
            for piece in range(share):
                value_ref[first + piece] = value[:, piece * depth : (piece + 1) * depth]
        scale = lax.rsqrt(squares / (width * n_tp) + EPSILON)
        for line in range(lines):
            out_ref[line] = (
                value_ref[line] * scale * gain_ref[line].astype(jnp.float32)
            ).astype(out_ref.dtype)

    vmem = pl.BlockSpec(memory_space=pltpu.VMEM)
    return pl.pallas_call(
        body,
        out_shape=jax.ShapeDtypeStruct((lines, positions, depth), jnp.bfloat16),
        in_specs=[pl.BlockSpec(memory_space=pltpu.SMEM)] + [vmem] * (1 + 2 * n_tp),
        out_specs=vmem,
        scratch_shapes=[pltpu.VMEM((lines, positions, depth), jnp.float32)],
        compiler_params=pltpu.CompilerParams(vmem_limit_bytes=VMEM),
        cost_estimate=LIGHT,
    )(tp_index, gain_planes, *texts, *images)


def shards(
    n_req, n_tp,
    patches, ln_gain, ln_bias, merge_weight, text_rows, norm_gain, qkv_weight, token_pos, text_len,
):
    row_count, width = text_rows.shape
    me = lax.axis_index("req")
    tp_index = lax.axis_index("tp").reshape(1)
    lines, line_perm, table = ring_tables(n_req)
    x_perm = [(i, i ^ 1) for i in range(n_req)]
    y_perm = [(i, i ^ 2) for i in range(n_req)]
    rows, columns = qkv_weight.shape
    cut = column_cut(columns)
    order = lax.dynamic_slice_in_dim(jnp.asarray(table), me, 1, 0).reshape(-1)

    def along_line(block):
        return lax.ppermute(block, "req", line_perm)

    def to_sides(block):
        return lax.ppermute(block, "req", x_perm), lax.ppermute(block, "req", y_perm)

    def to_corner(step):
        by_x, by_y = sides[step]
        if step >= lines - 2 and cut:
            return (
                lax.ppermute(by_y[:, :cut], "req", x_perm),
                lax.ppermute(by_x[:, cut:], "req", y_perm),
            )
        if step % 2:
            return (lax.ppermute(by_x, "req", y_perm),)
        return (lax.ppermute(by_y, "req", x_perm),)

    held = [qkv_weight]
    held.append(along_line(held[0]))
    sides = [to_sides(held[0])]
    corners = []
    stats_own = row_stats(patches)
    stats = [stats_own] + [tp_shift(stats_own, n_tp, d) for d in range(1, n_tp)]
    gain_bias = jnp.stack([ln_gain, ln_bias])
    texts = [text_rows] + [tp_shift(text_rows, n_tp, d) for d in range(1, n_tp)]

    token_count = token_pos.shape[0]
    target = lax.div(token_pos, row_count)
    same = target[:, None] == target[None, :]
    ids = jnp.arange(token_count, dtype=jnp.int32)
    before = jnp.sum((same & (ids[None, :] < ids[:, None])).astype(jnp.int32), axis=1)
    slot = target * IMG_CAP + before
    slot_count = n_req * IMG_CAP
    place = (
        jnp.arange(slot_count, dtype=jnp.int32)[:, None] == slot[None, :]
    ).astype(jnp.bfloat16)
    code = lax.rem(token_pos, row_count) + 1
    code_cols = jnp.stack([lax.div(code, 256), lax.rem(code, 256)], axis=1).astype(jnp.bfloat16)
    gain_planes = norm_gain.reshape(lines, 1, 4 * rows)

    stats, held[1], sides[0], gain_bias, gain_planes = tie(
        stats, held[1], sides[0], gain_bias, gain_planes
    )
    held.append(along_line(held[1]))
    sides.append(to_sides(held[1]))
    corners.append(to_corner(0))
    partial_value = merge(patches, stats, gain_bias, merge_weight)

    partial_value, held[2], sides[1] = tie(partial_value, held[2], sides[1])
    held.append(along_line(held[2]))
    sides.append(to_sides(held[2]))
    corners.append(to_corner(1))
    merged = tp_scatter_sum(partial_value, n_tp, 1).astype(jnp.bfloat16)
    padding = (-width - 2) % 128
    payload = jnp.concatenate(
        [merged, code_cols, jnp.zeros((token_count, padding), jnp.bfloat16)], axis=1
    )
    outgoing = jnp.dot(place, payload, preferred_element_type=jnp.float32).astype(jnp.bfloat16)

    outgoing, held[3], sides[2], texts = tie(outgoing, held[3], sides[2], texts)
    sides.append(to_sides(held[3]))
    arrived = lax.all_to_all(
        outgoing.reshape(n_req, IMG_CAP, -1), "req", split_axis=0, concat_axis=0
    ).reshape(slot_count, -1)

    arrived, sides[3], corners = tie(arrived, sides[3], corners)
    for step in range(4, lines):
        held.append(along_line(held[step - 1]))
        sides.append(to_sides(held[step]))
    for step in range(2, lines):
        corners.append(to_corner(step))
    images = [arrived] + [tp_shift(arrived, n_tp, d) for d in range(1, n_tp)]
    scaled = combine(tp_index, texts, images, gain_planes)

    early, late = [], []
    for step in range(lines):
        pieces = [(held[step],), (sides[step][0],), (sides[step][1],)]
        if step < lines - 2:
            early.append((step, pieces + [corners[step]]))
        else:
            early.append((step, pieces + [None]))
            late.append((step, [None, None, None, corners[step]]))
    run = project if rows % 8 == 0 else project_plain
    total = run(order, scaled, early, False, columns)
    base = (me * row_count).reshape(1)
    return run(order, scaled, late, True, columns, total=total, base=base, text_len=text_len).T


def solution(mesh):
    placed = (
        P("req", "tp"),
        P("tp"),
        P("tp"),
        P(None, "tp", None),
        P("req", "tp"),
        P(),
        P("req", "tp"),
        P("req"),
        P(),
    )
    body = functools.partial(shards, mesh.shape["req"], mesh.shape["tp"])
    return jax.shard_map(
        body, mesh=mesh, in_specs=placed, out_specs=P("req", "tp"), check_vma=False
    )
```

time: 263 us -> 130 us (0.49)
  waiting for transfers between devices: 190 us -> 42.5 us
  Pallas kernels: 0 us -> 41 us
  starting transfers between devices: 0.31 us -> 26.8 us
  matrix products: 18.9 us -> 1.06 us
  blocking collectives: 17.5 us -> 0 us
  between operations: 13.8 us -> 0.19 us
  other arithmetic: 6.37 us -> 2.65 us
    all_gather x3 -> x0, waiting for transfers between devices: 178 us -> none  [the longest x1 116 us: shards(): whole_weight = lax.all_gather(qkv_weight, 'req', axis=0, tiled=True)]
    ppermute x0 -> x21, waiting for transfers between devices: none -> 42.5 us  [the longest x1 15.5 us: to_corner(): return (lax.ppermute(by_y, 'req', x_perm),)]
    pallas_call x0 -> x5, Pallas kernels: none -> 41 us  [the longest x2 23.3 us: project(): pl.pallas_call(body, out_shape=out_shape, grid_spec=pltpu.PrefetchScalarG...]
    ppermute x0 -> x21, starting transfers between devices: none -> 22.2 us  [the longest x3 6.84 us: along_line(): return lax.ppermute(block, 'req', line_perm)]
    dot_general x2 -> x1, matrix products: 18.9 us -> 1.06 us  [shards(): jnp.dot(place, payload, preferred_element_type=jnp.float32)]
    unnamed x1 -> x0, blocking collectives: 14.9 us -> none
    scatter x2 -> x0, local copies, waits for them, and re-layouts: 13.1 us -> none  [shards(): text_rows.at[jnp.where(inside, local_pos, row_count)]]
    unnamed x5 -> x0, waiting for transfers between devices: 11.4 us -> none
  transfers between devices with their start and end apart: 4 -> 22, of which waited for: 4 -> 8; matrix products, arithmetic and copies ran while one was open for 1% -> 11% of each run, Pallas kernels for 0% -> 24%
where the time goes in v5:
time: 130 us; the launch traced here: 129 us
  waiting for transfers between devices  42.5 us (33%)
  Pallas kernels  41 us (32%)
  starting transfers between devices  26.8 us (21%)
  local copies, waits for them, and re-layouts  14.5 us (11%)
  other arithmetic  2.65 us (2%)
    pallas_call x2, Pallas kernels, project(): pl.pallas_call(body, out_shape=out_shape, grid_spec=pltpu.PrefetchScalarG...  23.3 us
    ppermute x1, waiting for transfers between devices, to_corner(): return (lax.ppermute(by_y, 'req', x_perm),)  15.5 us
    ppermute x4, waiting for transfers between devices, to_sides(): lax.ppermute(block, 'req', y_perm)  10.4 us
    ppermute x4, waiting for transfers between devices, to_sides(): lax.ppermute(block, 'req', x_perm)  9.91 us
    pallas_call x1, Pallas kernels, merge(): pl.pallas_call(body, out_shape=jax.ShapeDtypeStruct((tokens, features), j...  9.64 us
    ppermute x3, starting transfers between devices, along_line(): return lax.ppermute(block, 'req', line_perm)  6.84 us
    ppermute x3, waiting for transfers between devices, along_line(): return lax.ppermute(block, 'req', line_perm)  6.64 us
    pallas_call x1, Pallas kernels, combine(): pl.pallas_call(body, out_shape=jax.ShapeDtypeStruct((lines, positions, de...  5.86 us
  transfers between devices with their start and end apart: 22, of which 8 were waited for; matrix products, arithmetic and copies ran while one was open for 11% of the time, Pallas kernels for 24%

profile of v5, /device:TPU:0, one launch (start us, length us, event | category | flops | bytes accessed | tf_op | source)
XLA Modules:
  0.0 128.8 jit_solution(17536899277740599547)
XLA Ops:
  0.0 3.0 %collective-permute-start.1 = (bf16[104,2496]{1,0:T(8,128)(2,1)}, bf16[104,2496]{1,0:T(8,128)(2,1)S(1)}, u32[]{:S(2)}, u32[]{:S(2)}) collective-permute-start(bf16[104,2496]{1,0:T(8,128)(2,1)} %refs_0_.1), channel_id=1, source_target_pairs={{0,8},{2,10},{4,12},{6,14},{8,24},{10,26},{12,28},{14,30},{16,0},{... | collective-permute-start | bytes 1557512 | tf_op jit(solution)/shard_map/ppermute | solution.py:335
  3.0 1.5 %collective-permute-start.2 = (bf16[104,2496]{1,0:T(8,128)(2,1)}, bf16[104,2496]{1,0:T(8,128)(2,1)S(1)}, u32[]{:S(2)}, u32[]{:S(2)}) collective-permute-start(bf16[104,2496]{1,0:T(8,128)(2,1)} %refs_0_.1), channel_id=1, source_target_pairs={{0,2},{2,0},{4,6},{6,4},{8,10},{10,8},{12,14},{14,12},{16,18},{18,... | collective-permute-start | bytes 1557512 | tf_op jit(solution)/shard_map/ppermute | solution.py:338
  4.5 1.5 %collective-permute-start.3 = (bf16[104,2496]{1,0:T(8,128)(2,1)}, bf16[104,2496]{1,0:T(8,128)(2,1)S(1)}, u32[]{:S(2)}, u32[]{:S(2)}) collective-permute-start(bf16[104,2496]{1,0:T(8,128)(2,1)} %refs_0_.1), channel_id=1, source_target_pairs={{0,4},{2,6},{4,0},{6,2},{8,12},{10,14},{12,8},{14,10},{16,20},{18,... | collective-permute-start | bytes 1557512 | tf_op jit(solution)/shard_map/ppermute | solution.py:338
  6.0 2.2 %shard_map.118.refs_0_ = f32[448,256]{1,0:T(8,128)} custom-call(bf16[448,832]{1,0:T(8,128)(2,1)} %patches_ref.3), custom_call_target="tpu_custom_call" | custom-call | flops 1000 | bytes 1000 | tf_op jit(solution)/shard_map/pallas_call | solution.py:211
  8.2 0.0 collective-permute-start
  8.2 0.7 stack.19
  8.9 0.7 stack.20
  9.6 0.8 reshape.23
  10.4 0.6 pad_maximum_fusion.gain_bias_ref
  11.0 0.0 collective-permute-done.refs_1_
  11.0 5.4 %collective-permute-done.1.refs_4_ = bf16[104,2496]{1,0:T(8,128)(2,1)S(1)} collective-permute-done((bf16[104,2496]{1,0:T(8,128)(2,1)}, bf16[104,2496]{1,0:T(8,128)(2,1)S(1)}, u32[]{:S(2)}, u32[]{:S(2)}) %collective-permute-start.1) | collective-permute-done | bytes 519200 | tf_op jit(solution)/shard_map/ppermute | solution.py:335
  16.3 0.4 collective-permute-done.2.refs_1_
  16.8 1.2 collective-permute-done.3.refs_2_
  18.0 2.6 %collective-permute-start.4 = (bf16[104,2496]{1,0:T(8,128)(2,1)S(1)}, bf16[104,2496]{1,0:T(8,128)(2,1)S(1)}, u32[]{:S(2)}, u32[]{:S(2)}) collective-permute-start(bf16[104,2496]{1,0:T(8,128)(2,1)S(1)} %collective-permute-done.1.refs_4_), channel_id=1, source_target_pairs={{0,8},{2,10},{4,12},{6,14},{8,24},{10,26},{12,28},{14,30},{16,0},{... | collective-permute-start | bytes 1557512 | tf_op jit(solution)/shard_map/ppermute | solution.py:335
  20.6 0.5 collective-permute-start.5
  21.1 1.5 %collective-permute-start.6 = (bf16[104,2496]{1,0:T(8,128)(2,1)S(1)}, bf16[104,2496]{1,0:T(8,128)(2,1)}, u32[]{:S(2)}, u32[]{:S(2)}) collective-permute-start(bf16[104,2496]{1,0:T(8,128)(2,1)S(1)} %collective-permute-done.1.refs_4_), channel_id=1, source_target_pairs={{0,4},{2,6},{4,0},{6,2},{8,12},{10,14},{12,8},{14,10},{16,20},{18,... | collective-permute-start | bytes 1557512 | tf_op jit(solution)/shard_map/ppermute | solution.py:338
  22.7 0.0 collective-permute-start.11
  22.7 0.7 convert_bitcast_fusion.1
  23.3 0.2 convert_reduce_fusion
  23.5 0.0 copy-start.1
  23.5 9.6 %shard_map.119 = f32[112,1664]{1,0:T(8,128)} custom-call(bf16[448,832]{1,0:T(8,128)(2,1)} %patches_ref.3, bf16[2,832]{1,0:T(2,128)(2,1)} %pad_maximum_fusion.gain_bias_ref, f32[448,256]{1,0:T(8,128)} %shard_map.118.refs_0_, f32[448,256]{1,0:T(8,128)} %copy-done.3, bf16[4,832,1664]{2,1,0:T(8,128)(2,1)} %refs_2_.1), custom_call_target="tpu_custom_call" | custom-call | flops 1000 | bytes 1000 | tf_op jit(solution)/shard_map/pallas_call | solution.py:259
  33.2 0.0 collective-permute-done.5.refs_5_
  33.2 0.8 copy-done.13
  34.0 1.2 constant_dynamic-slice_fusion
  35.2 0.6 collective-permute-start.7
  35.8 0.5 collective-permute-start.10
  36.3 1.2 collective-permute-start.8
  37.5 0.7 collective-permute-start.9
  38.2 0.1 copy.26
  38.3 0.1 copy.25
  38.5 0.1 pad.3.clone
  38.6 1.2 add_convert_fusion
  39.8 1.1 convolution_convert_fusion
  40.8 9.2 %collective-permute-done.10.refs_10_ = bf16[104,2496]{1,0:T(8,128)(2,1)S(1)} collective-permute-done((bf16[104,2496]{1,0:T(8,128)(2,1)}, bf16[104,2496]{1,0:T(8,128)(2,1)S(1)}, u32[]{:S(2)}, u32[]{:S(2)}) %collective-permute-start.10) | collective-permute-done | bytes 519200 | tf_op jit(solution)/shard_map/ppermute | solution.py:338
  50.1 1.3 collective-permute-done.8.refs_11_
  51.3 0.4 collective-permute-done.9.refs_9_
  51.7 4.6 %all-to-all-start = ((bf16[16,16,896]{2,1,0:T(8,128)(2,1)}), bf16[16,16,896]{2,1,0:T(8,128)(2,1)S(1)}, u32[]{:S(2)}, u32[]{:S(2)}) async-start(bf16[16,16,896]{2,1,0:T(8,128)(2,1)} %bitcast.4), calls=%async_computation | async-start | bytes 917504 | tf_op jit(solution)/shard_map/all_to_all | solution.py:395
  56.3 1.9 %collective-permute-start.14 = (bf16[104,2496]{1,0:T(8,128)(2,1)}, bf16[104,2496]{1,0:T(8,128)(2,1)S(1)}, u32[]{:S(2)}, u32[]{:S(2)}) collective-permute-start(bf16[104,2496]{1,0:T(8,128)(2,1)} %copy-done.12), channel_id=1, source_target_pairs={{0,2},{2,0},{4,6},{6,4},{8,10},{10,8},{12,14},{14,12},{16,18},{18,... | collective-permute-start | bytes 1557512 | tf_op jit(solution)/shard_map/ppermute | solution.py:349
  58.2 1.5 %collective-permute-start.15 = (bf16[104,2496]{1,0:T(8,128)(2,1)}, bf16[104,2496]{1,0:T(8,128)(2,1)S(1)}, u32[]{:S(2)}, u32[]{:S(2)}) collective-permute-start(bf16[104,2496]{1,0:T(8,128)(2,1)} %collective-permute-done.5.refs_5_), channel_id=1, source_target_pairs={{0,4},{2,6},{4,0},{6,2},{8,12},{10,14},{12,8},{14,10},{16,20},{18,... | collective-permute-start | bytes 1557512 | tf_op jit(solution)/shard_map/ppermute | solution.py:348
  59.7 0.6 collective-permute-start.12
  60.3 0.2 collective-permute-start.13
  60.4 15.5 %collective-permute-done.14.refs_3_ = bf16[104,2496]{1,0:T(8,128)(2,1)S(1)} collective-permute-done((bf16[104,2496]{1,0:T(8,128)(2,1)}, bf16[104,2496]{1,0:T(8,128)(2,1)S(1)}, u32[]{:S(2)}, u32[]{:S(2)}) %collective-permute-start.14) | collective-permute-done | bytes 519200 | tf_op jit(solution)/shard_map/ppermute | solution.py:349
  76.0 9.1 %collective-permute-done.12.refs_12_ = bf16[104,2496]{1,0:T(8,128)(2,1)S(1)} collective-permute-done((bf16[104,2496]{1,0:T(8,128)(2,1)}, bf16[104,2496]{1,0:T(8,128)(2,1)S(1)}, u32[]{:S(2)}, u32[]{:S(2)}) %collective-permute-start.12) | collective-permute-done | bytes 519200 | tf_op jit(solution)/shard_map/ppermute | solution.py:338
  85.1 0.8 copy-done.9
  85.9 0.1 collective-permute-start.16
  86.0 1.3 %fusion.9.order_ref = s32[16]{0:T(128)} fusion(s32[16,16]{1,0:T(8,128)} %constant.51.clone, s32[]{:T(128)S(6)} %select_n.16), kind=kLoop, calls=%fused_computation.23 | loop fusion | bytes 132 | tf_op jit(solution)/shard_map/reshape | solution.py:332
  87.3 0.6 copy.27.gain_ref
  87.9 1.3 copy.28.refs_0_
  89.2 1.3 %copy.29.refs_1_ = bf16[512,832]{1,0:T(8,128)(2,1)} copy(bf16[512,832]{0,1:T(8,128)(2,1)S(1)} %collective-permute-done.11) | data formatting | bytes 1703936 | tf_op jit(solution)/shard_map/optimization_barrier | solution.py:54
  90.5 1.2 collective-permute-start.17
  91.7 1.0 slice.13
  92.7 1.5 %collective-permute-start.18 = (bf16[104,1216]{1,0:T(8,128)(2,1)S(1)}, bf16[104,1216]{1,0:T(8,128)(2,1)S(1)}, u32[]{:S(2)}, u32[]{:S(2)}) collective-permute-start(bf16[104,1216]{1,0:T(8,128)(2,1)S(1)} %slice.13), channel_id=1, source_target_pairs={{0,4},{2,6},{4,0},{6,2},{8,12},{10,14},{12,8},{14,10},{16,20},{18,... | collective-permute-start | bytes 758792 | tf_op jit(solution)/shard_map/ppermute | solution.py:345
  94.2 1.0 slice.14
  95.2 1.0 collective-permute-start.19
  96.1 1.0 slice.15
  97.1 0.6 collective-permute-start.20
  97.7 0.8 copy-done.2
  98.5 5.9 %shard_map.120.scaled_ref = bf16[4,512,416]{2,1,0:T(8,128)(2,1)} custom-call(s32[1]{0:T(128)} %bitcast.1.index_ref, bf16[4,1,416]{2,1,0:T(2,128)(2,1)} %copy.27.gain_ref, bf16[512,832]{1,0:T(8,128)(2,1)} %copy.28.refs_0_, bf16[512,832]{1,0:T(8,128)(2,1)} %copy.29.refs_1_, bf16[256,896]{1,0:T(8,128)(2,1)} %bitcast.12, bf16[256,896]{1,0:T(8,128)(2,1)} %copy-done.2), custom_call_target="tpu_custom_call" | custom-call | flops 1000 | bytes 1000 | tf_op jit(solution)/shard_map/pallas_call | solution.py:309
  104.4 13.0 %shard_map.121.refs_2_ = f32[512,2496]{1,0:T(8,128)} custom-call(s32[16]{0:T(128)} %fusion.9.order_ref, bf16[4,512,416]{2,1,0:T(8,128)(2,1)} %shard_map.120.scaled_ref, bf16[104,2496]{1,0:T(8,128)(2,1)} %refs_0_.1, bf16[104,2496]{1,0:T(8,128)(2,1)} %copy-done.11, bf16[104,2496]{1,0:T(8,128)(2,1)} %copy-done.12, bf16[104,2496]{1,0:T(8,128)(2,1)} %copy-done.14, ...), custom_call_target="tpu_custom_call" | custom-call | flops 4253024256 | bytes 15974400 | tf_op jit(solution)/shard_map/pallas_call | solution.py:157
  117.5 0.7 copy-done.5
  118.2 0.1 copy-done.4
  118.3 0.1 copy-done.7
  118.3 0.2 copy-done.6
  118.5 10.3 %shard_map.122 = bf16[2496,512]{1,0:T(8,128)(2,1)} custom-call(s32[16]{0:T(128)} %fusion.9.order_ref, bf16[4,512,416]{2,1,0:T(8,128)(2,1)} %shard_map.120.scaled_ref, s32[1]{0:T(128)} %bitcast.6.refs_0_, s32[2]{0:T(128)} %refs_1_.1, f32[512,2496]{1,0:T(8,128)} %shard_map.121.refs_2_, bf16[104,1280]{1,0:T(8,128)(2,1)} %copy-done.4, ...), custom_call_target="tpu_custom_call" | custom-call | flops 2126512128 | bytes 11821056 | tf_op jit(solution)/shard_map/pallas_call | solution.py:157
  (40 shorter events, 0.1 us)
Async XLA Ops:
  0.0 16.3 %collective-permute-start.1 = (bf16[104,2496]{1,0:T(8,128)(2,1)}, bf16[104,2496]{1,0:T(8,128)(2,1)S(1)}, u32[]{:S(2)}, u32[]{:S(2)}) collective-permute-start(bf16[104,2496]{1,0:T(8,128)(2,1)} %refs_0_.1), channel_id=1, source_target_pairs={{0,8},{2,10},{4,12},{6,14},{8,24},{10,26},{12,28},{14,30},{16,0},{... | collective-permute-start | bytes 1557512 | tf_op jit(solution)/shard_map/ppermute | solution.py:335
  3.0 13.8 %collective-permute-start.2 = (bf16[104,2496]{1,0:T(8,128)(2,1)}, bf16[104,2496]{1,0:T(8,128)(2,1)S(1)}, u32[]{:S(2)}, u32[]{:S(2)}) collective-permute-start(bf16[104,2496]{1,0:T(8,128)(2,1)} %refs_0_.1), channel_id=1, source_target_pairs={{0,2},{2,0},{4,6},{6,4},{8,10},{10,8},{12,14},{14,12},{16,18},{18,... | collective-permute-start | bytes 1557512 | tf_op jit(solution)/shard_map/ppermute | solution.py:338
  4.5 13.5 %collective-permute-start.3 = (bf16[104,2496]{1,0:T(8,128)(2,1)}, bf16[104,2496]{1,0:T(8,128)(2,1)S(1)}, u32[]{:S(2)}, u32[]{:S(2)}) collective-permute-start(bf16[104,2496]{1,0:T(8,128)(2,1)} %refs_0_.1), channel_id=1, source_target_pairs={{0,4},{2,6},{4,0},{6,2},{8,12},{10,14},{12,8},{14,10},{16,20},{18,... | collective-permute-start | bytes 1557512 | tf_op jit(solution)/shard_map/ppermute | solution.py:338
  8.2 2.8 %collective-permute-start = (f32[448,256]{1,0:T(8,128)}, f32[448,256]{1,0:T(8,128)S(1)}, u32[]{:S(2)}, u32[]{:S(2)}) collective-permute-start(f32[448,256]{1,0:T(8,128)} %shard_map.118.refs_0_), channel_id=1, source_target_pairs={{0,1},{1,0},{2,3},{3,2},{4,5},{5,4},{6,7},{7,6},{8,9},{9,8},{10,11... | collective-permute-start | bytes 1376264 | tf_op jit(solution)/shard_map/ppermute | solution.py:26
  11.0 12.5 %copy-start.3 = (f32[448,256]{1,0:T(8,128)}, f32[448,256]{1,0:T(8,128)S(1)}, u32[]{:S(2)}) copy-start(f32[448,256]{1,0:T(8,128)S(1)} %collective-permute-done.refs_1_) | copy-start | bytes 1376260
  16.3 16.8 %copy-start.10 = (bf16[104,2496]{1,0:T(8,128)(2,1)}, bf16[104,2496]{1,0:T(8,128)(2,1)S(1)}, u32[]{:S(2)}) copy-start(bf16[104,2496]{1,0:T(8,128)(2,1)S(1)} %collective-permute-done.1.refs_4_) | copy-start | bytes 1557508
  16.8 4.3 %copy-start.11 = (bf16[104,2496]{1,0:T(8,128)(2,1)}, bf16[104,2496]{1,0:T(8,128)(2,1)S(1)}, u32[]{:S(2)}) copy-start(bf16[104,2496]{1,0:T(8,128)(2,1)S(1)} %collective-permute-done.2.refs_1_) | copy-start | bytes 1557508
  18.0 5.3 %copy-start.12 = (bf16[104,2496]{1,0:T(8,128)(2,1)}, bf16[104,2496]{1,0:T(8,128)(2,1)S(1)}, u32[]{:S(2)}) copy-start(bf16[104,2496]{1,0:T(8,128)(2,1)S(1)} %collective-permute-done.3.refs_2_) | copy-start | bytes 1557508
  18.0 15.2 %collective-permute-start.4 = (bf16[104,2496]{1,0:T(8,128)(2,1)S(1)}, bf16[104,2496]{1,0:T(8,128)(2,1)S(1)}, u32[]{:S(2)}, u32[]{:S(2)}) collective-permute-start(bf16[104,2496]{1,0:T(8,128)(2,1)S(1)} %collective-permute-done.1.refs_4_), channel_id=1, source_target_pairs={{0,8},{2,10},{4,12},{6,14},{8,24},{10,26},{12,28},{14,30},{16,0},{... | collective-permute-start | bytes 1557512 | tf_op jit(solution)/shard_map/ppermute | solution.py:335
  20.6 12.6 %collective-permute-start.5 = (bf16[104,2496]{1,0:T(8,128)(2,1)S(1)}, bf16[104,2496]{1,0:T(8,128)(2,1)}, u32[]{:S(2)}, u32[]{:S(2)}) collective-permute-start(bf16[104,2496]{1,0:T(8,128)(2,1)S(1)} %collective-permute-done.1.refs_4_), channel_id=1, source_target_pairs={{0,2},{2,0},{4,6},{6,4},{8,10},{10,8},{12,14},{14,12},{16,18},{18,... | collective-permute-start | bytes 1557512 | tf_op jit(solution)/shard_map/ppermute | solution.py:338
  21.1 12.9 %collective-permute-start.6 = (bf16[104,2496]{1,0:T(8,128)(2,1)S(1)}, bf16[104,2496]{1,0:T(8,128)(2,1)}, u32[]{:S(2)}, u32[]{:S(2)}) collective-permute-start(bf16[104,2496]{1,0:T(8,128)(2,1)S(1)} %collective-permute-done.1.refs_4_), channel_id=1, source_target_pairs={{0,4},{2,6},{4,0},{6,2},{8,12},{10,14},{12,8},{14,10},{16,20},{18,... | collective-permute-start | bytes 1557512 | tf_op jit(solution)/shard_map/ppermute | solution.py:338
  22.7 18.2 %collective-permute-start.11 = (bf16[512,832]{0,1:T(8,128)(2,1)}, bf16[512,832]{0,1:T(8,128)(2,1)S(1)}, u32[]{:S(2)}, u32[]{:S(2)}) collective-permute-start(bf16[512,832]{0,1:T(8,128)(2,1)} %param.14), channel_id=1, source_target_pairs={{0,1},{1,0},{2,3},{3,2},{4,5},{5,4},{6,7},{7,6},{8,9},{9,8},{10,11... | collective-permute-start | bytes 2555912 | tf_op jit(solution)/shard_map/ppermute | solution.py:26
  23.5 64.4 %copy-start.1 = (bf16[512,832]{0,1:T(8,128)(2,1)S(1)}, bf16[512,832]{0,1:T(8,128)(2,1)}, u32[]{:S(2)}) copy-start(bf16[512,832]{0,1:T(8,128)(2,1)} %param.14) | copy-start | bytes 2555908
  33.2 0.8 copy-start.13
  35.2 3.4 %collective-permute-start.7 = (f32[112,832]{1,0:T(8,128)S(1)}, f32[112,832]{1,0:T(8,128)S(1)}, u32[]{:S(2)}, u32[]{:S(2)}) collective-permute-start(f32[112,832]{1,0:T(8,128)S(1)} %constant_dynamic-slice_fusion), channel_id=1, source_target_pairs={{0,1},{1,0},{2,3},{3,2},{4,5},{5,4},{6,7},{7,6},{8,9},{9,8},{10,11... | collective-permute-start | bytes 1118216 | tf_op jit(solution)/shard_map/ppermute | solution.py:26
  35.8 14.3 %collective-permute-start.10 = (bf16[104,2496]{1,0:T(8,128)(2,1)}, bf16[104,2496]{1,0:T(8,128)(2,1)S(1)}, u32[]{:S(2)}, u32[]{:S(2)}) collective-permute-start(bf16[104,2496]{1,0:T(8,128)(2,1)} %copy-done.13), channel_id=1, source_target_pairs={{0,4},{2,6},{4,0},{6,2},{8,12},{10,14},{12,8},{14,10},{16,20},{18,... | collective-permute-start | bytes 1557512 | tf_op jit(solution)/shard_map/ppermute | solution.py:338
  36.3 15.1 %collective-permute-start.8 = (bf16[104,2496]{1,0:T(8,128)(2,1)}, bf16[104,2496]{1,0:T(8,128)(2,1)}, u32[]{:S(2)}, u32[]{:S(2)}) collective-permute-start(bf16[104,2496]{1,0:T(8,128)(2,1)} %copy-done.13), channel_id=1, source_target_pairs={{0,8},{2,10},{4,12},{6,14},{8,24},{10,26},{12,28},{14,30},{16,0},{... | collective-permute-start | bytes 1557512 | tf_op jit(solution)/shard_map/ppermute | solution.py:335
  37.5 14.2 %collective-permute-start.9 = (bf16[104,2496]{1,0:T(8,128)(2,1)}, bf16[104,2496]{1,0:T(8,128)(2,1)}, u32[]{:S(2)}, u32[]{:S(2)}) collective-permute-start(bf16[104,2496]{1,0:T(8,128)(2,1)} %copy-done.13), channel_id=1, source_target_pairs={{0,2},{2,0},{4,6},{6,4},{8,10},{10,8},{12,14},{14,12},{16,18},{18,... | collective-permute-start | bytes 1557512 | tf_op jit(solution)/shard_map/ppermute | solution.py:338
  50.1 54.3 %copy-start.8 = (bf16[104,2496]{1,0:T(8,128)(2,1)}, bf16[104,2496]{1,0:T(8,128)(2,1)S(1)}, u32[]{:S(2)}) copy-start(bf16[104,2496]{1,0:T(8,128)(2,1)S(1)} %collective-permute-done.10.refs_10_) | copy-start | bytes 1557508
  51.7 34.2 %all-to-all-start = ((bf16[16,16,896]{2,1,0:T(8,128)(2,1)}), bf16[16,16,896]{2,1,0:T(8,128)(2,1)S(1)}, u32[]{:S(2)}, u32[]{:S(2)}) async-start(bf16[16,16,896]{2,1,0:T(8,128)(2,1)} %bitcast.4), calls=%async_computation | async-start | bytes 917504 | tf_op jit(solution)/shard_map/all_to_all | solution.py:395
  56.3 19.6 %collective-permute-start.14 = (bf16[104,2496]{1,0:T(8,128)(2,1)}, bf16[104,2496]{1,0:T(8,128)(2,1)S(1)}, u32[]{:S(2)}, u32[]{:S(2)}) collective-permute-start(bf16[104,2496]{1,0:T(8,128)(2,1)} %copy-done.12), channel_id=1, source_target_pairs={{0,2},{2,0},{4,6},{6,4},{8,10},{10,8},{12,14},{14,12},{16,18},{18,... | collective-permute-start | bytes 1557512 | tf_op jit(solution)/shard_map/ppermute | solution.py:349
  58.2 17.7 %collective-permute-start.15 = (bf16[104,2496]{1,0:T(8,128)(2,1)}, bf16[104,2496]{1,0:T(8,128)(2,1)S(1)}, u32[]{:S(2)}, u32[]{:S(2)}) collective-permute-start(bf16[104,2496]{1,0:T(8,128)(2,1)} %collective-permute-done.5.refs_5_), channel_id=1, source_target_pairs={{0,4},{2,6},{4,0},{6,2},{8,12},{10,14},{12,8},{14,10},{16,20},{18,... | collective-permute-start | bytes 1557512 | tf_op jit(solution)/shard_map/ppermute | solution.py:348
  59.7 25.4 %collective-permute-start.12 = (bf16[104,2496]{1,0:T(8,128)(2,1)}, bf16[104,2496]{1,0:T(8,128)(2,1)S(1)}, u32[]{:S(2)}, u32[]{:S(2)}) collective-permute-start(bf16[104,2496]{1,0:T(8,128)(2,1)} %collective-permute-done.8.refs_11_), channel_id=1, source_target_pairs={{0,2},{2,0},{4,6},{6,4},{8,10},{10,8},{12,14},{14,12},{16,18},{18,... | collective-permute-start | bytes 1557512 | tf_op jit(solution)/shard_map/ppermute | solution.py:338
  60.3 25.6 %collective-permute-start.13 = (bf16[104,2496]{1,0:T(8,128)(2,1)}, bf16[104,2496]{1,0:T(8,128)(2,1)}, u32[]{:S(2)}, u32[]{:S(2)}) collective-permute-start(bf16[104,2496]{1,0:T(8,128)(2,1)} %collective-permute-done.8.refs_11_), channel_id=1, source_target_pairs={{0,4},{2,6},{4,0},{6,2},{8,12},{10,14},{12,8},{14,10},{16,20},{18,... | collective-permute-start | bytes 1557512 | tf_op jit(solution)/shard_map/ppermute | solution.py:338
  76.0 9.1 %copy-start.14 = (bf16[104,2496]{1,0:T(8,128)(2,1)}, bf16[104,2496]{1,0:T(8,128)(2,1)S(1)}, u32[]{:S(2)}) copy-start(bf16[104,2496]{1,0:T(8,128)(2,1)S(1)} %collective-permute-done.14.refs_3_) | copy-start | bytes 1557508
  76.0 9.1 %copy-start.15 = (bf16[104,2496]{1,0:T(8,128)(2,1)}, bf16[104,2496]{1,0:T(8,128)(2,1)S(1)}, u32[]{:S(2)}) copy-start(bf16[104,2496]{1,0:T(8,128)(2,1)S(1)} %collective-permute-done.15.refs_7_) | copy-start | bytes 1557508
  85.1 0.8 copy-start.9
  85.9 11.8 %copy-start = (bf16[16,16,896]{2,1,0:T(8,128)(2,1)}, bf16[16,16,896]{2,1,0:T(8,128)(2,1)S(1)}, u32[]{:S(2)}) copy-start(bf16[16,16,896]{2,1,0:T(8,128)(2,1)S(1)} %all-to-all-done) | copy-start | bytes 1376260
  85.9 11.8 %collective-permute-start.16 = (bf16[256,896]{1,0:T(8,128)(2,1)S(1)}, bf16[256,896]{1,0:T(8,128)(2,1)S(1)}, u32[]{:S(2)}, u32[]{:S(2)}) collective-permute-start(bf16[256,896]{1,0:T(8,128)(2,1)S(1)} %bitcast.11), channel_id=1, source_target_pairs={{0,1},{1,0},{2,3},{3,2},{4,5},{5,4},{6,7},{7,6},{8,9},{9,8},{10,11... | collective-permute-start | bytes 1376264 | tf_op jit(solution)/shard_map/ppermute | solution.py:26
  90.5 26.9 %collective-permute-start.17 = (bf16[104,1280]{1,0:T(8,128)(2,1)S(1)}, bf16[104,1280]{1,0:T(8,128)(2,1)S(1)}, u32[]{:S(2)}, u32[]{:S(2)}) collective-permute-start(bf16[104,1280]{1,0:T(8,128)(2,1)S(1)} %slice.12), channel_id=1, source_target_pairs={{0,2},{2,0},{4,6},{6,4},{8,10},{10,8},{12,14},{14,12},{16,18},{18,... | collective-permute-start | bytes 798728 | tf_op jit(solution)/shard_map/ppermute | solution.py:344
  92.7 24.7 %collective-permute-start.18 = (bf16[104,1216]{1,0:T(8,128)(2,1)S(1)}, bf16[104,1216]{1,0:T(8,128)(2,1)S(1)}, u32[]{:S(2)}, u32[]{:S(2)}) collective-permute-start(bf16[104,1216]{1,0:T(8,128)(2,1)S(1)} %slice.13), channel_id=1, source_target_pairs={{0,4},{2,6},{4,0},{6,2},{8,12},{10,14},{12,8},{14,10},{16,20},{18,... | collective-permute-start | bytes 758792 | tf_op jit(solution)/shard_map/ppermute | solution.py:345
  95.2 22.3 %collective-permute-start.19 = (bf16[104,1280]{1,0:T(8,128)(2,1)S(1)}, bf16[104,1280]{1,0:T(8,128)(2,1)S(1)}, u32[]{:S(2)}, u32[]{:S(2)}) collective-permute-start(bf16[104,1280]{1,0:T(8,128)(2,1)S(1)} %slice.14), channel_id=1, source_target_pairs={{0,2},{2,0},{4,6},{6,4},{8,10},{10,8},{12,14},{14,12},{16,18},{18,... | collective-permute-start | bytes 798728 | tf_op jit(solution)/shard_map/ppermute | solution.py:344
  97.1 20.3 %collective-permute-start.20 = (bf16[104,1216]{1,0:T(8,128)(2,1)S(1)}, bf16[104,1216]{1,0:T(8,128)(2,1)S(1)}, u32[]{:S(2)}, u32[]{:S(2)}) collective-permute-start(bf16[104,1216]{1,0:T(8,128)(2,1)S(1)} %slice.15), channel_id=1, source_target_pairs={{0,4},{2,6},{4,0},{6,2},{8,12},{10,14},{12,8},{14,10},{16,20},{18,... | collective-permute-start | bytes 758792 | tf_op jit(solution)/shard_map/ppermute | solution.py:345
  97.7 0.8 copy-start.2
  117.4 0.8 copy-start.5
  117.4 0.8 copy-start.4
  117.5 0.9 copy-start.7
  117.5 1.0 copy-start.6

commit v6 on v4

v6 whole, which is shorter than its diff:
```python
import functools

import jax
import jax.numpy as jnp
import numpy as np
from jax import lax
from jax.experimental import pallas as pl
from jax.experimental.pallas import tpu as pltpu
from jax.sharding import PartitionSpec as P

DV = 1664
SEQ = 4096
IMG_CAP = 16
EPSILON = 1e-06
VMEM = 32 << 20
LIGHT = pl.CostEstimate(flops=1000, bytes_accessed=1000, transcendentals=0)


def folded_ring(count):
    odd = list(range(1, count, 2))
    even = list(range(0, count, 2))
    return even[:1] + odd + even[:0:-1]


def tp_shift(value, n_tp, distance):
    return lax.ppermute(value, "tp", [(i, (i + distance) % n_tp) for i in range(n_tp)])


def tp_scatter_sum(value, n_tp, axis):
    me = lax.axis_index("tp")
    width = value.shape[axis] // n_tp
    total = lax.dynamic_slice_in_dim(value, me * width, width, axis)
    for distance in range(1, n_tp):
        block = lax.dynamic_slice_in_dim(value, (me + distance) % n_tp * width, width, axis)
        total = total + tp_shift(block, n_tp, distance)
    return total


def ring_tables(n_req):
    lines = n_req // 4
    order = folded_ring(lines)
    following = {order[i]: order[(i + 1) % lines] for i in range(lines)}
    line_perm = [(z * 4 + p, following[z] * 4 + p) for z in range(lines) for p in range(4)]
    table = np.zeros((n_req, n_req), np.int32)
    for index in range(n_req):
        for step in range(lines):
            z = order[(order.index(index // 4) - step) % lines]
            for flip in range(4):
                table[index, step * 4 + flip] = z * 4 + ((index % 4) ^ flip)
    return lines, line_perm, table


def tie(*values):
    return lax.optimization_barrier(values)


def row_stats(patches):
    rows, _ = patches.shape

    def body(patches_ref, out_ref):
        values = patches_ref[...].astype(jnp.float32)
        sums = jnp.sum(values, axis=1, keepdims=True)
        squares = jnp.sum(values * values, axis=1, keepdims=True)
        out_ref[:, :128] = jnp.broadcast_to(sums, (rows, 128))
        out_ref[:, 128:] = jnp.broadcast_to(squares, (rows, 128))

    vmem = pl.BlockSpec(memory_space=pltpu.VMEM)
    return pl.pallas_call(
        body,
        out_shape=jax.ShapeDtypeStruct((rows, 256), jnp.float32),
        in_specs=[vmem],
        out_specs=vmem,
        compiler_params=pltpu.CompilerParams(vmem_limit_bytes=VMEM),
        cost_estimate=LIGHT,
    )(patches)


def merge(patches, stats, gain_bias, merge_weight):
    rows, width = patches.shape
    window, _, features = merge_weight.shape
    tokens = rows // window
    count = len(stats)

    def body(patches_ref, gain_bias_ref, *refs):
        stats_refs, (weight_ref, out_ref, normed_ref) = refs[:count], refs[count:]
        step = pl.program_id(0)

        @pl.when(step == 0)
        def _():
            sums = sum(ref[...] for ref in stats_refs) / DV
            row_mean = sums[:, 0:1]
            row_scale = lax.rsqrt(sums[:, 128:129] - row_mean * row_mean + EPSILON)
            gain_bias = gain_bias_ref[...].astype(jnp.float32)
            normed_ref[...] = (
                (patches_ref[...].astype(jnp.float32) - row_mean) * row_scale * gain_bias[0:1]
                + gain_bias[1:2]
            ).astype(jnp.bfloat16)
            out_ref[...] = jnp.zeros_like(out_ref)

        wanted = lax.broadcasted_iota(jnp.int32, (tokens, rows), 0) * window + step
        chosen = (lax.broadcasted_iota(jnp.int32, (tokens, rows), 1) == wanted).astype(jnp.bfloat16)
        part = jnp.dot(chosen, normed_ref[...], preferred_element_type=jnp.float32)
        out_ref[...] += jnp.dot(
            part.astype(jnp.bfloat16), weight_ref[0], preferred_element_type=jnp.float32
        )

    def whole(shape):
        return pl.BlockSpec(shape, lambda i: (0, 0))

    return pl.pallas_call(
        body,
        out_shape=jax.ShapeDtypeStruct((tokens, features), jnp.float32),
        grid=(window,),
        in_specs=[whole((rows, width)), whole((2, width))]
        + [whole((rows, 256))] * count
        + [pl.BlockSpec((1, width, features), lambda i: (i, 0, 0))],
        out_specs=whole((tokens, features)),
        scratch_shapes=[pltpu.VMEM((rows, width), jnp.bfloat16)],
        compiler_params=pltpu.CompilerParams(vmem_limit_bytes=VMEM),
        cost_estimate=LIGHT,
    )(patches, gain_bias, *stats, merge_weight)


def combine(tp_index, texts, images, gain_column):
    n_tp = len(texts)
    width, positions = texts[0].shape
    slots = images[0].shape[0]

    def body(index_ref, gain_ref, *refs):
        text_refs, image_refs = refs[:n_tp], refs[n_tp : 2 * n_tp]
        out_ref, value_ref = refs[2 * n_tp :]
        code = image_refs[0][:, width : width + 2].astype(jnp.float32)
        local = code[:, 0:1] * 256.0 + code[:, 1:2] - 1.0
        place = lax.broadcasted_iota(jnp.int32, (slots, positions), 1).astype(jnp.float32)
        hit = jnp.where(local == place, 1.0, 0.0)
        covered = jnp.max(hit, axis=0, keepdims=True)
        hit = hit.astype(jnp.bfloat16)
        squares = jnp.zeros((1, positions), jnp.float32)
        starts = []
        for distance in range(n_tp):
            start = pl.multiple_of(
                lax.rem(index_ref[0] + n_tp - distance, n_tp) * width, 16
            )
            starts.append(start)
            image = lax.dot_general(
                image_refs[distance][...],
                hit,
                (((0,), (0,)), ((), ())),
                preferred_element_type=jnp.float32,
            )[:width]
            value = jnp.where(covered > 0.0, image, text_refs[distance][...].astype(jnp.float32))
            squares += jnp.sum(value * value, axis=0, keepdims=True)
            value_ref[pl.ds(start, width), :] = value
        scale = lax.rsqrt(squares / (width * n_tp) + EPSILON)
        out_ref[...] = (
            value_ref[...] * scale * gain_ref[...].astype(jnp.float32)
        ).astype(out_ref.dtype)

    vmem = pl.BlockSpec(memory_space=pltpu.VMEM)
    return pl.pallas_call(
        body,
        out_shape=jax.ShapeDtypeStruct((width * n_tp, positions), jnp.bfloat16),
        in_specs=[pl.BlockSpec(memory_space=pltpu.SMEM)] + [vmem] * (1 + 2 * n_tp),
        out_specs=vmem,
        scratch_shapes=[pltpu.VMEM((width * n_tp, positions), jnp.float32)],
        compiler_params=pltpu.CompilerParams(vmem_limit_bytes=VMEM),
        cost_estimate=LIGHT,
    )(tp_index, gain_column, *texts, *images)


def shards(
    n_req, n_tp,
    patches, ln_gain, ln_bias, merge_weight, text_rows, norm_gain, qkv_weight, token_pos, text_len,
):
    row_count, width = text_rows.shape
    me = lax.axis_index("req")
    tp_index = lax.axis_index("tp").reshape(1)
    lines, line_perm, table = ring_tables(n_req)
    x_perm = [(i, i ^ 1) for i in range(n_req)]
    y_perm = [(i, i ^ 2) for i in range(n_req)]
    rows, columns = qkv_weight.shape
    cut = (columns + 255) // 256 * 128
    order = lax.dynamic_slice_in_dim(jnp.asarray(table), me, 1, 0).reshape(-1)

    def along_line(block):
        return lax.ppermute(block, "req", line_perm)

    def to_sides(block):
        return lax.ppermute(block, "req", x_perm), lax.ppermute(block, "req", y_perm)

    def to_corner(by_x, by_y):
        left = lax.ppermute(by_y[:, :cut], "req", x_perm)
        right = lax.ppermute(by_x[:, cut:], "req", y_perm)
        return jnp.concatenate([left, right], axis=1)

    held = [qkv_weight]
    held.append(along_line(held[0]))
    sides = [to_sides(held[0])]
    corners = []
    stats_own = row_stats(patches)
    stats = [stats_own] + [tp_shift(stats_own, n_tp, d) for d in range(1, n_tp)]
    gain_bias = jnp.stack([ln_gain, ln_bias])
    text_turned = text_rows.T
    texts = [text_turned] + [tp_shift(text_turned, n_tp, d) for d in range(1, n_tp)]

    token_count = token_pos.shape[0]
    target = lax.div(token_pos, row_count)
    same = target[:, None] == target[None, :]
    ids = jnp.arange(token_count, dtype=jnp.int32)
    before = jnp.sum((same & (ids[None, :] < ids[:, None])).astype(jnp.int32), axis=1)
    slot = target * IMG_CAP + before
    slot_count = n_req * IMG_CAP
    place = (
        jnp.arange(slot_count, dtype=jnp.int32)[:, None] == slot[None, :]
    ).astype(jnp.bfloat16)
    code = lax.rem(token_pos, row_count) + 1
    code_cols = jnp.stack([lax.div(code, 256), lax.rem(code, 256)], axis=1).astype(jnp.bfloat16)
    gain_column = norm_gain[:, None]

    stats, held[1], sides[0], gain_bias, gain_column, order = tie(
        stats, held[1], sides[0], gain_bias, gain_column, order
    )
    held.append(along_line(held[1]))
    sides.append(to_sides(held[1]))
    corners.append(to_corner(*sides[0]))
    partial_value = merge(patches, stats, gain_bias, merge_weight)

    partial_value, held[2], sides[1] = tie(partial_value, held[2], sides[1])
    held.append(along_line(held[2]))
    sides.append(to_sides(held[2]))
    corners.append(along_line(corners[0]))
    merged = tp_scatter_sum(partial_value, n_tp, 1).astype(jnp.bfloat16)
    padding = (-width - 2) % 128
    payload = jnp.concatenate(
        [merged, code_cols, jnp.zeros((token_count, padding), jnp.bfloat16)], axis=1
    )
    outgoing = jnp.dot(place, payload, preferred_element_type=jnp.float32).astype(jnp.bfloat16)
    arrived = lax.all_to_all(
        outgoing.reshape(n_req, IMG_CAP, -1), "req", split_axis=0, concat_axis=0
    ).reshape(slot_count, -1)

    def group(step, corner=True):
        pieces = [held[step], *sides[step]] + ([corners[step]] if corner else [])
        return jnp.concatenate(pieces, axis=0)

    first_group = group(0)
    arrived, held[3], sides[2], texts, first_group = tie(
        arrived, held[3], sides[2], texts, first_group
    )
    sides.append(to_sides(held[3]))
    corners.append(along_line(corners[1]))
    images = [arrived] + [tp_shift(arrived, n_tp, d) for d in range(1, n_tp)]
    scaled = combine(tp_index, texts, images, gain_column)
    scaled, sides[3], corners[1] = tie(scaled, sides[3], corners[1])

    for step in range(4, lines):
        held.append(along_line(held[step - 1]))
        sides.append(to_sides(held[step]))
        corners.append(along_line(corners[step - 2]))
    corners.append(to_corner(*sides[-1]))

    blocks = scaled.reshape(n_req, rows, row_count)

    def rows_of(step, flips):
        return jnp.concatenate(
            [
                lax.dynamic_index_in_dim(blocks, order[step * 4 + flip], 0, keepdims=False)
                for flip in flips
            ],
            axis=0,
        )

    def product(source, weight):
        source, weight = tie(source, weight)
        return lax.dot_general(
            source, weight, (((0,), (0,)), ((), ())), preferred_element_type=jnp.float32
        )

    total = product(rows_of(0, range(4)), first_group)
    for step in range(1, lines - 1):
        total += product(rows_of(step, range(4)), group(step))
    total += product(rows_of(lines - 1, range(3)), group(lines - 1, False))
    total, corners[-1] = tie(total, corners[-1])

    position = me * row_count + jnp.arange(row_count, dtype=jnp.int32)
    request_ids = jnp.arange(text_len.shape[0], dtype=jnp.int32)
    limits = jnp.sum(
        jnp.where(
            lax.div(position, SEQ)[:, None] == request_ids[None, :], text_len[None, :], 0
        ),
        axis=1,
    )
    keep = lax.rem(position, SEQ) < limits
    total += product(rows_of(lines - 1, [3]), corners[lines - 1])
    return jnp.where(keep[:, None], total, 0.0).astype(jnp.bfloat16)


def solution(mesh):
    placed = (
        P("req", "tp"),
        P("tp"),
        P("tp"),
        P(None, "tp", None),
        P("req", "tp"),
        P(),
        P("req", "tp"),
        P("req"),
        P(),
    )
    body = functools.partial(shards, mesh.shape["req"], mesh.shape["tp"])
    return jax.shard_map(
        body, mesh=mesh, in_specs=placed, out_specs=P("req", "tp"), check_vma=False
    )
```

time: 133 us -> 136 us (1.023)
  Pallas kernels: 41.7 us -> 5.64 us
  between operations: 0.21 us -> 30.5 us
  other arithmetic: 3.53 us -> 11.6 us
  matrix products: 1.09 us -> 8.44 us
  waiting for transfers between devices: 39.6 us -> 34.6 us
  blocking collectives: 2.47 us -> 0 us
  starting transfers between devices: 25.6 us -> 27.8 us
  local copies, waits for them, and re-layouts: 17.6 us -> 16 us
    pallas_call x3 -> x1, Pallas kernels: 29 us -> 0.29 us  [row_stats(): pl.pallas_call(body, out_shape=jax.ShapeDtypeStruct((rows, 256), jnp.floa...]
    concatenate x0 -> x8, other arithmetic: none -> 7.6 us  [the longest x4 7.42 us: group(): return jnp.concatenate(pieces, axis=0)]
    dot_general x0 -> x5, matrix products: none -> 7.35 us  [product(): lax.dot_general(source, weight, (((0,), (0,)), ((), ())), preferred_eleme...]
    ppermute x19 -> x17, waiting for transfers between devices: 39.6 us -> 34.6 us  [the longest x5 28.1 us: along_line(): return lax.ppermute(block, 'req', line_perm)]
    pallas_call x1, Pallas kernels: 7.82 us -> 3.61 us  [merge(): pl.pallas_call(body, out_shape=jax.ShapeDtypeStruct((tokens, features), j...]
    broadcast_in_dim x4 -> x1, local copies, waits for them, and re-layouts: 4.46 us -> 0.69 us  [shards(): gain_column = norm_gain[:, None]]
    unnamed x32 -> x19, local copies, waits for them, and re-layouts: 5.15 us -> 8.77 us
    pallas_call x1, Pallas kernels: 4.84 us -> 1.74 us  [combine(): pl.pallas_call(body, out_shape=jax.ShapeDtypeStruct((width * n_tp, positi...]
  transfers between devices with their start and end apart: 23 -> 22, of which waited for: 8 -> 10; matrix products, arithmetic and copies ran while one was open for 13% -> 14% of each run, Pallas kernels for 26% -> 4%
where the time goes in v6:
time: 136 us; the launch traced here: 135 us
  waiting for transfers between devices  34.6 us (25%)
  between operations  30.5 us (22%)
  starting transfers between devices  27.8 us (20%)
  local copies, waits for them, and re-layouts  16 us (12%)
  other arithmetic  11.6 us (9%)
  matrix products  8.44 us (6%)
  Pallas kernels  5.64 us (4%)
    ppermute x5, waiting for transfers between devices, along_line(): return lax.ppermute(block, 'req', line_perm)  28.1 us
    unnamed x19, local copies, waits for them, and re-layouts  8.77 us
    ppermute x5, starting transfers between devices, along_line(): return lax.ppermute(block, 'req', line_perm)  8.73 us
    concatenate x4, other arithmetic, group(): return jnp.concatenate(pieces, axis=0)  7.42 us
    dot_general x5, matrix products, product(): lax.dot_general(source, weight, (((0,), (0,)), ((), ())), preferred_eleme...  7.35 us
    ppermute x4, starting transfers between devices, to_sides(): lax.ppermute(block, 'req', y_perm)  6.02 us
    all_to_all x1, starting transfers between devices, shards(): lax.all_to_all(outgoing.reshape(n_req, IMG_CAP, -1), 'req', split_axis=0,...  4.54 us
    ppermute x4, starting transfers between devices, to_sides(): lax.ppermute(block, 'req', x_perm)  4.48 us
  transfers between devices with their start and end apart: 22, of which 10 were waited for; matrix products, arithmetic and copies ran while one was open for 14% of the time, Pallas kernels for 4%

profile of v6, /device:TPU:0, one launch (start us, length us, event | category | flops | bytes accessed | tf_op | source)
XLA Modules:
  0.0 134.6 jit_solution(2791594484150543662)
XLA Ops:
  0.0 3.0 %collective-permute-start.1 = (bf16[104,2496]{1,0:T(8,128)(2,1)}, bf16[104,2496]{1,0:T(8,128)(2,1)}, u32[]{:S(2)}, u32[]{:S(2)}) collective-permute-start(bf16[104,2496]{1,0:T(8,128)(2,1)} %param.16), channel_id=1, source_target_pairs={{0,8},{2,10},{4,12},{6,14},{8,24},{10,26},{12,28},{14,30},{16,0},{... | collective-permute-start | bytes 1557512 | tf_op jit(solution)/shard_map/ppermute | solution.py:186
  3.0 1.5 %collective-permute-start.2 = (bf16[104,2496]{1,0:T(8,128)(2,1)}, bf16[104,2496]{1,0:T(8,128)(2,1)S(1)}, u32[]{:S(2)}, u32[]{:S(2)}) collective-permute-start(bf16[104,2496]{1,0:T(8,128)(2,1)} %param.16), channel_id=1, source_target_pairs={{0,2},{2,0},{4,6},{6,4},{8,10},{10,8},{12,14},{14,12},{16,18},{18,... | collective-permute-start | bytes 1557512 | tf_op jit(solution)/shard_map/ppermute | solution.py:189
  4.5 1.5 %collective-permute-start.3 = (bf16[104,2496]{1,0:T(8,128)(2,1)}, bf16[104,2496]{1,0:T(8,128)(2,1)S(1)}, u32[]{:S(2)}, u32[]{:S(2)}) collective-permute-start(bf16[104,2496]{1,0:T(8,128)(2,1)} %param.16), channel_id=1, source_target_pairs={{0,4},{2,6},{4,0},{6,2},{8,12},{10,14},{12,8},{14,10},{16,20},{18,... | collective-permute-start | bytes 1557512 | tf_op jit(solution)/shard_map/ppermute | solution.py:189
  6.0 1.1 copy-done.1
  7.2 0.3 shard_map.118.refs_0_
  7.6 0.7 stack.20
  8.2 0.7 stack.19
  8.9 0.7 broadcast_in_dim.43
  9.6 0.7 fusion.12
  10.3 0.7 convert_bitcast_fusion.1
  11.0 5.4 %collective-permute-done.1 = bf16[104,2496]{1,0:T(8,128)(2,1)} collective-permute-done((bf16[104,2496]{1,0:T(8,128)(2,1)}, bf16[104,2496]{1,0:T(8,128)(2,1)}, u32[]{:S(2)}, u32[]{:S(2)}) %collective-permute-start.1) | collective-permute-done | bytes 519200 | tf_op jit(solution)/shard_map/ppermute | solution.py:186
  16.4 0.3 collective-permute-done.2
  16.8 1.2 collective-permute-done.3
  18.0 2.6 %collective-permute-start.4 = (bf16[104,2496]{1,0:T(8,128)(2,1)}, bf16[104,2496]{1,0:T(8,128)(2,1)}, u32[]{:S(2)}, u32[]{:S(2)}) collective-permute-start(bf16[104,2496]{1,0:T(8,128)(2,1)} %collective-permute-done.1), channel_id=1, source_target_pairs={{0,8},{2,10},{4,12},{6,14},{8,24},{10,26},{12,28},{14,30},{16,0},{... | collective-permute-start | bytes 1557512 | tf_op jit(solution)/shard_map/ppermute | solution.py:186
  20.6 0.5 collective-permute-start.5
  21.1 1.5 %collective-permute-start.6 = (bf16[104,2496]{1,0:T(8,128)(2,1)}, bf16[104,2496]{1,0:T(8,128)(2,1)}, u32[]{:S(2)}, u32[]{:S(2)}) collective-permute-start(bf16[104,2496]{1,0:T(8,128)(2,1)} %collective-permute-done.1), channel_id=1, source_target_pairs={{0,4},{2,6},{4,0},{6,2},{8,12},{10,14},{12,8},{14,10},{16,20},{18,... | collective-permute-start | bytes 1557512 | tf_op jit(solution)/shard_map/ppermute | solution.py:189
  22.7 0.1 copy.17
  22.8 0.1 copy.16
  23.0 0.2 convert_reduce_fusion
  23.2 1.6 %collective-permute-start.12 = (bf16[104,1280]{1,0:T(8,128)(2,1)S(1)}, bf16[104,1280]{1,0:T(8,128)(2,1)S(1)}, u32[]{:S(2)}, u32[]{:S(2)}) collective-permute-start(bf16[104,1280]{1,0:T(8,128)(2,1)S(1)} %slice.60), channel_id=1, source_target_pairs={{0,2},{2,0},{4,6},{6,4},{8,10},{10,8},{12,14},{14,12},{16,18},{18,... | collective-permute-start | bytes 798728 | tf_op jit(solution)/shard_map/ppermute | solution.py:192
  24.8 0.6 collective-permute-start.13
  25.4 4.1 %copy-done = bf16[4,832,1664]{2,1,0:T(8,128)(2,1)S(1)} copy-done((bf16[4,832,1664]{2,1,0:T(8,128)(2,1)S(1)}, bf16[4,832,1664]{2,1,0:T(8,128)(2,1)}, u32[]{:S(2)}) %copy-start) | copy-done | bytes 11075608
  29.5 1.1 copy-done.2
  30.7 3.6 %shard_map.119 = f32[112,1664]{1,0:T(8,128)S(1)} custom-call(bf16[448,832]{1,0:T(8,128)(2,1)S(1)} %copy-done.2, bf16[2,832]{1,0:T(2,128)(2,1)S(1)} %pad_maximum_fusion.9.gain_bias_ref, f32[448,256]{1,0:T(8,128)S(1)} %shard_map.118.refs_0_, f32[448,256]{1,0:T(8,128)S(1)} %collective-permute-done.refs_1_, bf16[4,832,1664]{2,1,0:T(8,128)(2,1)S(1)} %copy-done), custom_call_target="tpu_custom_call" | custom-call | flops 1000 | bytes 1000 | tf_op jit(solution)/shard_map/pallas_call | solution.py:110
  34.3 1.5 %collective-permute-done.5 = bf16[104,2496]{1,0:T(8,128)(2,1)} collective-permute-done((bf16[104,2496]{1,0:T(8,128)(2,1)}, bf16[104,2496]{1,0:T(8,128)(2,1)}, u32[]{:S(2)}, u32[]{:S(2)}) %collective-permute-start.5) | collective-permute-done | bytes 519200 | tf_op jit(solution)/shard_map/ppermute | solution.py:189
  35.8 0.3 collective-permute-done.6
  36.1 0.2 constant_dynamic-slice_fusion
  36.4 2.2 %collective-permute-done.12 = bf16[104,1280]{1,0:T(8,128)(2,1)S(1)} collective-permute-done((bf16[104,1280]{1,0:T(8,128)(2,1)S(1)}, bf16[104,1280]{1,0:T(8,128)(2,1)S(1)}, u32[]{:S(2)}, u32[]{:S(2)}) %collective-permute-start.12) | collective-permute-done | bytes 266272 | tf_op jit(solution)/shard_map/ppermute | solution.py:192
  38.6 0.8 constant_dynamic-update-slice_fusion.1
  39.3 0.7 constant_dynamic-update-slice_fusion
  40.1 1.1 collective-permute-start.17
  41.2 0.2 add_convert_fusion
  41.4 1.1 convolution_convert_fusion
  42.5 4.5 %all-to-all-start = ((bf16[16,16,896]{2,1,0:T(8,128)(2,1)}), bf16[16,16,896]{2,1,0:T(8,128)(2,1)S(1)}, u32[]{:S(2)}, u32[]{:S(2)}) async-start(bf16[16,16,896]{2,1,0:T(8,128)(2,1)} %bitcast.4), calls=%async_computation | async-start | bytes 917504 | tf_op jit(solution)/shard_map/all_to_all | solution.py:238
  47.1 2.0 %collective-permute-start.8 = (bf16[104,2496]{1,0:T(8,128)(2,1)}, bf16[104,2496]{1,0:T(8,128)(2,1)S(1)}, u32[]{:S(2)}, u32[]{:S(2)}) collective-permute-start(bf16[104,2496]{1,0:T(8,128)(2,1)} %collective-permute-done.4), channel_id=1, source_target_pairs={{0,8},{2,10},{4,12},{6,14},{8,24},{10,26},{12,28},{14,30},{16,0},{... | collective-permute-start | bytes 1557512 | tf_op jit(solution)/shard_map/ppermute | solution.py:186
  49.1 1.5 %collective-permute-start.9 = (bf16[104,2496]{1,0:T(8,128)(2,1)}, bf16[104,2496]{1,0:T(8,128)(2,1)S(1)}, u32[]{:S(2)}, u32[]{:S(2)}) collective-permute-start(bf16[104,2496]{1,0:T(8,128)(2,1)} %collective-permute-done.4), channel_id=1, source_target_pairs={{0,2},{2,0},{4,6},{6,4},{8,10},{10,8},{12,14},{14,12},{16,18},{18,... | collective-permute-start | bytes 1557512 | tf_op jit(solution)/shard_map/ppermute | solution.py:189
  50.6 1.5 %collective-permute-start.10 = (bf16[104,2496]{1,0:T(8,128)(2,1)}, bf16[104,2496]{1,0:T(8,128)(2,1)}, u32[]{:S(2)}, u32[]{:S(2)}) collective-permute-start(bf16[104,2496]{1,0:T(8,128)(2,1)} %collective-permute-done.4), channel_id=1, source_target_pairs={{0,4},{2,6},{4,0},{6,2},{8,12},{10,14},{12,8},{14,10},{16,20},{18,... | collective-permute-start | bytes 1557512 | tf_op jit(solution)/shard_map/ppermute | solution.py:189
  52.1 0.1 fusion.9
  52.1 9.1 %collective-permute-done.17 = bf16[104,2496]{1,0:T(8,128)(2,1)} collective-permute-done((bf16[104,2496]{1,0:T(8,128)(2,1)}, bf16[104,2496]{1,0:T(8,128)(2,1)}, u32[]{:S(2)}, u32[]{:S(2)}) %collective-permute-start.17) | collective-permute-done | bytes 519200 | tf_op jit(solution)/shard_map/ppermute | solution.py:186
  61.2 2.7 %pad_maximum_fusion = bf16[416,2496]{1,0:T(8,128)(2,1)} fusion(bf16[104,2496]{1,0:T(8,128)(2,1)} %constant_dynamic-update-slice_fusion, bf16[104,2496]{1,0:T(8,128)(2,1)S(1)} %collective-permute-done.3, bf16[104,2496]{1,0:T(8,128)(2,1)S(1)} %collective-permute-done.2, bf16[104,2496]{1,0:T(8,128)(2,1)} %param.16), kind=kLoop, calls=%fused_computation.2 | loop fusion | flops 8306688 | bytes 4153344 | tf_op jit(solution)/shard_map/concatenate | solution.py:244
  63.9 13.6 %collective-permute-done.8 = bf16[104,2496]{1,0:T(8,128)(2,1)S(1)} collective-permute-done((bf16[104,2496]{1,0:T(8,128)(2,1)}, bf16[104,2496]{1,0:T(8,128)(2,1)S(1)}, u32[]{:S(2)}, u32[]{:S(2)}) %collective-permute-start.8) | collective-permute-done | bytes 519200 | tf_op jit(solution)/shard_map/ppermute | solution.py:186
  77.5 0.8 copy-done.5
  78.3 0.8 copy-done.7
  79.1 1.0 collective-permute-start.15
  80.1 1.5 %collective-permute-start.16 = (bf16[104,2496]{1,0:T(8,128)(2,1)}, bf16[104,2496]{1,0:T(8,128)(2,1)}, u32[]{:S(2)}, u32[]{:S(2)}) collective-permute-start(bf16[104,2496]{1,0:T(8,128)(2,1)} %copy-done.5), channel_id=1, source_target_pairs={{0,4},{2,6},{4,0},{6,2},{8,12},{10,14},{12,8},{14,10},{16,20},{18,... | collective-permute-start | bytes 1557512 | tf_op jit(solution)/shard_map/ppermute | solution.py:189
  81.7 0.7 fusion.16
  102.5 0.3 copy.18.gain_ref
  112.9 1.7 %pad_maximum_fusion.2 = bf16[416,2496]{1,0:T(8,128)(2,1)S(1)} fusion(bf16[104,2496]{1,0:T(8,128)(2,1)} %collective-permute-done.18, bf16[104,2496]{1,0:T(8,128)(2,1)} %collective-permute-done.10, bf16[104,2496]{1,0:T(8,128)(2,1)} %copy-done.7, bf16[104,2496]{1,0:T(8,128)(2,1)} %collective-permute-done.4), kind=kLoop, calls=%fused_computation.4 | loop fusion | flops 8306688 | bytes 4153344 | tf_op jit(solution)/shard_map/concatenate | solution.py:244
  114.6 1.7 %shard_map.120 = bf16[1664,512]{1,0:T(8,128)(2,1)S(1)} custom-call(s32[1]{0:T(128)} %bitcast.index_ref, bf16[1664,1]{1,0:T(8,128)(2,1)S(1)} %copy.18.gain_ref, bf16[832,512]{1,0:T(8,128)(2,1)S(1)} %bitcast.73, bf16[832,512]{1,0:T(8,128)(2,1)S(1)} %collective-permute-done.11.refs_1_, bf16[256,896]{1,0:T(8,128)(2,1)S(1)} %bitcast.71, ...), custom_call_target="tpu_custom_call" | custom-call | flops 1000 | bytes 1000 | tf_op jit(solution)/shard_map/pallas_call | solution.py:160
  116.4 1.0 slice.78
  117.4 1.3 pad_maximum_fusion.3
  118.7 1.0 slice.77
  119.7 0.2 dynamic-slice_bitcast_fusion
  120.0 1.7 %pad_maximum_fusion.1 = bf16[416,2496]{1,0:T(8,128)(2,1)S(1)} fusion(bf16[104,2496]{1,0:T(8,128)(2,1)} %collective-permute-done.17, bf16[104,2496]{1,0:T(8,128)(2,1)} %collective-permute-done.6, bf16[104,2496]{1,0:T(8,128)(2,1)} %collective-permute-done.5, bf16[104,2496]{1,0:T(8,128)(2,1)} %collective-permute-done.1), kind=kLoop, calls=%fused_computation.3 | loop fusion | flops 8306688 | bytes 4153344 | tf_op jit(solution)/shard_map/concatenate | solution.py:244
  121.7 0.6 collective-permute-start.20
  122.3 1.0 collective-permute-start.19
  123.3 1.5 %fusion.19 = f32[512,2496]{0,1:T(8,128)S(1)} fusion(bf16[416,512]{1,0:T(8,128)(2,1)S(1)} %pad_maximum_fusion.7, bf16[416,2496]{1,0:T(8,128)(2,1)S(1)} %pad_maximum_fusion.2), kind=kOutput, calls=%fused_computation.69 | convolution fusion | flops 1063256064 | bytes 7614464 | tf_op jit(solution)/shard_map/dot_general | solution.py:275
  124.9 1.5 %fusion.17 = f32[512,2496]{0,1:T(8,128)S(1)} fusion(bf16[416,512]{1,0:T(8,128)(2,1)S(1)} %get-tuple-element.56, bf16[416,2496]{1,0:T(8,128)(2,1)S(1)} %copy-done.4), kind=kOutput, calls=%fused_computation.67 | convolution fusion | flops 1063256064 | bytes 7614464 | tf_op jit(solution)/shard_map/dot_general | solution.py:275
  126.4 1.6 %fusion.18 = f32[512,2496]{0,1:T(8,128)S(1)} fusion(bf16[416,512]{1,0:T(8,128)(2,1)S(1)} %get-tuple-element.61, bf16[416,2496]{1,0:T(8,128)(2,1)S(1)} %pad_maximum_fusion.1), kind=kOutput, calls=%fused_computation.68 | convolution fusion | flops 1063256064 | bytes 7614464 | tf_op jit(solution)/shard_map/dot_general | solution.py:275
  128.0 1.8 %add_add_fusion = f32[512,2496]{0,1:T(8,128)S(1)} fusion(f32[512,2496]{0,1:T(8,128)S(1)} %fusion.19, f32[512,2496]{0,1:T(8,128)S(1)} %fusion.17, f32[512,2496]{0,1:T(8,128)S(1)} %fusion.18, bf16[312,512]{1,0:T(8,128)(2,1)S(1)} %pad_maximum_fusion.8, bf16[312,2496]{1,0:T(8,128)(2,1)S(1)} %pad_maximum_fusion.3), kind=kOutput, calls=%fused_computation.1 | convolution fusion | flops 801275904 | bytes 22324224 | tf_op jit(solution)/shard_map/dot_general | solution.py:275
  129.8 0.7 collective-permute-done.20
  130.6 0.2 collective-permute-done.19
  130.8 0.9 fusion.20
  131.7 2.8 %select_convert_fusion = bf16[512,2496]{0,1:T(8,128)(2,1)} fusion(f32[512,2496]{0,1:T(8,128)S(1)} %add_add_fusion, f32[512,2496]{0,1:T(8,128)S(1)} %fusion.20, pred[512]{0:T(512)(128)(4,1)S(1)} %fusion.10), kind=kLoop, calls=%fused_computation | loop fusion | flops 3833856 | bytes 12780032 | tf_op jit(solution)/shard_map/convert_element_type | solution.py:295
  (43 shorter events, 0.7 us)
Async XLA Ops:
  0.0 16.4 %collective-permute-start.1 = (bf16[104,2496]{1,0:T(8,128)(2,1)}, bf16[104,2496]{1,0:T(8,128)(2,1)}, u32[]{:S(2)}, u32[]{:S(2)}) collective-permute-start(bf16[104,2496]{1,0:T(8,128)(2,1)} %param.16), channel_id=1, source_target_pairs={{0,8},{2,10},{4,12},{6,14},{8,24},{10,26},{12,28},{14,30},{16,0},{... | collective-permute-start | bytes 1557512 | tf_op jit(solution)/shard_map/ppermute | solution.py:186
  3.0 13.8 %collective-permute-start.2 = (bf16[104,2496]{1,0:T(8,128)(2,1)}, bf16[104,2496]{1,0:T(8,128)(2,1)S(1)}, u32[]{:S(2)}, u32[]{:S(2)}) collective-permute-start(bf16[104,2496]{1,0:T(8,128)(2,1)} %param.16), channel_id=1, source_target_pairs={{0,2},{2,0},{4,6},{6,4},{8,10},{10,8},{12,14},{14,12},{16,18},{18,... | collective-permute-start | bytes 1557512 | tf_op jit(solution)/shard_map/ppermute | solution.py:189
  4.5 13.5 %collective-permute-start.3 = (bf16[104,2496]{1,0:T(8,128)(2,1)}, bf16[104,2496]{1,0:T(8,128)(2,1)S(1)}, u32[]{:S(2)}, u32[]{:S(2)}) collective-permute-start(bf16[104,2496]{1,0:T(8,128)(2,1)} %param.16), channel_id=1, source_target_pairs={{0,4},{2,6},{4,0},{6,2},{8,12},{10,14},{12,8},{14,10},{16,20},{18,... | collective-permute-start | bytes 1557512 | tf_op jit(solution)/shard_map/ppermute | solution.py:189
  6.0 1.1 copy-start.1
  7.5 3.5 %collective-permute-start = (f32[448,256]{1,0:T(8,128)S(1)}, f32[448,256]{1,0:T(8,128)S(1)}, u32[]{:S(2)}, u32[]{:S(2)}) collective-permute-start(f32[448,256]{1,0:T(8,128)S(1)} %shard_map.118.refs_0_), channel_id=1, source_target_pairs={{0,1},{1,0},{2,3},{3,2},{4,5},{5,4},{6,7},{7,6},{8,9},{9,8},{10,11... | collective-permute-start | bytes 1376264 | tf_op jit(solution)/shard_map/ppermute | solution.py:26
  18.0 16.3 %collective-permute-start.4 = (bf16[104,2496]{1,0:T(8,128)(2,1)}, bf16[104,2496]{1,0:T(8,128)(2,1)}, u32[]{:S(2)}, u32[]{:S(2)}) collective-permute-start(bf16[104,2496]{1,0:T(8,128)(2,1)} %collective-permute-done.1), channel_id=1, source_target_pairs={{0,8},{2,10},{4,12},{6,14},{8,24},{10,26},{12,28},{14,30},{16,0},{... | collective-permute-start | bytes 1557512 | tf_op jit(solution)/shard_map/ppermute | solution.py:186
  20.6 15.2 %collective-permute-start.5 = (bf16[104,2496]{1,0:T(8,128)(2,1)}, bf16[104,2496]{1,0:T(8,128)(2,1)}, u32[]{:S(2)}, u32[]{:S(2)}) collective-permute-start(bf16[104,2496]{1,0:T(8,128)(2,1)} %collective-permute-done.1), channel_id=1, source_target_pairs={{0,2},{2,0},{4,6},{6,4},{8,10},{10,8},{12,14},{14,12},{16,18},{18,... | collective-permute-start | bytes 1557512 | tf_op jit(solution)/shard_map/ppermute | solution.py:189
  21.1 15.0 %collective-permute-start.6 = (bf16[104,2496]{1,0:T(8,128)(2,1)}, bf16[104,2496]{1,0:T(8,128)(2,1)}, u32[]{:S(2)}, u32[]{:S(2)}) collective-permute-start(bf16[104,2496]{1,0:T(8,128)(2,1)} %collective-permute-done.1), channel_id=1, source_target_pairs={{0,4},{2,6},{4,0},{6,2},{8,12},{10,14},{12,8},{14,10},{16,20},{18,... | collective-permute-start | bytes 1557512 | tf_op jit(solution)/shard_map/ppermute | solution.py:189
  23.2 15.4 %collective-permute-start.12 = (bf16[104,1280]{1,0:T(8,128)(2,1)S(1)}, bf16[104,1280]{1,0:T(8,128)(2,1)S(1)}, u32[]{:S(2)}, u32[]{:S(2)}) collective-permute-start(bf16[104,1280]{1,0:T(8,128)(2,1)S(1)} %slice.60), channel_id=1, source_target_pairs={{0,2},{2,0},{4,6},{6,4},{8,10},{10,8},{12,14},{14,12},{16,18},{18,... | collective-permute-start | bytes 798728 | tf_op jit(solution)/shard_map/ppermute | solution.py:192
  24.8 14.5 %collective-permute-start.13 = (bf16[104,1216]{1,0:T(8,128)(2,1)S(1)}, bf16[104,1216]{1,0:T(8,128)(2,1)S(1)}, u32[]{:S(2)}, u32[]{:S(2)}) collective-permute-start(bf16[104,1216]{1,0:T(8,128)(2,1)S(1)} %slice.61), channel_id=1, source_target_pairs={{0,4},{2,6},{4,0},{6,2},{8,12},{10,14},{12,8},{14,10},{16,20},{18,... | collective-permute-start | bytes 758792 | tf_op jit(solution)/shard_map/ppermute | solution.py:193
  25.4 4.1 %copy-start = (bf16[4,832,1664]{2,1,0:T(8,128)(2,1)S(1)}, bf16[4,832,1664]{2,1,0:T(8,128)(2,1)}, u32[]{:S(2)}) copy-start(bf16[4,832,1664]{2,1,0:T(8,128)(2,1)} %refs_2_.1) | copy-start | bytes 33226756
  29.5 1.1 copy-start.2
  34.3 12.8 %copy-start.3 = (bf16[512,832]{0,1:T(8,128)(2,1)S(1)}, bf16[512,832]{0,1:T(8,128)(2,1)}, u32[]{:S(2)}) copy-start(bf16[512,832]{0,1:T(8,128)(2,1)} %param.14) | copy-start | bytes 2555908
  34.3 17.8 %copy-start.8 = (s32[2]{0:T(128)S(1)}, s32[2]{0:T(128)}, u32[]{:S(2)}) copy-start(s32[2]{0:T(128)} %param.18) | copy-start | bytes 28
  36.3 4.9 %collective-permute-start.7 = (f32[112,832]{1,0:T(8,128)S(1)}, f32[112,832]{1,0:T(8,128)S(1)}, u32[]{:S(2)}, u32[]{:S(2)}) collective-permute-start(f32[112,832]{1,0:T(8,128)S(1)} %constant_dynamic-slice_fusion), channel_id=1, source_target_pairs={{0,1},{1,0},{2,3},{3,2},{4,5},{5,4},{6,7},{7,6},{8,9},{9,8},{10,11... | collective-permute-start | bytes 1118216 | tf_op jit(solution)/shard_map/ppermute | solution.py:26
  40.1 21.1 %collective-permute-start.17 = (bf16[104,2496]{1,0:T(8,128)(2,1)}, bf16[104,2496]{1,0:T(8,128)(2,1)}, u32[]{:S(2)}, u32[]{:S(2)}) collective-permute-start(bf16[104,2496]{1,0:T(8,128)(2,1)} %constant_dynamic-update-slice_fusion), channel_id=1, source_target_pairs={{0,8},{2,10},{4,12},{6,14},{8,24},{10,26},{12,28},{14,30},{16,0},{... | collective-permute-start | bytes 1557512 | tf_op jit(solution)/shard_map/ppermute | solution.py:186
  42.5 36.6 %all-to-all-start = ((bf16[16,16,896]{2,1,0:T(8,128)(2,1)}), bf16[16,16,896]{2,1,0:T(8,128)(2,1)S(1)}, u32[]{:S(2)}, u32[]{:S(2)}) async-start(bf16[16,16,896]{2,1,0:T(8,128)(2,1)} %bitcast.4), calls=%async_computation | async-start | bytes 917504 | tf_op jit(solution)/shard_map/all_to_all | solution.py:238
  47.1 16.9 %collective-permute-start.11 = (bf16[832,512]{1,0:T(8,128)(2,1)S(1)}, bf16[832,512]{1,0:T(8,128)(2,1)S(1)}, u32[]{:S(2)}, u32[]{:S(2)}) collective-permute-start(bf16[832,512]{1,0:T(8,128)(2,1)S(1)} %bitcast.72), channel_id=1, source_target_pairs={{0,1},{1,0},{2,3},{3,2},{4,5},{5,4},{6,7},{7,6},{8,9},{9,8},{10,11... | collective-permute-start | bytes 2555912 | tf_op jit(solution)/shard_map/ppermute | solution.py:26
  47.1 30.4 %collective-permute-start.8 = (bf16[104,2496]{1,0:T(8,128)(2,1)}, bf16[104,2496]{1,0:T(8,128)(2,1)S(1)}, u32[]{:S(2)}, u32[]{:S(2)}) collective-permute-start(bf16[104,2496]{1,0:T(8,128)(2,1)} %collective-permute-done.4), channel_id=1, source_target_pairs={{0,8},{2,10},{4,12},{6,14},{8,24},{10,26},{12,28},{14,30},{16,0},{... | collective-permute-start | bytes 1557512 | tf_op jit(solution)/shard_map/ppermute | solution.py:186
  49.1 28.4 %collective-permute-start.9 = (bf16[104,2496]{1,0:T(8,128)(2,1)}, bf16[104,2496]{1,0:T(8,128)(2,1)S(1)}, u32[]{:S(2)}, u32[]{:S(2)}) collective-permute-start(bf16[104,2496]{1,0:T(8,128)(2,1)} %collective-permute-done.4), channel_id=1, source_target_pairs={{0,2},{2,0},{4,6},{6,4},{8,10},{10,8},{12,14},{14,12},{16,18},{18,... | collective-permute-start | bytes 1557512 | tf_op jit(solution)/shard_map/ppermute | solution.py:189
  50.6 28.5 %collective-permute-start.10 = (bf16[104,2496]{1,0:T(8,128)(2,1)}, bf16[104,2496]{1,0:T(8,128)(2,1)}, u32[]{:S(2)}, u32[]{:S(2)}) collective-permute-start(bf16[104,2496]{1,0:T(8,128)(2,1)} %collective-permute-done.4), channel_id=1, source_target_pairs={{0,4},{2,6},{4,0},{6,2},{8,12},{10,14},{12,8},{14,10},{16,20},{18,... | collective-permute-start | bytes 1557512 | tf_op jit(solution)/shard_map/ppermute | solution.py:189
  61.2 51.7 %collective-permute-start.18 = (bf16[104,2496]{1,0:T(8,128)(2,1)}, bf16[104,2496]{1,0:T(8,128)(2,1)}, u32[]{:S(2)}, u32[]{:S(2)}) collective-permute-start(bf16[104,2496]{1,0:T(8,128)(2,1)} %collective-permute-done.17), channel_id=1, source_target_pairs={{0,8},{2,10},{4,12},{6,14},{8,24},{10,26},{12,28},{14,30},{16,0},{... | collective-permute-start | bytes 1557512 | tf_op jit(solution)/shard_map/ppermute | solution.py:186
  77.5 0.8 copy-start.5
  78.3 0.8 copy-start.7
  79.1 37.3 %collective-permute-start.15 = (bf16[104,2496]{1,0:T(8,128)(2,1)}, bf16[104,2496]{1,0:T(8,128)(2,1)}, u32[]{:S(2)}, u32[]{:S(2)}) collective-permute-start(bf16[104,2496]{1,0:T(8,128)(2,1)} %copy-done.5), channel_id=1, source_target_pairs={{0,2},{2,0},{4,6},{6,4},{8,10},{10,8},{12,14},{14,12},{16,18},{18,... | collective-permute-start | bytes 1557512 | tf_op jit(solution)/shard_map/ppermute | solution.py:189
  80.1 36.3 %collective-permute-start.16 = (bf16[104,2496]{1,0:T(8,128)(2,1)}, bf16[104,2496]{1,0:T(8,128)(2,1)}, u32[]{:S(2)}, u32[]{:S(2)}) collective-permute-start(bf16[104,2496]{1,0:T(8,128)(2,1)} %copy-done.5), channel_id=1, source_target_pairs={{0,4},{2,6},{4,0},{6,2},{8,12},{10,14},{12,8},{14,10},{16,20},{18,... | collective-permute-start | bytes 1557512 | tf_op jit(solution)/shard_map/ppermute | solution.py:189
  81.6 33.0 %collective-permute-start.14 = (bf16[256,896]{1,0:T(8,128)(2,1)S(1)}, bf16[256,896]{1,0:T(8,128)(2,1)S(1)}, u32[]{:S(2)}, u32[]{:S(2)}) collective-permute-start(bf16[256,896]{1,0:T(8,128)(2,1)S(1)} %bitcast.70), channel_id=1, source_target_pairs={{0,1},{1,0},{2,3},{3,2},{4,5},{5,4},{6,7},{7,6},{8,9},{9,8},{10,11... | collective-permute-start | bytes 1376264 | tf_op jit(solution)/shard_map/ppermute | solution.py:26
  114.6 2.8 %copy-start.6 = (bf16[104,2496]{1,0:T(8,128)(2,1)S(1)}, bf16[104,2496]{1,0:T(8,128)(2,1)}, u32[]{:S(2)}) copy-start(bf16[104,2496]{1,0:T(8,128)(2,1)} %copy-done.5) | copy-start | bytes 1557508
  121.7 3.2 %copy-start.4 = (bf16[416,2496]{1,0:T(8,128)(2,1)S(1)}, bf16[416,2496]{1,0:T(8,128)(2,1)}, u32[]{:S(2)}) copy-start(bf16[416,2496]{1,0:T(8,128)(2,1)} %pad_maximum_fusion) | copy-start | bytes 6230020
  121.7 8.9 %collective-permute-start.20 = (bf16[104,1216]{1,0:T(8,128)(2,1)S(1)}, bf16[104,1216]{1,0:T(8,128)(2,1)S(1)}, u32[]{:S(2)}, u32[]{:S(2)}) collective-permute-start(bf16[104,1216]{1,0:T(8,128)(2,1)S(1)} %slice.78), channel_id=1, source_target_pairs={{0,4},{2,6},{4,0},{6,2},{8,12},{10,14},{12,8},{14,10},{16,20},{18,... | collective-permute-start | bytes 758792 | tf_op jit(solution)/shard_map/ppermute | solution.py:193
  122.3 8.5 %collective-permute-start.19 = (bf16[104,1280]{1,0:T(8,128)(2,1)S(1)}, bf16[104,1280]{1,0:T(8,128)(2,1)S(1)}, u32[]{:S(2)}, u32[]{:S(2)}) collective-permute-start(bf16[104,1280]{1,0:T(8,128)(2,1)S(1)} %slice.77), channel_id=1, source_target_pairs={{0,2},{2,0},{4,6},{6,4},{8,10},{10,8},{12,14},{14,12},{16,18},{18,... | collective-permute-start | bytes 798728 | tf_op jit(solution)/shard_map/ppermute | solution.py:192

commit v7 on v6

--- a/solution.py
+++ b/solution.py
@@ -121,12 +121,15 @@
     )(patches, gain_bias, *stats, merge_weight)
 
 
-def combine(tp_index, texts, images, gain_column):
+def combine(tp_index, order, texts, images, gain_column):
     n_tp = len(texts)
     width, positions = texts[0].shape
     slots = images[0].shape[0]
-
-    def body(index_ref, gain_ref, *refs):
+    count = order.shape[0]
+    rows = width * n_tp // count
+    share = width // rows
+
+    def body(index_ref, order_ref, gain_ref, *refs):
         text_refs, image_refs = refs[:n_tp], refs[n_tp : 2 * n_tp]
         out_ref, value_ref = refs[2 * n_tp :]
         code = image_refs[0][:, width : width + 2].astype(jnp.float32)
@@ -136,12 +139,8 @@
         covered = jnp.max(hit, axis=0, keepdims=True)
         hit = hit.astype(jnp.bfloat16)
         squares = jnp.zeros((1, positions), jnp.float32)
-        starts = []
         for distance in range(n_tp):
-            start = pl.multiple_of(
-                lax.rem(index_ref[0] + n_tp - distance, n_tp) * width, 16
-            )
-            starts.append(start)
+            first = lax.rem(index_ref[0] + n_tp - distance, n_tp) * share
             image = lax.dot_general(
                 image_refs[distance][...],
                 hit,
@@ -150,22 +149,25 @@
             )[:width]
             value = jnp.where(covered > 0.0, image, text_refs[distance][...].astype(jnp.float32))
             squares += jnp.sum(value * value, axis=0, keepdims=True)
-            value_ref[pl.ds(start, width), :] = value
+            for block in range(share):
+                value_ref[first + block] = value[block * rows : (block + 1) * rows]
         scale = lax.rsqrt(squares / (width * n_tp) + EPSILON)
-        out_ref[...] = (
-            value_ref[...] * scale * gain_ref[...].astype(jnp.float32)
-        ).astype(out_ref.dtype)
+        for block in range(count):
+            source = order_ref[block]
+            gain = gain_ref[source].astype(jnp.float32)
+            out_ref[block] = (value_ref[source] * scale * gain).astype(out_ref.dtype)
 
     vmem = pl.BlockSpec(memory_space=pltpu.VMEM)
+    smem = pl.BlockSpec(memory_space=pltpu.SMEM)
     return pl.pallas_call(
         body,
-        out_shape=jax.ShapeDtypeStruct((width * n_tp, positions), jnp.bfloat16),
-        in_specs=[pl.BlockSpec(memory_space=pltpu.SMEM)] + [vmem] * (1 + 2 * n_tp),
+        out_shape=jax.ShapeDtypeStruct((count, rows, positions), jnp.bfloat16),
+        in_specs=[smem, smem] + [vmem] * (1 + 2 * n_tp),
         out_specs=vmem,
-        scratch_shapes=[pltpu.VMEM((width * n_tp, positions), jnp.float32)],
+        scratch_shapes=[pltpu.VMEM((count, rows, positions), jnp.float32)],
         compiler_params=pltpu.CompilerParams(vmem_limit_bytes=VMEM),
         cost_estimate=LIGHT,
-    )(tp_index, gain_column, *texts, *images)
+    )(tp_index, order, gain_column, *texts, *images)
 
 
 def shards(
@@ -215,7 +217,7 @@
     ).astype(jnp.bfloat16)
     code = lax.rem(token_pos, row_count) + 1
     code_cols = jnp.stack([lax.div(code, 256), lax.rem(code, 256)], axis=1).astype(jnp.bfloat16)
-    gain_column = norm_gain[:, None]
+    gain_column = norm_gain.reshape(n_req, rows, 1)
 
     stats, held[1], sides[0], gain_bias, gain_column, order = tie(
         stats, held[1], sides[0], gain_bias, gain_column, order
@@ -228,58 +230,49 @@
     partial_value, held[2], sides[1] = tie(partial_value, held[2], sides[1])
     held.append(along_line(held[2]))
     sides.append(to_sides(held[2]))
-    corners.append(along_line(corners[0]))
     merged = tp_scatter_sum(partial_value, n_tp, 1).astype(jnp.bfloat16)
     padding = (-width - 2) % 128
     payload = jnp.concatenate(
         [merged, code_cols, jnp.zeros((token_count, padding), jnp.bfloat16)], axis=1
     )
     outgoing = jnp.dot(place, payload, preferred_element_type=jnp.float32).astype(jnp.bfloat16)
+
+    def group(step, corner=True):
+        pieces = [held[step], *sides[step]] + ([corners[step]] if corner else [])
+        return jnp.concatenate(pieces, axis=0)
+
+    first_group = group(0)
+
+    outgoing, held[3], sides[2], corners[0], texts, first_group = tie(
+        outgoing, held[3], sides[2], corners[0], texts, first_group
+    )
+    sides.append(to_sides(held[3]))
+    corners.append(along_line(corners[0]))
+    corners.append(to_corner(*sides[2]))
     arrived = lax.all_to_all(
         outgoing.reshape(n_req, IMG_CAP, -1), "req", split_axis=0, concat_axis=0
     ).reshape(slot_count, -1)
-
-    def group(step, corner=True):
-        pieces = [held[step], *sides[step]] + ([corners[step]] if corner else [])
-        return jnp.concatenate(pieces, axis=0)
-
-    first_group = group(0)
-    arrived, held[3], sides[2], texts, first_group = tie(
-        arrived, held[3], sides[2], texts, first_group
-    )
-    sides.append(to_sides(held[3]))
-    corners.append(along_line(corners[1]))
     images = [arrived] + [tp_shift(arrived, n_tp, d) for d in range(1, n_tp)]
-    scaled = combine(tp_index, texts, images, gain_column)
-    scaled, sides[3], corners[1] = tie(scaled, sides[3], corners[1])
-
+    blocks = combine(tp_index, order, texts, images, gain_column)
+
+    def product(first, count, weight):
+        source = blocks[first : first + count].reshape(count * rows, row_count)
+        weight, source = tie(weight, source)
+        return lax.dot_general(
+            source, weight, (((0,), (0,)), ((), ())), preferred_element_type=jnp.float32
+        )
+
+    total = product(0, 4, first_group) + product(4, 4, group(1))
+
+    total, sides[3] = tie(total, sides[3])
     for step in range(4, lines):
         held.append(along_line(held[step - 1]))
         sides.append(to_sides(held[step]))
-        corners.append(along_line(corners[step - 2]))
+        corners.append(to_corner(*sides[step - 1]))
     corners.append(to_corner(*sides[-1]))
-
-    blocks = scaled.reshape(n_req, rows, row_count)
-
-    def rows_of(step, flips):
-        return jnp.concatenate(
-            [
-                lax.dynamic_index_in_dim(blocks, order[step * 4 + flip], 0, keepdims=False)
-                for flip in flips
-            ],
-            axis=0,
-        )
-
-    def product(source, weight):
-        source, weight = tie(source, weight)
-        return lax.dot_general(
-            source, weight, (((0,), (0,)), ((), ())), preferred_element_type=jnp.float32
-        )
-
-    total = product(rows_of(0, range(4)), first_group)
-    for step in range(1, lines - 1):
-        total += product(rows_of(step, range(4)), group(step))
-    total += product(rows_of(lines - 1, range(3)), group(lines - 1, False))
+    for step in range(2, lines - 1):
+        total += product(step * 4, 4, group(step))
+    total += product(lines * 4 - 4, 3, group(lines - 1, False))
     total, corners[-1] = tie(total, corners[-1])
 
     position = me * row_count + jnp.arange(row_count, dtype=jnp.int32)
@@ -291,7 +284,7 @@
         axis=1,
     )
     keep = lax.rem(position, SEQ) < limits
-    total += product(rows_of(lines - 1, [3]), corners[lines - 1])
+    total += product(lines * 4 - 1, 1, corners[-1])
     return jnp.where(keep[:, None], total, 0.0).astype(jnp.bfloat16)
 
 

time: 136 us -> 109 us (0.80)
  between operations: 30.5 us -> 0.39 us
  waiting for transfers between devices: 34.6 us -> 22.3 us
  other arithmetic: 11.6 us -> 19.2 us
  matrix products: 8.44 us -> 12.9 us
  starting transfers between devices: 27.8 us -> 31.7 us
    ppermute x5 -> x4, waiting for transfers between devices: 28.1 us -> 4.22 us  [along_line(): return lax.ppermute(block, 'req', line_perm)]
    ppermute x2 -> x3, waiting for transfers between devices: 0.73 us -> 8.22 us  [to_corner(): right = lax.ppermute(by_x[:, cut:], 'req', y_perm)]
    add x0 -> x1, other arithmetic: none -> 6.03 us  [shards(): total += product(lines * 4 - 4, 3, group(lines - 1, False))]
    dot_general x5, matrix products: 7.35 us -> 11.8 us  [product(): lax.dot_general(source, weight, (((0,), (0,)), ((), ())), preferred_eleme...]
    ppermute x4, waiting for transfers between devices: 1.87 us -> 5.21 us  [to_sides(): lax.ppermute(block, 'req', x_perm)]
    ppermute x4, waiting for transfers between devices: 1.52 us -> 4.42 us  [to_sides(): lax.ppermute(block, 'req', y_perm)]
    ppermute x2 -> x3, waiting for transfers between devices: 2.42 us -> 0.01 us  [to_corner(): left = lax.ppermute(by_y[:, :cut], 'req', x_perm)]
    slice x2 -> x3, local copies, waits for them, and re-layouts: 0.99 us -> 3.36 us  [to_corner(): right = lax.ppermute(by_x[:, cut:], 'req', y_perm)]
  transfers between devices with their start and end apart: 22 -> 23, of which waited for: 10 -> 10; matrix products, arithmetic and copies ran while one was open for 14% -> 33% of each run, Pallas kernels for 4% -> 5%
where the time goes in v7:
time: 109 us; the launch traced here: 108 us
  starting transfers between devices  31.7 us (29%)
  waiting for transfers between devices  22.3 us (20%)
  other arithmetic  19.2 us (18%)
  local copies, waits for them, and re-layouts  16.3 us (15%)
  matrix products  12.9 us (12%)
  Pallas kernels  5.77 us (5%)
    dot_general x5, matrix products, product(): lax.dot_general(source, weight, (((0,), (0,)), ((), ())), preferred_eleme...  11.8 us
    concatenate x4, other arithmetic, group(): return jnp.concatenate(pieces, axis=0)  9.05 us
    ppermute x3, waiting for transfers between devices, to_corner(): right = lax.ppermute(by_x[:, cut:], 'req', y_perm)  8.22 us
    ppermute x4, starting transfers between devices, along_line(): return lax.ppermute(block, 'req', line_perm)  8.11 us
    ppermute x4, starting transfers between devices, to_sides(): lax.ppermute(block, 'req', x_perm)  6.48 us
    unnamed x25, local copies, waits for them, and re-layouts  6.48 us
    add x1, other arithmetic, shards(): total += product(lines * 4 - 4, 3, group(lines - 1, False))  6.03 us
    ppermute x4, waiting for transfers between devices, to_sides(): lax.ppermute(block, 'req', x_perm)  5.21 us
  transfers between devices with their start and end apart: 23, of which 10 were waited for; matrix products, arithmetic and copies ran while one was open for 33% of the time, Pallas kernels for 5%

profile of v7, /device:TPU:0, one launch (start us, length us, event | category | flops | bytes accessed | tf_op | source)
XLA Modules:
  0.0 108.5 jit_solution(6047148567561938630)
XLA Ops:
  0.0 2.9 %collective-permute-start.2 = (bf16[104,2496]{1,0:T(8,128)(2,1)}, bf16[104,2496]{1,0:T(8,128)(2,1)S(1)}, u32[]{:S(2)}, u32[]{:S(2)}) collective-permute-start(bf16[104,2496]{1,0:T(8,128)(2,1)} %param.16), channel_id=1, source_target_pairs={{0,2},{2,0},{4,6},{6,4},{8,10},{10,8},{12,14},{14,12},{16,18},{18,... | collective-permute-start | bytes 1557512 | tf_op jit(solution)/shard_map/ppermute | solution.py:191
  2.9 1.6 %collective-permute-start.1 = (bf16[104,2496]{1,0:T(8,128)(2,1)}, bf16[104,2496]{1,0:T(8,128)(2,1)}, u32[]{:S(2)}, u32[]{:S(2)}) collective-permute-start(bf16[104,2496]{1,0:T(8,128)(2,1)} %param.16), channel_id=1, source_target_pairs={{0,8},{2,10},{4,12},{6,14},{8,24},{10,26},{12,28},{14,30},{16,0},{... | collective-permute-start | bytes 1557512 | tf_op jit(solution)/shard_map/ppermute | solution.py:188
  4.5 1.5 %collective-permute-start.3 = (bf16[104,2496]{1,0:T(8,128)(2,1)}, bf16[104,2496]{1,0:T(8,128)(2,1)S(1)}, u32[]{:S(2)}, u32[]{:S(2)}) collective-permute-start(bf16[104,2496]{1,0:T(8,128)(2,1)} %param.16), channel_id=1, source_target_pairs={{0,4},{2,6},{4,0},{6,2},{8,12},{10,14},{12,8},{14,10},{16,20},{18,... | collective-permute-start | bytes 1557512 | tf_op jit(solution)/shard_map/ppermute | solution.py:191
  6.0 1.1 %copy-done.3 = bf16[448,832]{1,0:T(8,128)(2,1)S(1)} copy-done((bf16[448,832]{1,0:T(8,128)(2,1)S(1)}, bf16[448,832]{1,0:T(8,128)(2,1)}, u32[]{:S(2)}) %copy-start.3) | copy-done | bytes 745496
  7.2 0.3 shard_map.118.refs_0_
  7.5 0.7 fusion.12.order_ref
  8.2 0.7 stack.19
  8.9 0.7 stack.20
  9.6 0.8 reshape.52
  10.4 0.7 convert_bitcast_fusion.1
  11.1 0.2 convert_reduce_fusion
  11.3 4.0 %collective-permute-done.2 = bf16[104,2496]{1,0:T(8,128)(2,1)S(1)} collective-permute-done((bf16[104,2496]{1,0:T(8,128)(2,1)}, bf16[104,2496]{1,0:T(8,128)(2,1)S(1)}, u32[]{:S(2)}, u32[]{:S(2)}) %collective-permute-start.2) | collective-permute-done | bytes 519200 | tf_op jit(solution)/shard_map/ppermute | solution.py:191
  15.2 2.5 %collective-permute-done.1 = bf16[104,2496]{1,0:T(8,128)(2,1)} collective-permute-done((bf16[104,2496]{1,0:T(8,128)(2,1)}, bf16[104,2496]{1,0:T(8,128)(2,1)}, u32[]{:S(2)}, u32[]{:S(2)}) %collective-permute-start.1) | collective-permute-done | bytes 519200 | tf_op jit(solution)/shard_map/ppermute | solution.py:188
  17.7 0.3 collective-permute-done.3
  18.0 0.6 collective-permute-start.11
  18.6 1.5 %collective-permute-start.6 = (bf16[104,2496]{1,0:T(8,128)(2,1)}, bf16[104,2496]{1,0:T(8,128)(2,1)}, u32[]{:S(2)}, u32[]{:S(2)}) collective-permute-start(bf16[104,2496]{1,0:T(8,128)(2,1)} %collective-permute-done.1), channel_id=1, source_target_pairs={{0,4},{2,6},{4,0},{6,2},{8,12},{10,14},{12,8},{14,10},{16,20},{18,... | collective-permute-start | bytes 1557512 | tf_op jit(solution)/shard_map/ppermute | solution.py:191
  20.2 1.5 %collective-permute-start.5 = (bf16[104,2496]{1,0:T(8,128)(2,1)}, bf16[104,2496]{1,0:T(8,128)(2,1)}, u32[]{:S(2)}, u32[]{:S(2)}) collective-permute-start(bf16[104,2496]{1,0:T(8,128)(2,1)} %collective-permute-done.1), channel_id=1, source_target_pairs={{0,2},{2,0},{4,6},{6,4},{8,10},{10,8},{12,14},{14,12},{16,18},{18,... | collective-permute-start | bytes 1557512 | tf_op jit(solution)/shard_map/ppermute | solution.py:191
  21.6 2.6 %collective-permute-start.4 = (bf16[104,2496]{1,0:T(8,128)(2,1)}, bf16[104,2496]{1,0:T(8,128)(2,1)}, u32[]{:S(2)}, u32[]{:S(2)}) collective-permute-start(bf16[104,2496]{1,0:T(8,128)(2,1)} %collective-permute-done.1), channel_id=1, source_target_pairs={{0,8},{2,10},{4,12},{6,14},{8,24},{10,26},{12,28},{14,30},{16,0},{... | collective-permute-start | bytes 1557512 | tf_op jit(solution)/shard_map/ppermute | solution.py:188
  24.2 0.7 slice.34
  25.0 0.5 collective-permute-start.12
  25.5 0.1 copy.17
  25.6 0.1 copy.16
  25.8 4.1 %copy-done = bf16[4,832,1664]{2,1,0:T(8,128)(2,1)S(1)} copy-done((bf16[4,832,1664]{2,1,0:T(8,128)(2,1)S(1)}, bf16[4,832,1664]{2,1,0:T(8,128)(2,1)}, u32[]{:S(2)}) %copy-start) | copy-done | bytes 11075608
  30.0 1.1 %copy-done.4 = bf16[448,832]{1,0:T(8,128)(2,1)S(1)} copy-done((bf16[448,832]{1,0:T(8,128)(2,1)S(1)}, bf16[448,832]{1,0:T(8,128)(2,1)}, u32[]{:S(2)}) %copy-start.4) | copy-done | bytes 745496
  31.1 3.6 %shard_map.119 = f32[112,1664]{1,0:T(8,128)S(1)} custom-call(bf16[448,832]{1,0:T(8,128)(2,1)S(1)} %copy-done.4, bf16[2,832]{1,0:T(2,128)(2,1)S(1)} %pad_maximum_fusion.4.gain_bias_ref, f32[448,256]{1,0:T(8,128)S(1)} %shard_map.118.refs_0_, f32[448,256]{1,0:T(8,128)S(1)} %collective-permute-done.refs_1_, bf16[4,832,1664]{2,1,0:T(8,128)(2,1)S(1)} %copy-done), custom_call_target="tpu_custom_call" | custom-call | flops 1000 | bytes 1000 | tf_op jit(solution)/shard_map/pallas_call | solution.py:110
  34.9 2.2 %collective-permute-done.12 = bf16[104,1216]{1,0:T(8,128)(2,1)} collective-permute-done((bf16[104,1216]{1,0:T(8,128)(2,1)}, bf16[104,1216]{1,0:T(8,128)(2,1)}, u32[]{:S(2)}, u32[]{:S(2)}) %collective-permute-start.12) | collective-permute-done | bytes 252960 | tf_op jit(solution)/shard_map/ppermute | solution.py:195
  37.0 1.0 constant_dynamic-update-slice_fusion
  38.0 1.4 %collective-permute-start.10 = (bf16[104,2496]{1,0:T(8,128)(2,1)}, bf16[104,2496]{1,0:T(8,128)(2,1)}, u32[]{:S(2)}, u32[]{:S(2)}) collective-permute-start(bf16[104,2496]{1,0:T(8,128)(2,1)} %collective-permute-done.4), channel_id=1, source_target_pairs={{0,4},{2,6},{4,0},{6,2},{8,12},{10,14},{12,8},{14,10},{16,20},{18,... | collective-permute-start | bytes 1557512 | tf_op jit(solution)/shard_map/ppermute | solution.py:191
  39.4 1.5 %collective-permute-start.9 = (bf16[104,2496]{1,0:T(8,128)(2,1)}, bf16[104,2496]{1,0:T(8,128)(2,1)}, u32[]{:S(2)}, u32[]{:S(2)}) collective-permute-start(bf16[104,2496]{1,0:T(8,128)(2,1)} %collective-permute-done.4), channel_id=1, source_target_pairs={{0,2},{2,0},{4,6},{6,4},{8,10},{10,8},{12,14},{14,12},{16,18},{18,... | collective-permute-start | bytes 1557512 | tf_op jit(solution)/shard_map/ppermute | solution.py:191
  40.9 2.5 %collective-permute-start.8 = (bf16[104,2496]{1,0:T(8,128)(2,1)}, bf16[104,2496]{1,0:T(8,128)(2,1)}, u32[]{:S(2)}, u32[]{:S(2)}) collective-permute-start(bf16[104,2496]{1,0:T(8,128)(2,1)} %collective-permute-done.4), channel_id=1, source_target_pairs={{0,8},{2,10},{4,12},{6,14},{8,24},{10,26},{12,28},{14,30},{16,0},{... | collective-permute-start | bytes 1557512 | tf_op jit(solution)/shard_map/ppermute | solution.py:188
  43.4 0.2 constant_dynamic-slice_fusion.1
  43.7 1.5 %pad_maximum_fusion = bf16[416,2496]{1,0:T(8,128)(2,1)} fusion(bf16[104,2496]{1,0:T(8,128)(2,1)S(1)} %constant_dynamic-update-slice_fusion, bf16[104,2496]{1,0:T(8,128)(2,1)S(1)} %copy-done.8, bf16[104,2496]{1,0:T(8,128)(2,1)S(1)} %collective-permute-done.2, bf16[104,2496]{1,0:T(8,128)(2,1)S(1)} %copy-done.10), kind=kLoop, calls=%fused_computation.3 | loop fusion | flops 8306688 | bytes 4153344 | tf_op jit(solution)/shard_map/concatenate | solution.py:242
  45.2 0.2 collective-permute-done.7
  45.4 0.2 add_convert_fusion
  45.6 1.1 convolution_convert_fusion
  46.6 4.1 %collective-permute-done.10 = bf16[104,2496]{1,0:T(8,128)(2,1)} collective-permute-done((bf16[104,2496]{1,0:T(8,128)(2,1)}, bf16[104,2496]{1,0:T(8,128)(2,1)}, u32[]{:S(2)}, u32[]{:S(2)}) %collective-permute-start.10) | collective-permute-done | bytes 519200 | tf_op jit(solution)/shard_map/ppermute | solution.py:191
  50.8 1.2 %collective-permute-done.9 = bf16[104,2496]{1,0:T(8,128)(2,1)} collective-permute-done((bf16[104,2496]{1,0:T(8,128)(2,1)}, bf16[104,2496]{1,0:T(8,128)(2,1)}, u32[]{:S(2)}, u32[]{:S(2)}) %collective-permute-start.9) | collective-permute-done | bytes 519200 | tf_op jit(solution)/shard_map/ppermute | solution.py:191
  52.0 1.1 %collective-permute-done.8 = bf16[104,2496]{1,0:T(8,128)(2,1)} collective-permute-done((bf16[104,2496]{1,0:T(8,128)(2,1)}, bf16[104,2496]{1,0:T(8,128)(2,1)}, u32[]{:S(2)}, u32[]{:S(2)}) %collective-permute-start.8) | collective-permute-done | bytes 519200 | tf_op jit(solution)/shard_map/ppermute | solution.py:188
  53.2 4.7 %all-to-all-start = ((bf16[16,16,896]{2,1,0:T(8,128)(2,1)}), bf16[16,16,896]{2,1,0:T(8,128)(2,1)S(1)}, u32[]{:S(2)}, u32[]{:S(2)}) async-start(bf16[16,16,896]{2,1,0:T(8,128)(2,1)} %bitcast.5), calls=%async_computation | async-start | bytes 917504 | tf_op jit(solution)/shard_map/all_to_all | solution.py:252
  57.9 1.7 %slice.38 = bf16[104,1216]{1,0:T(8,128)(2,1)} slice(bf16[104,2496]{1,0:T(8,128)(2,1)} %collective-permute-done.9), slice={[0:104], [1280:2496]} | slice | bytes 505856 | tf_op jit(solution)/shard_map/slice | solution.py:195
  59.6 1.7 %slice.37 = bf16[104,1280]{1,0:T(8,128)(2,1)} slice(bf16[104,2496]{1,0:T(8,128)(2,1)} %collective-permute-done.10), slice={[0:104], [0:1280]} | slice | bytes 532480 | tf_op jit(solution)/shard_map/slice | solution.py:194
  61.3 1.9 %collective-permute-start.18 = (bf16[104,1280]{1,0:T(8,128)(2,1)}, bf16[104,1280]{1,0:T(8,128)(2,1)S(1)}, u32[]{:S(2)}, u32[]{:S(2)}) collective-permute-start(bf16[104,1280]{1,0:T(8,128)(2,1)} %slice.37), channel_id=1, source_target_pairs={{0,2},{2,0},{4,6},{6,4},{8,10},{10,8},{12,14},{14,12},{16,18},{18,... | collective-permute-start | bytes 798728 | tf_op jit(solution)/shard_map/ppermute | solution.py:194
  63.2 1.5 %collective-permute-start.19 = (bf16[104,1216]{1,0:T(8,128)(2,1)}, bf16[104,1216]{1,0:T(8,128)(2,1)}, u32[]{:S(2)}, u32[]{:S(2)}) collective-permute-start(bf16[104,1216]{1,0:T(8,128)(2,1)} %slice.38), channel_id=1, source_target_pairs={{0,4},{2,6},{4,0},{6,2},{8,12},{10,14},{12,8},{14,10},{16,20},{18,... | collective-permute-start | bytes 758792 | tf_op jit(solution)/shard_map/ppermute | solution.py:195
  64.8 1.5 %collective-permute-start.15 = (bf16[104,2496]{1,0:T(8,128)(2,1)}, bf16[104,2496]{1,0:T(8,128)(2,1)}, u32[]{:S(2)}, u32[]{:S(2)}) collective-permute-start(bf16[104,2496]{1,0:T(8,128)(2,1)} %copy-done.9), channel_id=1, source_target_pairs={{0,8},{2,10},{4,12},{6,14},{8,24},{10,26},{12,28},{14,30},{16,0},{... | collective-permute-start | bytes 1557512 | tf_op jit(solution)/shard_map/ppermute | solution.py:188
  66.2 0.3 copy.18.gain_ref
  66.5 0.6 collective-permute-start.17
  67.2 0.6 collective-permute-start.16
  67.7 6.1 %collective-permute-done.19 = bf16[104,1216]{1,0:T(8,128)(2,1)} collective-permute-done((bf16[104,1216]{1,0:T(8,128)(2,1)}, bf16[104,1216]{1,0:T(8,128)(2,1)}, u32[]{:S(2)}, u32[]{:S(2)}) %collective-permute-start.19) | collective-permute-done | bytes 252960 | tf_op jit(solution)/shard_map/ppermute | solution.py:195
  73.8 4.5 %maximum_maximum_fusion = bf16[416,2496]{1,0:T(8,128)(2,1)S(1)} fusion(bf16[104,1216]{1,0:T(8,128)(2,1)} %collective-permute-done.19, bf16[104,1280]{1,0:T(8,128)(2,1)S(1)} %collective-permute-done.18, bf16[104,2496]{1,0:T(8,128)(2,1)} %collective-permute-done.10, bf16[104,2496]{1,0:T(8,128)(2,1)} %collective-permute-done.9, ...), kind=kLoop, calls=%fused_computation.5 | loop fusion | flops 10383360 | bytes 4153344 | tf_op jit(solution)/shard_map/concatenate | solution.py:242
  78.3 0.6 collective-permute-done.15
  78.9 1.7 %pad_maximum_fusion.1 = bf16[416,2496]{1,0:T(8,128)(2,1)S(1)} fusion(bf16[104,2496]{1,0:T(8,128)(2,1)} %collective-permute-done.15, bf16[104,2496]{1,0:T(8,128)(2,1)} %collective-permute-done.6, bf16[104,2496]{1,0:T(8,128)(2,1)} %collective-permute-done.5, bf16[104,2496]{1,0:T(8,128)(2,1)} %collective-permute-done.1), kind=kLoop, calls=%fused_computation.4 | loop fusion | flops 8306688 | bytes 4153344 | tf_op jit(solution)/shard_map/concatenate | solution.py:242
  80.6 1.9 %shard_map.120 = bf16[16,104,512]{2,1,0:T(8,128)(2,1)S(1)} custom-call(s32[1]{0:T(128)} %bitcast.4.index_ref, s32[16]{0:T(128)S(1)} %fusion.12.order_ref, bf16[16,104,1]{2,1,0:T(8,128)(2,1)S(1)} %copy.18.gain_ref, bf16[832,512]{1,0:T(8,128)(2,1)S(1)} %bitcast.30, bf16[832,512]{1,0:T(8,128)(2,1)S(1)} %collective-permute-done.13.refs_1_, ...), custom_call_target="tpu_custom_call" | custom-call | flops 1000 | bytes 1000 | tf_op jit(solution)/shard_map/pallas_call | solution.py:162
  82.5 0.1 fusion.16
  82.6 1.6 %fusion.17 = f32[512,2496]{0,1:T(8,128)S(1)} fusion(bf16[416,512]{1,0:T(8,128)(2,1)S(1)} %bitcast.33, bf16[416,2496]{1,0:T(8,128)(2,1)S(1)} %copy-done.6), kind=kOutput, calls=%fused_computation.49 | convolution fusion | flops 1063256064 | bytes 7614464 | tf_op jit(solution)/shard_map/dot_general | solution.py:261
  84.2 1.7 %convolution_add_fusion = f32[512,2496]{0,1:T(8,128)S(1)} fusion(f32[512,2496]{0,1:T(8,128)S(1)} %fusion.17, bf16[416,512]{1,0:T(8,128)(2,1)S(1)} %bitcast.31, bf16[416,2496]{1,0:T(8,128)(2,1)S(1)} %pad_maximum_fusion.1), kind=kOutput, calls=%fused_computation.2 | convolution fusion | flops 1064534016 | bytes 12726272 | tf_op jit(solution)/shard_map/dot_general | solution.py:261
  85.9 1.0 slice.42
  86.9 1.3 %pad_maximum_fusion.2 = bf16[312,2496]{1,0:T(8,128)(2,1)S(1)} fusion(bf16[104,2496]{1,0:T(8,128)(2,1)S(1)} %collective-permute-done.17, bf16[104,2496]{1,0:T(8,128)(2,1)} %collective-permute-done.16, bf16[104,2496]{1,0:T(8,128)(2,1)} %collective-permute-done.8), kind=kLoop, calls=%fused_computation.6 | loop fusion | flops 4672512 | bytes 3115008 | tf_op jit(solution)/shard_map/concatenate | solution.py:242
  88.2 1.5 %collective-permute-start.20 = (bf16[104,1280]{1,0:T(8,128)(2,1)S(1)}, bf16[104,1280]{1,0:T(8,128)(2,1)S(1)}, u32[]{:S(2)}, u32[]{:S(2)}) collective-permute-start(bf16[104,1280]{1,0:T(8,128)(2,1)S(1)} %slice.41), channel_id=1, source_target_pairs={{0,2},{2,0},{4,6},{6,4},{8,10},{10,8},{12,14},{14,12},{16,18},{18,... | collective-permute-start | bytes 798728 | tf_op jit(solution)/shard_map/ppermute | solution.py:194
  89.7 1.1 %collective-permute-start.21 = (bf16[104,1216]{1,0:T(8,128)(2,1)S(1)}, bf16[104,1216]{1,0:T(8,128)(2,1)S(1)}, u32[]{:S(2)}, u32[]{:S(2)}) collective-permute-start(bf16[104,1216]{1,0:T(8,128)(2,1)S(1)} %slice.42), channel_id=1, source_target_pairs={{0,4},{2,6},{4,0},{6,2},{8,12},{10,14},{12,8},{14,10},{16,20},{18,... | collective-permute-start | bytes 758792 | tf_op jit(solution)/shard_map/ppermute | solution.py:195
  90.8 3.9 %fusion.18 = f32[512,2496]{0,1:T(8,128)} fusion(bf16[416,512]{1,0:T(8,128)(2,1)S(1)} %bitcast.32, bf16[416,2496]{1,0:T(8,128)(2,1)S(1)} %maximum_maximum_fusion), kind=kOutput, calls=%fused_computation.50 | convolution fusion | flops 1063256064 | bytes 7614464 | tf_op jit(solution)/shard_map/dot_general | solution.py:261
  94.7 3.8 %fusion.19 = f32[512,2496]{0,1:T(8,128)} fusion(bf16[312,512]{1,0:T(8,128)(2,1)S(1)} %bitcast.26, bf16[312,2496]{1,0:T(8,128)(2,1)S(1)} %pad_maximum_fusion.2), kind=kOutput, calls=%fused_computation.51 | convolution fusion | flops 797442048 | bytes 6988800 | tf_op jit(solution)/shard_map/dot_general | solution.py:261
  98.6 6.0 %add_add_fusion = f32[512,2496]{0,1:T(8,128)S(1)} fusion(f32[512,2496]{0,1:T(8,128)} %fusion.19, f32[512,2496]{0,1:T(8,128)S(1)} %convolution_add_fusion, f32[512,2496]{0,1:T(8,128)} %fusion.18), kind=kLoop, calls=%fused_computation.1 | loop fusion | flops 2555904 | bytes 20447232 | tf_op jit(solution)/shard_map/add | solution.py:275
  104.7 0.9 fusion.20
  105.6 2.9 %select_convert_fusion = bf16[512,2496]{0,1:T(8,128)(2,1)} fusion(f32[512,2496]{0,1:T(8,128)S(1)} %add_add_fusion, f32[512,2496]{0,1:T(8,128)S(1)} %fusion.20, pred[512]{0:T(512)(128)(4,1)S(1)} %fusion.10), kind=kLoop, calls=%fused_computation | loop fusion | flops 3833856 | bytes 12780032 | tf_op jit(solution)/shard_map/convert_element_type | solution.py:288
  (53 shorter events, 0.6 us)
Async XLA Ops:
  0.0 15.2 %collective-permute-start.2 = (bf16[104,2496]{1,0:T(8,128)(2,1)}, bf16[104,2496]{1,0:T(8,128)(2,1)S(1)}, u32[]{:S(2)}, u32[]{:S(2)}) collective-permute-start(bf16[104,2496]{1,0:T(8,128)(2,1)} %param.16), channel_id=1, source_target_pairs={{0,2},{2,0},{4,6},{6,4},{8,10},{10,8},{12,14},{14,12},{16,18},{18,... | collective-permute-start | bytes 1557512 | tf_op jit(solution)/shard_map/ppermute | solution.py:191
  2.9 14.8 %collective-permute-start.1 = (bf16[104,2496]{1,0:T(8,128)(2,1)}, bf16[104,2496]{1,0:T(8,128)(2,1)}, u32[]{:S(2)}, u32[]{:S(2)}) collective-permute-start(bf16[104,2496]{1,0:T(8,128)(2,1)} %param.16), channel_id=1, source_target_pairs={{0,8},{2,10},{4,12},{6,14},{8,24},{10,26},{12,28},{14,30},{16,0},{... | collective-permute-start | bytes 1557512 | tf_op jit(solution)/shard_map/ppermute | solution.py:188
  4.5 13.5 %collective-permute-start.3 = (bf16[104,2496]{1,0:T(8,128)(2,1)}, bf16[104,2496]{1,0:T(8,128)(2,1)S(1)}, u32[]{:S(2)}, u32[]{:S(2)}) collective-permute-start(bf16[104,2496]{1,0:T(8,128)(2,1)} %param.16), channel_id=1, source_target_pairs={{0,4},{2,6},{4,0},{6,2},{8,12},{10,14},{12,8},{14,10},{16,20},{18,... | collective-permute-start | bytes 1557512 | tf_op jit(solution)/shard_map/ppermute | solution.py:191
  6.0 1.1 %copy-start.3 = (bf16[448,832]{1,0:T(8,128)(2,1)S(1)}, bf16[448,832]{1,0:T(8,128)(2,1)}, u32[]{:S(2)}) copy-start(bf16[448,832]{1,0:T(8,128)(2,1)} %patches_ref.3) | copy-start | bytes 2236420
  7.5 3.8 %collective-permute-start = (f32[448,256]{1,0:T(8,128)S(1)}, f32[448,256]{1,0:T(8,128)S(1)}, u32[]{:S(2)}, u32[]{:S(2)}) collective-permute-start(f32[448,256]{1,0:T(8,128)S(1)} %shard_map.118.refs_0_), channel_id=1, source_target_pairs={{0,1},{1,0},{2,3},{3,2},{4,5},{5,4},{6,7},{7,6},{8,9},{9,8},{10,11... | collective-permute-start | bytes 1376264 | tf_op jit(solution)/shard_map/ppermute | solution.py:26
  18.0 7.7 %copy-start.7 = (bf16[104,2496]{1,0:T(8,128)(2,1)}, bf16[104,2496]{1,0:T(8,128)(2,1)S(1)}, u32[]{:S(2)}) copy-start(bf16[104,2496]{1,0:T(8,128)(2,1)S(1)} %collective-permute-done.3) | copy-start | bytes 1557508
  18.0 16.7 %collective-permute-start.11 = (bf16[104,1280]{1,0:T(8,128)(2,1)S(1)}, bf16[104,1280]{1,0:T(8,128)(2,1)S(1)}, u32[]{:S(2)}, u32[]{:S(2)}) collective-permute-start(bf16[104,1280]{1,0:T(8,128)(2,1)S(1)} %slice.33), channel_id=1, source_target_pairs={{0,2},{2,0},{4,6},{6,4},{8,10},{10,8},{12,14},{14,12},{16,18},{18,... | collective-permute-start | bytes 798728 | tf_op jit(solution)/shard_map/ppermute | solution.py:194
  18.6 19.4 %collective-permute-start.6 = (bf16[104,2496]{1,0:T(8,128)(2,1)}, bf16[104,2496]{1,0:T(8,128)(2,1)}, u32[]{:S(2)}, u32[]{:S(2)}) collective-permute-start(bf16[104,2496]{1,0:T(8,128)(2,1)} %collective-permute-done.1), channel_id=1, source_target_pairs={{0,4},{2,6},{4,0},{6,2},{8,12},{10,14},{12,8},{14,10},{16,20},{18,... | collective-permute-start | bytes 1557512 | tf_op jit(solution)/shard_map/ppermute | solution.py:191
  20.2 17.9 %collective-permute-start.5 = (bf16[104,2496]{1,0:T(8,128)(2,1)}, bf16[104,2496]{1,0:T(8,128)(2,1)}, u32[]{:S(2)}, u32[]{:S(2)}) collective-permute-start(bf16[104,2496]{1,0:T(8,128)(2,1)} %collective-permute-done.1), channel_id=1, source_target_pairs={{0,2},{2,0},{4,6},{6,4},{8,10},{10,8},{12,14},{14,12},{16,18},{18,... | collective-permute-start | bytes 1557512 | tf_op jit(solution)/shard_map/ppermute | solution.py:191
  21.6 16.4 %collective-permute-start.4 = (bf16[104,2496]{1,0:T(8,128)(2,1)}, bf16[104,2496]{1,0:T(8,128)(2,1)}, u32[]{:S(2)}, u32[]{:S(2)}) collective-permute-start(bf16[104,2496]{1,0:T(8,128)(2,1)} %collective-permute-done.1), channel_id=1, source_target_pairs={{0,8},{2,10},{4,12},{6,14},{8,24},{10,26},{12,28},{14,30},{16,0},{... | collective-permute-start | bytes 1557512 | tf_op jit(solution)/shard_map/ppermute | solution.py:188
  25.0 12.1 %collective-permute-start.12 = (bf16[104,1216]{1,0:T(8,128)(2,1)}, bf16[104,1216]{1,0:T(8,128)(2,1)}, u32[]{:S(2)}, u32[]{:S(2)}) collective-permute-start(bf16[104,1216]{1,0:T(8,128)(2,1)} %slice.34), channel_id=1, source_target_pairs={{0,4},{2,6},{4,0},{6,2},{8,12},{10,14},{12,8},{14,10},{16,20},{18,... | collective-permute-start | bytes 758792 | tf_op jit(solution)/shard_map/ppermute | solution.py:195
  25.8 4.1 %copy-start = (bf16[4,832,1664]{2,1,0:T(8,128)(2,1)S(1)}, bf16[4,832,1664]{2,1,0:T(8,128)(2,1)}, u32[]{:S(2)}) copy-start(bf16[4,832,1664]{2,1,0:T(8,128)(2,1)} %refs_2_.1) | copy-start | bytes 33226756
  30.0 1.1 %copy-start.4 = (bf16[448,832]{1,0:T(8,128)(2,1)S(1)}, bf16[448,832]{1,0:T(8,128)(2,1)}, u32[]{:S(2)}) copy-start(bf16[448,832]{1,0:T(8,128)(2,1)} %patches_ref.3) | copy-start | bytes 2236420
  31.1 3.6 %copy-start.5 = (bf16[512,832]{0,1:T(8,128)(2,1)S(1)}, bf16[512,832]{0,1:T(8,128)(2,1)}, u32[]{:S(2)}) copy-start(bf16[512,832]{0,1:T(8,128)(2,1)} %param.14) | copy-start | bytes 2555908
  31.1 12.6 %copy-start.8 = (bf16[104,2496]{1,0:T(8,128)(2,1)S(1)}, bf16[104,2496]{1,0:T(8,128)(2,1)}, u32[]{:S(2)}) copy-start(bf16[104,2496]{1,0:T(8,128)(2,1)} %copy-done.7) | copy-start | bytes 1557508
  31.1 12.6 %copy-start.10 = (bf16[104,2496]{1,0:T(8,128)(2,1)S(1)}, bf16[104,2496]{1,0:T(8,128)(2,1)}, u32[]{:S(2)}) copy-start(bf16[104,2496]{1,0:T(8,128)(2,1)} %param.16) | copy-start | bytes 1557508
  34.8 11.9 %collective-permute-start.13 = (bf16[832,512]{1,0:T(8,128)(2,1)S(1)}, bf16[832,512]{1,0:T(8,128)(2,1)S(1)}, u32[]{:S(2)}, u32[]{:S(2)}) collective-permute-start(bf16[832,512]{1,0:T(8,128)(2,1)S(1)} %bitcast.29), channel_id=1, source_target_pairs={{0,1},{1,0},{2,3},{3,2},{4,5},{5,4},{6,7},{7,6},{8,9},{9,8},{10,11... | collective-permute-start | bytes 2555912 | tf_op jit(solution)/shard_map/ppermute | solution.py:26
  38.0 8.6 %copy-start.9 = (bf16[104,2496]{1,0:T(8,128)(2,1)}, bf16[104,2496]{1,0:T(8,128)(2,1)S(1)}, u32[]{:S(2)}) copy-start(bf16[104,2496]{1,0:T(8,128)(2,1)S(1)} %constant_dynamic-update-slice_fusion) | copy-start | bytes 1557508
  38.0 12.7 %collective-permute-start.10 = (bf16[104,2496]{1,0:T(8,128)(2,1)}, bf16[104,2496]{1,0:T(8,128)(2,1)}, u32[]{:S(2)}, u32[]{:S(2)}) collective-permute-start(bf16[104,2496]{1,0:T(8,128)(2,1)} %collective-permute-done.4), channel_id=1, source_target_pairs={{0,4},{2,6},{4,0},{6,2},{8,12},{10,14},{12,8},{14,10},{16,20},{18,... | collective-permute-start | bytes 1557512 | tf_op jit(solution)/shard_map/ppermute | solution.py:191
  39.4 12.6 %collective-permute-start.9 = (bf16[104,2496]{1,0:T(8,128)(2,1)}, bf16[104,2496]{1,0:T(8,128)(2,1)}, u32[]{:S(2)}, u32[]{:S(2)}) collective-permute-start(bf16[104,2496]{1,0:T(8,128)(2,1)} %collective-permute-done.4), channel_id=1, source_target_pairs={{0,2},{2,0},{4,6},{6,4},{8,10},{10,8},{12,14},{14,12},{16,18},{18,... | collective-permute-start | bytes 1557512 | tf_op jit(solution)/shard_map/ppermute | solution.py:191
  40.9 12.2 %collective-permute-start.8 = (bf16[104,2496]{1,0:T(8,128)(2,1)}, bf16[104,2496]{1,0:T(8,128)(2,1)}, u32[]{:S(2)}, u32[]{:S(2)}) collective-permute-start(bf16[104,2496]{1,0:T(8,128)(2,1)} %collective-permute-done.4), channel_id=1, source_target_pairs={{0,8},{2,10},{4,12},{6,14},{8,24},{10,26},{12,28},{14,30},{16,0},{... | collective-permute-start | bytes 1557512 | tf_op jit(solution)/shard_map/ppermute | solution.py:188
  43.6 21.1 %copy-start.11 = (s32[2]{0:T(128)S(1)}, s32[2]{0:T(128)}, u32[]{:S(2)}) copy-start(s32[2]{0:T(128)} %param.18) | copy-start | bytes 28
  43.6 1.8 %collective-permute-start.7 = (f32[112,832]{1,0:T(8,128)S(1)}, f32[112,832]{1,0:T(8,128)S(1)}, u32[]{:S(2)}, u32[]{:S(2)}) collective-permute-start(f32[112,832]{1,0:T(8,128)S(1)} %constant_dynamic-slice_fusion.1), channel_id=1, source_target_pairs={{0,1},{1,0},{2,3},{3,2},{4,5},{5,4},{6,7},{7,6},{8,9},{9,8},{10,11... | collective-permute-start | bytes 1118216 | tf_op jit(solution)/shard_map/ppermute | solution.py:26
  53.2 20.6 %all-to-all-start = ((bf16[16,16,896]{2,1,0:T(8,128)(2,1)}), bf16[16,16,896]{2,1,0:T(8,128)(2,1)S(1)}, u32[]{:S(2)}, u32[]{:S(2)}) async-start(bf16[16,16,896]{2,1,0:T(8,128)(2,1)} %bitcast.5), calls=%async_computation | async-start | bytes 917504 | tf_op jit(solution)/shard_map/all_to_all | solution.py:252
  61.3 12.5 %collective-permute-start.18 = (bf16[104,1280]{1,0:T(8,128)(2,1)}, bf16[104,1280]{1,0:T(8,128)(2,1)S(1)}, u32[]{:S(2)}, u32[]{:S(2)}) collective-permute-start(bf16[104,1280]{1,0:T(8,128)(2,1)} %slice.37), channel_id=1, source_target_pairs={{0,2},{2,0},{4,6},{6,4},{8,10},{10,8},{12,14},{14,12},{16,18},{18,... | collective-permute-start | bytes 798728 | tf_op jit(solution)/shard_map/ppermute | solution.py:194
  63.2 10.6 %collective-permute-start.19 = (bf16[104,1216]{1,0:T(8,128)(2,1)}, bf16[104,1216]{1,0:T(8,128)(2,1)}, u32[]{:S(2)}, u32[]{:S(2)}) collective-permute-start(bf16[104,1216]{1,0:T(8,128)(2,1)} %slice.38), channel_id=1, source_target_pairs={{0,4},{2,6},{4,0},{6,2},{8,12},{10,14},{12,8},{14,10},{16,20},{18,... | collective-permute-start | bytes 758792 | tf_op jit(solution)/shard_map/ppermute | solution.py:195
  64.8 14.2 %collective-permute-start.15 = (bf16[104,2496]{1,0:T(8,128)(2,1)}, bf16[104,2496]{1,0:T(8,128)(2,1)}, u32[]{:S(2)}, u32[]{:S(2)}) collective-permute-start(bf16[104,2496]{1,0:T(8,128)(2,1)} %copy-done.9), channel_id=1, source_target_pairs={{0,8},{2,10},{4,12},{6,14},{8,24},{10,26},{12,28},{14,30},{16,0},{... | collective-permute-start | bytes 1557512 | tf_op jit(solution)/shard_map/ppermute | solution.py:188
  66.5 19.3 %collective-permute-start.17 = (bf16[104,2496]{1,0:T(8,128)(2,1)}, bf16[104,2496]{1,0:T(8,128)(2,1)S(1)}, u32[]{:S(2)}, u32[]{:S(2)}) collective-permute-start(bf16[104,2496]{1,0:T(8,128)(2,1)} %collective-permute-done.8), channel_id=1, source_target_pairs={{0,4},{2,6},{4,0},{6,2},{8,12},{10,14},{12,8},{14,10},{16,20},{18,... | collective-permute-start | bytes 1557512 | tf_op jit(solution)/shard_map/ppermute | solution.py:191
  67.2 18.7 %collective-permute-start.16 = (bf16[104,2496]{1,0:T(8,128)(2,1)}, bf16[104,2496]{1,0:T(8,128)(2,1)}, u32[]{:S(2)}, u32[]{:S(2)}) collective-permute-start(bf16[104,2496]{1,0:T(8,128)(2,1)} %collective-permute-done.8), channel_id=1, source_target_pairs={{0,2},{2,0},{4,6},{6,4},{8,10},{10,8},{12,14},{14,12},{16,18},{18,... | collective-permute-start | bytes 1557512 | tf_op jit(solution)/shard_map/ppermute | solution.py:191
  73.8 6.8 %collective-permute-start.14 = (bf16[256,896]{1,0:T(8,128)(2,1)S(1)}, bf16[256,896]{1,0:T(8,128)(2,1)S(1)}, u32[]{:S(2)}, u32[]{:S(2)}) collective-permute-start(bf16[256,896]{1,0:T(8,128)(2,1)S(1)} %bitcast.27), channel_id=1, source_target_pairs={{0,1},{1,0},{2,3},{3,2},{4,5},{5,4},{6,7},{7,6},{8,9},{9,8},{10,11... | collective-permute-start | bytes 1376264 | tf_op jit(solution)/shard_map/ppermute | solution.py:26
  80.6 2.0 %copy-start.6 = (bf16[416,2496]{1,0:T(8,128)(2,1)S(1)}, bf16[416,2496]{1,0:T(8,128)(2,1)}, u32[]{:S(2)}) copy-start(bf16[416,2496]{1,0:T(8,128)(2,1)} %pad_maximum_fusion) | copy-start | bytes 6230020
  82.5 1.7 %copy-start.1 = (bf16[16,104,512]{2,1,0:T(8,128)(2,1)}, bf16[16,104,512]{2,1,0:T(8,128)(2,1)S(1)}, u32[]{:S(2)}) copy-start(bf16[16,104,512]{2,1,0:T(8,128)(2,1)S(1)} %shard_map.120) | copy-start | bytes 5111812
  88.2 6.5 %slice-start = ((bf16[16,104,512]{2,1,0:T(8,128)(2,1)}), bf16[3,104,512]{2,1,0:T(8,128)(2,1)S(1)}, s32[]{:S(2)}) async-start(bf16[16,104,512]{2,1,0:T(8,128)(2,1)} %copy-done.1), calls=%async_computation.1 | async-start | bytes 638976 | tf_op jit(solution)/shard_map/slice | solution.py:259
  88.2 16.4 %collective-permute-start.20 = (bf16[104,1280]{1,0:T(8,128)(2,1)S(1)}, bf16[104,1280]{1,0:T(8,128)(2,1)S(1)}, u32[]{:S(2)}, u32[]{:S(2)}) collective-permute-start(bf16[104,1280]{1,0:T(8,128)(2,1)S(1)} %slice.41), channel_id=1, source_target_pairs={{0,2},{2,0},{4,6},{6,4},{8,10},{10,8},{12,14},{14,12},{16,18},{18,... | collective-permute-start | bytes 798728 | tf_op jit(solution)/shard_map/ppermute | solution.py:194
  89.7 14.9 %collective-permute-start.21 = (bf16[104,1216]{1,0:T(8,128)(2,1)S(1)}, bf16[104,1216]{1,0:T(8,128)(2,1)S(1)}, u32[]{:S(2)}, u32[]{:S(2)}) collective-permute-start(bf16[104,1216]{1,0:T(8,128)(2,1)S(1)} %slice.42), channel_id=1, source_target_pairs={{0,4},{2,6},{4,0},{6,2},{8,12},{10,14},{12,8},{14,10},{16,20},{18,... | collective-permute-start | bytes 758792 | tf_op jit(solution)/shard_map/ppermute | solution.py:195
  98.6 6.0 %copy-start.2 = (bf16[16,104,512]{2,1,0:T(8,128)(2,1)S(1)}, bf16[16,104,512]{2,1,0:T(8,128)(2,1)}, u32[]{:S(2)}) copy-start(bf16[16,104,512]{2,1,0:T(8,128)(2,1)} %copy-done.1) | copy-start | bytes 5111812

commit v8 on v7

--- a/solution.py
+++ b/solution.py
@@ -231,6 +231,8 @@
     held.append(along_line(held[2]))
     sides.append(to_sides(held[2]))
     merged = tp_scatter_sum(partial_value, n_tp, 1).astype(jnp.bfloat16)
+    merged, corners[0] = tie(merged, corners[0])
+    corners.append(along_line(corners[0]))
     padding = (-width - 2) % 128
     payload = jnp.concatenate(
         [merged, code_cols, jnp.zeros((token_count, padding), jnp.bfloat16)], axis=1
@@ -243,17 +245,19 @@
 
     first_group = group(0)
 
-    outgoing, held[3], sides[2], corners[0], texts, first_group = tie(
-        outgoing, held[3], sides[2], corners[0], texts, first_group
+    outgoing, held[3], sides[2], texts, first_group = tie(
+        outgoing, held[3], sides[2], texts, first_group
     )
     sides.append(to_sides(held[3]))
-    corners.append(along_line(corners[0]))
-    corners.append(to_corner(*sides[2]))
     arrived = lax.all_to_all(
         outgoing.reshape(n_req, IMG_CAP, -1), "req", split_axis=0, concat_axis=0
     ).reshape(slot_count, -1)
+    arrived, corners[1] = tie(arrived, corners[1])
+    corners.append(along_line(corners[1]))
     images = [arrived] + [tp_shift(arrived, n_tp, d) for d in range(1, n_tp)]
     blocks = combine(tp_index, order, texts, images, gain_column)
+    second_group = group(1)
+    blocks, sides[3], second_group = tie(blocks, sides[3], second_group)
 
     def product(first, count, weight):
         source = blocks[first : first + count].reshape(count * rows, row_count)
@@ -262,17 +266,17 @@
             source, weight, (((0,), (0,)), ((), ())), preferred_element_type=jnp.float32
         )
 
-    total = product(0, 4, first_group) + product(4, 4, group(1))
-
-    total, sides[3] = tie(total, sides[3])
+    total = product(0, 4, first_group)
+    (total,) = tie(total + product(4, 4, second_group))
+
     for step in range(4, lines):
         held.append(along_line(held[step - 1]))
         sides.append(to_sides(held[step]))
-        corners.append(to_corner(*sides[step - 1]))
+        corners.append(along_line(corners[step - 2]))
     corners.append(to_corner(*sides[-1]))
+    (total,) = tie(total + product(lines * 4 - 4, 3, group(lines - 1, False)))
     for step in range(2, lines - 1):
-        total += product(step * 4, 4, group(step))
-    total += product(lines * 4 - 4, 3, group(lines - 1, False))
+        (total,) = tie(total + product(step * 4, 4, group(step)))
     total, corners[-1] = tie(total, corners[-1])
 
     position = me * row_count + jnp.arange(row_count, dtype=jnp.int32)

time: 109 us -> 103 us (0.945)
  waiting for transfers between devices: 22.3 us -> 31.5 us
  other arithmetic: 19.2 us -> 12.8 us
  matrix products: 12.9 us -> 8.37 us
  local copies, waits for them, and re-layouts: 16.3 us -> 13.3 us
  starting transfers between devices: 31.7 us -> 29.8 us
    ppermute x4 -> x5, waiting for transfers between devices: 4.22 us -> 19.1 us  [along_line(): return lax.ppermute(block, 'req', line_perm)]
    ppermute x3 -> x2, waiting for transfers between devices: 8.22 us -> 0.18 us  [to_corner(): right = lax.ppermute(by_x[:, cut:], 'req', y_perm)]
    add x1 -> x0, other arithmetic: 6.03 us -> none  [shards(): total += product(lines * 4 - 4, 3, group(lines - 1, False))]
    dot_general x5, matrix products: 11.8 us -> 7.29 us  [product(): lax.dot_general(source, weight, (((0,), (0,)), ((), ())), preferred_eleme...]
    ppermute x3 -> x2, waiting for transfers between devices: 0.01 us -> 4.23 us  [to_corner(): left = lax.ppermute(by_y[:, :cut], 'req', x_perm)]
    slice x3 -> x2, local copies, waits for them, and re-layouts: 3.36 us -> 1.19 us  [to_corner(): right = lax.ppermute(by_x[:, cut:], 'req', y_perm)]
    ppermute x4, waiting for transfers between devices: 4.42 us -> 2.46 us  [to_sides(): lax.ppermute(block, 'req', y_perm)]
    concatenate x4, other arithmetic: 9.05 us -> 7.7 us  [group(): return jnp.concatenate(pieces, axis=0)]
  transfers between devices with their start and end apart: 23 -> 22, of which waited for: 10 -> 10; matrix products, arithmetic and copies ran while one was open for 33% -> 24% of each run, Pallas kernels for 5% -> 6%
where the time goes in v8:
time: 103 us; the launch traced here: 102 us
  waiting for transfers between devices  31.5 us (31%)
  starting transfers between devices  29.8 us (29%)
  local copies, waits for them, and re-layouts  13.3 us (13%)
  other arithmetic  12.8 us (12%)
  matrix products  8.37 us (8%)
  Pallas kernels  5.76 us (6%)
    ppermute x5, waiting for transfers between devices, along_line(): return lax.ppermute(block, 'req', line_perm)  19.1 us
    concatenate x4, other arithmetic, group(): return jnp.concatenate(pieces, axis=0)  7.7 us
    ppermute x5, starting transfers between devices, along_line(): return lax.ppermute(block, 'req', line_perm)  7.52 us
    dot_general x5, matrix products, product(): lax.dot_general(source, weight, (((0,), (0,)), ((), ())), preferred_eleme...  7.29 us
    unnamed x20, local copies, waits for them, and re-layouts  6.46 us
    ppermute x4, starting transfers between devices, to_sides(): lax.ppermute(block, 'req', x_perm)  6.44 us
    ppermute x4, starting transfers between devices, to_sides(): lax.ppermute(block, 'req', y_perm)  6.09 us
    ppermute x4, waiting for transfers between devices, to_sides(): lax.ppermute(block, 'req', x_perm)  5.56 us
  transfers between devices with their start and end apart: 22, of which 10 were waited for; matrix products, arithmetic and copies ran while one was open for 24% of the time, Pallas kernels for 6%

profile of v8, /device:TPU:0, one launch (start us, length us, event | category | flops | bytes accessed | tf_op | source)
XLA Modules:
  0.0 101.9 jit_solution(13365526911260653968)
XLA Ops:
  0.0 2.9 %collective-permute-start.2 = (bf16[104,2496]{1,0:T(8,128)(2,1)}, bf16[104,2496]{1,0:T(8,128)(2,1)S(1)}, u32[]{:S(2)}, u32[]{:S(2)}) collective-permute-start(bf16[104,2496]{1,0:T(8,128)(2,1)} %param.16), channel_id=1, source_target_pairs={{0,2},{2,0},{4,6},{6,4},{8,10},{10,8},{12,14},{14,12},{16,18},{18,... | collective-permute-start | bytes 1557512 | tf_op jit(solution)/shard_map/ppermute | solution.py:191
  2.9 1.6 %collective-permute-start.1 = (bf16[104,2496]{1,0:T(8,128)(2,1)}, bf16[104,2496]{1,0:T(8,128)(2,1)}, u32[]{:S(2)}, u32[]{:S(2)}) collective-permute-start(bf16[104,2496]{1,0:T(8,128)(2,1)} %param.16), channel_id=1, source_target_pairs={{0,8},{2,10},{4,12},{6,14},{8,24},{10,26},{12,28},{14,30},{16,0},{... | collective-permute-start | bytes 1557512 | tf_op jit(solution)/shard_map/ppermute | solution.py:188
  4.5 1.5 %collective-permute-start.3 = (bf16[104,2496]{1,0:T(8,128)(2,1)}, bf16[104,2496]{1,0:T(8,128)(2,1)}, u32[]{:S(2)}, u32[]{:S(2)}) collective-permute-start(bf16[104,2496]{1,0:T(8,128)(2,1)} %param.16), channel_id=1, source_target_pairs={{0,4},{2,6},{4,0},{6,2},{8,12},{10,14},{12,8},{14,10},{16,20},{18,... | collective-permute-start | bytes 1557512 | tf_op jit(solution)/shard_map/ppermute | solution.py:191
  6.0 1.1 %copy-done.3 = bf16[448,832]{1,0:T(8,128)(2,1)S(1)} copy-done((bf16[448,832]{1,0:T(8,128)(2,1)S(1)}, bf16[448,832]{1,0:T(8,128)(2,1)}, u32[]{:S(2)}) %copy-start.3) | copy-done | bytes 745496
  7.2 0.3 shard_map.118.refs_0_
  7.5 0.5 collective-permute-start.13
  8.0 0.7 stack.19
  8.7 0.7 stack.20
  9.4 0.8 reshape.52
  10.2 0.7 fusion.12.order_ref
  10.9 4.3 %collective-permute-done.2 = bf16[104,2496]{1,0:T(8,128)(2,1)S(1)} collective-permute-done((bf16[104,2496]{1,0:T(8,128)(2,1)}, bf16[104,2496]{1,0:T(8,128)(2,1)S(1)}, u32[]{:S(2)}, u32[]{:S(2)}) %collective-permute-start.2) | collective-permute-done | bytes 519200 | tf_op jit(solution)/shard_map/ppermute | solution.py:191
  15.2 2.5 %collective-permute-done.1 = bf16[104,2496]{1,0:T(8,128)(2,1)} collective-permute-done((bf16[104,2496]{1,0:T(8,128)(2,1)}, bf16[104,2496]{1,0:T(8,128)(2,1)}, u32[]{:S(2)}, u32[]{:S(2)}) %collective-permute-start.1) | collective-permute-done | bytes 519200 | tf_op jit(solution)/shard_map/ppermute | solution.py:188
  17.7 0.4 collective-permute-done.3
  18.1 1.5 %collective-permute-start.6 = (bf16[104,2496]{1,0:T(8,128)(2,1)}, bf16[104,2496]{1,0:T(8,128)(2,1)}, u32[]{:S(2)}, u32[]{:S(2)}) collective-permute-start(bf16[104,2496]{1,0:T(8,128)(2,1)} %collective-permute-done.1), channel_id=1, source_target_pairs={{0,4},{2,6},{4,0},{6,2},{8,12},{10,14},{12,8},{14,10},{16,20},{18,... | collective-permute-start | bytes 1557512 | tf_op jit(solution)/shard_map/ppermute | solution.py:191
  19.6 0.5 collective-permute-start.5
  20.2 2.6 %collective-permute-start.4 = (bf16[104,2496]{1,0:T(8,128)(2,1)}, bf16[104,2496]{1,0:T(8,128)(2,1)}, u32[]{:S(2)}, u32[]{:S(2)}) collective-permute-start(bf16[104,2496]{1,0:T(8,128)(2,1)} %collective-permute-done.1), channel_id=1, source_target_pairs={{0,8},{2,10},{4,12},{6,14},{8,24},{10,26},{12,28},{14,30},{16,0},{... | collective-permute-start | bytes 1557512 | tf_op jit(solution)/shard_map/ppermute | solution.py:188
  22.8 0.7 convert_bitcast_fusion.1
  23.4 0.2 convert_reduce_fusion
  23.6 0.6 collective-permute-start.9
  24.2 4.1 %copy-done = bf16[4,832,1664]{2,1,0:T(8,128)(2,1)S(1)} copy-done((bf16[4,832,1664]{2,1,0:T(8,128)(2,1)S(1)}, bf16[4,832,1664]{2,1,0:T(8,128)(2,1)}, u32[]{:S(2)}) %copy-start) | copy-done | bytes 11075608
  28.4 1.1 %copy-done.4 = bf16[448,832]{1,0:T(8,128)(2,1)S(1)} copy-done((bf16[448,832]{1,0:T(8,128)(2,1)S(1)}, bf16[448,832]{1,0:T(8,128)(2,1)}, u32[]{:S(2)}) %copy-start.4) | copy-done | bytes 745496
  29.5 3.6 %shard_map.119 = f32[112,1664]{1,0:T(8,128)S(1)} custom-call(bf16[448,832]{1,0:T(8,128)(2,1)S(1)} %copy-done.4, bf16[2,832]{1,0:T(2,128)(2,1)S(1)} %pad_maximum_fusion.6.gain_bias_ref, f32[448,256]{1,0:T(8,128)S(1)} %shard_map.118.refs_0_, f32[448,256]{1,0:T(8,128)S(1)} %collective-permute-done.refs_1_, bf16[4,832,1664]{2,1,0:T(8,128)(2,1)S(1)} %copy-done), custom_call_target="tpu_custom_call" | custom-call | flops 1000 | bytes 1000 | tf_op jit(solution)/shard_map/pallas_call | solution.py:110
  33.1 1.0 slice.27
  34.1 1.6 %collective-permute-start.8 = (bf16[104,1280]{1,0:T(8,128)(2,1)S(1)}, bf16[104,1280]{1,0:T(8,128)(2,1)}, u32[]{:S(2)}, u32[]{:S(2)}) collective-permute-start(bf16[104,1280]{1,0:T(8,128)(2,1)S(1)} %slice.27), channel_id=1, source_target_pairs={{0,2},{2,0},{4,6},{6,4},{8,10},{10,8},{12,14},{14,12},{16,18},{18,... | collective-permute-start | bytes 798728 | tf_op jit(solution)/shard_map/ppermute | solution.py:194
  35.7 0.2 constant_dynamic-slice_fusion.1
  36.0 0.1 copy.17
  36.1 0.1 copy.16
  36.2 0.1 pad.20.clone
  36.3 0.2 collective-permute-done.9
  36.5 4.2 %collective-permute-done.8 = bf16[104,1280]{1,0:T(8,128)(2,1)} collective-permute-done((bf16[104,1280]{1,0:T(8,128)(2,1)S(1)}, bf16[104,1280]{1,0:T(8,128)(2,1)}, u32[]{:S(2)}, u32[]{:S(2)}) %collective-permute-start.8) | collective-permute-done | bytes 266272 | tf_op jit(solution)/shard_map/ppermute | solution.py:194
  40.7 1.1 %pad_maximum_fusion.4 = bf16[104,2496]{1,0:T(8,128)(2,1)S(1)} fusion(bf16[104,1216]{1,0:T(8,128)(2,1)} %collective-permute-done.9, bf16[104,1280]{1,0:T(8,128)(2,1)} %collective-permute-done.8), kind=kLoop, calls=%fused_computation.9 | loop fusion | flops 1038336 | bytes 1038336 | tf_op jit(solution)/shard_map/concatenate | solution.py:196
  41.8 1.6 %collective-permute-start.12 = (bf16[104,2496]{1,0:T(8,128)(2,1)}, bf16[104,2496]{1,0:T(8,128)(2,1)}, u32[]{:S(2)}, u32[]{:S(2)}) collective-permute-start(bf16[104,2496]{1,0:T(8,128)(2,1)} %collective-permute-done.4), channel_id=1, source_target_pairs={{0,4},{2,6},{4,0},{6,2},{8,12},{10,14},{12,8},{14,10},{16,20},{18,... | collective-permute-start | bytes 1557512 | tf_op jit(solution)/shard_map/ppermute | solution.py:191
  43.4 1.5 %collective-permute-start.11 = (bf16[104,2496]{1,0:T(8,128)(2,1)}, bf16[104,2496]{1,0:T(8,128)(2,1)}, u32[]{:S(2)}, u32[]{:S(2)}) collective-permute-start(bf16[104,2496]{1,0:T(8,128)(2,1)} %collective-permute-done.4), channel_id=1, source_target_pairs={{0,2},{2,0},{4,6},{6,4},{8,10},{10,8},{12,14},{14,12},{16,18},{18,... | collective-permute-start | bytes 1557512 | tf_op jit(solution)/shard_map/ppermute | solution.py:191
  44.9 1.2 %collective-permute-start.10 = (bf16[104,2496]{1,0:T(8,128)(2,1)}, bf16[104,2496]{1,0:T(8,128)(2,1)}, u32[]{:S(2)}, u32[]{:S(2)}) collective-permute-start(bf16[104,2496]{1,0:T(8,128)(2,1)} %collective-permute-done.4), channel_id=1, source_target_pairs={{0,8},{2,10},{4,12},{6,14},{8,24},{10,26},{12,28},{14,30},{16,0},{... | collective-permute-start | bytes 1557512 | tf_op jit(solution)/shard_map/ppermute | solution.py:188
  46.1 0.2 add_convert_fusion
  46.3 1.1 %convolution_convert_fusion = bf16[256,896]{1,0:T(8,128)(2,1)} fusion(bf16[112,1]{1,0:T(8,128)(2,1)S(1)} %copy.17, bf16[112,1]{1,0:T(8,128)(2,1)S(1)} %copy.16, bf16[112,832]{1,0:T(8,128)(2,1)S(1)} %add_convert_fusion, bf16[896]{0:T(1024)(128)(2,1)S(1)} %pad.20.clone, s32[112]{0:T(128)S(1)} %multiply_add_fusion), kind=kOutput, calls=%fused_computation.8 | convolution fusion | flops 52441088 | bytes 647808 | tf_op jit(solution)/shard_map/dot_general | solution.py:240
  47.4 2.9 %pad_maximum_fusion = bf16[416,2496]{1,0:T(8,128)(2,1)} fusion(bf16[104,2496]{1,0:T(8,128)(2,1)S(1)} %pad_maximum_fusion.4, bf16[104,2496]{1,0:T(8,128)(2,1)} %collective-permute-done.3, bf16[104,2496]{1,0:T(8,128)(2,1)} %copy-done.8, bf16[104,2496]{1,0:T(8,128)(2,1)} %param.16), kind=kLoop, calls=%fused_computation.4 | loop fusion | flops 8306688 | bytes 4153344 | tf_op jit(solution)/shard_map/concatenate | solution.py:244
  50.2 2.1 %collective-permute-done.12 = bf16[104,2496]{1,0:T(8,128)(2,1)} collective-permute-done((bf16[104,2496]{1,0:T(8,128)(2,1)}, bf16[104,2496]{1,0:T(8,128)(2,1)}, u32[]{:S(2)}, u32[]{:S(2)}) %collective-permute-start.12) | collective-permute-done | bytes 519200 | tf_op jit(solution)/shard_map/ppermute | solution.py:191
  52.3 1.2 %collective-permute-done.11 = bf16[104,2496]{1,0:T(8,128)(2,1)} collective-permute-done((bf16[104,2496]{1,0:T(8,128)(2,1)}, bf16[104,2496]{1,0:T(8,128)(2,1)}, u32[]{:S(2)}, u32[]{:S(2)}) %collective-permute-start.11) | collective-permute-done | bytes 519200 | tf_op jit(solution)/shard_map/ppermute | solution.py:191
  53.5 2.1 %collective-permute-done.10 = bf16[104,2496]{1,0:T(8,128)(2,1)} collective-permute-done((bf16[104,2496]{1,0:T(8,128)(2,1)}, bf16[104,2496]{1,0:T(8,128)(2,1)}, u32[]{:S(2)}, u32[]{:S(2)}) %collective-permute-start.10) | collective-permute-done | bytes 519200 | tf_op jit(solution)/shard_map/ppermute | solution.py:188
  55.6 3.9 %all-to-all-start = ((bf16[16,16,896]{2,1,0:T(8,128)(2,1)}), bf16[16,16,896]{2,1,0:T(8,128)(2,1)S(1)}, u32[]{:S(2)}, u32[]{:S(2)}) async-start(bf16[16,16,896]{2,1,0:T(8,128)(2,1)} %bitcast.5), calls=%async_computation | async-start | bytes 917504 | tf_op jit(solution)/shard_map/all_to_all | solution.py:252
  59.5 1.9 %collective-permute-start.14 = (bf16[104,2496]{1,0:T(8,128)(2,1)}, bf16[104,2496]{1,0:T(8,128)(2,1)}, u32[]{:S(2)}, u32[]{:S(2)}) collective-permute-start(bf16[104,2496]{1,0:T(8,128)(2,1)} %copy-done.7), channel_id=1, source_target_pairs={{0,8},{2,10},{4,12},{6,14},{8,24},{10,26},{12,28},{14,30},{16,0},{... | collective-permute-start | bytes 1557512 | tf_op jit(solution)/shard_map/ppermute | solution.py:188
  61.5 0.1 fusion.9
  61.6 1.5 %collective-permute-start.17 = (bf16[104,2496]{1,0:T(8,128)(2,1)}, bf16[104,2496]{1,0:T(8,128)(2,1)}, u32[]{:S(2)}, u32[]{:S(2)}) collective-permute-start(bf16[104,2496]{1,0:T(8,128)(2,1)} %collective-permute-done.10), channel_id=1, source_target_pairs={{0,4},{2,6},{4,0},{6,2},{8,12},{10,14},{12,8},{14,10},{16,20},{18,... | collective-permute-start | bytes 1557512 | tf_op jit(solution)/shard_map/ppermute | solution.py:191
  63.0 1.5 %collective-permute-start.16 = (bf16[104,2496]{1,0:T(8,128)(2,1)}, bf16[104,2496]{1,0:T(8,128)(2,1)}, u32[]{:S(2)}, u32[]{:S(2)}) collective-permute-start(bf16[104,2496]{1,0:T(8,128)(2,1)} %collective-permute-done.10), channel_id=1, source_target_pairs={{0,2},{2,0},{4,6},{6,4},{8,10},{10,8},{12,14},{14,12},{16,18},{18,... | collective-permute-start | bytes 1557512 | tf_op jit(solution)/shard_map/ppermute | solution.py:191
  64.5 14.2 %collective-permute-done.14 = bf16[104,2496]{1,0:T(8,128)(2,1)} collective-permute-done((bf16[104,2496]{1,0:T(8,128)(2,1)}, bf16[104,2496]{1,0:T(8,128)(2,1)}, u32[]{:S(2)}, u32[]{:S(2)}) %collective-permute-start.14) | collective-permute-done | bytes 519200 | tf_op jit(solution)/shard_map/ppermute | solution.py:188
  78.7 0.3 copy.18.gain_ref
  79.0 0.2 collective-permute-start.18
  79.3 1.7 %pad_maximum_fusion.1 = bf16[416,2496]{1,0:T(8,128)(2,1)S(1)} fusion(bf16[104,2496]{1,0:T(8,128)(2,1)} %collective-permute-done.14, bf16[104,2496]{1,0:T(8,128)(2,1)} %collective-permute-done.6, bf16[104,2496]{1,0:T(8,128)(2,1)} %collective-permute-done.5, bf16[104,2496]{1,0:T(8,128)(2,1)} %collective-permute-done.1), kind=kLoop, calls=%fused_computation.5 | loop fusion | flops 8306688 | bytes 4153344 | tf_op jit(solution)/shard_map/concatenate | solution.py:244
  81.0 1.8 %shard_map.120 = bf16[16,104,512]{2,1,0:T(8,128)(2,1)S(1)} custom-call(s32[1]{0:T(128)} %bitcast.4.index_ref, s32[16]{0:T(128)S(1)} %fusion.12.order_ref, bf16[16,104,1]{2,1,0:T(8,128)(2,1)S(1)} %copy.18.gain_ref, bf16[832,512]{1,0:T(8,128)(2,1)S(1)} %bitcast.30, bf16[832,512]{1,0:T(8,128)(2,1)S(1)} %collective-permute-done.13.refs_1_, ...), custom_call_target="tpu_custom_call" | custom-call | flops 1000 | bytes 1000 | tf_op jit(solution)/shard_map/pallas_call | solution.py:162
  82.9 1.2 %slice.34 = bf16[104,1216]{1,0:T(8,128)(2,1)S(1)} slice(bf16[104,2496]{1,0:T(8,128)(2,1)} %collective-permute-done.16), slice={[0:104], [1280:2496]} | slice | bytes 505856 | tf_op jit(solution)/shard_map/slice | solution.py:195
  84.0 1.0 slice.33
  85.0 1.6 %pad_maximum_fusion.3 = bf16[312,2496]{1,0:T(8,128)(2,1)S(1)} fusion(bf16[104,2496]{1,0:T(8,128)(2,1)} %collective-permute-done.17, bf16[104,2496]{1,0:T(8,128)(2,1)} %collective-permute-done.16, bf16[104,2496]{1,0:T(8,128)(2,1)} %collective-permute-done.10), kind=kLoop, calls=%fused_computation.7 | loop fusion | flops 4672512 | bytes 3115008 | tf_op jit(solution)/shard_map/concatenate | solution.py:244
  86.7 0.1 fusion.16
  86.8 1.5 %collective-permute-start.19 = (bf16[104,1280]{1,0:T(8,128)(2,1)S(1)}, bf16[104,1280]{1,0:T(8,128)(2,1)S(1)}, u32[]{:S(2)}, u32[]{:S(2)}) collective-permute-start(bf16[104,1280]{1,0:T(8,128)(2,1)S(1)} %slice.33), channel_id=1, source_target_pairs={{0,2},{2,0},{4,6},{6,4},{8,10},{10,8},{12,14},{14,12},{16,18},{18,... | collective-permute-start | bytes 798728 | tf_op jit(solution)/shard_map/ppermute | solution.py:194
  88.3 1.5 %collective-permute-start.20 = (bf16[104,1216]{1,0:T(8,128)(2,1)S(1)}, bf16[104,1216]{1,0:T(8,128)(2,1)S(1)}, u32[]{:S(2)}, u32[]{:S(2)}) collective-permute-start(bf16[104,1216]{1,0:T(8,128)(2,1)S(1)} %slice.34), channel_id=1, source_target_pairs={{0,4},{2,6},{4,0},{6,2},{8,12},{10,14},{12,8},{14,10},{16,20},{18,... | collective-permute-start | bytes 758792 | tf_op jit(solution)/shard_map/ppermute | solution.py:195
  89.8 1.6 %fusion.17 = f32[512,2496]{0,1:T(8,128)S(1)} fusion(bf16[416,512]{1,0:T(8,128)(2,1)S(1)} %bitcast.33, bf16[416,2496]{1,0:T(8,128)(2,1)S(1)} %copy-done.6), kind=kOutput, calls=%fused_computation.49 | convolution fusion | flops 1063256064 | bytes 7614464 | tf_op jit(solution)/shard_map/dot_general | solution.py:265
  91.4 1.7 %convolution_add_fusion.2 = f32[512,2496]{0,1:T(8,128)S(1)} fusion(f32[512,2496]{0,1:T(8,128)S(1)} %fusion.17, bf16[416,512]{1,0:T(8,128)(2,1)S(1)} %bitcast.32, bf16[416,2496]{1,0:T(8,128)(2,1)S(1)} %pad_maximum_fusion.1), kind=kOutput, calls=%fused_computation.3 | convolution fusion | flops 1064534016 | bytes 12726272 | tf_op jit(solution)/shard_map/dot_general | solution.py:265
  93.0 1.5 %convolution_add_fusion = f32[512,2496]{0,1:T(8,128)S(1)} fusion(f32[512,2496]{0,1:T(8,128)S(1)} %convolution_add_fusion.2, bf16[312,512]{1,0:T(8,128)(2,1)S(1)} %bitcast.26, bf16[312,2496]{1,0:T(8,128)(2,1)S(1)} %pad_maximum_fusion.3), kind=kOutput, calls=%fused_computation.1 | convolution fusion | flops 798720000 | bytes 12100608 | tf_op jit(solution)/shard_map/dot_general | solution.py:265
  94.6 0.3 collective-permute-done.18
  94.9 1.5 %pad_maximum_fusion.2 = bf16[416,2496]{1,0:T(8,128)(2,1)S(1)} fusion(bf16[104,2496]{1,0:T(8,128)(2,1)S(1)} %collective-permute-done.18, bf16[104,2496]{1,0:T(8,128)(2,1)} %collective-permute-done.12, bf16[104,2496]{1,0:T(8,128)(2,1)} %collective-permute-done.11, bf16[104,2496]{1,0:T(8,128)(2,1)} %collective-permute-done.4), kind=kLoop, calls=%fused_computation.6 | loop fusion | flops 8306688 | bytes 4153344 | tf_op jit(solution)/shard_map/concatenate | solution.py:244
  96.4 1.7 %convolution_add_fusion.1 = f32[512,2496]{0,1:T(8,128)S(1)} fusion(f32[512,2496]{0,1:T(8,128)S(1)} %convolution_add_fusion, bf16[416,512]{1,0:T(8,128)(2,1)S(1)} %bitcast.31, bf16[416,2496]{1,0:T(8,128)(2,1)S(1)} %pad_maximum_fusion.2), kind=kOutput, calls=%fused_computation.2 | convolution fusion | flops 1064534016 | bytes 12726272 | tf_op jit(solution)/shard_map/dot_general | solution.py:265
  98.2 0.9 fusion.18
  99.0 2.8 %select_convert_fusion = bf16[512,2496]{0,1:T(8,128)(2,1)} fusion(f32[512,2496]{0,1:T(8,128)S(1)} %convolution_add_fusion.1, f32[512,2496]{0,1:T(8,128)S(1)} %fusion.18, pred[512]{0:T(512)(128)(4,1)S(1)} %fusion.10), kind=kLoop, calls=%fused_computation | loop fusion | flops 3833856 | bytes 12780032 | tf_op jit(solution)/shard_map/convert_element_type | solution.py:292
  (43 shorter events, 0.3 us)
Async XLA Ops:
  0.0 15.2 %collective-permute-start.2 = (bf16[104,2496]{1,0:T(8,128)(2,1)}, bf16[104,2496]{1,0:T(8,128)(2,1)S(1)}, u32[]{:S(2)}, u32[]{:S(2)}) collective-permute-start(bf16[104,2496]{1,0:T(8,128)(2,1)} %param.16), channel_id=1, source_target_pairs={{0,2},{2,0},{4,6},{6,4},{8,10},{10,8},{12,14},{14,12},{16,18},{18,... | collective-permute-start | bytes 1557512 | tf_op jit(solution)/shard_map/ppermute | solution.py:191
  2.9 14.8 %collective-permute-start.1 = (bf16[104,2496]{1,0:T(8,128)(2,1)}, bf16[104,2496]{1,0:T(8,128)(2,1)}, u32[]{:S(2)}, u32[]{:S(2)}) collective-permute-start(bf16[104,2496]{1,0:T(8,128)(2,1)} %param.16), channel_id=1, source_target_pairs={{0,8},{2,10},{4,12},{6,14},{8,24},{10,26},{12,28},{14,30},{16,0},{... | collective-permute-start | bytes 1557512 | tf_op jit(solution)/shard_map/ppermute | solution.py:188
  4.5 13.6 %collective-permute-start.3 = (bf16[104,2496]{1,0:T(8,128)(2,1)}, bf16[104,2496]{1,0:T(8,128)(2,1)}, u32[]{:S(2)}, u32[]{:S(2)}) collective-permute-start(bf16[104,2496]{1,0:T(8,128)(2,1)} %param.16), channel_id=1, source_target_pairs={{0,4},{2,6},{4,0},{6,2},{8,12},{10,14},{12,8},{14,10},{16,20},{18,... | collective-permute-start | bytes 1557512 | tf_op jit(solution)/shard_map/ppermute | solution.py:191
  6.0 1.1 %copy-start.3 = (bf16[448,832]{1,0:T(8,128)(2,1)S(1)}, bf16[448,832]{1,0:T(8,128)(2,1)}, u32[]{:S(2)}) copy-start(bf16[448,832]{1,0:T(8,128)(2,1)} %patches_ref.3) | copy-start | bytes 2236420
  7.5 3.5 %collective-permute-start = (f32[448,256]{1,0:T(8,128)S(1)}, f32[448,256]{1,0:T(8,128)S(1)}, u32[]{:S(2)}, u32[]{:S(2)}) collective-permute-start(f32[448,256]{1,0:T(8,128)S(1)} %shard_map.118.refs_0_), channel_id=1, source_target_pairs={{0,1},{1,0},{2,3},{3,2},{4,5},{5,4},{6,7},{7,6},{8,9},{9,8},{10,11... | collective-permute-start | bytes 1376264 | tf_op jit(solution)/shard_map/ppermute | solution.py:26
  7.5 42.7 %collective-permute-start.13 = (bf16[832,512]{1,0:T(8,128)(2,1)}, bf16[832,512]{1,0:T(8,128)(2,1)S(1)}, u32[]{:S(2)}, u32[]{:S(2)}) collective-permute-start(bf16[832,512]{1,0:T(8,128)(2,1)} %bitcast.29), channel_id=1, source_target_pairs={{0,1},{1,0},{2,3},{3,2},{4,5},{5,4},{6,7},{7,6},{8,9},{9,8},{10,11... | collective-permute-start | bytes 2555912 | tf_op jit(solution)/shard_map/ppermute | solution.py:26
  15.2 8.4 %copy-start.8 = (bf16[104,2496]{1,0:T(8,128)(2,1)}, bf16[104,2496]{1,0:T(8,128)(2,1)S(1)}, u32[]{:S(2)}) copy-start(bf16[104,2496]{1,0:T(8,128)(2,1)S(1)} %collective-permute-done.2) | copy-start | bytes 1557508
  18.1 16.0 %collective-permute-start.6 = (bf16[104,2496]{1,0:T(8,128)(2,1)}, bf16[104,2496]{1,0:T(8,128)(2,1)}, u32[]{:S(2)}, u32[]{:S(2)}) collective-permute-start(bf16[104,2496]{1,0:T(8,128)(2,1)} %collective-permute-done.1), channel_id=1, source_target_pairs={{0,4},{2,6},{4,0},{6,2},{8,12},{10,14},{12,8},{14,10},{16,20},{18,... | collective-permute-start | bytes 1557512 | tf_op jit(solution)/shard_map/ppermute | solution.py:191
  19.6 16.1 %collective-permute-start.5 = (bf16[104,2496]{1,0:T(8,128)(2,1)}, bf16[104,2496]{1,0:T(8,128)(2,1)}, u32[]{:S(2)}, u32[]{:S(2)}) collective-permute-start(bf16[104,2496]{1,0:T(8,128)(2,1)} %collective-permute-done.1), channel_id=1, source_target_pairs={{0,2},{2,0},{4,6},{6,4},{8,10},{10,8},{12,14},{14,12},{16,18},{18,... | collective-permute-start | bytes 1557512 | tf_op jit(solution)/shard_map/ppermute | solution.py:191
  20.2 15.5 %collective-permute-start.4 = (bf16[104,2496]{1,0:T(8,128)(2,1)}, bf16[104,2496]{1,0:T(8,128)(2,1)}, u32[]{:S(2)}, u32[]{:S(2)}) collective-permute-start(bf16[104,2496]{1,0:T(8,128)(2,1)} %collective-permute-done.1), channel_id=1, source_target_pairs={{0,8},{2,10},{4,12},{6,14},{8,24},{10,26},{12,28},{14,30},{16,0},{... | collective-permute-start | bytes 1557512 | tf_op jit(solution)/shard_map/ppermute | solution.py:188
  23.6 12.8 %collective-permute-start.9 = (bf16[104,1216]{1,0:T(8,128)(2,1)S(1)}, bf16[104,1216]{1,0:T(8,128)(2,1)}, u32[]{:S(2)}, u32[]{:S(2)}) collective-permute-start(bf16[104,1216]{1,0:T(8,128)(2,1)S(1)} %slice.28), channel_id=1, source_target_pairs={{0,4},{2,6},{4,0},{6,2},{8,12},{10,14},{12,8},{14,10},{16,20},{18,... | collective-permute-start | bytes 758792 | tf_op jit(solution)/shard_map/ppermute | solution.py:195
  24.2 4.1 %copy-start = (bf16[4,832,1664]{2,1,0:T(8,128)(2,1)S(1)}, bf16[4,832,1664]{2,1,0:T(8,128)(2,1)}, u32[]{:S(2)}) copy-start(bf16[4,832,1664]{2,1,0:T(8,128)(2,1)} %refs_2_.1) | copy-start | bytes 33226756
  28.4 1.1 %copy-start.4 = (bf16[448,832]{1,0:T(8,128)(2,1)S(1)}, bf16[448,832]{1,0:T(8,128)(2,1)}, u32[]{:S(2)}) copy-start(bf16[448,832]{1,0:T(8,128)(2,1)} %patches_ref.3) | copy-start | bytes 2236420
  34.1 6.6 %collective-permute-start.8 = (bf16[104,1280]{1,0:T(8,128)(2,1)S(1)}, bf16[104,1280]{1,0:T(8,128)(2,1)}, u32[]{:S(2)}, u32[]{:S(2)}) collective-permute-start(bf16[104,1280]{1,0:T(8,128)(2,1)S(1)} %slice.27), channel_id=1, source_target_pairs={{0,2},{2,0},{4,6},{6,4},{8,10},{10,8},{12,14},{14,12},{16,18},{18,... | collective-permute-start | bytes 798728 | tf_op jit(solution)/shard_map/ppermute | solution.py:194
  35.9 10.2 %collective-permute-start.7 = (f32[112,832]{1,0:T(8,128)S(1)}, f32[112,832]{1,0:T(8,128)S(1)}, u32[]{:S(2)}, u32[]{:S(2)}) collective-permute-start(f32[112,832]{1,0:T(8,128)S(1)} %constant_dynamic-slice_fusion.1), channel_id=1, source_target_pairs={{0,1},{1,0},{2,3},{3,2},{4,5},{5,4},{6,7},{7,6},{8,9},{9,8},{10,11... | collective-permute-start | bytes 1118216 | tf_op jit(solution)/shard_map/ppermute | solution.py:26
  41.8 5.6 %copy-start.7 = (bf16[104,2496]{1,0:T(8,128)(2,1)}, bf16[104,2496]{1,0:T(8,128)(2,1)S(1)}, u32[]{:S(2)}) copy-start(bf16[104,2496]{1,0:T(8,128)(2,1)S(1)} %pad_maximum_fusion.4) | copy-start | bytes 1557508
  41.8 10.5 %collective-permute-start.12 = (bf16[104,2496]{1,0:T(8,128)(2,1)}, bf16[104,2496]{1,0:T(8,128)(2,1)}, u32[]{:S(2)}, u32[]{:S(2)}) collective-permute-start(bf16[104,2496]{1,0:T(8,128)(2,1)} %collective-permute-done.4), channel_id=1, source_target_pairs={{0,4},{2,6},{4,0},{6,2},{8,12},{10,14},{12,8},{14,10},{16,20},{18,... | collective-permute-start | bytes 1557512 | tf_op jit(solution)/shard_map/ppermute | solution.py:191
  43.4 10.2 %collective-permute-start.11 = (bf16[104,2496]{1,0:T(8,128)(2,1)}, bf16[104,2496]{1,0:T(8,128)(2,1)}, u32[]{:S(2)}, u32[]{:S(2)}) collective-permute-start(bf16[104,2496]{1,0:T(8,128)(2,1)} %collective-permute-done.4), channel_id=1, source_target_pairs={{0,2},{2,0},{4,6},{6,4},{8,10},{10,8},{12,14},{14,12},{16,18},{18,... | collective-permute-start | bytes 1557512 | tf_op jit(solution)/shard_map/ppermute | solution.py:191
  44.9 10.7 %collective-permute-start.10 = (bf16[104,2496]{1,0:T(8,128)(2,1)}, bf16[104,2496]{1,0:T(8,128)(2,1)}, u32[]{:S(2)}, u32[]{:S(2)}) collective-permute-start(bf16[104,2496]{1,0:T(8,128)(2,1)} %collective-permute-done.4), channel_id=1, source_target_pairs={{0,8},{2,10},{4,12},{6,14},{8,24},{10,26},{12,28},{14,30},{16,0},{... | collective-permute-start | bytes 1557512 | tf_op jit(solution)/shard_map/ppermute | solution.py:188
  46.3 15.2 %copy-start.9 = (s32[2]{0:T(128)S(1)}, s32[2]{0:T(128)}, u32[]{:S(2)}) copy-start(s32[2]{0:T(128)} %param.18) | copy-start | bytes 28
  50.2 30.8 %copy-start.5 = (bf16[512,832]{0,1:T(8,128)(2,1)S(1)}, bf16[512,832]{0,1:T(8,128)(2,1)}, u32[]{:S(2)}) copy-start(bf16[512,832]{0,1:T(8,128)(2,1)} %param.14) | copy-start | bytes 2555908
  55.6 23.1 %all-to-all-start = ((bf16[16,16,896]{2,1,0:T(8,128)(2,1)}), bf16[16,16,896]{2,1,0:T(8,128)(2,1)S(1)}, u32[]{:S(2)}, u32[]{:S(2)}) async-start(bf16[16,16,896]{2,1,0:T(8,128)(2,1)} %bitcast.5), calls=%async_computation | async-start | bytes 917504 | tf_op jit(solution)/shard_map/all_to_all | solution.py:252
  59.5 19.2 %collective-permute-start.14 = (bf16[104,2496]{1,0:T(8,128)(2,1)}, bf16[104,2496]{1,0:T(8,128)(2,1)}, u32[]{:S(2)}, u32[]{:S(2)}) collective-permute-start(bf16[104,2496]{1,0:T(8,128)(2,1)} %copy-done.7), channel_id=1, source_target_pairs={{0,8},{2,10},{4,12},{6,14},{8,24},{10,26},{12,28},{14,30},{16,0},{... | collective-permute-start | bytes 1557512 | tf_op jit(solution)/shard_map/ppermute | solution.py:188
  61.6 21.3 %collective-permute-start.17 = (bf16[104,2496]{1,0:T(8,128)(2,1)}, bf16[104,2496]{1,0:T(8,128)(2,1)}, u32[]{:S(2)}, u32[]{:S(2)}) collective-permute-start(bf16[104,2496]{1,0:T(8,128)(2,1)} %collective-permute-done.10), channel_id=1, source_target_pairs={{0,4},{2,6},{4,0},{6,2},{8,12},{10,14},{12,8},{14,10},{16,20},{18,... | collective-permute-start | bytes 1557512 | tf_op jit(solution)/shard_map/ppermute | solution.py:191
  63.0 19.8 %collective-permute-start.16 = (bf16[104,2496]{1,0:T(8,128)(2,1)}, bf16[104,2496]{1,0:T(8,128)(2,1)}, u32[]{:S(2)}, u32[]{:S(2)}) collective-permute-start(bf16[104,2496]{1,0:T(8,128)(2,1)} %collective-permute-done.10), channel_id=1, source_target_pairs={{0,2},{2,0},{4,6},{6,4},{8,10},{10,8},{12,14},{14,12},{16,18},{18,... | collective-permute-start | bytes 1557512 | tf_op jit(solution)/shard_map/ppermute | solution.py:191
  78.7 2.2 %collective-permute-start.15 = (bf16[256,896]{1,0:T(8,128)(2,1)S(1)}, bf16[256,896]{1,0:T(8,128)(2,1)S(1)}, u32[]{:S(2)}, u32[]{:S(2)}) collective-permute-start(bf16[256,896]{1,0:T(8,128)(2,1)S(1)} %bitcast.27), channel_id=1, source_target_pairs={{0,1},{1,0},{2,3},{3,2},{4,5},{5,4},{6,7},{7,6},{8,9},{9,8},{10,11... | collective-permute-start | bytes 1376264 | tf_op jit(solution)/shard_map/ppermute | solution.py:26
  79.0 15.9 %collective-permute-start.18 = (bf16[104,2496]{1,0:T(8,128)(2,1)}, bf16[104,2496]{1,0:T(8,128)(2,1)S(1)}, u32[]{:S(2)}, u32[]{:S(2)}) collective-permute-start(bf16[104,2496]{1,0:T(8,128)(2,1)} %collective-permute-done.14), channel_id=1, source_target_pairs={{0,8},{2,10},{4,12},{6,14},{8,24},{10,26},{12,28},{14,30},{16,0},{... | collective-permute-start | bytes 1557512 | tf_op jit(solution)/shard_map/ppermute | solution.py:188
  82.8 3.9 %copy-start.1 = (bf16[16,104,512]{2,1,0:T(8,128)(2,1)}, bf16[16,104,512]{2,1,0:T(8,128)(2,1)S(1)}, u32[]{:S(2)}) copy-start(bf16[16,104,512]{2,1,0:T(8,128)(2,1)S(1)} %shard_map.120) | copy-start | bytes 5111812
  85.0 4.8 %copy-start.6 = (bf16[416,2496]{1,0:T(8,128)(2,1)S(1)}, bf16[416,2496]{1,0:T(8,128)(2,1)}, u32[]{:S(2)}) copy-start(bf16[416,2496]{1,0:T(8,128)(2,1)} %pad_maximum_fusion) | copy-start | bytes 6230020
  86.8 11.3 %collective-permute-start.19 = (bf16[104,1280]{1,0:T(8,128)(2,1)S(1)}, bf16[104,1280]{1,0:T(8,128)(2,1)S(1)}, u32[]{:S(2)}, u32[]{:S(2)}) collective-permute-start(bf16[104,1280]{1,0:T(8,128)(2,1)S(1)} %slice.33), channel_id=1, source_target_pairs={{0,2},{2,0},{4,6},{6,4},{8,10},{10,8},{12,14},{14,12},{16,18},{18,... | collective-permute-start | bytes 798728 | tf_op jit(solution)/shard_map/ppermute | solution.py:194
  88.3 9.8 %collective-permute-start.20 = (bf16[104,1216]{1,0:T(8,128)(2,1)S(1)}, bf16[104,1216]{1,0:T(8,128)(2,1)S(1)}, u32[]{:S(2)}, u32[]{:S(2)}) collective-permute-start(bf16[104,1216]{1,0:T(8,128)(2,1)S(1)} %slice.34), channel_id=1, source_target_pairs={{0,4},{2,6},{4,0},{6,2},{8,12},{10,14},{12,8},{14,10},{16,20},{18,... | collective-permute-start | bytes 758792 | tf_op jit(solution)/shard_map/ppermute | solution.py:195
  91.3 1.7 %slice-start = ((bf16[16,104,512]{2,1,0:T(8,128)(2,1)}), bf16[3,104,512]{2,1,0:T(8,128)(2,1)S(1)}, s32[]{:S(2)}) async-start(bf16[16,104,512]{2,1,0:T(8,128)(2,1)} %copy-done.1), calls=%async_computation.1 | async-start | bytes 638976 | tf_op jit(solution)/shard_map/slice | solution.py:263
  93.0 1.6 %copy-start.2 = (bf16[16,104,512]{2,1,0:T(8,128)(2,1)S(1)}, bf16[16,104,512]{2,1,0:T(8,128)(2,1)}, u32[]{:S(2)}) copy-start(bf16[16,104,512]{2,1,0:T(8,128)(2,1)} %copy-done.1) | copy-start | bytes 5111812

commit v9 on v7

--- a/solution.py
+++ b/solution.py
@@ -41,12 +41,14 @@
     order = folded_ring(lines)
     following = {order[i]: order[(i + 1) % lines] for i in range(lines)}
     line_perm = [(z * 4 + p, following[z] * 4 + p) for z in range(lines) for p in range(4)]
+    arrivals = [(0, flip) for flip in range(4)]
+    arrivals += [(step, flip) for step in range(1, lines) for flip in range(3)]
+    arrivals += [(step, 3) for step in range(1, lines)]
     table = np.zeros((n_req, n_req), np.int32)
     for index in range(n_req):
-        for step in range(lines):
+        for place, (step, flip) in enumerate(arrivals):
             z = order[(order.index(index // 4) - step) % lines]
-            for flip in range(4):
-                table[index, step * 4 + flip] = z * 4 + ((index % 4) ^ flip)
+            table[index, place] = z * 4 + ((index % 4) ^ flip)
     return lines, line_perm, table
 
 
@@ -227,7 +229,9 @@
     corners.append(to_corner(*sides[0]))
     partial_value = merge(patches, stats, gain_bias, merge_weight)
 
-    partial_value, held[2], sides[1] = tie(partial_value, held[2], sides[1])
+    partial_value, held[2], sides[1], corners[0] = tie(
+        partial_value, held[2], sides[1], corners[0]
+    )
     held.append(along_line(held[2]))
     sides.append(to_sides(held[2]))
     merged = tp_scatter_sum(partial_value, n_tp, 1).astype(jnp.bfloat16)
@@ -236,44 +240,39 @@
         [merged, code_cols, jnp.zeros((token_count, padding), jnp.bfloat16)], axis=1
     )
     outgoing = jnp.dot(place, payload, preferred_element_type=jnp.float32).astype(jnp.bfloat16)
-
-    def group(step, corner=True):
-        pieces = [held[step], *sides[step]] + ([corners[step]] if corner else [])
-        return jnp.concatenate(pieces, axis=0)
-
-    first_group = group(0)
-
-    outgoing, held[3], sides[2], corners[0], texts, first_group = tie(
-        outgoing, held[3], sides[2], corners[0], texts, first_group
-    )
-    sides.append(to_sides(held[3]))
-    corners.append(along_line(corners[0]))
-    corners.append(to_corner(*sides[2]))
     arrived = lax.all_to_all(
         outgoing.reshape(n_req, IMG_CAP, -1), "req", split_axis=0, concat_axis=0
     ).reshape(slot_count, -1)
+
+    held[3], sides[2], behind = tie(held[3], sides[2], corners[0])
+    sides.append(to_sides(held[3]))
+    corners.append(along_line(behind))
     images = [arrived] + [tp_shift(arrived, n_tp, d) for d in range(1, n_tp)]
     blocks = combine(tp_index, order, texts, images, gain_column)
-
-    def product(first, count, weight):
-        source = blocks[first : first + count].reshape(count * rows, row_count)
+    for step in range(4, lines):
+        held.append(along_line(held[step - 1]))
+        sides.append(to_sides(held[step]))
+    early = [held[0], *sides[0], corners[0]]
+    for step in range(1, lines - 1):
+        early += [held[step], *sides[step]]
+    early = jnp.concatenate(early, axis=0)
+    blocks, sides[-1], early = tie(blocks, sides[-1], early)
+
+    def product(first, weight):
+        count = weight.shape[0]
+        source = blocks[first : first + count // rows].reshape(count, row_count)
         weight, source = tie(weight, source)
         return lax.dot_general(
             source, weight, (((0,), (0,)), ((), ())), preferred_element_type=jnp.float32
         )
 
-    total = product(0, 4, first_group) + product(4, 4, group(1))
-
-    total, sides[3] = tie(total, sides[3])
-    for step in range(4, lines):
-        held.append(along_line(held[step - 1]))
-        sides.append(to_sides(held[step]))
-        corners.append(to_corner(*sides[step - 1]))
+    for step in range(2, lines - 1):
+        corners.append(along_line(corners[step - 1]))
     corners.append(to_corner(*sides[-1]))
-    for step in range(2, lines - 1):
-        total += product(step * 4, 4, group(step))
-    total += product(lines * 4 - 4, 3, group(lines - 1, False))
-    total, corners[-1] = tie(total, corners[-1])
+    (total,) = tie(product(0, early))
+    late = jnp.concatenate([held[-1], *sides[-1]], axis=0)
+    (total,) = tie(total + product(lines * 3 - 2, late))
+    last = jnp.concatenate(corners[1:], axis=0)
 
     position = me * row_count + jnp.arange(row_count, dtype=jnp.int32)
     request_ids = jnp.arange(text_len.shape[0], dtype=jnp.int32)
@@ -284,7 +283,7 @@
         axis=1,
     )
     keep = lax.rem(position, SEQ) < limits
-    total += product(lines * 4 - 1, 1, corners[-1])
+    total += product(lines * 3 + 1, last)
     return jnp.where(keep[:, None], total, 0.0).astype(jnp.bfloat16)
 
 

time: 109 us -> 98.6 us (0.905)
  other arithmetic: 19.2 us -> 5.53 us
  local copies, waits for them, and re-layouts: 16.3 us -> 29.4 us
  waiting for transfers between devices: 22.3 us -> 17.2 us
  starting transfers between devices: 31.7 us -> 27.7 us
  matrix products: 12.9 us -> 11.2 us
    unnamed x25 -> x21, local copies, waits for them, and re-layouts: 6.48 us -> 19.1 us
    concatenate x4 -> x2, other arithmetic: 9.05 us -> 2.65 us  [the longest x1 1.48 us: shards(): late = jnp.concatenate([held[-1], *sides[-1]], axis=0)]
    add x1 -> x0, other arithmetic: 6.03 us -> none  [shards(): total += product(lines * 4 - 4, 3, group(lines - 1, False))]
    ppermute x3 -> x2, waiting for transfers between devices: 8.22 us -> 3.1 us  [to_corner(): right = lax.ppermute(by_x[:, cut:], 'req', y_perm)]
    ppermute x4, waiting for transfers between devices: 5.21 us -> 0.35 us  [to_sides(): lax.ppermute(block, 'req', x_perm)]
    ppermute x4 -> x5, waiting for transfers between devices: 4.22 us -> 8.56 us  [along_line(): return lax.ppermute(block, 'req', line_perm)]
    all_to_all x1, waiting for transfers between devices: 0.01 us -> 3.5 us  [shards(): lax.all_to_all(outgoing.reshape(n_req, IMG_CAP, -1), 'req', split_axis=0,...]
    convert_element_type x1 -> x0, other arithmetic: 2.89 us -> none  [shards(): return jnp.where(keep[:, None], total, 0.0).astype(jnp.bfloat16)]
  transfers between devices with their start and end apart: 23 -> 22, of which waited for: 10 -> 7; matrix products, arithmetic and copies ran while one was open for 33% -> 38% of each run, Pallas kernels for 5% -> 7%
where the time goes in v9:
time: 98.6 us; the launch traced here: 97.7 us
  local copies, waits for them, and re-layouts  29.4 us (30%)
  starting transfers between devices  27.7 us (28%)
  waiting for transfers between devices  17.2 us (17%)
  matrix products  11.2 us (11%)
  Pallas kernels  6.36 us (6%)
  other arithmetic  5.53 us (6%)
    unnamed x21, local copies, waits for them, and re-layouts  19.1 us
    dot_general x3, matrix products, product(): lax.dot_general(source, weight, (((0,), (0,)), ((), ())), preferred_eleme...  10.2 us
    ppermute x5, waiting for transfers between devices, along_line(): return lax.ppermute(block, 'req', line_perm)  8.56 us
    ppermute x5, starting transfers between devices, along_line(): return lax.ppermute(block, 'req', line_perm)  8.17 us
    ppermute x4, starting transfers between devices, to_sides(): lax.ppermute(block, 'req', y_perm)  6.1 us
    ppermute x4, starting transfers between devices, to_sides(): lax.ppermute(block, 'req', x_perm)  4.58 us
    all_to_all x1, starting transfers between devices, shards(): lax.all_to_all(outgoing.reshape(n_req, IMG_CAP, -1), 'req', split_axis=0,...  3.63 us
    pallas_call x1, Pallas kernels, merge(): pl.pallas_call(body, out_shape=jax.ShapeDtypeStruct((tokens, features), j...  3.62 us
  transfers between devices with their start and end apart: 22, of which 7 were waited for; matrix products, arithmetic and copies ran while one was open for 38% of the time, Pallas kernels for 7%

profile of v9, /device:TPU:0, one launch (start us, length us, event | category | flops | bytes accessed | tf_op | source)
XLA Modules:
  0.0 97.7 jit_solution(16791122067567612597)
XLA Ops:
  0.0 3.0 %collective-permute-start.1 = (bf16[104,2496]{1,0:T(8,128)(2,1)}, bf16[104,2496]{1,0:T(8,128)(2,1)}, u32[]{:S(2)}, u32[]{:S(2)}) collective-permute-start(bf16[104,2496]{1,0:T(8,128)(2,1)} %param.16), channel_id=1, source_target_pairs={{0,8},{2,10},{4,12},{6,14},{8,24},{10,26},{12,28},{14,30},{16,0},{... | collective-permute-start | bytes 1557512 | tf_op jit(solution)/shard_map/ppermute | solution.py:190
  3.0 1.5 %collective-permute-start.2 = (bf16[104,2496]{1,0:T(8,128)(2,1)}, bf16[104,2496]{1,0:T(8,128)(2,1)S(1)}, u32[]{:S(2)}, u32[]{:S(2)}) collective-permute-start(bf16[104,2496]{1,0:T(8,128)(2,1)} %param.16), channel_id=1, source_target_pairs={{0,2},{2,0},{4,6},{6,4},{8,10},{10,8},{12,14},{14,12},{16,18},{18,... | collective-permute-start | bytes 1557512 | tf_op jit(solution)/shard_map/ppermute | solution.py:193
  4.5 1.5 %collective-permute-start.3 = (bf16[104,2496]{1,0:T(8,128)(2,1)}, bf16[104,2496]{1,0:T(8,128)(2,1)S(1)}, u32[]{:S(2)}, u32[]{:S(2)}) collective-permute-start(bf16[104,2496]{1,0:T(8,128)(2,1)} %param.16), channel_id=1, source_target_pairs={{0,4},{2,6},{4,0},{6,2},{8,12},{10,14},{12,8},{14,10},{16,20},{18,... | collective-permute-start | bytes 1557512 | tf_op jit(solution)/shard_map/ppermute | solution.py:193
  6.0 1.1 %copy-done.1 = bf16[448,832]{1,0:T(8,128)(2,1)S(1)} copy-done((bf16[448,832]{1,0:T(8,128)(2,1)S(1)}, bf16[448,832]{1,0:T(8,128)(2,1)}, u32[]{:S(2)}) %copy-start.1) | copy-done | bytes 745496
  7.2 0.3 shard_map.118.refs_0_
  7.5 0.1 collective-permute-start
  7.6 0.7 stack.19
  8.2 0.7 stack.20
  8.9 0.7 convert_bitcast_fusion.1
  9.6 0.2 convert_reduce_fusion
  9.8 0.7 fusion.9
  10.6 0.8 reshape.47
  11.4 0.7 copy.17
  12.1 0.7 copy.16
  12.8 0.1 pad.10.clone
  12.9 0.7 fusion.12.order_ref
  13.6 1.9 %constant_dynamic-update-slice_fusion.9 = bf16[1040,2496]{1,0:T(8,128)(2,1)} fusion(bf16[104,2496]{1,0:T(8,128)(2,1)} %param.16), kind=kLoop, calls=%fused_computation.28 | loop fusion | bytes 1051648
  15.5 1.0 collective-permute-done.1
  16.4 0.3 collective-permute-done.2
  16.8 1.2 %collective-permute-done.3 = bf16[104,2496]{1,0:T(8,128)(2,1)S(1)} collective-permute-done((bf16[104,2496]{1,0:T(8,128)(2,1)}, bf16[104,2496]{1,0:T(8,128)(2,1)S(1)}, u32[]{:S(2)}, u32[]{:S(2)}) %collective-permute-start.3) | collective-permute-done | bytes 519200 | tf_op jit(solution)/shard_map/ppermute | solution.py:193
  18.0 2.6 %collective-permute-start.5 = (bf16[104,2496]{1,0:T(8,128)(2,1)}, bf16[104,2496]{1,0:T(8,128)(2,1)}, u32[]{:S(2)}, u32[]{:S(2)}) collective-permute-start(bf16[104,2496]{1,0:T(8,128)(2,1)} %collective-permute-done.1), channel_id=1, source_target_pairs={{0,8},{2,10},{4,12},{6,14},{8,24},{10,26},{12,28},{14,30},{16,0},{... | collective-permute-start | bytes 1557512 | tf_op jit(solution)/shard_map/ppermute | solution.py:190
  20.6 0.5 collective-permute-start.6
  21.1 1.5 %collective-permute-start.7 = (bf16[104,2496]{1,0:T(8,128)(2,1)}, bf16[104,2496]{1,0:T(8,128)(2,1)}, u32[]{:S(2)}, u32[]{:S(2)}) collective-permute-start(bf16[104,2496]{1,0:T(8,128)(2,1)} %collective-permute-done.1), channel_id=1, source_target_pairs={{0,4},{2,6},{4,0},{6,2},{8,12},{10,14},{12,8},{14,10},{16,20},{18,... | collective-permute-start | bytes 1557512 | tf_op jit(solution)/shard_map/ppermute | solution.py:193
  22.7 0.7 slice.21
  23.4 1.5 %collective-permute-start.8 = (bf16[104,1280]{1,0:T(8,128)(2,1)}, bf16[104,1280]{1,0:T(8,128)(2,1)}, u32[]{:S(2)}, u32[]{:S(2)}) collective-permute-start(bf16[104,1280]{1,0:T(8,128)(2,1)} %slice.21), channel_id=1, source_target_pairs={{0,2},{2,0},{4,6},{6,4},{8,10},{10,8},{12,14},{14,12},{16,18},{18,... | collective-permute-start | bytes 798728 | tf_op jit(solution)/shard_map/ppermute | solution.py:196
  24.9 0.7 slice.22
  25.6 0.5 collective-permute-start.9
  26.1 0.8 constant_dynamic-update-slice_fusion.8
  27.0 0.9 constant_dynamic-update-slice_fusion.7
  27.8 4.1 %copy-done = bf16[4,832,1664]{2,1,0:T(8,128)(2,1)S(1)} copy-done((bf16[4,832,1664]{2,1,0:T(8,128)(2,1)S(1)}, bf16[4,832,1664]{2,1,0:T(8,128)(2,1)}, u32[]{:S(2)}) %copy-start) | copy-done | bytes 11075608
  32.0 3.6 %shard_map.119 = f32[112,1664]{1,0:T(8,128)S(1)} custom-call(bf16[448,832]{1,0:T(8,128)(2,1)S(1)} %copy-done.2, bf16[2,832]{1,0:T(2,128)(2,1)S(1)} %pad_maximum_fusion.2.gain_bias_ref, f32[448,256]{1,0:T(8,128)S(1)} %shard_map.118.refs_0_, f32[448,256]{1,0:T(8,128)S(1)} %collective-permute-done.refs_1_, bf16[4,832,1664]{2,1,0:T(8,128)(2,1)S(1)} %copy-done), custom_call_target="tpu_custom_call" | custom-call | flops 1000 | bytes 1000 | tf_op jit(solution)/shard_map/pallas_call | solution.py:112
  35.6 0.3 copy.18.gain_ref
  35.9 3.1 %collective-permute-done.9 = bf16[104,1216]{1,0:T(8,128)(2,1)} collective-permute-done((bf16[104,1216]{1,0:T(8,128)(2,1)}, bf16[104,1216]{1,0:T(8,128)(2,1)}, u32[]{:S(2)}, u32[]{:S(2)}) %collective-permute-start.9) | collective-permute-done | bytes 252960 | tf_op jit(solution)/shard_map/ppermute | solution.py:197
  39.0 1.1 %pad_maximum_fusion.1 = bf16[104,2496]{1,0:T(8,128)(2,1)S(1)} fusion(bf16[104,1216]{1,0:T(8,128)(2,1)} %collective-permute-done.9, bf16[104,1280]{1,0:T(8,128)(2,1)} %collective-permute-done.8), kind=kLoop, calls=%fused_computation.5 | loop fusion | flops 1038336 | bytes 1038336 | tf_op jit(solution)/shard_map/concatenate | solution.py:198
  40.1 1.7 %collective-permute-start.12 = (bf16[104,2496]{1,0:T(8,128)(2,1)}, bf16[104,2496]{1,0:T(8,128)(2,1)}, u32[]{:S(2)}, u32[]{:S(2)}) collective-permute-start(bf16[104,2496]{1,0:T(8,128)(2,1)} %collective-permute-done.5), channel_id=1, source_target_pairs={{0,8},{2,10},{4,12},{6,14},{8,24},{10,26},{12,28},{14,30},{16,0},{... | collective-permute-start | bytes 1557512 | tf_op jit(solution)/shard_map/ppermute | solution.py:190
  41.8 0.5 collective-permute-start.13
  42.3 1.5 %collective-permute-start.14 = (bf16[104,2496]{1,0:T(8,128)(2,1)}, bf16[104,2496]{1,0:T(8,128)(2,1)}, u32[]{:S(2)}, u32[]{:S(2)}) collective-permute-start(bf16[104,2496]{1,0:T(8,128)(2,1)} %collective-permute-done.5), channel_id=1, source_target_pairs={{0,4},{2,6},{4,0},{6,2},{8,12},{10,14},{12,8},{14,10},{16,20},{18,... | collective-permute-start | bytes 1557512 | tf_op jit(solution)/shard_map/ppermute | solution.py:193
  43.8 0.2 constant_dynamic-slice_fusion.1
  44.1 0.8 constant_dynamic-update-slice_fusion.6
  44.9 1.9 %constant_dynamic-update-slice_fusion.5 = bf16[1040,2496]{1,0:T(8,128)(2,1)} fusion(bf16[1040,2496]{1,0:T(8,128)(2,1)} %constant_dynamic-update-slice_fusion.6, bf16[104,2496]{1,0:T(8,128)(2,1)} %collective-permute-done.1), kind=kLoop, calls=%fused_computation.24 | loop fusion | bytes 1064960
  46.8 0.2 add_convert_fusion
  47.0 1.1 %convolution_convert_fusion = bf16[256,896]{1,0:T(8,128)(2,1)} fusion(bf16[112,1]{1,0:T(8,128)(2,1)S(1)} %copy-done.4, bf16[112,1]{1,0:T(8,128)(2,1)S(1)} %copy-done.5, bf16[112,832]{1,0:T(8,128)(2,1)S(1)} %add_convert_fusion, bf16[896]{0:T(1024)(128)(2,1)S(1)} %pad.10.clone, s32[112]{0:T(128)S(1)} %multiply_add_fusion), kind=kOutput, calls=%fused_computation.4 | convolution fusion | flops 52441088 | bytes 647808 | tf_op jit(solution)/shard_map/dot_general | solution.py:242
  48.1 3.6 %all-to-all-start = ((bf16[16,16,896]{2,1,0:T(8,128)(2,1)}), bf16[16,16,896]{2,1,0:T(8,128)(2,1)S(1)}, u32[]{:S(2)}, u32[]{:S(2)}) async-start(bf16[16,16,896]{2,1,0:T(8,128)(2,1)} %bitcast.5), calls=%async_computation | async-start | bytes 917504 | tf_op jit(solution)/shard_map/all_to_all | solution.py:243
  51.7 1.9 %constant_dynamic-update-slice_fusion.4 = bf16[1040,2496]{1,0:T(8,128)(2,1)} fusion(bf16[1040,2496]{1,0:T(8,128)(2,1)} %constant_dynamic-update-slice_fusion.5, bf16[104,2496]{1,0:T(8,128)(2,1)} %collective-permute-done.6), kind=kLoop, calls=%fused_computation.23 | loop fusion | bytes 1064960
  53.6 1.9 %constant_dynamic-update-slice_fusion.3 = bf16[1040,2496]{1,0:T(8,128)(2,1)} fusion(bf16[1040,2496]{1,0:T(8,128)(2,1)} %constant_dynamic-update-slice_fusion.4, bf16[104,2496]{1,0:T(8,128)(2,1)} %collective-permute-done.7), kind=kLoop, calls=%fused_computation.22 | loop fusion | bytes 1064960
  55.5 1.9 %constant_dynamic-update-slice_fusion.2 = bf16[1040,2496]{1,0:T(8,128)(2,1)} fusion(bf16[1040,2496]{1,0:T(8,128)(2,1)} %constant_dynamic-update-slice_fusion.3, bf16[104,2496]{1,0:T(8,128)(2,1)} %collective-permute-done.5), kind=kLoop, calls=%fused_computation.21 | loop fusion | bytes 1064960
  57.3 0.5 collective-permute-done.14
  57.8 2.0 %collective-permute-start.15 = (bf16[104,2496]{1,0:T(8,128)(2,1)}, bf16[104,2496]{1,0:T(8,128)(2,1)}, u32[]{:S(2)}, u32[]{:S(2)}) collective-permute-start(bf16[104,2496]{1,0:T(8,128)(2,1)} %collective-permute-done.12), channel_id=1, source_target_pairs={{0,2},{2,0},{4,6},{6,4},{8,10},{10,8},{12,14},{14,12},{16,18},{18,... | collective-permute-start | bytes 1557512 | tf_op jit(solution)/shard_map/ppermute | solution.py:193
  59.8 1.5 %collective-permute-start.16 = (bf16[104,2496]{1,0:T(8,128)(2,1)}, bf16[104,2496]{1,0:T(8,128)(2,1)}, u32[]{:S(2)}, u32[]{:S(2)}) collective-permute-start(bf16[104,2496]{1,0:T(8,128)(2,1)} %collective-permute-done.12), channel_id=1, source_target_pairs={{0,4},{2,6},{4,0},{6,2},{8,12},{10,14},{12,8},{14,10},{16,20},{18,... | collective-permute-start | bytes 1557512 | tf_op jit(solution)/shard_map/ppermute | solution.py:193
  61.4 0.9 collective-permute-start.17
  62.3 3.5 %all-to-all-done = bf16[16,16,896]{2,1,0:T(8,128)(2,1)S(1)} async-done(((bf16[16,16,896]{2,1,0:T(8,128)(2,1)}), bf16[16,16,896]{2,1,0:T(8,128)(2,1)S(1)}, u32[]{:S(2)}, u32[]{:S(2)}) %all-to-all-start) | async-done | bytes 458784 | tf_op jit(solution)/shard_map/all_to_all | solution.py:243
  65.8 1.9 %constant_dynamic-update-slice_fusion.1 = bf16[1040,2496]{1,0:T(8,128)(2,1)} fusion(bf16[1040,2496]{1,0:T(8,128)(2,1)} %constant_dynamic-update-slice_fusion.2, bf16[104,2496]{1,0:T(8,128)(2,1)} %collective-permute-done.13), kind=kLoop, calls=%fused_computation.20 | loop fusion | bytes 1064960
  67.7 1.9 %constant_dynamic-update-slice_fusion = bf16[1040,2496]{1,0:T(8,128)(2,1)} fusion(bf16[1040,2496]{1,0:T(8,128)(2,1)} %constant_dynamic-update-slice_fusion.1, bf16[104,2496]{1,0:T(8,128)(2,1)} %collective-permute-done.14), kind=kLoop, calls=%fused_computation.19 | loop fusion | bytes 1064960 | tf_op jit(solution)/shard_map/concatenate | solution.py:258
  69.6 7.6 %collective-permute-done.17 = bf16[104,2496]{1,0:T(8,128)(2,1)} collective-permute-done((bf16[104,2496]{1,0:T(8,128)(2,1)S(1)}, bf16[104,2496]{1,0:T(8,128)(2,1)}, u32[]{:S(2)}, u32[]{:S(2)}) %collective-permute-start.17) | collective-permute-done | bytes 519200 | tf_op jit(solution)/shard_map/ppermute | solution.py:190
  77.2 2.5 %shard_map.120 = bf16[16,104,512]{2,1,0:T(8,128)(2,1)S(1)} custom-call(s32[1]{0:T(128)} %bitcast.index_ref, s32[16]{0:T(128)S(1)} %fusion.12.order_ref, bf16[16,104,1]{2,1,0:T(8,128)(2,1)S(1)} %copy.18.gain_ref, bf16[832,512]{1,0:T(8,128)(2,1)S(1)} %bitcast.22, bf16[832,512]{1,0:T(8,128)(2,1)} %collective-permute-done.4.refs_1_, ...), custom_call_target="tpu_custom_call" | custom-call | flops 1000 | bytes 1000 | tf_op jit(solution)/shard_map/pallas_call | solution.py:164
  79.7 1.0 slice.25
  80.7 1.0 slice.26
  81.6 1.5 %pad_maximum_fusion = bf16[312,2496]{1,0:T(8,128)(2,1)S(1)} fusion(bf16[104,2496]{1,0:T(8,128)(2,1)} %collective-permute-done.16, bf16[104,2496]{1,0:T(8,128)(2,1)} %collective-permute-done.15, bf16[104,2496]{1,0:T(8,128)(2,1)} %collective-permute-done.12), kind=kLoop, calls=%fused_computation.2 | loop fusion | flops 4672512 | bytes 3115008 | tf_op jit(solution)/shard_map/concatenate | solution.py:273
  83.2 1.5 %collective-permute-start.19 = (bf16[104,1280]{1,0:T(8,128)(2,1)S(1)}, bf16[104,1280]{1,0:T(8,128)(2,1)S(1)}, u32[]{:S(2)}, u32[]{:S(2)}) collective-permute-start(bf16[104,1280]{1,0:T(8,128)(2,1)S(1)} %slice.25), channel_id=1, source_target_pairs={{0,2},{2,0},{4,6},{6,4},{8,10},{10,8},{12,14},{14,12},{16,18},{18,... | collective-permute-start | bytes 798728 | tf_op jit(solution)/shard_map/ppermute | solution.py:196
  84.8 1.5 %collective-permute-start.20 = (bf16[104,1216]{1,0:T(8,128)(2,1)S(1)}, bf16[104,1216]{1,0:T(8,128)(2,1)S(1)}, u32[]{:S(2)}, u32[]{:S(2)}) collective-permute-start(bf16[104,1216]{1,0:T(8,128)(2,1)S(1)} %slice.26), channel_id=1, source_target_pairs={{0,4},{2,6},{4,0},{6,2},{8,12},{10,14},{12,8},{14,10},{16,20},{18,... | collective-permute-start | bytes 758792 | tf_op jit(solution)/shard_map/ppermute | solution.py:197
  86.3 5.6 %fusion.17 = f32[512,2496]{0,1:T(8,128)S(1)} fusion(bf16[1040,512]{1,0:T(8,128)(2,1)S(1)} %bitcast.25, bf16[1040,2496]{1,0:T(8,128)(2,1)} %constant_dynamic-update-slice_fusion), kind=kOutput, calls=%fused_computation.53 | convolution fusion | flops 2658140160 | bytes 11368448 | tf_op jit(solution)/shard_map/dot_general | solution.py:265
  91.9 1.5 %convolution_add_fusion = f32[512,2496]{0,1:T(8,128)S(1)} fusion(f32[512,2496]{0,1:T(8,128)S(1)} %fusion.17, bf16[312,512]{1,0:T(8,128)(2,1)S(1)} %bitcast.24, bf16[312,2496]{1,0:T(8,128)(2,1)S(1)} %pad_maximum_fusion), kind=kOutput, calls=%fused_computation.1 | convolution fusion | flops 798720000 | bytes 12100608 | tf_op jit(solution)/shard_map/dot_general | solution.py:265
  93.5 1.2 %maximum_maximum_fusion = bf16[312,2496]{1,0:T(8,128)(2,1)S(1)} fusion(bf16[104,1216]{1,0:T(8,128)(2,1)S(1)} %collective-permute-done.20, bf16[104,1280]{1,0:T(8,128)(2,1)S(1)} %collective-permute-done.19, bf16[104,2496]{1,0:T(8,128)(2,1)S(1)} %collective-permute-done.18, bf16[104,2496]{1,0:T(8,128)(2,1)} %collective-permute-done.17), kind=kLoop, calls=%fused_computation.3 | loop fusion | flops 6230016 | bytes 3115008 | tf_op jit(solution)/shard_map/concatenate | solution.py:275
  94.7 3.0 %select_convert_fusion = bf16[512,2496]{0,1:T(8,128)(2,1)} fusion(f32[512,2496]{0,1:T(8,128)S(1)} %convolution_add_fusion, bf16[312,512]{1,0:T(8,128)(2,1)S(1)} %bitcast.23, bf16[312,2496]{1,0:T(8,128)(2,1)S(1)} %maximum_maximum_fusion, pred[512]{0:T(512)(128)(4,1)S(1)} %fusion.10), kind=kOutput, calls=%fused_computation | convolution fusion | flops 801275904 | bytes 9545216 | tf_op jit(solution)/shard_map/dot_general | solution.py:265
  (37 shorter events, 0.3 us)
Async XLA Ops:
  0.0 16.4 %collective-permute-start.1 = (bf16[104,2496]{1,0:T(8,128)(2,1)}, bf16[104,2496]{1,0:T(8,128)(2,1)}, u32[]{:S(2)}, u32[]{:S(2)}) collective-permute-start(bf16[104,2496]{1,0:T(8,128)(2,1)} %param.16), channel_id=1, source_target_pairs={{0,8},{2,10},{4,12},{6,14},{8,24},{10,26},{12,28},{14,30},{16,0},{... | collective-permute-start | bytes 1557512 | tf_op jit(solution)/shard_map/ppermute | solution.py:190
  3.0 13.8 %collective-permute-start.2 = (bf16[104,2496]{1,0:T(8,128)(2,1)}, bf16[104,2496]{1,0:T(8,128)(2,1)S(1)}, u32[]{:S(2)}, u32[]{:S(2)}) collective-permute-start(bf16[104,2496]{1,0:T(8,128)(2,1)} %param.16), channel_id=1, source_target_pairs={{0,2},{2,0},{4,6},{6,4},{8,10},{10,8},{12,14},{14,12},{16,18},{18,... | collective-permute-start | bytes 1557512 | tf_op jit(solution)/shard_map/ppermute | solution.py:193
  4.5 13.5 %collective-permute-start.3 = (bf16[104,2496]{1,0:T(8,128)(2,1)}, bf16[104,2496]{1,0:T(8,128)(2,1)S(1)}, u32[]{:S(2)}, u32[]{:S(2)}) collective-permute-start(bf16[104,2496]{1,0:T(8,128)(2,1)} %param.16), channel_id=1, source_target_pairs={{0,4},{2,6},{4,0},{6,2},{8,12},{10,14},{12,8},{14,10},{16,20},{18,... | collective-permute-start | bytes 1557512 | tf_op jit(solution)/shard_map/ppermute | solution.py:193
  6.0 1.1 %copy-start.1 = (bf16[448,832]{1,0:T(8,128)(2,1)S(1)}, bf16[448,832]{1,0:T(8,128)(2,1)}, u32[]{:S(2)}) copy-start(bf16[448,832]{1,0:T(8,128)(2,1)} %patches_ref.3) | copy-start | bytes 2236420
  7.2 20.6 %copy-start.2 = (bf16[448,832]{1,0:T(8,128)(2,1)S(1)}, bf16[448,832]{1,0:T(8,128)(2,1)}, u32[]{:S(2)}) copy-start(bf16[448,832]{1,0:T(8,128)(2,1)} %patches_ref.3) | copy-start | bytes 2236420
  7.5 8.0 %collective-permute-start = (f32[448,256]{1,0:T(8,128)S(1)}, f32[448,256]{1,0:T(8,128)S(1)}, u32[]{:S(2)}, u32[]{:S(2)}) collective-permute-start(f32[448,256]{1,0:T(8,128)S(1)} %shard_map.118.refs_0_), channel_id=1, source_target_pairs={{0,1},{1,0},{2,3},{3,2},{4,5},{5,4},{6,7},{7,6},{8,9},{9,8},{10,11... | collective-permute-start | bytes 1376264 | tf_op jit(solution)/shard_map/ppermute | solution.py:26
  18.0 22.1 %collective-permute-start.5 = (bf16[104,2496]{1,0:T(8,128)(2,1)}, bf16[104,2496]{1,0:T(8,128)(2,1)}, u32[]{:S(2)}, u32[]{:S(2)}) collective-permute-start(bf16[104,2496]{1,0:T(8,128)(2,1)} %collective-permute-done.1), channel_id=1, source_target_pairs={{0,8},{2,10},{4,12},{6,14},{8,24},{10,26},{12,28},{14,30},{16,0},{... | collective-permute-start | bytes 1557512 | tf_op jit(solution)/shard_map/ppermute | solution.py:190
  20.6 19.5 %collective-permute-start.6 = (bf16[104,2496]{1,0:T(8,128)(2,1)}, bf16[104,2496]{1,0:T(8,128)(2,1)}, u32[]{:S(2)}, u32[]{:S(2)}) collective-permute-start(bf16[104,2496]{1,0:T(8,128)(2,1)} %collective-permute-done.1), channel_id=1, source_target_pairs={{0,2},{2,0},{4,6},{6,4},{8,10},{10,8},{12,14},{14,12},{16,18},{18,... | collective-permute-start | bytes 1557512 | tf_op jit(solution)/shard_map/ppermute | solution.py:193
  21.1 19.0 %collective-permute-start.7 = (bf16[104,2496]{1,0:T(8,128)(2,1)}, bf16[104,2496]{1,0:T(8,128)(2,1)}, u32[]{:S(2)}, u32[]{:S(2)}) collective-permute-start(bf16[104,2496]{1,0:T(8,128)(2,1)} %collective-permute-done.1), channel_id=1, source_target_pairs={{0,4},{2,6},{4,0},{6,2},{8,12},{10,14},{12,8},{14,10},{16,20},{18,... | collective-permute-start | bytes 1557512 | tf_op jit(solution)/shard_map/ppermute | solution.py:193
  23.4 15.6 %collective-permute-start.8 = (bf16[104,1280]{1,0:T(8,128)(2,1)}, bf16[104,1280]{1,0:T(8,128)(2,1)}, u32[]{:S(2)}, u32[]{:S(2)}) collective-permute-start(bf16[104,1280]{1,0:T(8,128)(2,1)} %slice.21), channel_id=1, source_target_pairs={{0,2},{2,0},{4,6},{6,4},{8,10},{10,8},{12,14},{14,12},{16,18},{18,... | collective-permute-start | bytes 798728 | tf_op jit(solution)/shard_map/ppermute | solution.py:196
  25.6 13.4 %collective-permute-start.9 = (bf16[104,1216]{1,0:T(8,128)(2,1)}, bf16[104,1216]{1,0:T(8,128)(2,1)}, u32[]{:S(2)}, u32[]{:S(2)}) collective-permute-start(bf16[104,1216]{1,0:T(8,128)(2,1)} %slice.22), channel_id=1, source_target_pairs={{0,4},{2,6},{4,0},{6,2},{8,12},{10,14},{12,8},{14,10},{16,20},{18,... | collective-permute-start | bytes 758792 | tf_op jit(solution)/shard_map/ppermute | solution.py:197
  27.8 4.1 %copy-start = (bf16[4,832,1664]{2,1,0:T(8,128)(2,1)S(1)}, bf16[4,832,1664]{2,1,0:T(8,128)(2,1)}, u32[]{:S(2)}) copy-start(bf16[4,832,1664]{2,1,0:T(8,128)(2,1)} %refs_2_.1) | copy-start | bytes 33226756
  32.0 7.0 %copy-start.3 = (bf16[512,832]{0,1:T(8,128)(2,1)S(1)}, bf16[512,832]{0,1:T(8,128)(2,1)}, u32[]{:S(2)}) copy-start(bf16[512,832]{0,1:T(8,128)(2,1)} %param.14) | copy-start | bytes 2555908
  35.6 11.4 %copy-start.4 = (bf16[112,1]{1,0:T(8,128)(2,1)S(1)}, bf16[112,1]{1,0:T(8,128)(2,1)}, u32[]{:S(2)}) copy-start(bf16[112,1]{1,0:T(8,128)(2,1)} %copy.17) | copy-start | bytes 676
  35.6 11.4 %copy-start.5 = (bf16[112,1]{1,0:T(8,128)(2,1)S(1)}, bf16[112,1]{1,0:T(8,128)(2,1)}, u32[]{:S(2)}) copy-start(bf16[112,1]{1,0:T(8,128)(2,1)} %copy.16) | copy-start | bytes 676
  39.0 38.2 %collective-permute-start.4 = (bf16[832,512]{1,0:T(8,128)(2,1)S(1)}, bf16[832,512]{1,0:T(8,128)(2,1)}, u32[]{:S(2)}, u32[]{:S(2)}) collective-permute-start(bf16[832,512]{1,0:T(8,128)(2,1)S(1)} %bitcast.21), channel_id=1, source_target_pairs={{0,1},{1,0},{2,3},{3,2},{4,5},{5,4},{6,7},{7,6},{8,9},{9,8},{10,11... | collective-permute-start | bytes 2555912 | tf_op jit(solution)/shard_map/ppermute | solution.py:26
  40.1 17.2 %collective-permute-start.12 = (bf16[104,2496]{1,0:T(8,128)(2,1)}, bf16[104,2496]{1,0:T(8,128)(2,1)}, u32[]{:S(2)}, u32[]{:S(2)}) collective-permute-start(bf16[104,2496]{1,0:T(8,128)(2,1)} %collective-permute-done.5), channel_id=1, source_target_pairs={{0,8},{2,10},{4,12},{6,14},{8,24},{10,26},{12,28},{14,30},{16,0},{... | collective-permute-start | bytes 1557512 | tf_op jit(solution)/shard_map/ppermute | solution.py:190
  41.8 15.6 %collective-permute-start.13 = (bf16[104,2496]{1,0:T(8,128)(2,1)}, bf16[104,2496]{1,0:T(8,128)(2,1)}, u32[]{:S(2)}, u32[]{:S(2)}) collective-permute-start(bf16[104,2496]{1,0:T(8,128)(2,1)} %collective-permute-done.5), channel_id=1, source_target_pairs={{0,2},{2,0},{4,6},{6,4},{8,10},{10,8},{12,14},{14,12},{16,18},{18,... | collective-permute-start | bytes 1557512 | tf_op jit(solution)/shard_map/ppermute | solution.py:193
  42.3 15.5 %collective-permute-start.14 = (bf16[104,2496]{1,0:T(8,128)(2,1)}, bf16[104,2496]{1,0:T(8,128)(2,1)}, u32[]{:S(2)}, u32[]{:S(2)}) collective-permute-start(bf16[104,2496]{1,0:T(8,128)(2,1)} %collective-permute-done.5), channel_id=1, source_target_pairs={{0,4},{2,6},{4,0},{6,2},{8,12},{10,14},{12,8},{14,10},{16,20},{18,... | collective-permute-start | bytes 1557512 | tf_op jit(solution)/shard_map/ppermute | solution.py:193
  44.0 2.8 %collective-permute-start.10 = (f32[112,832]{1,0:T(8,128)S(1)}, f32[112,832]{1,0:T(8,128)S(1)}, u32[]{:S(2)}, u32[]{:S(2)}) collective-permute-start(f32[112,832]{1,0:T(8,128)S(1)} %constant_dynamic-slice_fusion.1), channel_id=1, source_target_pairs={{0,1},{1,0},{2,3},{3,2},{4,5},{5,4},{6,7},{7,6},{8,9},{9,8},{10,11... | collective-permute-start | bytes 1118216 | tf_op jit(solution)/shard_map/ppermute | solution.py:26
  48.1 17.7 %all-to-all-start = ((bf16[16,16,896]{2,1,0:T(8,128)(2,1)}), bf16[16,16,896]{2,1,0:T(8,128)(2,1)S(1)}, u32[]{:S(2)}, u32[]{:S(2)}) async-start(bf16[16,16,896]{2,1,0:T(8,128)(2,1)} %bitcast.5), calls=%async_computation | async-start | bytes 917504 | tf_op jit(solution)/shard_map/all_to_all | solution.py:243
  57.8 21.8 %collective-permute-start.15 = (bf16[104,2496]{1,0:T(8,128)(2,1)}, bf16[104,2496]{1,0:T(8,128)(2,1)}, u32[]{:S(2)}, u32[]{:S(2)}) collective-permute-start(bf16[104,2496]{1,0:T(8,128)(2,1)} %collective-permute-done.12), channel_id=1, source_target_pairs={{0,2},{2,0},{4,6},{6,4},{8,10},{10,8},{12,14},{14,12},{16,18},{18,... | collective-permute-start | bytes 1557512 | tf_op jit(solution)/shard_map/ppermute | solution.py:193
  59.8 19.8 %collective-permute-start.16 = (bf16[104,2496]{1,0:T(8,128)(2,1)}, bf16[104,2496]{1,0:T(8,128)(2,1)}, u32[]{:S(2)}, u32[]{:S(2)}) collective-permute-start(bf16[104,2496]{1,0:T(8,128)(2,1)} %collective-permute-done.12), channel_id=1, source_target_pairs={{0,4},{2,6},{4,0},{6,2},{8,12},{10,14},{12,8},{14,10},{16,20},{18,... | collective-permute-start | bytes 1557512 | tf_op jit(solution)/shard_map/ppermute | solution.py:193
  61.4 15.8 %collective-permute-start.17 = (bf16[104,2496]{1,0:T(8,128)(2,1)S(1)}, bf16[104,2496]{1,0:T(8,128)(2,1)}, u32[]{:S(2)}, u32[]{:S(2)}) collective-permute-start(bf16[104,2496]{1,0:T(8,128)(2,1)S(1)} %pad_maximum_fusion.1), channel_id=1, source_target_pairs={{0,8},{2,10},{4,12},{6,14},{8,24},{10,26},{12,28},{14,30},{16,0},{... | collective-permute-start | bytes 1557512 | tf_op jit(solution)/shard_map/ppermute | solution.py:190
  65.8 11.4 %collective-permute-start.11 = (bf16[256,896]{1,0:T(8,128)(2,1)S(1)}, bf16[256,896]{1,0:T(8,128)(2,1)S(1)}, u32[]{:S(2)}, u32[]{:S(2)}) collective-permute-start(bf16[256,896]{1,0:T(8,128)(2,1)S(1)} %bitcast.19), channel_id=1, source_target_pairs={{0,1},{1,0},{2,3},{3,2},{4,5},{5,4},{6,7},{7,6},{8,9},{9,8},{10,11... | collective-permute-start | bytes 1376264 | tf_op jit(solution)/shard_map/ppermute | solution.py:26
  77.2 16.3 %collective-permute-start.18 = (bf16[104,2496]{1,0:T(8,128)(2,1)}, bf16[104,2496]{1,0:T(8,128)(2,1)S(1)}, u32[]{:S(2)}, u32[]{:S(2)}) collective-permute-start(bf16[104,2496]{1,0:T(8,128)(2,1)} %collective-permute-done.17), channel_id=1, source_target_pairs={{0,8},{2,10},{4,12},{6,14},{8,24},{10,26},{12,28},{14,30},{16,0},{... | collective-permute-start | bytes 1557512 | tf_op jit(solution)/shard_map/ppermute | solution.py:190
  83.2 10.2 %collective-permute-start.19 = (bf16[104,1280]{1,0:T(8,128)(2,1)S(1)}, bf16[104,1280]{1,0:T(8,128)(2,1)S(1)}, u32[]{:S(2)}, u32[]{:S(2)}) collective-permute-start(bf16[104,1280]{1,0:T(8,128)(2,1)S(1)} %slice.25), channel_id=1, source_target_pairs={{0,2},{2,0},{4,6},{6,4},{8,10},{10,8},{12,14},{14,12},{16,18},{18,... | collective-permute-start | bytes 798728 | tf_op jit(solution)/shard_map/ppermute | solution.py:196
  84.8 8.7 %collective-permute-start.20 = (bf16[104,1216]{1,0:T(8,128)(2,1)S(1)}, bf16[104,1216]{1,0:T(8,128)(2,1)S(1)}, u32[]{:S(2)}, u32[]{:S(2)}) collective-permute-start(bf16[104,1216]{1,0:T(8,128)(2,1)S(1)} %slice.26), channel_id=1, source_target_pairs={{0,4},{2,6},{4,0},{6,2},{8,12},{10,14},{12,8},{14,10},{16,20},{18,... | collective-permute-start | bytes 758792 | tf_op jit(solution)/shard_map/ppermute | solution.py:197

commit v10 on v9

--- a/solution.py
+++ b/solution.py
@@ -214,51 +214,49 @@
     before = jnp.sum((same & (ids[None, :] < ids[:, None])).astype(jnp.int32), axis=1)
     slot = target * IMG_CAP + before
     slot_count = n_req * IMG_CAP
-    place = (
-        jnp.arange(slot_count, dtype=jnp.int32)[:, None] == slot[None, :]
-    ).astype(jnp.bfloat16)
     code = lax.rem(token_pos, row_count) + 1
     code_cols = jnp.stack([lax.div(code, 256), lax.rem(code, 256)], axis=1).astype(jnp.bfloat16)
     gain_column = norm_gain.reshape(n_req, rows, 1)
 
-    stats, held[1], sides[0], gain_bias, gain_column, order = tie(
-        stats, held[1], sides[0], gain_bias, gain_column, order
+    partial_value = merge(patches, stats, gain_bias, merge_weight)
+
+    partial_value, held[1], sides[0], gain_column, order, slot, code_cols = tie(
+        partial_value, held[1], sides[0], gain_column, order, slot, code_cols
     )
     held.append(along_line(held[1]))
     sides.append(to_sides(held[1]))
     corners.append(to_corner(*sides[0]))
-    partial_value = merge(patches, stats, gain_bias, merge_weight)
-
-    partial_value, held[2], sides[1], corners[0] = tie(
-        partial_value, held[2], sides[1], corners[0]
-    )
-    held.append(along_line(held[2]))
-    sides.append(to_sides(held[2]))
     merged = tp_scatter_sum(partial_value, n_tp, 1).astype(jnp.bfloat16)
     padding = (-width - 2) % 128
     payload = jnp.concatenate(
         [merged, code_cols, jnp.zeros((token_count, padding), jnp.bfloat16)], axis=1
     )
+    place = (
+        jnp.arange(slot_count, dtype=jnp.int32)[:, None] == slot[None, :]
+    ).astype(jnp.bfloat16)
     outgoing = jnp.dot(place, payload, preferred_element_type=jnp.float32).astype(jnp.bfloat16)
     arrived = lax.all_to_all(
         outgoing.reshape(n_req, IMG_CAP, -1), "req", split_axis=0, concat_axis=0
     ).reshape(slot_count, -1)
 
-    held[3], sides[2], behind = tie(held[3], sides[2], corners[0])
-    sides.append(to_sides(held[3]))
-    corners.append(along_line(behind))
+    held[2], sides[1] = tie(held[2], sides[1])
+    held.append(along_line(held[2]))
+    sides.append(to_sides(held[2]))
+    corners.append(along_line(corners[0]))
     images = [arrived] + [tp_shift(arrived, n_tp, d) for d in range(1, n_tp)]
     blocks = combine(tp_index, order, texts, images, gain_column)
+
+    held[3], sides[2] = tie(held[3], sides[2])
+    sides.append(to_sides(held[3]))
     for step in range(4, lines):
         held.append(along_line(held[step - 1]))
         sides.append(to_sides(held[step]))
-    early = [held[0], *sides[0], corners[0]]
-    for step in range(1, lines - 1):
-        early += [held[step], *sides[step]]
-    early = jnp.concatenate(early, axis=0)
-    blocks, sides[-1], early = tie(blocks, sides[-1], early)
-
-    def product(first, weight):
+    blocks, corners[1] = tie(blocks, corners[1])
+    for step in range(2, lines - 1):
+        corners.append(along_line(corners[step - 1]))
+
+    def product(first, weights):
+        weight = jnp.concatenate(weights, axis=0)
         count = weight.shape[0]
         source = blocks[first : first + count // rows].reshape(count, row_count)
         weight, source = tie(weight, source)
@@ -266,13 +264,13 @@
             source, weight, (((0,), (0,)), ((), ())), preferred_element_type=jnp.float32
         )
 
-    for step in range(2, lines - 1):
-        corners.append(along_line(corners[step - 1]))
+    total = product(0, [held[0], *sides[0], corners[0]])
+    for step in range(1, lines - 1):
+        (total,) = tie(total + product(step * 3 + 1, [held[step], *sides[step]]))
+
+    total, sides[-1] = tie(total, sides[-1])
     corners.append(to_corner(*sides[-1]))
-    (total,) = tie(product(0, early))
-    late = jnp.concatenate([held[-1], *sides[-1]], axis=0)
-    (total,) = tie(total + product(lines * 3 - 2, late))
-    last = jnp.concatenate(corners[1:], axis=0)
+    (total,) = tie(total + product(lines * 3 - 2, [held[-1], *sides[-1]]))
 
     position = me * row_count + jnp.arange(row_count, dtype=jnp.int32)
     request_ids = jnp.arange(text_len.shape[0], dtype=jnp.int32)
@@ -283,7 +281,7 @@
         axis=1,
     )
     keep = lax.rem(position, SEQ) < limits
-    total += product(lines * 3 + 1, last)
+    total += product(lines * 3 + 1, corners[1:])
     return jnp.where(keep[:, None], total, 0.0).astype(jnp.bfloat16)
 
 

time: 98.6 us -> 104 us (1.055)
  waiting for transfers between devices: 17.2 us -> 38.1 us
  local copies, waits for them, and re-layouts: 29.4 us -> 15.7 us
  other arithmetic: 5.53 us -> 13.5 us
  starting transfers between devices: 27.7 us -> 20.9 us
  matrix products: 11.2 us -> 8.89 us
    ppermute x2, waiting for transfers between devices: 0.01 us -> 13.3 us  [to_corner(): left = lax.ppermute(by_y[:, :cut], 'req', x_perm)]
    ppermute x5, waiting for transfers between devices: 8.56 us -> 21 us  [along_line(): return lax.ppermute(block, 'req', line_perm)]
    unnamed x21 -> x15, local copies, waits for them, and re-layouts: 19.1 us -> 8.13 us
    concatenate x3 -> x5, other arithmetic: 3.73 us -> 8.16 us  [product(): weight = jnp.concatenate(weights, axis=0)]
    all_to_all x1, waiting for transfers between devices: 3.5 us -> 0.01 us  [shards(): lax.all_to_all(outgoing.reshape(n_req, IMG_CAP, -1), 'req', split_axis=0,...]
    ppermute x4, starting transfers between devices: 6.1 us -> 2.67 us  [to_sides(): lax.ppermute(block, 'req', y_perm)]
    convert_element_type x0 -> x1, other arithmetic: none -> 2.88 us  [shards(): return jnp.where(keep[:, None], total, 0.0).astype(jnp.bfloat16)]
    dot_general x3 -> x5, matrix products: 10.2 us -> 7.83 us  [product(): lax.dot_general(source, weight, (((0,), (0,)), ((), ())), preferred_eleme...]
  transfers between devices with their start and end apart: 22 -> 22, of which waited for: 7 -> 8; matrix products, arithmetic and copies ran while one was open for 38% -> 24% of each run, Pallas kernels for 7% -> 6%
where the time goes in v10:
time: 104 us; the launch traced here: 103 us
  waiting for transfers between devices  38.1 us (37%)
  starting transfers between devices  20.9 us (20%)
  local copies, waits for them, and re-layouts  15.7 us (15%)
  other arithmetic  13.5 us (13%)
  matrix products  8.89 us (9%)
  Pallas kernels  5.77 us (6%)
    ppermute x5, waiting for transfers between devices, along_line(): return lax.ppermute(block, 'req', line_perm)  21 us
    ppermute x2, waiting for transfers between devices, to_corner(): left = lax.ppermute(by_y[:, :cut], 'req', x_perm)  13.3 us
    concatenate x5, other arithmetic, product(): weight = jnp.concatenate(weights, axis=0)  8.16 us
    unnamed x15, local copies, waits for them, and re-layouts  8.13 us
    dot_general x5, matrix products, product(): lax.dot_general(source, weight, (((0,), (0,)), ((), ())), preferred_eleme...  7.83 us
    ppermute x5, starting transfers between devices, along_line(): return lax.ppermute(block, 'req', line_perm)  6.21 us
    pallas_call x1, Pallas kernels, merge(): pl.pallas_call(body, out_shape=jax.ShapeDtypeStruct((tokens, features), j...  3.61 us
    all_to_all x1, starting transfers between devices, shards(): lax.all_to_all(outgoing.reshape(n_req, IMG_CAP, -1), 'req', split_axis=0,...  3.56 us
  transfers between devices with their start and end apart: 22, of which 8 were waited for; matrix products, arithmetic and copies ran while one was open for 24% of the time, Pallas kernels for 6%

profile of v10, /device:TPU:0, one launch (start us, length us, event | category | flops | bytes accessed | tf_op | source)
XLA Modules:
  0.0 103.2 jit_solution(5724229237000302092)
XLA Ops:
  0.0 3.0 %collective-permute-start.1 = (bf16[104,2496]{1,0:T(8,128)(2,1)}, bf16[104,2496]{1,0:T(8,128)(2,1)}, u32[]{:S(2)}, u32[]{:S(2)}) collective-permute-start(bf16[104,2496]{1,0:T(8,128)(2,1)} %param.16), channel_id=1, source_target_pairs={{0,8},{2,10},{4,12},{6,14},{8,24},{10,26},{12,28},{14,30},{16,0},{... | collective-permute-start | bytes 1557512 | tf_op jit(solution)/shard_map/ppermute | solution.py:190
  3.0 1.5 %collective-permute-start.2 = (bf16[104,2496]{1,0:T(8,128)(2,1)}, bf16[104,2496]{1,0:T(8,128)(2,1)S(1)}, u32[]{:S(2)}, u32[]{:S(2)}) collective-permute-start(bf16[104,2496]{1,0:T(8,128)(2,1)} %param.16), channel_id=1, source_target_pairs={{0,2},{2,0},{4,6},{6,4},{8,10},{10,8},{12,14},{14,12},{16,18},{18,... | collective-permute-start | bytes 1557512 | tf_op jit(solution)/shard_map/ppermute | solution.py:193
  4.5 1.5 %collective-permute-start.3 = (bf16[104,2496]{1,0:T(8,128)(2,1)}, bf16[104,2496]{1,0:T(8,128)(2,1)S(1)}, u32[]{:S(2)}, u32[]{:S(2)}) collective-permute-start(bf16[104,2496]{1,0:T(8,128)(2,1)} %param.16), channel_id=1, source_target_pairs={{0,4},{2,6},{4,0},{6,2},{8,12},{10,14},{12,8},{14,10},{16,20},{18,... | collective-permute-start | bytes 1557512 | tf_op jit(solution)/shard_map/ppermute | solution.py:193
  6.0 1.1 %copy-done.1 = bf16[448,832]{1,0:T(8,128)(2,1)S(1)} copy-done((bf16[448,832]{1,0:T(8,128)(2,1)S(1)}, bf16[448,832]{1,0:T(8,128)(2,1)}, u32[]{:S(2)}) %copy-start.1) | copy-done | bytes 745496
  7.2 0.3 shard_map.118.refs_0_
  7.5 0.1 collective-permute-start
  7.5 0.7 convert_bitcast_fusion.1
  8.2 0.7 fusion.10.order_ref
  8.9 0.7 stack.22
  9.6 0.7 stack.21
  10.3 0.8 reshape.52
  11.1 0.2 convert_reduce_fusion
  11.3 0.0 copy-start
  11.4 4.1 %copy-done = bf16[4,832,1664]{2,1,0:T(8,128)(2,1)S(1)} copy-done((bf16[4,832,1664]{2,1,0:T(8,128)(2,1)S(1)}, bf16[4,832,1664]{2,1,0:T(8,128)(2,1)}, u32[]{:S(2)}) %copy-start) | copy-done | bytes 11075608
  15.5 1.1 %copy-done.2 = bf16[448,832]{1,0:T(8,128)(2,1)S(1)} copy-done((bf16[448,832]{1,0:T(8,128)(2,1)S(1)}, bf16[448,832]{1,0:T(8,128)(2,1)}, u32[]{:S(2)}) %copy-start.2) | copy-done | bytes 745496
  16.6 3.6 %shard_map.119 = f32[112,1664]{1,0:T(8,128)S(1)} custom-call(bf16[448,832]{1,0:T(8,128)(2,1)S(1)} %copy-done.2, bf16[2,832]{1,0:T(2,128)(2,1)S(1)} %pad_maximum_fusion.4.gain_bias_ref, f32[448,256]{1,0:T(8,128)S(1)} %shard_map.118.refs_0_, f32[448,256]{1,0:T(8,128)S(1)} %collective-permute-done.refs_1_, bf16[4,832,1664]{2,1,0:T(8,128)(2,1)S(1)} %copy-done), custom_call_target="tpu_custom_call" | custom-call | flops 1000 | bytes 1000 | tf_op jit(solution)/shard_map/pallas_call | solution.py:112
  20.3 0.9 constant_dynamic-slice_fusion.1
  21.2 0.5 collective-permute-start.7
  21.7 0.1 pad.15.clone
  21.8 0.1 fusion.7
  21.9 2.6 %collective-permute-start.10 = (bf16[104,2496]{1,0:T(8,128)(2,1)}, bf16[104,2496]{1,0:T(8,128)(2,1)}, u32[]{:S(2)}, u32[]{:S(2)}) collective-permute-start(bf16[104,2496]{1,0:T(8,128)(2,1)} %collective-permute-done.1), channel_id=1, source_target_pairs={{0,8},{2,10},{4,12},{6,14},{8,24},{10,26},{12,28},{14,30},{16,0},{... | collective-permute-start | bytes 1557512 | tf_op jit(solution)/shard_map/ppermute | solution.py:190
  24.6 0.5 collective-permute-start.11
  25.1 0.5 collective-permute-start.12
  25.6 0.7 slice.27
  26.3 1.5 %collective-permute-start.4 = (bf16[104,1280]{1,0:T(8,128)(2,1)}, bf16[104,1280]{1,0:T(8,128)(2,1)}, u32[]{:S(2)}, u32[]{:S(2)}) collective-permute-start(bf16[104,1280]{1,0:T(8,128)(2,1)} %slice.27), channel_id=1, source_target_pairs={{0,2},{2,0},{4,6},{6,4},{8,10},{10,8},{12,14},{14,12},{16,18},{18,... | collective-permute-start | bytes 798728 | tf_op jit(solution)/shard_map/ppermute | solution.py:196
  27.8 0.7 slice.28
  28.5 0.3 copy.19.gain_ref
  28.8 0.1 copy.18
  29.0 1.6 %collective-permute-start.5 = (bf16[104,1216]{1,0:T(8,128)(2,1)}, bf16[104,1216]{1,0:T(8,128)(2,1)}, u32[]{:S(2)}, u32[]{:S(2)}) collective-permute-start(bf16[104,1216]{1,0:T(8,128)(2,1)} %slice.28), channel_id=1, source_target_pairs={{0,4},{2,6},{4,0},{6,2},{8,12},{10,14},{12,8},{14,10},{16,20},{18,... | collective-permute-start | bytes 758792 | tf_op jit(solution)/shard_map/ppermute | solution.py:197
  30.6 0.2 add_convert_fusion
  30.7 1.1 %convolution_convert_fusion = bf16[256,896]{1,0:T(8,128)(2,1)} fusion(bf16[112,2]{1,0:T(8,128)(2,1)S(1)} %copy.18, bf16[112,832]{1,0:T(8,128)(2,1)S(1)} %add_convert_fusion, bf16[896]{0:T(1024)(128)(2,1)S(1)} %pad.15.clone, s32[112]{0:T(128)S(1)} %multiply_add_fusion), kind=kOutput, calls=%fused_computation.8 | convolution fusion | flops 52240384 | bytes 647808 | tf_op jit(solution)/shard_map/dot_general | solution.py:237
  31.8 3.6 %all-to-all-start = ((bf16[16,16,896]{2,1,0:T(8,128)(2,1)}), bf16[16,16,896]{2,1,0:T(8,128)(2,1)S(1)}, u32[]{:S(2)}, u32[]{:S(2)}) async-start(bf16[16,16,896]{2,1,0:T(8,128)(2,1)} %bitcast.5), calls=%async_computation | async-start | bytes 917504 | tf_op jit(solution)/shard_map/all_to_all | solution.py:238
  35.4 13.2 %collective-permute-done.4 = bf16[104,1280]{1,0:T(8,128)(2,1)} collective-permute-done((bf16[104,1280]{1,0:T(8,128)(2,1)}, bf16[104,1280]{1,0:T(8,128)(2,1)}, u32[]{:S(2)}, u32[]{:S(2)}) %collective-permute-start.4) | collective-permute-done | bytes 266272 | tf_op jit(solution)/shard_map/ppermute | solution.py:196
  48.6 1.7 %constant_dynamic-update-slice_fusion.1 = bf16[104,2496]{1,0:T(8,128)(2,1)} fusion(bf16[104,1280]{1,0:T(8,128)(2,1)} %collective-permute-done.4), kind=kLoop, calls=%fused_computation.22 | loop fusion | bytes 532480
  50.3 0.5 collective-permute-start.13
  50.8 1.7 %constant_dynamic-update-slice_fusion = bf16[104,2496]{1,0:T(8,128)(2,1)} fusion(bf16[104,2496]{1,0:T(8,128)(2,1)} %constant_dynamic-update-slice_fusion.1, bf16[104,1216]{1,0:T(8,128)(2,1)} %collective-permute-done.5), kind=kLoop, calls=%fused_computation.21 | loop fusion | bytes 532480 | tf_op jit(solution)/shard_map/concatenate | solution.py:198
  52.6 0.1 collective-permute-start.14
  52.7 0.3 collective-permute-start.15
  53.0 2.9 %pad_maximum_fusion = bf16[416,2496]{1,0:T(8,128)(2,1)} fusion(bf16[104,2496]{1,0:T(8,128)(2,1)} %constant_dynamic-update-slice_fusion, bf16[104,2496]{1,0:T(8,128)(2,1)} %copy-done.5, bf16[104,2496]{1,0:T(8,128)(2,1)S(1)} %collective-permute-done.2, bf16[104,2496]{1,0:T(8,128)(2,1)} %param.16), kind=kLoop, calls=%fused_computation.3 | loop fusion | flops 8306688 | bytes 4153344 | tf_op jit(solution)/shard_map/concatenate | solution.py:259
  55.9 0.0 collective-permute-start.9
  55.9 10.6 %collective-permute-done.13 = bf16[104,2496]{1,0:T(8,128)(2,1)} collective-permute-done((bf16[104,2496]{1,0:T(8,128)(2,1)}, bf16[104,2496]{1,0:T(8,128)(2,1)}, u32[]{:S(2)}, u32[]{:S(2)}) %collective-permute-start.13) | collective-permute-done | bytes 519200 | tf_op jit(solution)/shard_map/ppermute | solution.py:190
  66.5 1.5 %pad_maximum_fusion.1 = bf16[312,2496]{1,0:T(8,128)(2,1)S(1)} fusion(bf16[104,2496]{1,0:T(8,128)(2,1)} %collective-permute-done.12, bf16[104,2496]{1,0:T(8,128)(2,1)} %collective-permute-done.11, bf16[104,2496]{1,0:T(8,128)(2,1)} %collective-permute-done.1), kind=kLoop, calls=%fused_computation.4 | loop fusion | flops 4672512 | bytes 3115008 | tf_op jit(solution)/shard_map/concatenate | solution.py:259
  68.0 0.9 collective-permute-start.16
  68.9 0.3 collective-permute-start.17
  69.2 1.5 %pad_maximum_fusion.2 = bf16[312,2496]{1,0:T(8,128)(2,1)S(1)} fusion(bf16[104,2496]{1,0:T(8,128)(2,1)} %collective-permute-done.15, bf16[104,2496]{1,0:T(8,128)(2,1)} %collective-permute-done.14, bf16[104,2496]{1,0:T(8,128)(2,1)} %collective-permute-done.10), kind=kLoop, calls=%fused_computation.5 | loop fusion | flops 4672512 | bytes 3115008 | tf_op jit(solution)/shard_map/concatenate | solution.py:259
  70.7 1.9 %shard_map.120 = bf16[16,104,512]{2,1,0:T(8,128)(2,1)S(1)} custom-call(s32[1]{0:T(128)} %bitcast.3.index_ref, s32[16]{0:T(128)S(1)} %fusion.10.order_ref, bf16[16,104,1]{2,1,0:T(8,128)(2,1)S(1)} %copy.19.gain_ref, bf16[832,512]{1,0:T(8,128)(2,1)S(1)} %bitcast.28, bf16[832,512]{1,0:T(8,128)(2,1)S(1)} %collective-permute-done.6.refs_1_, ...), custom_call_target="tpu_custom_call" | custom-call | flops 1000 | bytes 1000 | tf_op jit(solution)/shard_map/pallas_call | solution.py:164
  72.6 4.9 %collective-permute-done.9 = bf16[104,2496]{1,0:T(8,128)(2,1)} collective-permute-done((bf16[104,2496]{1,0:T(8,128)(2,1)}, bf16[104,2496]{1,0:T(8,128)(2,1)}, u32[]{:S(2)}, u32[]{:S(2)}) %collective-permute-start.9) | collective-permute-done | bytes 519200 | tf_op jit(solution)/shard_map/ppermute | solution.py:190
  77.6 0.1 fusion.14
  77.7 1.5 %fusion.15 = f32[512,2496]{0,1:T(8,128)S(1)} fusion(bf16[416,512]{1,0:T(8,128)(2,1)S(1)} %bitcast.29, bf16[416,2496]{1,0:T(8,128)(2,1)S(1)} %copy-done.4), kind=kOutput, calls=%fused_computation.47 | convolution fusion | flops 1063256064 | bytes 7614464 | tf_op jit(solution)/shard_map/dot_general | solution.py:263
  79.2 1.6 %convolution_add_fusion.1 = f32[512,2496]{0,1:T(8,128)S(1)} fusion(f32[512,2496]{0,1:T(8,128)S(1)} %fusion.15, bf16[312,512]{1,0:T(8,128)(2,1)S(1)} %bitcast.33, bf16[312,2496]{1,0:T(8,128)(2,1)S(1)} %pad_maximum_fusion.1), kind=kOutput, calls=%fused_computation.2 | convolution fusion | flops 798720000 | bytes 12100608 | tf_op jit(solution)/shard_map/dot_general | solution.py:263
  80.8 1.6 %convolution_add_fusion = f32[512,2496]{0,1:T(8,128)S(1)} fusion(f32[512,2496]{0,1:T(8,128)S(1)} %convolution_add_fusion.1, bf16[312,512]{1,0:T(8,128)(2,1)S(1)} %bitcast.32, bf16[312,2496]{1,0:T(8,128)(2,1)S(1)} %pad_maximum_fusion.2), kind=kOutput, calls=%fused_computation.1 | convolution fusion | flops 798720000 | bytes 12100608 | tf_op jit(solution)/shard_map/dot_general | solution.py:263
  82.4 0.4 collective-permute-done.16
  82.8 0.3 collective-permute-done.17
  83.1 1.2 %pad_maximum_fusion.3 = bf16[312,2496]{1,0:T(8,128)(2,1)S(1)} fusion(bf16[104,2496]{1,0:T(8,128)(2,1)S(1)} %collective-permute-done.17, bf16[104,2496]{1,0:T(8,128)(2,1)S(1)} %collective-permute-done.16, bf16[104,2496]{1,0:T(8,128)(2,1)} %collective-permute-done.13), kind=kLoop, calls=%fused_computation.6 | loop fusion | flops 4672512 | bytes 3115008 | tf_op jit(solution)/shard_map/concatenate | solution.py:259
  84.3 0.4 collective-permute-start.20
  84.7 1.5 %collective-permute-start.19 = (bf16[104,1280]{1,0:T(8,128)(2,1)S(1)}, bf16[104,1280]{1,0:T(8,128)(2,1)S(1)}, u32[]{:S(2)}, u32[]{:S(2)}) collective-permute-start(bf16[104,1280]{1,0:T(8,128)(2,1)S(1)} %slice.33), channel_id=1, source_target_pairs={{0,2},{2,0},{4,6},{6,4},{8,10},{10,8},{12,14},{14,12},{16,18},{18,... | collective-permute-start | bytes 798728 | tf_op jit(solution)/shard_map/ppermute | solution.py:196
  86.2 1.5 %fusion.16 = f32[512,2496]{0,1:T(8,128)S(1)} fusion(bf16[312,512]{1,0:T(8,128)(2,1)S(1)} %bitcast.31, bf16[312,2496]{1,0:T(8,128)(2,1)S(1)} %pad_maximum_fusion.3), kind=kOutput, calls=%fused_computation.48 | convolution fusion | flops 797442048 | bytes 6988800 | tf_op jit(solution)/shard_map/dot_general | solution.py:263
  87.7 1.3 %add.66 = f32[512,2496]{0,1:T(8,128)S(1)} add(f32[512,2496]{0,1:T(8,128)S(1)} %convolution_add_fusion, f32[512,2496]{0,1:T(8,128)S(1)} %fusion.16) | non-fusion elementwise | flops 1277952 | bytes 15335424 | tf_op jit(solution)/shard_map/add | solution.py:273
  89.0 3.1 %collective-permute-done.20 = bf16[104,1216]{1,0:T(8,128)(2,1)S(1)} collective-permute-done((bf16[104,1216]{1,0:T(8,128)(2,1)S(1)}, bf16[104,1216]{1,0:T(8,128)(2,1)S(1)}, u32[]{:S(2)}, u32[]{:S(2)}) %collective-permute-start.20) | collective-permute-done | bytes 252960 | tf_op jit(solution)/shard_map/ppermute | solution.py:197
  92.1 0.1 collective-permute-done.19
  92.2 5.4 %collective-permute-done.18 = bf16[104,2496]{1,0:T(8,128)(2,1)S(1)} collective-permute-done((bf16[104,2496]{1,0:T(8,128)(2,1)}, bf16[104,2496]{1,0:T(8,128)(2,1)S(1)}, u32[]{:S(2)}, u32[]{:S(2)}) %collective-permute-start.18) | collective-permute-done | bytes 519200 | tf_op jit(solution)/shard_map/ppermute | solution.py:190
  97.6 1.2 %maximum_maximum_fusion = bf16[312,2496]{1,0:T(8,128)(2,1)S(1)} fusion(bf16[104,1216]{1,0:T(8,128)(2,1)S(1)} %collective-permute-done.20, bf16[104,1280]{1,0:T(8,128)(2,1)S(1)} %collective-permute-done.19, bf16[104,2496]{1,0:T(8,128)(2,1)S(1)} %collective-permute-done.18, bf16[104,2496]{1,0:T(8,128)(2,1)} %collective-permute-done.9), kind=kLoop, calls=%fused_computation.7 | loop fusion | flops 6230016 | bytes 3115008 | tf_op jit(solution)/shard_map/concatenate | solution.py:259
  98.8 1.5 %fusion.17 = f32[512,2496]{0,1:T(8,128)S(1)} fusion(bf16[312,512]{1,0:T(8,128)(2,1)S(1)} %bitcast.30, bf16[312,2496]{1,0:T(8,128)(2,1)S(1)} %maximum_maximum_fusion), kind=kOutput, calls=%fused_computation.49 | convolution fusion | flops 797442048 | bytes 6988800 | tf_op jit(solution)/shard_map/dot_general | solution.py:263
  100.4 2.9 %select_convert_fusion = bf16[512,2496]{0,1:T(8,128)(2,1)} fusion(f32[512,2496]{0,1:T(8,128)S(1)} %add.66, f32[512,2496]{0,1:T(8,128)S(1)} %fusion.17, pred[512]{0:T(512)(128)(4,1)S(1)} %fusion.8), kind=kLoop, calls=%fused_computation | loop fusion | flops 3833856 | bytes 12780032 | tf_op jit(solution)/shard_map/convert_element_type | solution.py:285
  (37 shorter events, 0.2 us)
Async XLA Ops:
  0.0 20.3 %collective-permute-start.1 = (bf16[104,2496]{1,0:T(8,128)(2,1)}, bf16[104,2496]{1,0:T(8,128)(2,1)}, u32[]{:S(2)}, u32[]{:S(2)}) collective-permute-start(bf16[104,2496]{1,0:T(8,128)(2,1)} %param.16), channel_id=1, source_target_pairs={{0,8},{2,10},{4,12},{6,14},{8,24},{10,26},{12,28},{14,30},{16,0},{... | collective-permute-start | bytes 1557512 | tf_op jit(solution)/shard_map/ppermute | solution.py:190
  3.0 17.2 %collective-permute-start.2 = (bf16[104,2496]{1,0:T(8,128)(2,1)}, bf16[104,2496]{1,0:T(8,128)(2,1)S(1)}, u32[]{:S(2)}, u32[]{:S(2)}) collective-permute-start(bf16[104,2496]{1,0:T(8,128)(2,1)} %param.16), channel_id=1, source_target_pairs={{0,2},{2,0},{4,6},{6,4},{8,10},{10,8},{12,14},{14,12},{16,18},{18,... | collective-permute-start | bytes 1557512 | tf_op jit(solution)/shard_map/ppermute | solution.py:193
  4.5 15.8 %collective-permute-start.3 = (bf16[104,2496]{1,0:T(8,128)(2,1)}, bf16[104,2496]{1,0:T(8,128)(2,1)S(1)}, u32[]{:S(2)}, u32[]{:S(2)}) collective-permute-start(bf16[104,2496]{1,0:T(8,128)(2,1)} %param.16), channel_id=1, source_target_pairs={{0,4},{2,6},{4,0},{6,2},{8,12},{10,14},{12,8},{14,10},{16,20},{18,... | collective-permute-start | bytes 1557512 | tf_op jit(solution)/shard_map/ppermute | solution.py:193
  6.0 1.1 %copy-start.1 = (bf16[448,832]{1,0:T(8,128)(2,1)S(1)}, bf16[448,832]{1,0:T(8,128)(2,1)}, u32[]{:S(2)}) copy-start(bf16[448,832]{1,0:T(8,128)(2,1)} %patches_ref.3) | copy-start | bytes 2236420
  7.5 3.9 %collective-permute-start = (f32[448,256]{1,0:T(8,128)S(1)}, f32[448,256]{1,0:T(8,128)S(1)}, u32[]{:S(2)}, u32[]{:S(2)}) collective-permute-start(f32[448,256]{1,0:T(8,128)S(1)} %shard_map.118.refs_0_), channel_id=1, source_target_pairs={{0,1},{1,0},{2,3},{3,2},{4,5},{5,4},{6,7},{7,6},{8,9},{9,8},{10,11... | collective-permute-start | bytes 1376264 | tf_op jit(solution)/shard_map/ppermute | solution.py:26
  11.3 4.1 %copy-start = (bf16[4,832,1664]{2,1,0:T(8,128)(2,1)S(1)}, bf16[4,832,1664]{2,1,0:T(8,128)(2,1)}, u32[]{:S(2)}) copy-start(bf16[4,832,1664]{2,1,0:T(8,128)(2,1)} %refs_2_.1) | copy-start | bytes 33226756
  15.5 1.1 %copy-start.2 = (bf16[448,832]{1,0:T(8,128)(2,1)S(1)}, bf16[448,832]{1,0:T(8,128)(2,1)}, u32[]{:S(2)}) copy-start(bf16[448,832]{1,0:T(8,128)(2,1)} %patches_ref.3) | copy-start | bytes 2236420
  16.6 5.2 %copy-start.6 = (s32[2]{0:T(128)S(1)}, s32[2]{0:T(128)}, u32[]{:S(2)}) copy-start(s32[2]{0:T(128)} %param.18) | copy-start | bytes 28
  20.2 28.4 %copy-start.3 = (bf16[512,832]{0,1:T(8,128)(2,1)S(1)}, bf16[512,832]{0,1:T(8,128)(2,1)}, u32[]{:S(2)}) copy-start(bf16[512,832]{0,1:T(8,128)(2,1)} %param.14) | copy-start | bytes 2555908
  20.3 28.3 %copy-start.5 = (bf16[104,2496]{1,0:T(8,128)(2,1)}, bf16[104,2496]{1,0:T(8,128)(2,1)S(1)}, u32[]{:S(2)}) copy-start(bf16[104,2496]{1,0:T(8,128)(2,1)S(1)} %collective-permute-done.3) | copy-start | bytes 1557508
  21.2 7.7 %collective-permute-start.7 = (f32[112,832]{1,0:T(8,128)}, f32[112,832]{1,0:T(8,128)S(1)}, u32[]{:S(2)}, u32[]{:S(2)}) collective-permute-start(f32[112,832]{1,0:T(8,128)} %constant_dynamic-slice_fusion.1), channel_id=1, source_target_pairs={{0,1},{1,0},{2,3},{3,2},{4,5},{5,4},{6,7},{7,6},{8,9},{9,8},{10,11... | collective-permute-start | bytes 1118216 | tf_op jit(solution)/shard_map/ppermute | solution.py:26
  21.9 28.4 %collective-permute-start.10 = (bf16[104,2496]{1,0:T(8,128)(2,1)}, bf16[104,2496]{1,0:T(8,128)(2,1)}, u32[]{:S(2)}, u32[]{:S(2)}) collective-permute-start(bf16[104,2496]{1,0:T(8,128)(2,1)} %collective-permute-done.1), channel_id=1, source_target_pairs={{0,8},{2,10},{4,12},{6,14},{8,24},{10,26},{12,28},{14,30},{16,0},{... | collective-permute-start | bytes 1557512 | tf_op jit(solution)/shard_map/ppermute | solution.py:190
  24.6 25.8 %collective-permute-start.11 = (bf16[104,2496]{1,0:T(8,128)(2,1)}, bf16[104,2496]{1,0:T(8,128)(2,1)}, u32[]{:S(2)}, u32[]{:S(2)}) collective-permute-start(bf16[104,2496]{1,0:T(8,128)(2,1)} %collective-permute-done.1), channel_id=1, source_target_pairs={{0,2},{2,0},{4,6},{6,4},{8,10},{10,8},{12,14},{14,12},{16,18},{18,... | collective-permute-start | bytes 1557512 | tf_op jit(solution)/shard_map/ppermute | solution.py:193
  25.1 25.2 %collective-permute-start.12 = (bf16[104,2496]{1,0:T(8,128)(2,1)}, bf16[104,2496]{1,0:T(8,128)(2,1)}, u32[]{:S(2)}, u32[]{:S(2)}) collective-permute-start(bf16[104,2496]{1,0:T(8,128)(2,1)} %collective-permute-done.1), channel_id=1, source_target_pairs={{0,4},{2,6},{4,0},{6,2},{8,12},{10,14},{12,8},{14,10},{16,20},{18,... | collective-permute-start | bytes 1557512 | tf_op jit(solution)/shard_map/ppermute | solution.py:193
  26.3 22.3 %collective-permute-start.4 = (bf16[104,1280]{1,0:T(8,128)(2,1)}, bf16[104,1280]{1,0:T(8,128)(2,1)}, u32[]{:S(2)}, u32[]{:S(2)}) collective-permute-start(bf16[104,1280]{1,0:T(8,128)(2,1)} %slice.27), channel_id=1, source_target_pairs={{0,2},{2,0},{4,6},{6,4},{8,10},{10,8},{12,14},{14,12},{16,18},{18,... | collective-permute-start | bytes 798728 | tf_op jit(solution)/shard_map/ppermute | solution.py:196
  29.0 21.9 %collective-permute-start.5 = (bf16[104,1216]{1,0:T(8,128)(2,1)}, bf16[104,1216]{1,0:T(8,128)(2,1)}, u32[]{:S(2)}, u32[]{:S(2)}) collective-permute-start(bf16[104,1216]{1,0:T(8,128)(2,1)} %slice.28), channel_id=1, source_target_pairs={{0,4},{2,6},{4,0},{6,2},{8,12},{10,14},{12,8},{14,10},{16,20},{18,... | collective-permute-start | bytes 758792 | tf_op jit(solution)/shard_map/ppermute | solution.py:197
  31.8 34.7 %all-to-all-start = ((bf16[16,16,896]{2,1,0:T(8,128)(2,1)}), bf16[16,16,896]{2,1,0:T(8,128)(2,1)S(1)}, u32[]{:S(2)}, u32[]{:S(2)}) async-start(bf16[16,16,896]{2,1,0:T(8,128)(2,1)} %bitcast.5), calls=%async_computation | async-start | bytes 917504 | tf_op jit(solution)/shard_map/all_to_all | solution.py:238
  48.6 22.0 %collective-permute-start.6 = (bf16[832,512]{1,0:T(8,128)(2,1)S(1)}, bf16[832,512]{1,0:T(8,128)(2,1)S(1)}, u32[]{:S(2)}, u32[]{:S(2)}) collective-permute-start(bf16[832,512]{1,0:T(8,128)(2,1)S(1)} %bitcast.27), channel_id=1, source_target_pairs={{0,1},{1,0},{2,3},{3,2},{4,5},{5,4},{6,7},{7,6},{8,9},{9,8},{10,11... | collective-permute-start | bytes 2555912 | tf_op jit(solution)/shard_map/ppermute | solution.py:26
  50.3 16.2 %collective-permute-start.13 = (bf16[104,2496]{1,0:T(8,128)(2,1)}, bf16[104,2496]{1,0:T(8,128)(2,1)}, u32[]{:S(2)}, u32[]{:S(2)}) collective-permute-start(bf16[104,2496]{1,0:T(8,128)(2,1)} %collective-permute-done.10), channel_id=1, source_target_pairs={{0,8},{2,10},{4,12},{6,14},{8,24},{10,26},{12,28},{14,30},{16,0},{... | collective-permute-start | bytes 1557512 | tf_op jit(solution)/shard_map/ppermute | solution.py:190
  52.6 15.4 %collective-permute-start.14 = (bf16[104,2496]{1,0:T(8,128)(2,1)}, bf16[104,2496]{1,0:T(8,128)(2,1)}, u32[]{:S(2)}, u32[]{:S(2)}) collective-permute-start(bf16[104,2496]{1,0:T(8,128)(2,1)} %collective-permute-done.10), channel_id=1, source_target_pairs={{0,2},{2,0},{4,6},{6,4},{8,10},{10,8},{12,14},{14,12},{16,18},{18,... | collective-permute-start | bytes 1557512 | tf_op jit(solution)/shard_map/ppermute | solution.py:193
  52.7 15.3 %collective-permute-start.15 = (bf16[104,2496]{1,0:T(8,128)(2,1)}, bf16[104,2496]{1,0:T(8,128)(2,1)}, u32[]{:S(2)}, u32[]{:S(2)}) collective-permute-start(bf16[104,2496]{1,0:T(8,128)(2,1)} %collective-permute-done.10), channel_id=1, source_target_pairs={{0,4},{2,6},{4,0},{6,2},{8,12},{10,14},{12,8},{14,10},{16,20},{18,... | collective-permute-start | bytes 1557512 | tf_op jit(solution)/shard_map/ppermute | solution.py:193
  55.9 21.7 %collective-permute-start.9 = (bf16[104,2496]{1,0:T(8,128)(2,1)}, bf16[104,2496]{1,0:T(8,128)(2,1)}, u32[]{:S(2)}, u32[]{:S(2)}) collective-permute-start(bf16[104,2496]{1,0:T(8,128)(2,1)} %constant_dynamic-update-slice_fusion), channel_id=1, source_target_pairs={{0,8},{2,10},{4,12},{6,14},{8,24},{10,26},{12,28},{14,30},{16,0},{... | collective-permute-start | bytes 1557512 | tf_op jit(solution)/shard_map/ppermute | solution.py:190
  66.5 4.2 %collective-permute-start.8 = (bf16[256,896]{1,0:T(8,128)(2,1)S(1)}, bf16[256,896]{1,0:T(8,128)(2,1)S(1)}, u32[]{:S(2)}, u32[]{:S(2)}) collective-permute-start(bf16[256,896]{1,0:T(8,128)(2,1)S(1)} %bitcast.25), channel_id=1, source_target_pairs={{0,1},{1,0},{2,3},{3,2},{4,5},{5,4},{6,7},{7,6},{8,9},{9,8},{10,11... | collective-permute-start | bytes 1376264 | tf_op jit(solution)/shard_map/ppermute | solution.py:26
  68.0 14.8 %collective-permute-start.16 = (bf16[104,2496]{1,0:T(8,128)(2,1)}, bf16[104,2496]{1,0:T(8,128)(2,1)S(1)}, u32[]{:S(2)}, u32[]{:S(2)}) collective-permute-start(bf16[104,2496]{1,0:T(8,128)(2,1)} %collective-permute-done.13), channel_id=1, source_target_pairs={{0,2},{2,0},{4,6},{6,4},{8,10},{10,8},{12,14},{14,12},{16,18},{18,... | collective-permute-start | bytes 1557512 | tf_op jit(solution)/shard_map/ppermute | solution.py:193
  68.9 14.2 %collective-permute-start.17 = (bf16[104,2496]{1,0:T(8,128)(2,1)}, bf16[104,2496]{1,0:T(8,128)(2,1)S(1)}, u32[]{:S(2)}, u32[]{:S(2)}) collective-permute-start(bf16[104,2496]{1,0:T(8,128)(2,1)} %collective-permute-done.13), channel_id=1, source_target_pairs={{0,4},{2,6},{4,0},{6,2},{8,12},{10,14},{12,8},{14,10},{16,20},{18,... | collective-permute-start | bytes 1557512 | tf_op jit(solution)/shard_map/ppermute | solution.py:193
  70.7 7.0 %copy-start.4 = (bf16[416,2496]{1,0:T(8,128)(2,1)S(1)}, bf16[416,2496]{1,0:T(8,128)(2,1)}, u32[]{:S(2)}) copy-start(bf16[416,2496]{1,0:T(8,128)(2,1)} %pad_maximum_fusion) | copy-start | bytes 6230020
  83.1 14.6 %collective-permute-start.18 = (bf16[104,2496]{1,0:T(8,128)(2,1)}, bf16[104,2496]{1,0:T(8,128)(2,1)S(1)}, u32[]{:S(2)}, u32[]{:S(2)}) collective-permute-start(bf16[104,2496]{1,0:T(8,128)(2,1)} %collective-permute-done.9), channel_id=1, source_target_pairs={{0,8},{2,10},{4,12},{6,14},{8,24},{10,26},{12,28},{14,30},{16,0},{... | collective-permute-start | bytes 1557512 | tf_op jit(solution)/shard_map/ppermute | solution.py:190
  84.3 7.8 %collective-permute-start.20 = (bf16[104,1216]{1,0:T(8,128)(2,1)S(1)}, bf16[104,1216]{1,0:T(8,128)(2,1)S(1)}, u32[]{:S(2)}, u32[]{:S(2)}) collective-permute-start(bf16[104,1216]{1,0:T(8,128)(2,1)S(1)} %slice.34), channel_id=1, source_target_pairs={{0,4},{2,6},{4,0},{6,2},{8,12},{10,14},{12,8},{14,10},{16,20},{18,... | collective-permute-start | bytes 758792 | tf_op jit(solution)/shard_map/ppermute | solution.py:197
  84.7 7.5 %collective-permute-start.19 = (bf16[104,1280]{1,0:T(8,128)(2,1)S(1)}, bf16[104,1280]{1,0:T(8,128)(2,1)S(1)}, u32[]{:S(2)}, u32[]{:S(2)}) collective-permute-start(bf16[104,1280]{1,0:T(8,128)(2,1)S(1)} %slice.33), channel_id=1, source_target_pairs={{0,2},{2,0},{4,6},{6,4},{8,10},{10,8},{12,14},{14,12},{16,18},{18,... | collective-permute-start | bytes 798728 | tf_op jit(solution)/shard_map/ppermute | solution.py:196

commit v11 on v10

--- a/solution.py
+++ b/solution.py
@@ -73,7 +73,7 @@
         in_specs=[vmem],
         out_specs=vmem,
         compiler_params=pltpu.CompilerParams(vmem_limit_bytes=VMEM),
-        cost_estimate=LIGHT,
+        cost_estimate=pl.CostEstimate(flops=1000, bytes_accessed=16 << 20, transcendentals=0),
     )(patches)
 
 
@@ -242,19 +242,16 @@
     held[2], sides[1] = tie(held[2], sides[1])
     held.append(along_line(held[2]))
     sides.append(to_sides(held[2]))
-    corners.append(along_line(corners[0]))
     images = [arrived] + [tp_shift(arrived, n_tp, d) for d in range(1, n_tp)]
     blocks = combine(tp_index, order, texts, images, gain_column)
 
+    held[3], corners[0] = tie(held[3], corners[0])
+    corners.append(along_line(corners[0]))
     held[3], sides[2] = tie(held[3], sides[2])
     sides.append(to_sides(held[3]))
     for step in range(4, lines):
         held.append(along_line(held[step - 1]))
         sides.append(to_sides(held[step]))
-    blocks, corners[1] = tie(blocks, corners[1])
-    for step in range(2, lines - 1):
-        corners.append(along_line(corners[step - 1]))
-
     def product(first, weights):
         weight = jnp.concatenate(weights, axis=0)
         count = weight.shape[0]
@@ -267,6 +264,10 @@
     total = product(0, [held[0], *sides[0], corners[0]])
     for step in range(1, lines - 1):
         (total,) = tie(total + product(step * 3 + 1, [held[step], *sides[step]]))
+        if step == 1:
+            total, corners[1] = tie(total, corners[1])
+            for other in range(2, lines - 1):
+                corners.append(along_line(corners[other - 1]))
 
     total, sides[-1] = tie(total, sides[-1])
     corners.append(to_corner(*sides[-1]))

time: 104 us -> 95.7 us (0.920)
  waiting for transfers between devices: 38.1 us -> 26.2 us
  starting transfers between devices: 20.9 us -> 24.8 us
  local copies, waits for them, and re-layouts: 15.7 us -> 14.4 us
  other arithmetic: 13.5 us -> 14.6 us
    ppermute x2, waiting for transfers between devices: 13.3 us -> 1.51 us  [to_corner(): left = lax.ppermute(by_y[:, :cut], 'req', x_perm)]
    ppermute x5, waiting for transfers between devices: 21 us -> 11.9 us  [along_line(): return lax.ppermute(block, 'req', line_perm)]
    ppermute x4, waiting for transfers between devices: 0.39 us -> 5.14 us  [to_sides(): lax.ppermute(block, 'req', x_perm)]
    ppermute x4, waiting for transfers between devices: 0.26 us -> 2.59 us  [to_sides(): lax.ppermute(block, 'req', y_perm)]
    ppermute x4, starting transfers between devices: 2.98 us -> 4.9 us  [to_sides(): lax.ppermute(block, 'req', x_perm)]
    ppermute x2, waiting for transfers between devices: 3.14 us -> 5.06 us  [to_corner(): right = lax.ppermute(by_x[:, cut:], 'req', y_perm)]
    concatenate x1 -> x0, local copies, waits for them, and re-layouts: 1.73 us -> none  [to_corner(): return jnp.concatenate([left, right], axis=1)]
    unnamed x15 -> x22, local copies, waits for them, and re-layouts: 8.13 us -> 6.59 us
  transfers between devices with their start and end apart: 22 -> 22, of which waited for: 8 -> 10; matrix products, arithmetic and copies ran while one was open for 24% -> 26% of each run, Pallas kernels for 6% -> 6%
where the time goes in v11:
time: 95.7 us; the launch traced here: 95.1 us
  waiting for transfers between devices  26.2 us (27%)
  starting transfers between devices  24.8 us (26%)
  other arithmetic  14.6 us (15%)
  local copies, waits for them, and re-layouts  14.4 us (15%)
  matrix products  8.86 us (9%)
  Pallas kernels  5.8 us (6%)
    ppermute x5, waiting for transfers between devices, along_line(): return lax.ppermute(block, 'req', line_perm)  11.9 us
    dot_general x5, matrix products, product(): lax.dot_general(source, weight, (((0,), (0,)), ((), ())), preferred_eleme...  7.78 us
    concatenate x5, other arithmetic, product(): weight = jnp.concatenate(weights, axis=0)  7.04 us
    unnamed x22, local copies, waits for them, and re-layouts  6.59 us
    ppermute x5, starting transfers between devices, along_line(): return lax.ppermute(block, 'req', line_perm)  6.46 us
    ppermute x4, waiting for transfers between devices, to_sides(): lax.ppermute(block, 'req', x_perm)  5.14 us
    ppermute x2, waiting for transfers between devices, to_corner(): right = lax.ppermute(by_x[:, cut:], 'req', y_perm)  5.06 us
    ppermute x4, starting transfers between devices, to_sides(): lax.ppermute(block, 'req', x_perm)  4.9 us
  transfers between devices with their start and end apart: 22, of which 10 were waited for; matrix products, arithmetic and copies ran while one was open for 26% of the time, Pallas kernels for 6%

profile of v11, /device:TPU:0, one launch (start us, length us, event | category | flops | bytes accessed | tf_op | source)
XLA Modules:
  0.0 95.1 jit_solution(701103798617501726)
XLA Ops:
  0.0 3.0 %collective-permute-start.1 = (bf16[104,2496]{1,0:T(8,128)(2,1)}, bf16[104,2496]{1,0:T(8,128)(2,1)}, u32[]{:S(2)}, u32[]{:S(2)}) collective-permute-start(bf16[104,2496]{1,0:T(8,128)(2,1)} %param.16), channel_id=1, source_target_pairs={{0,8},{2,10},{4,12},{6,14},{8,24},{10,26},{12,28},{14,30},{16,0},{... | collective-permute-start | bytes 1557512 | tf_op jit(solution)/shard_map/ppermute | solution.py:190
  3.0 1.5 %collective-permute-start.2 = (bf16[104,2496]{1,0:T(8,128)(2,1)}, bf16[104,2496]{1,0:T(8,128)(2,1)S(1)}, u32[]{:S(2)}, u32[]{:S(2)}) collective-permute-start(bf16[104,2496]{1,0:T(8,128)(2,1)} %param.16), channel_id=1, source_target_pairs={{0,2},{2,0},{4,6},{6,4},{8,10},{10,8},{12,14},{14,12},{16,18},{18,... | collective-permute-start | bytes 1557512 | tf_op jit(solution)/shard_map/ppermute | solution.py:193
  4.5 1.5 %collective-permute-start.3 = (bf16[104,2496]{1,0:T(8,128)(2,1)}, bf16[104,2496]{1,0:T(8,128)(2,1)S(1)}, u32[]{:S(2)}, u32[]{:S(2)}) collective-permute-start(bf16[104,2496]{1,0:T(8,128)(2,1)} %param.16), channel_id=1, source_target_pairs={{0,4},{2,6},{4,0},{6,2},{8,12},{10,14},{12,8},{14,10},{16,20},{18,... | collective-permute-start | bytes 1557512 | tf_op jit(solution)/shard_map/ppermute | solution.py:193
  6.0 1.1 %copy-done.1 = bf16[448,832]{1,0:T(8,128)(2,1)S(1)} copy-done((bf16[448,832]{1,0:T(8,128)(2,1)S(1)}, bf16[448,832]{1,0:T(8,128)(2,1)}, u32[]{:S(2)}) %copy-start.1) | copy-done | bytes 745496
  7.2 0.3 shard_map.118.refs_0_
  7.5 0.7 convert_bitcast_fusion.1
  8.2 0.7 fusion.10.order_ref
  8.9 0.7 stack.22
  9.6 0.7 stack.21
  10.3 0.8 reshape.52
  11.1 0.2 convert_reduce_fusion
  11.4 4.1 %copy-done = bf16[4,832,1664]{2,1,0:T(8,128)(2,1)S(1)} copy-done((bf16[4,832,1664]{2,1,0:T(8,128)(2,1)S(1)}, bf16[4,832,1664]{2,1,0:T(8,128)(2,1)}, u32[]{:S(2)}) %copy-start) | copy-done | bytes 11075608
  15.5 1.1 %copy-done.2 = bf16[448,832]{1,0:T(8,128)(2,1)S(1)} copy-done((bf16[448,832]{1,0:T(8,128)(2,1)S(1)}, bf16[448,832]{1,0:T(8,128)(2,1)}, u32[]{:S(2)}) %copy-start.2) | copy-done | bytes 745496
  16.6 3.6 %shard_map.119 = f32[112,1664]{1,0:T(8,128)S(1)} custom-call(bf16[448,832]{1,0:T(8,128)(2,1)S(1)} %copy-done.2, bf16[2,832]{1,0:T(2,128)(2,1)S(1)} %pad_maximum_fusion.5.gain_bias_ref, f32[448,256]{1,0:T(8,128)S(1)} %shard_map.118.refs_0_, f32[448,256]{1,0:T(8,128)S(1)} %collective-permute-done.refs_1_, bf16[4,832,1664]{2,1,0:T(8,128)(2,1)S(1)} %copy-done), custom_call_target="tpu_custom_call" | custom-call | flops 1000 | bytes 1000 | tf_op jit(solution)/shard_map/pallas_call | solution.py:112
  20.3 0.9 constant_dynamic-slice_fusion.1
  21.3 0.5 collective-permute-start.11
  21.9 2.6 %collective-permute-start.4 = (bf16[104,2496]{1,0:T(8,128)(2,1)}, bf16[104,2496]{1,0:T(8,128)(2,1)}, u32[]{:S(2)}, u32[]{:S(2)}) collective-permute-start(bf16[104,2496]{1,0:T(8,128)(2,1)} %collective-permute-done.1), channel_id=1, source_target_pairs={{0,8},{2,10},{4,12},{6,14},{8,24},{10,26},{12,28},{14,30},{16,0},{... | collective-permute-start | bytes 1557512 | tf_op jit(solution)/shard_map/ppermute | solution.py:190
  24.5 0.5 collective-permute-start.5
  25.1 0.5 collective-permute-start.6
  25.6 0.7 slice.28
  26.3 1.5 %collective-permute-start.9 = (bf16[104,1216]{1,0:T(8,128)(2,1)}, bf16[104,1216]{1,0:T(8,128)(2,1)}, u32[]{:S(2)}, u32[]{:S(2)}) collective-permute-start(bf16[104,1216]{1,0:T(8,128)(2,1)} %slice.28), channel_id=1, source_target_pairs={{0,4},{2,6},{4,0},{6,2},{8,12},{10,14},{12,8},{14,10},{16,20},{18,... | collective-permute-start | bytes 758792 | tf_op jit(solution)/shard_map/ppermute | solution.py:197
  27.8 0.7 slice.27
  28.6 0.1 copy.18
  28.7 1.6 %collective-permute-start.8 = (bf16[104,1280]{1,0:T(8,128)(2,1)}, bf16[104,1280]{1,0:T(8,128)(2,1)}, u32[]{:S(2)}, u32[]{:S(2)}) collective-permute-start(bf16[104,1280]{1,0:T(8,128)(2,1)} %slice.27), channel_id=1, source_target_pairs={{0,2},{2,0},{4,6},{6,4},{8,10},{10,8},{12,14},{14,12},{16,18},{18,... | collective-permute-start | bytes 798728 | tf_op jit(solution)/shard_map/ppermute | solution.py:196
  30.3 0.2 add_convert_fusion
  30.4 1.1 %convolution_convert_fusion = bf16[256,896]{1,0:T(8,128)(2,1)} fusion(bf16[112,2]{1,0:T(8,128)(2,1)S(1)} %copy.18, bf16[112,832]{1,0:T(8,128)(2,1)S(1)} %add_convert_fusion, bf16[896]{0:T(1024)(128)(2,1)S(1)} %pad.15.clone, s32[112]{0:T(128)S(1)} %multiply_add_fusion), kind=kOutput, calls=%fused_computation.7 | convolution fusion | flops 52240384 | bytes 647808 | tf_op jit(solution)/shard_map/dot_general | solution.py:237
  31.5 3.6 %all-to-all-start = ((bf16[16,16,896]{2,1,0:T(8,128)(2,1)}), bf16[16,16,896]{2,1,0:T(8,128)(2,1)S(1)}, u32[]{:S(2)}, u32[]{:S(2)}) async-start(bf16[16,16,896]{2,1,0:T(8,128)(2,1)} %bitcast.5), calls=%async_computation | async-start | bytes 917504 | tf_op jit(solution)/shard_map/all_to_all | solution.py:238
  35.1 0.3 copy.19.gain_ref
  35.4 1.9 %collective-permute-done.4 = bf16[104,2496]{1,0:T(8,128)(2,1)} collective-permute-done((bf16[104,2496]{1,0:T(8,128)(2,1)}, bf16[104,2496]{1,0:T(8,128)(2,1)}, u32[]{:S(2)}, u32[]{:S(2)}) %collective-permute-start.4) | collective-permute-done | bytes 519200 | tf_op jit(solution)/shard_map/ppermute | solution.py:190
  37.3 3.1 %collective-permute-done.5 = bf16[104,2496]{1,0:T(8,128)(2,1)} collective-permute-done((bf16[104,2496]{1,0:T(8,128)(2,1)}, bf16[104,2496]{1,0:T(8,128)(2,1)}, u32[]{:S(2)}, u32[]{:S(2)}) %collective-permute-start.5) | collective-permute-done | bytes 519200 | tf_op jit(solution)/shard_map/ppermute | solution.py:193
  40.5 2.2 %collective-permute-done.6 = bf16[104,2496]{1,0:T(8,128)(2,1)} collective-permute-done((bf16[104,2496]{1,0:T(8,128)(2,1)}, bf16[104,2496]{1,0:T(8,128)(2,1)}, u32[]{:S(2)}, u32[]{:S(2)}) %collective-permute-start.6) | collective-permute-done | bytes 519200 | tf_op jit(solution)/shard_map/ppermute | solution.py:193
  42.7 1.5 %collective-permute-start.14 = (bf16[104,2496]{1,0:T(8,128)(2,1)}, bf16[104,2496]{1,0:T(8,128)(2,1)}, u32[]{:S(2)}, u32[]{:S(2)}) collective-permute-start(bf16[104,2496]{1,0:T(8,128)(2,1)} %collective-permute-done.4), channel_id=1, source_target_pairs={{0,2},{2,0},{4,6},{6,4},{8,10},{10,8},{12,14},{14,12},{16,18},{18,... | collective-permute-start | bytes 1557512 | tf_op jit(solution)/shard_map/ppermute | solution.py:193
  44.2 4.4 %collective-permute-done.9 = bf16[104,1216]{1,0:T(8,128)(2,1)} collective-permute-done((bf16[104,1216]{1,0:T(8,128)(2,1)}, bf16[104,1216]{1,0:T(8,128)(2,1)}, u32[]{:S(2)}, u32[]{:S(2)}) %collective-permute-start.9) | collective-permute-done | bytes 252960 | tf_op jit(solution)/shard_map/ppermute | solution.py:197
  48.6 0.6 collective-permute-start.15
  49.2 1.1 %pad_maximum_fusion.4 = bf16[104,2496]{1,0:T(8,128)(2,1)S(1)} fusion(bf16[104,1216]{1,0:T(8,128)(2,1)} %collective-permute-done.9, bf16[104,1280]{1,0:T(8,128)(2,1)} %collective-permute-done.8), kind=kLoop, calls=%fused_computation.8 | loop fusion | flops 1038336 | bytes 1038336 | tf_op jit(solution)/shard_map/concatenate | solution.py:198
  50.3 2.6 %pad_maximum_fusion.1 = bf16[312,2496]{1,0:T(8,128)(2,1)} fusion(bf16[104,2496]{1,0:T(8,128)(2,1)} %collective-permute-done.6, bf16[104,2496]{1,0:T(8,128)(2,1)} %collective-permute-done.5, bf16[104,2496]{1,0:T(8,128)(2,1)} %collective-permute-done.1), kind=kLoop, calls=%fused_computation.3 | loop fusion | flops 4672512 | bytes 3115008 | tf_op jit(solution)/shard_map/concatenate | solution.py:256
  53.0 5.7 %collective-permute-done.7 = bf16[104,2496]{1,0:T(8,128)(2,1)} collective-permute-done((bf16[104,2496]{1,0:T(8,128)(2,1)}, bf16[104,2496]{1,0:T(8,128)(2,1)}, u32[]{:S(2)}, u32[]{:S(2)}) %collective-permute-start.7) | collective-permute-done | bytes 519200 | tf_op jit(solution)/shard_map/ppermute | solution.py:190
  58.6 2.0 %collective-permute-done.14 = bf16[104,2496]{1,0:T(8,128)(2,1)} collective-permute-done((bf16[104,2496]{1,0:T(8,128)(2,1)}, bf16[104,2496]{1,0:T(8,128)(2,1)}, u32[]{:S(2)}, u32[]{:S(2)}) %collective-permute-start.14) | collective-permute-done | bytes 519200 | tf_op jit(solution)/shard_map/ppermute | solution.py:193
  60.6 0.4 collective-permute-done.15
  61.0 1.4 %collective-permute-start.16 = (bf16[104,2496]{1,0:T(8,128)(2,1)}, bf16[104,2496]{1,0:T(8,128)(2,1)}, u32[]{:S(2)}, u32[]{:S(2)}) collective-permute-start(bf16[104,2496]{1,0:T(8,128)(2,1)} %collective-permute-done.7), channel_id=1, source_target_pairs={{0,2},{2,0},{4,6},{6,4},{8,10},{10,8},{12,14},{14,12},{16,18},{18,... | collective-permute-start | bytes 1557512 | tf_op jit(solution)/shard_map/ppermute | solution.py:193
  62.4 0.5 collective-permute-start.17
  62.9 0.6 collective-permute-start.13
  63.5 1.6 %pad_maximum_fusion.2 = bf16[312,2496]{1,0:T(8,128)(2,1)S(1)} fusion(bf16[104,2496]{1,0:T(8,128)(2,1)} %collective-permute-done.15, bf16[104,2496]{1,0:T(8,128)(2,1)} %collective-permute-done.14, bf16[104,2496]{1,0:T(8,128)(2,1)} %collective-permute-done.4), kind=kLoop, calls=%fused_computation.4 | loop fusion | flops 4672512 | bytes 3115008 | tf_op jit(solution)/shard_map/concatenate | solution.py:256
  65.1 0.1 copy-done.9
  65.3 0.2 pad_maximum_fusion
  65.5 1.9 %shard_map.120 = bf16[16,104,512]{2,1,0:T(8,128)(2,1)S(1)} custom-call(s32[1]{0:T(128)} %bitcast.3.index_ref, s32[16]{0:T(128)S(1)} %fusion.10.order_ref, bf16[16,104,1]{2,1,0:T(8,128)(2,1)S(1)} %copy.19.gain_ref, bf16[832,512]{1,0:T(8,128)(2,1)S(1)} %bitcast.28, bf16[832,512]{1,0:T(8,128)(2,1)S(1)} %collective-permute-done.10.refs_1_, ...), custom_call_target="tpu_custom_call" | custom-call | flops 1000 | bytes 1000 | tf_op jit(solution)/shard_map/pallas_call | solution.py:164
  67.5 1.6 %fusion.15 = f32[512,2496]{0,1:T(8,128)S(1)} fusion(bf16[416,512]{1,0:T(8,128)(2,1)S(1)} %bitcast.29, bf16[416,2496]{1,0:T(8,128)(2,1)S(1)} %pad_maximum_fusion), kind=kOutput, calls=%fused_computation.45 | convolution fusion | flops 1063256064 | bytes 7614464 | tf_op jit(solution)/shard_map/dot_general | solution.py:260
  69.1 1.6 %convolution_add_fusion = f32[512,2496]{0,1:T(8,128)S(1)} fusion(f32[512,2496]{0,1:T(8,128)S(1)} %fusion.15, bf16[312,512]{1,0:T(8,128)(2,1)S(1)} %bitcast.33, bf16[312,2496]{1,0:T(8,128)(2,1)S(1)} %copy-done.4), kind=kOutput, calls=%fused_computation.1 | convolution fusion | flops 798720000 | bytes 12100608 | tf_op jit(solution)/shard_map/dot_general | solution.py:260
  70.7 4.3 %collective-permute-done.13 = bf16[104,2496]{1,0:T(8,128)(2,1)} collective-permute-done((bf16[104,2496]{1,0:T(8,128)(2,1)S(1)}, bf16[104,2496]{1,0:T(8,128)(2,1)}, u32[]{:S(2)}, u32[]{:S(2)}) %collective-permute-start.13) | collective-permute-done | bytes 519200 | tf_op jit(solution)/shard_map/ppermute | solution.py:190
  75.0 1.5 %fusion.16 = f32[512,2496]{0,1:T(8,128)S(1)} fusion(bf16[312,512]{1,0:T(8,128)(2,1)S(1)} %bitcast.32, bf16[312,2496]{1,0:T(8,128)(2,1)S(1)} %pad_maximum_fusion.2), kind=kOutput, calls=%fused_computation.46 | convolution fusion | flops 797442048 | bytes 6988800 | tf_op jit(solution)/shard_map/dot_general | solution.py:260
  76.5 1.3 %add.65 = f32[512,2496]{0,1:T(8,128)S(1)} add(f32[512,2496]{0,1:T(8,128)S(1)} %convolution_add_fusion, f32[512,2496]{0,1:T(8,128)S(1)} %fusion.16) | non-fusion elementwise | flops 1277952 | bytes 15335424 | tf_op jit(solution)/shard_map/add | solution.py:266
  77.8 0.3 collective-permute-start.18
  78.1 1.5 %pad_maximum_fusion.3 = bf16[312,2496]{1,0:T(8,128)(2,1)S(1)} fusion(bf16[104,2496]{1,0:T(8,128)(2,1)} %collective-permute-done.17, bf16[104,2496]{1,0:T(8,128)(2,1)} %collective-permute-done.16, bf16[104,2496]{1,0:T(8,128)(2,1)} %collective-permute-done.7), kind=kLoop, calls=%fused_computation.5 | loop fusion | flops 4672512 | bytes 3115008 | tf_op jit(solution)/shard_map/concatenate | solution.py:256
  79.6 1.0 %slice.34 = bf16[104,1216]{1,0:T(8,128)(2,1)S(1)} slice(bf16[104,2496]{1,0:T(8,128)(2,1)} %collective-permute-done.16), slice={[0:104], [1280:2496]} | slice | bytes 505856 | tf_op jit(solution)/shard_map/slice | solution.py:197
  80.6 1.0 %slice.33 = bf16[104,1280]{1,0:T(8,128)(2,1)S(1)} slice(bf16[104,2496]{1,0:T(8,128)(2,1)} %collective-permute-done.17), slice={[0:104], [0:1280]} | slice | bytes 532480 | tf_op jit(solution)/shard_map/slice | solution.py:196
  81.5 1.5 %collective-permute-start.20 = (bf16[104,1216]{1,0:T(8,128)(2,1)S(1)}, bf16[104,1216]{1,0:T(8,128)(2,1)S(1)}, u32[]{:S(2)}, u32[]{:S(2)}) collective-permute-start(bf16[104,1216]{1,0:T(8,128)(2,1)S(1)} %slice.34), channel_id=1, source_target_pairs={{0,4},{2,6},{4,0},{6,2},{8,12},{10,14},{12,8},{14,10},{16,20},{18,... | collective-permute-start | bytes 758792 | tf_op jit(solution)/shard_map/ppermute | solution.py:197
  83.1 1.5 %collective-permute-start.19 = (bf16[104,1280]{1,0:T(8,128)(2,1)S(1)}, bf16[104,1280]{1,0:T(8,128)(2,1)S(1)}, u32[]{:S(2)}, u32[]{:S(2)}) collective-permute-start(bf16[104,1280]{1,0:T(8,128)(2,1)S(1)} %slice.33), channel_id=1, source_target_pairs={{0,2},{2,0},{4,6},{6,4},{8,10},{10,8},{12,14},{14,12},{16,18},{18,... | collective-permute-start | bytes 798728 | tf_op jit(solution)/shard_map/ppermute | solution.py:196
  84.6 1.5 %fusion.17 = f32[512,2496]{0,1:T(8,128)S(1)} fusion(bf16[312,512]{1,0:T(8,128)(2,1)S(1)} %bitcast.31, bf16[312,2496]{1,0:T(8,128)(2,1)S(1)} %pad_maximum_fusion.3), kind=kOutput, calls=%fused_computation.47 | convolution fusion | flops 797442048 | bytes 6988800 | tf_op jit(solution)/shard_map/dot_general | solution.py:260
  86.1 1.3 %add.66 = f32[512,2496]{0,1:T(8,128)S(1)} add(f32[512,2496]{0,1:T(8,128)S(1)} %add.65, f32[512,2496]{0,1:T(8,128)S(1)} %fusion.17) | non-fusion elementwise | flops 1277952 | bytes 15335424 | tf_op jit(solution)/shard_map/add | solution.py:274
  87.4 0.6 collective-permute-done.20
  88.0 1.5 %collective-permute-done.19 = bf16[104,1280]{1,0:T(8,128)(2,1)S(1)} collective-permute-done((bf16[104,1280]{1,0:T(8,128)(2,1)S(1)}, bf16[104,1280]{1,0:T(8,128)(2,1)S(1)}, u32[]{:S(2)}, u32[]{:S(2)}) %collective-permute-start.19) | collective-permute-done | bytes 266272 | tf_op jit(solution)/shard_map/ppermute | solution.py:196
  89.5 1.2 %maximum_maximum_fusion = bf16[312,2496]{1,0:T(8,128)(2,1)S(1)} fusion(bf16[104,1216]{1,0:T(8,128)(2,1)S(1)} %collective-permute-done.20, bf16[104,1280]{1,0:T(8,128)(2,1)S(1)} %collective-permute-done.19, bf16[104,2496]{1,0:T(8,128)(2,1)S(1)} %collective-permute-done.18, bf16[104,2496]{1,0:T(8,128)(2,1)} %collective-permute-done.13), kind=kLoop, calls=%fused_computation.6 | loop fusion | flops 6230016 | bytes 3115008 | tf_op jit(solution)/shard_map/concatenate | solution.py:256
  90.7 1.5 %fusion.18 = f32[512,2496]{0,1:T(8,128)S(1)} fusion(bf16[312,512]{1,0:T(8,128)(2,1)S(1)} %bitcast.30, bf16[312,2496]{1,0:T(8,128)(2,1)S(1)} %maximum_maximum_fusion), kind=kOutput, calls=%fused_computation.48 | convolution fusion | flops 797442048 | bytes 6988800 | tf_op jit(solution)/shard_map/dot_general | solution.py:260
  92.2 2.8 %select_convert_fusion = bf16[512,2496]{0,1:T(8,128)(2,1)} fusion(f32[512,2496]{0,1:T(8,128)S(1)} %add.66, f32[512,2496]{0,1:T(8,128)S(1)} %fusion.18, pred[512]{0:T(512)(128)(4,1)S(1)} %fusion.8), kind=kLoop, calls=%fused_computation | loop fusion | flops 3833856 | bytes 12780032 | tf_op jit(solution)/shard_map/convert_element_type | solution.py:286
  (45 shorter events, 0.6 us)
Async XLA Ops:
  0.0 20.3 %collective-permute-start.1 = (bf16[104,2496]{1,0:T(8,128)(2,1)}, bf16[104,2496]{1,0:T(8,128)(2,1)}, u32[]{:S(2)}, u32[]{:S(2)}) collective-permute-start(bf16[104,2496]{1,0:T(8,128)(2,1)} %param.16), channel_id=1, source_target_pairs={{0,8},{2,10},{4,12},{6,14},{8,24},{10,26},{12,28},{14,30},{16,0},{... | collective-permute-start | bytes 1557512 | tf_op jit(solution)/shard_map/ppermute | solution.py:190
  3.0 17.3 %collective-permute-start.2 = (bf16[104,2496]{1,0:T(8,128)(2,1)}, bf16[104,2496]{1,0:T(8,128)(2,1)S(1)}, u32[]{:S(2)}, u32[]{:S(2)}) collective-permute-start(bf16[104,2496]{1,0:T(8,128)(2,1)} %param.16), channel_id=1, source_target_pairs={{0,2},{2,0},{4,6},{6,4},{8,10},{10,8},{12,14},{14,12},{16,18},{18,... | collective-permute-start | bytes 1557512 | tf_op jit(solution)/shard_map/ppermute | solution.py:193
  4.5 15.8 %collective-permute-start.3 = (bf16[104,2496]{1,0:T(8,128)(2,1)}, bf16[104,2496]{1,0:T(8,128)(2,1)S(1)}, u32[]{:S(2)}, u32[]{:S(2)}) collective-permute-start(bf16[104,2496]{1,0:T(8,128)(2,1)} %param.16), channel_id=1, source_target_pairs={{0,4},{2,6},{4,0},{6,2},{8,12},{10,14},{12,8},{14,10},{16,20},{18,... | collective-permute-start | bytes 1557512 | tf_op jit(solution)/shard_map/ppermute | solution.py:193
  6.0 1.1 %copy-start.1 = (bf16[448,832]{1,0:T(8,128)(2,1)S(1)}, bf16[448,832]{1,0:T(8,128)(2,1)}, u32[]{:S(2)}) copy-start(bf16[448,832]{1,0:T(8,128)(2,1)} %patches_ref.3) | copy-start | bytes 2236420
  7.5 3.9 %collective-permute-start = (f32[448,256]{1,0:T(8,128)S(1)}, f32[448,256]{1,0:T(8,128)S(1)}, u32[]{:S(2)}, u32[]{:S(2)}) collective-permute-start(f32[448,256]{1,0:T(8,128)S(1)} %shard_map.118.refs_0_), channel_id=1, source_target_pairs={{0,1},{1,0},{2,3},{3,2},{4,5},{5,4},{6,7},{7,6},{8,9},{9,8},{10,11... | collective-permute-start | bytes 1376264 | tf_op jit(solution)/shard_map/ppermute | solution.py:26
  11.3 4.1 %copy-start = (bf16[4,832,1664]{2,1,0:T(8,128)(2,1)S(1)}, bf16[4,832,1664]{2,1,0:T(8,128)(2,1)}, u32[]{:S(2)}) copy-start(bf16[4,832,1664]{2,1,0:T(8,128)(2,1)} %refs_2_.1) | copy-start | bytes 33226756
  15.5 1.1 %copy-start.2 = (bf16[448,832]{1,0:T(8,128)(2,1)S(1)}, bf16[448,832]{1,0:T(8,128)(2,1)}, u32[]{:S(2)}) copy-start(bf16[448,832]{1,0:T(8,128)(2,1)} %patches_ref.3) | copy-start | bytes 2236420
  16.6 5.2 %copy-start.10 = (s32[2]{0:T(128)S(1)}, s32[2]{0:T(128)}, u32[]{:S(2)}) copy-start(s32[2]{0:T(128)} %param.18) | copy-start | bytes 28
  20.3 17.1 %copy-start.3 = (bf16[512,832]{0,1:T(8,128)(2,1)S(1)}, bf16[512,832]{0,1:T(8,128)(2,1)}, u32[]{:S(2)}) copy-start(bf16[512,832]{0,1:T(8,128)(2,1)} %param.14) | copy-start | bytes 2555908
  20.3 17.0 %copy-start.5 = (bf16[104,2496]{1,0:T(8,128)(2,1)}, bf16[104,2496]{1,0:T(8,128)(2,1)S(1)}, u32[]{:S(2)}) copy-start(bf16[104,2496]{1,0:T(8,128)(2,1)S(1)} %collective-permute-done.2) | copy-start | bytes 1557508
  20.3 28.9 %copy-start.7 = (bf16[104,2496]{1,0:T(8,128)(2,1)}, bf16[104,2496]{1,0:T(8,128)(2,1)S(1)}, u32[]{:S(2)}) copy-start(bf16[104,2496]{1,0:T(8,128)(2,1)S(1)} %collective-permute-done.3) | copy-start | bytes 1557508
  21.3 7.4 %collective-permute-start.11 = (f32[112,832]{1,0:T(8,128)}, f32[112,832]{1,0:T(8,128)S(1)}, u32[]{:S(2)}, u32[]{:S(2)}) collective-permute-start(f32[112,832]{1,0:T(8,128)} %constant_dynamic-slice_fusion.1), channel_id=1, source_target_pairs={{0,1},{1,0},{2,3},{3,2},{4,5},{5,4},{6,7},{7,6},{8,9},{9,8},{10,11... | collective-permute-start | bytes 1118216 | tf_op jit(solution)/shard_map/ppermute | solution.py:26
  21.9 15.4 %collective-permute-start.4 = (bf16[104,2496]{1,0:T(8,128)(2,1)}, bf16[104,2496]{1,0:T(8,128)(2,1)}, u32[]{:S(2)}, u32[]{:S(2)}) collective-permute-start(bf16[104,2496]{1,0:T(8,128)(2,1)} %collective-permute-done.1), channel_id=1, source_target_pairs={{0,8},{2,10},{4,12},{6,14},{8,24},{10,26},{12,28},{14,30},{16,0},{... | collective-permute-start | bytes 1557512 | tf_op jit(solution)/shard_map/ppermute | solution.py:190
  24.5 15.9 %collective-permute-start.5 = (bf16[104,2496]{1,0:T(8,128)(2,1)}, bf16[104,2496]{1,0:T(8,128)(2,1)}, u32[]{:S(2)}, u32[]{:S(2)}) collective-permute-start(bf16[104,2496]{1,0:T(8,128)(2,1)} %collective-permute-done.1), channel_id=1, source_target_pairs={{0,2},{2,0},{4,6},{6,4},{8,10},{10,8},{12,14},{14,12},{16,18},{18,... | collective-permute-start | bytes 1557512 | tf_op jit(solution)/shard_map/ppermute | solution.py:193
  25.1 17.6 %collective-permute-start.6 = (bf16[104,2496]{1,0:T(8,128)(2,1)}, bf16[104,2496]{1,0:T(8,128)(2,1)}, u32[]{:S(2)}, u32[]{:S(2)}) collective-permute-start(bf16[104,2496]{1,0:T(8,128)(2,1)} %collective-permute-done.1), channel_id=1, source_target_pairs={{0,4},{2,6},{4,0},{6,2},{8,12},{10,14},{12,8},{14,10},{16,20},{18,... | collective-permute-start | bytes 1557512 | tf_op jit(solution)/shard_map/ppermute | solution.py:193
  26.3 22.3 %collective-permute-start.9 = (bf16[104,1216]{1,0:T(8,128)(2,1)}, bf16[104,1216]{1,0:T(8,128)(2,1)}, u32[]{:S(2)}, u32[]{:S(2)}) collective-permute-start(bf16[104,1216]{1,0:T(8,128)(2,1)} %slice.28), channel_id=1, source_target_pairs={{0,4},{2,6},{4,0},{6,2},{8,12},{10,14},{12,8},{14,10},{16,20},{18,... | collective-permute-start | bytes 758792 | tf_op jit(solution)/shard_map/ppermute | solution.py:197
  28.7 20.6 %collective-permute-start.8 = (bf16[104,1280]{1,0:T(8,128)(2,1)}, bf16[104,1280]{1,0:T(8,128)(2,1)}, u32[]{:S(2)}, u32[]{:S(2)}) collective-permute-start(bf16[104,1280]{1,0:T(8,128)(2,1)} %slice.27), channel_id=1, source_target_pairs={{0,2},{2,0},{4,6},{6,4},{8,10},{10,8},{12,14},{14,12},{16,18},{18,... | collective-permute-start | bytes 798728 | tf_op jit(solution)/shard_map/ppermute | solution.py:196
  31.5 31.9 %all-to-all-start = ((bf16[16,16,896]{2,1,0:T(8,128)(2,1)}), bf16[16,16,896]{2,1,0:T(8,128)(2,1)S(1)}, u32[]{:S(2)}, u32[]{:S(2)}) async-start(bf16[16,16,896]{2,1,0:T(8,128)(2,1)} %bitcast.5), calls=%async_computation | async-start | bytes 917504 | tf_op jit(solution)/shard_map/all_to_all | solution.py:238
  37.3 28.1 %collective-permute-start.10 = (bf16[832,512]{1,0:T(8,128)(2,1)S(1)}, bf16[832,512]{1,0:T(8,128)(2,1)S(1)}, u32[]{:S(2)}, u32[]{:S(2)}) collective-permute-start(bf16[832,512]{1,0:T(8,128)(2,1)S(1)} %bitcast.27), channel_id=1, source_target_pairs={{0,1},{1,0},{2,3},{3,2},{4,5},{5,4},{6,7},{7,6},{8,9},{9,8},{10,11... | collective-permute-start | bytes 2555912 | tf_op jit(solution)/shard_map/ppermute | solution.py:26
  42.7 15.9 %collective-permute-start.7 = (bf16[104,2496]{1,0:T(8,128)(2,1)}, bf16[104,2496]{1,0:T(8,128)(2,1)}, u32[]{:S(2)}, u32[]{:S(2)}) collective-permute-start(bf16[104,2496]{1,0:T(8,128)(2,1)} %collective-permute-done.4), channel_id=1, source_target_pairs={{0,8},{2,10},{4,12},{6,14},{8,24},{10,26},{12,28},{14,30},{16,0},{... | collective-permute-start | bytes 1557512 | tf_op jit(solution)/shard_map/ppermute | solution.py:190
  42.7 17.9 %collective-permute-start.14 = (bf16[104,2496]{1,0:T(8,128)(2,1)}, bf16[104,2496]{1,0:T(8,128)(2,1)}, u32[]{:S(2)}, u32[]{:S(2)}) collective-permute-start(bf16[104,2496]{1,0:T(8,128)(2,1)} %collective-permute-done.4), channel_id=1, source_target_pairs={{0,2},{2,0},{4,6},{6,4},{8,10},{10,8},{12,14},{14,12},{16,18},{18,... | collective-permute-start | bytes 1557512 | tf_op jit(solution)/shard_map/ppermute | solution.py:193
  48.6 12.4 %collective-permute-start.15 = (bf16[104,2496]{1,0:T(8,128)(2,1)}, bf16[104,2496]{1,0:T(8,128)(2,1)}, u32[]{:S(2)}, u32[]{:S(2)}) collective-permute-start(bf16[104,2496]{1,0:T(8,128)(2,1)} %collective-permute-done.4), channel_id=1, source_target_pairs={{0,4},{2,6},{4,0},{6,2},{8,12},{10,14},{12,8},{14,10},{16,20},{18,... | collective-permute-start | bytes 1557512 | tf_op jit(solution)/shard_map/ppermute | solution.py:193
  61.0 16.8 %collective-permute-start.16 = (bf16[104,2496]{1,0:T(8,128)(2,1)}, bf16[104,2496]{1,0:T(8,128)(2,1)}, u32[]{:S(2)}, u32[]{:S(2)}) collective-permute-start(bf16[104,2496]{1,0:T(8,128)(2,1)} %collective-permute-done.7), channel_id=1, source_target_pairs={{0,2},{2,0},{4,6},{6,4},{8,10},{10,8},{12,14},{14,12},{16,18},{18,... | collective-permute-start | bytes 1557512 | tf_op jit(solution)/shard_map/ppermute | solution.py:193
  62.4 15.4 %collective-permute-start.17 = (bf16[104,2496]{1,0:T(8,128)(2,1)}, bf16[104,2496]{1,0:T(8,128)(2,1)}, u32[]{:S(2)}, u32[]{:S(2)}) collective-permute-start(bf16[104,2496]{1,0:T(8,128)(2,1)} %collective-permute-done.7), channel_id=1, source_target_pairs={{0,4},{2,6},{4,0},{6,2},{8,12},{10,14},{12,8},{14,10},{16,20},{18,... | collective-permute-start | bytes 1557512 | tf_op jit(solution)/shard_map/ppermute | solution.py:193
  62.9 12.1 %collective-permute-start.13 = (bf16[104,2496]{1,0:T(8,128)(2,1)S(1)}, bf16[104,2496]{1,0:T(8,128)(2,1)}, u32[]{:S(2)}, u32[]{:S(2)}) collective-permute-start(bf16[104,2496]{1,0:T(8,128)(2,1)S(1)} %pad_maximum_fusion.4), channel_id=1, source_target_pairs={{0,8},{2,10},{4,12},{6,14},{8,24},{10,26},{12,28},{14,30},{16,0},{... | collective-permute-start | bytes 1557512 | tf_op jit(solution)/shard_map/ppermute | solution.py:190
  63.4 1.7 %copy-start.6 = (bf16[104,2496]{1,0:T(8,128)(2,1)S(1)}, bf16[104,2496]{1,0:T(8,128)(2,1)}, u32[]{:S(2)}) copy-start(bf16[104,2496]{1,0:T(8,128)(2,1)} %copy-done.5) | copy-start | bytes 1557508
  63.4 1.7 %copy-start.8 = (bf16[104,2496]{1,0:T(8,128)(2,1)S(1)}, bf16[104,2496]{1,0:T(8,128)(2,1)}, u32[]{:S(2)}) copy-start(bf16[104,2496]{1,0:T(8,128)(2,1)} %copy-done.7) | copy-start | bytes 1557508
  63.4 1.8 %copy-start.9 = (bf16[104,2496]{1,0:T(8,128)(2,1)S(1)}, bf16[104,2496]{1,0:T(8,128)(2,1)}, u32[]{:S(2)}) copy-start(bf16[104,2496]{1,0:T(8,128)(2,1)} %param.16) | copy-start | bytes 1557508
  63.4 2.0 %collective-permute-start.12 = (bf16[256,896]{1,0:T(8,128)(2,1)S(1)}, bf16[256,896]{1,0:T(8,128)(2,1)S(1)}, u32[]{:S(2)}, u32[]{:S(2)}) collective-permute-start(bf16[256,896]{1,0:T(8,128)(2,1)S(1)} %bitcast.25), channel_id=1, source_target_pairs={{0,1},{1,0},{2,3},{3,2},{4,5},{5,4},{6,7},{7,6},{8,9},{9,8},{10,11... | collective-permute-start | bytes 1376264 | tf_op jit(solution)/shard_map/ppermute | solution.py:26
  67.5 1.6 %copy-start.4 = (bf16[312,2496]{1,0:T(8,128)(2,1)S(1)}, bf16[312,2496]{1,0:T(8,128)(2,1)}, u32[]{:S(2)}) copy-start(bf16[312,2496]{1,0:T(8,128)(2,1)} %pad_maximum_fusion.1) | copy-start | bytes 4672516
  77.8 11.7 %collective-permute-start.18 = (bf16[104,2496]{1,0:T(8,128)(2,1)}, bf16[104,2496]{1,0:T(8,128)(2,1)S(1)}, u32[]{:S(2)}, u32[]{:S(2)}) collective-permute-start(bf16[104,2496]{1,0:T(8,128)(2,1)} %collective-permute-done.13), channel_id=1, source_target_pairs={{0,8},{2,10},{4,12},{6,14},{8,24},{10,26},{12,28},{14,30},{16,0},{... | collective-permute-start | bytes 1557512 | tf_op jit(solution)/shard_map/ppermute | solution.py:190
  81.5 6.5 %collective-permute-start.20 = (bf16[104,1216]{1,0:T(8,128)(2,1)S(1)}, bf16[104,1216]{1,0:T(8,128)(2,1)S(1)}, u32[]{:S(2)}, u32[]{:S(2)}) collective-permute-start(bf16[104,1216]{1,0:T(8,128)(2,1)S(1)} %slice.34), channel_id=1, source_target_pairs={{0,4},{2,6},{4,0},{6,2},{8,12},{10,14},{12,8},{14,10},{16,20},{18,... | collective-permute-start | bytes 758792 | tf_op jit(solution)/shard_map/ppermute | solution.py:197
  83.1 6.4 %collective-permute-start.19 = (bf16[104,1280]{1,0:T(8,128)(2,1)S(1)}, bf16[104,1280]{1,0:T(8,128)(2,1)S(1)}, u32[]{:S(2)}, u32[]{:S(2)}) collective-permute-start(bf16[104,1280]{1,0:T(8,128)(2,1)S(1)} %slice.33), channel_id=1, source_target_pairs={{0,2},{2,0},{4,6},{6,4},{8,10},{10,8},{12,14},{14,12},{16,18},{18,... | collective-permute-start | bytes 798728 | tf_op jit(solution)/shard_map/ppermute | solution.py:196

commit v12 on v10

--- a/solution.py
+++ b/solution.py
@@ -73,7 +73,7 @@
         in_specs=[vmem],
         out_specs=vmem,
         compiler_params=pltpu.CompilerParams(vmem_limit_bytes=VMEM),
-        cost_estimate=LIGHT,
+        cost_estimate=pl.CostEstimate(flops=1000, bytes_accessed=16 << 20, transcendentals=0),
     )(patches)
 
 
@@ -195,13 +195,12 @@
     def to_corner(by_x, by_y):
         left = lax.ppermute(by_y[:, :cut], "req", x_perm)
         right = lax.ppermute(by_x[:, cut:], "req", y_perm)
-        return jnp.concatenate([left, right], axis=1)
-
+        return left, right
+
+    stats_own, qkv_weight = tie(row_stats(patches), qkv_weight)
     held = [qkv_weight]
     held.append(along_line(held[0]))
     sides = [to_sides(held[0])]
-    corners = []
-    stats_own = row_stats(patches)
     stats = [stats_own] + [tp_shift(stats_own, n_tp, d) for d in range(1, n_tp)]
     gain_bias = jnp.stack([ln_gain, ln_bias])
     text_turned = text_rows.T
@@ -225,7 +224,7 @@
     )
     held.append(along_line(held[1]))
     sides.append(to_sides(held[1]))
-    corners.append(to_corner(*sides[0]))
+    halves = to_corner(*sides[0])
     merged = tp_scatter_sum(partial_value, n_tp, 1).astype(jnp.bfloat16)
     padding = (-width - 2) % 128
     payload = jnp.concatenate(
@@ -239,9 +238,11 @@
         outgoing.reshape(n_req, IMG_CAP, -1), "req", split_axis=0, concat_axis=0
     ).reshape(slot_count, -1)
 
-    held[2], sides[1] = tie(held[2], sides[1])
+    held[2], sides[1], halves = tie(held[2], sides[1], halves)
     held.append(along_line(held[2]))
     sides.append(to_sides(held[2]))
+    arrived, halves = tie(arrived, halves)
+    corners = [jnp.concatenate(halves, axis=1)]
     corners.append(along_line(corners[0]))
     images = [arrived] + [tp_shift(arrived, n_tp, d) for d in range(1, n_tp)]
     blocks = combine(tp_index, order, texts, images, gain_column)
@@ -251,9 +252,6 @@
     for step in range(4, lines):
         held.append(along_line(held[step - 1]))
         sides.append(to_sides(held[step]))
-    blocks, corners[1] = tie(blocks, corners[1])
-    for step in range(2, lines - 1):
-        corners.append(along_line(corners[step - 1]))
 
     def product(first, weights):
         weight = jnp.concatenate(weights, axis=0)
@@ -265,11 +263,14 @@
         )
 
     total = product(0, [held[0], *sides[0], corners[0]])
+    total, corners[1] = tie(total, corners[1])
+    for step in range(2, lines - 1):
+        corners.append(along_line(corners[step - 1]))
     for step in range(1, lines - 1):
         (total,) = tie(total + product(step * 3 + 1, [held[step], *sides[step]]))
 
     total, sides[-1] = tie(total, sides[-1])
-    corners.append(to_corner(*sides[-1]))
+    corners.append(jnp.concatenate(to_corner(*sides[-1]), axis=1))
     (total,) = tie(total + product(lines * 3 - 2, [held[-1], *sides[-1]]))
 
     position = me * row_count + jnp.arange(row_count, dtype=jnp.int32)

time: 104 us -> 110 us (1.058)
  other arithmetic: 13.5 us -> 17.1 us
  starting transfers between devices: 20.9 us -> 24.4 us
    ppermute x2, waiting for transfers between devices: 13.3 us -> 1.24 us  [to_corner(): left = lax.ppermute(by_y[:, :cut], 'req', x_perm)]
    ppermute x2, waiting for transfers between devices: 3.14 us -> 15.2 us  [to_corner(): right = lax.ppermute(by_x[:, cut:], 'req', y_perm)]
    add x0 -> x2, other arithmetic: none -> 2.51 us  [shards(): total, = tie(total + product(step * 3 + 1, [held[step], *sides[step]]))]
    ppermute x4, starting transfers between devices: 2.98 us -> 4.63 us  [to_sides(): lax.ppermute(block, 'req', x_perm)]
    ppermute x2, starting transfers between devices: 1.98 us -> 3.1 us  [to_corner(): right = lax.ppermute(by_x[:, cut:], 'req', y_perm)]
    unnamed x15 -> x23, local copies, waits for them, and re-layouts: 8.13 us -> 8.14 us
  transfers between devices with their start and end apart: 22 -> 22, of which waited for: 8 -> 7; matrix products, arithmetic and copies ran while one was open for 24% -> 27% of each run, Pallas kernels for 6% -> 5%
where the time goes in v12:
time: 110 us
  waiting for transfers between devices  37.1 us (34%)
  starting transfers between devices  24.4 us (22%)
  other arithmetic  17.1 us (16%)
  local copies, waits for them, and re-layouts  15.9 us (14%)
  matrix products  8.76 us (8%)
  Pallas kernels  5.8 us (5%)
    ppermute x5, waiting for transfers between devices, along_line(): return lax.ppermute(block, 'req', line_perm)  20 us
    ppermute x2, waiting for transfers between devices, to_corner(): right = lax.ppermute(by_x[:, cut:], 'req', y_perm)  15.2 us
    concatenate x5, other arithmetic, product(): weight = jnp.concatenate(weights, axis=0)  8.31 us
    unnamed x23, local copies, waits for them, and re-layouts  8.14 us
    dot_general x5, matrix products, product(): lax.dot_general(source, weight, (((0,), (0,)), ((), ())), preferred_eleme...  7.7 us
    ppermute x5, starting transfers between devices, along_line(): return lax.ppermute(block, 'req', line_perm)  7.03 us
    ppermute x4, starting transfers between devices, to_sides(): lax.ppermute(block, 'req', x_perm)  4.63 us
    pallas_call x1, Pallas kernels, merge(): pl.pallas_call(body, out_shape=jax.ShapeDtypeStruct((tokens, features), j...  3.64 us
  transfers between devices with their start and end apart: 22, of which 7 were waited for; matrix products, arithmetic and copies ran while one was open for 27% of the time, Pallas kernels for 5%

profile of v12, /device:TPU:0, one launch (start us, length us, event | category | flops | bytes accessed | tf_op | source)
XLA Modules:
  0.0 109.5 jit_solution(1955012862373972542)
XLA Ops:
  0.0 1.1 %copy-done.1 = bf16[448,832]{1,0:T(8,128)(2,1)S(1)} copy-done((bf16[448,832]{1,0:T(8,128)(2,1)S(1)}, bf16[448,832]{1,0:T(8,128)(2,1)}, u32[]{:S(2)}) %copy-start.1) | copy-done | bytes 745496
  1.1 0.3 shard_map.118.refs_0_
  1.4 3.1 %collective-permute-start.1 = (bf16[104,2496]{1,0:T(8,128)(2,1)}, bf16[104,2496]{1,0:T(8,128)(2,1)S(1)}, u32[]{:S(2)}, u32[]{:S(2)}) collective-permute-start(bf16[104,2496]{1,0:T(8,128)(2,1)} %param.16), channel_id=1, source_target_pairs={{0,8},{2,10},{4,12},{6,14},{8,24},{10,26},{12,28},{14,30},{16,0},{... | collective-permute-start | bytes 1557512 | tf_op jit(solution)/shard_map/ppermute | solution.py:190
  4.5 1.5 %collective-permute-start.2 = (bf16[104,2496]{1,0:T(8,128)(2,1)}, bf16[104,2496]{1,0:T(8,128)(2,1)S(1)}, u32[]{:S(2)}, u32[]{:S(2)}) collective-permute-start(bf16[104,2496]{1,0:T(8,128)(2,1)} %param.16), channel_id=1, source_target_pairs={{0,2},{2,0},{4,6},{6,4},{8,10},{10,8},{12,14},{14,12},{16,18},{18,... | collective-permute-start | bytes 1557512 | tf_op jit(solution)/shard_map/ppermute | solution.py:193
  6.0 1.5 %collective-permute-start.3 = (bf16[104,2496]{1,0:T(8,128)(2,1)}, bf16[104,2496]{1,0:T(8,128)(2,1)S(1)}, u32[]{:S(2)}, u32[]{:S(2)}) collective-permute-start(bf16[104,2496]{1,0:T(8,128)(2,1)} %param.16), channel_id=1, source_target_pairs={{0,4},{2,6},{4,0},{6,2},{8,12},{10,14},{12,8},{14,10},{16,20},{18,... | collective-permute-start | bytes 1557512 | tf_op jit(solution)/shard_map/ppermute | solution.py:193
  7.5 0.7 convert_bitcast_fusion.1
  8.2 0.7 fusion.10.order_ref
  8.9 0.7 stack.22
  9.6 0.7 stack.21
  10.3 0.8 reshape.52
  11.1 0.2 convert_reduce_fusion
  11.3 4.1 %copy-done = bf16[4,832,1664]{2,1,0:T(8,128)(2,1)S(1)} copy-done((bf16[4,832,1664]{2,1,0:T(8,128)(2,1)S(1)}, bf16[4,832,1664]{2,1,0:T(8,128)(2,1)}, u32[]{:S(2)}) %copy-start) | copy-done | bytes 11075608
  15.5 1.1 %copy-done.2 = bf16[448,832]{1,0:T(8,128)(2,1)S(1)} copy-done((bf16[448,832]{1,0:T(8,128)(2,1)S(1)}, bf16[448,832]{1,0:T(8,128)(2,1)}, u32[]{:S(2)}) %copy-start.2) | copy-done | bytes 745496
  16.6 3.6 %shard_map.119 = f32[112,1664]{1,0:T(8,128)S(1)} custom-call(bf16[448,832]{1,0:T(8,128)(2,1)S(1)} %copy-done.2, bf16[2,832]{1,0:T(2,128)(2,1)S(1)} %pad_maximum_fusion.4.gain_bias_ref, f32[448,256]{1,0:T(8,128)S(1)} %shard_map.118.refs_0_, f32[448,256]{1,0:T(8,128)S(1)} %collective-permute-done.refs_1_, bf16[4,832,1664]{2,1,0:T(8,128)(2,1)S(1)} %copy-done), custom_call_target="tpu_custom_call" | custom-call | flops 1000 | bytes 1000 | tf_op jit(solution)/shard_map/pallas_call | solution.py:112
  20.3 0.9 constant_dynamic-slice_fusion.1
  21.2 0.5 collective-permute-start.4
  21.8 2.6 %collective-permute-start.5 = (bf16[104,2496]{1,0:T(8,128)(2,1)S(1)}, bf16[104,2496]{1,0:T(8,128)(2,1)}, u32[]{:S(2)}, u32[]{:S(2)}) collective-permute-start(bf16[104,2496]{1,0:T(8,128)(2,1)S(1)} %collective-permute-done.1), channel_id=1, source_target_pairs={{0,8},{2,10},{4,12},{6,14},{8,24},{10,26},{12,28},{14,30},{16,0},{... | collective-permute-start | bytes 1557512 | tf_op jit(solution)/shard_map/ppermute | solution.py:190
  24.4 0.5 collective-permute-start.6
  24.9 0.5 collective-permute-start.7
  25.6 0.1 copy.18
  25.7 0.7 slice.27
  26.4 1.5 %collective-permute-start.8 = (bf16[104,1280]{1,0:T(8,128)(2,1)}, bf16[104,1280]{1,0:T(8,128)(2,1)}, u32[]{:S(2)}, u32[]{:S(2)}) collective-permute-start(bf16[104,1280]{1,0:T(8,128)(2,1)} %slice.27), channel_id=1, source_target_pairs={{0,2},{2,0},{4,6},{6,4},{8,10},{10,8},{12,14},{14,12},{16,18},{18,... | collective-permute-start | bytes 798728 | tf_op jit(solution)/shard_map/ppermute | solution.py:196
  27.9 0.7 slice.28
  28.6 1.5 %collective-permute-start.9 = (bf16[104,1216]{1,0:T(8,128)(2,1)}, bf16[104,1216]{1,0:T(8,128)(2,1)S(1)}, u32[]{:S(2)}, u32[]{:S(2)}) collective-permute-start(bf16[104,1216]{1,0:T(8,128)(2,1)} %slice.28), channel_id=1, source_target_pairs={{0,4},{2,6},{4,0},{6,2},{8,12},{10,14},{12,8},{14,10},{16,20},{18,... | collective-permute-start | bytes 758792 | tf_op jit(solution)/shard_map/ppermute | solution.py:197
  30.2 1.2 %add_convert_fusion = bf16[112,832]{1,0:T(8,128)(2,1)S(1)} fusion(f32[112,832]{1,0:T(8,128)} %collective-permute-done.4, f32[112,1664]{1,0:T(8,128)S(1)} %shard_map.119, s32[]{:T(128)S(6)} %select_n.26), kind=kLoop, calls=%fused_computation.7 | loop fusion | flops 186368 | bytes 931844 | tf_op jit(solution)/shard_map/convert_element_type | solution.py:228
  31.3 1.1 convolution_convert_fusion
  32.4 3.6 %all-to-all-start = ((bf16[16,16,896]{2,1,0:T(8,128)(2,1)}), bf16[16,16,896]{2,1,0:T(8,128)(2,1)S(1)}, u32[]{:S(2)}, u32[]{:S(2)}) async-start(bf16[16,16,896]{2,1,0:T(8,128)(2,1)} %bitcast.3), calls=%async_computation | async-start | bytes 917504 | tf_op jit(solution)/shard_map/all_to_all | solution.py:237
  36.0 12.4 %collective-permute-done.9 = bf16[104,1216]{1,0:T(8,128)(2,1)S(1)} collective-permute-done((bf16[104,1216]{1,0:T(8,128)(2,1)}, bf16[104,1216]{1,0:T(8,128)(2,1)S(1)}, u32[]{:S(2)}, u32[]{:S(2)}) %collective-permute-start.9) | collective-permute-done | bytes 252960 | tf_op jit(solution)/shard_map/ppermute | solution.py:197
  48.4 0.7 copy-done.9
  49.2 0.5 collective-permute-start.13
  49.7 1.5 %collective-permute-start.14 = (bf16[104,2496]{1,0:T(8,128)(2,1)}, bf16[104,2496]{1,0:T(8,128)(2,1)}, u32[]{:S(2)}, u32[]{:S(2)}) collective-permute-start(bf16[104,2496]{1,0:T(8,128)(2,1)} %collective-permute-done.5), channel_id=1, source_target_pairs={{0,2},{2,0},{4,6},{6,4},{8,10},{10,8},{12,14},{14,12},{16,18},{18,... | collective-permute-start | bytes 1557512 | tf_op jit(solution)/shard_map/ppermute | solution.py:193
  51.2 0.6 collective-permute-start.15
  51.8 0.3 copy.19.gain_ref
  52.1 2.6 %pad_maximum_fusion.1 = bf16[312,2496]{1,0:T(8,128)(2,1)} fusion(bf16[104,2496]{1,0:T(8,128)(2,1)} %collective-permute-done.7, bf16[104,2496]{1,0:T(8,128)(2,1)} %collective-permute-done.6, bf16[104,2496]{1,0:T(8,128)(2,1)} %copy-done.8), kind=kLoop, calls=%fused_computation.2 | loop fusion | flops 4672512 | bytes 3115008 | tf_op jit(solution)/shard_map/concatenate | solution.py:257
  54.7 10.2 %collective-permute-done.13 = bf16[104,2496]{1,0:T(8,128)(2,1)} collective-permute-done((bf16[104,2496]{1,0:T(8,128)(2,1)}, bf16[104,2496]{1,0:T(8,128)(2,1)}, u32[]{:S(2)}, u32[]{:S(2)}) %collective-permute-start.13) | collective-permute-done | bytes 519200 | tf_op jit(solution)/shard_map/ppermute | solution.py:190
  64.9 0.7 collective-permute-done.15
  65.6 1.1 collective-permute-start.16
  66.7 0.5 collective-permute-start.17
  67.3 2.7 %pad_maximum_fusion.2 = bf16[312,2496]{1,0:T(8,128)(2,1)} fusion(bf16[104,2496]{1,0:T(8,128)(2,1)} %collective-permute-done.15, bf16[104,2496]{1,0:T(8,128)(2,1)} %collective-permute-done.14, bf16[104,2496]{1,0:T(8,128)(2,1)} %collective-permute-done.5), kind=kLoop, calls=%fused_computation.3 | loop fusion | flops 4672512 | bytes 3115008 | tf_op jit(solution)/shard_map/concatenate | solution.py:257
  69.9 1.0 constant_dynamic-update-slice_fusion.1
  70.9 1.0 constant_dynamic-update-slice_fusion
  71.9 0.6 collective-permute-start.12
  72.5 1.5 %pad_maximum_fusion = bf16[416,2496]{1,0:T(8,128)(2,1)S(1)} fusion(bf16[104,2496]{1,0:T(8,128)(2,1)S(1)} %constant_dynamic-update-slice_fusion, bf16[104,2496]{1,0:T(8,128)(2,1)} %copy-done.7, bf16[104,2496]{1,0:T(8,128)(2,1)} %copy-done.6, bf16[104,2496]{1,0:T(8,128)(2,1)} %param.16), kind=kLoop, calls=%fused_computation.1 | loop fusion | flops 8306688 | bytes 4153344 | tf_op jit(solution)/shard_map/concatenate | solution.py:257
  74.0 1.9 %shard_map.120 = bf16[16,104,512]{2,1,0:T(8,128)(2,1)S(1)} custom-call(s32[1]{0:T(128)} %bitcast.5.index_ref, s32[16]{0:T(128)S(1)} %fusion.10.order_ref, bf16[16,104,1]{2,1,0:T(8,128)(2,1)S(1)} %copy.19.gain_ref, bf16[832,512]{1,0:T(8,128)(2,1)S(1)} %bitcast.28, bf16[832,512]{1,0:T(8,128)(2,1)S(1)} %collective-permute-done.10.refs_1_, ...), custom_call_target="tpu_custom_call" | custom-call | flops 1000 | bytes 1000 | tf_op jit(solution)/shard_map/pallas_call | solution.py:164
  75.9 0.1 fusion.14
  76.1 1.5 %fusion.16 = f32[512,2496]{0,1:T(8,128)S(1)} fusion(bf16[312,512]{1,0:T(8,128)(2,1)S(1)} %bitcast.33, bf16[312,2496]{1,0:T(8,128)(2,1)S(1)} %copy-done.4), kind=kOutput, calls=%fused_computation.46 | convolution fusion | flops 797442048 | bytes 6988800 | tf_op jit(solution)/shard_map/dot_general | solution.py:261
  77.6 1.5 %fusion.17 = f32[512,2496]{0,1:T(8,128)S(1)} fusion(bf16[312,512]{1,0:T(8,128)(2,1)S(1)} %bitcast.32, bf16[312,2496]{1,0:T(8,128)(2,1)S(1)} %copy-done.5), kind=kOutput, calls=%fused_computation.47 | convolution fusion | flops 797442048 | bytes 6988800 | tf_op jit(solution)/shard_map/dot_general | solution.py:261
  79.2 1.6 %fusion.15 = f32[512,2496]{0,1:T(8,128)S(1)} fusion(bf16[416,512]{1,0:T(8,128)(2,1)S(1)} %bitcast.29, bf16[416,2496]{1,0:T(8,128)(2,1)S(1)} %pad_maximum_fusion), kind=kOutput, calls=%fused_computation.45 | convolution fusion | flops 1063256064 | bytes 7614464 | tf_op jit(solution)/shard_map/dot_general | solution.py:261
  80.7 6.8 %collective-permute-done.12 = bf16[104,2496]{1,0:T(8,128)(2,1)S(1)} collective-permute-done((bf16[104,2496]{1,0:T(8,128)(2,1)S(1)}, bf16[104,2496]{1,0:T(8,128)(2,1)S(1)}, u32[]{:S(2)}, u32[]{:S(2)}) %collective-permute-start.12) | collective-permute-done | bytes 519200 | tf_op jit(solution)/shard_map/ppermute | solution.py:190
  87.5 1.3 %add.64 = f32[512,2496]{0,1:T(8,128)S(1)} add(f32[512,2496]{0,1:T(8,128)S(1)} %fusion.15, f32[512,2496]{0,1:T(8,128)S(1)} %fusion.16) | non-fusion elementwise | flops 1277952 | bytes 15335424 | tf_op jit(solution)/shard_map/add | solution.py:270
  88.8 1.3 %add.65 = f32[512,2496]{0,1:T(8,128)S(1)} add(f32[512,2496]{0,1:T(8,128)S(1)} %add.64, f32[512,2496]{0,1:T(8,128)S(1)} %fusion.17) | non-fusion elementwise | flops 1277952 | bytes 15335424 | tf_op jit(solution)/shard_map/add | solution.py:270
  90.1 0.3 collective-permute-start.18
  90.4 1.3 %pad_maximum_fusion.3 = bf16[312,2496]{1,0:T(8,128)(2,1)S(1)} fusion(bf16[104,2496]{1,0:T(8,128)(2,1)} %collective-permute-done.17, bf16[104,2496]{1,0:T(8,128)(2,1)S(1)} %collective-permute-done.16, bf16[104,2496]{1,0:T(8,128)(2,1)} %collective-permute-done.13), kind=kLoop, calls=%fused_computation.4 | loop fusion | flops 4672512 | bytes 3115008 | tf_op jit(solution)/shard_map/concatenate | solution.py:257
  91.7 1.0 slice.33
  92.7 1.6 %collective-permute-start.20 = (bf16[104,1216]{1,0:T(8,128)(2,1)S(1)}, bf16[104,1216]{1,0:T(8,128)(2,1)S(1)}, u32[]{:S(2)}, u32[]{:S(2)}) collective-permute-start(bf16[104,1216]{1,0:T(8,128)(2,1)S(1)} %slice.34), channel_id=1, source_target_pairs={{0,4},{2,6},{4,0},{6,2},{8,12},{10,14},{12,8},{14,10},{16,20},{18,... | collective-permute-start | bytes 758792 | tf_op jit(solution)/shard_map/ppermute | solution.py:197
  94.3 0.9 collective-permute-start.19
  95.2 1.5 %fusion.18 = f32[512,2496]{0,1:T(8,128)S(1)} fusion(bf16[312,512]{1,0:T(8,128)(2,1)S(1)} %bitcast.31, bf16[312,2496]{1,0:T(8,128)(2,1)S(1)} %pad_maximum_fusion.3), kind=kOutput, calls=%fused_computation.48 | convolution fusion | flops 797442048 | bytes 6988800 | tf_op jit(solution)/shard_map/dot_general | solution.py:261
  96.8 1.3 %add.66 = f32[512,2496]{0,1:T(8,128)S(1)} add(f32[512,2496]{0,1:T(8,128)S(1)} %add.65, f32[512,2496]{0,1:T(8,128)S(1)} %fusion.18) | non-fusion elementwise | flops 1277952 | bytes 15335424 | tf_op jit(solution)/shard_map/add | solution.py:274
  98.0 2.8 %collective-permute-done.20 = bf16[104,1216]{1,0:T(8,128)(2,1)S(1)} collective-permute-done((bf16[104,1216]{1,0:T(8,128)(2,1)S(1)}, bf16[104,1216]{1,0:T(8,128)(2,1)S(1)}, u32[]{:S(2)}, u32[]{:S(2)}) %collective-permute-start.20) | collective-permute-done | bytes 252960 | tf_op jit(solution)/shard_map/ppermute | solution.py:197
  100.8 1.2 %collective-permute-done.19 = bf16[104,1280]{1,0:T(8,128)(2,1)S(1)} collective-permute-done((bf16[104,1280]{1,0:T(8,128)(2,1)S(1)}, bf16[104,1280]{1,0:T(8,128)(2,1)S(1)}, u32[]{:S(2)}, u32[]{:S(2)}) %collective-permute-start.19) | collective-permute-done | bytes 266272 | tf_op jit(solution)/shard_map/ppermute | solution.py:196
  102.0 3.0 %collective-permute-done.18 = bf16[104,2496]{1,0:T(8,128)(2,1)S(1)} collective-permute-done((bf16[104,2496]{1,0:T(8,128)(2,1)S(1)}, bf16[104,2496]{1,0:T(8,128)(2,1)S(1)}, u32[]{:S(2)}, u32[]{:S(2)}) %collective-permute-start.18) | collective-permute-done | bytes 519200 | tf_op jit(solution)/shard_map/ppermute | solution.py:190
  105.0 0.1 maximum_maximum_fusion
  105.1 1.5 %fusion.19 = f32[512,2496]{0,1:T(8,128)S(1)} fusion(bf16[312,512]{1,0:T(8,128)(2,1)S(1)} %bitcast.30, bf16[312,2496]{1,0:T(8,128)(2,1)S(1)} %maximum_maximum_fusion), kind=kOutput, calls=%fused_computation.49 | convolution fusion | flops 797442048 | bytes 6988800 | tf_op jit(solution)/shard_map/dot_general | solution.py:261
  106.6 2.9 %select_convert_fusion = bf16[512,2496]{0,1:T(8,128)(2,1)} fusion(f32[512,2496]{0,1:T(8,128)S(1)} %add.66, f32[512,2496]{0,1:T(8,128)S(1)} %fusion.19, pred[512]{0:T(512)(128)(4,1)S(1)} %fusion.8), kind=kLoop, calls=%fused_computation | loop fusion | flops 3833856 | bytes 12780032 | tf_op jit(solution)/shard_map/convert_element_type | solution.py:286
  (47 shorter events, 0.4 us)
Async XLA Ops:
  0.0 1.1 %copy-start.1 = (bf16[448,832]{1,0:T(8,128)(2,1)S(1)}, bf16[448,832]{1,0:T(8,128)(2,1)}, u32[]{:S(2)}) copy-start(bf16[448,832]{1,0:T(8,128)(2,1)} %patches_ref.3) | copy-start | bytes 2236420
  1.4 18.8 %collective-permute-start.1 = (bf16[104,2496]{1,0:T(8,128)(2,1)}, bf16[104,2496]{1,0:T(8,128)(2,1)S(1)}, u32[]{:S(2)}, u32[]{:S(2)}) collective-permute-start(bf16[104,2496]{1,0:T(8,128)(2,1)} %param.16), channel_id=1, source_target_pairs={{0,8},{2,10},{4,12},{6,14},{8,24},{10,26},{12,28},{14,30},{16,0},{... | collective-permute-start | bytes 1557512 | tf_op jit(solution)/shard_map/ppermute | solution.py:190
  4.5 15.8 %collective-permute-start.2 = (bf16[104,2496]{1,0:T(8,128)(2,1)}, bf16[104,2496]{1,0:T(8,128)(2,1)S(1)}, u32[]{:S(2)}, u32[]{:S(2)}) collective-permute-start(bf16[104,2496]{1,0:T(8,128)(2,1)} %param.16), channel_id=1, source_target_pairs={{0,2},{2,0},{4,6},{6,4},{8,10},{10,8},{12,14},{14,12},{16,18},{18,... | collective-permute-start | bytes 1557512 | tf_op jit(solution)/shard_map/ppermute | solution.py:193
  6.0 14.3 %collective-permute-start.3 = (bf16[104,2496]{1,0:T(8,128)(2,1)}, bf16[104,2496]{1,0:T(8,128)(2,1)S(1)}, u32[]{:S(2)}, u32[]{:S(2)}) collective-permute-start(bf16[104,2496]{1,0:T(8,128)(2,1)} %param.16), channel_id=1, source_target_pairs={{0,4},{2,6},{4,0},{6,2},{8,12},{10,14},{12,8},{14,10},{16,20},{18,... | collective-permute-start | bytes 1557512 | tf_op jit(solution)/shard_map/ppermute | solution.py:193
  7.5 3.8 %collective-permute-start = (f32[448,256]{1,0:T(8,128)S(1)}, f32[448,256]{1,0:T(8,128)S(1)}, u32[]{:S(2)}, u32[]{:S(2)}) collective-permute-start(f32[448,256]{1,0:T(8,128)S(1)} %shard_map.118.refs_0_), channel_id=1, source_target_pairs={{0,1},{1,0},{2,3},{3,2},{4,5},{5,4},{6,7},{7,6},{8,9},{9,8},{10,11... | collective-permute-start | bytes 1376264 | tf_op jit(solution)/shard_map/ppermute | solution.py:26
  11.3 4.1 %copy-start = (bf16[4,832,1664]{2,1,0:T(8,128)(2,1)S(1)}, bf16[4,832,1664]{2,1,0:T(8,128)(2,1)}, u32[]{:S(2)}) copy-start(bf16[4,832,1664]{2,1,0:T(8,128)(2,1)} %refs_2_.1) | copy-start | bytes 33226756
  15.5 1.1 %copy-start.2 = (bf16[448,832]{1,0:T(8,128)(2,1)S(1)}, bf16[448,832]{1,0:T(8,128)(2,1)}, u32[]{:S(2)}) copy-start(bf16[448,832]{1,0:T(8,128)(2,1)} %patches_ref.3) | copy-start | bytes 2236420
  16.6 8.8 %copy-start.10 = (s32[2]{0:T(128)S(1)}, s32[2]{0:T(128)}, u32[]{:S(2)}) copy-start(s32[2]{0:T(128)} %param.18) | copy-start | bytes 28
  20.2 28.9 %copy-start.3 = (bf16[512,832]{0,1:T(8,128)(2,1)S(1)}, bf16[512,832]{0,1:T(8,128)(2,1)}, u32[]{:S(2)}) copy-start(bf16[512,832]{0,1:T(8,128)(2,1)} %param.14) | copy-start | bytes 2555908
  20.3 31.5 %copy-start.8 = (bf16[104,2496]{1,0:T(8,128)(2,1)}, bf16[104,2496]{1,0:T(8,128)(2,1)S(1)}, u32[]{:S(2)}) copy-start(bf16[104,2496]{1,0:T(8,128)(2,1)S(1)} %collective-permute-done.1) | copy-start | bytes 1557508
  20.3 12.1 %copy-start.6 = (bf16[104,2496]{1,0:T(8,128)(2,1)}, bf16[104,2496]{1,0:T(8,128)(2,1)S(1)}, u32[]{:S(2)}) copy-start(bf16[104,2496]{1,0:T(8,128)(2,1)S(1)} %collective-permute-done.2) | copy-start | bytes 1557508
  20.3 28.1 %copy-start.7 = (bf16[104,2496]{1,0:T(8,128)(2,1)}, bf16[104,2496]{1,0:T(8,128)(2,1)S(1)}, u32[]{:S(2)}) copy-start(bf16[104,2496]{1,0:T(8,128)(2,1)S(1)} %collective-permute-done.3) | copy-start | bytes 1557508
  21.2 7.4 %collective-permute-start.4 = (f32[112,832]{1,0:T(8,128)}, f32[112,832]{1,0:T(8,128)}, u32[]{:S(2)}, u32[]{:S(2)}) collective-permute-start(f32[112,832]{1,0:T(8,128)} %constant_dynamic-slice_fusion.1), channel_id=1, source_target_pairs={{0,1},{1,0},{2,3},{3,2},{4,5},{5,4},{6,7},{7,6},{8,9},{9,8},{10,11... | collective-permute-start | bytes 1118216 | tf_op jit(solution)/shard_map/ppermute | solution.py:26
  21.8 27.4 %collective-permute-start.5 = (bf16[104,2496]{1,0:T(8,128)(2,1)S(1)}, bf16[104,2496]{1,0:T(8,128)(2,1)}, u32[]{:S(2)}, u32[]{:S(2)}) collective-permute-start(bf16[104,2496]{1,0:T(8,128)(2,1)S(1)} %collective-permute-done.1), channel_id=1, source_target_pairs={{0,8},{2,10},{4,12},{6,14},{8,24},{10,26},{12,28},{14,30},{16,0},{... | collective-permute-start | bytes 1557512 | tf_op jit(solution)/shard_map/ppermute | solution.py:190
  24.4 24.8 %collective-permute-start.6 = (bf16[104,2496]{1,0:T(8,128)(2,1)S(1)}, bf16[104,2496]{1,0:T(8,128)(2,1)}, u32[]{:S(2)}, u32[]{:S(2)}) collective-permute-start(bf16[104,2496]{1,0:T(8,128)(2,1)S(1)} %collective-permute-done.1), channel_id=1, source_target_pairs={{0,2},{2,0},{4,6},{6,4},{8,10},{10,8},{12,14},{14,12},{16,18},{18,... | collective-permute-start | bytes 1557512 | tf_op jit(solution)/shard_map/ppermute | solution.py:193
  24.9 24.3 %collective-permute-start.7 = (bf16[104,2496]{1,0:T(8,128)(2,1)S(1)}, bf16[104,2496]{1,0:T(8,128)(2,1)}, u32[]{:S(2)}, u32[]{:S(2)}) collective-permute-start(bf16[104,2496]{1,0:T(8,128)(2,1)S(1)} %collective-permute-done.1), channel_id=1, source_target_pairs={{0,4},{2,6},{4,0},{6,2},{8,12},{10,14},{12,8},{14,10},{16,20},{18,... | collective-permute-start | bytes 1557512 | tf_op jit(solution)/shard_map/ppermute | solution.py:193
  26.4 22.7 %collective-permute-start.8 = (bf16[104,1280]{1,0:T(8,128)(2,1)}, bf16[104,1280]{1,0:T(8,128)(2,1)}, u32[]{:S(2)}, u32[]{:S(2)}) collective-permute-start(bf16[104,1280]{1,0:T(8,128)(2,1)} %slice.27), channel_id=1, source_target_pairs={{0,2},{2,0},{4,6},{6,4},{8,10},{10,8},{12,14},{14,12},{16,18},{18,... | collective-permute-start | bytes 798728 | tf_op jit(solution)/shard_map/ppermute | solution.py:196
  28.6 19.8 %collective-permute-start.9 = (bf16[104,1216]{1,0:T(8,128)(2,1)}, bf16[104,1216]{1,0:T(8,128)(2,1)S(1)}, u32[]{:S(2)}, u32[]{:S(2)}) collective-permute-start(bf16[104,1216]{1,0:T(8,128)(2,1)} %slice.28), channel_id=1, source_target_pairs={{0,4},{2,6},{4,0},{6,2},{8,12},{10,14},{12,8},{14,10},{16,20},{18,... | collective-permute-start | bytes 758792 | tf_op jit(solution)/shard_map/ppermute | solution.py:197
  32.4 37.5 %all-to-all-start = ((bf16[16,16,896]{2,1,0:T(8,128)(2,1)}), bf16[16,16,896]{2,1,0:T(8,128)(2,1)S(1)}, u32[]{:S(2)}, u32[]{:S(2)}) async-start(bf16[16,16,896]{2,1,0:T(8,128)(2,1)} %bitcast.3), calls=%async_computation | async-start | bytes 917504 | tf_op jit(solution)/shard_map/all_to_all | solution.py:237
  48.4 0.7 copy-start.9
  49.1 24.9 %collective-permute-start.10 = (bf16[832,512]{1,0:T(8,128)(2,1)S(1)}, bf16[832,512]{1,0:T(8,128)(2,1)S(1)}, u32[]{:S(2)}, u32[]{:S(2)}) collective-permute-start(bf16[832,512]{1,0:T(8,128)(2,1)S(1)} %bitcast.27), channel_id=1, source_target_pairs={{0,1},{1,0},{2,3},{3,2},{4,5},{5,4},{6,7},{7,6},{8,9},{9,8},{10,11... | collective-permute-start | bytes 2555912 | tf_op jit(solution)/shard_map/ppermute | solution.py:26
  49.2 15.8 %collective-permute-start.13 = (bf16[104,2496]{1,0:T(8,128)(2,1)}, bf16[104,2496]{1,0:T(8,128)(2,1)}, u32[]{:S(2)}, u32[]{:S(2)}) collective-permute-start(bf16[104,2496]{1,0:T(8,128)(2,1)} %collective-permute-done.5), channel_id=1, source_target_pairs={{0,8},{2,10},{4,12},{6,14},{8,24},{10,26},{12,28},{14,30},{16,0},{... | collective-permute-start | bytes 1557512 | tf_op jit(solution)/shard_map/ppermute | solution.py:190
  49.7 15.3 %collective-permute-start.14 = (bf16[104,2496]{1,0:T(8,128)(2,1)}, bf16[104,2496]{1,0:T(8,128)(2,1)}, u32[]{:S(2)}, u32[]{:S(2)}) collective-permute-start(bf16[104,2496]{1,0:T(8,128)(2,1)} %collective-permute-done.5), channel_id=1, source_target_pairs={{0,2},{2,0},{4,6},{6,4},{8,10},{10,8},{12,14},{14,12},{16,18},{18,... | collective-permute-start | bytes 1557512 | tf_op jit(solution)/shard_map/ppermute | solution.py:193
  51.2 14.5 %collective-permute-start.15 = (bf16[104,2496]{1,0:T(8,128)(2,1)}, bf16[104,2496]{1,0:T(8,128)(2,1)}, u32[]{:S(2)}, u32[]{:S(2)}) collective-permute-start(bf16[104,2496]{1,0:T(8,128)(2,1)} %collective-permute-done.5), channel_id=1, source_target_pairs={{0,4},{2,6},{4,0},{6,2},{8,12},{10,14},{12,8},{14,10},{16,20},{18,... | collective-permute-start | bytes 1557512 | tf_op jit(solution)/shard_map/ppermute | solution.py:193
  65.6 24.4 %collective-permute-start.16 = (bf16[104,2496]{1,0:T(8,128)(2,1)}, bf16[104,2496]{1,0:T(8,128)(2,1)S(1)}, u32[]{:S(2)}, u32[]{:S(2)}) collective-permute-start(bf16[104,2496]{1,0:T(8,128)(2,1)} %collective-permute-done.13), channel_id=1, source_target_pairs={{0,2},{2,0},{4,6},{6,4},{8,10},{10,8},{12,14},{14,12},{16,18},{18,... | collective-permute-start | bytes 1557512 | tf_op jit(solution)/shard_map/ppermute | solution.py:193
  66.7 23.3 %collective-permute-start.17 = (bf16[104,2496]{1,0:T(8,128)(2,1)}, bf16[104,2496]{1,0:T(8,128)(2,1)}, u32[]{:S(2)}, u32[]{:S(2)}) collective-permute-start(bf16[104,2496]{1,0:T(8,128)(2,1)} %collective-permute-done.13), channel_id=1, source_target_pairs={{0,4},{2,6},{4,0},{6,2},{8,12},{10,14},{12,8},{14,10},{16,20},{18,... | collective-permute-start | bytes 1557512 | tf_op jit(solution)/shard_map/ppermute | solution.py:193
  69.9 4.1 %collective-permute-start.11 = (bf16[256,896]{1,0:T(8,128)(2,1)S(1)}, bf16[256,896]{1,0:T(8,128)(2,1)S(1)}, u32[]{:S(2)}, u32[]{:S(2)}) collective-permute-start(bf16[256,896]{1,0:T(8,128)(2,1)S(1)} %bitcast.25), channel_id=1, source_target_pairs={{0,1},{1,0},{2,3},{3,2},{4,5},{5,4},{6,7},{7,6},{8,9},{9,8},{10,11... | collective-permute-start | bytes 1376264 | tf_op jit(solution)/shard_map/ppermute | solution.py:26
  71.9 15.6 %collective-permute-start.12 = (bf16[104,2496]{1,0:T(8,128)(2,1)S(1)}, bf16[104,2496]{1,0:T(8,128)(2,1)S(1)}, u32[]{:S(2)}, u32[]{:S(2)}) collective-permute-start(bf16[104,2496]{1,0:T(8,128)(2,1)S(1)} %constant_dynamic-update-slice_fusion), channel_id=1, source_target_pairs={{0,8},{2,10},{4,12},{6,14},{8,24},{10,26},{12,28},{14,30},{16,0},{... | collective-permute-start | bytes 1557512 | tf_op jit(solution)/shard_map/ppermute | solution.py:190
  74.0 2.0 %copy-start.4 = (bf16[312,2496]{1,0:T(8,128)(2,1)S(1)}, bf16[312,2496]{1,0:T(8,128)(2,1)}, u32[]{:S(2)}) copy-start(bf16[312,2496]{1,0:T(8,128)(2,1)} %pad_maximum_fusion.1) | copy-start | bytes 4672516
  76.0 1.6 %copy-start.5 = (bf16[312,2496]{1,0:T(8,128)(2,1)S(1)}, bf16[312,2496]{1,0:T(8,128)(2,1)}, u32[]{:S(2)}) copy-start(bf16[312,2496]{1,0:T(8,128)(2,1)} %pad_maximum_fusion.2) | copy-start | bytes 4672516
  90.1 14.9 %collective-permute-start.18 = (bf16[104,2496]{1,0:T(8,128)(2,1)S(1)}, bf16[104,2496]{1,0:T(8,128)(2,1)S(1)}, u32[]{:S(2)}, u32[]{:S(2)}) collective-permute-start(bf16[104,2496]{1,0:T(8,128)(2,1)S(1)} %collective-permute-done.12), channel_id=1, source_target_pairs={{0,8},{2,10},{4,12},{6,14},{8,24},{10,26},{12,28},{14,30},{16,0},{... | collective-permute-start | bytes 1557512 | tf_op jit(solution)/shard_map/ppermute | solution.py:190
  92.7 8.1 %collective-permute-start.20 = (bf16[104,1216]{1,0:T(8,128)(2,1)S(1)}, bf16[104,1216]{1,0:T(8,128)(2,1)S(1)}, u32[]{:S(2)}, u32[]{:S(2)}) collective-permute-start(bf16[104,1216]{1,0:T(8,128)(2,1)S(1)} %slice.34), channel_id=1, source_target_pairs={{0,4},{2,6},{4,0},{6,2},{8,12},{10,14},{12,8},{14,10},{16,20},{18,... | collective-permute-start | bytes 758792 | tf_op jit(solution)/shard_map/ppermute | solution.py:197
  94.3 7.7 %collective-permute-start.19 = (bf16[104,1280]{1,0:T(8,128)(2,1)S(1)}, bf16[104,1280]{1,0:T(8,128)(2,1)S(1)}, u32[]{:S(2)}, u32[]{:S(2)}) collective-permute-start(bf16[104,1280]{1,0:T(8,128)(2,1)S(1)} %slice.33), channel_id=1, source_target_pairs={{0,2},{2,0},{4,6},{6,4},{8,10},{10,8},{12,14},{14,12},{16,18},{18,... | collective-permute-start | bytes 798728 | tf_op jit(solution)/shard_map/ppermute | solution.py:196

commit v13 on v12

--- a/solution.py
+++ b/solution.py
@@ -197,7 +197,7 @@
         right = lax.ppermute(by_x[:, cut:], "req", y_perm)
         return left, right
 
-    stats_own, qkv_weight = tie(row_stats(patches), qkv_weight)
+    stats_own = row_stats(patches)
     held = [qkv_weight]
     held.append(along_line(held[0]))
     sides = [to_sides(held[0])]
@@ -217,15 +217,22 @@
     code_cols = jnp.stack([lax.div(code, 256), lax.rem(code, 256)], axis=1).astype(jnp.bfloat16)
     gain_column = norm_gain.reshape(n_req, rows, 1)
 
-    partial_value = merge(patches, stats, gain_bias, merge_weight)
-
-    partial_value, held[1], sides[0], gain_column, order, slot, code_cols = tie(
-        partial_value, held[1], sides[0], gain_column, order, slot, code_cols
+
+    stats, held[1], sides[0], gain_bias, gain_column, order, slot, code_cols = tie(
+        stats, held[1], sides[0], gain_bias, gain_column, order, slot, code_cols
     )
     held.append(along_line(held[1]))
     sides.append(to_sides(held[1]))
     halves = to_corner(*sides[0])
+    partial_value = merge(patches, stats, gain_bias, merge_weight)
+
+    partial_value, held[2], sides[1] = tie(partial_value, held[2], sides[1])
+    held.append(along_line(held[2]))
+    sides.append(to_sides(held[2]))
     merged = tp_scatter_sum(partial_value, n_tp, 1).astype(jnp.bfloat16)
+    merged, halves = tie(merged, halves)
+    corners = [jnp.concatenate(halves, axis=1)]
+    corners.append(along_line(corners[0]))
     padding = (-width - 2) % 128
     payload = jnp.concatenate(
         [merged, code_cols, jnp.zeros((token_count, padding), jnp.bfloat16)], axis=1
@@ -238,40 +245,37 @@
         outgoing.reshape(n_req, IMG_CAP, -1), "req", split_axis=0, concat_axis=0
     ).reshape(slot_count, -1)
 
-    held[2], sides[1], halves = tie(held[2], sides[1], halves)
-    held.append(along_line(held[2]))
-    sides.append(to_sides(held[2]))
-    arrived, halves = tie(arrived, halves)
-    corners = [jnp.concatenate(halves, axis=1)]
-    corners.append(along_line(corners[0]))
+    held[3], sides[2] = tie(held[3], sides[2])
+    sides.append(to_sides(held[3]))
     images = [arrived] + [tp_shift(arrived, n_tp, d) for d in range(1, n_tp)]
     blocks = combine(tp_index, order, texts, images, gain_column)
-
-    held[3], sides[2] = tie(held[3], sides[2])
-    sides.append(to_sides(held[3]))
+    blocks, corners[1] = tie(blocks, corners[1])
     for step in range(4, lines):
         held.append(along_line(held[step - 1]))
         sides.append(to_sides(held[step]))
-
-    def product(first, weights):
+    for step in range(2, lines - 1):
+        corners.append(along_line(corners[step - 1]))
+
+    def add_product(total, first, weights):
         weight = jnp.concatenate(weights, axis=0)
         count = weight.shape[0]
         source = blocks[first : first + count // rows].reshape(count, row_count)
-        weight, source = tie(weight, source)
-        return lax.dot_general(
+        if total is None:
+            weight, source = tie(weight, source)
+        else:
+            weight, source, total = tie(weight, source, total)
+        part = lax.dot_general(
             source, weight, (((0,), (0,)), ((), ())), preferred_element_type=jnp.float32
         )
-
-    total = product(0, [held[0], *sides[0], corners[0]])
-    total, corners[1] = tie(total, corners[1])
-    for step in range(2, lines - 1):
-        corners.append(along_line(corners[step - 1]))
-    for step in range(1, lines - 1):
-        (total,) = tie(total + product(step * 3 + 1, [held[step], *sides[step]]))
+        return part if total is None else total + part
+
+    total = add_product(None, 0, [held[0], *sides[0], corners[0]])
+    total = add_product(total, 4, [held[1], *sides[1]])
 
     total, sides[-1] = tie(total, sides[-1])
     corners.append(jnp.concatenate(to_corner(*sides[-1]), axis=1))
-    (total,) = tie(total + product(lines * 3 - 2, [held[-1], *sides[-1]]))
+    for step in range(2, lines):
+        total = add_product(total, step * 3 + 1, [held[step], *sides[step]])
 
     position = me * row_count + jnp.arange(row_count, dtype=jnp.int32)
     request_ids = jnp.arange(text_len.shape[0], dtype=jnp.int32)
@@ -282,7 +286,7 @@
         axis=1,
     )
     keep = lax.rem(position, SEQ) < limits
-    total += product(lines * 3 + 1, corners[1:])
+    total = add_product(total, lines * 3 + 1, corners[1:])
     return jnp.where(keep[:, None], total, 0.0).astype(jnp.bfloat16)
 
 

time: 110 us -> 118 us (1.073)
  other arithmetic: 17.1 us -> 9.14 us
  waiting for transfers between devices: 37.1 us -> 44.7 us
  starting transfers between devices: 24.4 us -> 30.5 us
  matrix products: 8.76 us -> 10.3 us
    ppermute x2, waiting for transfers between devices: 15.2 us -> 7.75 us  [to_corner(): right = lax.ppermute(by_x[:, cut:], 'req', y_perm)]
    ppermute x5, waiting for transfers between devices: 20 us -> 26.9 us  [along_line(): return lax.ppermute(block, 'req', line_perm)]
    ppermute x4, waiting for transfers between devices: 0.01 us -> 4.42 us  [to_sides(): lax.ppermute(block, 'req', x_perm)]
    add x3 -> x0, other arithmetic: 3.78 us -> none  [the longest x2 2.51 us: shards(): total, = tie(total + product(step * 3 + 1, [held[step], *sides[step]]))]
    ppermute x4, starting transfers between devices: 3.16 us -> 6.18 us  [to_sides(): lax.ppermute(block, 'req', y_perm)]
    convert_element_type x1 -> x0, other arithmetic: 2.88 us -> none  [shards(): return jnp.where(keep[:, None], total, 0.0).astype(jnp.bfloat16)]
    ppermute x5, starting transfers between devices: 7.03 us -> 9.9 us  [along_line(): return lax.ppermute(block, 'req', line_perm)]
    ppermute x4, waiting for transfers between devices: 0.72 us -> 2.7 us  [to_sides(): lax.ppermute(block, 'req', y_perm)]
  transfers between devices with their start and end apart: 22 -> 22, of which waited for: 7 -> 14; matrix products, arithmetic and copies ran while one was open for 27% -> 19% of each run, Pallas kernels for 5% -> 5%
where the time goes in v13:
time: 118 us; the launch traced here: 117 us
  waiting for transfers between devices  44.7 us (38%)
  starting transfers between devices  30.5 us (26%)
  local copies, waits for them, and re-layouts  16.6 us (14%)
  matrix products  10.3 us (9%)
  other arithmetic  9.14 us (8%)
  Pallas kernels  5.77 us (5%)
    ppermute x5, waiting for transfers between devices, along_line(): return lax.ppermute(block, 'req', line_perm)  26.9 us
    ppermute x5, starting transfers between devices, along_line(): return lax.ppermute(block, 'req', line_perm)  9.9 us
    dot_general x5, matrix products, add_product(): lax.dot_general(source, weight, (((0,), (0,)), ((), ())), preferred_eleme...  9.22 us
    unnamed x15, local copies, waits for them, and re-layouts  8.15 us
    concatenate x5, other arithmetic, add_product(): weight = jnp.concatenate(weights, axis=0)  7.98 us
    ppermute x2, waiting for transfers between devices, to_corner(): right = lax.ppermute(by_x[:, cut:], 'req', y_perm)  7.75 us
    ppermute x4, starting transfers between devices, to_sides(): lax.ppermute(block, 'req', y_perm)  6.18 us
    ppermute x4, starting transfers between devices, to_sides(): lax.ppermute(block, 'req', x_perm)  5.03 us
  transfers between devices with their start and end apart: 22, of which 14 were waited for; matrix products, arithmetic and copies ran while one was open for 19% of the time, Pallas kernels for 5%

profile of v13, /device:TPU:0, one launch (start us, length us, event | category | flops | bytes accessed | tf_op | source)
XLA Modules:
  0.0 117.3 jit_solution(10518128784235285521)
XLA Ops:
  0.0 3.0 %collective-permute-start.1 = (bf16[104,2496]{1,0:T(8,128)(2,1)}, bf16[104,2496]{1,0:T(8,128)(2,1)}, u32[]{:S(2)}, u32[]{:S(2)}) collective-permute-start(bf16[104,2496]{1,0:T(8,128)(2,1)} %param.16), channel_id=1, source_target_pairs={{0,8},{2,10},{4,12},{6,14},{8,24},{10,26},{12,28},{14,30},{16,0},{... | collective-permute-start | bytes 1557512 | tf_op jit(solution)/shard_map/ppermute | solution.py:190
  3.0 1.5 %collective-permute-start.2 = (bf16[104,2496]{1,0:T(8,128)(2,1)}, bf16[104,2496]{1,0:T(8,128)(2,1)S(1)}, u32[]{:S(2)}, u32[]{:S(2)}) collective-permute-start(bf16[104,2496]{1,0:T(8,128)(2,1)} %param.16), channel_id=1, source_target_pairs={{0,2},{2,0},{4,6},{6,4},{8,10},{10,8},{12,14},{14,12},{16,18},{18,... | collective-permute-start | bytes 1557512 | tf_op jit(solution)/shard_map/ppermute | solution.py:193
  4.5 1.5 %collective-permute-start.3 = (bf16[104,2496]{1,0:T(8,128)(2,1)}, bf16[104,2496]{1,0:T(8,128)(2,1)S(1)}, u32[]{:S(2)}, u32[]{:S(2)}) collective-permute-start(bf16[104,2496]{1,0:T(8,128)(2,1)} %param.16), channel_id=1, source_target_pairs={{0,4},{2,6},{4,0},{6,2},{8,12},{10,14},{12,8},{14,10},{16,20},{18,... | collective-permute-start | bytes 1557512 | tf_op jit(solution)/shard_map/ppermute | solution.py:193
  6.0 1.1 copy-done.1
  7.2 0.3 shard_map.118.refs_0_
  7.5 0.7 convert_bitcast_fusion.1
  8.2 0.7 fusion.10.order_ref
  8.9 0.7 stack.21
  9.6 0.7 stack.22
  10.3 0.8 reshape.53
  11.1 0.2 convert_reduce_fusion
  11.3 5.1 %collective-permute-done.1 = bf16[104,2496]{1,0:T(8,128)(2,1)} collective-permute-done((bf16[104,2496]{1,0:T(8,128)(2,1)}, bf16[104,2496]{1,0:T(8,128)(2,1)}, u32[]{:S(2)}, u32[]{:S(2)}) %collective-permute-start.1) | collective-permute-done | bytes 519200 | tf_op jit(solution)/shard_map/ppermute | solution.py:190
  16.4 0.3 collective-permute-done.2
  16.8 1.2 %collective-permute-done.3 = bf16[104,2496]{1,0:T(8,128)(2,1)S(1)} collective-permute-done((bf16[104,2496]{1,0:T(8,128)(2,1)}, bf16[104,2496]{1,0:T(8,128)(2,1)S(1)}, u32[]{:S(2)}, u32[]{:S(2)}) %collective-permute-start.3) | collective-permute-done | bytes 519200 | tf_op jit(solution)/shard_map/ppermute | solution.py:193
  18.0 2.6 %collective-permute-start.5 = (bf16[104,2496]{1,0:T(8,128)(2,1)}, bf16[104,2496]{1,0:T(8,128)(2,1)}, u32[]{:S(2)}, u32[]{:S(2)}) collective-permute-start(bf16[104,2496]{1,0:T(8,128)(2,1)} %collective-permute-done.1), channel_id=1, source_target_pairs={{0,8},{2,10},{4,12},{6,14},{8,24},{10,26},{12,28},{14,30},{16,0},{... | collective-permute-start | bytes 1557512 | tf_op jit(solution)/shard_map/ppermute | solution.py:190
  20.6 0.5 collective-permute-start.6
  21.1 1.5 %collective-permute-start.7 = (bf16[104,2496]{1,0:T(8,128)(2,1)}, bf16[104,2496]{1,0:T(8,128)(2,1)}, u32[]{:S(2)}, u32[]{:S(2)}) collective-permute-start(bf16[104,2496]{1,0:T(8,128)(2,1)} %collective-permute-done.1), channel_id=1, source_target_pairs={{0,4},{2,6},{4,0},{6,2},{8,12},{10,14},{12,8},{14,10},{16,20},{18,... | collective-permute-start | bytes 1557512 | tf_op jit(solution)/shard_map/ppermute | solution.py:193
  22.7 4.1 %copy-done = bf16[4,832,1664]{2,1,0:T(8,128)(2,1)S(1)} copy-done((bf16[4,832,1664]{2,1,0:T(8,128)(2,1)S(1)}, bf16[4,832,1664]{2,1,0:T(8,128)(2,1)}, u32[]{:S(2)}) %copy-start) | copy-done | bytes 11075608
  26.8 1.1 copy-done.2
  27.9 3.6 %shard_map.119 = f32[112,1664]{1,0:T(8,128)S(1)} custom-call(bf16[448,832]{1,0:T(8,128)(2,1)S(1)} %copy-done.2, bf16[2,832]{1,0:T(2,128)(2,1)S(1)} %pad_maximum_fusion.4.gain_bias_ref, f32[448,256]{1,0:T(8,128)S(1)} %shard_map.118.refs_0_, f32[448,256]{1,0:T(8,128)S(1)} %collective-permute-done.refs_1_, bf16[4,832,1664]{2,1,0:T(8,128)(2,1)S(1)} %copy-done), custom_call_target="tpu_custom_call" | custom-call | flops 1000 | bytes 1000 | tf_op jit(solution)/shard_map/pallas_call | solution.py:112
  31.6 0.1 collective-permute-done.5
  31.7 1.3 %collective-permute-done.6 = bf16[104,2496]{1,0:T(8,128)(2,1)} collective-permute-done((bf16[104,2496]{1,0:T(8,128)(2,1)}, bf16[104,2496]{1,0:T(8,128)(2,1)}, u32[]{:S(2)}, u32[]{:S(2)}) %collective-permute-start.6) | collective-permute-done | bytes 519200 | tf_op jit(solution)/shard_map/ppermute | solution.py:193
  33.0 0.3 collective-permute-done.7
  33.3 0.9 constant_dynamic-slice_fusion.1
  34.2 0.5 collective-permute-start.4
  34.7 0.7 slice.28
  35.5 1.5 %collective-permute-start.10 = (bf16[104,1216]{1,0:T(8,128)(2,1)}, bf16[104,1216]{1,0:T(8,128)(2,1)}, u32[]{:S(2)}, u32[]{:S(2)}) collective-permute-start(bf16[104,1216]{1,0:T(8,128)(2,1)} %slice.28), channel_id=1, source_target_pairs={{0,4},{2,6},{4,0},{6,2},{8,12},{10,14},{12,8},{14,10},{16,20},{18,... | collective-permute-start | bytes 758792 | tf_op jit(solution)/shard_map/ppermute | solution.py:197
  37.0 1.7 %slice.27 = bf16[104,1280]{1,0:T(8,128)(2,1)} slice(bf16[104,2496]{1,0:T(8,128)(2,1)} %copy-done.5), slice={[0:104], [0:1280]} | slice | bytes 532480 | tf_op jit(solution)/shard_map/slice | solution.py:196
  38.6 1.4 %collective-permute-start.9 = (bf16[104,1280]{1,0:T(8,128)(2,1)}, bf16[104,1280]{1,0:T(8,128)(2,1)}, u32[]{:S(2)}, u32[]{:S(2)}) collective-permute-start(bf16[104,1280]{1,0:T(8,128)(2,1)} %slice.27), channel_id=1, source_target_pairs={{0,2},{2,0},{4,6},{6,4},{8,10},{10,8},{12,14},{14,12},{16,18},{18,... | collective-permute-start | bytes 798728 | tf_op jit(solution)/shard_map/ppermute | solution.py:196
  40.3 0.1 copy.18
  40.4 0.2 add_convert_fusion
  40.6 3.5 %collective-permute-done.10 = bf16[104,1216]{1,0:T(8,128)(2,1)} collective-permute-done((bf16[104,1216]{1,0:T(8,128)(2,1)}, bf16[104,1216]{1,0:T(8,128)(2,1)}, u32[]{:S(2)}, u32[]{:S(2)}) %collective-permute-start.10) | collective-permute-done | bytes 252960 | tf_op jit(solution)/shard_map/ppermute | solution.py:197
  44.1 2.9 %collective-permute-done.9 = bf16[104,1280]{1,0:T(8,128)(2,1)} collective-permute-done((bf16[104,1280]{1,0:T(8,128)(2,1)}, bf16[104,1280]{1,0:T(8,128)(2,1)}, u32[]{:S(2)}, u32[]{:S(2)}) %collective-permute-start.9) | collective-permute-done | bytes 266272 | tf_op jit(solution)/shard_map/ppermute | solution.py:196
  47.0 1.1 convolution_convert_fusion
  48.1 3.6 %all-to-all-start = ((bf16[16,16,896]{2,1,0:T(8,128)(2,1)}), bf16[16,16,896]{2,1,0:T(8,128)(2,1)S(1)}, u32[]{:S(2)}, u32[]{:S(2)}) async-start(bf16[16,16,896]{2,1,0:T(8,128)(2,1)} %bitcast.5), calls=%async_computation | async-start | bytes 917504 | tf_op jit(solution)/shard_map/all_to_all | solution.py:244
  51.6 0.3 copy.19.gain_ref
  51.9 1.9 %collective-permute-start.14 = (bf16[104,2496]{1,0:T(8,128)(2,1)}, bf16[104,2496]{1,0:T(8,128)(2,1)}, u32[]{:S(2)}, u32[]{:S(2)}) collective-permute-start(bf16[104,2496]{1,0:T(8,128)(2,1)} %collective-permute-done.5), channel_id=1, source_target_pairs={{0,8},{2,10},{4,12},{6,14},{8,24},{10,26},{12,28},{14,30},{16,0},{... | collective-permute-start | bytes 1557512 | tf_op jit(solution)/shard_map/ppermute | solution.py:190
  53.8 1.5 %collective-permute-start.15 = (bf16[104,2496]{1,0:T(8,128)(2,1)}, bf16[104,2496]{1,0:T(8,128)(2,1)}, u32[]{:S(2)}, u32[]{:S(2)}) collective-permute-start(bf16[104,2496]{1,0:T(8,128)(2,1)} %collective-permute-done.5), channel_id=1, source_target_pairs={{0,2},{2,0},{4,6},{6,4},{8,10},{10,8},{12,14},{14,12},{16,18},{18,... | collective-permute-start | bytes 1557512 | tf_op jit(solution)/shard_map/ppermute | solution.py:193
  55.3 1.5 %collective-permute-start.16 = (bf16[104,2496]{1,0:T(8,128)(2,1)}, bf16[104,2496]{1,0:T(8,128)(2,1)}, u32[]{:S(2)}, u32[]{:S(2)}) collective-permute-start(bf16[104,2496]{1,0:T(8,128)(2,1)} %collective-permute-done.5), channel_id=1, source_target_pairs={{0,4},{2,6},{4,0},{6,2},{8,12},{10,14},{12,8},{14,10},{16,20},{18,... | collective-permute-start | bytes 1557512 | tf_op jit(solution)/shard_map/ppermute | solution.py:193
  56.8 2.6 %pad_maximum_fusion.1 = bf16[312,2496]{1,0:T(8,128)(2,1)} fusion(bf16[104,2496]{1,0:T(8,128)(2,1)} %collective-permute-done.7, bf16[104,2496]{1,0:T(8,128)(2,1)} %collective-permute-done.6, bf16[104,2496]{1,0:T(8,128)(2,1)} %collective-permute-done.1), kind=kLoop, calls=%fused_computation.5 | loop fusion | flops 4672512 | bytes 3115008 | tf_op jit(solution)/shard_map/concatenate | solution.py:260
  59.4 1.7 %constant_dynamic-update-slice_fusion.1 = bf16[104,2496]{1,0:T(8,128)(2,1)} fusion(bf16[104,1280]{1,0:T(8,128)(2,1)} %collective-permute-done.9), kind=kLoop, calls=%fused_computation.23 | loop fusion | bytes 532480
  61.1 1.7 %constant_dynamic-update-slice_fusion = bf16[104,2496]{1,0:T(8,128)(2,1)} fusion(bf16[104,2496]{1,0:T(8,128)(2,1)} %constant_dynamic-update-slice_fusion.1, bf16[104,1216]{1,0:T(8,128)(2,1)} %collective-permute-done.10), kind=kLoop, calls=%fused_computation.22 | loop fusion | bytes 532480 | tf_op jit(solution)/shard_map/concatenate | solution.py:234
  62.8 2.4 %collective-permute-start.12 = (bf16[104,2496]{1,0:T(8,128)(2,1)}, bf16[104,2496]{1,0:T(8,128)(2,1)}, u32[]{:S(2)}, u32[]{:S(2)}) collective-permute-start(bf16[104,2496]{1,0:T(8,128)(2,1)} %constant_dynamic-update-slice_fusion), channel_id=1, source_target_pairs={{0,8},{2,10},{4,12},{6,14},{8,24},{10,26},{12,28},{14,30},{16,0},{... | collective-permute-start | bytes 1557512 | tf_op jit(solution)/shard_map/ppermute | solution.py:190
  65.2 11.3 %collective-permute-done.14 = bf16[104,2496]{1,0:T(8,128)(2,1)} collective-permute-done((bf16[104,2496]{1,0:T(8,128)(2,1)}, bf16[104,2496]{1,0:T(8,128)(2,1)}, u32[]{:S(2)}, u32[]{:S(2)}) %collective-permute-start.14) | collective-permute-done | bytes 519200 | tf_op jit(solution)/shard_map/ppermute | solution.py:190
  76.5 1.5 %pad_maximum_fusion = bf16[416,2496]{1,0:T(8,128)(2,1)S(1)} fusion(bf16[104,2496]{1,0:T(8,128)(2,1)} %constant_dynamic-update-slice_fusion, bf16[104,2496]{1,0:T(8,128)(2,1)} %copy-done.5, bf16[104,2496]{1,0:T(8,128)(2,1)S(1)} %collective-permute-done.2, bf16[104,2496]{1,0:T(8,128)(2,1)} %param.16), kind=kLoop, calls=%fused_computation.4 | loop fusion | flops 8306688 | bytes 4153344 | tf_op jit(solution)/shard_map/concatenate | solution.py:260
  78.0 1.5 %collective-permute-start.17 = (bf16[104,2496]{1,0:T(8,128)(2,1)}, bf16[104,2496]{1,0:T(8,128)(2,1)S(1)}, u32[]{:S(2)}, u32[]{:S(2)}) collective-permute-start(bf16[104,2496]{1,0:T(8,128)(2,1)} %collective-permute-done.14), channel_id=1, source_target_pairs={{0,2},{2,0},{4,6},{6,4},{8,10},{10,8},{12,14},{14,12},{16,18},{18,... | collective-permute-start | bytes 1557512 | tf_op jit(solution)/shard_map/ppermute | solution.py:193
  79.6 1.7 %collective-permute-start.18 = (bf16[104,2496]{1,0:T(8,128)(2,1)}, bf16[104,2496]{1,0:T(8,128)(2,1)S(1)}, u32[]{:S(2)}, u32[]{:S(2)}) collective-permute-start(bf16[104,2496]{1,0:T(8,128)(2,1)} %collective-permute-done.14), channel_id=1, source_target_pairs={{0,4},{2,6},{4,0},{6,2},{8,12},{10,14},{12,8},{14,10},{16,20},{18,... | collective-permute-start | bytes 1557512 | tf_op jit(solution)/shard_map/ppermute | solution.py:193
  81.2 1.5 %pad_maximum_fusion.3 = bf16[312,2496]{1,0:T(8,128)(2,1)S(1)} fusion(bf16[104,2496]{1,0:T(8,128)(2,1)} %collective-permute-done.16, bf16[104,2496]{1,0:T(8,128)(2,1)} %collective-permute-done.15, bf16[104,2496]{1,0:T(8,128)(2,1)} %collective-permute-done.5), kind=kLoop, calls=%fused_computation.8 | loop fusion | flops 4672512 | bytes 3115008 | tf_op jit(solution)/shard_map/concatenate | solution.py:260
  82.7 1.9 %shard_map.120 = bf16[16,104,512]{2,1,0:T(8,128)(2,1)S(1)} custom-call(s32[1]{0:T(128)} %bitcast.index_ref, s32[16]{0:T(128)S(1)} %fusion.10.order_ref, bf16[16,104,1]{2,1,0:T(8,128)(2,1)S(1)} %copy.19.gain_ref, bf16[832,512]{1,0:T(8,128)(2,1)S(1)} %bitcast.28, bf16[832,512]{1,0:T(8,128)(2,1)S(1)} %collective-permute-done.4.refs_1_, ...), custom_call_target="tpu_custom_call" | custom-call | flops 1000 | bytes 1000 | tf_op jit(solution)/shard_map/pallas_call | solution.py:164
  84.6 2.2 %collective-permute-done.12 = bf16[104,2496]{1,0:T(8,128)(2,1)} collective-permute-done((bf16[104,2496]{1,0:T(8,128)(2,1)}, bf16[104,2496]{1,0:T(8,128)(2,1)}, u32[]{:S(2)}, u32[]{:S(2)}) %collective-permute-start.12) | collective-permute-done | bytes 519200 | tf_op jit(solution)/shard_map/ppermute | solution.py:190
  86.8 0.1 fusion.14
  86.9 1.5 %fusion.15 = f32[512,2496]{0,1:T(8,128)S(1)} fusion(bf16[416,512]{1,0:T(8,128)(2,1)S(1)} %bitcast.30, bf16[416,2496]{1,0:T(8,128)(2,1)S(1)} %pad_maximum_fusion), kind=kOutput, calls=%fused_computation.48 | convolution fusion | flops 1063256064 | bytes 7614464 | tf_op jit(solution)/shard_map/dot_general | solution.py:267
  88.5 1.5 %convolution_add_fusion.2 = f32[512,2496]{0,1:T(8,128)S(1)} fusion(f32[512,2496]{0,1:T(8,128)S(1)} %fusion.15, bf16[312,512]{1,0:T(8,128)(2,1)S(1)} %bitcast.33, bf16[312,2496]{1,0:T(8,128)(2,1)S(1)} %copy-done.4), kind=kOutput, calls=%fused_computation.3 | convolution fusion | flops 798720000 | bytes 12100608 | tf_op jit(solution)/shard_map/dot_general | solution.py:267
  90.0 2.8 %collective-permute-done.17 = bf16[104,2496]{1,0:T(8,128)(2,1)S(1)} collective-permute-done((bf16[104,2496]{1,0:T(8,128)(2,1)}, bf16[104,2496]{1,0:T(8,128)(2,1)S(1)}, u32[]{:S(2)}, u32[]{:S(2)}) %collective-permute-start.17) | collective-permute-done | bytes 519200 | tf_op jit(solution)/shard_map/ppermute | solution.py:193
  92.8 1.2 %collective-permute-done.18 = bf16[104,2496]{1,0:T(8,128)(2,1)S(1)} collective-permute-done((bf16[104,2496]{1,0:T(8,128)(2,1)}, bf16[104,2496]{1,0:T(8,128)(2,1)S(1)}, u32[]{:S(2)}, u32[]{:S(2)}) %collective-permute-start.18) | collective-permute-done | bytes 519200 | tf_op jit(solution)/shard_map/ppermute | solution.py:193
  94.0 1.2 %pad_maximum_fusion.2 = bf16[312,2496]{1,0:T(8,128)(2,1)S(1)} fusion(bf16[104,2496]{1,0:T(8,128)(2,1)S(1)} %collective-permute-done.18, bf16[104,2496]{1,0:T(8,128)(2,1)S(1)} %collective-permute-done.17, bf16[104,2496]{1,0:T(8,128)(2,1)} %collective-permute-done.14), kind=kLoop, calls=%fused_computation.7 | loop fusion | flops 4672512 | bytes 3115008 | tf_op jit(solution)/shard_map/concatenate | solution.py:260
  95.2 1.5 %convolution_add_fusion.1 = f32[512,2496]{0,1:T(8,128)S(1)} fusion(f32[512,2496]{0,1:T(8,128)S(1)} %convolution_add_fusion.2, bf16[312,512]{1,0:T(8,128)(2,1)S(1)} %bitcast.32, bf16[312,2496]{1,0:T(8,128)(2,1)S(1)} %pad_maximum_fusion.3), kind=kOutput, calls=%fused_computation.2 | convolution fusion | flops 798720000 | bytes 12100608 | tf_op jit(solution)/shard_map/dot_general | solution.py:267
  96.8 0.6 collective-permute-start.19
  97.4 1.7 %collective-permute-start.20 = (bf16[104,1216]{1,0:T(8,128)(2,1)S(1)}, bf16[104,1216]{1,0:T(8,128)(2,1)S(1)}, u32[]{:S(2)}, u32[]{:S(2)}) collective-permute-start(bf16[104,1216]{1,0:T(8,128)(2,1)S(1)} %slice.32), channel_id=1, source_target_pairs={{0,4},{2,6},{4,0},{6,2},{8,12},{10,14},{12,8},{14,10},{16,20},{18,... | collective-permute-start | bytes 758792 | tf_op jit(solution)/shard_map/ppermute | solution.py:197
  99.1 1.5 %convolution_add_fusion = f32[512,2496]{0,1:T(8,128)S(1)} fusion(f32[512,2496]{0,1:T(8,128)S(1)} %convolution_add_fusion.1, bf16[312,512]{1,0:T(8,128)(2,1)S(1)} %bitcast.31, bf16[312,2496]{1,0:T(8,128)(2,1)S(1)} %pad_maximum_fusion.2), kind=kOutput, calls=%fused_computation.1 | convolution fusion | flops 798720000 | bytes 12100608 | tf_op jit(solution)/shard_map/dot_general | solution.py:267
  100.6 4.2 %collective-permute-done.20 = bf16[104,1216]{1,0:T(8,128)(2,1)S(1)} collective-permute-done((bf16[104,1216]{1,0:T(8,128)(2,1)S(1)}, bf16[104,1216]{1,0:T(8,128)(2,1)S(1)}, u32[]{:S(2)}, u32[]{:S(2)}) %collective-permute-start.20) | collective-permute-done | bytes 252960 | tf_op jit(solution)/shard_map/ppermute | solution.py:197
  104.9 8.2 %collective-permute-done.13 = bf16[104,2496]{1,0:T(8,128)(2,1)S(1)} collective-permute-done((bf16[104,2496]{1,0:T(8,128)(2,1)}, bf16[104,2496]{1,0:T(8,128)(2,1)S(1)}, u32[]{:S(2)}, u32[]{:S(2)}) %collective-permute-start.13) | collective-permute-done | bytes 519200 | tf_op jit(solution)/shard_map/ppermute | solution.py:190
  113.1 1.2 maximum_maximum_fusion
  114.2 3.1 %select_convert_fusion = bf16[512,2496]{0,1:T(8,128)(2,1)} fusion(f32[512,2496]{0,1:T(8,128)S(1)} %convolution_add_fusion, bf16[312,512]{1,0:T(8,128)(2,1)S(1)} %bitcast.29, bf16[312,2496]{1,0:T(8,128)(2,1)S(1)} %maximum_maximum_fusion, pred[512]{0:T(512)(128)(4,1)S(1)} %fusion.8), kind=kOutput, calls=%fused_computation | convolution fusion | flops 801275904 | bytes 9545216 | tf_op jit(solution)/shard_map/dot_general | solution.py:267
  (35 shorter events, 0.4 us)
Async XLA Ops:
  0.0 16.4 %collective-permute-start.1 = (bf16[104,2496]{1,0:T(8,128)(2,1)}, bf16[104,2496]{1,0:T(8,128)(2,1)}, u32[]{:S(2)}, u32[]{:S(2)}) collective-permute-start(bf16[104,2496]{1,0:T(8,128)(2,1)} %param.16), channel_id=1, source_target_pairs={{0,8},{2,10},{4,12},{6,14},{8,24},{10,26},{12,28},{14,30},{16,0},{... | collective-permute-start | bytes 1557512 | tf_op jit(solution)/shard_map/ppermute | solution.py:190
  3.0 13.8 %collective-permute-start.2 = (bf16[104,2496]{1,0:T(8,128)(2,1)}, bf16[104,2496]{1,0:T(8,128)(2,1)S(1)}, u32[]{:S(2)}, u32[]{:S(2)}) collective-permute-start(bf16[104,2496]{1,0:T(8,128)(2,1)} %param.16), channel_id=1, source_target_pairs={{0,2},{2,0},{4,6},{6,4},{8,10},{10,8},{12,14},{14,12},{16,18},{18,... | collective-permute-start | bytes 1557512 | tf_op jit(solution)/shard_map/ppermute | solution.py:193
  4.5 13.5 %collective-permute-start.3 = (bf16[104,2496]{1,0:T(8,128)(2,1)}, bf16[104,2496]{1,0:T(8,128)(2,1)S(1)}, u32[]{:S(2)}, u32[]{:S(2)}) collective-permute-start(bf16[104,2496]{1,0:T(8,128)(2,1)} %param.16), channel_id=1, source_target_pairs={{0,4},{2,6},{4,0},{6,2},{8,12},{10,14},{12,8},{14,10},{16,20},{18,... | collective-permute-start | bytes 1557512 | tf_op jit(solution)/shard_map/ppermute | solution.py:193
  6.0 1.1 copy-start.1
  7.5 3.8 %collective-permute-start = (f32[448,256]{1,0:T(8,128)S(1)}, f32[448,256]{1,0:T(8,128)S(1)}, u32[]{:S(2)}, u32[]{:S(2)}) collective-permute-start(f32[448,256]{1,0:T(8,128)S(1)} %shard_map.118.refs_0_), channel_id=1, source_target_pairs={{0,1},{1,0},{2,3},{3,2},{4,5},{5,4},{6,7},{7,6},{8,9},{9,8},{10,11... | collective-permute-start | bytes 1376264 | tf_op jit(solution)/shard_map/ppermute | solution.py:26
  18.0 4.6 %copy-start.5 = (bf16[104,2496]{1,0:T(8,128)(2,1)}, bf16[104,2496]{1,0:T(8,128)(2,1)S(1)}, u32[]{:S(2)}) copy-start(bf16[104,2496]{1,0:T(8,128)(2,1)S(1)} %collective-permute-done.3) | copy-start | bytes 1557508
  18.0 13.7 %collective-permute-start.5 = (bf16[104,2496]{1,0:T(8,128)(2,1)}, bf16[104,2496]{1,0:T(8,128)(2,1)}, u32[]{:S(2)}, u32[]{:S(2)}) collective-permute-start(bf16[104,2496]{1,0:T(8,128)(2,1)} %collective-permute-done.1), channel_id=1, source_target_pairs={{0,8},{2,10},{4,12},{6,14},{8,24},{10,26},{12,28},{14,30},{16,0},{... | collective-permute-start | bytes 1557512 | tf_op jit(solution)/shard_map/ppermute | solution.py:190
  20.6 12.4 %collective-permute-start.6 = (bf16[104,2496]{1,0:T(8,128)(2,1)}, bf16[104,2496]{1,0:T(8,128)(2,1)}, u32[]{:S(2)}, u32[]{:S(2)}) collective-permute-start(bf16[104,2496]{1,0:T(8,128)(2,1)} %collective-permute-done.1), channel_id=1, source_target_pairs={{0,2},{2,0},{4,6},{6,4},{8,10},{10,8},{12,14},{14,12},{16,18},{18,... | collective-permute-start | bytes 1557512 | tf_op jit(solution)/shard_map/ppermute | solution.py:193
  21.1 12.2 %collective-permute-start.7 = (bf16[104,2496]{1,0:T(8,128)(2,1)}, bf16[104,2496]{1,0:T(8,128)(2,1)}, u32[]{:S(2)}, u32[]{:S(2)}) collective-permute-start(bf16[104,2496]{1,0:T(8,128)(2,1)} %collective-permute-done.1), channel_id=1, source_target_pairs={{0,4},{2,6},{4,0},{6,2},{8,12},{10,14},{12,8},{14,10},{16,20},{18,... | collective-permute-start | bytes 1557512 | tf_op jit(solution)/shard_map/ppermute | solution.py:193
  22.7 4.1 %copy-start = (bf16[4,832,1664]{2,1,0:T(8,128)(2,1)S(1)}, bf16[4,832,1664]{2,1,0:T(8,128)(2,1)}, u32[]{:S(2)}) copy-start(bf16[4,832,1664]{2,1,0:T(8,128)(2,1)} %refs_2_.1) | copy-start | bytes 33226756
  26.8 1.1 copy-start.2
  27.9 6.3 %copy-start.3 = (bf16[512,832]{0,1:T(8,128)(2,1)S(1)}, bf16[512,832]{0,1:T(8,128)(2,1)}, u32[]{:S(2)}) copy-start(bf16[512,832]{0,1:T(8,128)(2,1)} %param.14) | copy-start | bytes 2555908
  27.9 12.1 %copy-start.6 = (s32[2]{0:T(128)S(1)}, s32[2]{0:T(128)}, u32[]{:S(2)}) copy-start(s32[2]{0:T(128)} %param.18) | copy-start | bytes 28
  34.2 6.2 %collective-permute-start.8 = (f32[112,832]{1,0:T(8,128)}, f32[112,832]{1,0:T(8,128)S(1)}, u32[]{:S(2)}, u32[]{:S(2)}) collective-permute-start(f32[112,832]{1,0:T(8,128)} %constant_dynamic-slice_fusion.1), channel_id=1, source_target_pairs={{0,1},{1,0},{2,3},{3,2},{4,5},{5,4},{6,7},{7,6},{8,9},{9,8},{10,11... | collective-permute-start | bytes 1118216 | tf_op jit(solution)/shard_map/ppermute | solution.py:26
  34.2 48.5 %collective-permute-start.4 = (bf16[832,512]{1,0:T(8,128)(2,1)S(1)}, bf16[832,512]{1,0:T(8,128)(2,1)S(1)}, u32[]{:S(2)}, u32[]{:S(2)}) collective-permute-start(bf16[832,512]{1,0:T(8,128)(2,1)S(1)} %bitcast.27), channel_id=1, source_target_pairs={{0,1},{1,0},{2,3},{3,2},{4,5},{5,4},{6,7},{7,6},{8,9},{9,8},{10,11... | collective-permute-start | bytes 2555912 | tf_op jit(solution)/shard_map/ppermute | solution.py:26
  35.5 8.6 %collective-permute-start.10 = (bf16[104,1216]{1,0:T(8,128)(2,1)}, bf16[104,1216]{1,0:T(8,128)(2,1)}, u32[]{:S(2)}, u32[]{:S(2)}) collective-permute-start(bf16[104,1216]{1,0:T(8,128)(2,1)} %slice.28), channel_id=1, source_target_pairs={{0,4},{2,6},{4,0},{6,2},{8,12},{10,14},{12,8},{14,10},{16,20},{18,... | collective-permute-start | bytes 758792 | tf_op jit(solution)/shard_map/ppermute | solution.py:197
  38.6 8.3 %collective-permute-start.9 = (bf16[104,1280]{1,0:T(8,128)(2,1)}, bf16[104,1280]{1,0:T(8,128)(2,1)}, u32[]{:S(2)}, u32[]{:S(2)}) collective-permute-start(bf16[104,1280]{1,0:T(8,128)(2,1)} %slice.27), channel_id=1, source_target_pairs={{0,2},{2,0},{4,6},{6,4},{8,10},{10,8},{12,14},{14,12},{16,18},{18,... | collective-permute-start | bytes 798728 | tf_op jit(solution)/shard_map/ppermute | solution.py:196
  48.1 28.4 %all-to-all-start = ((bf16[16,16,896]{2,1,0:T(8,128)(2,1)}), bf16[16,16,896]{2,1,0:T(8,128)(2,1)S(1)}, u32[]{:S(2)}, u32[]{:S(2)}) async-start(bf16[16,16,896]{2,1,0:T(8,128)(2,1)} %bitcast.5), calls=%async_computation | async-start | bytes 917504 | tf_op jit(solution)/shard_map/all_to_all | solution.py:244
  51.9 24.5 %collective-permute-start.14 = (bf16[104,2496]{1,0:T(8,128)(2,1)}, bf16[104,2496]{1,0:T(8,128)(2,1)}, u32[]{:S(2)}, u32[]{:S(2)}) collective-permute-start(bf16[104,2496]{1,0:T(8,128)(2,1)} %collective-permute-done.5), channel_id=1, source_target_pairs={{0,8},{2,10},{4,12},{6,14},{8,24},{10,26},{12,28},{14,30},{16,0},{... | collective-permute-start | bytes 1557512 | tf_op jit(solution)/shard_map/ppermute | solution.py:190
  53.8 24.2 %collective-permute-start.15 = (bf16[104,2496]{1,0:T(8,128)(2,1)}, bf16[104,2496]{1,0:T(8,128)(2,1)}, u32[]{:S(2)}, u32[]{:S(2)}) collective-permute-start(bf16[104,2496]{1,0:T(8,128)(2,1)} %collective-permute-done.5), channel_id=1, source_target_pairs={{0,2},{2,0},{4,6},{6,4},{8,10},{10,8},{12,14},{14,12},{16,18},{18,... | collective-permute-start | bytes 1557512 | tf_op jit(solution)/shard_map/ppermute | solution.py:193
  55.3 22.7 %collective-permute-start.16 = (bf16[104,2496]{1,0:T(8,128)(2,1)}, bf16[104,2496]{1,0:T(8,128)(2,1)}, u32[]{:S(2)}, u32[]{:S(2)}) collective-permute-start(bf16[104,2496]{1,0:T(8,128)(2,1)} %collective-permute-done.5), channel_id=1, source_target_pairs={{0,4},{2,6},{4,0},{6,2},{8,12},{10,14},{12,8},{14,10},{16,20},{18,... | collective-permute-start | bytes 1557512 | tf_op jit(solution)/shard_map/ppermute | solution.py:193
  62.8 24.0 %collective-permute-start.12 = (bf16[104,2496]{1,0:T(8,128)(2,1)}, bf16[104,2496]{1,0:T(8,128)(2,1)}, u32[]{:S(2)}, u32[]{:S(2)}) collective-permute-start(bf16[104,2496]{1,0:T(8,128)(2,1)} %constant_dynamic-update-slice_fusion), channel_id=1, source_target_pairs={{0,8},{2,10},{4,12},{6,14},{8,24},{10,26},{12,28},{14,30},{16,0},{... | collective-permute-start | bytes 1557512 | tf_op jit(solution)/shard_map/ppermute | solution.py:190
  76.5 6.2 %collective-permute-start.11 = (bf16[256,896]{1,0:T(8,128)(2,1)S(1)}, bf16[256,896]{1,0:T(8,128)(2,1)S(1)}, u32[]{:S(2)}, u32[]{:S(2)}) collective-permute-start(bf16[256,896]{1,0:T(8,128)(2,1)S(1)} %bitcast.25), channel_id=1, source_target_pairs={{0,1},{1,0},{2,3},{3,2},{4,5},{5,4},{6,7},{7,6},{8,9},{9,8},{10,11... | collective-permute-start | bytes 1376264 | tf_op jit(solution)/shard_map/ppermute | solution.py:26
  78.0 14.8 %collective-permute-start.17 = (bf16[104,2496]{1,0:T(8,128)(2,1)}, bf16[104,2496]{1,0:T(8,128)(2,1)S(1)}, u32[]{:S(2)}, u32[]{:S(2)}) collective-permute-start(bf16[104,2496]{1,0:T(8,128)(2,1)} %collective-permute-done.14), channel_id=1, source_target_pairs={{0,2},{2,0},{4,6},{6,4},{8,10},{10,8},{12,14},{14,12},{16,18},{18,... | collective-permute-start | bytes 1557512 | tf_op jit(solution)/shard_map/ppermute | solution.py:193
  79.6 14.4 %collective-permute-start.18 = (bf16[104,2496]{1,0:T(8,128)(2,1)}, bf16[104,2496]{1,0:T(8,128)(2,1)S(1)}, u32[]{:S(2)}, u32[]{:S(2)}) collective-permute-start(bf16[104,2496]{1,0:T(8,128)(2,1)} %collective-permute-done.14), channel_id=1, source_target_pairs={{0,4},{2,6},{4,0},{6,2},{8,12},{10,14},{12,8},{14,10},{16,20},{18,... | collective-permute-start | bytes 1557512 | tf_op jit(solution)/shard_map/ppermute | solution.py:193
  86.9 1.6 %copy-start.4 = (bf16[312,2496]{1,0:T(8,128)(2,1)S(1)}, bf16[312,2496]{1,0:T(8,128)(2,1)}, u32[]{:S(2)}) copy-start(bf16[312,2496]{1,0:T(8,128)(2,1)} %pad_maximum_fusion.1) | copy-start | bytes 4672516
  96.8 8.1 %collective-permute-start.19 = (bf16[104,1280]{1,0:T(8,128)(2,1)S(1)}, bf16[104,1280]{1,0:T(8,128)(2,1)S(1)}, u32[]{:S(2)}, u32[]{:S(2)}) collective-permute-start(bf16[104,1280]{1,0:T(8,128)(2,1)S(1)} %slice.31), channel_id=1, source_target_pairs={{0,2},{2,0},{4,6},{6,4},{8,10},{10,8},{12,14},{14,12},{16,18},{18,... | collective-permute-start | bytes 798728 | tf_op jit(solution)/shard_map/ppermute | solution.py:196
  97.4 7.5 %collective-permute-start.20 = (bf16[104,1216]{1,0:T(8,128)(2,1)S(1)}, bf16[104,1216]{1,0:T(8,128)(2,1)S(1)}, u32[]{:S(2)}, u32[]{:S(2)}) collective-permute-start(bf16[104,1216]{1,0:T(8,128)(2,1)S(1)} %slice.32), channel_id=1, source_target_pairs={{0,4},{2,6},{4,0},{6,2},{8,12},{10,14},{12,8},{14,10},{16,20},{18,... | collective-permute-start | bytes 758792 | tf_op jit(solution)/shard_map/ppermute | solution.py:197
  99.1 14.0 %collective-permute-start.13 = (bf16[104,2496]{1,0:T(8,128)(2,1)}, bf16[104,2496]{1,0:T(8,128)(2,1)S(1)}, u32[]{:S(2)}, u32[]{:S(2)}) collective-permute-start(bf16[104,2496]{1,0:T(8,128)(2,1)} %collective-permute-done.12), channel_id=1, source_target_pairs={{0,8},{2,10},{4,12},{6,14},{8,24},{10,26},{12,28},{14,30},{16,0},{... | collective-permute-start | bytes 1557512 | tf_op jit(solution)/shard_map/ppermute | solution.py:190

commit v14 on v12

--- a/solution.py
+++ b/solution.py
@@ -182,8 +182,8 @@
     lines, line_perm, table = ring_tables(n_req)
     x_perm = [(i, i ^ 1) for i in range(n_req)]
     y_perm = [(i, i ^ 2) for i in range(n_req)]
+    corner_perm = [(i, i ^ 3) for i in range(n_req)]
     rows, columns = qkv_weight.shape
-    cut = (columns + 255) // 256 * 128
     order = lax.dynamic_slice_in_dim(jnp.asarray(table), me, 1, 0).reshape(-1)
 
     def along_line(block):
@@ -192,15 +192,14 @@
     def to_sides(block):
         return lax.ppermute(block, "req", x_perm), lax.ppermute(block, "req", y_perm)
 
-    def to_corner(by_x, by_y):
-        left = lax.ppermute(by_y[:, :cut], "req", x_perm)
-        right = lax.ppermute(by_x[:, cut:], "req", y_perm)
-        return left, right
-
-    stats_own, qkv_weight = tie(row_stats(patches), qkv_weight)
+    def to_corner(block):
+        return lax.ppermute(block, "req", corner_perm)
+
     held = [qkv_weight]
     held.append(along_line(held[0]))
     sides = [to_sides(held[0])]
+    corners = [to_corner(held[0])]
+    stats_own = row_stats(patches)
     stats = [stats_own] + [tp_shift(stats_own, n_tp, d) for d in range(1, n_tp)]
     gain_bias = jnp.stack([ln_gain, ln_bias])
     text_turned = text_rows.T
@@ -224,7 +223,6 @@
     )
     held.append(along_line(held[1]))
     sides.append(to_sides(held[1]))
-    halves = to_corner(*sides[0])
     merged = tp_scatter_sum(partial_value, n_tp, 1).astype(jnp.bfloat16)
     padding = (-width - 2) % 128
     payload = jnp.concatenate(
@@ -234,44 +232,45 @@
         jnp.arange(slot_count, dtype=jnp.int32)[:, None] == slot[None, :]
     ).astype(jnp.bfloat16)
     outgoing = jnp.dot(place, payload, preferred_element_type=jnp.float32).astype(jnp.bfloat16)
+    outgoing, corners[0] = tie(outgoing, corners[0])
     arrived = lax.all_to_all(
         outgoing.reshape(n_req, IMG_CAP, -1), "req", split_axis=0, concat_axis=0
     ).reshape(slot_count, -1)
 
-    held[2], sides[1], halves = tie(held[2], sides[1], halves)
+    held[2], sides[1], corners[0] = tie(held[2], sides[1], corners[0])
     held.append(along_line(held[2]))
     sides.append(to_sides(held[2]))
-    arrived, halves = tie(arrived, halves)
-    corners = [jnp.concatenate(halves, axis=1)]
-    corners.append(along_line(corners[0]))
     images = [arrived] + [tp_shift(arrived, n_tp, d) for d in range(1, n_tp)]
     blocks = combine(tp_index, order, texts, images, gain_column)
 
+    corners.append(along_line(corners[0]))
     held[3], sides[2] = tie(held[3], sides[2])
     sides.append(to_sides(held[3]))
     for step in range(4, lines):
         held.append(along_line(held[step - 1]))
         sides.append(to_sides(held[step]))
-
-    def product(first, weights):
+    corner_last = to_corner(held[-1])
+
+    def add_product(total, first, weights):
         weight = jnp.concatenate(weights, axis=0)
         count = weight.shape[0]
         source = blocks[first : first + count // rows].reshape(count, row_count)
-        weight, source = tie(weight, source)
-        return lax.dot_general(
+        if total is None:
+            weight, source = tie(weight, source)
+        else:
+            weight, source, total = tie(weight, source, total)
+        part = lax.dot_general(
             source, weight, (((0,), (0,)), ((), ())), preferred_element_type=jnp.float32
         )
-
-    total = product(0, [held[0], *sides[0], corners[0]])
+        return part if total is None else total + part
+
+    total = add_product(None, 0, [held[0], *sides[0], corners[0]])
     total, corners[1] = tie(total, corners[1])
     for step in range(2, lines - 1):
         corners.append(along_line(corners[step - 1]))
-    for step in range(1, lines - 1):
-        (total,) = tie(total + product(step * 3 + 1, [held[step], *sides[step]]))
-
-    total, sides[-1] = tie(total, sides[-1])
-    corners.append(jnp.concatenate(to_corner(*sides[-1]), axis=1))
-    (total,) = tie(total + product(lines * 3 - 2, [held[-1], *sides[-1]]))
+    corners.append(corner_last)
+    for step in range(1, lines):
+        total = add_product(total, step * 3 + 1, [held[step], *sides[step]])
 
     position = me * row_count + jnp.arange(row_count, dtype=jnp.int32)
     request_ids = jnp.arange(text_len.shape[0], dtype=jnp.int32)
@@ -282,7 +281,7 @@
         axis=1,
     )
     keep = lax.rem(position, SEQ) < limits
-    total += product(lines * 3 + 1, corners[1:])
+    total = add_product(total, lines * 3 + 1, corners[1:])
     return jnp.where(keep[:, None], total, 0.0).astype(jnp.bfloat16)
 
 

time: 110 us -> 115 us (1.045)
  starting transfers between devices: 24.4 us -> 36.6 us
  local copies, waits for them, and re-layouts: 15.9 us -> 10.1 us
  other arithmetic: 17.1 us -> 15 us
    ppermute x4, waiting for transfers between devices: 0.01 us -> 16.4 us  [to_sides(): lax.ppermute(block, 'req', x_perm)]
    ppermute x5, starting transfers between devices: 7.03 us -> 21.3 us  [along_line(): return lax.ppermute(block, 'req', line_perm)]
    ppermute x5, waiting for transfers between devices: 20 us -> 11.3 us  [along_line(): return lax.ppermute(block, 'req', line_perm)]
    ppermute x4 -> x2, waiting for transfers between devices: 16.4 us -> 8.5 us  [to_corner(): return lax.ppermute(block, 'req', corner_perm)]
    ppermute x4 -> x2, starting transfers between devices: 5.52 us -> 1.56 us  [to_corner(): return lax.ppermute(block, 'req', corner_perm)]
    add x3 -> x1, other arithmetic: 3.78 us -> 1.25 us  [add_product(): return part if total is None else total + part]
    slice x6 -> x2, local copies, waits for them, and re-layouts: 2.56 us -> 0.13 us  [add_product(): source = blocks[first:first + count // rows].reshape(count, row_count)]
    unnamed x23 -> x14, local copies, waits for them, and re-layouts: 8.14 us -> 6.44 us
  transfers between devices with their start and end apart: 22 -> 20, of which waited for: 7 -> 9; matrix products, arithmetic and copies ran while one was open for 27% -> 19% of each run, Pallas kernels for 5% -> 5%
where the time goes in v14:
time: 115 us; the launch traced here: 114 us
  waiting for transfers between devices  37.6 us (33%)
  starting transfers between devices  36.6 us (32%)
  other arithmetic  15 us (13%)
  local copies, waits for them, and re-layouts  10.1 us (9%)
  matrix products  8.85 us (8%)
  Pallas kernels  5.79 us (5%)
    ppermute x5, starting transfers between devices, along_line(): return lax.ppermute(block, 'req', line_perm)  21.3 us
    ppermute x4, waiting for transfers between devices, to_sides(): lax.ppermute(block, 'req', x_perm)  16.4 us
    ppermute x5, waiting for transfers between devices, along_line(): return lax.ppermute(block, 'req', line_perm)  11.3 us
    concatenate x5, other arithmetic, add_product(): weight = jnp.concatenate(weights, axis=0)  9.66 us
    ppermute x2, waiting for transfers between devices, to_corner(): return lax.ppermute(block, 'req', corner_perm)  8.5 us
    dot_general x5, matrix products, add_product(): lax.dot_general(source, weight, (((0,), (0,)), ((), ())), preferred_eleme...  7.8 us
    unnamed x14, local copies, waits for them, and re-layouts  6.44 us
    ppermute x4, starting transfers between devices, to_sides(): lax.ppermute(block, 'req', x_perm)  4.99 us
  transfers between devices with their start and end apart: 20, of which 9 were waited for; matrix products, arithmetic and copies ran while one was open for 19% of the time, Pallas kernels for 5%

profile of v14, /device:TPU:0, one launch (start us, length us, event | category | flops | bytes accessed | tf_op | source)
XLA Modules:
  0.0 114.1 jit_solution(14759006478145143857)
XLA Ops:
  0.0 3.0 %collective-permute-start.1 = (bf16[104,2496]{1,0:T(8,128)(2,1)}, bf16[104,2496]{1,0:T(8,128)(2,1)S(1)}, u32[]{:S(2)}, u32[]{:S(2)}) collective-permute-start(bf16[104,2496]{1,0:T(8,128)(2,1)} %param.16), channel_id=1, source_target_pairs={{0,8},{2,10},{4,12},{6,14},{8,24},{10,26},{12,28},{14,30},{16,0},{... | collective-permute-start | bytes 1557512 | tf_op jit(solution)/shard_map/ppermute | solution.py:190
  3.0 1.5 %collective-permute-start.2 = (bf16[104,2496]{1,0:T(8,128)(2,1)}, bf16[104,2496]{1,0:T(8,128)(2,1)}, u32[]{:S(2)}, u32[]{:S(2)}) collective-permute-start(bf16[104,2496]{1,0:T(8,128)(2,1)} %param.16), channel_id=1, source_target_pairs={{0,2},{2,0},{4,6},{6,4},{8,10},{10,8},{12,14},{14,12},{16,18},{18,... | collective-permute-start | bytes 1557512 | tf_op jit(solution)/shard_map/ppermute | solution.py:193
  4.5 1.5 %collective-permute-start.3 = (bf16[104,2496]{1,0:T(8,128)(2,1)}, bf16[104,2496]{1,0:T(8,128)(2,1)}, u32[]{:S(2)}, u32[]{:S(2)}) collective-permute-start(bf16[104,2496]{1,0:T(8,128)(2,1)} %param.16), channel_id=1, source_target_pairs={{0,4},{2,6},{4,0},{6,2},{8,12},{10,14},{12,8},{14,10},{16,20},{18,... | collective-permute-start | bytes 1557512 | tf_op jit(solution)/shard_map/ppermute | solution.py:193
  6.0 1.1 copy-done.1
  7.2 0.3 shard_map.118.refs_0_
  7.5 0.1 collective-permute-start
  7.5 0.7 convert_bitcast_fusion.1
  8.2 0.7 fusion.10.order_ref
  9.0 0.7 stack.21
  9.6 0.7 stack.22
  10.3 0.8 reshape.52
  11.1 0.2 convert_reduce_fusion
  11.3 0.0 copy-start
  11.3 4.1 %copy-done = bf16[4,832,1664]{2,1,0:T(8,128)(2,1)S(1)} copy-done((bf16[4,832,1664]{2,1,0:T(8,128)(2,1)S(1)}, bf16[4,832,1664]{2,1,0:T(8,128)(2,1)}, u32[]{:S(2)}) %copy-start) | copy-done | bytes 11075608
  15.5 1.1 copy-done.2
  16.6 3.6 %shard_map.119 = f32[112,1664]{1,0:T(8,128)S(1)} custom-call(bf16[448,832]{1,0:T(8,128)(2,1)S(1)} %copy-done.2, bf16[2,832]{1,0:T(2,128)(2,1)S(1)} %pad_maximum_fusion.5.gain_bias_ref, f32[448,256]{1,0:T(8,128)S(1)} %shard_map.118.refs_0_, f32[448,256]{1,0:T(8,128)S(1)} %collective-permute-done.refs_1_, bf16[4,832,1664]{2,1,0:T(8,128)(2,1)S(1)} %copy-done), custom_call_target="tpu_custom_call" | custom-call | flops 1000 | bytes 1000 | tf_op jit(solution)/shard_map/pallas_call | solution.py:112
  20.3 0.0 collective-permute-done.1
  20.3 0.0 collective-permute-done.3
  20.3 0.2 constant_dynamic-slice_fusion.1
  20.5 0.6 collective-permute-start.7
  21.0 0.5 collective-permute-start.8
  21.5 2.6 %collective-permute-start.4 = (bf16[104,2496]{1,0:T(8,128)(2,1)S(1)}, bf16[104,2496]{1,0:T(8,128)(2,1)}, u32[]{:S(2)}, u32[]{:S(2)}) collective-permute-start(bf16[104,2496]{1,0:T(8,128)(2,1)S(1)} %collective-permute-done.1), channel_id=1, source_target_pairs={{0,8},{2,10},{4,12},{6,14},{8,24},{10,26},{12,28},{14,30},{16,0},{... | collective-permute-start | bytes 1557512 | tf_op jit(solution)/shard_map/ppermute | solution.py:190
  24.1 1.5 %collective-permute-start.5 = (bf16[104,2496]{1,0:T(8,128)(2,1)S(1)}, bf16[104,2496]{1,0:T(8,128)(2,1)}, u32[]{:S(2)}, u32[]{:S(2)}) collective-permute-start(bf16[104,2496]{1,0:T(8,128)(2,1)S(1)} %collective-permute-done.1), channel_id=1, source_target_pairs={{0,2},{2,0},{4,6},{6,4},{8,10},{10,8},{12,14},{14,12},{16,18},{18,... | collective-permute-start | bytes 1557512 | tf_op jit(solution)/shard_map/ppermute | solution.py:193
  25.6 1.5 %collective-permute-start.6 = (bf16[104,2496]{1,0:T(8,128)(2,1)S(1)}, bf16[104,2496]{1,0:T(8,128)(2,1)}, u32[]{:S(2)}, u32[]{:S(2)}) collective-permute-start(bf16[104,2496]{1,0:T(8,128)(2,1)S(1)} %collective-permute-done.1), channel_id=1, source_target_pairs={{0,4},{2,6},{4,0},{6,2},{8,12},{10,14},{12,8},{14,10},{16,20},{18,... | collective-permute-start | bytes 1557512 | tf_op jit(solution)/shard_map/ppermute | solution.py:193
  27.1 0.1 fusion.7
  27.2 0.1 pad.18.clone
  27.3 0.1 copy.18
  27.4 0.1 collective-permute-start.9
  27.5 0.2 add_convert_fusion
  27.7 1.1 convolution_convert_fusion
  28.8 8.5 %collective-permute-done.8 = bf16[104,2496]{1,0:T(8,128)(2,1)} collective-permute-done((bf16[104,2496]{1,0:T(8,128)(2,1)}, bf16[104,2496]{1,0:T(8,128)(2,1)}, u32[]{:S(2)}, u32[]{:S(2)}) %collective-permute-start.8) | collective-permute-done | bytes 519200 | tf_op jit(solution)/shard_map/ppermute | solution.py:196
  37.3 4.0 %all-to-all-start = ((bf16[16,16,896]{2,1,0:T(8,128)(2,1)}), bf16[16,16,896]{2,1,0:T(8,128)(2,1)S(1)}, u32[]{:S(2)}, u32[]{:S(2)}) async-start(bf16[16,16,896]{2,1,0:T(8,128)(2,1)} %bitcast.5), calls=%async_computation | async-start | bytes 917504 | tf_op jit(solution)/shard_map/all_to_all | solution.py:236
  41.2 8.7 %collective-permute-done.5 = bf16[104,2496]{1,0:T(8,128)(2,1)} collective-permute-done((bf16[104,2496]{1,0:T(8,128)(2,1)S(1)}, bf16[104,2496]{1,0:T(8,128)(2,1)}, u32[]{:S(2)}, u32[]{:S(2)}) %collective-permute-start.5) | collective-permute-done | bytes 519200 | tf_op jit(solution)/shard_map/ppermute | solution.py:193
  49.9 1.0 collective-permute-done.6
  50.9 3.2 %collective-permute-start.13 = (bf16[104,2496]{1,0:T(8,128)(2,1)}, bf16[104,2496]{1,0:T(8,128)(2,1)}, u32[]{:S(2)}, u32[]{:S(2)}) collective-permute-start(bf16[104,2496]{1,0:T(8,128)(2,1)} %collective-permute-done.4), channel_id=1, source_target_pairs={{0,8},{2,10},{4,12},{6,14},{8,24},{10,26},{12,28},{14,30},{16,0},{... | collective-permute-start | bytes 1557512 | tf_op jit(solution)/shard_map/ppermute | solution.py:190
  54.1 0.5 collective-permute-start.14
  54.7 0.5 collective-permute-start.15
  55.2 0.3 copy.19.gain_ref
  55.5 0.1 collective-permute-start.11
  55.5 3.0 %pad_maximum_fusion = bf16[416,2496]{1,0:T(8,128)(2,1)} fusion(bf16[104,2496]{1,0:T(8,128)(2,1)} %collective-permute-done.8, bf16[104,2496]{1,0:T(8,128)(2,1)} %collective-permute-done.3, bf16[104,2496]{1,0:T(8,128)(2,1)} %collective-permute-done.2, bf16[104,2496]{1,0:T(8,128)(2,1)} %param.16), kind=kLoop, calls=%fused_computation.3 | loop fusion | flops 8306688 | bytes 4153344 | tf_op jit(solution)/shard_map/concatenate | solution.py:255
  58.6 8.6 %collective-permute-done.13 = bf16[104,2496]{1,0:T(8,128)(2,1)} collective-permute-done((bf16[104,2496]{1,0:T(8,128)(2,1)}, bf16[104,2496]{1,0:T(8,128)(2,1)}, u32[]{:S(2)}, u32[]{:S(2)}) %collective-permute-start.13) | collective-permute-done | bytes 519200 | tf_op jit(solution)/shard_map/ppermute | solution.py:190
  67.1 1.0 collective-permute-done.14
  68.1 0.3 collective-permute-done.15
  68.3 1.5 %collective-permute-start.17 = (bf16[104,2496]{1,0:T(8,128)(2,1)}, bf16[104,2496]{1,0:T(8,128)(2,1)}, u32[]{:S(2)}, u32[]{:S(2)}) collective-permute-start(bf16[104,2496]{1,0:T(8,128)(2,1)} %collective-permute-done.13), channel_id=1, source_target_pairs={{0,2},{2,0},{4,6},{6,4},{8,10},{10,8},{12,14},{14,12},{16,18},{18,... | collective-permute-start | bytes 1557512 | tf_op jit(solution)/shard_map/ppermute | solution.py:193
  69.8 0.5 collective-permute-start.18
  70.3 2.5 %pad_maximum_fusion.4 = bf16[312,2496]{1,0:T(8,128)(2,1)} fusion(bf16[104,2496]{1,0:T(8,128)(2,1)} %collective-permute-done.6, bf16[104,2496]{1,0:T(8,128)(2,1)} %collective-permute-done.5, bf16[104,2496]{1,0:T(8,128)(2,1)S(1)} %collective-permute-done.1), kind=kLoop, calls=%fused_computation.7 | loop fusion | flops 4672512 | bytes 3115008 | tf_op jit(solution)/shard_map/concatenate | solution.py:255
  72.9 1.5 %pad_maximum_fusion.3 = bf16[312,2496]{1,0:T(8,128)(2,1)S(1)} fusion(bf16[104,2496]{1,0:T(8,128)(2,1)} %collective-permute-done.15, bf16[104,2496]{1,0:T(8,128)(2,1)} %collective-permute-done.14, bf16[104,2496]{1,0:T(8,128)(2,1)} %collective-permute-done.4), kind=kLoop, calls=%fused_computation.6 | loop fusion | flops 4672512 | bytes 3115008 | tf_op jit(solution)/shard_map/concatenate | solution.py:255
  74.3 6.8 %collective-permute-done.17 = bf16[104,2496]{1,0:T(8,128)(2,1)} collective-permute-done((bf16[104,2496]{1,0:T(8,128)(2,1)}, bf16[104,2496]{1,0:T(8,128)(2,1)}, u32[]{:S(2)}, u32[]{:S(2)}) %collective-permute-start.17) | collective-permute-done | bytes 519200 | tf_op jit(solution)/shard_map/ppermute | solution.py:193
  81.1 1.1 collective-permute-start.16
  82.2 0.1 collective-permute-done.18
  82.3 1.5 %pad_maximum_fusion.2 = bf16[312,2496]{1,0:T(8,128)(2,1)S(1)} fusion(bf16[104,2496]{1,0:T(8,128)(2,1)} %collective-permute-done.18, bf16[104,2496]{1,0:T(8,128)(2,1)} %collective-permute-done.17, bf16[104,2496]{1,0:T(8,128)(2,1)} %collective-permute-done.13), kind=kLoop, calls=%fused_computation.5 | loop fusion | flops 4672512 | bytes 3115008 | tf_op jit(solution)/shard_map/concatenate | solution.py:255
  83.8 0.0 copy-start.4
  83.8 1.9 %shard_map.120 = bf16[16,104,512]{2,1,0:T(8,128)(2,1)S(1)} custom-call(s32[1]{0:T(128)} %bitcast.3.index_ref, s32[16]{0:T(128)S(1)} %fusion.10.order_ref, bf16[16,104,1]{2,1,0:T(8,128)(2,1)S(1)} %copy.19.gain_ref, bf16[832,512]{1,0:T(8,128)(2,1)S(1)} %bitcast.28, bf16[832,512]{1,0:T(8,128)(2,1)S(1)} %collective-permute-done.9.refs_1_, ...), custom_call_target="tpu_custom_call" | custom-call | flops 1000 | bytes 1000 | tf_op jit(solution)/shard_map/pallas_call | solution.py:164
  85.7 0.1 fusion.14
  85.9 1.5 %fusion.15 = f32[512,2496]{0,1:T(8,128)S(1)} fusion(bf16[416,512]{1,0:T(8,128)(2,1)S(1)} %bitcast.29, bf16[416,2496]{1,0:T(8,128)(2,1)S(1)} %copy-done.4), kind=kOutput, calls=%fused_computation.45 | convolution fusion | flops 1063256064 | bytes 7614464 | tf_op jit(solution)/shard_map/dot_general | solution.py:262
  87.4 1.6 %convolution_add_fusion.1 = f32[512,2496]{0,1:T(8,128)S(1)} fusion(f32[512,2496]{0,1:T(8,128)S(1)} %fusion.15, bf16[312,512]{1,0:T(8,128)(2,1)S(1)} %bitcast.33, bf16[312,2496]{1,0:T(8,128)(2,1)S(1)} %copy-done.5), kind=kOutput, calls=%fused_computation.2 | convolution fusion | flops 798720000 | bytes 12100608 | tf_op jit(solution)/shard_map/dot_general | solution.py:262
  89.0 12.4 %collective-permute-start.12 = (bf16[104,2496]{1,0:T(8,128)(2,1)}, bf16[104,2496]{1,0:T(8,128)(2,1)S(1)}, u32[]{:S(2)}, u32[]{:S(2)}) collective-permute-start(bf16[104,2496]{1,0:T(8,128)(2,1)} %collective-permute-done.11), channel_id=1, source_target_pairs={{0,8},{2,10},{4,12},{6,14},{8,24},{10,26},{12,28},{14,30},{16,0},{... | collective-permute-start | bytes 1557512 | tf_op jit(solution)/shard_map/ppermute | solution.py:190
  101.4 1.6 %convolution_add_fusion = f32[512,2496]{0,1:T(8,128)S(1)} fusion(f32[512,2496]{0,1:T(8,128)S(1)} %convolution_add_fusion.1, bf16[312,512]{1,0:T(8,128)(2,1)S(1)} %bitcast.32, bf16[312,2496]{1,0:T(8,128)(2,1)S(1)} %pad_maximum_fusion.3), kind=kOutput, calls=%fused_computation.1 | convolution fusion | flops 798720000 | bytes 12100608 | tf_op jit(solution)/shard_map/dot_general | solution.py:262
  103.1 1.5 %fusion.16 = f32[512,2496]{0,1:T(8,128)S(1)} fusion(bf16[312,512]{1,0:T(8,128)(2,1)S(1)} %bitcast.31, bf16[312,2496]{1,0:T(8,128)(2,1)S(1)} %pad_maximum_fusion.2), kind=kOutput, calls=%fused_computation.46 | convolution fusion | flops 797442048 | bytes 6988800 | tf_op jit(solution)/shard_map/dot_general | solution.py:262
  104.6 1.3 %add.66 = f32[512,2496]{0,1:T(8,128)S(1)} add(f32[512,2496]{0,1:T(8,128)S(1)} %convolution_add_fusion, f32[512,2496]{0,1:T(8,128)S(1)} %fusion.16) | non-fusion elementwise | flops 1277952 | bytes 15335424 | tf_op jit(solution)/shard_map/add | solution.py:265
  105.9 2.7 %collective-permute-done.12 = bf16[104,2496]{1,0:T(8,128)(2,1)S(1)} collective-permute-done((bf16[104,2496]{1,0:T(8,128)(2,1)}, bf16[104,2496]{1,0:T(8,128)(2,1)S(1)}, u32[]{:S(2)}, u32[]{:S(2)}) %collective-permute-start.12) | collective-permute-done | bytes 519200 | tf_op jit(solution)/shard_map/ppermute | solution.py:190
  108.6 1.2 %pad_maximum_fusion.1 = bf16[312,2496]{1,0:T(8,128)(2,1)S(1)} fusion(bf16[104,2496]{1,0:T(8,128)(2,1)S(1)} %collective-permute-done.16, bf16[104,2496]{1,0:T(8,128)(2,1)S(1)} %collective-permute-done.12, bf16[104,2496]{1,0:T(8,128)(2,1)} %collective-permute-done.11), kind=kLoop, calls=%fused_computation.4 | loop fusion | flops 4672512 | bytes 3115008 | tf_op jit(solution)/shard_map/concatenate | solution.py:255
  109.7 1.5 %fusion.17 = f32[512,2496]{0,1:T(8,128)S(1)} fusion(bf16[312,512]{1,0:T(8,128)(2,1)S(1)} %bitcast.30, bf16[312,2496]{1,0:T(8,128)(2,1)S(1)} %pad_maximum_fusion.1), kind=kOutput, calls=%fused_computation.47 | convolution fusion | flops 797442048 | bytes 6988800 | tf_op jit(solution)/shard_map/dot_general | solution.py:262
  111.3 2.9 %select_convert_fusion = bf16[512,2496]{0,1:T(8,128)(2,1)} fusion(f32[512,2496]{0,1:T(8,128)S(1)} %add.66, f32[512,2496]{0,1:T(8,128)S(1)} %fusion.17, pred[512]{0:T(512)(128)(4,1)S(1)} %fusion.8), kind=kLoop, calls=%fused_computation | loop fusion | flops 3833856 | bytes 12780032 | tf_op jit(solution)/shard_map/convert_element_type | solution.py:285
  (27 shorter events, 0.1 us)
Async XLA Ops:
  0.0 20.3 %collective-permute-start.1 = (bf16[104,2496]{1,0:T(8,128)(2,1)}, bf16[104,2496]{1,0:T(8,128)(2,1)S(1)}, u32[]{:S(2)}, u32[]{:S(2)}) collective-permute-start(bf16[104,2496]{1,0:T(8,128)(2,1)} %param.16), channel_id=1, source_target_pairs={{0,8},{2,10},{4,12},{6,14},{8,24},{10,26},{12,28},{14,30},{16,0},{... | collective-permute-start | bytes 1557512 | tf_op jit(solution)/shard_map/ppermute | solution.py:190
  3.0 17.3 %collective-permute-start.2 = (bf16[104,2496]{1,0:T(8,128)(2,1)}, bf16[104,2496]{1,0:T(8,128)(2,1)}, u32[]{:S(2)}, u32[]{:S(2)}) collective-permute-start(bf16[104,2496]{1,0:T(8,128)(2,1)} %param.16), channel_id=1, source_target_pairs={{0,2},{2,0},{4,6},{6,4},{8,10},{10,8},{12,14},{14,12},{16,18},{18,... | collective-permute-start | bytes 1557512 | tf_op jit(solution)/shard_map/ppermute | solution.py:193
  4.5 15.8 %collective-permute-start.3 = (bf16[104,2496]{1,0:T(8,128)(2,1)}, bf16[104,2496]{1,0:T(8,128)(2,1)}, u32[]{:S(2)}, u32[]{:S(2)}) collective-permute-start(bf16[104,2496]{1,0:T(8,128)(2,1)} %param.16), channel_id=1, source_target_pairs={{0,4},{2,6},{4,0},{6,2},{8,12},{10,14},{12,8},{14,10},{16,20},{18,... | collective-permute-start | bytes 1557512 | tf_op jit(solution)/shard_map/ppermute | solution.py:193
  6.0 1.1 copy-start.1
  7.5 3.9 %collective-permute-start = (f32[448,256]{1,0:T(8,128)S(1)}, f32[448,256]{1,0:T(8,128)S(1)}, u32[]{:S(2)}, u32[]{:S(2)}) collective-permute-start(f32[448,256]{1,0:T(8,128)S(1)} %shard_map.118.refs_0_), channel_id=1, source_target_pairs={{0,1},{1,0},{2,3},{3,2},{4,5},{5,4},{6,7},{7,6},{8,9},{9,8},{10,11... | collective-permute-start | bytes 1376264 | tf_op jit(solution)/shard_map/ppermute | solution.py:26
  11.3 4.1 %copy-start = (bf16[4,832,1664]{2,1,0:T(8,128)(2,1)S(1)}, bf16[4,832,1664]{2,1,0:T(8,128)(2,1)}, u32[]{:S(2)}) copy-start(bf16[4,832,1664]{2,1,0:T(8,128)(2,1)} %refs_2_.1) | copy-start | bytes 33226756
  15.5 1.1 copy-start.2
  16.6 10.5 %copy-start.6 = (s32[2]{0:T(128)S(1)}, s32[2]{0:T(128)}, u32[]{:S(2)}) copy-start(s32[2]{0:T(128)} %param.18) | copy-start | bytes 28
  16.6 10.8 %copy-start.3 = (bf16[512,832]{0,1:T(8,128)(2,1)S(1)}, bf16[512,832]{0,1:T(8,128)(2,1)}, u32[]{:S(2)}) copy-start(bf16[512,832]{0,1:T(8,128)(2,1)} %param.14) | copy-start | bytes 2555908
  20.5 6.9 %collective-permute-start.7 = (f32[112,832]{1,0:T(8,128)S(1)}, f32[112,832]{1,0:T(8,128)S(1)}, u32[]{:S(2)}, u32[]{:S(2)}) collective-permute-start(f32[112,832]{1,0:T(8,128)S(1)} %constant_dynamic-slice_fusion.1), channel_id=1, source_target_pairs={{0,1},{1,0},{2,3},{3,2},{4,5},{5,4},{6,7},{7,6},{8,9},{9,8},{10,11... | collective-permute-start | bytes 1118216 | tf_op jit(solution)/shard_map/ppermute | solution.py:26
  21.0 16.2 %collective-permute-start.8 = (bf16[104,2496]{1,0:T(8,128)(2,1)}, bf16[104,2496]{1,0:T(8,128)(2,1)}, u32[]{:S(2)}, u32[]{:S(2)}) collective-permute-start(bf16[104,2496]{1,0:T(8,128)(2,1)} %param.16), channel_id=1, source_target_pairs={{0,6},{2,4},{4,2},{6,0},{8,14},{10,12},{12,10},{14,8},{16,22},{18,... | collective-permute-start | bytes 1557512 | tf_op jit(solution)/shard_map/ppermute | solution.py:196
  21.5 19.7 %collective-permute-start.4 = (bf16[104,2496]{1,0:T(8,128)(2,1)S(1)}, bf16[104,2496]{1,0:T(8,128)(2,1)}, u32[]{:S(2)}, u32[]{:S(2)}) collective-permute-start(bf16[104,2496]{1,0:T(8,128)(2,1)S(1)} %collective-permute-done.1), channel_id=1, source_target_pairs={{0,8},{2,10},{4,12},{6,14},{8,24},{10,26},{12,28},{14,30},{16,0},{... | collective-permute-start | bytes 1557512 | tf_op jit(solution)/shard_map/ppermute | solution.py:190
  24.1 25.8 %collective-permute-start.5 = (bf16[104,2496]{1,0:T(8,128)(2,1)S(1)}, bf16[104,2496]{1,0:T(8,128)(2,1)}, u32[]{:S(2)}, u32[]{:S(2)}) collective-permute-start(bf16[104,2496]{1,0:T(8,128)(2,1)S(1)} %collective-permute-done.1), channel_id=1, source_target_pairs={{0,2},{2,0},{4,6},{6,4},{8,10},{10,8},{12,14},{14,12},{16,18},{18,... | collective-permute-start | bytes 1557512 | tf_op jit(solution)/shard_map/ppermute | solution.py:193
  25.6 25.3 %collective-permute-start.6 = (bf16[104,2496]{1,0:T(8,128)(2,1)S(1)}, bf16[104,2496]{1,0:T(8,128)(2,1)}, u32[]{:S(2)}, u32[]{:S(2)}) collective-permute-start(bf16[104,2496]{1,0:T(8,128)(2,1)S(1)} %collective-permute-done.1), channel_id=1, source_target_pairs={{0,4},{2,6},{4,0},{6,2},{8,12},{10,14},{12,8},{14,10},{16,20},{18,... | collective-permute-start | bytes 1557512 | tf_op jit(solution)/shard_map/ppermute | solution.py:193
  27.4 56.4 %collective-permute-start.9 = (bf16[832,512]{1,0:T(8,128)(2,1)S(1)}, bf16[832,512]{1,0:T(8,128)(2,1)S(1)}, u32[]{:S(2)}, u32[]{:S(2)}) collective-permute-start(bf16[832,512]{1,0:T(8,128)(2,1)S(1)} %bitcast.27), channel_id=1, source_target_pairs={{0,1},{1,0},{2,3},{3,2},{4,5},{5,4},{6,7},{7,6},{8,9},{9,8},{10,11... | collective-permute-start | bytes 2555912 | tf_op jit(solution)/shard_map/ppermute | solution.py:26
  37.3 35.6 %all-to-all-start = ((bf16[16,16,896]{2,1,0:T(8,128)(2,1)}), bf16[16,16,896]{2,1,0:T(8,128)(2,1)S(1)}, u32[]{:S(2)}, u32[]{:S(2)}) async-start(bf16[16,16,896]{2,1,0:T(8,128)(2,1)} %bitcast.5), calls=%async_computation | async-start | bytes 917504 | tf_op jit(solution)/shard_map/all_to_all | solution.py:236
  50.9 16.2 %collective-permute-start.13 = (bf16[104,2496]{1,0:T(8,128)(2,1)}, bf16[104,2496]{1,0:T(8,128)(2,1)}, u32[]{:S(2)}, u32[]{:S(2)}) collective-permute-start(bf16[104,2496]{1,0:T(8,128)(2,1)} %collective-permute-done.4), channel_id=1, source_target_pairs={{0,8},{2,10},{4,12},{6,14},{8,24},{10,26},{12,28},{14,30},{16,0},{... | collective-permute-start | bytes 1557512 | tf_op jit(solution)/shard_map/ppermute | solution.py:190
  54.1 14.0 %collective-permute-start.14 = (bf16[104,2496]{1,0:T(8,128)(2,1)}, bf16[104,2496]{1,0:T(8,128)(2,1)}, u32[]{:S(2)}, u32[]{:S(2)}) collective-permute-start(bf16[104,2496]{1,0:T(8,128)(2,1)} %collective-permute-done.4), channel_id=1, source_target_pairs={{0,2},{2,0},{4,6},{6,4},{8,10},{10,8},{12,14},{14,12},{16,18},{18,... | collective-permute-start | bytes 1557512 | tf_op jit(solution)/shard_map/ppermute | solution.py:193
  54.7 13.7 %collective-permute-start.15 = (bf16[104,2496]{1,0:T(8,128)(2,1)}, bf16[104,2496]{1,0:T(8,128)(2,1)}, u32[]{:S(2)}, u32[]{:S(2)}) collective-permute-start(bf16[104,2496]{1,0:T(8,128)(2,1)} %collective-permute-done.4), channel_id=1, source_target_pairs={{0,4},{2,6},{4,0},{6,2},{8,12},{10,14},{12,8},{14,10},{16,20},{18,... | collective-permute-start | bytes 1557512 | tf_op jit(solution)/shard_map/ppermute | solution.py:193
  55.5 31.9 %collective-permute-start.11 = (bf16[104,2496]{1,0:T(8,128)(2,1)}, bf16[104,2496]{1,0:T(8,128)(2,1)}, u32[]{:S(2)}, u32[]{:S(2)}) collective-permute-start(bf16[104,2496]{1,0:T(8,128)(2,1)} %collective-permute-done.8), channel_id=1, source_target_pairs={{0,8},{2,10},{4,12},{6,14},{8,24},{10,26},{12,28},{14,30},{16,0},{... | collective-permute-start | bytes 1557512 | tf_op jit(solution)/shard_map/ppermute | solution.py:190
  68.3 12.8 %collective-permute-start.17 = (bf16[104,2496]{1,0:T(8,128)(2,1)}, bf16[104,2496]{1,0:T(8,128)(2,1)}, u32[]{:S(2)}, u32[]{:S(2)}) collective-permute-start(bf16[104,2496]{1,0:T(8,128)(2,1)} %collective-permute-done.13), channel_id=1, source_target_pairs={{0,2},{2,0},{4,6},{6,4},{8,10},{10,8},{12,14},{14,12},{16,18},{18,... | collective-permute-start | bytes 1557512 | tf_op jit(solution)/shard_map/ppermute | solution.py:193
  69.8 12.5 %collective-permute-start.18 = (bf16[104,2496]{1,0:T(8,128)(2,1)}, bf16[104,2496]{1,0:T(8,128)(2,1)}, u32[]{:S(2)}, u32[]{:S(2)}) collective-permute-start(bf16[104,2496]{1,0:T(8,128)(2,1)} %collective-permute-done.13), channel_id=1, source_target_pairs={{0,4},{2,6},{4,0},{6,2},{8,12},{10,14},{12,8},{14,10},{16,20},{18,... | collective-permute-start | bytes 1557512 | tf_op jit(solution)/shard_map/ppermute | solution.py:193
  72.9 11.0 %collective-permute-start.10 = (bf16[256,896]{1,0:T(8,128)(2,1)S(1)}, bf16[256,896]{1,0:T(8,128)(2,1)S(1)}, u32[]{:S(2)}, u32[]{:S(2)}) collective-permute-start(bf16[256,896]{1,0:T(8,128)(2,1)S(1)} %bitcast.25), channel_id=1, source_target_pairs={{0,1},{1,0},{2,3},{3,2},{4,5},{5,4},{6,7},{7,6},{8,9},{9,8},{10,11... | collective-permute-start | bytes 1376264 | tf_op jit(solution)/shard_map/ppermute | solution.py:26
  81.1 24.7 %collective-permute-start.16 = (bf16[104,2496]{1,0:T(8,128)(2,1)}, bf16[104,2496]{1,0:T(8,128)(2,1)S(1)}, u32[]{:S(2)}, u32[]{:S(2)}) collective-permute-start(bf16[104,2496]{1,0:T(8,128)(2,1)} %collective-permute-done.13), channel_id=1, source_target_pairs={{0,6},{2,4},{4,2},{6,0},{8,14},{10,12},{12,10},{14,8},{16,22},{18,... | collective-permute-start | bytes 1557512 | tf_op jit(solution)/shard_map/ppermute | solution.py:196
  83.8 2.0 %copy-start.4 = (bf16[416,2496]{1,0:T(8,128)(2,1)S(1)}, bf16[416,2496]{1,0:T(8,128)(2,1)}, u32[]{:S(2)}) copy-start(bf16[416,2496]{1,0:T(8,128)(2,1)} %pad_maximum_fusion) | copy-start | bytes 6230020
  85.9 1.6 %copy-start.5 = (bf16[312,2496]{1,0:T(8,128)(2,1)S(1)}, bf16[312,2496]{1,0:T(8,128)(2,1)}, u32[]{:S(2)}) copy-start(bf16[312,2496]{1,0:T(8,128)(2,1)} %pad_maximum_fusion.4) | copy-start | bytes 4672516
  89.0 19.5 %collective-permute-start.12 = (bf16[104,2496]{1,0:T(8,128)(2,1)}, bf16[104,2496]{1,0:T(8,128)(2,1)S(1)}, u32[]{:S(2)}, u32[]{:S(2)}) collective-permute-start(bf16[104,2496]{1,0:T(8,128)(2,1)} %collective-permute-done.11), channel_id=1, source_target_pairs={{0,8},{2,10},{4,12},{6,14},{8,24},{10,26},{12,28},{14,30},{16,0},{... | collective-permute-start | bytes 1557512 | tf_op jit(solution)/shard_map/ppermute | solution.py:190

commit v15 on v10

--- a/solution.py
+++ b/solution.py
@@ -73,7 +73,7 @@
         in_specs=[vmem],
         out_specs=vmem,
         compiler_params=pltpu.CompilerParams(vmem_limit_bytes=VMEM),
-        cost_estimate=LIGHT,
+        cost_estimate=pl.CostEstimate(flops=1000, bytes_accessed=16 << 20, transcendentals=0),
     )(patches)
 
 
@@ -242,35 +242,39 @@
     held[2], sides[1] = tie(held[2], sides[1])
     held.append(along_line(held[2]))
     sides.append(to_sides(held[2]))
-    corners.append(along_line(corners[0]))
     images = [arrived] + [tp_shift(arrived, n_tp, d) for d in range(1, n_tp)]
     blocks = combine(tp_index, order, texts, images, gain_column)
 
+    corners.append(along_line(corners[0]))
+    blocks, corners[1] = tie(blocks, corners[1])
     held[3], sides[2] = tie(held[3], sides[2])
     sides.append(to_sides(held[3]))
     for step in range(4, lines):
         held.append(along_line(held[step - 1]))
         sides.append(to_sides(held[step]))
-    blocks, corners[1] = tie(blocks, corners[1])
     for step in range(2, lines - 1):
         corners.append(along_line(corners[step - 1]))
 
-    def product(first, weights):
+    def add_product(total, first, weights):
         weight = jnp.concatenate(weights, axis=0)
         count = weight.shape[0]
         source = blocks[first : first + count // rows].reshape(count, row_count)
-        weight, source = tie(weight, source)
-        return lax.dot_general(
+        if total is None:
+            weight, source = tie(weight, source)
+        else:
+            weight, source, total = tie(weight, source, total)
+        part = lax.dot_general(
             source, weight, (((0,), (0,)), ((), ())), preferred_element_type=jnp.float32
         )
-
-    total = product(0, [held[0], *sides[0], corners[0]])
-    for step in range(1, lines - 1):
-        (total,) = tie(total + product(step * 3 + 1, [held[step], *sides[step]]))
+        return part if total is None else total + part
+
+    total = add_product(None, 0, [held[0], *sides[0], corners[0]])
+    total = add_product(total, 4, [held[1], *sides[1]])
 
     total, sides[-1] = tie(total, sides[-1])
     corners.append(to_corner(*sides[-1]))
-    (total,) = tie(total + product(lines * 3 - 2, [held[-1], *sides[-1]]))
+    for step in range(2, lines):
+        total = add_product(total, step * 3 + 1, [held[step], *sides[step]])
 
     position = me * row_count + jnp.arange(row_count, dtype=jnp.int32)
     request_ids = jnp.arange(text_len.shape[0], dtype=jnp.int32)
@@ -281,7 +285,7 @@
         axis=1,
     )
     keep = lax.rem(position, SEQ) < limits
-    total += product(lines * 3 + 1, corners[1:])
+    total = add_product(total, lines * 3 + 1, corners[1:])
     return jnp.where(keep[:, None], total, 0.0).astype(jnp.bfloat16)
 
 

time: 104 us -> 107 us (1.029)
  waiting for transfers between devices: 38.1 us -> 43.8 us
  other arithmetic: 13.5 us -> 9.3 us
  matrix products: 8.89 us -> 10.6 us
    convert_element_type x1 -> x0, other arithmetic: 2.88 us -> none  [shards(): return jnp.where(keep[:, None], total, 0.0).astype(jnp.bfloat16)]
    ppermute x2, waiting for transfers between devices: 3.14 us -> 5.5 us  [to_corner(): right = lax.ppermute(by_x[:, cut:], 'req', y_perm)]
    ppermute x5, waiting for transfers between devices: 21 us -> 22.7 us  [along_line(): return lax.ppermute(block, 'req', line_perm)]
    dot_general x5, matrix products: 7.83 us -> 9.49 us  [add_product(): lax.dot_general(source, weight, (((0,), (0,)), ((), ())), preferred_eleme...]
    ppermute x4, waiting for transfers between devices: 0.39 us -> 1.94 us  [to_sides(): lax.ppermute(block, 'req', x_perm)]
    add x1 -> x0, other arithmetic: 1.27 us -> none  [shards(): total, = tie(total + product(lines * 3 - 2, [held[-1], *sides[-1]]))]
  transfers between devices with their start and end apart: 22 -> 22, of which waited for: 8 -> 7; matrix products, arithmetic and copies ran while one was open for 24% -> 20% of each run, Pallas kernels for 6% -> 5%
where the time goes in v15:
time: 107 us; the launch traced here: 106 us
  waiting for transfers between devices  43.8 us (41%)
  starting transfers between devices  20.9 us (20%)
  local copies, waits for them, and re-layouts  15.7 us (15%)
  matrix products  10.6 us (10%)
  other arithmetic  9.3 us (9%)
  Pallas kernels  5.76 us (5%)
    ppermute x5, waiting for transfers between devices, along_line(): return lax.ppermute(block, 'req', line_perm)  22.7 us
    ppermute x2, waiting for transfers between devices, to_corner(): left = lax.ppermute(by_y[:, :cut], 'req', x_perm)  13.3 us
    dot_general x5, matrix products, add_product(): lax.dot_general(source, weight, (((0,), (0,)), ((), ())), preferred_eleme...  9.49 us
    unnamed x15, local copies, waits for them, and re-layouts  8.16 us
    concatenate x5, other arithmetic, add_product(): weight = jnp.concatenate(weights, axis=0)  8.14 us
    ppermute x5, starting transfers between devices, along_line(): return lax.ppermute(block, 'req', line_perm)  6.19 us
    ppermute x2, waiting for transfers between devices, to_corner(): right = lax.ppermute(by_x[:, cut:], 'req', y_perm)  5.5 us
    pallas_call x1, Pallas kernels, merge(): pl.pallas_call(body, out_shape=jax.ShapeDtypeStruct((tokens, features), j...  3.61 us
  transfers between devices with their start and end apart: 22, of which 7 were waited for; matrix products, arithmetic and copies ran while one was open for 20% of the time, Pallas kernels for 5%

profile of v15, /device:TPU:0, one launch (start us, length us, event | category | flops | bytes accessed | tf_op | source)
XLA Modules:
  0.0 106.3 jit_solution(809036567117584616)
XLA Ops:
  0.0 3.0 %collective-permute-start.1 = (bf16[104,2496]{1,0:T(8,128)(2,1)}, bf16[104,2496]{1,0:T(8,128)(2,1)}, u32[]{:S(2)}, u32[]{:S(2)}) collective-permute-start(bf16[104,2496]{1,0:T(8,128)(2,1)} %param.16), channel_id=1, source_target_pairs={{0,8},{2,10},{4,12},{6,14},{8,24},{10,26},{12,28},{14,30},{16,0},{... | collective-permute-start | bytes 1557512 | tf_op jit(solution)/shard_map/ppermute | solution.py:190
  3.0 1.5 %collective-permute-start.2 = (bf16[104,2496]{1,0:T(8,128)(2,1)}, bf16[104,2496]{1,0:T(8,128)(2,1)S(1)}, u32[]{:S(2)}, u32[]{:S(2)}) collective-permute-start(bf16[104,2496]{1,0:T(8,128)(2,1)} %param.16), channel_id=1, source_target_pairs={{0,2},{2,0},{4,6},{6,4},{8,10},{10,8},{12,14},{14,12},{16,18},{18,... | collective-permute-start | bytes 1557512 | tf_op jit(solution)/shard_map/ppermute | solution.py:193
  4.5 1.5 %collective-permute-start.3 = (bf16[104,2496]{1,0:T(8,128)(2,1)}, bf16[104,2496]{1,0:T(8,128)(2,1)S(1)}, u32[]{:S(2)}, u32[]{:S(2)}) collective-permute-start(bf16[104,2496]{1,0:T(8,128)(2,1)} %param.16), channel_id=1, source_target_pairs={{0,4},{2,6},{4,0},{6,2},{8,12},{10,14},{12,8},{14,10},{16,20},{18,... | collective-permute-start | bytes 1557512 | tf_op jit(solution)/shard_map/ppermute | solution.py:193
  6.0 1.1 %copy-done.1 = bf16[448,832]{1,0:T(8,128)(2,1)S(1)} copy-done((bf16[448,832]{1,0:T(8,128)(2,1)S(1)}, bf16[448,832]{1,0:T(8,128)(2,1)}, u32[]{:S(2)}) %copy-start.1) | copy-done | bytes 745496
  7.2 0.3 shard_map.118.refs_0_
  7.5 0.1 collective-permute-start
  7.5 0.7 convert_bitcast_fusion.1
  8.2 0.7 fusion.10.order_ref
  8.9 0.7 stack.21
  9.6 0.7 stack.22
  10.3 0.8 reshape.53
  11.1 0.2 convert_reduce_fusion
  11.3 0.0 collective-permute-done.refs_1_
  11.3 0.0 copy-start
  11.4 4.1 %copy-done = bf16[4,832,1664]{2,1,0:T(8,128)(2,1)S(1)} copy-done((bf16[4,832,1664]{2,1,0:T(8,128)(2,1)S(1)}, bf16[4,832,1664]{2,1,0:T(8,128)(2,1)}, u32[]{:S(2)}) %copy-start) | copy-done | bytes 11075608
  15.5 1.1 %copy-done.2 = bf16[448,832]{1,0:T(8,128)(2,1)S(1)} copy-done((bf16[448,832]{1,0:T(8,128)(2,1)S(1)}, bf16[448,832]{1,0:T(8,128)(2,1)}, u32[]{:S(2)}) %copy-start.2) | copy-done | bytes 745496
  16.6 3.6 %shard_map.119 = f32[112,1664]{1,0:T(8,128)S(1)} custom-call(bf16[448,832]{1,0:T(8,128)(2,1)S(1)} %copy-done.2, bf16[2,832]{1,0:T(2,128)(2,1)S(1)} %pad_maximum_fusion.4.gain_bias_ref, f32[448,256]{1,0:T(8,128)S(1)} %shard_map.118.refs_0_, f32[448,256]{1,0:T(8,128)S(1)} %collective-permute-done.refs_1_, bf16[4,832,1664]{2,1,0:T(8,128)(2,1)S(1)} %copy-done), custom_call_target="tpu_custom_call" | custom-call | flops 1000 | bytes 1000 | tf_op jit(solution)/shard_map/pallas_call | solution.py:112
  20.2 0.0 copy-start.3
  20.3 0.9 constant_dynamic-slice_fusion.1
  21.2 0.5 collective-permute-start.5
  21.7 0.1 pad.19.clone
  21.8 0.1 fusion.7
  21.9 2.6 %collective-permute-start.11 = (bf16[104,2496]{1,0:T(8,128)(2,1)}, bf16[104,2496]{1,0:T(8,128)(2,1)}, u32[]{:S(2)}, u32[]{:S(2)}) collective-permute-start(bf16[104,2496]{1,0:T(8,128)(2,1)} %collective-permute-done.1), channel_id=1, source_target_pairs={{0,8},{2,10},{4,12},{6,14},{8,24},{10,26},{12,28},{14,30},{16,0},{... | collective-permute-start | bytes 1557512 | tf_op jit(solution)/shard_map/ppermute | solution.py:190
  24.6 0.5 collective-permute-start.12
  25.1 0.5 collective-permute-start.13
  25.6 0.1 copy.18
  25.7 0.3 copy.19.gain_ref
  26.0 0.7 slice.27
  26.7 1.5 %collective-permute-start.7 = (bf16[104,1280]{1,0:T(8,128)(2,1)}, bf16[104,1280]{1,0:T(8,128)(2,1)}, u32[]{:S(2)}, u32[]{:S(2)}) collective-permute-start(bf16[104,1280]{1,0:T(8,128)(2,1)} %slice.27), channel_id=1, source_target_pairs={{0,2},{2,0},{4,6},{6,4},{8,10},{10,8},{12,14},{14,12},{16,18},{18,... | collective-permute-start | bytes 798728 | tf_op jit(solution)/shard_map/ppermute | solution.py:196
  28.2 0.7 slice.28
  28.9 1.5 %collective-permute-start.8 = (bf16[104,1216]{1,0:T(8,128)(2,1)}, bf16[104,1216]{1,0:T(8,128)(2,1)}, u32[]{:S(2)}, u32[]{:S(2)}) collective-permute-start(bf16[104,1216]{1,0:T(8,128)(2,1)} %slice.28), channel_id=1, source_target_pairs={{0,4},{2,6},{4,0},{6,2},{8,12},{10,14},{12,8},{14,10},{16,20},{18,... | collective-permute-start | bytes 758792 | tf_op jit(solution)/shard_map/ppermute | solution.py:197
  30.5 0.2 add_convert_fusion
  30.7 1.1 %convolution_convert_fusion = bf16[256,896]{1,0:T(8,128)(2,1)} fusion(bf16[112,2]{1,0:T(8,128)(2,1)S(1)} %copy.18, bf16[112,832]{1,0:T(8,128)(2,1)S(1)} %add_convert_fusion, bf16[896]{0:T(1024)(128)(2,1)S(1)} %pad.19.clone, s32[112]{0:T(128)S(1)} %multiply_add_fusion), kind=kOutput, calls=%fused_computation.9 | convolution fusion | flops 52240384 | bytes 647808 | tf_op jit(solution)/shard_map/dot_general | solution.py:237
  31.7 3.6 %all-to-all-start = ((bf16[16,16,896]{2,1,0:T(8,128)(2,1)}), bf16[16,16,896]{2,1,0:T(8,128)(2,1)S(1)}, u32[]{:S(2)}, u32[]{:S(2)}) async-start(bf16[16,16,896]{2,1,0:T(8,128)(2,1)} %bitcast.5), calls=%async_computation | async-start | bytes 917504 | tf_op jit(solution)/shard_map/all_to_all | solution.py:238
  35.3 13.3 %collective-permute-done.7 = bf16[104,1280]{1,0:T(8,128)(2,1)} collective-permute-done((bf16[104,1280]{1,0:T(8,128)(2,1)}, bf16[104,1280]{1,0:T(8,128)(2,1)}, u32[]{:S(2)}, u32[]{:S(2)}) %collective-permute-start.7) | collective-permute-done | bytes 266272 | tf_op jit(solution)/shard_map/ppermute | solution.py:196
  48.6 1.7 %constant_dynamic-update-slice_fusion.1 = bf16[104,2496]{1,0:T(8,128)(2,1)} fusion(bf16[104,1280]{1,0:T(8,128)(2,1)} %collective-permute-done.7), kind=kLoop, calls=%fused_computation.23 | loop fusion | bytes 532480
  50.4 0.5 collective-permute-start.14
  50.9 1.7 %constant_dynamic-update-slice_fusion = bf16[104,2496]{1,0:T(8,128)(2,1)} fusion(bf16[104,2496]{1,0:T(8,128)(2,1)} %constant_dynamic-update-slice_fusion.1, bf16[104,1216]{1,0:T(8,128)(2,1)} %collective-permute-done.8), kind=kLoop, calls=%fused_computation.22 | loop fusion | bytes 532480 | tf_op jit(solution)/shard_map/concatenate | solution.py:198
  52.5 0.0 collective-permute-start.9
  52.6 0.5 collective-permute-start.15
  53.1 2.8 %pad_maximum_fusion = bf16[416,2496]{1,0:T(8,128)(2,1)} fusion(bf16[104,2496]{1,0:T(8,128)(2,1)} %constant_dynamic-update-slice_fusion, bf16[104,2496]{1,0:T(8,128)(2,1)} %copy-done.5, bf16[104,2496]{1,0:T(8,128)(2,1)S(1)} %collective-permute-done.2, bf16[104,2496]{1,0:T(8,128)(2,1)} %param.16), kind=kLoop, calls=%fused_computation.4 | loop fusion | flops 8306688 | bytes 4153344 | tf_op jit(solution)/shard_map/concatenate | solution.py:259
  56.0 10.6 %collective-permute-done.14 = bf16[104,2496]{1,0:T(8,128)(2,1)} collective-permute-done((bf16[104,2496]{1,0:T(8,128)(2,1)}, bf16[104,2496]{1,0:T(8,128)(2,1)}, u32[]{:S(2)}, u32[]{:S(2)}) %collective-permute-start.14) | collective-permute-done | bytes 519200 | tf_op jit(solution)/shard_map/ppermute | solution.py:190
  66.5 1.5 %pad_maximum_fusion.1 = bf16[312,2496]{1,0:T(8,128)(2,1)S(1)} fusion(bf16[104,2496]{1,0:T(8,128)(2,1)} %collective-permute-done.13, bf16[104,2496]{1,0:T(8,128)(2,1)} %collective-permute-done.12, bf16[104,2496]{1,0:T(8,128)(2,1)} %collective-permute-done.1), kind=kLoop, calls=%fused_computation.5 | loop fusion | flops 4672512 | bytes 3115008 | tf_op jit(solution)/shard_map/concatenate | solution.py:259
  68.0 0.8 collective-permute-start.17
  68.9 0.3 collective-permute-start.18
  69.2 1.5 %pad_maximum_fusion.3 = bf16[312,2496]{1,0:T(8,128)(2,1)S(1)} fusion(bf16[104,2496]{1,0:T(8,128)(2,1)} %collective-permute-done.16, bf16[104,2496]{1,0:T(8,128)(2,1)} %collective-permute-done.15, bf16[104,2496]{1,0:T(8,128)(2,1)} %collective-permute-done.11), kind=kLoop, calls=%fused_computation.8 | loop fusion | flops 4672512 | bytes 3115008 | tf_op jit(solution)/shard_map/concatenate | solution.py:259
  70.7 0.0 copy-start.4
  70.7 1.9 %shard_map.120 = bf16[16,104,512]{2,1,0:T(8,128)(2,1)S(1)} custom-call(s32[1]{0:T(128)} %bitcast.index_ref, s32[16]{0:T(128)S(1)} %fusion.10.order_ref, bf16[16,104,1]{2,1,0:T(8,128)(2,1)S(1)} %copy.19.gain_ref, bf16[832,512]{1,0:T(8,128)(2,1)S(1)} %bitcast.28, bf16[832,512]{1,0:T(8,128)(2,1)S(1)} %collective-permute-done.4.refs_1_, ...), custom_call_target="tpu_custom_call" | custom-call | flops 1000 | bytes 1000 | tf_op jit(solution)/shard_map/pallas_call | solution.py:164
  72.6 5.0 %collective-permute-done.9 = bf16[104,2496]{1,0:T(8,128)(2,1)} collective-permute-done((bf16[104,2496]{1,0:T(8,128)(2,1)}, bf16[104,2496]{1,0:T(8,128)(2,1)}, u32[]{:S(2)}, u32[]{:S(2)}) %collective-permute-start.9) | collective-permute-done | bytes 519200 | tf_op jit(solution)/shard_map/ppermute | solution.py:190
  77.6 0.1 fusion.14
  77.7 1.6 %fusion.15 = f32[512,2496]{0,1:T(8,128)S(1)} fusion(bf16[416,512]{1,0:T(8,128)(2,1)S(1)} %bitcast.30, bf16[416,2496]{1,0:T(8,128)(2,1)S(1)} %copy-done.4), kind=kOutput, calls=%fused_computation.48 | convolution fusion | flops 1063256064 | bytes 7614464 | tf_op jit(solution)/shard_map/dot_general | solution.py:266
  79.3 1.6 %convolution_add_fusion.2 = f32[512,2496]{0,1:T(8,128)S(1)} fusion(f32[512,2496]{0,1:T(8,128)S(1)} %fusion.15, bf16[312,512]{1,0:T(8,128)(2,1)S(1)} %bitcast.33, bf16[312,2496]{1,0:T(8,128)(2,1)S(1)} %pad_maximum_fusion.1), kind=kOutput, calls=%fused_computation.3 | convolution fusion | flops 798720000 | bytes 12100608 | tf_op jit(solution)/shard_map/dot_general | solution.py:266
  80.9 1.9 %collective-permute-done.17 = bf16[104,2496]{1,0:T(8,128)(2,1)S(1)} collective-permute-done((bf16[104,2496]{1,0:T(8,128)(2,1)}, bf16[104,2496]{1,0:T(8,128)(2,1)S(1)}, u32[]{:S(2)}, u32[]{:S(2)}) %collective-permute-start.17) | collective-permute-done | bytes 519200 | tf_op jit(solution)/shard_map/ppermute | solution.py:193
  82.8 0.3 collective-permute-done.18
  83.1 1.2 %pad_maximum_fusion.2 = bf16[312,2496]{1,0:T(8,128)(2,1)S(1)} fusion(bf16[104,2496]{1,0:T(8,128)(2,1)S(1)} %collective-permute-done.18, bf16[104,2496]{1,0:T(8,128)(2,1)S(1)} %collective-permute-done.17, bf16[104,2496]{1,0:T(8,128)(2,1)} %collective-permute-done.14), kind=kLoop, calls=%fused_computation.7 | loop fusion | flops 4672512 | bytes 3115008 | tf_op jit(solution)/shard_map/concatenate | solution.py:259
  84.3 1.6 %convolution_add_fusion.1 = f32[512,2496]{0,1:T(8,128)S(1)} fusion(f32[512,2496]{0,1:T(8,128)S(1)} %convolution_add_fusion.2, bf16[312,512]{1,0:T(8,128)(2,1)S(1)} %bitcast.32, bf16[312,2496]{1,0:T(8,128)(2,1)S(1)} %pad_maximum_fusion.3), kind=kOutput, calls=%fused_computation.2 | convolution fusion | flops 798720000 | bytes 12100608 | tf_op jit(solution)/shard_map/dot_general | solution.py:266
  85.9 1.6 %collective-permute-start.19 = (bf16[104,1280]{1,0:T(8,128)(2,1)S(1)}, bf16[104,1280]{1,0:T(8,128)(2,1)S(1)}, u32[]{:S(2)}, u32[]{:S(2)}) collective-permute-start(bf16[104,1280]{1,0:T(8,128)(2,1)S(1)} %slice.31), channel_id=1, source_target_pairs={{0,2},{2,0},{4,6},{6,4},{8,10},{10,8},{12,14},{14,12},{16,18},{18,... | collective-permute-start | bytes 798728 | tf_op jit(solution)/shard_map/ppermute | solution.py:196
  87.5 0.3 collective-permute-start.20
  87.8 0.0 collective-permute-start.10
  87.8 1.6 %convolution_add_fusion = f32[512,2496]{0,1:T(8,128)S(1)} fusion(f32[512,2496]{0,1:T(8,128)S(1)} %convolution_add_fusion.1, bf16[312,512]{1,0:T(8,128)(2,1)S(1)} %bitcast.31, bf16[312,2496]{1,0:T(8,128)(2,1)S(1)} %pad_maximum_fusion.2), kind=kOutput, calls=%fused_computation.1 | convolution fusion | flops 798720000 | bytes 12100608 | tf_op jit(solution)/shard_map/dot_general | solution.py:266
  89.4 5.5 %collective-permute-done.20 = bf16[104,1216]{1,0:T(8,128)(2,1)S(1)} collective-permute-done((bf16[104,1216]{1,0:T(8,128)(2,1)S(1)}, bf16[104,1216]{1,0:T(8,128)(2,1)S(1)}, u32[]{:S(2)}, u32[]{:S(2)}) %collective-permute-start.20) | collective-permute-done | bytes 252960 | tf_op jit(solution)/shard_map/ppermute | solution.py:197
  94.9 7.2 %collective-permute-done.10 = bf16[104,2496]{1,0:T(8,128)(2,1)S(1)} collective-permute-done((bf16[104,2496]{1,0:T(8,128)(2,1)}, bf16[104,2496]{1,0:T(8,128)(2,1)S(1)}, u32[]{:S(2)}, u32[]{:S(2)}) %collective-permute-start.10) | collective-permute-done | bytes 519200 | tf_op jit(solution)/shard_map/ppermute | solution.py:190
  102.1 1.2 %maximum_maximum_fusion = bf16[312,2496]{1,0:T(8,128)(2,1)S(1)} fusion(bf16[104,1216]{1,0:T(8,128)(2,1)S(1)} %collective-permute-done.20, bf16[104,1280]{1,0:T(8,128)(2,1)S(1)} %collective-permute-done.19, bf16[104,2496]{1,0:T(8,128)(2,1)S(1)} %collective-permute-done.10, bf16[104,2496]{1,0:T(8,128)(2,1)} %collective-permute-done.9), kind=kLoop, calls=%fused_computation.6 | loop fusion | flops 6230016 | bytes 3115008 | tf_op jit(solution)/shard_map/concatenate | solution.py:259
  103.3 3.1 %select_convert_fusion = bf16[512,2496]{0,1:T(8,128)(2,1)} fusion(f32[512,2496]{0,1:T(8,128)S(1)} %convolution_add_fusion, bf16[312,512]{1,0:T(8,128)(2,1)S(1)} %bitcast.29, bf16[312,2496]{1,0:T(8,128)(2,1)S(1)} %maximum_maximum_fusion, pred[512]{0:T(512)(128)(4,1)S(1)} %fusion.8), kind=kOutput, calls=%fused_computation | convolution fusion | flops 801275904 | bytes 9545216 | tf_op jit(solution)/shard_map/dot_general | solution.py:266
  (35 shorter events, 0.2 us)
Async XLA Ops:
  0.0 20.3 %collective-permute-start.1 = (bf16[104,2496]{1,0:T(8,128)(2,1)}, bf16[104,2496]{1,0:T(8,128)(2,1)}, u32[]{:S(2)}, u32[]{:S(2)}) collective-permute-start(bf16[104,2496]{1,0:T(8,128)(2,1)} %param.16), channel_id=1, source_target_pairs={{0,8},{2,10},{4,12},{6,14},{8,24},{10,26},{12,28},{14,30},{16,0},{... | collective-permute-start | bytes 1557512 | tf_op jit(solution)/shard_map/ppermute | solution.py:190
  3.0 17.2 %collective-permute-start.2 = (bf16[104,2496]{1,0:T(8,128)(2,1)}, bf16[104,2496]{1,0:T(8,128)(2,1)S(1)}, u32[]{:S(2)}, u32[]{:S(2)}) collective-permute-start(bf16[104,2496]{1,0:T(8,128)(2,1)} %param.16), channel_id=1, source_target_pairs={{0,2},{2,0},{4,6},{6,4},{8,10},{10,8},{12,14},{14,12},{16,18},{18,... | collective-permute-start | bytes 1557512 | tf_op jit(solution)/shard_map/ppermute | solution.py:193
  4.5 15.8 %collective-permute-start.3 = (bf16[104,2496]{1,0:T(8,128)(2,1)}, bf16[104,2496]{1,0:T(8,128)(2,1)S(1)}, u32[]{:S(2)}, u32[]{:S(2)}) collective-permute-start(bf16[104,2496]{1,0:T(8,128)(2,1)} %param.16), channel_id=1, source_target_pairs={{0,4},{2,6},{4,0},{6,2},{8,12},{10,14},{12,8},{14,10},{16,20},{18,... | collective-permute-start | bytes 1557512 | tf_op jit(solution)/shard_map/ppermute | solution.py:193
  6.0 1.1 %copy-start.1 = (bf16[448,832]{1,0:T(8,128)(2,1)S(1)}, bf16[448,832]{1,0:T(8,128)(2,1)}, u32[]{:S(2)}) copy-start(bf16[448,832]{1,0:T(8,128)(2,1)} %patches_ref.3) | copy-start | bytes 2236420
  7.5 3.9 %collective-permute-start = (f32[448,256]{1,0:T(8,128)S(1)}, f32[448,256]{1,0:T(8,128)S(1)}, u32[]{:S(2)}, u32[]{:S(2)}) collective-permute-start(f32[448,256]{1,0:T(8,128)S(1)} %shard_map.118.refs_0_), channel_id=1, source_target_pairs={{0,1},{1,0},{2,3},{3,2},{4,5},{5,4},{6,7},{7,6},{8,9},{9,8},{10,11... | collective-permute-start | bytes 1376264 | tf_op jit(solution)/shard_map/ppermute | solution.py:26
  11.3 4.1 %copy-start = (bf16[4,832,1664]{2,1,0:T(8,128)(2,1)S(1)}, bf16[4,832,1664]{2,1,0:T(8,128)(2,1)}, u32[]{:S(2)}) copy-start(bf16[4,832,1664]{2,1,0:T(8,128)(2,1)} %refs_2_.1) | copy-start | bytes 33226756
  15.5 1.1 %copy-start.2 = (bf16[448,832]{1,0:T(8,128)(2,1)S(1)}, bf16[448,832]{1,0:T(8,128)(2,1)}, u32[]{:S(2)}) copy-start(bf16[448,832]{1,0:T(8,128)(2,1)} %patches_ref.3) | copy-start | bytes 2236420
  16.6 5.2 %copy-start.6 = (s32[2]{0:T(128)S(1)}, s32[2]{0:T(128)}, u32[]{:S(2)}) copy-start(s32[2]{0:T(128)} %param.18) | copy-start | bytes 28
  20.2 28.4 %copy-start.3 = (bf16[512,832]{0,1:T(8,128)(2,1)S(1)}, bf16[512,832]{0,1:T(8,128)(2,1)}, u32[]{:S(2)}) copy-start(bf16[512,832]{0,1:T(8,128)(2,1)} %param.14) | copy-start | bytes 2555908
  20.3 28.3 %copy-start.5 = (bf16[104,2496]{1,0:T(8,128)(2,1)}, bf16[104,2496]{1,0:T(8,128)(2,1)S(1)}, u32[]{:S(2)}) copy-start(bf16[104,2496]{1,0:T(8,128)(2,1)S(1)} %collective-permute-done.3) | copy-start | bytes 1557508
  21.2 7.7 %collective-permute-start.5 = (f32[112,832]{1,0:T(8,128)}, f32[112,832]{1,0:T(8,128)S(1)}, u32[]{:S(2)}, u32[]{:S(2)}) collective-permute-start(f32[112,832]{1,0:T(8,128)} %constant_dynamic-slice_fusion.1), channel_id=1, source_target_pairs={{0,1},{1,0},{2,3},{3,2},{4,5},{5,4},{6,7},{7,6},{8,9},{9,8},{10,11... | collective-permute-start | bytes 1118216 | tf_op jit(solution)/shard_map/ppermute | solution.py:26
  21.9 28.4 %collective-permute-start.11 = (bf16[104,2496]{1,0:T(8,128)(2,1)}, bf16[104,2496]{1,0:T(8,128)(2,1)}, u32[]{:S(2)}, u32[]{:S(2)}) collective-permute-start(bf16[104,2496]{1,0:T(8,128)(2,1)} %collective-permute-done.1), channel_id=1, source_target_pairs={{0,8},{2,10},{4,12},{6,14},{8,24},{10,26},{12,28},{14,30},{16,0},{... | collective-permute-start | bytes 1557512 | tf_op jit(solution)/shard_map/ppermute | solution.py:190
  24.6 25.8 %collective-permute-start.12 = (bf16[104,2496]{1,0:T(8,128)(2,1)}, bf16[104,2496]{1,0:T(8,128)(2,1)}, u32[]{:S(2)}, u32[]{:S(2)}) collective-permute-start(bf16[104,2496]{1,0:T(8,128)(2,1)} %collective-permute-done.1), channel_id=1, source_target_pairs={{0,2},{2,0},{4,6},{6,4},{8,10},{10,8},{12,14},{14,12},{16,18},{18,... | collective-permute-start | bytes 1557512 | tf_op jit(solution)/shard_map/ppermute | solution.py:193
  25.1 25.3 %collective-permute-start.13 = (bf16[104,2496]{1,0:T(8,128)(2,1)}, bf16[104,2496]{1,0:T(8,128)(2,1)}, u32[]{:S(2)}, u32[]{:S(2)}) collective-permute-start(bf16[104,2496]{1,0:T(8,128)(2,1)} %collective-permute-done.1), channel_id=1, source_target_pairs={{0,4},{2,6},{4,0},{6,2},{8,12},{10,14},{12,8},{14,10},{16,20},{18,... | collective-permute-start | bytes 1557512 | tf_op jit(solution)/shard_map/ppermute | solution.py:193
  26.7 21.9 %collective-permute-start.7 = (bf16[104,1280]{1,0:T(8,128)(2,1)}, bf16[104,1280]{1,0:T(8,128)(2,1)}, u32[]{:S(2)}, u32[]{:S(2)}) collective-permute-start(bf16[104,1280]{1,0:T(8,128)(2,1)} %slice.27), channel_id=1, source_target_pairs={{0,2},{2,0},{4,6},{6,4},{8,10},{10,8},{12,14},{14,12},{16,18},{18,... | collective-permute-start | bytes 798728 | tf_op jit(solution)/shard_map/ppermute | solution.py:196
  28.9 21.9 %collective-permute-start.8 = (bf16[104,1216]{1,0:T(8,128)(2,1)}, bf16[104,1216]{1,0:T(8,128)(2,1)}, u32[]{:S(2)}, u32[]{:S(2)}) collective-permute-start(bf16[104,1216]{1,0:T(8,128)(2,1)} %slice.28), channel_id=1, source_target_pairs={{0,4},{2,6},{4,0},{6,2},{8,12},{10,14},{12,8},{14,10},{16,20},{18,... | collective-permute-start | bytes 758792 | tf_op jit(solution)/shard_map/ppermute | solution.py:197
  31.7 34.8 %all-to-all-start = ((bf16[16,16,896]{2,1,0:T(8,128)(2,1)}), bf16[16,16,896]{2,1,0:T(8,128)(2,1)S(1)}, u32[]{:S(2)}, u32[]{:S(2)}) async-start(bf16[16,16,896]{2,1,0:T(8,128)(2,1)} %bitcast.5), calls=%async_computation | async-start | bytes 917504 | tf_op jit(solution)/shard_map/all_to_all | solution.py:238
  48.6 22.0 %collective-permute-start.4 = (bf16[832,512]{1,0:T(8,128)(2,1)S(1)}, bf16[832,512]{1,0:T(8,128)(2,1)S(1)}, u32[]{:S(2)}, u32[]{:S(2)}) collective-permute-start(bf16[832,512]{1,0:T(8,128)(2,1)S(1)} %bitcast.27), channel_id=1, source_target_pairs={{0,1},{1,0},{2,3},{3,2},{4,5},{5,4},{6,7},{7,6},{8,9},{9,8},{10,11... | collective-permute-start | bytes 2555912 | tf_op jit(solution)/shard_map/ppermute | solution.py:26
  50.4 16.2 %collective-permute-start.14 = (bf16[104,2496]{1,0:T(8,128)(2,1)}, bf16[104,2496]{1,0:T(8,128)(2,1)}, u32[]{:S(2)}, u32[]{:S(2)}) collective-permute-start(bf16[104,2496]{1,0:T(8,128)(2,1)} %collective-permute-done.11), channel_id=1, source_target_pairs={{0,8},{2,10},{4,12},{6,14},{8,24},{10,26},{12,28},{14,30},{16,0},{... | collective-permute-start | bytes 1557512 | tf_op jit(solution)/shard_map/ppermute | solution.py:190
  52.5 25.0 %collective-permute-start.9 = (bf16[104,2496]{1,0:T(8,128)(2,1)}, bf16[104,2496]{1,0:T(8,128)(2,1)}, u32[]{:S(2)}, u32[]{:S(2)}) collective-permute-start(bf16[104,2496]{1,0:T(8,128)(2,1)} %constant_dynamic-update-slice_fusion), channel_id=1, source_target_pairs={{0,8},{2,10},{4,12},{6,14},{8,24},{10,26},{12,28},{14,30},{16,0},{... | collective-permute-start | bytes 1557512 | tf_op jit(solution)/shard_map/ppermute | solution.py:190
  52.6 15.5 %collective-permute-start.15 = (bf16[104,2496]{1,0:T(8,128)(2,1)}, bf16[104,2496]{1,0:T(8,128)(2,1)}, u32[]{:S(2)}, u32[]{:S(2)}) collective-permute-start(bf16[104,2496]{1,0:T(8,128)(2,1)} %collective-permute-done.11), channel_id=1, source_target_pairs={{0,2},{2,0},{4,6},{6,4},{8,10},{10,8},{12,14},{14,12},{16,18},{18,... | collective-permute-start | bytes 1557512 | tf_op jit(solution)/shard_map/ppermute | solution.py:193
  53.1 14.9 %collective-permute-start.16 = (bf16[104,2496]{1,0:T(8,128)(2,1)}, bf16[104,2496]{1,0:T(8,128)(2,1)}, u32[]{:S(2)}, u32[]{:S(2)}) collective-permute-start(bf16[104,2496]{1,0:T(8,128)(2,1)} %collective-permute-done.11), channel_id=1, source_target_pairs={{0,4},{2,6},{4,0},{6,2},{8,12},{10,14},{12,8},{14,10},{16,20},{18,... | collective-permute-start | bytes 1557512 | tf_op jit(solution)/shard_map/ppermute | solution.py:193
  66.5 4.1 %collective-permute-start.6 = (bf16[256,896]{1,0:T(8,128)(2,1)S(1)}, bf16[256,896]{1,0:T(8,128)(2,1)S(1)}, u32[]{:S(2)}, u32[]{:S(2)}) collective-permute-start(bf16[256,896]{1,0:T(8,128)(2,1)S(1)} %bitcast.25), channel_id=1, source_target_pairs={{0,1},{1,0},{2,3},{3,2},{4,5},{5,4},{6,7},{7,6},{8,9},{9,8},{10,11... | collective-permute-start | bytes 1376264 | tf_op jit(solution)/shard_map/ppermute | solution.py:26
  68.0 14.8 %collective-permute-start.17 = (bf16[104,2496]{1,0:T(8,128)(2,1)}, bf16[104,2496]{1,0:T(8,128)(2,1)S(1)}, u32[]{:S(2)}, u32[]{:S(2)}) collective-permute-start(bf16[104,2496]{1,0:T(8,128)(2,1)} %collective-permute-done.14), channel_id=1, source_target_pairs={{0,2},{2,0},{4,6},{6,4},{8,10},{10,8},{12,14},{14,12},{16,18},{18,... | collective-permute-start | bytes 1557512 | tf_op jit(solution)/shard_map/ppermute | solution.py:193
  68.9 14.2 %collective-permute-start.18 = (bf16[104,2496]{1,0:T(8,128)(2,1)}, bf16[104,2496]{1,0:T(8,128)(2,1)S(1)}, u32[]{:S(2)}, u32[]{:S(2)}) collective-permute-start(bf16[104,2496]{1,0:T(8,128)(2,1)} %collective-permute-done.14), channel_id=1, source_target_pairs={{0,4},{2,6},{4,0},{6,2},{8,12},{10,14},{12,8},{14,10},{16,20},{18,... | collective-permute-start | bytes 1557512 | tf_op jit(solution)/shard_map/ppermute | solution.py:193
  70.7 7.0 %copy-start.4 = (bf16[416,2496]{1,0:T(8,128)(2,1)S(1)}, bf16[416,2496]{1,0:T(8,128)(2,1)}, u32[]{:S(2)}) copy-start(bf16[416,2496]{1,0:T(8,128)(2,1)} %pad_maximum_fusion) | copy-start | bytes 6230020
  85.9 9.0 %collective-permute-start.19 = (bf16[104,1280]{1,0:T(8,128)(2,1)S(1)}, bf16[104,1280]{1,0:T(8,128)(2,1)S(1)}, u32[]{:S(2)}, u32[]{:S(2)}) collective-permute-start(bf16[104,1280]{1,0:T(8,128)(2,1)S(1)} %slice.31), channel_id=1, source_target_pairs={{0,2},{2,0},{4,6},{6,4},{8,10},{10,8},{12,14},{14,12},{16,18},{18,... | collective-permute-start | bytes 798728 | tf_op jit(solution)/shard_map/ppermute | solution.py:196
  87.5 7.4 %collective-permute-start.20 = (bf16[104,1216]{1,0:T(8,128)(2,1)S(1)}, bf16[104,1216]{1,0:T(8,128)(2,1)S(1)}, u32[]{:S(2)}, u32[]{:S(2)}) collective-permute-start(bf16[104,1216]{1,0:T(8,128)(2,1)S(1)} %slice.32), channel_id=1, source_target_pairs={{0,4},{2,6},{4,0},{6,2},{8,12},{10,14},{12,8},{14,10},{16,20},{18,... | collective-permute-start | bytes 758792 | tf_op jit(solution)/shard_map/ppermute | solution.py:197
  87.8 14.3 %collective-permute-start.10 = (bf16[104,2496]{1,0:T(8,128)(2,1)}, bf16[104,2496]{1,0:T(8,128)(2,1)S(1)}, u32[]{:S(2)}, u32[]{:S(2)}) collective-permute-start(bf16[104,2496]{1,0:T(8,128)(2,1)} %collective-permute-done.9), channel_id=1, source_target_pairs={{0,8},{2,10},{4,12},{6,14},{8,24},{10,26},{12,28},{14,30},{16,0},{... | collective-permute-start | bytes 1557512 | tf_op jit(solution)/shard_map/ppermute | solution.py:190

commit v16 on v15

--- a/solution.py
+++ b/solution.py
@@ -245,15 +245,16 @@
     images = [arrived] + [tp_shift(arrived, n_tp, d) for d in range(1, n_tp)]
     blocks = combine(tp_index, order, texts, images, gain_column)
 
+    held[3], corners[0] = tie(held[3], corners[0])
     corners.append(along_line(corners[0]))
-    blocks, corners[1] = tie(blocks, corners[1])
     held[3], sides[2] = tie(held[3], sides[2])
     sides.append(to_sides(held[3]))
     for step in range(4, lines):
         held.append(along_line(held[step - 1]))
         sides.append(to_sides(held[step]))
-    for step in range(2, lines - 1):
+    for step in range(2, lines - 2):
         corners.append(along_line(corners[step - 1]))
+    corners.append(to_corner(*sides[-2]))
 
     def add_product(total, first, weights):
         weight = jnp.concatenate(weights, axis=0)

time: 107 us -> 91.9 us (0.86)
  waiting for transfers between devices: 43.8 us -> 25.3 us
  starting transfers between devices: 20.9 us -> 25.7 us
  local copies, waits for them, and re-layouts: 15.7 us -> 14.4 us
    ppermute x5 -> x4, waiting for transfers between devices: 22.7 us -> 7.6 us  [along_line(): return lax.ppermute(block, 'req', line_perm)]
    ppermute x2 -> x3, waiting for transfers between devices: 13.3 us -> 0.71 us  [to_corner(): left = lax.ppermute(by_y[:, :cut], 'req', x_perm)]
    ppermute x4, waiting for transfers between devices: 1.94 us -> 7.07 us  [to_sides(): lax.ppermute(block, 'req', x_perm)]
    ppermute x4, waiting for transfers between devices: 0.26 us -> 3.77 us  [to_sides(): lax.ppermute(block, 'req', y_perm)]
    concatenate x5, other arithmetic: 8.14 us -> 6.05 us  [add_product(): weight = jnp.concatenate(weights, axis=0)]
    ppermute x2 -> x3, starting transfers between devices: 1.84 us -> 3.75 us  [to_corner(): right = lax.ppermute(by_x[:, cut:], 'req', y_perm)]
    ppermute x4, starting transfers between devices: 3.38 us -> 5.07 us  [to_sides(): lax.ppermute(block, 'req', x_perm)]
    concatenate x1 -> x0, local copies, waits for them, and re-layouts: 1.67 us -> none  [to_corner(): return jnp.concatenate([left, right], axis=1)]
  transfers between devices with their start and end apart: 22 -> 23, of which waited for: 7 -> 12; matrix products, arithmetic and copies ran while one was open for 20% -> 25% of each run, Pallas kernels for 5% -> 6%
where the time goes in v16:
time: 91.9 us; the launch traced here: 91.2 us
  starting transfers between devices  25.7 us (28%)
  waiting for transfers between devices  25.3 us (28%)
  local copies, waits for them, and re-layouts  14.4 us (16%)
  matrix products  10.3 us (11%)
  other arithmetic  9.28 us (10%)
  Pallas kernels  5.79 us (6%)
    dot_general x5, matrix products, add_product(): lax.dot_general(source, weight, (((0,), (0,)), ((), ())), preferred_eleme...  9.25 us
    ppermute x4, waiting for transfers between devices, along_line(): return lax.ppermute(block, 'req', line_perm)  7.6 us
    unnamed x32, local copies, waits for them, and re-layouts  7.27 us
    ppermute x4, waiting for transfers between devices, to_sides(): lax.ppermute(block, 'req', x_perm)  7.07 us
    ppermute x4, starting transfers between devices, along_line(): return lax.ppermute(block, 'req', line_perm)  6.3 us
    ppermute x3, waiting for transfers between devices, to_corner(): right = lax.ppermute(by_x[:, cut:], 'req', y_perm)  6.18 us
    concatenate x5, other arithmetic, add_product(): weight = jnp.concatenate(weights, axis=0)  6.05 us
    ppermute x4, starting transfers between devices, to_sides(): lax.ppermute(block, 'req', x_perm)  5.07 us
  transfers between devices with their start and end apart: 23, of which 12 were waited for; matrix products, arithmetic and copies ran while one was open for 25% of the time, Pallas kernels for 6%

profile of v16, /device:TPU:0, one launch (start us, length us, event | category | flops | bytes accessed | tf_op | source)
XLA Modules:
  0.0 91.2 jit_solution(11721347418776560718)
XLA Ops:
  0.0 3.0 %collective-permute-start.1 = (bf16[104,2496]{1,0:T(8,128)(2,1)}, bf16[104,2496]{1,0:T(8,128)(2,1)}, u32[]{:S(2)}, u32[]{:S(2)}) collective-permute-start(bf16[104,2496]{1,0:T(8,128)(2,1)} %param.16), channel_id=1, source_target_pairs={{0,8},{2,10},{4,12},{6,14},{8,24},{10,26},{12,28},{14,30},{16,0},{... | collective-permute-start | bytes 1557512 | tf_op jit(solution)/shard_map/ppermute | solution.py:190
  3.0 1.5 %collective-permute-start.2 = (bf16[104,2496]{1,0:T(8,128)(2,1)}, bf16[104,2496]{1,0:T(8,128)(2,1)S(1)}, u32[]{:S(2)}, u32[]{:S(2)}) collective-permute-start(bf16[104,2496]{1,0:T(8,128)(2,1)} %param.16), channel_id=1, source_target_pairs={{0,2},{2,0},{4,6},{6,4},{8,10},{10,8},{12,14},{14,12},{16,18},{18,... | collective-permute-start | bytes 1557512 | tf_op jit(solution)/shard_map/ppermute | solution.py:193
  4.5 1.5 %collective-permute-start.3 = (bf16[104,2496]{1,0:T(8,128)(2,1)}, bf16[104,2496]{1,0:T(8,128)(2,1)S(1)}, u32[]{:S(2)}, u32[]{:S(2)}) collective-permute-start(bf16[104,2496]{1,0:T(8,128)(2,1)} %param.16), channel_id=1, source_target_pairs={{0,4},{2,6},{4,0},{6,2},{8,12},{10,14},{12,8},{14,10},{16,20},{18,... | collective-permute-start | bytes 1557512 | tf_op jit(solution)/shard_map/ppermute | solution.py:193
  6.0 1.1 %copy-done.1 = bf16[448,832]{1,0:T(8,128)(2,1)S(1)} copy-done((bf16[448,832]{1,0:T(8,128)(2,1)S(1)}, bf16[448,832]{1,0:T(8,128)(2,1)}, u32[]{:S(2)}) %copy-start.1) | copy-done | bytes 745496
  7.2 0.3 shard_map.118.refs_0_
  7.5 0.7 convert_bitcast_fusion.1
  8.2 0.7 fusion.10.order_ref
  8.9 0.7 stack.22
  9.6 0.7 stack.21
  10.3 0.8 reshape.52
  11.1 0.2 convert_reduce_fusion
  11.4 4.1 %copy-done = bf16[4,832,1664]{2,1,0:T(8,128)(2,1)S(1)} copy-done((bf16[4,832,1664]{2,1,0:T(8,128)(2,1)S(1)}, bf16[4,832,1664]{2,1,0:T(8,128)(2,1)}, u32[]{:S(2)}) %copy-start) | copy-done | bytes 11075608
  15.5 1.1 %copy-done.2 = bf16[448,832]{1,0:T(8,128)(2,1)S(1)} copy-done((bf16[448,832]{1,0:T(8,128)(2,1)S(1)}, bf16[448,832]{1,0:T(8,128)(2,1)}, u32[]{:S(2)}) %copy-start.2) | copy-done | bytes 745496
  16.6 3.6 %shard_map.119 = f32[112,1664]{1,0:T(8,128)S(1)} custom-call(bf16[448,832]{1,0:T(8,128)(2,1)S(1)} %copy-done.2, bf16[2,832]{1,0:T(2,128)(2,1)S(1)} %pad_maximum_fusion.5.gain_bias_ref, f32[448,256]{1,0:T(8,128)S(1)} %shard_map.118.refs_0_, f32[448,256]{1,0:T(8,128)S(1)} %collective-permute-done.refs_1_, bf16[4,832,1664]{2,1,0:T(8,128)(2,1)S(1)} %copy-done), custom_call_target="tpu_custom_call" | custom-call | flops 1000 | bytes 1000 | tf_op jit(solution)/shard_map/pallas_call | solution.py:112
  20.3 0.9 %constant_dynamic-slice_fusion.1 = f32[112,832]{1,0:T(8,128)} fusion(f32[112,1664]{1,0:T(8,128)S(1)} %shard_map.119, s32[]{:T(128)S(6)} %select_n.28), kind=kLoop, calls=%fused_computation.38 | loop fusion | bytes 745476 | tf_op jit(solution)/shard_map/dynamic_slice | solution.py:34
  21.3 0.5 collective-permute-start.16
  21.9 2.6 %collective-permute-start.4 = (bf16[104,2496]{1,0:T(8,128)(2,1)}, bf16[104,2496]{1,0:T(8,128)(2,1)S(1)}, u32[]{:S(2)}, u32[]{:S(2)}) collective-permute-start(bf16[104,2496]{1,0:T(8,128)(2,1)} %collective-permute-done.1), channel_id=1, source_target_pairs={{0,8},{2,10},{4,12},{6,14},{8,24},{10,26},{12,28},{14,30},{16,0},{... | collective-permute-start | bytes 1557512 | tf_op jit(solution)/shard_map/ppermute | solution.py:190
  24.5 0.5 collective-permute-start.5
  25.1 0.5 collective-permute-start.6
  25.6 0.1 copy.18
  25.7 0.7 slice.34
  26.4 1.5 %collective-permute-start.9 = (bf16[104,1216]{1,0:T(8,128)(2,1)}, bf16[104,1216]{1,0:T(8,128)(2,1)}, u32[]{:S(2)}, u32[]{:S(2)}) collective-permute-start(bf16[104,1216]{1,0:T(8,128)(2,1)} %slice.34), channel_id=1, source_target_pairs={{0,4},{2,6},{4,0},{6,2},{8,12},{10,14},{12,8},{14,10},{16,20},{18,... | collective-permute-start | bytes 758792 | tf_op jit(solution)/shard_map/ppermute | solution.py:197
  28.0 1.6 %collective-permute-start.8 = (bf16[104,1280]{1,0:T(8,128)(2,1)S(1)}, bf16[104,1280]{1,0:T(8,128)(2,1)}, u32[]{:S(2)}, u32[]{:S(2)}) collective-permute-start(bf16[104,1280]{1,0:T(8,128)(2,1)S(1)} %slice.33), channel_id=1, source_target_pairs={{0,2},{2,0},{4,6},{6,4},{8,10},{10,8},{12,14},{14,12},{16,18},{18,... | collective-permute-start | bytes 798728 | tf_op jit(solution)/shard_map/ppermute | solution.py:196
  29.5 1.2 %add_convert_fusion = bf16[112,832]{1,0:T(8,128)(2,1)S(1)} fusion(f32[112,832]{1,0:T(8,128)} %collective-permute-done.16, f32[112,1664]{1,0:T(8,128)S(1)} %shard_map.119, s32[]{:T(128)S(6)} %select_n.26), kind=kLoop, calls=%fused_computation.11 | loop fusion | flops 186368 | bytes 931844 | tf_op jit(solution)/shard_map/convert_element_type | solution.py:229
  30.7 1.1 %convolution_convert_fusion = bf16[256,896]{1,0:T(8,128)(2,1)} fusion(bf16[112,2]{1,0:T(8,128)(2,1)S(1)} %copy.18, bf16[112,832]{1,0:T(8,128)(2,1)S(1)} %add_convert_fusion, bf16[896]{0:T(1024)(128)(2,1)S(1)} %pad.17.clone, s32[112]{0:T(128)S(1)} %multiply_add_fusion), kind=kOutput, calls=%fused_computation.9 | convolution fusion | flops 52240384 | bytes 647808 | tf_op jit(solution)/shard_map/dot_general | solution.py:237
  31.8 3.6 %all-to-all-start = ((bf16[16,16,896]{2,1,0:T(8,128)(2,1)}), bf16[16,16,896]{2,1,0:T(8,128)(2,1)S(1)}, u32[]{:S(2)}, u32[]{:S(2)}) async-start(bf16[16,16,896]{2,1,0:T(8,128)(2,1)} %bitcast.5), calls=%async_computation | async-start | bytes 917504 | tf_op jit(solution)/shard_map/all_to_all | solution.py:238
  35.4 0.3 copy.19.gain_ref
  35.7 1.6 %collective-permute-done.4 = bf16[104,2496]{1,0:T(8,128)(2,1)S(1)} collective-permute-done((bf16[104,2496]{1,0:T(8,128)(2,1)}, bf16[104,2496]{1,0:T(8,128)(2,1)S(1)}, u32[]{:S(2)}, u32[]{:S(2)}) %collective-permute-start.4) | collective-permute-done | bytes 519200 | tf_op jit(solution)/shard_map/ppermute | solution.py:190
  37.3 0.8 copy-done.13
  38.1 2.3 %collective-permute-done.5 = bf16[104,2496]{1,0:T(8,128)(2,1)} collective-permute-done((bf16[104,2496]{1,0:T(8,128)(2,1)}, bf16[104,2496]{1,0:T(8,128)(2,1)}, u32[]{:S(2)}, u32[]{:S(2)}) %collective-permute-start.5) | collective-permute-done | bytes 519200 | tf_op jit(solution)/shard_map/ppermute | solution.py:193
  40.4 2.1 %collective-permute-done.6 = bf16[104,2496]{1,0:T(8,128)(2,1)} collective-permute-done((bf16[104,2496]{1,0:T(8,128)(2,1)}, bf16[104,2496]{1,0:T(8,128)(2,1)}, u32[]{:S(2)}, u32[]{:S(2)}) %collective-permute-start.6) | collective-permute-done | bytes 519200 | tf_op jit(solution)/shard_map/ppermute | solution.py:193
  42.5 1.6 %collective-permute-start.11 = (bf16[104,2496]{1,0:T(8,128)(2,1)}, bf16[104,2496]{1,0:T(8,128)(2,1)S(1)}, u32[]{:S(2)}, u32[]{:S(2)}) collective-permute-start(bf16[104,2496]{1,0:T(8,128)(2,1)} %copy-done.13), channel_id=1, source_target_pairs={{0,2},{2,0},{4,6},{6,4},{8,10},{10,8},{12,14},{14,12},{16,18},{18,... | collective-permute-start | bytes 1557512 | tf_op jit(solution)/shard_map/ppermute | solution.py:193
  44.1 4.3 %collective-permute-done.9 = bf16[104,1216]{1,0:T(8,128)(2,1)} collective-permute-done((bf16[104,1216]{1,0:T(8,128)(2,1)}, bf16[104,1216]{1,0:T(8,128)(2,1)}, u32[]{:S(2)}, u32[]{:S(2)}) %collective-permute-start.9) | collective-permute-done | bytes 252960 | tf_op jit(solution)/shard_map/ppermute | solution.py:197
  48.4 0.7 collective-permute-start.12
  49.1 0.1 collective-permute-done.8
  49.2 1.1 %pad_maximum_fusion.4 = bf16[104,2496]{1,0:T(8,128)(2,1)S(1)} fusion(bf16[104,1216]{1,0:T(8,128)(2,1)} %collective-permute-done.9, bf16[104,1280]{1,0:T(8,128)(2,1)} %collective-permute-done.8), kind=kLoop, calls=%fused_computation.10 | loop fusion | flops 1038336 | bytes 1038336 | tf_op jit(solution)/shard_map/concatenate | solution.py:198
  50.3 2.6 %pad_maximum_fusion.1 = bf16[312,2496]{1,0:T(8,128)(2,1)} fusion(bf16[104,2496]{1,0:T(8,128)(2,1)} %collective-permute-done.6, bf16[104,2496]{1,0:T(8,128)(2,1)} %collective-permute-done.5, bf16[104,2496]{1,0:T(8,128)(2,1)} %collective-permute-done.1), kind=kLoop, calls=%fused_computation.5 | loop fusion | flops 4672512 | bytes 3115008 | tf_op jit(solution)/shard_map/concatenate | solution.py:260
  52.9 6.0 %collective-permute-done.7 = bf16[104,2496]{1,0:T(8,128)(2,1)} collective-permute-done((bf16[104,2496]{1,0:T(8,128)(2,1)}, bf16[104,2496]{1,0:T(8,128)(2,1)}, u32[]{:S(2)}, u32[]{:S(2)}) %collective-permute-start.7) | collective-permute-done | bytes 519200 | tf_op jit(solution)/shard_map/ppermute | solution.py:190
  58.9 1.6 %collective-permute-done.11 = bf16[104,2496]{1,0:T(8,128)(2,1)S(1)} collective-permute-done((bf16[104,2496]{1,0:T(8,128)(2,1)}, bf16[104,2496]{1,0:T(8,128)(2,1)S(1)}, u32[]{:S(2)}, u32[]{:S(2)}) %collective-permute-start.11) | collective-permute-done | bytes 519200 | tf_op jit(solution)/shard_map/ppermute | solution.py:193
  60.5 0.3 collective-permute-done.12
  60.8 1.5 %collective-permute-start.18 = (bf16[104,2496]{1,0:T(8,128)(2,1)}, bf16[104,2496]{1,0:T(8,128)(2,1)}, u32[]{:S(2)}, u32[]{:S(2)}) collective-permute-start(bf16[104,2496]{1,0:T(8,128)(2,1)} %collective-permute-done.7), channel_id=1, source_target_pairs={{0,2},{2,0},{4,6},{6,4},{8,10},{10,8},{12,14},{14,12},{16,18},{18,... | collective-permute-start | bytes 1557512 | tf_op jit(solution)/shard_map/ppermute | solution.py:193
  62.3 0.5 collective-permute-start.19
  62.9 1.6 %pad_maximum_fusion.3 = bf16[312,2496]{1,0:T(8,128)(2,1)S(1)} fusion(bf16[104,2496]{1,0:T(8,128)(2,1)} %copy-done.7, bf16[104,2496]{1,0:T(8,128)(2,1)} %copy-done.5, bf16[104,2496]{1,0:T(8,128)(2,1)} %copy-done.13), kind=kLoop, calls=%fused_computation.8 | loop fusion | flops 4672512 | bytes 3115008 | tf_op jit(solution)/shard_map/concatenate | solution.py:260
  64.6 0.7 collective-permute-start.10
  65.3 0.2 pad_maximum_fusion
  65.5 1.6 %collective-permute-start.14 = (bf16[104,1216]{1,0:T(8,128)(2,1)S(1)}, bf16[104,1216]{1,0:T(8,128)(2,1)S(1)}, u32[]{:S(2)}, u32[]{:S(2)}) collective-permute-start(bf16[104,1216]{1,0:T(8,128)(2,1)S(1)} %slice.36), channel_id=1, source_target_pairs={{0,4},{2,6},{4,0},{6,2},{8,12},{10,14},{12,8},{14,10},{16,20},{18,... | collective-permute-start | bytes 758792 | tf_op jit(solution)/shard_map/ppermute | solution.py:197
  67.1 0.8 collective-permute-start.13
  67.9 1.9 %shard_map.120 = bf16[16,104,512]{2,1,0:T(8,128)(2,1)S(1)} custom-call(s32[1]{0:T(128)} %bitcast.3.index_ref, s32[16]{0:T(128)S(1)} %fusion.10.order_ref, bf16[16,104,1]{2,1,0:T(8,128)(2,1)S(1)} %copy.19.gain_ref, bf16[832,512]{1,0:T(8,128)(2,1)S(1)} %bitcast.28, bf16[832,512]{1,0:T(8,128)(2,1)S(1)} %collective-permute-done.15.refs_1_, ...), custom_call_target="tpu_custom_call" | custom-call | flops 1000 | bytes 1000 | tf_op jit(solution)/shard_map/pallas_call | solution.py:164
  69.8 0.1 fusion.14
  69.9 1.5 %fusion.15 = f32[512,2496]{0,1:T(8,128)S(1)} fusion(bf16[416,512]{1,0:T(8,128)(2,1)S(1)} %bitcast.30, bf16[416,2496]{1,0:T(8,128)(2,1)S(1)} %pad_maximum_fusion), kind=kOutput, calls=%fused_computation.47 | convolution fusion | flops 1063256064 | bytes 7614464 | tf_op jit(solution)/shard_map/dot_general | solution.py:267
  71.5 1.5 %convolution_add_fusion.2 = f32[512,2496]{0,1:T(8,128)S(1)} fusion(f32[512,2496]{0,1:T(8,128)S(1)} %fusion.15, bf16[312,512]{1,0:T(8,128)(2,1)S(1)} %bitcast.33, bf16[312,2496]{1,0:T(8,128)(2,1)S(1)} %copy-done.4), kind=kOutput, calls=%fused_computation.3 | convolution fusion | flops 798720000 | bytes 12100608 | tf_op jit(solution)/shard_map/dot_general | solution.py:267
  73.0 3.1 %collective-permute-done.18 = bf16[104,2496]{1,0:T(8,128)(2,1)} collective-permute-done((bf16[104,2496]{1,0:T(8,128)(2,1)}, bf16[104,2496]{1,0:T(8,128)(2,1)}, u32[]{:S(2)}, u32[]{:S(2)}) %collective-permute-start.18) | collective-permute-done | bytes 519200 | tf_op jit(solution)/shard_map/ppermute | solution.py:193
  76.2 1.4 %collective-permute-done.19 = bf16[104,2496]{1,0:T(8,128)(2,1)} collective-permute-done((bf16[104,2496]{1,0:T(8,128)(2,1)}, bf16[104,2496]{1,0:T(8,128)(2,1)}, u32[]{:S(2)}, u32[]{:S(2)}) %collective-permute-start.19) | collective-permute-done | bytes 519200 | tf_op jit(solution)/shard_map/ppermute | solution.py:193
  77.5 1.0 %slice.40 = bf16[104,1216]{1,0:T(8,128)(2,1)S(1)} slice(bf16[104,2496]{1,0:T(8,128)(2,1)} %collective-permute-done.18), slice={[0:104], [1280:2496]} | slice | bytes 505856 | tf_op jit(solution)/shard_map/slice | solution.py:197
  78.5 1.0 %slice.39 = bf16[104,1280]{1,0:T(8,128)(2,1)S(1)} slice(bf16[104,2496]{1,0:T(8,128)(2,1)} %collective-permute-done.19), slice={[0:104], [0:1280]} | slice | bytes 532480 | tf_op jit(solution)/shard_map/slice | solution.py:196
  79.5 1.5 %pad_maximum_fusion.2 = bf16[312,2496]{1,0:T(8,128)(2,1)S(1)} fusion(bf16[104,2496]{1,0:T(8,128)(2,1)} %collective-permute-done.19, bf16[104,2496]{1,0:T(8,128)(2,1)} %collective-permute-done.18, bf16[104,2496]{1,0:T(8,128)(2,1)} %collective-permute-done.7), kind=kLoop, calls=%fused_computation.7 | loop fusion | flops 4672512 | bytes 3115008 | tf_op jit(solution)/shard_map/concatenate | solution.py:260
  81.0 0.6 collective-permute-start.21
  81.6 0.8 collective-permute-start.20
  82.4 1.5 %convolution_add_fusion.1 = f32[512,2496]{0,1:T(8,128)S(1)} fusion(f32[512,2496]{0,1:T(8,128)S(1)} %convolution_add_fusion.2, bf16[312,512]{1,0:T(8,128)(2,1)S(1)} %bitcast.32, bf16[312,2496]{1,0:T(8,128)(2,1)S(1)} %pad_maximum_fusion.3), kind=kOutput, calls=%fused_computation.2 | convolution fusion | flops 798720000 | bytes 12100608 | tf_op jit(solution)/shard_map/dot_general | solution.py:267
  84.0 1.5 %convolution_add_fusion = f32[512,2496]{0,1:T(8,128)S(1)} fusion(f32[512,2496]{0,1:T(8,128)S(1)} %convolution_add_fusion.1, bf16[312,512]{1,0:T(8,128)(2,1)S(1)} %bitcast.31, bf16[312,2496]{1,0:T(8,128)(2,1)S(1)} %pad_maximum_fusion.2), kind=kOutput, calls=%fused_computation.1 | convolution fusion | flops 798720000 | bytes 12100608 | tf_op jit(solution)/shard_map/dot_general | solution.py:267
  85.6 1.9 %collective-permute-done.21 = bf16[104,1216]{1,0:T(8,128)(2,1)S(1)} collective-permute-done((bf16[104,1216]{1,0:T(8,128)(2,1)S(1)}, bf16[104,1216]{1,0:T(8,128)(2,1)S(1)}, u32[]{:S(2)}, u32[]{:S(2)}) %collective-permute-start.21) | collective-permute-done | bytes 252960 | tf_op jit(solution)/shard_map/ppermute | solution.py:197
  87.5 0.6 collective-permute-done.20
  88.0 0.1 maximum_maximum_fusion
  88.2 3.1 %select_convert_fusion = bf16[512,2496]{0,1:T(8,128)(2,1)} fusion(f32[512,2496]{0,1:T(8,128)S(1)} %convolution_add_fusion, bf16[312,512]{1,0:T(8,128)(2,1)S(1)} %bitcast.29, bf16[312,2496]{1,0:T(8,128)(2,1)S(1)} %maximum_maximum_fusion, pred[512]{0:T(512)(128)(4,1)S(1)} %fusion.8), kind=kOutput, calls=%fused_computation | convolution fusion | flops 801275904 | bytes 9545216 | tf_op jit(solution)/shard_map/dot_general | solution.py:267
  (56 shorter events, 0.6 us)
Async XLA Ops:
  0.0 20.3 %collective-permute-start.1 = (bf16[104,2496]{1,0:T(8,128)(2,1)}, bf16[104,2496]{1,0:T(8,128)(2,1)}, u32[]{:S(2)}, u32[]{:S(2)}) collective-permute-start(bf16[104,2496]{1,0:T(8,128)(2,1)} %param.16), channel_id=1, source_target_pairs={{0,8},{2,10},{4,12},{6,14},{8,24},{10,26},{12,28},{14,30},{16,0},{... | collective-permute-start | bytes 1557512 | tf_op jit(solution)/shard_map/ppermute | solution.py:190
  3.0 17.3 %collective-permute-start.2 = (bf16[104,2496]{1,0:T(8,128)(2,1)}, bf16[104,2496]{1,0:T(8,128)(2,1)S(1)}, u32[]{:S(2)}, u32[]{:S(2)}) collective-permute-start(bf16[104,2496]{1,0:T(8,128)(2,1)} %param.16), channel_id=1, source_target_pairs={{0,2},{2,0},{4,6},{6,4},{8,10},{10,8},{12,14},{14,12},{16,18},{18,... | collective-permute-start | bytes 1557512 | tf_op jit(solution)/shard_map/ppermute | solution.py:193
  4.5 15.8 %collective-permute-start.3 = (bf16[104,2496]{1,0:T(8,128)(2,1)}, bf16[104,2496]{1,0:T(8,128)(2,1)S(1)}, u32[]{:S(2)}, u32[]{:S(2)}) collective-permute-start(bf16[104,2496]{1,0:T(8,128)(2,1)} %param.16), channel_id=1, source_target_pairs={{0,4},{2,6},{4,0},{6,2},{8,12},{10,14},{12,8},{14,10},{16,20},{18,... | collective-permute-start | bytes 1557512 | tf_op jit(solution)/shard_map/ppermute | solution.py:193
  6.0 1.1 %copy-start.1 = (bf16[448,832]{1,0:T(8,128)(2,1)S(1)}, bf16[448,832]{1,0:T(8,128)(2,1)}, u32[]{:S(2)}) copy-start(bf16[448,832]{1,0:T(8,128)(2,1)} %patches_ref.3) | copy-start | bytes 2236420
  7.5 3.9 %collective-permute-start = (f32[448,256]{1,0:T(8,128)S(1)}, f32[448,256]{1,0:T(8,128)S(1)}, u32[]{:S(2)}, u32[]{:S(2)}) collective-permute-start(f32[448,256]{1,0:T(8,128)S(1)} %shard_map.118.refs_0_), channel_id=1, source_target_pairs={{0,1},{1,0},{2,3},{3,2},{4,5},{5,4},{6,7},{7,6},{8,9},{9,8},{10,11... | collective-permute-start | bytes 1376264 | tf_op jit(solution)/shard_map/ppermute | solution.py:26
  11.3 4.1 %copy-start = (bf16[4,832,1664]{2,1,0:T(8,128)(2,1)S(1)}, bf16[4,832,1664]{2,1,0:T(8,128)(2,1)}, u32[]{:S(2)}) copy-start(bf16[4,832,1664]{2,1,0:T(8,128)(2,1)} %refs_2_.1) | copy-start | bytes 33226756
  15.5 1.1 %copy-start.2 = (bf16[448,832]{1,0:T(8,128)(2,1)S(1)}, bf16[448,832]{1,0:T(8,128)(2,1)}, u32[]{:S(2)}) copy-start(bf16[448,832]{1,0:T(8,128)(2,1)} %patches_ref.3) | copy-start | bytes 2236420
  16.6 5.2 %copy-start.15 = (s32[2]{0:T(128)S(1)}, s32[2]{0:T(128)}, u32[]{:S(2)}) copy-start(s32[2]{0:T(128)} %param.18) | copy-start | bytes 28
  20.3 17.8 %copy-start.3 = (bf16[512,832]{0,1:T(8,128)(2,1)S(1)}, bf16[512,832]{0,1:T(8,128)(2,1)}, u32[]{:S(2)}) copy-start(bf16[512,832]{0,1:T(8,128)(2,1)} %param.14) | copy-start | bytes 2555908
  20.3 11.5 %copy-start.9 = (bf16[104,2496]{1,0:T(8,128)(2,1)}, bf16[104,2496]{1,0:T(8,128)(2,1)S(1)}, u32[]{:S(2)}) copy-start(bf16[104,2496]{1,0:T(8,128)(2,1)S(1)} %collective-permute-done.2) | copy-start | bytes 1557508
  20.3 15.1 %copy-start.11 = (bf16[104,2496]{1,0:T(8,128)(2,1)}, bf16[104,2496]{1,0:T(8,128)(2,1)S(1)}, u32[]{:S(2)}) copy-start(bf16[104,2496]{1,0:T(8,128)(2,1)S(1)} %collective-permute-done.3) | copy-start | bytes 1557508
  21.3 6.7 %collective-permute-start.16 = (f32[112,832]{1,0:T(8,128)}, f32[112,832]{1,0:T(8,128)}, u32[]{:S(2)}, u32[]{:S(2)}) collective-permute-start(f32[112,832]{1,0:T(8,128)} %constant_dynamic-slice_fusion.1), channel_id=1, source_target_pairs={{0,1},{1,0},{2,3},{3,2},{4,5},{5,4},{6,7},{7,6},{8,9},{9,8},{10,11... | collective-permute-start | bytes 1118216 | tf_op jit(solution)/shard_map/ppermute | solution.py:26
  21.9 15.4 %collective-permute-start.4 = (bf16[104,2496]{1,0:T(8,128)(2,1)}, bf16[104,2496]{1,0:T(8,128)(2,1)S(1)}, u32[]{:S(2)}, u32[]{:S(2)}) collective-permute-start(bf16[104,2496]{1,0:T(8,128)(2,1)} %collective-permute-done.1), channel_id=1, source_target_pairs={{0,8},{2,10},{4,12},{6,14},{8,24},{10,26},{12,28},{14,30},{16,0},{... | collective-permute-start | bytes 1557512 | tf_op jit(solution)/shard_map/ppermute | solution.py:190
  24.5 15.9 %collective-permute-start.5 = (bf16[104,2496]{1,0:T(8,128)(2,1)}, bf16[104,2496]{1,0:T(8,128)(2,1)}, u32[]{:S(2)}, u32[]{:S(2)}) collective-permute-start(bf16[104,2496]{1,0:T(8,128)(2,1)} %collective-permute-done.1), channel_id=1, source_target_pairs={{0,2},{2,0},{4,6},{6,4},{8,10},{10,8},{12,14},{14,12},{16,18},{18,... | collective-permute-start | bytes 1557512 | tf_op jit(solution)/shard_map/ppermute | solution.py:193
  25.1 17.5 %collective-permute-start.6 = (bf16[104,2496]{1,0:T(8,128)(2,1)}, bf16[104,2496]{1,0:T(8,128)(2,1)}, u32[]{:S(2)}, u32[]{:S(2)}) collective-permute-start(bf16[104,2496]{1,0:T(8,128)(2,1)} %collective-permute-done.1), channel_id=1, source_target_pairs={{0,4},{2,6},{4,0},{6,2},{8,12},{10,14},{12,8},{14,10},{16,20},{18,... | collective-permute-start | bytes 1557512 | tf_op jit(solution)/shard_map/ppermute | solution.py:193
  26.4 22.0 %collective-permute-start.9 = (bf16[104,1216]{1,0:T(8,128)(2,1)}, bf16[104,1216]{1,0:T(8,128)(2,1)}, u32[]{:S(2)}, u32[]{:S(2)}) collective-permute-start(bf16[104,1216]{1,0:T(8,128)(2,1)} %slice.34), channel_id=1, source_target_pairs={{0,4},{2,6},{4,0},{6,2},{8,12},{10,14},{12,8},{14,10},{16,20},{18,... | collective-permute-start | bytes 758792 | tf_op jit(solution)/shard_map/ppermute | solution.py:197
  28.0 21.2 %collective-permute-start.8 = (bf16[104,1280]{1,0:T(8,128)(2,1)S(1)}, bf16[104,1280]{1,0:T(8,128)(2,1)}, u32[]{:S(2)}, u32[]{:S(2)}) collective-permute-start(bf16[104,1280]{1,0:T(8,128)(2,1)S(1)} %slice.33), channel_id=1, source_target_pairs={{0,2},{2,0},{4,6},{6,4},{8,10},{10,8},{12,14},{14,12},{16,18},{18,... | collective-permute-start | bytes 798728 | tf_op jit(solution)/shard_map/ppermute | solution.py:196
  31.8 31.0 %all-to-all-start = ((bf16[16,16,896]{2,1,0:T(8,128)(2,1)}), bf16[16,16,896]{2,1,0:T(8,128)(2,1)S(1)}, u32[]{:S(2)}, u32[]{:S(2)}) async-start(bf16[16,16,896]{2,1,0:T(8,128)(2,1)} %bitcast.5), calls=%async_computation | async-start | bytes 917504 | tf_op jit(solution)/shard_map/all_to_all | solution.py:238
  37.3 0.8 copy-start.13
  38.1 27.4 %collective-permute-start.15 = (bf16[832,512]{1,0:T(8,128)(2,1)S(1)}, bf16[832,512]{1,0:T(8,128)(2,1)S(1)}, u32[]{:S(2)}, u32[]{:S(2)}) collective-permute-start(bf16[832,512]{1,0:T(8,128)(2,1)S(1)} %bitcast.27), channel_id=1, source_target_pairs={{0,1},{1,0},{2,3},{3,2},{4,5},{5,4},{6,7},{7,6},{8,9},{9,8},{10,11... | collective-permute-start | bytes 2555912 | tf_op jit(solution)/shard_map/ppermute | solution.py:26
  42.5 16.4 %collective-permute-start.7 = (bf16[104,2496]{1,0:T(8,128)(2,1)}, bf16[104,2496]{1,0:T(8,128)(2,1)}, u32[]{:S(2)}, u32[]{:S(2)}) collective-permute-start(bf16[104,2496]{1,0:T(8,128)(2,1)} %copy-done.13), channel_id=1, source_target_pairs={{0,8},{2,10},{4,12},{6,14},{8,24},{10,26},{12,28},{14,30},{16,0},{... | collective-permute-start | bytes 1557512 | tf_op jit(solution)/shard_map/ppermute | solution.py:190
  42.5 18.0 %collective-permute-start.11 = (bf16[104,2496]{1,0:T(8,128)(2,1)}, bf16[104,2496]{1,0:T(8,128)(2,1)S(1)}, u32[]{:S(2)}, u32[]{:S(2)}) collective-permute-start(bf16[104,2496]{1,0:T(8,128)(2,1)} %copy-done.13), channel_id=1, source_target_pairs={{0,2},{2,0},{4,6},{6,4},{8,10},{10,8},{12,14},{14,12},{16,18},{18,... | collective-permute-start | bytes 1557512 | tf_op jit(solution)/shard_map/ppermute | solution.py:193
  48.4 12.4 %collective-permute-start.12 = (bf16[104,2496]{1,0:T(8,128)(2,1)}, bf16[104,2496]{1,0:T(8,128)(2,1)S(1)}, u32[]{:S(2)}, u32[]{:S(2)}) collective-permute-start(bf16[104,2496]{1,0:T(8,128)(2,1)} %copy-done.13), channel_id=1, source_target_pairs={{0,4},{2,6},{4,0},{6,2},{8,12},{10,14},{12,8},{14,10},{16,20},{18,... | collective-permute-start | bytes 1557512 | tf_op jit(solution)/shard_map/ppermute | solution.py:193
  60.5 1.8 %copy-start.5 = (bf16[104,2496]{1,0:T(8,128)(2,1)}, bf16[104,2496]{1,0:T(8,128)(2,1)S(1)}, u32[]{:S(2)}) copy-start(bf16[104,2496]{1,0:T(8,128)(2,1)S(1)} %collective-permute-done.11) | copy-start | bytes 1557508
  60.8 1.5 %copy-start.7 = (bf16[104,2496]{1,0:T(8,128)(2,1)}, bf16[104,2496]{1,0:T(8,128)(2,1)S(1)}, u32[]{:S(2)}) copy-start(bf16[104,2496]{1,0:T(8,128)(2,1)S(1)} %collective-permute-done.12) | copy-start | bytes 1557508
  60.8 15.4 %collective-permute-start.18 = (bf16[104,2496]{1,0:T(8,128)(2,1)}, bf16[104,2496]{1,0:T(8,128)(2,1)}, u32[]{:S(2)}, u32[]{:S(2)}) collective-permute-start(bf16[104,2496]{1,0:T(8,128)(2,1)} %collective-permute-done.7), channel_id=1, source_target_pairs={{0,2},{2,0},{4,6},{6,4},{8,10},{10,8},{12,14},{14,12},{16,18},{18,... | collective-permute-start | bytes 1557512 | tf_op jit(solution)/shard_map/ppermute | solution.py:193
  62.3 15.3 %collective-permute-start.19 = (bf16[104,2496]{1,0:T(8,128)(2,1)}, bf16[104,2496]{1,0:T(8,128)(2,1)}, u32[]{:S(2)}, u32[]{:S(2)}) collective-permute-start(bf16[104,2496]{1,0:T(8,128)(2,1)} %collective-permute-done.7), channel_id=1, source_target_pairs={{0,4},{2,6},{4,0},{6,2},{8,12},{10,14},{12,8},{14,10},{16,20},{18,... | collective-permute-start | bytes 1557512 | tf_op jit(solution)/shard_map/ppermute | solution.py:193
  62.8 1.8 %copy-start.6 = (bf16[104,2496]{1,0:T(8,128)(2,1)S(1)}, bf16[104,2496]{1,0:T(8,128)(2,1)}, u32[]{:S(2)}) copy-start(bf16[104,2496]{1,0:T(8,128)(2,1)} %copy-done.5) | copy-start | bytes 1557508
  62.8 1.8 %copy-start.8 = (bf16[104,2496]{1,0:T(8,128)(2,1)S(1)}, bf16[104,2496]{1,0:T(8,128)(2,1)}, u32[]{:S(2)}) copy-start(bf16[104,2496]{1,0:T(8,128)(2,1)} %copy-done.7) | copy-start | bytes 1557508
  62.8 2.5 %copy-start.10 = (bf16[104,2496]{1,0:T(8,128)(2,1)S(1)}, bf16[104,2496]{1,0:T(8,128)(2,1)}, u32[]{:S(2)}) copy-start(bf16[104,2496]{1,0:T(8,128)(2,1)} %copy-done.9) | copy-start | bytes 1557508
  62.8 2.5 %copy-start.12 = (bf16[104,2496]{1,0:T(8,128)(2,1)S(1)}, bf16[104,2496]{1,0:T(8,128)(2,1)}, u32[]{:S(2)}) copy-start(bf16[104,2496]{1,0:T(8,128)(2,1)} %copy-done.11) | copy-start | bytes 1557508
  62.8 2.5 %copy-start.14 = (bf16[104,2496]{1,0:T(8,128)(2,1)S(1)}, bf16[104,2496]{1,0:T(8,128)(2,1)}, u32[]{:S(2)}) copy-start(bf16[104,2496]{1,0:T(8,128)(2,1)} %param.16) | copy-start | bytes 1557508
  62.8 4.3 %collective-permute-start.17 = (bf16[256,896]{1,0:T(8,128)(2,1)S(1)}, bf16[256,896]{1,0:T(8,128)(2,1)S(1)}, u32[]{:S(2)}, u32[]{:S(2)}) collective-permute-start(bf16[256,896]{1,0:T(8,128)(2,1)S(1)} %bitcast.25), channel_id=1, source_target_pairs={{0,1},{1,0},{2,3},{3,2},{4,5},{5,4},{6,7},{7,6},{8,9},{9,8},{10,11... | collective-permute-start | bytes 1376264 | tf_op jit(solution)/shard_map/ppermute | solution.py:26
  64.6 20.9 %collective-permute-start.10 = (bf16[104,2496]{1,0:T(8,128)(2,1)S(1)}, bf16[104,2496]{1,0:T(8,128)(2,1)S(1)}, u32[]{:S(2)}, u32[]{:S(2)}) collective-permute-start(bf16[104,2496]{1,0:T(8,128)(2,1)S(1)} %pad_maximum_fusion.4), channel_id=1, source_target_pairs={{0,8},{2,10},{4,12},{6,14},{8,24},{10,26},{12,28},{14,30},{16,0},{... | collective-permute-start | bytes 1557512 | tf_op jit(solution)/shard_map/ppermute | solution.py:190
  65.5 20.0 %collective-permute-start.14 = (bf16[104,1216]{1,0:T(8,128)(2,1)S(1)}, bf16[104,1216]{1,0:T(8,128)(2,1)S(1)}, u32[]{:S(2)}, u32[]{:S(2)}) collective-permute-start(bf16[104,1216]{1,0:T(8,128)(2,1)S(1)} %slice.36), channel_id=1, source_target_pairs={{0,4},{2,6},{4,0},{6,2},{8,12},{10,14},{12,8},{14,10},{16,20},{18,... | collective-permute-start | bytes 758792 | tf_op jit(solution)/shard_map/ppermute | solution.py:197
  67.1 18.5 %collective-permute-start.13 = (bf16[104,1280]{1,0:T(8,128)(2,1)S(1)}, bf16[104,1280]{1,0:T(8,128)(2,1)S(1)}, u32[]{:S(2)}, u32[]{:S(2)}) collective-permute-start(bf16[104,1280]{1,0:T(8,128)(2,1)S(1)} %slice.35), channel_id=1, source_target_pairs={{0,2},{2,0},{4,6},{6,4},{8,10},{10,8},{12,14},{14,12},{16,18},{18,... | collective-permute-start | bytes 798728 | tf_op jit(solution)/shard_map/ppermute | solution.py:196
  69.9 1.6 %copy-start.4 = (bf16[312,2496]{1,0:T(8,128)(2,1)S(1)}, bf16[312,2496]{1,0:T(8,128)(2,1)}, u32[]{:S(2)}) copy-start(bf16[312,2496]{1,0:T(8,128)(2,1)} %pad_maximum_fusion.1) | copy-start | bytes 4672516
  81.0 6.5 %collective-permute-start.21 = (bf16[104,1216]{1,0:T(8,128)(2,1)S(1)}, bf16[104,1216]{1,0:T(8,128)(2,1)S(1)}, u32[]{:S(2)}, u32[]{:S(2)}) collective-permute-start(bf16[104,1216]{1,0:T(8,128)(2,1)S(1)} %slice.40), channel_id=1, source_target_pairs={{0,4},{2,6},{4,0},{6,2},{8,12},{10,14},{12,8},{14,10},{16,20},{18,... | collective-permute-start | bytes 758792 | tf_op jit(solution)/shard_map/ppermute | solution.py:197
  81.6 6.4 %collective-permute-start.20 = (bf16[104,1280]{1,0:T(8,128)(2,1)S(1)}, bf16[104,1280]{1,0:T(8,128)(2,1)S(1)}, u32[]{:S(2)}, u32[]{:S(2)}) collective-permute-start(bf16[104,1280]{1,0:T(8,128)(2,1)S(1)} %slice.39), channel_id=1, source_target_pairs={{0,2},{2,0},{4,6},{6,4},{8,10},{10,8},{12,14},{14,12},{16,18},{18,... | collective-permute-start | bytes 798728 | tf_op jit(solution)/shard_map/ppermute | solution.py:196

commit v17 on v16

--- a/solution.py
+++ b/solution.py
@@ -77,14 +77,25 @@
     )(patches)
 
 
+def row_chunks(width):
+    chunks = [(first, 256) for first in range(0, width - 255, 256)]
+    rest = width % 256
+    if rest:
+        chunks.append((width - rest, rest))
+    if any(first % size for first, size in chunks):
+        return [(0, width)]
+    return chunks
+
+
 def merge(patches, stats, gain_bias, merge_weight):
     rows, width = patches.shape
     window, _, features = merge_weight.shape
     tokens = rows // window
     count = len(stats)
+    chunks = row_chunks(width)
 
     def body(patches_ref, gain_bias_ref, *refs):
-        stats_refs, (weight_ref, out_ref, normed_ref) = refs[:count], refs[count:]
+        stats_refs, (*weight_refs, out_ref, normed_ref) = refs[:count], refs[count:]
         step = pl.program_id(0)
 
         @pl.when(step == 0)
@@ -101,13 +112,21 @@
 
         wanted = lax.broadcasted_iota(jnp.int32, (tokens, rows), 0) * window + step
         chosen = (lax.broadcasted_iota(jnp.int32, (tokens, rows), 1) == wanted).astype(jnp.bfloat16)
-        part = jnp.dot(chosen, normed_ref[...], preferred_element_type=jnp.float32)
-        out_ref[...] += jnp.dot(
-            part.astype(jnp.bfloat16), weight_ref[0], preferred_element_type=jnp.float32
+        part = jnp.dot(chosen, normed_ref[...], preferred_element_type=jnp.float32).astype(
+            jnp.bfloat16
         )
+        value = out_ref[...]
+        for (first, size), ref in zip(chunks, weight_refs):
+            value += jnp.dot(
+                part[:, first : first + size], ref[0], preferred_element_type=jnp.float32
+            )
+        out_ref[...] = value
 
     def whole(shape):
         return pl.BlockSpec(shape, lambda i: (0, 0))
+
+    def chunk(first, size):
+        return pl.BlockSpec((1, size, features), lambda i: (i, first // size, 0))
 
     return pl.pallas_call(
         body,
@@ -115,12 +134,12 @@
         grid=(window,),
         in_specs=[whole((rows, width)), whole((2, width))]
         + [whole((rows, 256))] * count
-        + [pl.BlockSpec((1, width, features), lambda i: (i, 0, 0))],
+        + [chunk(first, size) for first, size in chunks],
         out_specs=whole((tokens, features)),
         scratch_shapes=[pltpu.VMEM((rows, width), jnp.bfloat16)],
-        compiler_params=pltpu.CompilerParams(vmem_limit_bytes=VMEM),
+        compiler_params=pltpu.CompilerParams(vmem_limit_bytes=56 << 20),
         cost_estimate=LIGHT,
-    )(patches, gain_bias, *stats, merge_weight)
+    )(patches, gain_bias, *stats, *([merge_weight] * len(chunks)))
 
 
 def combine(tp_index, order, texts, images, gain_column):
@@ -274,8 +293,10 @@
 
     total, sides[-1] = tie(total, sides[-1])
     corners.append(to_corner(*sides[-1]))
-    for step in range(2, lines):
+    for step in range(2, lines - 1):
         total = add_product(total, step * 3 + 1, [held[step], *sides[step]])
+    total, late = tie(total, [held[-1], *sides[-1]])
+    total = add_product(total, lines * 3 - 2, late)
 
     position = me * row_count + jnp.arange(row_count, dtype=jnp.int32)
     request_ids = jnp.arange(text_len.shape[0], dtype=jnp.int32)

time: 91.9 us -> 92.4 us (level)
  Pallas kernels: 5.79 us -> 10.3 us
  local copies, waits for them, and re-layouts: 14.4 us -> 11.3 us
  waiting for transfers between devices: 25.3 us -> 23.3 us
    pallas_call x1, Pallas kernels: 3.63 us -> 8.12 us  [merge(): pl.pallas_call(body, out_shape=jax.ShapeDtypeStruct((tokens, features), j...]
    unnamed x32, local copies, waits for them, and re-layouts: 7.27 us -> 2.87 us
    ppermute x4, waiting for transfers between devices: 7.07 us -> 6.03 us  [to_sides(): lax.ppermute(block, 'req', x_perm)]
  transfers between devices with their start and end apart: 23 -> 23, of which waited for: 12 -> 11; matrix products, arithmetic and copies ran while one was open for 25% -> 27% of each run, Pallas kernels for 6% -> 11%
where the time goes in v17:
time: 92.4 us; the launch traced here: 91.7 us
  starting transfers between devices  25.5 us (28%)
  waiting for transfers between devices  23.3 us (25%)
  local copies, waits for them, and re-layouts  11.3 us (12%)
  matrix products  11.1 us (12%)
  Pallas kernels  10.3 us (11%)
  other arithmetic  9.92 us (11%)
    dot_general x5, matrix products, add_product(): lax.dot_general(source, weight, (((0,), (0,)), ((), ())), preferred_eleme...  9.26 us
    pallas_call x1, Pallas kernels, merge(): pl.pallas_call(body, out_shape=jax.ShapeDtypeStruct((tokens, features), j...  8.12 us
    ppermute x4, waiting for transfers between devices, along_line(): return lax.ppermute(block, 'req', line_perm)  7.6 us
    concatenate x5, other arithmetic, add_product(): weight = jnp.concatenate(weights, axis=0)  6.04 us
    ppermute x4, waiting for transfers between devices, to_sides(): lax.ppermute(block, 'req', x_perm)  6.03 us
    ppermute x4, starting transfers between devices, along_line(): return lax.ppermute(block, 'req', line_perm)  5.85 us
    ppermute x3, waiting for transfers between devices, to_corner(): right = lax.ppermute(by_x[:, cut:], 'req', y_perm)  5.41 us
    ppermute x4, starting transfers between devices, to_sides(): lax.ppermute(block, 'req', x_perm)  4.47 us
  transfers between devices with their start and end apart: 23, of which 11 were waited for; matrix products, arithmetic and copies ran while one was open for 27% of the time, Pallas kernels for 11%

profile of v17, /device:TPU:0, one launch (start us, length us, event | category | flops | bytes accessed | tf_op | source)
XLA Modules:
  0.0 91.7 jit_solution(64500759545448757)
XLA Ops:
  0.0 3.0 %collective-permute-start.1 = (bf16[104,2496]{1,0:T(8,128)(2,1)}, bf16[104,2496]{1,0:T(8,128)(2,1)}, u32[]{:S(2)}, u32[]{:S(2)}) collective-permute-start(bf16[104,2496]{1,0:T(8,128)(2,1)} %param.16), channel_id=1, source_target_pairs={{0,8},{2,10},{4,12},{6,14},{8,24},{10,26},{12,28},{14,30},{16,0},{... | collective-permute-start | bytes 1557512 | tf_op jit(solution)/shard_map/ppermute | solution.py:209
  3.0 1.5 %collective-permute-start.2 = (bf16[104,2496]{1,0:T(8,128)(2,1)}, bf16[104,2496]{1,0:T(8,128)(2,1)S(1)}, u32[]{:S(2)}, u32[]{:S(2)}) collective-permute-start(bf16[104,2496]{1,0:T(8,128)(2,1)} %param.16), channel_id=1, source_target_pairs={{0,2},{2,0},{4,6},{6,4},{8,10},{10,8},{12,14},{14,12},{16,18},{18,... | collective-permute-start | bytes 1557512 | tf_op jit(solution)/shard_map/ppermute | solution.py:212
  4.5 1.5 %collective-permute-start.3 = (bf16[104,2496]{1,0:T(8,128)(2,1)}, bf16[104,2496]{1,0:T(8,128)(2,1)S(1)}, u32[]{:S(2)}, u32[]{:S(2)}) collective-permute-start(bf16[104,2496]{1,0:T(8,128)(2,1)} %param.16), channel_id=1, source_target_pairs={{0,4},{2,6},{4,0},{6,2},{8,12},{10,14},{12,8},{14,10},{16,20},{18,... | collective-permute-start | bytes 1557512 | tf_op jit(solution)/shard_map/ppermute | solution.py:212
  6.0 1.1 %copy-done = bf16[448,832]{1,0:T(8,128)(2,1)S(1)} copy-done((bf16[448,832]{1,0:T(8,128)(2,1)S(1)}, bf16[448,832]{1,0:T(8,128)(2,1)}, u32[]{:S(2)}) %copy-start) | copy-done | bytes 745496
  7.2 0.3 shard_map.118.refs_0_
  7.6 0.7 convert_bitcast_fusion.1
  8.3 0.7 fusion.10.order_ref
  9.0 0.7 stack.22
  9.7 0.7 stack.21
  10.4 0.8 reshape.52
  11.2 0.6 pad_maximum_fusion.5.gain_bias_ref
  11.8 0.2 convert_reduce_fusion
  12.0 0.8 copy-done.14
  12.8 8.1 %shard_map.119 = f32[112,1664]{1,0:T(8,128)} custom-call(bf16[448,832]{1,0:T(8,128)(2,1)} %patches_ref.3, bf16[2,832]{1,0:T(2,128)(2,1)} %pad_maximum_fusion.5.gain_bias_ref, f32[448,256]{1,0:T(8,128)} %copy-done.1, f32[448,256]{1,0:T(8,128)} %copy-done.14, bf16[4,832,1664]{2,1,0:T(8,128)(2,1)} %refs_5_.1, bf16[4,832,1664]{2,1,0:T(8,128)(2,1)} %refs_5_.1, ...), custom_call_target="tpu_custom_call" | custom-call | flops 1000 | bytes 1000 | tf_op jit(solution)/shard_map/pallas_call | solution.py:131
  20.9 1.6 %constant_dynamic-slice_fusion.1 = f32[112,832]{1,0:T(8,128)S(1)} fusion(f32[112,1664]{1,0:T(8,128)} %shard_map.119, s32[]{:T(128)S(6)} %select_n.28), kind=kLoop, calls=%fused_computation.38 | loop fusion | bytes 745476 | tf_op jit(solution)/shard_map/dynamic_slice | solution.py:34
  22.5 0.5 collective-permute-start.16
  23.2 0.1 fusion.7
  23.3 2.6 %collective-permute-start.4 = (bf16[104,2496]{1,0:T(8,128)(2,1)}, bf16[104,2496]{1,0:T(8,128)(2,1)S(1)}, u32[]{:S(2)}, u32[]{:S(2)}) collective-permute-start(bf16[104,2496]{1,0:T(8,128)(2,1)} %collective-permute-done.1), channel_id=1, source_target_pairs={{0,8},{2,10},{4,12},{6,14},{8,24},{10,26},{12,28},{14,30},{16,0},{... | collective-permute-start | bytes 1557512 | tf_op jit(solution)/shard_map/ppermute | solution.py:209
  25.9 0.5 collective-permute-start.5
  26.4 0.5 collective-permute-start.6
  26.9 0.7 copy.18
  27.6 0.7 slice.34
  28.4 1.5 %collective-permute-start.9 = (bf16[104,1216]{1,0:T(8,128)(2,1)}, bf16[104,1216]{1,0:T(8,128)(2,1)}, u32[]{:S(2)}, u32[]{:S(2)}) collective-permute-start(bf16[104,1216]{1,0:T(8,128)(2,1)} %slice.34), channel_id=1, source_target_pairs={{0,4},{2,6},{4,0},{6,2},{8,12},{10,14},{12,8},{14,10},{16,20},{18,... | collective-permute-start | bytes 758792 | tf_op jit(solution)/shard_map/ppermute | solution.py:216
  29.9 1.6 %collective-permute-start.8 = (bf16[104,1280]{1,0:T(8,128)(2,1)S(1)}, bf16[104,1280]{1,0:T(8,128)(2,1)}, u32[]{:S(2)}, u32[]{:S(2)}) collective-permute-start(bf16[104,1280]{1,0:T(8,128)(2,1)S(1)} %slice.33), channel_id=1, source_target_pairs={{0,2},{2,0},{4,6},{6,4},{8,10},{10,8},{12,14},{14,12},{16,18},{18,... | collective-permute-start | bytes 798728 | tf_op jit(solution)/shard_map/ppermute | solution.py:215
  31.5 1.2 %add_convert_fusion = bf16[112,832]{1,0:T(8,128)(2,1)S(1)} fusion(f32[112,832]{1,0:T(8,128)S(1)} %collective-permute-done.16, f32[112,1664]{1,0:T(8,128)} %shard_map.119, s32[]{:T(128)S(6)} %select_n.26), kind=kLoop, calls=%fused_computation.11 | loop fusion | flops 186368 | bytes 931844 | tf_op jit(solution)/shard_map/convert_element_type | solution.py:248
  32.7 1.8 %convolution_convert_fusion = bf16[256,896]{1,0:T(8,128)(2,1)} fusion(bf16[112,2]{1,0:T(8,128)(2,1)} %copy.18, bf16[112,832]{1,0:T(8,128)(2,1)S(1)} %add_convert_fusion, bf16[896]{0:T(1024)(128)(2,1)S(1)} %pad.17.clone, s32[112]{0:T(128)S(1)} %multiply_add_fusion), kind=kOutput, calls=%fused_computation.9 | convolution fusion | flops 52240384 | bytes 647808 | tf_op jit(solution)/shard_map/dot_general | solution.py:256
  34.5 3.6 %all-to-all-start = ((bf16[16,16,896]{2,1,0:T(8,128)(2,1)}), bf16[16,16,896]{2,1,0:T(8,128)(2,1)S(1)}, u32[]{:S(2)}, u32[]{:S(2)}) async-start(bf16[16,16,896]{2,1,0:T(8,128)(2,1)} %bitcast.5), calls=%async_computation | async-start | bytes 917504 | tf_op jit(solution)/shard_map/all_to_all | solution.py:257
  38.1 0.3 copy.19.gain_ref
  38.4 0.8 copy-done.12
  39.2 2.3 %collective-permute-done.5 = bf16[104,2496]{1,0:T(8,128)(2,1)} collective-permute-done((bf16[104,2496]{1,0:T(8,128)(2,1)}, bf16[104,2496]{1,0:T(8,128)(2,1)}, u32[]{:S(2)}, u32[]{:S(2)}) %collective-permute-start.5) | collective-permute-done | bytes 519200 | tf_op jit(solution)/shard_map/ppermute | solution.py:212
  41.6 1.4 %collective-permute-done.6 = bf16[104,2496]{1,0:T(8,128)(2,1)} collective-permute-done((bf16[104,2496]{1,0:T(8,128)(2,1)}, bf16[104,2496]{1,0:T(8,128)(2,1)}, u32[]{:S(2)}, u32[]{:S(2)}) %collective-permute-start.6) | collective-permute-done | bytes 519200 | tf_op jit(solution)/shard_map/ppermute | solution.py:212
  43.0 1.2 %collective-permute-start.11 = (bf16[104,2496]{1,0:T(8,128)(2,1)}, bf16[104,2496]{1,0:T(8,128)(2,1)S(1)}, u32[]{:S(2)}, u32[]{:S(2)}) collective-permute-start(bf16[104,2496]{1,0:T(8,128)(2,1)} %copy-done.12), channel_id=1, source_target_pairs={{0,2},{2,0},{4,6},{6,4},{8,10},{10,8},{12,14},{14,12},{16,18},{18,... | collective-permute-start | bytes 1557512 | tf_op jit(solution)/shard_map/ppermute | solution.py:212
  44.2 5.4 %collective-permute-done.9 = bf16[104,1216]{1,0:T(8,128)(2,1)} collective-permute-done((bf16[104,1216]{1,0:T(8,128)(2,1)}, bf16[104,1216]{1,0:T(8,128)(2,1)}, u32[]{:S(2)}, u32[]{:S(2)}) %collective-permute-start.9) | collective-permute-done | bytes 252960 | tf_op jit(solution)/shard_map/ppermute | solution.py:216
  49.6 0.5 collective-permute-start.12
  50.1 0.2 collective-permute-done.8
  50.3 1.1 %pad_maximum_fusion.4 = bf16[104,2496]{1,0:T(8,128)(2,1)S(1)} fusion(bf16[104,1216]{1,0:T(8,128)(2,1)} %collective-permute-done.9, bf16[104,1280]{1,0:T(8,128)(2,1)} %collective-permute-done.8), kind=kLoop, calls=%fused_computation.10 | loop fusion | flops 1038336 | bytes 1038336 | tf_op jit(solution)/shard_map/concatenate | solution.py:217
  51.4 2.6 %pad_maximum_fusion.1 = bf16[312,2496]{1,0:T(8,128)(2,1)} fusion(bf16[104,2496]{1,0:T(8,128)(2,1)} %collective-permute-done.6, bf16[104,2496]{1,0:T(8,128)(2,1)} %collective-permute-done.5, bf16[104,2496]{1,0:T(8,128)(2,1)} %collective-permute-done.1), kind=kLoop, calls=%fused_computation.5 | loop fusion | flops 4672512 | bytes 3115008 | tf_op jit(solution)/shard_map/concatenate | solution.py:279
  54.0 7.5 %collective-permute-done.7 = bf16[104,2496]{1,0:T(8,128)(2,1)} collective-permute-done((bf16[104,2496]{1,0:T(8,128)(2,1)}, bf16[104,2496]{1,0:T(8,128)(2,1)}, u32[]{:S(2)}, u32[]{:S(2)}) %collective-permute-start.7) | collective-permute-done | bytes 519200 | tf_op jit(solution)/shard_map/ppermute | solution.py:209
  61.6 0.3 collective-permute-done.11
  61.9 0.5 collective-permute-done.12
  62.4 1.2 %collective-permute-start.18 = (bf16[104,2496]{1,0:T(8,128)(2,1)}, bf16[104,2496]{1,0:T(8,128)(2,1)}, u32[]{:S(2)}, u32[]{:S(2)}) collective-permute-start(bf16[104,2496]{1,0:T(8,128)(2,1)} %collective-permute-done.7), channel_id=1, source_target_pairs={{0,2},{2,0},{4,6},{6,4},{8,10},{10,8},{12,14},{14,12},{16,18},{18,... | collective-permute-start | bytes 1557512 | tf_op jit(solution)/shard_map/ppermute | solution.py:212
  63.6 1.0 %collective-permute-start.19 = (bf16[104,2496]{1,0:T(8,128)(2,1)}, bf16[104,2496]{1,0:T(8,128)(2,1)}, u32[]{:S(2)}, u32[]{:S(2)}) collective-permute-start(bf16[104,2496]{1,0:T(8,128)(2,1)} %collective-permute-done.7), channel_id=1, source_target_pairs={{0,4},{2,6},{4,0},{6,2},{8,12},{10,14},{12,8},{14,10},{16,20},{18,... | collective-permute-start | bytes 1557512 | tf_op jit(solution)/shard_map/ppermute | solution.py:212
  64.7 1.6 %pad_maximum_fusion.2 = bf16[312,2496]{1,0:T(8,128)(2,1)S(1)} fusion(bf16[104,2496]{1,0:T(8,128)(2,1)} %copy-done.6, bf16[104,2496]{1,0:T(8,128)(2,1)} %copy-done.4, bf16[104,2496]{1,0:T(8,128)(2,1)} %copy-done.12), kind=kLoop, calls=%fused_computation.7 | loop fusion | flops 4672512 | bytes 3115008 | tf_op jit(solution)/shard_map/concatenate | solution.py:279
  66.4 0.2 collective-permute-start.10
  66.7 0.1 copy-done.13
  66.8 0.2 pad_maximum_fusion
  67.0 1.4 %collective-permute-start.14 = (bf16[104,1216]{1,0:T(8,128)(2,1)S(1)}, bf16[104,1216]{1,0:T(8,128)(2,1)S(1)}, u32[]{:S(2)}, u32[]{:S(2)}) collective-permute-start(bf16[104,1216]{1,0:T(8,128)(2,1)S(1)} %slice.36), channel_id=1, source_target_pairs={{0,4},{2,6},{4,0},{6,2},{8,12},{10,14},{12,8},{14,10},{16,20},{18,... | collective-permute-start | bytes 758792 | tf_op jit(solution)/shard_map/ppermute | solution.py:216
  68.4 0.8 collective-permute-start.13
  69.2 1.9 %shard_map.120 = bf16[16,104,512]{2,1,0:T(8,128)(2,1)S(1)} custom-call(s32[1]{0:T(128)} %bitcast.3.index_ref, s32[16]{0:T(128)S(1)} %fusion.10.order_ref, bf16[16,104,1]{2,1,0:T(8,128)(2,1)S(1)} %copy.19.gain_ref, bf16[832,512]{1,0:T(8,128)(2,1)S(1)} %bitcast.28, bf16[832,512]{1,0:T(8,128)(2,1)S(1)} %collective-permute-done.15.refs_1_, ...), custom_call_target="tpu_custom_call" | custom-call | flops 1000 | bytes 1000 | tf_op jit(solution)/shard_map/pallas_call | solution.py:183
  71.1 0.1 fusion.14
  71.2 1.5 %fusion.15 = f32[512,2496]{0,1:T(8,128)S(1)} fusion(bf16[416,512]{1,0:T(8,128)(2,1)S(1)} %bitcast.30, bf16[416,2496]{1,0:T(8,128)(2,1)S(1)} %pad_maximum_fusion), kind=kOutput, calls=%fused_computation.47 | convolution fusion | flops 1063256064 | bytes 7614464 | tf_op jit(solution)/shard_map/dot_general | solution.py:286
  72.8 1.6 %convolution_add_fusion.2 = f32[512,2496]{0,1:T(8,128)S(1)} fusion(f32[512,2496]{0,1:T(8,128)S(1)} %fusion.15, bf16[312,512]{1,0:T(8,128)(2,1)S(1)} %bitcast.33, bf16[312,2496]{1,0:T(8,128)(2,1)S(1)} %copy-done.3), kind=kOutput, calls=%fused_computation.3 | convolution fusion | flops 798720000 | bytes 12100608 | tf_op jit(solution)/shard_map/dot_general | solution.py:286
  74.3 3.4 %collective-permute-done.18 = bf16[104,2496]{1,0:T(8,128)(2,1)} collective-permute-done((bf16[104,2496]{1,0:T(8,128)(2,1)}, bf16[104,2496]{1,0:T(8,128)(2,1)}, u32[]{:S(2)}, u32[]{:S(2)}) %collective-permute-start.18) | collective-permute-done | bytes 519200 | tf_op jit(solution)/shard_map/ppermute | solution.py:212
  77.7 1.2 %collective-permute-done.19 = bf16[104,2496]{1,0:T(8,128)(2,1)} collective-permute-done((bf16[104,2496]{1,0:T(8,128)(2,1)}, bf16[104,2496]{1,0:T(8,128)(2,1)}, u32[]{:S(2)}, u32[]{:S(2)}) %collective-permute-start.19) | collective-permute-done | bytes 519200 | tf_op jit(solution)/shard_map/ppermute | solution.py:212
  79.0 1.0 %slice.40 = bf16[104,1216]{1,0:T(8,128)(2,1)S(1)} slice(bf16[104,2496]{1,0:T(8,128)(2,1)} %collective-permute-done.18), slice={[0:104], [1280:2496]} | slice | bytes 505856 | tf_op jit(solution)/shard_map/slice | solution.py:216
  79.9 1.1 %collective-permute-start.21 = (bf16[104,1216]{1,0:T(8,128)(2,1)S(1)}, bf16[104,1216]{1,0:T(8,128)(2,1)S(1)}, u32[]{:S(2)}, u32[]{:S(2)}) collective-permute-start(bf16[104,1216]{1,0:T(8,128)(2,1)S(1)} %slice.40), channel_id=1, source_target_pairs={{0,4},{2,6},{4,0},{6,2},{8,12},{10,14},{12,8},{14,10},{16,20},{18,... | collective-permute-start | bytes 758792 | tf_op jit(solution)/shard_map/ppermute | solution.py:216
  81.0 1.0 %slice.39 = bf16[104,1280]{1,0:T(8,128)(2,1)S(1)} slice(bf16[104,2496]{1,0:T(8,128)(2,1)} %collective-permute-done.19), slice={[0:104], [0:1280]} | slice | bytes 532480 | tf_op jit(solution)/shard_map/slice | solution.py:215
  82.0 1.0 %collective-permute-start.20 = (bf16[104,1280]{1,0:T(8,128)(2,1)S(1)}, bf16[104,1280]{1,0:T(8,128)(2,1)S(1)}, u32[]{:S(2)}, u32[]{:S(2)}) collective-permute-start(bf16[104,1280]{1,0:T(8,128)(2,1)S(1)} %slice.39), channel_id=1, source_target_pairs={{0,2},{2,0},{4,6},{6,4},{8,10},{10,8},{12,14},{14,12},{16,18},{18,... | collective-permute-start | bytes 798728 | tf_op jit(solution)/shard_map/ppermute | solution.py:215
  83.0 1.5 %convolution_add_fusion.1 = f32[512,2496]{0,1:T(8,128)S(1)} fusion(f32[512,2496]{0,1:T(8,128)S(1)} %convolution_add_fusion.2, bf16[312,512]{1,0:T(8,128)(2,1)S(1)} %bitcast.32, bf16[312,2496]{1,0:T(8,128)(2,1)S(1)} %pad_maximum_fusion.2), kind=kOutput, calls=%fused_computation.2 | convolution fusion | flops 798720000 | bytes 12100608 | tf_op jit(solution)/shard_map/dot_general | solution.py:286
  84.5 1.5 %pad_maximum_fusion.3 = bf16[312,2496]{1,0:T(8,128)(2,1)S(1)} fusion(bf16[104,2496]{1,0:T(8,128)(2,1)} %collective-permute-done.19, bf16[104,2496]{1,0:T(8,128)(2,1)} %collective-permute-done.18, bf16[104,2496]{1,0:T(8,128)(2,1)} %collective-permute-done.7), kind=kLoop, calls=%fused_computation.8 | loop fusion | flops 4672512 | bytes 3115008 | tf_op jit(solution)/shard_map/concatenate | solution.py:279
  86.0 1.6 %convolution_add_fusion = f32[512,2496]{0,1:T(8,128)S(1)} fusion(f32[512,2496]{0,1:T(8,128)S(1)} %convolution_add_fusion.1, bf16[312,512]{1,0:T(8,128)(2,1)S(1)} %bitcast.31, bf16[312,2496]{1,0:T(8,128)(2,1)S(1)} %pad_maximum_fusion.3), kind=kOutput, calls=%fused_computation.1 | convolution fusion | flops 798720000 | bytes 12100608 | tf_op jit(solution)/shard_map/dot_general | solution.py:286
  87.6 0.9 collective-permute-done.20
  88.5 0.1 maximum_maximum_fusion
  88.6 3.1 %select_convert_fusion = bf16[512,2496]{0,1:T(8,128)(2,1)} fusion(f32[512,2496]{0,1:T(8,128)S(1)} %convolution_add_fusion, bf16[312,512]{1,0:T(8,128)(2,1)S(1)} %bitcast.29, bf16[312,2496]{1,0:T(8,128)(2,1)S(1)} %maximum_maximum_fusion, pred[512]{0:T(512)(128)(4,1)S(1)} %fusion.8), kind=kOutput, calls=%fused_computation | convolution fusion | flops 801275904 | bytes 9545216 | tf_op jit(solution)/shard_map/dot_general | solution.py:286
  (56 shorter events, 0.5 us)
Async XLA Ops:
  0.0 20.9 %collective-permute-start.1 = (bf16[104,2496]{1,0:T(8,128)(2,1)}, bf16[104,2496]{1,0:T(8,128)(2,1)}, u32[]{:S(2)}, u32[]{:S(2)}) collective-permute-start(bf16[104,2496]{1,0:T(8,128)(2,1)} %param.16), channel_id=1, source_target_pairs={{0,8},{2,10},{4,12},{6,14},{8,24},{10,26},{12,28},{14,30},{16,0},{... | collective-permute-start | bytes 1557512 | tf_op jit(solution)/shard_map/ppermute | solution.py:209
  3.0 17.9 %collective-permute-start.2 = (bf16[104,2496]{1,0:T(8,128)(2,1)}, bf16[104,2496]{1,0:T(8,128)(2,1)S(1)}, u32[]{:S(2)}, u32[]{:S(2)}) collective-permute-start(bf16[104,2496]{1,0:T(8,128)(2,1)} %param.16), channel_id=1, source_target_pairs={{0,2},{2,0},{4,6},{6,4},{8,10},{10,8},{12,14},{14,12},{16,18},{18,... | collective-permute-start | bytes 1557512 | tf_op jit(solution)/shard_map/ppermute | solution.py:212
  4.5 16.4 %collective-permute-start.3 = (bf16[104,2496]{1,0:T(8,128)(2,1)}, bf16[104,2496]{1,0:T(8,128)(2,1)S(1)}, u32[]{:S(2)}, u32[]{:S(2)}) collective-permute-start(bf16[104,2496]{1,0:T(8,128)(2,1)} %param.16), channel_id=1, source_target_pairs={{0,4},{2,6},{4,0},{6,2},{8,12},{10,14},{12,8},{14,10},{16,20},{18,... | collective-permute-start | bytes 1557512 | tf_op jit(solution)/shard_map/ppermute | solution.py:212
  6.0 1.1 %copy-start = (bf16[448,832]{1,0:T(8,128)(2,1)S(1)}, bf16[448,832]{1,0:T(8,128)(2,1)}, u32[]{:S(2)}) copy-start(bf16[448,832]{1,0:T(8,128)(2,1)} %patches_ref.3) | copy-start | bytes 2236420
  7.5 4.5 %copy-start.1 = (f32[448,256]{1,0:T(8,128)}, f32[448,256]{1,0:T(8,128)S(1)}, u32[]{:S(2)}) copy-start(f32[448,256]{1,0:T(8,128)S(1)} %shard_map.118.refs_0_) | copy-start | bytes 1376260
  7.5 4.5 %collective-permute-start = (f32[448,256]{1,0:T(8,128)S(1)}, f32[448,256]{1,0:T(8,128)S(1)}, u32[]{:S(2)}, u32[]{:S(2)}) collective-permute-start(f32[448,256]{1,0:T(8,128)S(1)} %shard_map.118.refs_0_), channel_id=1, source_target_pairs={{0,1},{1,0},{2,3},{3,2},{4,5},{5,4},{6,7},{7,6},{8,9},{9,8},{10,11... | collective-permute-start | bytes 1376264 | tf_op jit(solution)/shard_map/ppermute | solution.py:26
  12.0 11.2 %copy-start.15 = (s32[2]{0:T(128)S(1)}, s32[2]{0:T(128)}, u32[]{:S(2)}) copy-start(s32[2]{0:T(128)} %param.18) | copy-start | bytes 28
  12.0 0.8 copy-start.14
  20.9 18.3 %copy-start.2 = (bf16[512,832]{0,1:T(8,128)(2,1)S(1)}, bf16[512,832]{0,1:T(8,128)(2,1)}, u32[]{:S(2)}) copy-start(bf16[512,832]{0,1:T(8,128)(2,1)} %param.14) | copy-start | bytes 2555908
  20.9 29.2 %copy-start.8 = (bf16[104,2496]{1,0:T(8,128)(2,1)}, bf16[104,2496]{1,0:T(8,128)(2,1)S(1)}, u32[]{:S(2)}) copy-start(bf16[104,2496]{1,0:T(8,128)(2,1)S(1)} %collective-permute-done.2) | copy-start | bytes 1557508
  20.9 13.5 %copy-start.10 = (bf16[104,2496]{1,0:T(8,128)(2,1)}, bf16[104,2496]{1,0:T(8,128)(2,1)S(1)}, u32[]{:S(2)}) copy-start(bf16[104,2496]{1,0:T(8,128)(2,1)S(1)} %collective-permute-done.3) | copy-start | bytes 1557508
  22.5 7.4 %collective-permute-start.16 = (f32[112,832]{1,0:T(8,128)S(1)}, f32[112,832]{1,0:T(8,128)S(1)}, u32[]{:S(2)}, u32[]{:S(2)}) collective-permute-start(f32[112,832]{1,0:T(8,128)S(1)} %constant_dynamic-slice_fusion.1), channel_id=1, source_target_pairs={{0,1},{1,0},{2,3},{3,2},{4,5},{5,4},{6,7},{7,6},{8,9},{9,8},{10,11... | collective-permute-start | bytes 1118216 | tf_op jit(solution)/shard_map/ppermute | solution.py:26
  23.3 15.1 %collective-permute-start.4 = (bf16[104,2496]{1,0:T(8,128)(2,1)}, bf16[104,2496]{1,0:T(8,128)(2,1)S(1)}, u32[]{:S(2)}, u32[]{:S(2)}) collective-permute-start(bf16[104,2496]{1,0:T(8,128)(2,1)} %collective-permute-done.1), channel_id=1, source_target_pairs={{0,8},{2,10},{4,12},{6,14},{8,24},{10,26},{12,28},{14,30},{16,0},{... | collective-permute-start | bytes 1557512 | tf_op jit(solution)/shard_map/ppermute | solution.py:209
  25.9 15.7 %collective-permute-start.5 = (bf16[104,2496]{1,0:T(8,128)(2,1)}, bf16[104,2496]{1,0:T(8,128)(2,1)}, u32[]{:S(2)}, u32[]{:S(2)}) collective-permute-start(bf16[104,2496]{1,0:T(8,128)(2,1)} %collective-permute-done.1), channel_id=1, source_target_pairs={{0,2},{2,0},{4,6},{6,4},{8,10},{10,8},{12,14},{14,12},{16,18},{18,... | collective-permute-start | bytes 1557512 | tf_op jit(solution)/shard_map/ppermute | solution.py:212
  26.4 16.6 %collective-permute-start.6 = (bf16[104,2496]{1,0:T(8,128)(2,1)}, bf16[104,2496]{1,0:T(8,128)(2,1)}, u32[]{:S(2)}, u32[]{:S(2)}) collective-permute-start(bf16[104,2496]{1,0:T(8,128)(2,1)} %collective-permute-done.1), channel_id=1, source_target_pairs={{0,4},{2,6},{4,0},{6,2},{8,12},{10,14},{12,8},{14,10},{16,20},{18,... | collective-permute-start | bytes 1557512 | tf_op jit(solution)/shard_map/ppermute | solution.py:212
  28.4 21.2 %collective-permute-start.9 = (bf16[104,1216]{1,0:T(8,128)(2,1)}, bf16[104,1216]{1,0:T(8,128)(2,1)}, u32[]{:S(2)}, u32[]{:S(2)}) collective-permute-start(bf16[104,1216]{1,0:T(8,128)(2,1)} %slice.34), channel_id=1, source_target_pairs={{0,4},{2,6},{4,0},{6,2},{8,12},{10,14},{12,8},{14,10},{16,20},{18,... | collective-permute-start | bytes 758792 | tf_op jit(solution)/shard_map/ppermute | solution.py:216
  29.9 20.4 %collective-permute-start.8 = (bf16[104,1280]{1,0:T(8,128)(2,1)S(1)}, bf16[104,1280]{1,0:T(8,128)(2,1)}, u32[]{:S(2)}, u32[]{:S(2)}) collective-permute-start(bf16[104,1280]{1,0:T(8,128)(2,1)S(1)} %slice.33), channel_id=1, source_target_pairs={{0,2},{2,0},{4,6},{6,4},{8,10},{10,8},{12,14},{14,12},{16,18},{18,... | collective-permute-start | bytes 798728 | tf_op jit(solution)/shard_map/ppermute | solution.py:215
  34.5 30.2 %all-to-all-start = ((bf16[16,16,896]{2,1,0:T(8,128)(2,1)}), bf16[16,16,896]{2,1,0:T(8,128)(2,1)S(1)}, u32[]{:S(2)}, u32[]{:S(2)}) async-start(bf16[16,16,896]{2,1,0:T(8,128)(2,1)} %bitcast.5), calls=%async_computation | async-start | bytes 917504 | tf_op jit(solution)/shard_map/all_to_all | solution.py:257
  38.4 0.8 copy-start.12
  39.2 27.7 %collective-permute-start.15 = (bf16[832,512]{1,0:T(8,128)(2,1)S(1)}, bf16[832,512]{1,0:T(8,128)(2,1)S(1)}, u32[]{:S(2)}, u32[]{:S(2)}) collective-permute-start(bf16[832,512]{1,0:T(8,128)(2,1)S(1)} %bitcast.27), channel_id=1, source_target_pairs={{0,1},{1,0},{2,3},{3,2},{4,5},{5,4},{6,7},{7,6},{8,9},{9,8},{10,11... | collective-permute-start | bytes 2555912 | tf_op jit(solution)/shard_map/ppermute | solution.py:26
  43.0 18.6 %collective-permute-start.7 = (bf16[104,2496]{1,0:T(8,128)(2,1)}, bf16[104,2496]{1,0:T(8,128)(2,1)}, u32[]{:S(2)}, u32[]{:S(2)}) collective-permute-start(bf16[104,2496]{1,0:T(8,128)(2,1)} %copy-done.12), channel_id=1, source_target_pairs={{0,8},{2,10},{4,12},{6,14},{8,24},{10,26},{12,28},{14,30},{16,0},{... | collective-permute-start | bytes 1557512 | tf_op jit(solution)/shard_map/ppermute | solution.py:209
  43.0 18.9 %collective-permute-start.11 = (bf16[104,2496]{1,0:T(8,128)(2,1)}, bf16[104,2496]{1,0:T(8,128)(2,1)S(1)}, u32[]{:S(2)}, u32[]{:S(2)}) collective-permute-start(bf16[104,2496]{1,0:T(8,128)(2,1)} %copy-done.12), channel_id=1, source_target_pairs={{0,2},{2,0},{4,6},{6,4},{8,10},{10,8},{12,14},{14,12},{16,18},{18,... | collective-permute-start | bytes 1557512 | tf_op jit(solution)/shard_map/ppermute | solution.py:212
  49.6 12.8 %collective-permute-start.12 = (bf16[104,2496]{1,0:T(8,128)(2,1)}, bf16[104,2496]{1,0:T(8,128)(2,1)S(1)}, u32[]{:S(2)}, u32[]{:S(2)}) collective-permute-start(bf16[104,2496]{1,0:T(8,128)(2,1)} %copy-done.12), channel_id=1, source_target_pairs={{0,4},{2,6},{4,0},{6,2},{8,12},{10,14},{12,8},{14,10},{16,20},{18,... | collective-permute-start | bytes 1557512 | tf_op jit(solution)/shard_map/ppermute | solution.py:212
  61.9 1.8 %copy-start.4 = (bf16[104,2496]{1,0:T(8,128)(2,1)}, bf16[104,2496]{1,0:T(8,128)(2,1)S(1)}, u32[]{:S(2)}) copy-start(bf16[104,2496]{1,0:T(8,128)(2,1)S(1)} %collective-permute-done.11) | copy-start | bytes 1557508
  62.4 1.2 %copy-start.6 = (bf16[104,2496]{1,0:T(8,128)(2,1)}, bf16[104,2496]{1,0:T(8,128)(2,1)S(1)}, u32[]{:S(2)}) copy-start(bf16[104,2496]{1,0:T(8,128)(2,1)S(1)} %collective-permute-done.12) | copy-start | bytes 1557508
  62.4 15.4 %collective-permute-start.18 = (bf16[104,2496]{1,0:T(8,128)(2,1)}, bf16[104,2496]{1,0:T(8,128)(2,1)}, u32[]{:S(2)}, u32[]{:S(2)}) collective-permute-start(bf16[104,2496]{1,0:T(8,128)(2,1)} %collective-permute-done.7), channel_id=1, source_target_pairs={{0,2},{2,0},{4,6},{6,4},{8,10},{10,8},{12,14},{14,12},{16,18},{18,... | collective-permute-start | bytes 1557512 | tf_op jit(solution)/shard_map/ppermute | solution.py:212
  63.6 15.4 %collective-permute-start.19 = (bf16[104,2496]{1,0:T(8,128)(2,1)}, bf16[104,2496]{1,0:T(8,128)(2,1)}, u32[]{:S(2)}, u32[]{:S(2)}) collective-permute-start(bf16[104,2496]{1,0:T(8,128)(2,1)} %collective-permute-done.7), channel_id=1, source_target_pairs={{0,4},{2,6},{4,0},{6,2},{8,12},{10,14},{12,8},{14,10},{16,20},{18,... | collective-permute-start | bytes 1557512 | tf_op jit(solution)/shard_map/ppermute | solution.py:212
  64.6 1.8 %copy-start.5 = (bf16[104,2496]{1,0:T(8,128)(2,1)S(1)}, bf16[104,2496]{1,0:T(8,128)(2,1)}, u32[]{:S(2)}) copy-start(bf16[104,2496]{1,0:T(8,128)(2,1)} %copy-done.4) | copy-start | bytes 1557508
  64.6 1.8 %copy-start.7 = (bf16[104,2496]{1,0:T(8,128)(2,1)S(1)}, bf16[104,2496]{1,0:T(8,128)(2,1)}, u32[]{:S(2)}) copy-start(bf16[104,2496]{1,0:T(8,128)(2,1)} %copy-done.6) | copy-start | bytes 1557508
  64.6 2.1 %copy-start.9 = (bf16[104,2496]{1,0:T(8,128)(2,1)S(1)}, bf16[104,2496]{1,0:T(8,128)(2,1)}, u32[]{:S(2)}) copy-start(bf16[104,2496]{1,0:T(8,128)(2,1)} %copy-done.8) | copy-start | bytes 1557508
  64.6 2.1 %copy-start.11 = (bf16[104,2496]{1,0:T(8,128)(2,1)S(1)}, bf16[104,2496]{1,0:T(8,128)(2,1)}, u32[]{:S(2)}) copy-start(bf16[104,2496]{1,0:T(8,128)(2,1)} %copy-done.10) | copy-start | bytes 1557508
  64.6 2.2 %copy-start.13 = (bf16[104,2496]{1,0:T(8,128)(2,1)S(1)}, bf16[104,2496]{1,0:T(8,128)(2,1)}, u32[]{:S(2)}) copy-start(bf16[104,2496]{1,0:T(8,128)(2,1)} %param.16) | copy-start | bytes 1557508
  64.7 3.8 %collective-permute-start.17 = (bf16[256,896]{1,0:T(8,128)(2,1)S(1)}, bf16[256,896]{1,0:T(8,128)(2,1)S(1)}, u32[]{:S(2)}, u32[]{:S(2)}) collective-permute-start(bf16[256,896]{1,0:T(8,128)(2,1)S(1)} %bitcast.25), channel_id=1, source_target_pairs={{0,1},{1,0},{2,3},{3,2},{4,5},{5,4},{6,7},{7,6},{8,9},{9,8},{10,11... | collective-permute-start | bytes 1376264 | tf_op jit(solution)/shard_map/ppermute | solution.py:26
  66.4 21.1 %collective-permute-start.10 = (bf16[104,2496]{1,0:T(8,128)(2,1)S(1)}, bf16[104,2496]{1,0:T(8,128)(2,1)S(1)}, u32[]{:S(2)}, u32[]{:S(2)}) collective-permute-start(bf16[104,2496]{1,0:T(8,128)(2,1)S(1)} %pad_maximum_fusion.4), channel_id=1, source_target_pairs={{0,8},{2,10},{4,12},{6,14},{8,24},{10,26},{12,28},{14,30},{16,0},{... | collective-permute-start | bytes 1557512 | tf_op jit(solution)/shard_map/ppermute | solution.py:209
  67.0 20.6 %collective-permute-start.14 = (bf16[104,1216]{1,0:T(8,128)(2,1)S(1)}, bf16[104,1216]{1,0:T(8,128)(2,1)S(1)}, u32[]{:S(2)}, u32[]{:S(2)}) collective-permute-start(bf16[104,1216]{1,0:T(8,128)(2,1)S(1)} %slice.36), channel_id=1, source_target_pairs={{0,4},{2,6},{4,0},{6,2},{8,12},{10,14},{12,8},{14,10},{16,20},{18,... | collective-permute-start | bytes 758792 | tf_op jit(solution)/shard_map/ppermute | solution.py:216
  68.4 19.1 %collective-permute-start.13 = (bf16[104,1280]{1,0:T(8,128)(2,1)S(1)}, bf16[104,1280]{1,0:T(8,128)(2,1)S(1)}, u32[]{:S(2)}, u32[]{:S(2)}) collective-permute-start(bf16[104,1280]{1,0:T(8,128)(2,1)S(1)} %slice.35), channel_id=1, source_target_pairs={{0,2},{2,0},{4,6},{6,4},{8,10},{10,8},{12,14},{14,12},{16,18},{18,... | collective-permute-start | bytes 798728 | tf_op jit(solution)/shard_map/ppermute | solution.py:215
  71.2 1.6 %copy-start.3 = (bf16[312,2496]{1,0:T(8,128)(2,1)S(1)}, bf16[312,2496]{1,0:T(8,128)(2,1)}, u32[]{:S(2)}) copy-start(bf16[312,2496]{1,0:T(8,128)(2,1)} %pad_maximum_fusion.1) | copy-start | bytes 4672516
  79.9 7.6 %collective-permute-start.21 = (bf16[104,1216]{1,0:T(8,128)(2,1)S(1)}, bf16[104,1216]{1,0:T(8,128)(2,1)S(1)}, u32[]{:S(2)}, u32[]{:S(2)}) collective-permute-start(bf16[104,1216]{1,0:T(8,128)(2,1)S(1)} %slice.40), channel_id=1, source_target_pairs={{0,4},{2,6},{4,0},{6,2},{8,12},{10,14},{12,8},{14,10},{16,20},{18,... | collective-permute-start | bytes 758792 | tf_op jit(solution)/shard_map/ppermute | solution.py:216
  82.0 6.5 %collective-permute-start.20 = (bf16[104,1280]{1,0:T(8,128)(2,1)S(1)}, bf16[104,1280]{1,0:T(8,128)(2,1)S(1)}, u32[]{:S(2)}, u32[]{:S(2)}) collective-permute-start(bf16[104,1280]{1,0:T(8,128)(2,1)S(1)} %slice.39), channel_id=1, source_target_pairs={{0,2},{2,0},{4,6},{6,4},{8,10},{10,8},{12,14},{14,12},{16,18},{18,... | collective-permute-start | bytes 798728 | tf_op jit(solution)/shard_map/ppermute | solution.py:215

commit v18 on v16

--- a/solution.py
+++ b/solution.py
@@ -56,55 +56,60 @@
     return lax.optimization_barrier(values)
 
 
-def row_stats(patches):
-    rows, _ = patches.shape
-
-    def body(patches_ref, out_ref):
-        values = patches_ref[...].astype(jnp.float32)
-        sums = jnp.sum(values, axis=1, keepdims=True)
-        squares = jnp.sum(values * values, axis=1, keepdims=True)
-        out_ref[:, :128] = jnp.broadcast_to(sums, (rows, 128))
-        out_ref[:, 128:] = jnp.broadcast_to(squares, (rows, 128))
+def pick_rows(patches, window):
+    rows, width = patches.shape
+    tokens = rows // window
+
+    def body(patches_ref, picked_ref, stats_ref):
+        taken = lax.broadcasted_iota(jnp.int32, (tokens, rows), 1)
+        first = lax.broadcasted_iota(jnp.int32, (tokens, rows), 0) * window
+        for slot in range(window):
+            chosen = (taken == first + slot).astype(jnp.bfloat16)
+            values = jnp.dot(chosen, patches_ref[...], preferred_element_type=jnp.float32)
+            picked_ref[slot] = values.astype(jnp.bfloat16)
+            sums = jnp.sum(values, axis=1, keepdims=True)
+            squares = jnp.sum(values * values, axis=1, keepdims=True)
+            stats_ref[slot, :, :128] = jnp.broadcast_to(sums, (tokens, 128))
+            stats_ref[slot, :, 128:] = jnp.broadcast_to(squares, (tokens, 128))
 
     vmem = pl.BlockSpec(memory_space=pltpu.VMEM)
     return pl.pallas_call(
         body,
-        out_shape=jax.ShapeDtypeStruct((rows, 256), jnp.float32),
+        out_shape=(
+            jax.ShapeDtypeStruct((window, tokens, width), jnp.bfloat16),
+            jax.ShapeDtypeStruct((window, tokens, 256), jnp.float32),
+        ),
         in_specs=[vmem],
-        out_specs=vmem,
+        out_specs=(vmem, vmem),
         compiler_params=pltpu.CompilerParams(vmem_limit_bytes=VMEM),
         cost_estimate=pl.CostEstimate(flops=1000, bytes_accessed=16 << 20, transcendentals=0),
     )(patches)
 
 
-def merge(patches, stats, gain_bias, merge_weight):
-    rows, width = patches.shape
-    window, _, features = merge_weight.shape
-    tokens = rows // window
+def merge(picked, stats, gain_bias, merge_weight):
+    window, tokens, width = picked.shape
+    features = merge_weight.shape[2]
     count = len(stats)
 
-    def body(patches_ref, gain_bias_ref, *refs):
-        stats_refs, (weight_ref, out_ref, normed_ref) = refs[:count], refs[count:]
-        step = pl.program_id(0)
-
-        @pl.when(step == 0)
+    def body(picked_ref, gain_bias_ref, *refs):
+        stats_refs, (weight_ref, out_ref) = refs[:count], refs[count:]
+
+        @pl.when(pl.program_id(0) == 0)
         def _():
-            sums = sum(ref[...] for ref in stats_refs) / DV
-            row_mean = sums[:, 0:1]
-            row_scale = lax.rsqrt(sums[:, 128:129] - row_mean * row_mean + EPSILON)
-            gain_bias = gain_bias_ref[...].astype(jnp.float32)
-            normed_ref[...] = (
-                (patches_ref[...].astype(jnp.float32) - row_mean) * row_scale * gain_bias[0:1]
-                + gain_bias[1:2]
-            ).astype(jnp.bfloat16)
             out_ref[...] = jnp.zeros_like(out_ref)
 
-        wanted = lax.broadcasted_iota(jnp.int32, (tokens, rows), 0) * window + step
-        chosen = (lax.broadcasted_iota(jnp.int32, (tokens, rows), 1) == wanted).astype(jnp.bfloat16)
-        part = jnp.dot(chosen, normed_ref[...], preferred_element_type=jnp.float32)
-        out_ref[...] += jnp.dot(
-            part.astype(jnp.bfloat16), weight_ref[0], preferred_element_type=jnp.float32
-        )
+        sums = sum(ref[0] for ref in stats_refs) / DV
+        row_mean = sums[:, 0:1]
+        row_scale = lax.rsqrt(sums[:, 128:129] - row_mean * row_mean + EPSILON)
+        gain_bias = gain_bias_ref[...].astype(jnp.float32)
+        normed = (
+            (picked_ref[0].astype(jnp.float32) - row_mean) * row_scale * gain_bias[0:1]
+            + gain_bias[1:2]
+        ).astype(jnp.bfloat16)
+        out_ref[...] += jnp.dot(normed, weight_ref[0], preferred_element_type=jnp.float32)
+
+    def by_slot(*shape):
+        return pl.BlockSpec((1, *shape), lambda i: (i, 0, 0))
 
     def whole(shape):
         return pl.BlockSpec(shape, lambda i: (0, 0))
@@ -113,14 +118,13 @@
         body,
         out_shape=jax.ShapeDtypeStruct((tokens, features), jnp.float32),
         grid=(window,),
-        in_specs=[whole((rows, width)), whole((2, width))]
-        + [whole((rows, 256))] * count
-        + [pl.BlockSpec((1, width, features), lambda i: (i, 0, 0))],
+        in_specs=[by_slot(tokens, width), whole((2, width))]
+        + [by_slot(tokens, 256)] * count
+        + [by_slot(width, features)],
         out_specs=whole((tokens, features)),
-        scratch_shapes=[pltpu.VMEM((rows, width), jnp.bfloat16)],
         compiler_params=pltpu.CompilerParams(vmem_limit_bytes=VMEM),
         cost_estimate=LIGHT,
-    )(patches, gain_bias, *stats, merge_weight)
+    )(picked, gain_bias, *stats, merge_weight)
 
 
 def combine(tp_index, order, texts, images, gain_column):
@@ -184,7 +188,6 @@
     y_perm = [(i, i ^ 2) for i in range(n_req)]
     rows, columns = qkv_weight.shape
     cut = (columns + 255) // 256 * 128
-    order = lax.dynamic_slice_in_dim(jnp.asarray(table), me, 1, 0).reshape(-1)
 
     def along_line(block):
         return lax.ppermute(block, "req", line_perm)
@@ -201,7 +204,7 @@
     held.append(along_line(held[0]))
     sides = [to_sides(held[0])]
     corners = []
-    stats_own = row_stats(patches)
+    picked, stats_own = pick_rows(patches, merge_weight.shape[0])
     stats = [stats_own] + [tp_shift(stats_own, n_tp, d) for d in range(1, n_tp)]
     gain_bias = jnp.stack([ln_gain, ln_bias])
     text_turned = text_rows.T
@@ -216,12 +219,11 @@
     slot_count = n_req * IMG_CAP
     code = lax.rem(token_pos, row_count) + 1
     code_cols = jnp.stack([lax.div(code, 256), lax.rem(code, 256)], axis=1).astype(jnp.bfloat16)
-    gain_column = norm_gain.reshape(n_req, rows, 1)
-
-    partial_value = merge(patches, stats, gain_bias, merge_weight)
-
-    partial_value, held[1], sides[0], gain_column, order, slot, code_cols = tie(
-        partial_value, held[1], sides[0], gain_column, order, slot, code_cols
+
+    partial_value = merge(picked, stats, gain_bias, merge_weight)
+
+    partial_value, held[1], sides[0], slot, code_cols = tie(
+        partial_value, held[1], sides[0], slot, code_cols
     )
     held.append(along_line(held[1]))
     sides.append(to_sides(held[1]))
@@ -239,7 +241,9 @@
         outgoing.reshape(n_req, IMG_CAP, -1), "req", split_axis=0, concat_axis=0
     ).reshape(slot_count, -1)
 
-    held[2], sides[1] = tie(held[2], sides[1])
+    held[2], sides[1], norm_gain, me = tie(held[2], sides[1], norm_gain, me)
+    gain_column = norm_gain.reshape(n_req, rows, 1)
+    order = lax.dynamic_slice_in_dim(jnp.asarray(table), me, 1, 0).reshape(-1)
     held.append(along_line(held[2]))
     sides.append(to_sides(held[2]))
     images = [arrived] + [tp_shift(arrived, n_tp, d) for d in range(1, n_tp)]
@@ -274,8 +278,10 @@
 
     total, sides[-1] = tie(total, sides[-1])
     corners.append(to_corner(*sides[-1]))
-    for step in range(2, lines):
+    for step in range(2, lines - 1):
         total = add_product(total, step * 3 + 1, [held[step], *sides[step]])
+    total, late = tie(total, [held[-1], *sides[-1]])
+    total = add_product(total, lines * 3 - 2, late)
 
     position = me * row_count + jnp.arange(row_count, dtype=jnp.int32)
     request_ids = jnp.arange(text_len.shape[0], dtype=jnp.int32)

time: 91.9 us -> 92.4 us (level)
  waiting for transfers between devices: 25.3 us -> 21.3 us
  starting transfers between devices: 25.7 us -> 29.5 us
  other arithmetic: 9.28 us -> 10.4 us
    ppermute x3, waiting for transfers between devices: 6.18 us -> 2.89 us  [to_corner(): right = lax.ppermute(by_x[:, cut:], 'req', y_perm)]
    ppermute x4, starting transfers between devices: 6.3 us -> 8.9 us  [along_line(): return lax.ppermute(block, 'req', line_perm)]
    all_to_all x1, starting transfers between devices: 3.56 us -> 5.47 us  [shards(): lax.all_to_all(outgoing.reshape(n_req, IMG_CAP, -1), 'req', split_axis=0,...]
    unnamed x32 -> x22, local copies, waits for them, and re-layouts: 7.27 us -> 5.67 us
    ppermute x3, starting transfers between devices: 3.15 us -> 1.79 us  [to_corner(): left = lax.ppermute(by_y[:, :cut], 'req', x_perm)]
    slice x3, local copies, waits for them, and re-layouts: 1.01 us -> 1.96 us  [to_corner(): left = lax.ppermute(by_y[:, :cut], 'req', x_perm)]
  transfers between devices with their start and end apart: 23 -> 23, of which waited for: 12 -> 9; matrix products, arithmetic and copies ran while one was open for 25% -> 29% of each run, Pallas kernels for 6% -> 6%
where the time goes in v18:
time: 92.4 us; the launch traced here: 91.8 us
  starting transfers between devices  29.5 us (32%)
  waiting for transfers between devices  21.3 us (23%)
  local copies, waits for them, and re-layouts  14.3 us (15%)
  matrix products  10.5 us (11%)
  other arithmetic  10.4 us (11%)
  Pallas kernels  5.52 us (6%)
    dot_general x5, matrix products, add_product(): lax.dot_general(source, weight, (((0,), (0,)), ((), ())), preferred_eleme...  9.4 us
    ppermute x4, starting transfers between devices, along_line(): return lax.ppermute(block, 'req', line_perm)  8.9 us
    ppermute x4, waiting for transfers between devices, along_line(): return lax.ppermute(block, 'req', line_perm)  7.86 us
    ppermute x4, waiting for transfers between devices, to_sides(): lax.ppermute(block, 'req', x_perm)  6.61 us
    concatenate x5, other arithmetic, add_product(): weight = jnp.concatenate(weights, axis=0)  6 us
    ppermute x4, starting transfers between devices, to_sides(): lax.ppermute(block, 'req', x_perm)  5.72 us
    unnamed x22, local copies, waits for them, and re-layouts  5.67 us
    all_to_all x1, starting transfers between devices, shards(): lax.all_to_all(outgoing.reshape(n_req, IMG_CAP, -1), 'req', split_axis=0,...  5.47 us
  transfers between devices with their start and end apart: 23, of which 9 were waited for; matrix products, arithmetic and copies ran while one was open for 29% of the time, Pallas kernels for 6%

profile of v18, /device:TPU:0, one launch (start us, length us, event | category | flops | bytes accessed | tf_op | source)
XLA Modules:
  0.0 91.8 jit_solution(3993130615422805017)
XLA Ops:
  0.0 3.0 %collective-permute-start.1 = (bf16[104,2496]{1,0:T(8,128)(2,1)}, bf16[104,2496]{1,0:T(8,128)(2,1)S(1)}, u32[]{:S(2)}, u32[]{:S(2)}) collective-permute-start(bf16[104,2496]{1,0:T(8,128)(2,1)} %param.16), channel_id=1, source_target_pairs={{0,8},{2,10},{4,12},{6,14},{8,24},{10,26},{12,28},{14,30},{16,0},{... | collective-permute-start | bytes 1557512 | tf_op jit(solution)/shard_map/ppermute | solution.py:193
  3.0 1.5 %collective-permute-start.2 = (bf16[104,2496]{1,0:T(8,128)(2,1)}, bf16[104,2496]{1,0:T(8,128)(2,1)S(1)}, u32[]{:S(2)}, u32[]{:S(2)}) collective-permute-start(bf16[104,2496]{1,0:T(8,128)(2,1)} %param.16), channel_id=1, source_target_pairs={{0,2},{2,0},{4,6},{6,4},{8,10},{10,8},{12,14},{14,12},{16,18},{18,... | collective-permute-start | bytes 1557512 | tf_op jit(solution)/shard_map/ppermute | solution.py:196
  4.5 1.5 %collective-permute-start.3 = (bf16[104,2496]{1,0:T(8,128)(2,1)}, bf16[104,2496]{1,0:T(8,128)(2,1)S(1)}, u32[]{:S(2)}, u32[]{:S(2)}) collective-permute-start(bf16[104,2496]{1,0:T(8,128)(2,1)} %param.16), channel_id=1, source_target_pairs={{0,4},{2,6},{4,0},{6,2},{8,12},{10,14},{12,8},{14,10},{16,20},{18,... | collective-permute-start | bytes 1557512 | tf_op jit(solution)/shard_map/ppermute | solution.py:196
  6.0 1.1 %copy-done.2 = bf16[448,832]{1,0:T(8,128)(2,1)S(1)} copy-done((bf16[448,832]{1,0:T(8,128)(2,1)S(1)}, bf16[448,832]{1,0:T(8,128)(2,1)}, u32[]{:S(2)}) %copy-start.2) | copy-done | bytes 745496
  7.2 0.8 shard_map.118
  8.0 0.7 convert_bitcast_fusion.1
  8.7 0.5 pad_maximum_fusion.6
  9.2 0.7 stack.22
  9.9 0.7 stack.21
  10.6 0.2 convert_reduce_fusion
  10.8 4.1 %copy-done = bf16[4,832,1664]{2,1,0:T(8,128)(2,1)S(1)} copy-done((bf16[4,832,1664]{2,1,0:T(8,128)(2,1)S(1)}, bf16[4,832,1664]{2,1,0:T(8,128)(2,1)}, u32[]{:S(2)}) %copy-start) | copy-done | bytes 11075608
  14.9 2.9 %shard_map.119 = f32[112,1664]{1,0:T(8,128)S(1)} custom-call(bf16[4,112,832]{2,1,0:T(8,128)(2,1)S(1)} %get-tuple-element.44.picked_ref, bf16[2,832]{1,0:T(2,128)(2,1)S(1)} %pad_maximum_fusion.5.gain_bias_ref, f32[4,112,256]{2,1,0:T(8,128)S(1)} %get-tuple-element.45.refs_0_, f32[4,112,256]{2,1,0:T(8,128)S(1)} %collective-permute-done.refs_1_, ...), custom_call_target="tpu_custom_call" | custom-call | flops 1000 | bytes 1000 | tf_op jit(solution)/shard_map/pallas_call | solution.py:117
  17.9 0.1 collective-permute-done.3
  18.0 0.6 collective-permute-start.8
  18.6 0.1 copy-done.4
  18.7 0.3 copy-done.6
  19.0 1.3 %collective-permute-start.9 = (bf16[104,1216]{1,0:T(8,128)(2,1)S(1)}, bf16[104,1216]{1,0:T(8,128)(2,1)}, u32[]{:S(2)}, u32[]{:S(2)}) collective-permute-start(bf16[104,1216]{1,0:T(8,128)(2,1)S(1)} %slice.34), channel_id=1, source_target_pairs={{0,4},{2,6},{4,0},{6,2},{8,12},{10,14},{12,8},{14,10},{16,20},{18,... | collective-permute-start | bytes 758792 | tf_op jit(solution)/shard_map/ppermute | solution.py:200
  20.3 0.9 %constant_dynamic-slice_fusion.1 = f32[112,832]{1,0:T(8,128)} fusion(f32[112,1664]{1,0:T(8,128)S(1)} %shard_map.119, s32[]{:T(128)S(6)} %select_n.28), kind=kLoop, calls=%fused_computation.38 | loop fusion | bytes 745476 | tf_op jit(solution)/shard_map/dynamic_slice | solution.py:34
  21.3 0.5 collective-permute-start.15
  21.8 0.1 pad.17.clone
  21.9 2.6 %collective-permute-start.4 = (bf16[104,2496]{1,0:T(8,128)(2,1)S(1)}, bf16[104,2496]{1,0:T(8,128)(2,1)}, u32[]{:S(2)}, u32[]{:S(2)}) collective-permute-start(bf16[104,2496]{1,0:T(8,128)(2,1)S(1)} %collective-permute-done.1), channel_id=1, source_target_pairs={{0,8},{2,10},{4,12},{6,14},{8,24},{10,26},{12,28},{14,30},{16,0},{... | collective-permute-start | bytes 1557512 | tf_op jit(solution)/shard_map/ppermute | solution.py:193
  24.4 0.7 copy.18
  25.1 2.7 %collective-permute-done.9 = bf16[104,1216]{1,0:T(8,128)(2,1)} collective-permute-done((bf16[104,1216]{1,0:T(8,128)(2,1)S(1)}, bf16[104,1216]{1,0:T(8,128)(2,1)}, u32[]{:S(2)}, u32[]{:S(2)}) %collective-permute-start.9) | collective-permute-done | bytes 252960 | tf_op jit(solution)/shard_map/ppermute | solution.py:200
  27.9 0.9 %collective-permute-start.5 = (bf16[104,2496]{1,0:T(8,128)(2,1)S(1)}, bf16[104,2496]{1,0:T(8,128)(2,1)}, u32[]{:S(2)}, u32[]{:S(2)}) collective-permute-start(bf16[104,2496]{1,0:T(8,128)(2,1)S(1)} %collective-permute-done.1), channel_id=1, source_target_pairs={{0,2},{2,0},{4,6},{6,4},{8,10},{10,8},{12,14},{14,12},{16,18},{18,... | collective-permute-start | bytes 1557512 | tf_op jit(solution)/shard_map/ppermute | solution.py:196
  28.8 0.5 collective-permute-start.6
  29.3 1.1 %pad_maximum_fusion.4 = bf16[104,2496]{1,0:T(8,128)(2,1)S(1)} fusion(bf16[104,1216]{1,0:T(8,128)(2,1)} %collective-permute-done.9, bf16[104,1280]{1,0:T(8,128)(2,1)} %collective-permute-done.8), kind=kLoop, calls=%fused_computation.10 | loop fusion | flops 1038336 | bytes 1038336 | tf_op jit(solution)/shard_map/concatenate | solution.py:201
  30.3 1.2 %add_convert_fusion = bf16[112,832]{1,0:T(8,128)(2,1)S(1)} fusion(f32[112,832]{1,0:T(8,128)} %collective-permute-done.16, f32[112,1664]{1,0:T(8,128)S(1)} %shard_map.119, s32[]{:T(128)S(6)} %select_n.26), kind=kLoop, calls=%fused_computation.11 | loop fusion | flops 186368 | bytes 931844 | tf_op jit(solution)/shard_map/convert_element_type | solution.py:231
  31.5 1.1 %convolution_convert_fusion = bf16[256,896]{1,0:T(8,128)(2,1)} fusion(bf16[112,2]{1,0:T(8,128)(2,1)S(1)} %copy.18, bf16[112,832]{1,0:T(8,128)(2,1)S(1)} %add_convert_fusion, bf16[896]{0:T(1024)(128)(2,1)S(1)} %pad.17.clone, s32[112]{0:T(128)S(1)} %multiply_add_fusion), kind=kOutput, calls=%fused_computation.9 | convolution fusion | flops 52240384 | bytes 647808 | tf_op jit(solution)/shard_map/dot_general | solution.py:239
  32.6 5.5 %all-to-all-start = ((bf16[16,16,896]{2,1,0:T(8,128)(2,1)}), bf16[16,16,896]{2,1,0:T(8,128)(2,1)S(1)}, u32[]{:S(2)}, u32[]{:S(2)}) async-start(bf16[16,16,896]{2,1,0:T(8,128)(2,1)} %bitcast.5), calls=%async_computation | async-start | bytes 917504 | tf_op jit(solution)/shard_map/all_to_all | solution.py:240
  38.1 4.7 %collective-permute-done.5 = bf16[104,2496]{1,0:T(8,128)(2,1)} collective-permute-done((bf16[104,2496]{1,0:T(8,128)(2,1)S(1)}, bf16[104,2496]{1,0:T(8,128)(2,1)}, u32[]{:S(2)}, u32[]{:S(2)}) %collective-permute-start.5) | collective-permute-done | bytes 519200 | tf_op jit(solution)/shard_map/ppermute | solution.py:196
  42.8 1.4 %collective-permute-done.6 = bf16[104,2496]{1,0:T(8,128)(2,1)} collective-permute-done((bf16[104,2496]{1,0:T(8,128)(2,1)S(1)}, bf16[104,2496]{1,0:T(8,128)(2,1)}, u32[]{:S(2)}, u32[]{:S(2)}) %collective-permute-start.6) | collective-permute-done | bytes 519200 | tf_op jit(solution)/shard_map/ppermute | solution.py:196
  44.2 3.0 %collective-permute-start.7 = (bf16[104,2496]{1,0:T(8,128)(2,1)}, bf16[104,2496]{1,0:T(8,128)(2,1)}, u32[]{:S(2)}, u32[]{:S(2)}) collective-permute-start(bf16[104,2496]{1,0:T(8,128)(2,1)} %collective-permute-done.4), channel_id=1, source_target_pairs={{0,8},{2,10},{4,12},{6,14},{8,24},{10,26},{12,28},{14,30},{16,0},{... | collective-permute-start | bytes 1557512 | tf_op jit(solution)/shard_map/ppermute | solution.py:193
  47.3 1.8 %collective-permute-start.11 = (bf16[104,2496]{1,0:T(8,128)(2,1)}, bf16[104,2496]{1,0:T(8,128)(2,1)}, u32[]{:S(2)}, u32[]{:S(2)}) collective-permute-start(bf16[104,2496]{1,0:T(8,128)(2,1)} %collective-permute-done.4), channel_id=1, source_target_pairs={{0,2},{2,0},{4,6},{6,4},{8,10},{10,8},{12,14},{14,12},{16,18},{18,... | collective-permute-start | bytes 1557512 | tf_op jit(solution)/shard_map/ppermute | solution.py:196
  49.1 0.7 fusion.7
  49.9 0.8 reshape.62.gain_ref
  50.7 2.6 %pad_maximum_fusion.1 = bf16[312,2496]{1,0:T(8,128)(2,1)} fusion(bf16[104,2496]{1,0:T(8,128)(2,1)} %collective-permute-done.6, bf16[104,2496]{1,0:T(8,128)(2,1)} %collective-permute-done.5, bf16[104,2496]{1,0:T(8,128)(2,1)} %copy-done.8), kind=kLoop, calls=%fused_computation.5 | loop fusion | flops 4672512 | bytes 3115008 | tf_op jit(solution)/shard_map/concatenate | solution.py:264
  53.4 0.7 fusion.10.order_ref
  54.0 7.9 %collective-permute-done.7 = bf16[104,2496]{1,0:T(8,128)(2,1)} collective-permute-done((bf16[104,2496]{1,0:T(8,128)(2,1)}, bf16[104,2496]{1,0:T(8,128)(2,1)}, u32[]{:S(2)}, u32[]{:S(2)}) %collective-permute-start.7) | collective-permute-done | bytes 519200 | tf_op jit(solution)/shard_map/ppermute | solution.py:193
  61.9 1.5 %collective-permute-start.18 = (bf16[104,2496]{1,0:T(8,128)(2,1)}, bf16[104,2496]{1,0:T(8,128)(2,1)}, u32[]{:S(2)}, u32[]{:S(2)}) collective-permute-start(bf16[104,2496]{1,0:T(8,128)(2,1)} %collective-permute-done.7), channel_id=1, source_target_pairs={{0,2},{2,0},{4,6},{6,4},{8,10},{10,8},{12,14},{14,12},{16,18},{18,... | collective-permute-start | bytes 1557512 | tf_op jit(solution)/shard_map/ppermute | solution.py:196
  63.4 1.5 %collective-permute-start.19 = (bf16[104,2496]{1,0:T(8,128)(2,1)}, bf16[104,2496]{1,0:T(8,128)(2,1)}, u32[]{:S(2)}, u32[]{:S(2)}) collective-permute-start(bf16[104,2496]{1,0:T(8,128)(2,1)} %collective-permute-done.7), channel_id=1, source_target_pairs={{0,4},{2,6},{4,0},{6,2},{8,12},{10,14},{12,8},{14,10},{16,20},{18,... | collective-permute-start | bytes 1557512 | tf_op jit(solution)/shard_map/ppermute | solution.py:196
  64.9 1.6 %pad_maximum_fusion.2 = bf16[312,2496]{1,0:T(8,128)(2,1)S(1)} fusion(bf16[104,2496]{1,0:T(8,128)(2,1)} %collective-permute-done.12, bf16[104,2496]{1,0:T(8,128)(2,1)} %collective-permute-done.11, bf16[104,2496]{1,0:T(8,128)(2,1)} %collective-permute-done.4), kind=kLoop, calls=%fused_computation.7 | loop fusion | flops 4672512 | bytes 3115008 | tf_op jit(solution)/shard_map/concatenate | solution.py:264
  66.5 1.0 %slice.36 = bf16[104,1216]{1,0:T(8,128)(2,1)S(1)} slice(bf16[104,2496]{1,0:T(8,128)(2,1)} %collective-permute-done.11), slice={[0:104], [1280:2496]} | slice | bytes 505856 | tf_op jit(solution)/shard_map/slice | solution.py:200
  67.5 1.0 %slice.35 = bf16[104,1280]{1,0:T(8,128)(2,1)S(1)} slice(bf16[104,2496]{1,0:T(8,128)(2,1)} %collective-permute-done.12), slice={[0:104], [0:1280]} | slice | bytes 532480 | tf_op jit(solution)/shard_map/slice | solution.py:199
  68.5 0.2 collective-permute-start.10
  68.7 0.2 pad_maximum_fusion
  68.9 0.7 collective-permute-start.14
  69.6 0.6 collective-permute-start.13
  70.2 1.9 %shard_map.120 = bf16[16,104,512]{2,1,0:T(8,128)(2,1)S(1)} custom-call(s32[1]{0:T(128)} %bitcast.2.index_ref, s32[16]{0:T(128)S(1)} %fusion.10.order_ref, bf16[16,104,1]{2,1,0:T(8,128)(2,1)S(1)} %reshape.62.gain_ref, bf16[832,512]{1,0:T(8,128)(2,1)S(1)} %bitcast.28, bf16[832,512]{1,0:T(8,128)(2,1)S(1)} %collective-permute-done.15.refs_1_, ...), custom_call_target="tpu_custom_call" | custom-call | flops 1000 | bytes 1000 | tf_op jit(solution)/shard_map/pallas_call | solution.py:168
  72.0 0.1 fusion.14
  72.2 1.5 %fusion.15 = f32[512,2496]{0,1:T(8,128)S(1)} fusion(bf16[416,512]{1,0:T(8,128)(2,1)S(1)} %bitcast.30, bf16[416,2496]{1,0:T(8,128)(2,1)S(1)} %pad_maximum_fusion), kind=kOutput, calls=%fused_computation.47 | convolution fusion | flops 1063256064 | bytes 7614464 | tf_op jit(solution)/shard_map/dot_general | solution.py:271
  73.7 1.6 %convolution_add_fusion.2 = f32[512,2496]{0,1:T(8,128)S(1)} fusion(f32[512,2496]{0,1:T(8,128)S(1)} %fusion.15, bf16[312,512]{1,0:T(8,128)(2,1)S(1)} %bitcast.33, bf16[312,2496]{1,0:T(8,128)(2,1)S(1)} %copy-done.3), kind=kOutput, calls=%fused_computation.3 | convolution fusion | flops 798720000 | bytes 12100608 | tf_op jit(solution)/shard_map/dot_general | solution.py:271
  75.4 1.9 %collective-permute-done.18 = bf16[104,2496]{1,0:T(8,128)(2,1)} collective-permute-done((bf16[104,2496]{1,0:T(8,128)(2,1)}, bf16[104,2496]{1,0:T(8,128)(2,1)}, u32[]{:S(2)}, u32[]{:S(2)}) %collective-permute-start.18) | collective-permute-done | bytes 519200 | tf_op jit(solution)/shard_map/ppermute | solution.py:196
  77.3 1.5 %collective-permute-done.19 = bf16[104,2496]{1,0:T(8,128)(2,1)} collective-permute-done((bf16[104,2496]{1,0:T(8,128)(2,1)}, bf16[104,2496]{1,0:T(8,128)(2,1)}, u32[]{:S(2)}, u32[]{:S(2)}) %collective-permute-start.19) | collective-permute-done | bytes 519200 | tf_op jit(solution)/shard_map/ppermute | solution.py:196
  78.7 1.0 %slice.40 = bf16[104,1216]{1,0:T(8,128)(2,1)S(1)} slice(bf16[104,2496]{1,0:T(8,128)(2,1)} %collective-permute-done.18), slice={[0:104], [1280:2496]} | slice | bytes 505856 | tf_op jit(solution)/shard_map/slice | solution.py:200
  79.7 1.5 %collective-permute-start.21 = (bf16[104,1216]{1,0:T(8,128)(2,1)S(1)}, bf16[104,1216]{1,0:T(8,128)(2,1)S(1)}, u32[]{:S(2)}, u32[]{:S(2)}) collective-permute-start(bf16[104,1216]{1,0:T(8,128)(2,1)S(1)} %slice.40), channel_id=1, source_target_pairs={{0,4},{2,6},{4,0},{6,2},{8,12},{10,14},{12,8},{14,10},{16,20},{18,... | collective-permute-start | bytes 758792 | tf_op jit(solution)/shard_map/ppermute | solution.py:200
  81.2 1.0 %slice.39 = bf16[104,1280]{1,0:T(8,128)(2,1)S(1)} slice(bf16[104,2496]{1,0:T(8,128)(2,1)} %collective-permute-done.19), slice={[0:104], [0:1280]} | slice | bytes 532480 | tf_op jit(solution)/shard_map/slice | solution.py:199
  82.2 0.6 collective-permute-start.20
  82.8 1.6 %convolution_add_fusion.1 = f32[512,2496]{0,1:T(8,128)S(1)} fusion(f32[512,2496]{0,1:T(8,128)S(1)} %convolution_add_fusion.2, bf16[312,512]{1,0:T(8,128)(2,1)S(1)} %bitcast.32, bf16[312,2496]{1,0:T(8,128)(2,1)S(1)} %pad_maximum_fusion.2), kind=kOutput, calls=%fused_computation.2 | convolution fusion | flops 798720000 | bytes 12100608 | tf_op jit(solution)/shard_map/dot_general | solution.py:271
  84.4 1.5 %pad_maximum_fusion.3 = bf16[312,2496]{1,0:T(8,128)(2,1)S(1)} fusion(bf16[104,2496]{1,0:T(8,128)(2,1)} %collective-permute-done.19, bf16[104,2496]{1,0:T(8,128)(2,1)} %collective-permute-done.18, bf16[104,2496]{1,0:T(8,128)(2,1)} %collective-permute-done.7), kind=kLoop, calls=%fused_computation.8 | loop fusion | flops 4672512 | bytes 3115008 | tf_op jit(solution)/shard_map/concatenate | solution.py:264
  85.9 1.6 %convolution_add_fusion = f32[512,2496]{0,1:T(8,128)S(1)} fusion(f32[512,2496]{0,1:T(8,128)S(1)} %convolution_add_fusion.1, bf16[312,512]{1,0:T(8,128)(2,1)S(1)} %bitcast.31, bf16[312,2496]{1,0:T(8,128)(2,1)S(1)} %pad_maximum_fusion.3), kind=kOutput, calls=%fused_computation.1 | convolution fusion | flops 798720000 | bytes 12100608 | tf_op jit(solution)/shard_map/dot_general | solution.py:271
  87.6 0.2 collective-permute-done.21
  87.8 0.9 collective-permute-done.20
  88.7 0.1 maximum_maximum_fusion
  88.8 3.0 %select_convert_fusion = bf16[512,2496]{0,1:T(8,128)(2,1)} fusion(f32[512,2496]{0,1:T(8,128)S(1)} %convolution_add_fusion, bf16[312,512]{1,0:T(8,128)(2,1)S(1)} %bitcast.29, bf16[312,2496]{1,0:T(8,128)(2,1)S(1)} %maximum_maximum_fusion, pred[512]{0:T(512)(128)(4,1)S(1)} %fusion.8), kind=kOutput, calls=%fused_computation | convolution fusion | flops 801275904 | bytes 9545216 | tf_op jit(solution)/shard_map/dot_general | solution.py:271
  (45 shorter events, 0.3 us)
Async XLA Ops:
  0.0 17.8 %collective-permute-start.1 = (bf16[104,2496]{1,0:T(8,128)(2,1)}, bf16[104,2496]{1,0:T(8,128)(2,1)S(1)}, u32[]{:S(2)}, u32[]{:S(2)}) collective-permute-start(bf16[104,2496]{1,0:T(8,128)(2,1)} %param.16), channel_id=1, source_target_pairs={{0,8},{2,10},{4,12},{6,14},{8,24},{10,26},{12,28},{14,30},{16,0},{... | collective-permute-start | bytes 1557512 | tf_op jit(solution)/shard_map/ppermute | solution.py:193
  3.0 14.8 %collective-permute-start.2 = (bf16[104,2496]{1,0:T(8,128)(2,1)}, bf16[104,2496]{1,0:T(8,128)(2,1)S(1)}, u32[]{:S(2)}, u32[]{:S(2)}) collective-permute-start(bf16[104,2496]{1,0:T(8,128)(2,1)} %param.16), channel_id=1, source_target_pairs={{0,2},{2,0},{4,6},{6,4},{8,10},{10,8},{12,14},{14,12},{16,18},{18,... | collective-permute-start | bytes 1557512 | tf_op jit(solution)/shard_map/ppermute | solution.py:196
  4.5 13.5 %collective-permute-start.3 = (bf16[104,2496]{1,0:T(8,128)(2,1)}, bf16[104,2496]{1,0:T(8,128)(2,1)S(1)}, u32[]{:S(2)}, u32[]{:S(2)}) collective-permute-start(bf16[104,2496]{1,0:T(8,128)(2,1)} %param.16), channel_id=1, source_target_pairs={{0,4},{2,6},{4,0},{6,2},{8,12},{10,14},{12,8},{14,10},{16,20},{18,... | collective-permute-start | bytes 1557512 | tf_op jit(solution)/shard_map/ppermute | solution.py:196
  6.0 1.1 %copy-start.2 = (bf16[448,832]{1,0:T(8,128)(2,1)S(1)}, bf16[448,832]{1,0:T(8,128)(2,1)}, u32[]{:S(2)}) copy-start(bf16[448,832]{1,0:T(8,128)(2,1)} %patches_ref.1) | copy-start | bytes 2236420
  7.9 2.8 %collective-permute-start = (f32[4,112,256]{2,1,0:T(8,128)S(1)}, f32[4,112,256]{2,1,0:T(8,128)S(1)}, u32[]{:S(2)}, u32[]{:S(2)}) collective-permute-start(f32[4,112,256]{2,1,0:T(8,128)S(1)} %get-tuple-element.45.refs_0_), channel_id=1, source_target_pairs={{0,1},{1,0},{2,3},{3,2},{4,5},{5,4},{6,7},{7,6},{8,9},{9,8},{10,11... | collective-permute-start | bytes 1376264 | tf_op jit(solution)/shard_map/ppermute | solution.py:26
  10.8 4.1 %copy-start = (bf16[4,832,1664]{2,1,0:T(8,128)(2,1)S(1)}, bf16[4,832,1664]{2,1,0:T(8,128)(2,1)}, u32[]{:S(2)}) copy-start(bf16[4,832,1664]{2,1,0:T(8,128)(2,1)} %refs_2_.1) | copy-start | bytes 33226756
  14.9 6.3 %copy-start.1 = (bf16[512,832]{0,1:T(8,128)(2,1)S(1)}, bf16[512,832]{0,1:T(8,128)(2,1)}, u32[]{:S(2)}) copy-start(bf16[512,832]{0,1:T(8,128)(2,1)} %param.14) | copy-start | bytes 2555908
  17.8 32.1 %copy-start.10 = (bf16[1664]{0:T(1024)(128)(2,1)S(1)}, bf16[1664]{0:T(1024)(128)(2,1)}, u32[]{:S(2)}) copy-start(bf16[1664]{0:T(1024)(128)(2,1)} %param.15) | copy-start | bytes 9988
  17.9 32.0 %copy-start.8 = (bf16[104,2496]{1,0:T(8,128)(2,1)}, bf16[104,2496]{1,0:T(8,128)(2,1)S(1)}, u32[]{:S(2)}) copy-start(bf16[104,2496]{1,0:T(8,128)(2,1)S(1)} %collective-permute-done.1) | copy-start | bytes 1557508
  17.9 0.8 copy-start.4
  18.0 1.0 %copy-start.6 = (bf16[104,2496]{1,0:T(8,128)(2,1)}, bf16[104,2496]{1,0:T(8,128)(2,1)S(1)}, u32[]{:S(2)}) copy-start(bf16[104,2496]{1,0:T(8,128)(2,1)S(1)} %collective-permute-done.3) | copy-start | bytes 1557508
  18.0 10.7 %collective-permute-start.8 = (bf16[104,1280]{1,0:T(8,128)(2,1)S(1)}, bf16[104,1280]{1,0:T(8,128)(2,1)}, u32[]{:S(2)}, u32[]{:S(2)}) collective-permute-start(bf16[104,1280]{1,0:T(8,128)(2,1)S(1)} %slice.33), channel_id=1, source_target_pairs={{0,2},{2,0},{4,6},{6,4},{8,10},{10,8},{12,14},{14,12},{16,18},{18,... | collective-permute-start | bytes 798728 | tf_op jit(solution)/shard_map/ppermute | solution.py:199
  19.0 8.8 %collective-permute-start.9 = (bf16[104,1216]{1,0:T(8,128)(2,1)S(1)}, bf16[104,1216]{1,0:T(8,128)(2,1)}, u32[]{:S(2)}, u32[]{:S(2)}) collective-permute-start(bf16[104,1216]{1,0:T(8,128)(2,1)S(1)} %slice.34), channel_id=1, source_target_pairs={{0,4},{2,6},{4,0},{6,2},{8,12},{10,14},{12,8},{14,10},{16,20},{18,... | collective-permute-start | bytes 758792 | tf_op jit(solution)/shard_map/ppermute | solution.py:200
  21.3 9.1 %collective-permute-start.16 = (f32[112,832]{1,0:T(8,128)}, f32[112,832]{1,0:T(8,128)}, u32[]{:S(2)}, u32[]{:S(2)}) collective-permute-start(f32[112,832]{1,0:T(8,128)} %constant_dynamic-slice_fusion.1), channel_id=1, source_target_pairs={{0,1},{1,0},{2,3},{3,2},{4,5},{5,4},{6,7},{7,6},{8,9},{9,8},{10,11... | collective-permute-start | bytes 1118216 | tf_op jit(solution)/shard_map/ppermute | solution.py:26
  21.3 47.7 %collective-permute-start.15 = (bf16[832,512]{1,0:T(8,128)(2,1)S(1)}, bf16[832,512]{1,0:T(8,128)(2,1)S(1)}, u32[]{:S(2)}, u32[]{:S(2)}) collective-permute-start(bf16[832,512]{1,0:T(8,128)(2,1)S(1)} %bitcast.27), channel_id=1, source_target_pairs={{0,1},{1,0},{2,3},{3,2},{4,5},{5,4},{6,7},{7,6},{8,9},{9,8},{10,11... | collective-permute-start | bytes 2555912 | tf_op jit(solution)/shard_map/ppermute | solution.py:26
  21.9 16.2 %collective-permute-start.4 = (bf16[104,2496]{1,0:T(8,128)(2,1)S(1)}, bf16[104,2496]{1,0:T(8,128)(2,1)}, u32[]{:S(2)}, u32[]{:S(2)}) collective-permute-start(bf16[104,2496]{1,0:T(8,128)(2,1)S(1)} %collective-permute-done.1), channel_id=1, source_target_pairs={{0,8},{2,10},{4,12},{6,14},{8,24},{10,26},{12,28},{14,30},{16,0},{... | collective-permute-start | bytes 1557512 | tf_op jit(solution)/shard_map/ppermute | solution.py:193
  27.9 15.0 %collective-permute-start.5 = (bf16[104,2496]{1,0:T(8,128)(2,1)S(1)}, bf16[104,2496]{1,0:T(8,128)(2,1)}, u32[]{:S(2)}, u32[]{:S(2)}) collective-permute-start(bf16[104,2496]{1,0:T(8,128)(2,1)S(1)} %collective-permute-done.1), channel_id=1, source_target_pairs={{0,2},{2,0},{4,6},{6,4},{8,10},{10,8},{12,14},{14,12},{16,18},{18,... | collective-permute-start | bytes 1557512 | tf_op jit(solution)/shard_map/ppermute | solution.py:196
  28.8 15.5 %collective-permute-start.6 = (bf16[104,2496]{1,0:T(8,128)(2,1)S(1)}, bf16[104,2496]{1,0:T(8,128)(2,1)}, u32[]{:S(2)}, u32[]{:S(2)}) collective-permute-start(bf16[104,2496]{1,0:T(8,128)(2,1)S(1)} %collective-permute-done.1), channel_id=1, source_target_pairs={{0,4},{2,6},{4,0},{6,2},{8,12},{10,14},{12,8},{14,10},{16,20},{18,... | collective-permute-start | bytes 1557512 | tf_op jit(solution)/shard_map/ppermute | solution.py:196
  32.6 32.2 %all-to-all-start = ((bf16[16,16,896]{2,1,0:T(8,128)(2,1)}), bf16[16,16,896]{2,1,0:T(8,128)(2,1)S(1)}, u32[]{:S(2)}, u32[]{:S(2)}) async-start(bf16[16,16,896]{2,1,0:T(8,128)(2,1)} %bitcast.5), calls=%async_computation | async-start | bytes 917504 | tf_op jit(solution)/shard_map/all_to_all | solution.py:240
  44.2 17.7 %collective-permute-start.7 = (bf16[104,2496]{1,0:T(8,128)(2,1)}, bf16[104,2496]{1,0:T(8,128)(2,1)}, u32[]{:S(2)}, u32[]{:S(2)}) collective-permute-start(bf16[104,2496]{1,0:T(8,128)(2,1)} %collective-permute-done.4), channel_id=1, source_target_pairs={{0,8},{2,10},{4,12},{6,14},{8,24},{10,26},{12,28},{14,30},{16,0},{... | collective-permute-start | bytes 1557512 | tf_op jit(solution)/shard_map/ppermute | solution.py:193
  47.3 14.6 %collective-permute-start.11 = (bf16[104,2496]{1,0:T(8,128)(2,1)}, bf16[104,2496]{1,0:T(8,128)(2,1)}, u32[]{:S(2)}, u32[]{:S(2)}) collective-permute-start(bf16[104,2496]{1,0:T(8,128)(2,1)} %collective-permute-done.4), channel_id=1, source_target_pairs={{0,2},{2,0},{4,6},{6,4},{8,10},{10,8},{12,14},{14,12},{16,18},{18,... | collective-permute-start | bytes 1557512 | tf_op jit(solution)/shard_map/ppermute | solution.py:196
  49.1 12.8 %collective-permute-start.12 = (bf16[104,2496]{1,0:T(8,128)(2,1)}, bf16[104,2496]{1,0:T(8,128)(2,1)}, u32[]{:S(2)}, u32[]{:S(2)}) collective-permute-start(bf16[104,2496]{1,0:T(8,128)(2,1)} %collective-permute-done.4), channel_id=1, source_target_pairs={{0,4},{2,6},{4,0},{6,2},{8,12},{10,14},{12,8},{14,10},{16,20},{18,... | collective-permute-start | bytes 1557512 | tf_op jit(solution)/shard_map/ppermute | solution.py:196
  61.9 15.4 %collective-permute-start.18 = (bf16[104,2496]{1,0:T(8,128)(2,1)}, bf16[104,2496]{1,0:T(8,128)(2,1)}, u32[]{:S(2)}, u32[]{:S(2)}) collective-permute-start(bf16[104,2496]{1,0:T(8,128)(2,1)} %collective-permute-done.7), channel_id=1, source_target_pairs={{0,2},{2,0},{4,6},{6,4},{8,10},{10,8},{12,14},{14,12},{16,18},{18,... | collective-permute-start | bytes 1557512 | tf_op jit(solution)/shard_map/ppermute | solution.py:196
  63.4 15.4 %collective-permute-start.19 = (bf16[104,2496]{1,0:T(8,128)(2,1)}, bf16[104,2496]{1,0:T(8,128)(2,1)}, u32[]{:S(2)}, u32[]{:S(2)}) collective-permute-start(bf16[104,2496]{1,0:T(8,128)(2,1)} %collective-permute-done.7), channel_id=1, source_target_pairs={{0,4},{2,6},{4,0},{6,2},{8,12},{10,14},{12,8},{14,10},{16,20},{18,... | collective-permute-start | bytes 1557512 | tf_op jit(solution)/shard_map/ppermute | solution.py:196
  64.8 3.9 %copy-start.5 = (bf16[104,2496]{1,0:T(8,128)(2,1)S(1)}, bf16[104,2496]{1,0:T(8,128)(2,1)}, u32[]{:S(2)}) copy-start(bf16[104,2496]{1,0:T(8,128)(2,1)} %copy-done.4) | copy-start | bytes 1557508
  64.8 3.9 %copy-start.7 = (bf16[104,2496]{1,0:T(8,128)(2,1)S(1)}, bf16[104,2496]{1,0:T(8,128)(2,1)}, u32[]{:S(2)}) copy-start(bf16[104,2496]{1,0:T(8,128)(2,1)} %copy-done.6) | copy-start | bytes 1557508
  64.8 3.9 %copy-start.9 = (bf16[104,2496]{1,0:T(8,128)(2,1)S(1)}, bf16[104,2496]{1,0:T(8,128)(2,1)}, u32[]{:S(2)}) copy-start(bf16[104,2496]{1,0:T(8,128)(2,1)} %param.16) | copy-start | bytes 1557508
  64.8 4.8 %collective-permute-start.17 = (bf16[256,896]{1,0:T(8,128)(2,1)S(1)}, bf16[256,896]{1,0:T(8,128)(2,1)S(1)}, u32[]{:S(2)}, u32[]{:S(2)}) collective-permute-start(bf16[256,896]{1,0:T(8,128)(2,1)S(1)} %bitcast.25), channel_id=1, source_target_pairs={{0,1},{1,0},{2,3},{3,2},{4,5},{5,4},{6,7},{7,6},{8,9},{9,8},{10,11... | collective-permute-start | bytes 1376264 | tf_op jit(solution)/shard_map/ppermute | solution.py:26
  68.5 19.1 %collective-permute-start.10 = (bf16[104,2496]{1,0:T(8,128)(2,1)S(1)}, bf16[104,2496]{1,0:T(8,128)(2,1)S(1)}, u32[]{:S(2)}, u32[]{:S(2)}) collective-permute-start(bf16[104,2496]{1,0:T(8,128)(2,1)S(1)} %pad_maximum_fusion.4), channel_id=1, source_target_pairs={{0,8},{2,10},{4,12},{6,14},{8,24},{10,26},{12,28},{14,30},{16,0},{... | collective-permute-start | bytes 1557512 | tf_op jit(solution)/shard_map/ppermute | solution.py:193
  68.9 18.6 %collective-permute-start.14 = (bf16[104,1216]{1,0:T(8,128)(2,1)S(1)}, bf16[104,1216]{1,0:T(8,128)(2,1)S(1)}, u32[]{:S(2)}, u32[]{:S(2)}) collective-permute-start(bf16[104,1216]{1,0:T(8,128)(2,1)S(1)} %slice.36), channel_id=1, source_target_pairs={{0,4},{2,6},{4,0},{6,2},{8,12},{10,14},{12,8},{14,10},{16,20},{18,... | collective-permute-start | bytes 758792 | tf_op jit(solution)/shard_map/ppermute | solution.py:200
  69.6 18.0 %collective-permute-start.13 = (bf16[104,1280]{1,0:T(8,128)(2,1)S(1)}, bf16[104,1280]{1,0:T(8,128)(2,1)S(1)}, u32[]{:S(2)}, u32[]{:S(2)}) collective-permute-start(bf16[104,1280]{1,0:T(8,128)(2,1)S(1)} %slice.35), channel_id=1, source_target_pairs={{0,2},{2,0},{4,6},{6,4},{8,10},{10,8},{12,14},{14,12},{16,18},{18,... | collective-permute-start | bytes 798728 | tf_op jit(solution)/shard_map/ppermute | solution.py:199
  72.2 1.6 %copy-start.3 = (bf16[312,2496]{1,0:T(8,128)(2,1)S(1)}, bf16[312,2496]{1,0:T(8,128)(2,1)}, u32[]{:S(2)}) copy-start(bf16[312,2496]{1,0:T(8,128)(2,1)} %pad_maximum_fusion.1) | copy-start | bytes 4672516
  79.7 8.1 %collective-permute-start.21 = (bf16[104,1216]{1,0:T(8,128)(2,1)S(1)}, bf16[104,1216]{1,0:T(8,128)(2,1)S(1)}, u32[]{:S(2)}, u32[]{:S(2)}) collective-permute-start(bf16[104,1216]{1,0:T(8,128)(2,1)S(1)} %slice.40), channel_id=1, source_target_pairs={{0,4},{2,6},{4,0},{6,2},{8,12},{10,14},{12,8},{14,10},{16,20},{18,... | collective-permute-start | bytes 758792 | tf_op jit(solution)/shard_map/ppermute | solution.py:200
  82.2 6.5 %collective-permute-start.20 = (bf16[104,1280]{1,0:T(8,128)(2,1)S(1)}, bf16[104,1280]{1,0:T(8,128)(2,1)S(1)}, u32[]{:S(2)}, u32[]{:S(2)}) collective-permute-start(bf16[104,1280]{1,0:T(8,128)(2,1)S(1)} %slice.39), channel_id=1, source_target_pairs={{0,2},{2,0},{4,6},{6,4},{8,10},{10,8},{12,14},{14,12},{16,18},{18,... | collective-permute-start | bytes 798728 | tf_op jit(solution)/shard_map/ppermute | solution.py:199

commit v19 on v18

--- a/solution.py
+++ b/solution.py
@@ -198,12 +198,11 @@
     def to_corner(by_x, by_y):
         left = lax.ppermute(by_y[:, :cut], "req", x_perm)
         right = lax.ppermute(by_x[:, cut:], "req", y_perm)
-        return jnp.concatenate([left, right], axis=1)
+        return left, right
 
     held = [qkv_weight]
     held.append(along_line(held[0]))
     sides = [to_sides(held[0])]
-    corners = []
     picked, stats_own = pick_rows(patches, merge_weight.shape[0])
     stats = [stats_own] + [tp_shift(stats_own, n_tp, d) for d in range(1, n_tp)]
     gain_bias = jnp.stack([ln_gain, ln_bias])
@@ -227,8 +226,9 @@
     )
     held.append(along_line(held[1]))
     sides.append(to_sides(held[1]))
-    corners.append(to_corner(*sides[0]))
     merged = tp_scatter_sum(partial_value, n_tp, 1).astype(jnp.bfloat16)
+    merged, sides[0] = tie(merged, sides[0])
+    halves = to_corner(*sides[0])
     padding = (-width - 2) % 128
     payload = jnp.concatenate(
         [merged, code_cols, jnp.zeros((token_count, padding), jnp.bfloat16)], axis=1
@@ -249,16 +249,16 @@
     images = [arrived] + [tp_shift(arrived, n_tp, d) for d in range(1, n_tp)]
     blocks = combine(tp_index, order, texts, images, gain_column)
 
-    held[3], corners[0] = tie(held[3], corners[0])
+    held[3], sides[2], halves = tie(held[3], sides[2], halves)
+    sides.append(to_sides(held[3]))
+    corners = [jnp.concatenate(halves, axis=1)]
     corners.append(along_line(corners[0]))
-    held[3], sides[2] = tie(held[3], sides[2])
-    sides.append(to_sides(held[3]))
     for step in range(4, lines):
         held.append(along_line(held[step - 1]))
         sides.append(to_sides(held[step]))
     for step in range(2, lines - 2):
         corners.append(along_line(corners[step - 1]))
-    corners.append(to_corner(*sides[-2]))
+    corners.append(jnp.concatenate(to_corner(*sides[-2]), axis=1))
 
     def add_product(total, first, weights):
         weight = jnp.concatenate(weights, axis=0)
@@ -277,7 +277,7 @@
     total = add_product(total, 4, [held[1], *sides[1]])
 
     total, sides[-1] = tie(total, sides[-1])
-    corners.append(to_corner(*sides[-1]))
+    corners.append(jnp.concatenate(to_corner(*sides[-1]), axis=1))
     for step in range(2, lines - 1):
         total = add_product(total, step * 3 + 1, [held[step], *sides[step]])
     total, late = tie(total, [held[-1], *sides[-1]])

time: 92.4 us -> 92.2 us (level)
  local copies, waits for them, and re-layouts: 14.3 us -> 17.3 us
  waiting for transfers between devices: 21.3 us -> 19.4 us
    ppermute x4, waiting for transfers between devices: 6.61 us -> 2.06 us  [to_sides(): lax.ppermute(block, 'req', x_perm)]
    ppermute x4, waiting for transfers between devices: 7.86 us -> 11.6 us  [along_line(): return lax.ppermute(block, 'req', line_perm)]
    ppermute x4, starting transfers between devices: 3.47 us -> 6.69 us  [to_sides(): lax.ppermute(block, 'req', y_perm)]
    ppermute x3, waiting for transfers between devices: 2.89 us -> 0.01 us  [to_corner(): right = lax.ppermute(by_x[:, cut:], 'req', y_perm)]
    concatenate x5, other arithmetic: 6 us -> 8.44 us  [add_product(): weight = jnp.concatenate(weights, axis=0)]
    ppermute x4, starting transfers between devices: 8.9 us -> 6.47 us  [along_line(): return lax.ppermute(block, 'req', line_perm)]
    unnamed x22 -> x21, local copies, waits for them, and re-layouts: 5.67 us -> 7.84 us
    ppermute x3, starting transfers between devices: 1.79 us -> 3.9 us  [to_corner(): left = lax.ppermute(by_y[:, :cut], 'req', x_perm)]
  transfers between devices with their start and end apart: 23 -> 23, of which waited for: 9 -> 6; matrix products, arithmetic and copies ran while one was open for 29% -> 30% of each run, Pallas kernels for 6% -> 6%
where the time goes in v19:
time: 92.2 us; the launch traced here: 91.5 us
  starting transfers between devices  29 us (31%)
  waiting for transfers between devices  19.4 us (21%)
  local copies, waits for them, and re-layouts  17.3 us (19%)
  matrix products  10.4 us (11%)
  other arithmetic  9.61 us (10%)
  Pallas kernels  5.51 us (6%)
    ppermute x4, waiting for transfers between devices, along_line(): return lax.ppermute(block, 'req', line_perm)  11.6 us
    dot_general x5, matrix products, add_product(): lax.dot_general(source, weight, (((0,), (0,)), ((), ())), preferred_eleme...  9.31 us
    concatenate x5, other arithmetic, add_product(): weight = jnp.concatenate(weights, axis=0)  8.44 us
    unnamed x21, local copies, waits for them, and re-layouts  7.84 us
    ppermute x4, starting transfers between devices, to_sides(): lax.ppermute(block, 'req', y_perm)  6.69 us
    ppermute x4, starting transfers between devices, along_line(): return lax.ppermute(block, 'req', line_perm)  6.47 us
    ppermute x4, starting transfers between devices, to_sides(): lax.ppermute(block, 'req', x_perm)  4.55 us
    ppermute x3, starting transfers between devices, to_corner(): left = lax.ppermute(by_y[:, :cut], 'req', x_perm)  3.9 us
  transfers between devices with their start and end apart: 23, of which 6 were waited for; matrix products, arithmetic and copies ran while one was open for 30% of the time, Pallas kernels for 6%

profile of v19, /device:TPU:0, one launch (start us, length us, event | category | flops | bytes accessed | tf_op | source)
XLA Modules:
  0.0 91.5 jit_solution(7618994811105378895)
XLA Ops:
  0.0 3.0 %collective-permute-start.1 = (bf16[104,2496]{1,0:T(8,128)(2,1)}, bf16[104,2496]{1,0:T(8,128)(2,1)}, u32[]{:S(2)}, u32[]{:S(2)}) collective-permute-start(bf16[104,2496]{1,0:T(8,128)(2,1)} %param.16), channel_id=1, source_target_pairs={{0,8},{2,10},{4,12},{6,14},{8,24},{10,26},{12,28},{14,30},{16,0},{... | collective-permute-start | bytes 1557512 | tf_op jit(solution)/shard_map/ppermute | solution.py:193
  3.0 1.5 %collective-permute-start.2 = (bf16[104,2496]{1,0:T(8,128)(2,1)}, bf16[104,2496]{1,0:T(8,128)(2,1)S(1)}, u32[]{:S(2)}, u32[]{:S(2)}) collective-permute-start(bf16[104,2496]{1,0:T(8,128)(2,1)} %param.16), channel_id=1, source_target_pairs={{0,2},{2,0},{4,6},{6,4},{8,10},{10,8},{12,14},{14,12},{16,18},{18,... | collective-permute-start | bytes 1557512 | tf_op jit(solution)/shard_map/ppermute | solution.py:196
  4.5 1.5 %collective-permute-start.3 = (bf16[104,2496]{1,0:T(8,128)(2,1)}, bf16[104,2496]{1,0:T(8,128)(2,1)S(1)}, u32[]{:S(2)}, u32[]{:S(2)}) collective-permute-start(bf16[104,2496]{1,0:T(8,128)(2,1)} %param.16), channel_id=1, source_target_pairs={{0,4},{2,6},{4,0},{6,2},{8,12},{10,14},{12,8},{14,10},{16,20},{18,... | collective-permute-start | bytes 1557512 | tf_op jit(solution)/shard_map/ppermute | solution.py:196
  6.0 1.1 %copy-done.2 = bf16[448,832]{1,0:T(8,128)(2,1)S(1)} copy-done((bf16[448,832]{1,0:T(8,128)(2,1)S(1)}, bf16[448,832]{1,0:T(8,128)(2,1)}, u32[]{:S(2)}) %copy-start.2) | copy-done | bytes 745496
  7.2 0.8 shard_map.118
  7.9 0.1 collective-permute-start
  8.0 0.7 convert_bitcast_fusion.1
  8.7 0.7 stack.22
  9.4 0.7 stack.21
  10.1 0.2 convert_reduce_fusion
  10.3 4.1 %copy-done = bf16[4,832,1664]{2,1,0:T(8,128)(2,1)S(1)} copy-done((bf16[4,832,1664]{2,1,0:T(8,128)(2,1)S(1)}, bf16[4,832,1664]{2,1,0:T(8,128)(2,1)}, u32[]{:S(2)}) %copy-start) | copy-done | bytes 11075608
  14.5 2.9 %shard_map.119 = f32[112,1664]{1,0:T(8,128)S(1)} custom-call(bf16[4,112,832]{2,1,0:T(8,128)(2,1)S(1)} %get-tuple-element.47.picked_ref, bf16[2,832]{1,0:T(2,128)(2,1)S(1)} %pad_maximum_fusion.4.gain_bias_ref, f32[4,112,256]{2,1,0:T(8,128)S(1)} %get-tuple-element.48.refs_0_, f32[4,112,256]{2,1,0:T(8,128)S(1)} %collective-permute-done.refs_1_, ...), custom_call_target="tpu_custom_call" | custom-call | flops 1000 | bytes 1000 | tf_op jit(solution)/shard_map/pallas_call | solution.py:117
  17.4 0.6 collective-permute-done.3
  18.0 0.2 constant_dynamic-slice_fusion
  18.2 0.1 collective-permute-start.10
  18.3 2.6 %collective-permute-start.4 = (bf16[104,2496]{1,0:T(8,128)(2,1)}, bf16[104,2496]{1,0:T(8,128)(2,1)}, u32[]{:S(2)}, u32[]{:S(2)}) collective-permute-start(bf16[104,2496]{1,0:T(8,128)(2,1)} %collective-permute-done.1), channel_id=1, source_target_pairs={{0,8},{2,10},{4,12},{6,14},{8,24},{10,26},{12,28},{14,30},{16,0},{... | collective-permute-start | bytes 1557512 | tf_op jit(solution)/shard_map/ppermute | solution.py:193
  20.9 0.5 collective-permute-start.5
  21.4 1.5 %collective-permute-start.6 = (bf16[104,2496]{1,0:T(8,128)(2,1)}, bf16[104,2496]{1,0:T(8,128)(2,1)}, u32[]{:S(2)}, u32[]{:S(2)}) collective-permute-start(bf16[104,2496]{1,0:T(8,128)(2,1)} %collective-permute-done.1), channel_id=1, source_target_pairs={{0,4},{2,6},{4,0},{6,2},{8,12},{10,14},{12,8},{14,10},{16,20},{18,... | collective-permute-start | bytes 1557512 | tf_op jit(solution)/shard_map/ppermute | solution.py:196
  23.0 0.1 pad.17.clone
  23.0 0.1 copy.18
  23.2 0.2 add_convert_fusion
  23.4 0.0 copy-start.1
  23.4 1.0 %convolution_convert_fusion = bf16[256,896]{1,0:T(8,128)(2,1)} fusion(bf16[112,2]{1,0:T(8,128)(2,1)S(1)} %copy.18, bf16[112,832]{1,0:T(8,128)(2,1)S(1)} %add_convert_fusion, bf16[896]{0:T(1024)(128)(2,1)S(1)} %pad.17.clone, s32[112]{0:T(128)S(1)} %multiply_add_fusion), kind=kOutput, calls=%fused_computation.9 | convolution fusion | flops 52240384 | bytes 647808 | tf_op jit(solution)/shard_map/dot_general | solution.py:239
  24.4 3.6 %all-to-all-start = ((bf16[16,16,896]{2,1,0:T(8,128)(2,1)}), bf16[16,16,896]{2,1,0:T(8,128)(2,1)S(1)}, u32[]{:S(2)}, u32[]{:S(2)}) async-start(bf16[16,16,896]{2,1,0:T(8,128)(2,1)} %bitcast.5), calls=%async_computation | async-start | bytes 917504 | tf_op jit(solution)/shard_map/all_to_all | solution.py:240
  28.0 0.7 slice.33
  28.7 1.8 %collective-permute-start.11 = (bf16[104,1280]{1,0:T(8,128)(2,1)}, bf16[104,1280]{1,0:T(8,128)(2,1)}, u32[]{:S(2)}, u32[]{:S(2)}) collective-permute-start(bf16[104,1280]{1,0:T(8,128)(2,1)} %slice.33), channel_id=1, source_target_pairs={{0,2},{2,0},{4,6},{6,4},{8,10},{10,8},{12,14},{14,12},{16,18},{18,... | collective-permute-start | bytes 798728 | tf_op jit(solution)/shard_map/ppermute | solution.py:199
  30.5 0.7 slice.34
  31.3 1.5 %collective-permute-start.12 = (bf16[104,1216]{1,0:T(8,128)(2,1)}, bf16[104,1216]{1,0:T(8,128)(2,1)}, u32[]{:S(2)}, u32[]{:S(2)}) collective-permute-start(bf16[104,1216]{1,0:T(8,128)(2,1)} %slice.34), channel_id=1, source_target_pairs={{0,4},{2,6},{4,0},{6,2},{8,12},{10,14},{12,8},{14,10},{16,20},{18,... | collective-permute-start | bytes 758792 | tf_op jit(solution)/shard_map/ppermute | solution.py:200
  32.7 4.2 %collective-permute-done.4 = bf16[104,2496]{1,0:T(8,128)(2,1)} collective-permute-done((bf16[104,2496]{1,0:T(8,128)(2,1)}, bf16[104,2496]{1,0:T(8,128)(2,1)}, u32[]{:S(2)}, u32[]{:S(2)}) %collective-permute-start.4) | collective-permute-done | bytes 519200 | tf_op jit(solution)/shard_map/ppermute | solution.py:193
  36.9 2.9 %collective-permute-done.6 = bf16[104,2496]{1,0:T(8,128)(2,1)} collective-permute-done((bf16[104,2496]{1,0:T(8,128)(2,1)}, bf16[104,2496]{1,0:T(8,128)(2,1)}, u32[]{:S(2)}, u32[]{:S(2)}) %collective-permute-start.6) | collective-permute-done | bytes 519200 | tf_op jit(solution)/shard_map/ppermute | solution.py:196
  39.8 1.5 %collective-permute-start.8 = (bf16[104,2496]{1,0:T(8,128)(2,1)}, bf16[104,2496]{1,0:T(8,128)(2,1)S(1)}, u32[]{:S(2)}, u32[]{:S(2)}) collective-permute-start(bf16[104,2496]{1,0:T(8,128)(2,1)} %collective-permute-done.4), channel_id=1, source_target_pairs={{0,2},{2,0},{4,6},{6,4},{8,10},{10,8},{12,14},{14,12},{16,18},{18,... | collective-permute-start | bytes 1557512 | tf_op jit(solution)/shard_map/ppermute | solution.py:196
  41.3 2.1 %collective-permute-start.9 = (bf16[104,2496]{1,0:T(8,128)(2,1)}, bf16[104,2496]{1,0:T(8,128)(2,1)}, u32[]{:S(2)}, u32[]{:S(2)}) collective-permute-start(bf16[104,2496]{1,0:T(8,128)(2,1)} %collective-permute-done.4), channel_id=1, source_target_pairs={{0,4},{2,6},{4,0},{6,2},{8,12},{10,14},{12,8},{14,10},{16,20},{18,... | collective-permute-start | bytes 1557512 | tf_op jit(solution)/shard_map/ppermute | solution.py:196
  43.4 2.6 %pad_maximum_fusion.1 = bf16[312,2496]{1,0:T(8,128)(2,1)} fusion(bf16[104,2496]{1,0:T(8,128)(2,1)} %collective-permute-done.6, bf16[104,2496]{1,0:T(8,128)(2,1)} %collective-permute-done.5, bf16[104,2496]{1,0:T(8,128)(2,1)} %collective-permute-done.1), kind=kLoop, calls=%fused_computation.5 | loop fusion | flops 4672512 | bytes 3115008 | tf_op jit(solution)/shard_map/concatenate | solution.py:264
  46.1 0.1 fusion.7
  46.2 0.7 fusion.10.order_ref
  46.9 0.8 reshape.62.gain_ref
  47.7 0.1 collective-permute-start.16
  47.8 7.4 %collective-permute-done.7 = bf16[104,2496]{1,0:T(8,128)(2,1)} collective-permute-done((bf16[104,2496]{1,0:T(8,128)(2,1)}, bf16[104,2496]{1,0:T(8,128)(2,1)}, u32[]{:S(2)}, u32[]{:S(2)}) %collective-permute-start.7) | collective-permute-done | bytes 519200 | tf_op jit(solution)/shard_map/ppermute | solution.py:193
  55.3 2.1 %collective-permute-done.8 = bf16[104,2496]{1,0:T(8,128)(2,1)S(1)} collective-permute-done((bf16[104,2496]{1,0:T(8,128)(2,1)}, bf16[104,2496]{1,0:T(8,128)(2,1)S(1)}, u32[]{:S(2)}, u32[]{:S(2)}) %collective-permute-start.8) | collective-permute-done | bytes 519200 | tf_op jit(solution)/shard_map/ppermute | solution.py:196
  57.3 0.8 copy-done.5
  58.2 1.0 %collective-permute-start.18 = (bf16[104,2496]{1,0:T(8,128)(2,1)}, bf16[104,2496]{1,0:T(8,128)(2,1)S(1)}, u32[]{:S(2)}, u32[]{:S(2)}) collective-permute-start(bf16[104,2496]{1,0:T(8,128)(2,1)} %collective-permute-done.7), channel_id=1, source_target_pairs={{0,2},{2,0},{4,6},{6,4},{8,10},{10,8},{12,14},{14,12},{16,18},{18,... | collective-permute-start | bytes 1557512 | tf_op jit(solution)/shard_map/ppermute | solution.py:196
  59.2 1.5 %collective-permute-start.19 = (bf16[104,2496]{1,0:T(8,128)(2,1)}, bf16[104,2496]{1,0:T(8,128)(2,1)}, u32[]{:S(2)}, u32[]{:S(2)}) collective-permute-start(bf16[104,2496]{1,0:T(8,128)(2,1)} %collective-permute-done.7), channel_id=1, source_target_pairs={{0,4},{2,6},{4,0},{6,2},{8,12},{10,14},{12,8},{14,10},{16,20},{18,... | collective-permute-start | bytes 1557512 | tf_op jit(solution)/shard_map/ppermute | solution.py:196
  60.7 2.7 %pad_maximum_fusion.2 = bf16[312,2496]{1,0:T(8,128)(2,1)} fusion(bf16[104,2496]{1,0:T(8,128)(2,1)} %collective-permute-done.9, bf16[104,2496]{1,0:T(8,128)(2,1)} %copy-done.5, bf16[104,2496]{1,0:T(8,128)(2,1)} %collective-permute-done.4), kind=kLoop, calls=%fused_computation.7 | loop fusion | flops 4672512 | bytes 3115008 | tf_op jit(solution)/shard_map/concatenate | solution.py:264
  63.4 1.7 %constant_dynamic-update-slice_fusion.1 = bf16[104,2496]{1,0:T(8,128)(2,1)} fusion(bf16[104,1280]{1,0:T(8,128)(2,1)} %collective-permute-done.11), kind=kLoop, calls=%fused_computation.23 | loop fusion | bytes 532480
  65.1 1.7 %constant_dynamic-update-slice_fusion = bf16[104,2496]{1,0:T(8,128)(2,1)} fusion(bf16[104,2496]{1,0:T(8,128)(2,1)} %constant_dynamic-update-slice_fusion.1, bf16[104,1216]{1,0:T(8,128)(2,1)} %collective-permute-done.12), kind=kLoop, calls=%fused_computation.22 | loop fusion | bytes 532480 | tf_op jit(solution)/shard_map/concatenate | solution.py:254
  66.8 1.0 %slice.36 = bf16[104,1216]{1,0:T(8,128)(2,1)S(1)} slice(bf16[104,2496]{1,0:T(8,128)(2,1)} %copy-done.5), slice={[0:104], [1280:2496]} | slice | bytes 505856 | tf_op jit(solution)/shard_map/slice | solution.py:200
  67.7 1.0 %slice.35 = bf16[104,1280]{1,0:T(8,128)(2,1)S(1)} slice(bf16[104,2496]{1,0:T(8,128)(2,1)} %collective-permute-done.9), slice={[0:104], [0:1280]} | slice | bytes 532480 | tf_op jit(solution)/shard_map/slice | solution.py:199
  68.7 0.8 collective-permute-start.13
  69.5 1.7 %pad_maximum_fusion = bf16[416,2496]{1,0:T(8,128)(2,1)S(1)} fusion(bf16[104,2496]{1,0:T(8,128)(2,1)} %constant_dynamic-update-slice_fusion, bf16[104,2496]{1,0:T(8,128)(2,1)} %copy-done.7, bf16[104,2496]{1,0:T(8,128)(2,1)} %copy-done.6, bf16[104,2496]{1,0:T(8,128)(2,1)} %param.16), kind=kLoop, calls=%fused_computation.4 | loop fusion | flops 8306688 | bytes 4153344 | tf_op jit(solution)/shard_map/concatenate | solution.py:264
  71.2 0.6 collective-permute-start.15
  71.8 1.0 %collective-permute-start.14 = (bf16[104,1280]{1,0:T(8,128)(2,1)S(1)}, bf16[104,1280]{1,0:T(8,128)(2,1)S(1)}, u32[]{:S(2)}, u32[]{:S(2)}) collective-permute-start(bf16[104,1280]{1,0:T(8,128)(2,1)S(1)} %slice.35), channel_id=1, source_target_pairs={{0,2},{2,0},{4,6},{6,4},{8,10},{10,8},{12,14},{14,12},{16,18},{18,... | collective-permute-start | bytes 798728 | tf_op jit(solution)/shard_map/ppermute | solution.py:199
  72.8 1.9 %shard_map.120 = bf16[16,104,512]{2,1,0:T(8,128)(2,1)S(1)} custom-call(s32[1]{0:T(128)} %bitcast.2.index_ref, s32[16]{0:T(128)S(1)} %fusion.10.order_ref, bf16[16,104,1]{2,1,0:T(8,128)(2,1)S(1)} %reshape.62.gain_ref, bf16[832,512]{1,0:T(8,128)(2,1)S(1)} %bitcast.28, bf16[832,512]{1,0:T(8,128)(2,1)S(1)} %collective-permute-done.16.refs_1_, ...), custom_call_target="tpu_custom_call" | custom-call | flops 1000 | bytes 1000 | tf_op jit(solution)/shard_map/pallas_call | solution.py:168
  74.7 0.1 fusion.14
  74.8 1.5 %fusion.15 = f32[512,2496]{0,1:T(8,128)S(1)} fusion(bf16[416,512]{1,0:T(8,128)(2,1)S(1)} %bitcast.30, bf16[416,2496]{1,0:T(8,128)(2,1)S(1)} %pad_maximum_fusion), kind=kOutput, calls=%fused_computation.48 | convolution fusion | flops 1063256064 | bytes 7614464 | tf_op jit(solution)/shard_map/dot_general | solution.py:271
  76.4 1.6 %convolution_add_fusion.2 = f32[512,2496]{0,1:T(8,128)S(1)} fusion(f32[512,2496]{0,1:T(8,128)S(1)} %fusion.15, bf16[312,512]{1,0:T(8,128)(2,1)S(1)} %bitcast.33, bf16[312,2496]{1,0:T(8,128)(2,1)S(1)} %copy-done.3), kind=kOutput, calls=%fused_computation.3 | convolution fusion | flops 798720000 | bytes 12100608 | tf_op jit(solution)/shard_map/dot_general | solution.py:271
  78.0 1.6 %collective-permute-start.21 = (bf16[104,1216]{1,0:T(8,128)(2,1)S(1)}, bf16[104,1216]{1,0:T(8,128)(2,1)S(1)}, u32[]{:S(2)}, u32[]{:S(2)}) collective-permute-start(bf16[104,1216]{1,0:T(8,128)(2,1)S(1)} %slice.40), channel_id=1, source_target_pairs={{0,4},{2,6},{4,0},{6,2},{8,12},{10,14},{12,8},{14,10},{16,20},{18,... | collective-permute-start | bytes 758792 | tf_op jit(solution)/shard_map/ppermute | solution.py:200
  79.6 1.0 %slice.39 = bf16[104,1280]{1,0:T(8,128)(2,1)S(1)} slice(bf16[104,2496]{1,0:T(8,128)(2,1)} %collective-permute-done.19), slice={[0:104], [0:1280]} | slice | bytes 532480 | tf_op jit(solution)/shard_map/slice | solution.py:199
  80.6 1.1 %collective-permute-start.20 = (bf16[104,1280]{1,0:T(8,128)(2,1)S(1)}, bf16[104,1280]{1,0:T(8,128)(2,1)S(1)}, u32[]{:S(2)}, u32[]{:S(2)}) collective-permute-start(bf16[104,1280]{1,0:T(8,128)(2,1)S(1)} %slice.39), channel_id=1, source_target_pairs={{0,2},{2,0},{4,6},{6,4},{8,10},{10,8},{12,14},{14,12},{16,18},{18,... | collective-permute-start | bytes 798728 | tf_op jit(solution)/shard_map/ppermute | solution.py:199
  81.7 1.5 %convolution_add_fusion.1 = f32[512,2496]{0,1:T(8,128)S(1)} fusion(f32[512,2496]{0,1:T(8,128)S(1)} %convolution_add_fusion.2, bf16[312,512]{1,0:T(8,128)(2,1)S(1)} %bitcast.32, bf16[312,2496]{1,0:T(8,128)(2,1)S(1)} %copy-done.4), kind=kOutput, calls=%fused_computation.2 | convolution fusion | flops 798720000 | bytes 12100608 | tf_op jit(solution)/shard_map/dot_general | solution.py:271
  83.2 1.3 %pad_maximum_fusion.3 = bf16[312,2496]{1,0:T(8,128)(2,1)S(1)} fusion(bf16[104,2496]{1,0:T(8,128)(2,1)} %collective-permute-done.19, bf16[104,2496]{1,0:T(8,128)(2,1)S(1)} %collective-permute-done.18, bf16[104,2496]{1,0:T(8,128)(2,1)} %collective-permute-done.7), kind=kLoop, calls=%fused_computation.8 | loop fusion | flops 4672512 | bytes 3115008 | tf_op jit(solution)/shard_map/concatenate | solution.py:264
  84.6 1.6 %convolution_add_fusion = f32[512,2496]{0,1:T(8,128)S(1)} fusion(f32[512,2496]{0,1:T(8,128)S(1)} %convolution_add_fusion.1, bf16[312,512]{1,0:T(8,128)(2,1)S(1)} %bitcast.31, bf16[312,2496]{1,0:T(8,128)(2,1)S(1)} %pad_maximum_fusion.3), kind=kOutput, calls=%fused_computation.1 | convolution fusion | flops 798720000 | bytes 12100608 | tf_op jit(solution)/shard_map/dot_general | solution.py:271
  86.2 2.2 %collective-permute-done.20 = bf16[104,1280]{1,0:T(8,128)(2,1)S(1)} collective-permute-done((bf16[104,1280]{1,0:T(8,128)(2,1)S(1)}, bf16[104,1280]{1,0:T(8,128)(2,1)S(1)}, u32[]{:S(2)}, u32[]{:S(2)}) %collective-permute-start.20) | collective-permute-done | bytes 266272 | tf_op jit(solution)/shard_map/ppermute | solution.py:199
  88.3 0.1 maximum_maximum_fusion
  88.5 3.1 %select_convert_fusion = bf16[512,2496]{0,1:T(8,128)(2,1)} fusion(f32[512,2496]{0,1:T(8,128)S(1)} %convolution_add_fusion, bf16[312,512]{1,0:T(8,128)(2,1)S(1)} %bitcast.29, bf16[312,2496]{1,0:T(8,128)(2,1)S(1)} %maximum_maximum_fusion, pred[512]{0:T(512)(128)(4,1)S(1)} %fusion.8), kind=kOutput, calls=%fused_computation | convolution fusion | flops 801275904 | bytes 9545216 | tf_op jit(solution)/shard_map/dot_general | solution.py:271
  (44 shorter events, 0.2 us)
Async XLA Ops:
  0.0 17.4 %collective-permute-start.1 = (bf16[104,2496]{1,0:T(8,128)(2,1)}, bf16[104,2496]{1,0:T(8,128)(2,1)}, u32[]{:S(2)}, u32[]{:S(2)}) collective-permute-start(bf16[104,2496]{1,0:T(8,128)(2,1)} %param.16), channel_id=1, source_target_pairs={{0,8},{2,10},{4,12},{6,14},{8,24},{10,26},{12,28},{14,30},{16,0},{... | collective-permute-start | bytes 1557512 | tf_op jit(solution)/shard_map/ppermute | solution.py:193
  3.0 14.4 %collective-permute-start.2 = (bf16[104,2496]{1,0:T(8,128)(2,1)}, bf16[104,2496]{1,0:T(8,128)(2,1)S(1)}, u32[]{:S(2)}, u32[]{:S(2)}) collective-permute-start(bf16[104,2496]{1,0:T(8,128)(2,1)} %param.16), channel_id=1, source_target_pairs={{0,2},{2,0},{4,6},{6,4},{8,10},{10,8},{12,14},{14,12},{16,18},{18,... | collective-permute-start | bytes 1557512 | tf_op jit(solution)/shard_map/ppermute | solution.py:196
  4.5 13.5 %collective-permute-start.3 = (bf16[104,2496]{1,0:T(8,128)(2,1)}, bf16[104,2496]{1,0:T(8,128)(2,1)S(1)}, u32[]{:S(2)}, u32[]{:S(2)}) collective-permute-start(bf16[104,2496]{1,0:T(8,128)(2,1)} %param.16), channel_id=1, source_target_pairs={{0,4},{2,6},{4,0},{6,2},{8,12},{10,14},{12,8},{14,10},{16,20},{18,... | collective-permute-start | bytes 1557512 | tf_op jit(solution)/shard_map/ppermute | solution.py:196
  6.0 1.1 %copy-start.2 = (bf16[448,832]{1,0:T(8,128)(2,1)S(1)}, bf16[448,832]{1,0:T(8,128)(2,1)}, u32[]{:S(2)}) copy-start(bf16[448,832]{1,0:T(8,128)(2,1)} %patches_ref.1) | copy-start | bytes 2236420
  7.9 2.4 %collective-permute-start = (f32[4,112,256]{2,1,0:T(8,128)S(1)}, f32[4,112,256]{2,1,0:T(8,128)S(1)}, u32[]{:S(2)}, u32[]{:S(2)}) collective-permute-start(f32[4,112,256]{2,1,0:T(8,128)S(1)} %get-tuple-element.48.refs_0_), channel_id=1, source_target_pairs={{0,1},{1,0},{2,3},{3,2},{4,5},{5,4},{6,7},{7,6},{8,9},{9,8},{10,11... | collective-permute-start | bytes 1376264 | tf_op jit(solution)/shard_map/ppermute | solution.py:26
  10.3 4.1 %copy-start = (bf16[4,832,1664]{2,1,0:T(8,128)(2,1)S(1)}, bf16[4,832,1664]{2,1,0:T(8,128)(2,1)}, u32[]{:S(2)}) copy-start(bf16[4,832,1664]{2,1,0:T(8,128)(2,1)} %refs_2_.1) | copy-start | bytes 33226756
  17.4 28.7 %copy-start.6 = (bf16[104,2496]{1,0:T(8,128)(2,1)}, bf16[104,2496]{1,0:T(8,128)(2,1)S(1)}, u32[]{:S(2)}) copy-start(bf16[104,2496]{1,0:T(8,128)(2,1)S(1)} %collective-permute-done.2) | copy-start | bytes 1557508
  18.0 29.7 %copy-start.7 = (bf16[104,2496]{1,0:T(8,128)(2,1)}, bf16[104,2496]{1,0:T(8,128)(2,1)S(1)}, u32[]{:S(2)}) copy-start(bf16[104,2496]{1,0:T(8,128)(2,1)S(1)} %collective-permute-done.3) | copy-start | bytes 1557508
  18.2 5.0 %collective-permute-start.10 = (f32[112,832]{1,0:T(8,128)S(1)}, f32[112,832]{1,0:T(8,128)S(1)}, u32[]{:S(2)}, u32[]{:S(2)}) collective-permute-start(f32[112,832]{1,0:T(8,128)S(1)} %constant_dynamic-slice_fusion), channel_id=1, source_target_pairs={{0,1},{1,0},{2,3},{3,2},{4,5},{5,4},{6,7},{7,6},{8,9},{9,8},{10,11... | collective-permute-start | bytes 1118216 | tf_op jit(solution)/shard_map/ppermute | solution.py:26
  18.3 18.7 %collective-permute-start.4 = (bf16[104,2496]{1,0:T(8,128)(2,1)}, bf16[104,2496]{1,0:T(8,128)(2,1)}, u32[]{:S(2)}, u32[]{:S(2)}) collective-permute-start(bf16[104,2496]{1,0:T(8,128)(2,1)} %collective-permute-done.1), channel_id=1, source_target_pairs={{0,8},{2,10},{4,12},{6,14},{8,24},{10,26},{12,28},{14,30},{16,0},{... | collective-permute-start | bytes 1557512 | tf_op jit(solution)/shard_map/ppermute | solution.py:193
  20.9 16.0 %collective-permute-start.5 = (bf16[104,2496]{1,0:T(8,128)(2,1)}, bf16[104,2496]{1,0:T(8,128)(2,1)}, u32[]{:S(2)}, u32[]{:S(2)}) collective-permute-start(bf16[104,2496]{1,0:T(8,128)(2,1)} %collective-permute-done.1), channel_id=1, source_target_pairs={{0,2},{2,0},{4,6},{6,4},{8,10},{10,8},{12,14},{14,12},{16,18},{18,... | collective-permute-start | bytes 1557512 | tf_op jit(solution)/shard_map/ppermute | solution.py:196
  21.4 18.4 %collective-permute-start.6 = (bf16[104,2496]{1,0:T(8,128)(2,1)}, bf16[104,2496]{1,0:T(8,128)(2,1)}, u32[]{:S(2)}, u32[]{:S(2)}) collective-permute-start(bf16[104,2496]{1,0:T(8,128)(2,1)} %collective-permute-done.1), channel_id=1, source_target_pairs={{0,4},{2,6},{4,0},{6,2},{8,12},{10,14},{12,8},{14,10},{16,20},{18,... | collective-permute-start | bytes 1557512 | tf_op jit(solution)/shard_map/ppermute | solution.py:196
  23.2 22.9 %copy-start.9 = (s32[2]{0:T(128)S(1)}, s32[2]{0:T(128)}, u32[]{:S(2)}) copy-start(s32[2]{0:T(128)} %param.18) | copy-start | bytes 28
  23.2 23.7 %copy-start.8 = (bf16[1664]{0:T(1024)(128)(2,1)S(1)}, bf16[1664]{0:T(1024)(128)(2,1)}, u32[]{:S(2)}) copy-start(bf16[1664]{0:T(1024)(128)(2,1)} %param.15) | copy-start | bytes 9988
  23.4 24.3 %copy-start.1 = (bf16[512,832]{0,1:T(8,128)(2,1)S(1)}, bf16[512,832]{0,1:T(8,128)(2,1)}, u32[]{:S(2)}) copy-start(bf16[512,832]{0,1:T(8,128)(2,1)} %param.14) | copy-start | bytes 2555908
  24.4 40.6 %all-to-all-start = ((bf16[16,16,896]{2,1,0:T(8,128)(2,1)}), bf16[16,16,896]{2,1,0:T(8,128)(2,1)S(1)}, u32[]{:S(2)}, u32[]{:S(2)}) async-start(bf16[16,16,896]{2,1,0:T(8,128)(2,1)} %bitcast.5), calls=%async_computation | async-start | bytes 917504 | tf_op jit(solution)/shard_map/all_to_all | solution.py:240
  28.7 19.1 %collective-permute-start.11 = (bf16[104,1280]{1,0:T(8,128)(2,1)}, bf16[104,1280]{1,0:T(8,128)(2,1)}, u32[]{:S(2)}, u32[]{:S(2)}) collective-permute-start(bf16[104,1280]{1,0:T(8,128)(2,1)} %slice.33), channel_id=1, source_target_pairs={{0,2},{2,0},{4,6},{6,4},{8,10},{10,8},{12,14},{14,12},{16,18},{18,... | collective-permute-start | bytes 798728 | tf_op jit(solution)/shard_map/ppermute | solution.py:199
  31.3 16.4 %collective-permute-start.12 = (bf16[104,1216]{1,0:T(8,128)(2,1)}, bf16[104,1216]{1,0:T(8,128)(2,1)}, u32[]{:S(2)}, u32[]{:S(2)}) collective-permute-start(bf16[104,1216]{1,0:T(8,128)(2,1)} %slice.34), channel_id=1, source_target_pairs={{0,4},{2,6},{4,0},{6,2},{8,12},{10,14},{12,8},{14,10},{16,20},{18,... | collective-permute-start | bytes 758792 | tf_op jit(solution)/shard_map/ppermute | solution.py:200
  39.8 15.5 %collective-permute-start.7 = (bf16[104,2496]{1,0:T(8,128)(2,1)}, bf16[104,2496]{1,0:T(8,128)(2,1)}, u32[]{:S(2)}, u32[]{:S(2)}) collective-permute-start(bf16[104,2496]{1,0:T(8,128)(2,1)} %collective-permute-done.4), channel_id=1, source_target_pairs={{0,8},{2,10},{4,12},{6,14},{8,24},{10,26},{12,28},{14,30},{16,0},{... | collective-permute-start | bytes 1557512 | tf_op jit(solution)/shard_map/ppermute | solution.py:193
  39.8 17.5 %collective-permute-start.8 = (bf16[104,2496]{1,0:T(8,128)(2,1)}, bf16[104,2496]{1,0:T(8,128)(2,1)S(1)}, u32[]{:S(2)}, u32[]{:S(2)}) collective-permute-start(bf16[104,2496]{1,0:T(8,128)(2,1)} %collective-permute-done.4), channel_id=1, source_target_pairs={{0,2},{2,0},{4,6},{6,4},{8,10},{10,8},{12,14},{14,12},{16,18},{18,... | collective-permute-start | bytes 1557512 | tf_op jit(solution)/shard_map/ppermute | solution.py:196
  41.3 16.8 %collective-permute-start.9 = (bf16[104,2496]{1,0:T(8,128)(2,1)}, bf16[104,2496]{1,0:T(8,128)(2,1)}, u32[]{:S(2)}, u32[]{:S(2)}) collective-permute-start(bf16[104,2496]{1,0:T(8,128)(2,1)} %collective-permute-done.4), channel_id=1, source_target_pairs={{0,4},{2,6},{4,0},{6,2},{8,12},{10,14},{12,8},{14,10},{16,20},{18,... | collective-permute-start | bytes 1557512 | tf_op jit(solution)/shard_map/ppermute | solution.py:196
  47.7 23.5 %collective-permute-start.16 = (bf16[832,512]{1,0:T(8,128)(2,1)S(1)}, bf16[832,512]{1,0:T(8,128)(2,1)S(1)}, u32[]{:S(2)}, u32[]{:S(2)}) collective-permute-start(bf16[832,512]{1,0:T(8,128)(2,1)S(1)} %bitcast.27), channel_id=1, source_target_pairs={{0,1},{1,0},{2,3},{3,2},{4,5},{5,4},{6,7},{7,6},{8,9},{9,8},{10,11... | collective-permute-start | bytes 2555912 | tf_op jit(solution)/shard_map/ppermute | solution.py:26
  57.3 0.8 copy-start.5
  58.2 19.8 %collective-permute-start.18 = (bf16[104,2496]{1,0:T(8,128)(2,1)}, bf16[104,2496]{1,0:T(8,128)(2,1)S(1)}, u32[]{:S(2)}, u32[]{:S(2)}) collective-permute-start(bf16[104,2496]{1,0:T(8,128)(2,1)} %collective-permute-done.7), channel_id=1, source_target_pairs={{0,2},{2,0},{4,6},{6,4},{8,10},{10,8},{12,14},{14,12},{16,18},{18,... | collective-permute-start | bytes 1557512 | tf_op jit(solution)/shard_map/ppermute | solution.py:196
  59.2 18.8 %collective-permute-start.19 = (bf16[104,2496]{1,0:T(8,128)(2,1)}, bf16[104,2496]{1,0:T(8,128)(2,1)}, u32[]{:S(2)}, u32[]{:S(2)}) collective-permute-start(bf16[104,2496]{1,0:T(8,128)(2,1)} %collective-permute-done.7), channel_id=1, source_target_pairs={{0,4},{2,6},{4,0},{6,2},{8,12},{10,14},{12,8},{14,10},{16,20},{18,... | collective-permute-start | bytes 1557512 | tf_op jit(solution)/shard_map/ppermute | solution.py:196
  65.1 6.7 %collective-permute-start.17 = (bf16[256,896]{1,0:T(8,128)(2,1)S(1)}, bf16[256,896]{1,0:T(8,128)(2,1)S(1)}, u32[]{:S(2)}, u32[]{:S(2)}) collective-permute-start(bf16[256,896]{1,0:T(8,128)(2,1)S(1)} %bitcast.25), channel_id=1, source_target_pairs={{0,1},{1,0},{2,3},{3,2},{4,5},{5,4},{6,7},{7,6},{8,9},{9,8},{10,11... | collective-permute-start | bytes 1376264 | tf_op jit(solution)/shard_map/ppermute | solution.py:26
  68.7 17.4 %collective-permute-start.13 = (bf16[104,2496]{1,0:T(8,128)(2,1)}, bf16[104,2496]{1,0:T(8,128)(2,1)S(1)}, u32[]{:S(2)}, u32[]{:S(2)}) collective-permute-start(bf16[104,2496]{1,0:T(8,128)(2,1)} %constant_dynamic-update-slice_fusion), channel_id=1, source_target_pairs={{0,8},{2,10},{4,12},{6,14},{8,24},{10,26},{12,28},{14,30},{16,0},{... | collective-permute-start | bytes 1557512 | tf_op jit(solution)/shard_map/ppermute | solution.py:193
  71.2 14.9 %collective-permute-start.15 = (bf16[104,1216]{1,0:T(8,128)(2,1)S(1)}, bf16[104,1216]{1,0:T(8,128)(2,1)S(1)}, u32[]{:S(2)}, u32[]{:S(2)}) collective-permute-start(bf16[104,1216]{1,0:T(8,128)(2,1)S(1)} %slice.36), channel_id=1, source_target_pairs={{0,4},{2,6},{4,0},{6,2},{8,12},{10,14},{12,8},{14,10},{16,20},{18,... | collective-permute-start | bytes 758792 | tf_op jit(solution)/shard_map/ppermute | solution.py:200
  71.8 14.4 %collective-permute-start.14 = (bf16[104,1280]{1,0:T(8,128)(2,1)S(1)}, bf16[104,1280]{1,0:T(8,128)(2,1)S(1)}, u32[]{:S(2)}, u32[]{:S(2)}) collective-permute-start(bf16[104,1280]{1,0:T(8,128)(2,1)S(1)} %slice.35), channel_id=1, source_target_pairs={{0,2},{2,0},{4,6},{6,4},{8,10},{10,8},{12,14},{14,12},{16,18},{18,... | collective-permute-start | bytes 798728 | tf_op jit(solution)/shard_map/ppermute | solution.py:199
  74.8 1.6 %copy-start.3 = (bf16[312,2496]{1,0:T(8,128)(2,1)S(1)}, bf16[312,2496]{1,0:T(8,128)(2,1)}, u32[]{:S(2)}) copy-start(bf16[312,2496]{1,0:T(8,128)(2,1)} %pad_maximum_fusion.1) | copy-start | bytes 4672516
  76.4 5.3 %copy-start.4 = (bf16[312,2496]{1,0:T(8,128)(2,1)S(1)}, bf16[312,2496]{1,0:T(8,128)(2,1)}, u32[]{:S(2)}) copy-start(bf16[312,2496]{1,0:T(8,128)(2,1)} %pad_maximum_fusion.2) | copy-start | bytes 4672516
  78.0 8.1 %collective-permute-start.21 = (bf16[104,1216]{1,0:T(8,128)(2,1)S(1)}, bf16[104,1216]{1,0:T(8,128)(2,1)S(1)}, u32[]{:S(2)}, u32[]{:S(2)}) collective-permute-start(bf16[104,1216]{1,0:T(8,128)(2,1)S(1)} %slice.40), channel_id=1, source_target_pairs={{0,4},{2,6},{4,0},{6,2},{8,12},{10,14},{12,8},{14,10},{16,20},{18,... | collective-permute-start | bytes 758792 | tf_op jit(solution)/shard_map/ppermute | solution.py:200
  80.6 7.8 %collective-permute-start.20 = (bf16[104,1280]{1,0:T(8,128)(2,1)S(1)}, bf16[104,1280]{1,0:T(8,128)(2,1)S(1)}, u32[]{:S(2)}, u32[]{:S(2)}) collective-permute-start(bf16[104,1280]{1,0:T(8,128)(2,1)S(1)} %slice.39), channel_id=1, source_target_pairs={{0,2},{2,0},{4,6},{6,4},{8,10},{10,8},{12,14},{14,12},{16,18},{18,... | collective-permute-start | bytes 798728 | tf_op jit(solution)/shard_map/ppermute | solution.py:199

commit v20 on v19

--- a/solution.py
+++ b/solution.py
@@ -249,9 +249,13 @@
     images = [arrived] + [tp_shift(arrived, n_tp, d) for d in range(1, n_tp)]
     blocks = combine(tp_index, order, texts, images, gain_column)
 
-    held[3], sides[2], halves = tie(held[3], sides[2], halves)
+    corners = [jnp.concatenate(halves, axis=1)]
+    first = jnp.concatenate([held[0], *sides[0], corners[0]], axis=0)
+    second = jnp.concatenate([held[1], *sides[1]], axis=0)
+    held[3], sides[2], corners[0], first, second = tie(
+        held[3], sides[2], corners[0], first, second
+    )
     sides.append(to_sides(held[3]))
-    corners = [jnp.concatenate(halves, axis=1)]
     corners.append(along_line(corners[0]))
     for step in range(4, lines):
         held.append(along_line(held[step - 1]))
@@ -273,8 +277,8 @@
         )
         return part if total is None else total + part
 
-    total = add_product(None, 0, [held[0], *sides[0], corners[0]])
-    total = add_product(total, 4, [held[1], *sides[1]])
+    total = add_product(None, 0, [first])
+    total = add_product(total, 4, [second])
 
     total, sides[-1] = tie(total, sides[-1])
     corners.append(jnp.concatenate(to_corner(*sides[-1]), axis=1))

time: 92.2 us -> 88.7 us (0.962)
  other arithmetic: 9.61 us -> 8.1 us
  local copies, waits for them, and re-layouts: 17.3 us -> 16.2 us
    concatenate x5 -> x3, other arithmetic: 8.44 us -> 2.61 us  [add_product(): weight = jnp.concatenate(weights, axis=0)]
    concatenate x0 -> x2, other arithmetic: none -> 4.32 us  [the longest x1 2.63 us: shards(): second = jnp.concatenate([held[1], *sides[1]], axis=0)]
    ppermute x3, waiting for transfers between devices: 0.01 us -> 3.15 us  [to_corner(): right = lax.ppermute(by_x[:, cut:], 'req', y_perm)]
    ppermute x4, waiting for transfers between devices: 11.6 us -> 8.52 us  [along_line(): return lax.ppermute(block, 'req', line_perm)]
    unnamed x21 -> x13, local copies, waits for them, and re-layouts: 7.84 us -> 6.05 us
    ppermute x4, starting transfers between devices: 6.47 us -> 8.23 us  [along_line(): return lax.ppermute(block, 'req', line_perm)]
    ppermute x4, waiting for transfers between devices: 3.47 us -> 2.2 us  [to_sides(): lax.ppermute(block, 'req', y_perm)]
  transfers between devices with their start and end apart: 23 -> 23, of which waited for: 6 -> 10; matrix products, arithmetic and copies ran while one was open for 30% -> 29% of each run, Pallas kernels for 6% -> 6%
where the time goes in v20:
time: 88.7 us; the launch traced here: 88.1 us
  starting transfers between devices  28.5 us (32%)
  waiting for transfers between devices  19.1 us (22%)
  local copies, waits for them, and re-layouts  16.2 us (18%)
  matrix products  10.4 us (12%)
  other arithmetic  8.1 us (9%)
  Pallas kernels  5.5 us (6%)
    dot_general x5, matrix products, add_product(): lax.dot_general(source, weight, (((0,), (0,)), ((), ())), preferred_eleme...  9.32 us
    ppermute x4, waiting for transfers between devices, along_line(): return lax.ppermute(block, 'req', line_perm)  8.52 us
    ppermute x4, starting transfers between devices, along_line(): return lax.ppermute(block, 'req', line_perm)  8.23 us
    ppermute x4, starting transfers between devices, to_sides(): lax.ppermute(block, 'req', y_perm)  6.19 us
    unnamed x13, local copies, waits for them, and re-layouts  6.05 us
    ppermute x4, starting transfers between devices, to_sides(): lax.ppermute(block, 'req', x_perm)  3.75 us
    ppermute x3, starting transfers between devices, to_corner(): right = lax.ppermute(by_x[:, cut:], 'req', y_perm)  3.68 us
    all_to_all x1, starting transfers between devices, shards(): lax.all_to_all(outgoing.reshape(n_req, IMG_CAP, -1), 'req', split_axis=0,...  3.56 us
  transfers between devices with their start and end apart: 23, of which 10 were waited for; matrix products, arithmetic and copies ran while one was open for 29% of the time, Pallas kernels for 6%

profile of v20, /device:TPU:0, one launch (start us, length us, event | category | flops | bytes accessed | tf_op | source)
XLA Modules:
  0.0 88.1 jit_solution(16291078053921984527)
XLA Ops:
  0.0 3.0 %collective-permute-start.1 = (bf16[104,2496]{1,0:T(8,128)(2,1)}, bf16[104,2496]{1,0:T(8,128)(2,1)}, u32[]{:S(2)}, u32[]{:S(2)}) collective-permute-start(bf16[104,2496]{1,0:T(8,128)(2,1)} %param.16), channel_id=1, source_target_pairs={{0,8},{2,10},{4,12},{6,14},{8,24},{10,26},{12,28},{14,30},{16,0},{... | collective-permute-start | bytes 1557512 | tf_op jit(solution)/shard_map/ppermute | solution.py:193
  3.0 1.5 %collective-permute-start.2 = (bf16[104,2496]{1,0:T(8,128)(2,1)}, bf16[104,2496]{1,0:T(8,128)(2,1)}, u32[]{:S(2)}, u32[]{:S(2)}) collective-permute-start(bf16[104,2496]{1,0:T(8,128)(2,1)} %param.16), channel_id=1, source_target_pairs={{0,2},{2,0},{4,6},{6,4},{8,10},{10,8},{12,14},{14,12},{16,18},{18,... | collective-permute-start | bytes 1557512 | tf_op jit(solution)/shard_map/ppermute | solution.py:196
  4.5 1.5 %collective-permute-start.3 = (bf16[104,2496]{1,0:T(8,128)(2,1)}, bf16[104,2496]{1,0:T(8,128)(2,1)}, u32[]{:S(2)}, u32[]{:S(2)}) collective-permute-start(bf16[104,2496]{1,0:T(8,128)(2,1)} %param.16), channel_id=1, source_target_pairs={{0,4},{2,6},{4,0},{6,2},{8,12},{10,14},{12,8},{14,10},{16,20},{18,... | collective-permute-start | bytes 1557512 | tf_op jit(solution)/shard_map/ppermute | solution.py:196
  6.0 1.1 %copy-done.2 = bf16[448,832]{1,0:T(8,128)(2,1)S(1)} copy-done((bf16[448,832]{1,0:T(8,128)(2,1)S(1)}, bf16[448,832]{1,0:T(8,128)(2,1)}, u32[]{:S(2)}) %copy-start.2) | copy-done | bytes 745496
  7.2 0.8 shard_map.118
  7.9 0.1 collective-permute-start
  8.0 0.7 convert_bitcast_fusion.1
  8.7 0.7 stack.22
  9.4 0.7 stack.21
  10.1 0.2 convert_reduce_fusion
  10.3 0.0 copy-start
  10.3 4.1 %copy-done = bf16[4,832,1664]{2,1,0:T(8,128)(2,1)S(1)} copy-done((bf16[4,832,1664]{2,1,0:T(8,128)(2,1)S(1)}, bf16[4,832,1664]{2,1,0:T(8,128)(2,1)}, u32[]{:S(2)}) %copy-start) | copy-done | bytes 11075608
  14.5 2.9 %shard_map.119 = f32[112,1664]{1,0:T(8,128)S(1)} custom-call(bf16[4,112,832]{2,1,0:T(8,128)(2,1)S(1)} %get-tuple-element.48.picked_ref, bf16[2,832]{1,0:T(2,128)(2,1)S(1)} %pad_maximum_fusion.4.gain_bias_ref, f32[4,112,256]{2,1,0:T(8,128)S(1)} %get-tuple-element.49.refs_0_, f32[4,112,256]{2,1,0:T(8,128)S(1)} %collective-permute-done.refs_1_, ...), custom_call_target="tpu_custom_call" | custom-call | flops 1000 | bytes 1000 | tf_op jit(solution)/shard_map/pallas_call | solution.py:117
  17.4 0.7 collective-permute-done.3
  18.1 0.9 %constant_dynamic-slice_fusion = f32[112,832]{1,0:T(8,128)} fusion(f32[112,1664]{1,0:T(8,128)S(1)} %shard_map.119, s32[]{:T(128)S(6)} %select_n.27), kind=kLoop, calls=%fused_computation.38 | loop fusion | bytes 745476 | tf_op jit(solution)/shard_map/dynamic_slice | solution.py:34
  19.0 2.6 %collective-permute-start.4 = (bf16[104,2496]{1,0:T(8,128)(2,1)}, bf16[104,2496]{1,0:T(8,128)(2,1)}, u32[]{:S(2)}, u32[]{:S(2)}) collective-permute-start(bf16[104,2496]{1,0:T(8,128)(2,1)} %collective-permute-done.1), channel_id=1, source_target_pairs={{0,8},{2,10},{4,12},{6,14},{8,24},{10,26},{12,28},{14,30},{16,0},{... | collective-permute-start | bytes 1557512 | tf_op jit(solution)/shard_map/ppermute | solution.py:193
  21.6 0.5 collective-permute-start.5
  22.2 1.5 %collective-permute-start.6 = (bf16[104,2496]{1,0:T(8,128)(2,1)}, bf16[104,2496]{1,0:T(8,128)(2,1)}, u32[]{:S(2)}, u32[]{:S(2)}) collective-permute-start(bf16[104,2496]{1,0:T(8,128)(2,1)} %collective-permute-done.1), channel_id=1, source_target_pairs={{0,4},{2,6},{4,0},{6,2},{8,12},{10,14},{12,8},{14,10},{16,20},{18,... | collective-permute-start | bytes 1557512 | tf_op jit(solution)/shard_map/ppermute | solution.py:196
  23.7 0.1 pad.13.clone
  23.8 0.1 copy.18
  23.9 0.2 add_convert_fusion
  24.1 1.7 %slice.33 = bf16[104,1280]{1,0:T(8,128)(2,1)} slice(bf16[104,2496]{1,0:T(8,128)(2,1)} %collective-permute-done.3), slice={[0:104], [0:1280]} | slice | bytes 532480 | tf_op jit(solution)/shard_map/slice | solution.py:199
  25.8 1.5 %collective-permute-start.11 = (bf16[104,1280]{1,0:T(8,128)(2,1)}, bf16[104,1280]{1,0:T(8,128)(2,1)S(1)}, u32[]{:S(2)}, u32[]{:S(2)}) collective-permute-start(bf16[104,1280]{1,0:T(8,128)(2,1)} %slice.33), channel_id=1, source_target_pairs={{0,2},{2,0},{4,6},{6,4},{8,10},{10,8},{12,14},{14,12},{16,18},{18,... | collective-permute-start | bytes 798728 | tf_op jit(solution)/shard_map/ppermute | solution.py:199
  27.3 1.7 %slice.34 = bf16[104,1216]{1,0:T(8,128)(2,1)} slice(bf16[104,2496]{1,0:T(8,128)(2,1)} %collective-permute-done.2), slice={[0:104], [1280:2496]} | slice | bytes 505856 | tf_op jit(solution)/shard_map/slice | solution.py:200
  29.0 1.1 %convolution_convert_fusion = bf16[256,896]{1,0:T(8,128)(2,1)} fusion(bf16[112,2]{1,0:T(8,128)(2,1)S(1)} %copy.18, bf16[112,832]{1,0:T(8,128)(2,1)S(1)} %add_convert_fusion, bf16[896]{0:T(1024)(128)(2,1)S(1)} %pad.13.clone, s32[112]{0:T(128)S(1)} %multiply_add_fusion), kind=kOutput, calls=%fused_computation.9 | convolution fusion | flops 52240384 | bytes 647808 | tf_op jit(solution)/shard_map/dot_general | solution.py:239
  30.0 3.6 %all-to-all-start = ((bf16[16,16,896]{2,1,0:T(8,128)(2,1)}), bf16[16,16,896]{2,1,0:T(8,128)(2,1)S(1)}, u32[]{:S(2)}, u32[]{:S(2)}) async-start(bf16[16,16,896]{2,1,0:T(8,128)(2,1)} %bitcast.5), calls=%async_computation | async-start | bytes 917504 | tf_op jit(solution)/shard_map/all_to_all | solution.py:240
  33.6 1.2 %collective-permute-done.4 = bf16[104,2496]{1,0:T(8,128)(2,1)} collective-permute-done((bf16[104,2496]{1,0:T(8,128)(2,1)}, bf16[104,2496]{1,0:T(8,128)(2,1)}, u32[]{:S(2)}, u32[]{:S(2)}) %collective-permute-start.4) | collective-permute-done | bytes 519200 | tf_op jit(solution)/shard_map/ppermute | solution.py:193
  34.8 1.5 %collective-permute-start.12 = (bf16[104,1216]{1,0:T(8,128)(2,1)}, bf16[104,1216]{1,0:T(8,128)(2,1)}, u32[]{:S(2)}, u32[]{:S(2)}) collective-permute-start(bf16[104,1216]{1,0:T(8,128)(2,1)} %slice.34), channel_id=1, source_target_pairs={{0,4},{2,6},{4,0},{6,2},{8,12},{10,14},{12,8},{14,10},{16,20},{18,... | collective-permute-start | bytes 758792 | tf_op jit(solution)/shard_map/ppermute | solution.py:200
  36.3 0.6 collective-permute-done.5
  36.9 1.1 %collective-permute-start.7 = (bf16[104,2496]{1,0:T(8,128)(2,1)}, bf16[104,2496]{1,0:T(8,128)(2,1)}, u32[]{:S(2)}, u32[]{:S(2)}) collective-permute-start(bf16[104,2496]{1,0:T(8,128)(2,1)} %collective-permute-done.4), channel_id=1, source_target_pairs={{0,8},{2,10},{4,12},{6,14},{8,24},{10,26},{12,28},{14,30},{16,0},{... | collective-permute-start | bytes 1557512 | tf_op jit(solution)/shard_map/ppermute | solution.py:193
  38.0 0.5 collective-permute-start.8
  38.5 2.6 %pad_maximum_fusion.1 = bf16[312,2496]{1,0:T(8,128)(2,1)} fusion(bf16[104,2496]{1,0:T(8,128)(2,1)} %collective-permute-done.6, bf16[104,2496]{1,0:T(8,128)(2,1)} %collective-permute-done.5, bf16[104,2496]{1,0:T(8,128)(2,1)} %collective-permute-done.1), kind=kLoop, calls=%fused_computation.5 | loop fusion | flops 4672512 | bytes 3115008 | tf_op jit(solution)/shard_map/concatenate | solution.py:254
  41.2 0.1 fusion.7
  41.3 0.7 fusion.10.order_ref
  42.0 0.8 reshape.62.gain_ref
  42.8 2.6 %collective-permute-done.11 = bf16[104,1280]{1,0:T(8,128)(2,1)S(1)} collective-permute-done((bf16[104,1280]{1,0:T(8,128)(2,1)}, bf16[104,1280]{1,0:T(8,128)(2,1)S(1)}, u32[]{:S(2)}, u32[]{:S(2)}) %collective-permute-start.11) | collective-permute-done | bytes 266272 | tf_op jit(solution)/shard_map/ppermute | solution.py:199
  45.3 1.7 %collective-permute-start.9 = (bf16[104,2496]{1,0:T(8,128)(2,1)}, bf16[104,2496]{1,0:T(8,128)(2,1)}, u32[]{:S(2)}, u32[]{:S(2)}) collective-permute-start(bf16[104,2496]{1,0:T(8,128)(2,1)} %collective-permute-done.4), channel_id=1, source_target_pairs={{0,4},{2,6},{4,0},{6,2},{8,12},{10,14},{12,8},{14,10},{16,20},{18,... | collective-permute-start | bytes 1557512 | tf_op jit(solution)/shard_map/ppermute | solution.py:196
  47.0 0.7 constant_dynamic-update-slice_fusion.1
  47.7 0.2 collective-permute-done.12
  48.0 1.7 %constant_dynamic-update-slice_fusion = bf16[104,2496]{1,0:T(8,128)(2,1)} fusion(bf16[104,2496]{1,0:T(8,128)(2,1)} %constant_dynamic-update-slice_fusion.1, bf16[104,1216]{1,0:T(8,128)(2,1)} %collective-permute-done.12), kind=kLoop, calls=%fused_computation.22 | loop fusion | bytes 532480 | tf_op jit(solution)/shard_map/concatenate | solution.py:252
  49.7 1.7 %pad_maximum_fusion = bf16[416,2496]{1,0:T(8,128)(2,1)S(1)} fusion(bf16[104,2496]{1,0:T(8,128)(2,1)} %constant_dynamic-update-slice_fusion, bf16[104,2496]{1,0:T(8,128)(2,1)} %collective-permute-done.3, bf16[104,2496]{1,0:T(8,128)(2,1)} %collective-permute-done.2, bf16[104,2496]{1,0:T(8,128)(2,1)} %param.16), kind=kLoop, calls=%fused_computation.4 | loop fusion | flops 8306688 | bytes 4153344 | tf_op jit(solution)/shard_map/concatenate | solution.py:253
  51.3 7.4 %collective-permute-done.7 = bf16[104,2496]{1,0:T(8,128)(2,1)} collective-permute-done((bf16[104,2496]{1,0:T(8,128)(2,1)}, bf16[104,2496]{1,0:T(8,128)(2,1)}, u32[]{:S(2)}, u32[]{:S(2)}) %collective-permute-start.7) | collective-permute-done | bytes 519200 | tf_op jit(solution)/shard_map/ppermute | solution.py:193
  58.7 0.3 collective-permute-done.9
  59.0 1.2 %collective-permute-start.18 = (bf16[104,2496]{1,0:T(8,128)(2,1)}, bf16[104,2496]{1,0:T(8,128)(2,1)S(1)}, u32[]{:S(2)}, u32[]{:S(2)}) collective-permute-start(bf16[104,2496]{1,0:T(8,128)(2,1)} %collective-permute-done.7), channel_id=1, source_target_pairs={{0,2},{2,0},{4,6},{6,4},{8,10},{10,8},{12,14},{14,12},{16,18},{18,... | collective-permute-start | bytes 1557512 | tf_op jit(solution)/shard_map/ppermute | solution.py:196
  60.2 1.5 %collective-permute-start.19 = (bf16[104,2496]{1,0:T(8,128)(2,1)}, bf16[104,2496]{1,0:T(8,128)(2,1)S(1)}, u32[]{:S(2)}, u32[]{:S(2)}) collective-permute-start(bf16[104,2496]{1,0:T(8,128)(2,1)} %collective-permute-done.7), channel_id=1, source_target_pairs={{0,4},{2,6},{4,0},{6,2},{8,12},{10,14},{12,8},{14,10},{16,20},{18,... | collective-permute-start | bytes 1557512 | tf_op jit(solution)/shard_map/ppermute | solution.py:196
  61.7 0.6 collective-permute-start.15
  62.3 1.0 %slice.35 = bf16[104,1280]{1,0:T(8,128)(2,1)S(1)} slice(bf16[104,2496]{1,0:T(8,128)(2,1)} %collective-permute-done.9), slice={[0:104], [0:1280]} | slice | bytes 532480 | tf_op jit(solution)/shard_map/slice | solution.py:199
  63.3 1.3 %pad_maximum_fusion.2 = bf16[312,2496]{1,0:T(8,128)(2,1)S(1)} fusion(bf16[104,2496]{1,0:T(8,128)(2,1)} %collective-permute-done.9, bf16[104,2496]{1,0:T(8,128)(2,1)S(1)} %collective-permute-done.8, bf16[104,2496]{1,0:T(8,128)(2,1)} %collective-permute-done.4), kind=kLoop, calls=%fused_computation.7 | loop fusion | flops 4672512 | bytes 3115008 | tf_op jit(solution)/shard_map/concatenate | solution.py:268
  64.6 0.9 %collective-permute-start.14 = (bf16[104,1280]{1,0:T(8,128)(2,1)S(1)}, bf16[104,1280]{1,0:T(8,128)(2,1)S(1)}, u32[]{:S(2)}, u32[]{:S(2)}) collective-permute-start(bf16[104,1280]{1,0:T(8,128)(2,1)S(1)} %slice.35), channel_id=1, source_target_pairs={{0,2},{2,0},{4,6},{6,4},{8,10},{10,8},{12,14},{14,12},{16,18},{18,... | collective-permute-start | bytes 798728 | tf_op jit(solution)/shard_map/ppermute | solution.py:199
  65.5 1.5 %collective-permute-start.13 = (bf16[104,2496]{1,0:T(8,128)(2,1)}, bf16[104,2496]{1,0:T(8,128)(2,1)S(1)}, u32[]{:S(2)}, u32[]{:S(2)}) collective-permute-start(bf16[104,2496]{1,0:T(8,128)(2,1)} %constant_dynamic-update-slice_fusion), channel_id=1, source_target_pairs={{0,8},{2,10},{4,12},{6,14},{8,24},{10,26},{12,28},{14,30},{16,0},{... | collective-permute-start | bytes 1557512 | tf_op jit(solution)/shard_map/ppermute | solution.py:193
  67.0 1.8 %shard_map.120 = bf16[16,104,512]{2,1,0:T(8,128)(2,1)S(1)} custom-call(s32[1]{0:T(128)} %bitcast.2.index_ref, s32[16]{0:T(128)S(1)} %fusion.10.order_ref, bf16[16,104,1]{2,1,0:T(8,128)(2,1)S(1)} %reshape.62.gain_ref, bf16[832,512]{1,0:T(8,128)(2,1)S(1)} %bitcast.28, bf16[832,512]{1,0:T(8,128)(2,1)S(1)} %collective-permute-done.16.refs_1_, ...), custom_call_target="tpu_custom_call" | custom-call | flops 1000 | bytes 1000 | tf_op jit(solution)/shard_map/pallas_call | solution.py:168
  68.9 0.1 fusion.14
  69.0 1.5 %fusion.15 = f32[512,2496]{0,1:T(8,128)S(1)} fusion(bf16[416,512]{1,0:T(8,128)(2,1)S(1)} %bitcast.30, bf16[416,2496]{1,0:T(8,128)(2,1)S(1)} %pad_maximum_fusion), kind=kOutput, calls=%fused_computation.48 | convolution fusion | flops 1063256064 | bytes 7614464 | tf_op jit(solution)/shard_map/dot_general | solution.py:275
  70.6 1.6 %convolution_add_fusion.2 = f32[512,2496]{0,1:T(8,128)S(1)} fusion(f32[512,2496]{0,1:T(8,128)S(1)} %fusion.15, bf16[312,512]{1,0:T(8,128)(2,1)S(1)} %bitcast.33, bf16[312,2496]{1,0:T(8,128)(2,1)S(1)} %copy-done.3), kind=kOutput, calls=%fused_computation.3 | convolution fusion | flops 798720000 | bytes 12100608 | tf_op jit(solution)/shard_map/dot_general | solution.py:275
  72.1 2.1 %collective-permute-done.18 = bf16[104,2496]{1,0:T(8,128)(2,1)S(1)} collective-permute-done((bf16[104,2496]{1,0:T(8,128)(2,1)}, bf16[104,2496]{1,0:T(8,128)(2,1)S(1)}, u32[]{:S(2)}, u32[]{:S(2)}) %collective-permute-start.18) | collective-permute-done | bytes 519200 | tf_op jit(solution)/shard_map/ppermute | solution.py:196
  74.2 1.2 %collective-permute-done.19 = bf16[104,2496]{1,0:T(8,128)(2,1)S(1)} collective-permute-done((bf16[104,2496]{1,0:T(8,128)(2,1)}, bf16[104,2496]{1,0:T(8,128)(2,1)S(1)}, u32[]{:S(2)}, u32[]{:S(2)}) %collective-permute-start.19) | collective-permute-done | bytes 519200 | tf_op jit(solution)/shard_map/ppermute | solution.py:196
  75.5 1.5 %collective-permute-start.21 = (bf16[104,1216]{1,0:T(8,128)(2,1)S(1)}, bf16[104,1216]{1,0:T(8,128)(2,1)S(1)}, u32[]{:S(2)}, u32[]{:S(2)}) collective-permute-start(bf16[104,1216]{1,0:T(8,128)(2,1)S(1)} %slice.40), channel_id=1, source_target_pairs={{0,4},{2,6},{4,0},{6,2},{8,12},{10,14},{12,8},{14,10},{16,20},{18,... | collective-permute-start | bytes 758792 | tf_op jit(solution)/shard_map/ppermute | solution.py:200
  77.0 0.6 collective-permute-start.20
  77.6 1.5 %convolution_add_fusion.1 = f32[512,2496]{0,1:T(8,128)S(1)} fusion(f32[512,2496]{0,1:T(8,128)S(1)} %convolution_add_fusion.2, bf16[312,512]{1,0:T(8,128)(2,1)S(1)} %bitcast.32, bf16[312,2496]{1,0:T(8,128)(2,1)S(1)} %pad_maximum_fusion.2), kind=kOutput, calls=%fused_computation.2 | convolution fusion | flops 798720000 | bytes 12100608 | tf_op jit(solution)/shard_map/dot_general | solution.py:275
  79.2 1.2 %pad_maximum_fusion.3 = bf16[312,2496]{1,0:T(8,128)(2,1)S(1)} fusion(bf16[104,2496]{1,0:T(8,128)(2,1)S(1)} %collective-permute-done.19, bf16[104,2496]{1,0:T(8,128)(2,1)S(1)} %collective-permute-done.18, bf16[104,2496]{1,0:T(8,128)(2,1)} %collective-permute-done.7), kind=kLoop, calls=%fused_computation.8 | loop fusion | flops 4672512 | bytes 3115008 | tf_op jit(solution)/shard_map/concatenate | solution.py:268
  80.4 1.6 %convolution_add_fusion = f32[512,2496]{0,1:T(8,128)S(1)} fusion(f32[512,2496]{0,1:T(8,128)S(1)} %convolution_add_fusion.1, bf16[312,512]{1,0:T(8,128)(2,1)S(1)} %bitcast.31, bf16[312,2496]{1,0:T(8,128)(2,1)S(1)} %pad_maximum_fusion.3), kind=kOutput, calls=%fused_computation.1 | convolution fusion | flops 798720000 | bytes 12100608 | tf_op jit(solution)/shard_map/dot_general | solution.py:275
  82.0 2.9 %collective-permute-done.21 = bf16[104,1216]{1,0:T(8,128)(2,1)S(1)} collective-permute-done((bf16[104,1216]{1,0:T(8,128)(2,1)S(1)}, bf16[104,1216]{1,0:T(8,128)(2,1)S(1)}, u32[]{:S(2)}, u32[]{:S(2)}) %collective-permute-start.21) | collective-permute-done | bytes 252960 | tf_op jit(solution)/shard_map/ppermute | solution.py:200
  84.9 0.1 maximum_maximum_fusion
  85.1 3.1 %select_convert_fusion = bf16[512,2496]{0,1:T(8,128)(2,1)} fusion(f32[512,2496]{0,1:T(8,128)S(1)} %convolution_add_fusion, bf16[312,512]{1,0:T(8,128)(2,1)S(1)} %bitcast.29, bf16[312,2496]{1,0:T(8,128)(2,1)S(1)} %maximum_maximum_fusion, pred[512]{0:T(512)(128)(4,1)S(1)} %fusion.8), kind=kOutput, calls=%fused_computation | convolution fusion | flops 801275904 | bytes 9545216 | tf_op jit(solution)/shard_map/dot_general | solution.py:275
  (36 shorter events, 0.2 us)
Async XLA Ops:
  0.0 17.4 %collective-permute-start.1 = (bf16[104,2496]{1,0:T(8,128)(2,1)}, bf16[104,2496]{1,0:T(8,128)(2,1)}, u32[]{:S(2)}, u32[]{:S(2)}) collective-permute-start(bf16[104,2496]{1,0:T(8,128)(2,1)} %param.16), channel_id=1, source_target_pairs={{0,8},{2,10},{4,12},{6,14},{8,24},{10,26},{12,28},{14,30},{16,0},{... | collective-permute-start | bytes 1557512 | tf_op jit(solution)/shard_map/ppermute | solution.py:193
  3.0 14.4 %collective-permute-start.2 = (bf16[104,2496]{1,0:T(8,128)(2,1)}, bf16[104,2496]{1,0:T(8,128)(2,1)}, u32[]{:S(2)}, u32[]{:S(2)}) collective-permute-start(bf16[104,2496]{1,0:T(8,128)(2,1)} %param.16), channel_id=1, source_target_pairs={{0,2},{2,0},{4,6},{6,4},{8,10},{10,8},{12,14},{14,12},{16,18},{18,... | collective-permute-start | bytes 1557512 | tf_op jit(solution)/shard_map/ppermute | solution.py:196
  4.5 13.6 %collective-permute-start.3 = (bf16[104,2496]{1,0:T(8,128)(2,1)}, bf16[104,2496]{1,0:T(8,128)(2,1)}, u32[]{:S(2)}, u32[]{:S(2)}) collective-permute-start(bf16[104,2496]{1,0:T(8,128)(2,1)} %param.16), channel_id=1, source_target_pairs={{0,4},{2,6},{4,0},{6,2},{8,12},{10,14},{12,8},{14,10},{16,20},{18,... | collective-permute-start | bytes 1557512 | tf_op jit(solution)/shard_map/ppermute | solution.py:196
  6.0 1.1 %copy-start.2 = (bf16[448,832]{1,0:T(8,128)(2,1)S(1)}, bf16[448,832]{1,0:T(8,128)(2,1)}, u32[]{:S(2)}) copy-start(bf16[448,832]{1,0:T(8,128)(2,1)} %patches_ref.1) | copy-start | bytes 2236420
  7.9 2.4 %collective-permute-start = (f32[4,112,256]{2,1,0:T(8,128)S(1)}, f32[4,112,256]{2,1,0:T(8,128)S(1)}, u32[]{:S(2)}, u32[]{:S(2)}) collective-permute-start(f32[4,112,256]{2,1,0:T(8,128)S(1)} %get-tuple-element.49.refs_0_), channel_id=1, source_target_pairs={{0,1},{1,0},{2,3},{3,2},{4,5},{5,4},{6,7},{7,6},{8,9},{9,8},{10,11... | collective-permute-start | bytes 1376264 | tf_op jit(solution)/shard_map/ppermute | solution.py:26
  10.3 4.1 %copy-start = (bf16[4,832,1664]{2,1,0:T(8,128)(2,1)S(1)}, bf16[4,832,1664]{2,1,0:T(8,128)(2,1)}, u32[]{:S(2)}) copy-start(bf16[4,832,1664]{2,1,0:T(8,128)(2,1)} %refs_2_.1) | copy-start | bytes 33226756
  14.5 9.2 %copy-start.1 = (bf16[512,832]{0,1:T(8,128)(2,1)S(1)}, bf16[512,832]{0,1:T(8,128)(2,1)}, u32[]{:S(2)}) copy-start(bf16[512,832]{0,1:T(8,128)(2,1)} %param.14) | copy-start | bytes 2555908
  19.0 4.9 %collective-permute-start.10 = (f32[112,832]{1,0:T(8,128)}, f32[112,832]{1,0:T(8,128)S(1)}, u32[]{:S(2)}, u32[]{:S(2)}) collective-permute-start(f32[112,832]{1,0:T(8,128)} %constant_dynamic-slice_fusion), channel_id=1, source_target_pairs={{0,1},{1,0},{2,3},{3,2},{4,5},{5,4},{6,7},{7,6},{8,9},{9,8},{10,11... | collective-permute-start | bytes 1118216 | tf_op jit(solution)/shard_map/ppermute | solution.py:26
  19.0 15.7 %collective-permute-start.4 = (bf16[104,2496]{1,0:T(8,128)(2,1)}, bf16[104,2496]{1,0:T(8,128)(2,1)}, u32[]{:S(2)}, u32[]{:S(2)}) collective-permute-start(bf16[104,2496]{1,0:T(8,128)(2,1)} %collective-permute-done.1), channel_id=1, source_target_pairs={{0,8},{2,10},{4,12},{6,14},{8,24},{10,26},{12,28},{14,30},{16,0},{... | collective-permute-start | bytes 1557512 | tf_op jit(solution)/shard_map/ppermute | solution.py:193
  21.6 15.2 %collective-permute-start.5 = (bf16[104,2496]{1,0:T(8,128)(2,1)}, bf16[104,2496]{1,0:T(8,128)(2,1)}, u32[]{:S(2)}, u32[]{:S(2)}) collective-permute-start(bf16[104,2496]{1,0:T(8,128)(2,1)} %collective-permute-done.1), channel_id=1, source_target_pairs={{0,2},{2,0},{4,6},{6,4},{8,10},{10,8},{12,14},{14,12},{16,18},{18,... | collective-permute-start | bytes 1557512 | tf_op jit(solution)/shard_map/ppermute | solution.py:196
  22.2 14.7 %collective-permute-start.6 = (bf16[104,2496]{1,0:T(8,128)(2,1)}, bf16[104,2496]{1,0:T(8,128)(2,1)}, u32[]{:S(2)}, u32[]{:S(2)}) collective-permute-start(bf16[104,2496]{1,0:T(8,128)(2,1)} %collective-permute-done.1), channel_id=1, source_target_pairs={{0,4},{2,6},{4,0},{6,2},{8,12},{10,14},{12,8},{14,10},{16,20},{18,... | collective-permute-start | bytes 1557512 | tf_op jit(solution)/shard_map/ppermute | solution.py:196
  23.7 40.9 %collective-permute-start.16 = (bf16[832,512]{1,0:T(8,128)(2,1)S(1)}, bf16[832,512]{1,0:T(8,128)(2,1)S(1)}, u32[]{:S(2)}, u32[]{:S(2)}) collective-permute-start(bf16[832,512]{1,0:T(8,128)(2,1)S(1)} %bitcast.27), channel_id=1, source_target_pairs={{0,1},{1,0},{2,3},{3,2},{4,5},{5,4},{6,7},{7,6},{8,9},{9,8},{10,11... | collective-permute-start | bytes 2555912 | tf_op jit(solution)/shard_map/ppermute | solution.py:26
  23.9 17.3 %copy-start.5 = (s32[2]{0:T(128)S(1)}, s32[2]{0:T(128)}, u32[]{:S(2)}) copy-start(s32[2]{0:T(128)} %param.18) | copy-start | bytes 28
  24.1 17.9 %copy-start.4 = (bf16[1664]{0:T(1024)(128)(2,1)S(1)}, bf16[1664]{0:T(1024)(128)(2,1)}, u32[]{:S(2)}) copy-start(bf16[1664]{0:T(1024)(128)(2,1)} %param.15) | copy-start | bytes 9988
  25.8 19.5 %collective-permute-start.11 = (bf16[104,1280]{1,0:T(8,128)(2,1)}, bf16[104,1280]{1,0:T(8,128)(2,1)S(1)}, u32[]{:S(2)}, u32[]{:S(2)}) collective-permute-start(bf16[104,1280]{1,0:T(8,128)(2,1)} %slice.33), channel_id=1, source_target_pairs={{0,2},{2,0},{4,6},{6,4},{8,10},{10,8},{12,14},{14,12},{16,18},{18,... | collective-permute-start | bytes 798728 | tf_op jit(solution)/shard_map/ppermute | solution.py:199
  30.0 19.6 %all-to-all-start = ((bf16[16,16,896]{2,1,0:T(8,128)(2,1)}), bf16[16,16,896]{2,1,0:T(8,128)(2,1)S(1)}, u32[]{:S(2)}, u32[]{:S(2)}) async-start(bf16[16,16,896]{2,1,0:T(8,128)(2,1)} %bitcast.5), calls=%async_computation | async-start | bytes 917504 | tf_op jit(solution)/shard_map/all_to_all | solution.py:240
  34.8 13.2 %collective-permute-start.12 = (bf16[104,1216]{1,0:T(8,128)(2,1)}, bf16[104,1216]{1,0:T(8,128)(2,1)}, u32[]{:S(2)}, u32[]{:S(2)}) collective-permute-start(bf16[104,1216]{1,0:T(8,128)(2,1)} %slice.34), channel_id=1, source_target_pairs={{0,4},{2,6},{4,0},{6,2},{8,12},{10,14},{12,8},{14,10},{16,20},{18,... | collective-permute-start | bytes 758792 | tf_op jit(solution)/shard_map/ppermute | solution.py:200
  36.9 21.8 %collective-permute-start.7 = (bf16[104,2496]{1,0:T(8,128)(2,1)}, bf16[104,2496]{1,0:T(8,128)(2,1)}, u32[]{:S(2)}, u32[]{:S(2)}) collective-permute-start(bf16[104,2496]{1,0:T(8,128)(2,1)} %collective-permute-done.4), channel_id=1, source_target_pairs={{0,8},{2,10},{4,12},{6,14},{8,24},{10,26},{12,28},{14,30},{16,0},{... | collective-permute-start | bytes 1557512 | tf_op jit(solution)/shard_map/ppermute | solution.py:193
  38.0 20.7 %collective-permute-start.8 = (bf16[104,2496]{1,0:T(8,128)(2,1)}, bf16[104,2496]{1,0:T(8,128)(2,1)S(1)}, u32[]{:S(2)}, u32[]{:S(2)}) collective-permute-start(bf16[104,2496]{1,0:T(8,128)(2,1)} %collective-permute-done.4), channel_id=1, source_target_pairs={{0,2},{2,0},{4,6},{6,4},{8,10},{10,8},{12,14},{14,12},{16,18},{18,... | collective-permute-start | bytes 1557512 | tf_op jit(solution)/shard_map/ppermute | solution.py:196
  45.3 13.7 %collective-permute-start.9 = (bf16[104,2496]{1,0:T(8,128)(2,1)}, bf16[104,2496]{1,0:T(8,128)(2,1)}, u32[]{:S(2)}, u32[]{:S(2)}) collective-permute-start(bf16[104,2496]{1,0:T(8,128)(2,1)} %collective-permute-done.4), channel_id=1, source_target_pairs={{0,4},{2,6},{4,0},{6,2},{8,12},{10,14},{12,8},{14,10},{16,20},{18,... | collective-permute-start | bytes 1557512 | tf_op jit(solution)/shard_map/ppermute | solution.py:196
  49.7 15.9 %collective-permute-start.17 = (bf16[256,896]{1,0:T(8,128)(2,1)S(1)}, bf16[256,896]{1,0:T(8,128)(2,1)S(1)}, u32[]{:S(2)}, u32[]{:S(2)}) collective-permute-start(bf16[256,896]{1,0:T(8,128)(2,1)S(1)} %bitcast.25), channel_id=1, source_target_pairs={{0,1},{1,0},{2,3},{3,2},{4,5},{5,4},{6,7},{7,6},{8,9},{9,8},{10,11... | collective-permute-start | bytes 1376264 | tf_op jit(solution)/shard_map/ppermute | solution.py:26
  59.0 15.2 %collective-permute-start.18 = (bf16[104,2496]{1,0:T(8,128)(2,1)}, bf16[104,2496]{1,0:T(8,128)(2,1)S(1)}, u32[]{:S(2)}, u32[]{:S(2)}) collective-permute-start(bf16[104,2496]{1,0:T(8,128)(2,1)} %collective-permute-done.7), channel_id=1, source_target_pairs={{0,2},{2,0},{4,6},{6,4},{8,10},{10,8},{12,14},{14,12},{16,18},{18,... | collective-permute-start | bytes 1557512 | tf_op jit(solution)/shard_map/ppermute | solution.py:196
  60.2 15.2 %collective-permute-start.19 = (bf16[104,2496]{1,0:T(8,128)(2,1)}, bf16[104,2496]{1,0:T(8,128)(2,1)S(1)}, u32[]{:S(2)}, u32[]{:S(2)}) collective-permute-start(bf16[104,2496]{1,0:T(8,128)(2,1)} %collective-permute-done.7), channel_id=1, source_target_pairs={{0,4},{2,6},{4,0},{6,2},{8,12},{10,14},{12,8},{14,10},{16,20},{18,... | collective-permute-start | bytes 1557512 | tf_op jit(solution)/shard_map/ppermute | solution.py:196
  61.7 20.3 %collective-permute-start.15 = (bf16[104,1216]{1,0:T(8,128)(2,1)S(1)}, bf16[104,1216]{1,0:T(8,128)(2,1)S(1)}, u32[]{:S(2)}, u32[]{:S(2)}) collective-permute-start(bf16[104,1216]{1,0:T(8,128)(2,1)S(1)} %slice.36), channel_id=1, source_target_pairs={{0,4},{2,6},{4,0},{6,2},{8,12},{10,14},{12,8},{14,10},{16,20},{18,... | collective-permute-start | bytes 758792 | tf_op jit(solution)/shard_map/ppermute | solution.py:200
  64.6 17.4 %collective-permute-start.14 = (bf16[104,1280]{1,0:T(8,128)(2,1)S(1)}, bf16[104,1280]{1,0:T(8,128)(2,1)S(1)}, u32[]{:S(2)}, u32[]{:S(2)}) collective-permute-start(bf16[104,1280]{1,0:T(8,128)(2,1)S(1)} %slice.35), channel_id=1, source_target_pairs={{0,2},{2,0},{4,6},{6,4},{8,10},{10,8},{12,14},{14,12},{16,18},{18,... | collective-permute-start | bytes 798728 | tf_op jit(solution)/shard_map/ppermute | solution.py:199
  65.5 16.5 %collective-permute-start.13 = (bf16[104,2496]{1,0:T(8,128)(2,1)}, bf16[104,2496]{1,0:T(8,128)(2,1)S(1)}, u32[]{:S(2)}, u32[]{:S(2)}) collective-permute-start(bf16[104,2496]{1,0:T(8,128)(2,1)} %constant_dynamic-update-slice_fusion), channel_id=1, source_target_pairs={{0,8},{2,10},{4,12},{6,14},{8,24},{10,26},{12,28},{14,30},{16,0},{... | collective-permute-start | bytes 1557512 | tf_op jit(solution)/shard_map/ppermute | solution.py:193
  69.0 1.6 %copy-start.3 = (bf16[312,2496]{1,0:T(8,128)(2,1)S(1)}, bf16[312,2496]{1,0:T(8,128)(2,1)}, u32[]{:S(2)}) copy-start(bf16[312,2496]{1,0:T(8,128)(2,1)} %pad_maximum_fusion.1) | copy-start | bytes 4672516
  75.5 9.5 %collective-permute-start.21 = (bf16[104,1216]{1,0:T(8,128)(2,1)S(1)}, bf16[104,1216]{1,0:T(8,128)(2,1)S(1)}, u32[]{:S(2)}, u32[]{:S(2)}) collective-permute-start(bf16[104,1216]{1,0:T(8,128)(2,1)S(1)} %slice.40), channel_id=1, source_target_pairs={{0,4},{2,6},{4,0},{6,2},{8,12},{10,14},{12,8},{14,10},{16,20},{18,... | collective-permute-start | bytes 758792 | tf_op jit(solution)/shard_map/ppermute | solution.py:200
  77.0 7.9 %collective-permute-start.20 = (bf16[104,1280]{1,0:T(8,128)(2,1)S(1)}, bf16[104,1280]{1,0:T(8,128)(2,1)S(1)}, u32[]{:S(2)}, u32[]{:S(2)}) collective-permute-start(bf16[104,1280]{1,0:T(8,128)(2,1)S(1)} %slice.39), channel_id=1, source_target_pairs={{0,2},{2,0},{4,6},{6,4},{8,10},{10,8},{12,14},{14,12},{16,18},{18,... | collective-permute-start | bytes 798728 | tf_op jit(solution)/shard_map/ppermute | solution.py:199

commit v21 on v20

--- a/solution.py
+++ b/solution.py
@@ -192,6 +192,11 @@
     def along_line(block):
         return lax.ppermute(block, "req", line_perm)
 
+    def from_line(step):
+        if step == lines - 1:
+            return lax.ppermute(own, "req", [(to, source) for source, to in line_perm])
+        return along_line(held[step - 1])
+
     def to_sides(block):
         return lax.ppermute(block, "req", x_perm), lax.ppermute(block, "req", y_perm)
 
@@ -200,7 +205,8 @@
         right = lax.ppermute(by_x[:, cut:], "req", y_perm)
         return left, right
 
-    held = [qkv_weight]
+    own = qkv_weight
+    held = [own]
     held.append(along_line(held[0]))
     sides = [to_sides(held[0])]
     picked, stats_own = pick_rows(patches, merge_weight.shape[0])
@@ -221,8 +227,8 @@
 
     partial_value = merge(picked, stats, gain_bias, merge_weight)
 
-    partial_value, held[1], sides[0], slot, code_cols = tie(
-        partial_value, held[1], sides[0], slot, code_cols
+    partial_value, held[1], sides[0], slot, code_cols, own = tie(
+        partial_value, held[1], sides[0], slot, code_cols, own
     )
     held.append(along_line(held[1]))
     sides.append(to_sides(held[1]))
@@ -244,8 +250,9 @@
     held[2], sides[1], norm_gain, me = tie(held[2], sides[1], norm_gain, me)
     gain_column = norm_gain.reshape(n_req, rows, 1)
     order = lax.dynamic_slice_in_dim(jnp.asarray(table), me, 1, 0).reshape(-1)
-    held.append(along_line(held[2]))
+    held.append(from_line(3))
     sides.append(to_sides(held[2]))
+    halves, held[3] = tie(halves, held[3])
     images = [arrived] + [tp_shift(arrived, n_tp, d) for d in range(1, n_tp)]
     blocks = combine(tp_index, order, texts, images, gain_column)
 
@@ -258,7 +265,7 @@
     sides.append(to_sides(held[3]))
     corners.append(along_line(corners[0]))
     for step in range(4, lines):
-        held.append(along_line(held[step - 1]))
+        held.append(from_line(step))
         sides.append(to_sides(held[step]))
     for step in range(2, lines - 2):
         corners.append(along_line(corners[step - 1]))

time: 88.7 us -> 96.1 us (1.083)
  waiting for transfers between devices: 19.1 us -> 27.8 us
  starting transfers between devices: 28.5 us -> 27 us
    ppermute x4 -> x3, waiting for transfers between devices: 8.52 us -> 15.4 us  [along_line(): return lax.ppermute(block, 'req', line_perm)]
    ppermute x4 -> x3, starting transfers between devices: 8.23 us -> 5.62 us  [along_line(): return lax.ppermute(block, 'req', line_perm)]
    ppermute x3, waiting for transfers between devices: 2.56 us -> 0.01 us  [to_corner(): left = lax.ppermute(by_y[:, :cut], 'req', x_perm)]
    ppermute x3, waiting for transfers between devices: 3.15 us -> 5.39 us  [to_corner(): right = lax.ppermute(by_x[:, cut:], 'req', y_perm)]
    all_to_all x1, starting transfers between devices: 3.56 us -> 4.78 us  [shards(): lax.all_to_all(outgoing.reshape(n_req, IMG_CAP, -1), 'req', split_axis=0,...]
    ppermute x4, waiting for transfers between devices: 2.2 us -> 3.37 us  [to_sides(): lax.ppermute(block, 'req', y_perm)]
    ppermute x4, starting transfers between devices: 3.75 us -> 4.87 us  [to_sides(): lax.ppermute(block, 'req', x_perm)]
    ppermute x4, starting transfers between devices: 6.19 us -> 5.23 us  [to_sides(): lax.ppermute(block, 'req', y_perm)]
  transfers between devices with their start and end apart: 23 -> 23, of which waited for: 10 -> 7; matrix products, arithmetic and copies ran while one was open for 29% -> 27% of each run, Pallas kernels for 6% -> 6%
where the time goes in v21:
time: 96.1 us; the launch traced here: 95.5 us
  waiting for transfers between devices  27.8 us (29%)
  starting transfers between devices  27 us (28%)
  local copies, waits for them, and re-layouts  16.5 us (17%)
  matrix products  10.3 us (11%)
  other arithmetic  8.09 us (8%)
  Pallas kernels  5.5 us (6%)
    ppermute x3, waiting for transfers between devices, along_line(): return lax.ppermute(block, 'req', line_perm)  15.4 us
    dot_general x5, matrix products, add_product(): lax.dot_general(source, weight, (((0,), (0,)), ((), ())), preferred_eleme...  9.29 us
    unnamed x13, local copies, waits for them, and re-layouts  7 us
    ppermute x3, starting transfers between devices, along_line(): return lax.ppermute(block, 'req', line_perm)  5.62 us
    ppermute x3, waiting for transfers between devices, to_corner(): right = lax.ppermute(by_x[:, cut:], 'req', y_perm)  5.39 us
    ppermute x4, starting transfers between devices, to_sides(): lax.ppermute(block, 'req', y_perm)  5.23 us
    ppermute x4, starting transfers between devices, to_sides(): lax.ppermute(block, 'req', x_perm)  4.87 us
    all_to_all x1, starting transfers between devices, shards(): lax.all_to_all(outgoing.reshape(n_req, IMG_CAP, -1), 'req', split_axis=0,...  4.78 us
  transfers between devices with their start and end apart: 23, of which 7 were waited for; matrix products, arithmetic and copies ran while one was open for 27% of the time, Pallas kernels for 6%

profile of v21, /device:TPU:0, one launch (start us, length us, event | category | flops | bytes accessed | tf_op | source)
XLA Modules:
  0.0 95.5 jit_solution(6548677134010335872)
XLA Ops:
  0.0 3.0 %collective-permute-start.1 = (bf16[104,2496]{1,0:T(8,128)(2,1)}, bf16[104,2496]{1,0:T(8,128)(2,1)}, u32[]{:S(2)}, u32[]{:S(2)}) collective-permute-start(bf16[104,2496]{1,0:T(8,128)(2,1)} %param.16), channel_id=1, source_target_pairs={{0,8},{2,10},{4,12},{6,14},{8,24},{10,26},{12,28},{14,30},{16,0},{... | collective-permute-start | bytes 1557512 | tf_op jit(solution)/shard_map/ppermute | solution.py:193
  3.0 1.5 %collective-permute-start.2 = (bf16[104,2496]{1,0:T(8,128)(2,1)}, bf16[104,2496]{1,0:T(8,128)(2,1)}, u32[]{:S(2)}, u32[]{:S(2)}) collective-permute-start(bf16[104,2496]{1,0:T(8,128)(2,1)} %param.16), channel_id=1, source_target_pairs={{0,2},{2,0},{4,6},{6,4},{8,10},{10,8},{12,14},{14,12},{16,18},{18,... | collective-permute-start | bytes 1557512 | tf_op jit(solution)/shard_map/ppermute | solution.py:201
  4.5 1.5 %collective-permute-start.3 = (bf16[104,2496]{1,0:T(8,128)(2,1)}, bf16[104,2496]{1,0:T(8,128)(2,1)}, u32[]{:S(2)}, u32[]{:S(2)}) collective-permute-start(bf16[104,2496]{1,0:T(8,128)(2,1)} %param.16), channel_id=1, source_target_pairs={{0,4},{2,6},{4,0},{6,2},{8,12},{10,14},{12,8},{14,10},{16,20},{18,... | collective-permute-start | bytes 1557512 | tf_op jit(solution)/shard_map/ppermute | solution.py:201
  6.0 1.1 %copy-done.2 = bf16[448,832]{1,0:T(8,128)(2,1)S(1)} copy-done((bf16[448,832]{1,0:T(8,128)(2,1)S(1)}, bf16[448,832]{1,0:T(8,128)(2,1)}, u32[]{:S(2)}) %copy-start.2) | copy-done | bytes 745496
  7.2 0.8 shard_map.118
  7.9 0.1 collective-permute-start
  8.0 0.7 convert_bitcast_fusion.1
  8.7 0.7 stack.22
  9.4 0.7 stack.21
  10.1 0.2 convert_reduce_fusion
  10.3 0.0 copy-start
  10.3 4.1 %copy-done = bf16[4,832,1664]{2,1,0:T(8,128)(2,1)S(1)} copy-done((bf16[4,832,1664]{2,1,0:T(8,128)(2,1)S(1)}, bf16[4,832,1664]{2,1,0:T(8,128)(2,1)}, u32[]{:S(2)}) %copy-start) | copy-done | bytes 11075608
  14.5 2.9 %shard_map.119 = f32[112,1664]{1,0:T(8,128)S(1)} custom-call(bf16[4,112,832]{2,1,0:T(8,128)(2,1)S(1)} %get-tuple-element.52.picked_ref, bf16[2,832]{1,0:T(2,128)(2,1)S(1)} %pad_maximum_fusion.4.gain_bias_ref, f32[4,112,256]{2,1,0:T(8,128)S(1)} %get-tuple-element.53.refs_0_, f32[4,112,256]{2,1,0:T(8,128)S(1)} %collective-permute-done.refs_1_, ...), custom_call_target="tpu_custom_call" | custom-call | flops 1000 | bytes 1000 | tf_op jit(solution)/shard_map/pallas_call | solution.py:117
  17.4 0.0 collective-permute-done.1
  17.4 0.0 collective-permute-done.2
  17.4 0.7 collective-permute-done.3
  18.1 0.9 constant_dynamic-slice_fusion
  19.0 2.6 %collective-permute-start.4 = (bf16[104,2496]{1,0:T(8,128)(2,1)}, bf16[104,2496]{1,0:T(8,128)(2,1)}, u32[]{:S(2)}, u32[]{:S(2)}) collective-permute-start(bf16[104,2496]{1,0:T(8,128)(2,1)} %collective-permute-done.1), channel_id=1, source_target_pairs={{0,8},{2,10},{4,12},{6,14},{8,24},{10,26},{12,28},{14,30},{16,0},{... | collective-permute-start | bytes 1557512 | tf_op jit(solution)/shard_map/ppermute | solution.py:193
  21.6 0.5 collective-permute-start.5
  22.2 1.5 %collective-permute-start.6 = (bf16[104,2496]{1,0:T(8,128)(2,1)}, bf16[104,2496]{1,0:T(8,128)(2,1)}, u32[]{:S(2)}, u32[]{:S(2)}) collective-permute-start(bf16[104,2496]{1,0:T(8,128)(2,1)} %collective-permute-done.1), channel_id=1, source_target_pairs={{0,4},{2,6},{4,0},{6,2},{8,12},{10,14},{12,8},{14,10},{16,20},{18,... | collective-permute-start | bytes 1557512 | tf_op jit(solution)/shard_map/ppermute | solution.py:201
  23.7 0.1 pad.13.clone
  23.8 0.1 copy.18
  23.9 0.0 copy-start.4
  23.9 0.4 collective-permute-start.10
  24.3 0.2 add_convert_fusion
  24.5 1.0 %slice.33 = bf16[104,1280]{1,0:T(8,128)(2,1)S(1)} slice(bf16[104,2496]{1,0:T(8,128)(2,1)} %collective-permute-done.3), slice={[0:104], [0:1280]} | slice | bytes 532480 | tf_op jit(solution)/shard_map/slice | solution.py:204
  25.5 1.7 %slice.34 = bf16[104,1216]{1,0:T(8,128)(2,1)} slice(bf16[104,2496]{1,0:T(8,128)(2,1)} %collective-permute-done.2), slice={[0:104], [1280:2496]} | slice | bytes 505856 | tf_op jit(solution)/shard_map/slice | solution.py:205
  27.2 1.1 %convolution_convert_fusion = bf16[256,896]{1,0:T(8,128)(2,1)} fusion(bf16[112,2]{1,0:T(8,128)(2,1)S(1)} %copy.18, bf16[112,832]{1,0:T(8,128)(2,1)S(1)} %add_convert_fusion, bf16[896]{0:T(1024)(128)(2,1)S(1)} %pad.13.clone, s32[112]{0:T(128)S(1)} %multiply_add_fusion), kind=kOutput, calls=%fused_computation.9 | convolution fusion | flops 52240384 | bytes 647808 | tf_op jit(solution)/shard_map/dot_general | solution.py:245
  28.2 4.8 %all-to-all-start = ((bf16[16,16,896]{2,1,0:T(8,128)(2,1)}), bf16[16,16,896]{2,1,0:T(8,128)(2,1)S(1)}, u32[]{:S(2)}, u32[]{:S(2)}) async-start(bf16[16,16,896]{2,1,0:T(8,128)(2,1)} %bitcast.5), calls=%async_computation | async-start | bytes 917504 | tf_op jit(solution)/shard_map/all_to_all | solution.py:246
  33.0 15.4 %collective-permute-done.4 = bf16[104,2496]{1,0:T(8,128)(2,1)} collective-permute-done((bf16[104,2496]{1,0:T(8,128)(2,1)}, bf16[104,2496]{1,0:T(8,128)(2,1)}, u32[]{:S(2)}, u32[]{:S(2)}) %collective-permute-start.4) | collective-permute-done | bytes 519200 | tf_op jit(solution)/shard_map/ppermute | solution.py:193
  48.4 0.9 collective-permute-start.9
  49.3 2.0 %collective-permute-start.11 = (bf16[104,2496]{1,0:T(8,128)(2,1)}, bf16[104,2496]{1,0:T(8,128)(2,1)S(1)}, u32[]{:S(2)}, u32[]{:S(2)}) collective-permute-start(bf16[104,2496]{1,0:T(8,128)(2,1)} %collective-permute-done.4), channel_id=1, source_target_pairs={{0,2},{2,0},{4,6},{6,4},{8,10},{10,8},{12,14},{14,12},{16,18},{18,... | collective-permute-start | bytes 1557512 | tf_op jit(solution)/shard_map/ppermute | solution.py:201
  51.3 2.6 %pad_maximum_fusion.1 = bf16[312,2496]{1,0:T(8,128)(2,1)} fusion(bf16[104,2496]{1,0:T(8,128)(2,1)} %collective-permute-done.6, bf16[104,2496]{1,0:T(8,128)(2,1)} %collective-permute-done.5, bf16[104,2496]{1,0:T(8,128)(2,1)} %collective-permute-done.1), kind=kLoop, calls=%fused_computation.5 | loop fusion | flops 4672512 | bytes 3115008 | tf_op jit(solution)/shard_map/concatenate | solution.py:261
  54.0 0.1 fusion.7
  54.1 0.7 fusion.10.order_ref
  54.8 0.8 reshape.62.gain_ref
  55.6 1.2 %collective-permute-start.12 = (bf16[104,2496]{1,0:T(8,128)(2,1)}, bf16[104,2496]{1,0:T(8,128)(2,1)}, u32[]{:S(2)}, u32[]{:S(2)}) collective-permute-start(bf16[104,2496]{1,0:T(8,128)(2,1)} %collective-permute-done.4), channel_id=1, source_target_pairs={{0,4},{2,6},{4,0},{6,2},{8,12},{10,14},{12,8},{14,10},{16,20},{18,... | collective-permute-start | bytes 1557512 | tf_op jit(solution)/shard_map/ppermute | solution.py:201
  56.8 2.5 %collective-permute-done.9 = bf16[104,1216]{1,0:T(8,128)(2,1)} collective-permute-done((bf16[104,1216]{1,0:T(8,128)(2,1)}, bf16[104,1216]{1,0:T(8,128)(2,1)}, u32[]{:S(2)}, u32[]{:S(2)}) %collective-permute-start.9) | collective-permute-done | bytes 252960 | tf_op jit(solution)/shard_map/ppermute | solution.py:205
  59.3 1.7 %constant_dynamic-update-slice_fusion.1 = bf16[104,2496]{1,0:T(8,128)(2,1)} fusion(bf16[104,1280]{1,0:T(8,128)(2,1)} %collective-permute-done.8), kind=kLoop, calls=%fused_computation.23 | loop fusion | bytes 532480
  61.0 1.7 %constant_dynamic-update-slice_fusion = bf16[104,2496]{1,0:T(8,128)(2,1)} fusion(bf16[104,2496]{1,0:T(8,128)(2,1)} %constant_dynamic-update-slice_fusion.1, bf16[104,1216]{1,0:T(8,128)(2,1)} %collective-permute-done.9), kind=kLoop, calls=%fused_computation.22 | loop fusion | bytes 532480 | tf_op jit(solution)/shard_map/concatenate | solution.py:259
  62.7 1.7 %pad_maximum_fusion = bf16[416,2496]{1,0:T(8,128)(2,1)S(1)} fusion(bf16[104,2496]{1,0:T(8,128)(2,1)} %constant_dynamic-update-slice_fusion, bf16[104,2496]{1,0:T(8,128)(2,1)} %collective-permute-done.3, bf16[104,2496]{1,0:T(8,128)(2,1)} %collective-permute-done.2, bf16[104,2496]{1,0:T(8,128)(2,1)} %param.16), kind=kLoop, calls=%fused_computation.4 | loop fusion | flops 8306688 | bytes 4153344 | tf_op jit(solution)/shard_map/concatenate | solution.py:260
  64.4 1.9 %collective-permute-done.12 = bf16[104,2496]{1,0:T(8,128)(2,1)} collective-permute-done((bf16[104,2496]{1,0:T(8,128)(2,1)}, bf16[104,2496]{1,0:T(8,128)(2,1)}, u32[]{:S(2)}, u32[]{:S(2)}) %collective-permute-start.12) | collective-permute-done | bytes 519200 | tf_op jit(solution)/shard_map/ppermute | solution.py:201
  66.2 0.8 collective-permute-start.18
  67.0 1.0 %collective-permute-start.19 = (bf16[104,2496]{1,0:T(8,128)(2,1)}, bf16[104,2496]{1,0:T(8,128)(2,1)S(1)}, u32[]{:S(2)}, u32[]{:S(2)}) collective-permute-start(bf16[104,2496]{1,0:T(8,128)(2,1)} %collective-permute-done.10), channel_id=1, source_target_pairs={{0,4},{2,6},{4,0},{6,2},{8,12},{10,14},{12,8},{14,10},{16,20},{18,... | collective-permute-start | bytes 1557512 | tf_op jit(solution)/shard_map/ppermute | solution.py:201
  68.1 1.1 %collective-permute-start.15 = (bf16[104,1216]{1,0:T(8,128)(2,1)S(1)}, bf16[104,1216]{1,0:T(8,128)(2,1)S(1)}, u32[]{:S(2)}, u32[]{:S(2)}) collective-permute-start(bf16[104,1216]{1,0:T(8,128)(2,1)S(1)} %slice.36), channel_id=1, source_target_pairs={{0,4},{2,6},{4,0},{6,2},{8,12},{10,14},{12,8},{14,10},{16,20},{18,... | collective-permute-start | bytes 758792 | tf_op jit(solution)/shard_map/ppermute | solution.py:205
  69.1 1.0 %slice.35 = bf16[104,1280]{1,0:T(8,128)(2,1)S(1)} slice(bf16[104,2496]{1,0:T(8,128)(2,1)} %collective-permute-done.12), slice={[0:104], [0:1280]} | slice | bytes 532480 | tf_op jit(solution)/shard_map/slice | solution.py:204
  70.1 1.3 %pad_maximum_fusion.2 = bf16[312,2496]{1,0:T(8,128)(2,1)S(1)} fusion(bf16[104,2496]{1,0:T(8,128)(2,1)} %collective-permute-done.12, bf16[104,2496]{1,0:T(8,128)(2,1)S(1)} %collective-permute-done.11, bf16[104,2496]{1,0:T(8,128)(2,1)} %collective-permute-done.4), kind=kLoop, calls=%fused_computation.7 | loop fusion | flops 4672512 | bytes 3115008 | tf_op jit(solution)/shard_map/concatenate | solution.py:275
  71.5 1.3 %collective-permute-start.14 = (bf16[104,1280]{1,0:T(8,128)(2,1)S(1)}, bf16[104,1280]{1,0:T(8,128)(2,1)S(1)}, u32[]{:S(2)}, u32[]{:S(2)}) collective-permute-start(bf16[104,1280]{1,0:T(8,128)(2,1)S(1)} %slice.35), channel_id=1, source_target_pairs={{0,2},{2,0},{4,6},{6,4},{8,10},{10,8},{12,14},{14,12},{16,18},{18,... | collective-permute-start | bytes 798728 | tf_op jit(solution)/shard_map/ppermute | solution.py:204
  72.7 0.0 collective-permute-start.13
  72.7 1.8 %shard_map.120 = bf16[16,104,512]{2,1,0:T(8,128)(2,1)S(1)} custom-call(s32[1]{0:T(128)} %bitcast.2.index_ref, s32[16]{0:T(128)S(1)} %fusion.10.order_ref, bf16[16,104,1]{2,1,0:T(8,128)(2,1)S(1)} %reshape.62.gain_ref, bf16[832,512]{1,0:T(8,128)(2,1)S(1)} %bitcast.28, bf16[832,512]{1,0:T(8,128)(2,1)S(1)} %collective-permute-done.16.refs_1_, ...), custom_call_target="tpu_custom_call" | custom-call | flops 1000 | bytes 1000 | tf_op jit(solution)/shard_map/pallas_call | solution.py:168
  74.6 0.1 fusion.14
  74.7 0.0 copy-start.3
  74.7 1.5 %fusion.15 = f32[512,2496]{0,1:T(8,128)S(1)} fusion(bf16[416,512]{1,0:T(8,128)(2,1)S(1)} %bitcast.30, bf16[416,2496]{1,0:T(8,128)(2,1)S(1)} %pad_maximum_fusion), kind=kOutput, calls=%fused_computation.48 | convolution fusion | flops 1063256064 | bytes 7614464 | tf_op jit(solution)/shard_map/dot_general | solution.py:282
  76.3 1.5 %convolution_add_fusion.2 = f32[512,2496]{0,1:T(8,128)S(1)} fusion(f32[512,2496]{0,1:T(8,128)S(1)} %fusion.15, bf16[312,512]{1,0:T(8,128)(2,1)S(1)} %bitcast.33, bf16[312,2496]{1,0:T(8,128)(2,1)S(1)} %copy-done.3), kind=kOutput, calls=%fused_computation.3 | convolution fusion | flops 798720000 | bytes 12100608 | tf_op jit(solution)/shard_map/dot_general | solution.py:282
  77.8 3.6 %collective-permute-done.18 = bf16[104,2496]{1,0:T(8,128)(2,1)S(1)} collective-permute-done((bf16[104,2496]{1,0:T(8,128)(2,1)}, bf16[104,2496]{1,0:T(8,128)(2,1)S(1)}, u32[]{:S(2)}, u32[]{:S(2)}) %collective-permute-start.18) | collective-permute-done | bytes 519200 | tf_op jit(solution)/shard_map/ppermute | solution.py:201
  81.5 0.8 collective-permute-done.19
  82.3 1.1 %collective-permute-start.21 = (bf16[104,1216]{1,0:T(8,128)(2,1)S(1)}, bf16[104,1216]{1,0:T(8,128)(2,1)S(1)}, u32[]{:S(2)}, u32[]{:S(2)}) collective-permute-start(bf16[104,1216]{1,0:T(8,128)(2,1)S(1)} %slice.40), channel_id=1, source_target_pairs={{0,4},{2,6},{4,0},{6,2},{8,12},{10,14},{12,8},{14,10},{16,20},{18,... | collective-permute-start | bytes 758792 | tf_op jit(solution)/shard_map/ppermute | solution.py:205
  83.4 1.6 %collective-permute-start.20 = (bf16[104,1280]{1,0:T(8,128)(2,1)S(1)}, bf16[104,1280]{1,0:T(8,128)(2,1)S(1)}, u32[]{:S(2)}, u32[]{:S(2)}) collective-permute-start(bf16[104,1280]{1,0:T(8,128)(2,1)S(1)} %slice.39), channel_id=1, source_target_pairs={{0,2},{2,0},{4,6},{6,4},{8,10},{10,8},{12,14},{14,12},{16,18},{18,... | collective-permute-start | bytes 798728 | tf_op jit(solution)/shard_map/ppermute | solution.py:204
  85.0 1.5 %convolution_add_fusion.1 = f32[512,2496]{0,1:T(8,128)S(1)} fusion(f32[512,2496]{0,1:T(8,128)S(1)} %convolution_add_fusion.2, bf16[312,512]{1,0:T(8,128)(2,1)S(1)} %bitcast.32, bf16[312,2496]{1,0:T(8,128)(2,1)S(1)} %pad_maximum_fusion.2), kind=kOutput, calls=%fused_computation.2 | convolution fusion | flops 798720000 | bytes 12100608 | tf_op jit(solution)/shard_map/dot_general | solution.py:282
  86.6 1.2 %pad_maximum_fusion.3 = bf16[312,2496]{1,0:T(8,128)(2,1)S(1)} fusion(bf16[104,2496]{1,0:T(8,128)(2,1)S(1)} %collective-permute-done.19, bf16[104,2496]{1,0:T(8,128)(2,1)S(1)} %collective-permute-done.18, bf16[104,2496]{1,0:T(8,128)(2,1)} %collective-permute-done.10), kind=kLoop, calls=%fused_computation.8 | loop fusion | flops 4672512 | bytes 3115008 | tf_op jit(solution)/shard_map/concatenate | solution.py:275
  87.8 1.6 %convolution_add_fusion = f32[512,2496]{0,1:T(8,128)S(1)} fusion(f32[512,2496]{0,1:T(8,128)S(1)} %convolution_add_fusion.1, bf16[312,512]{1,0:T(8,128)(2,1)S(1)} %bitcast.31, bf16[312,2496]{1,0:T(8,128)(2,1)S(1)} %pad_maximum_fusion.3), kind=kOutput, calls=%fused_computation.1 | convolution fusion | flops 798720000 | bytes 12100608 | tf_op jit(solution)/shard_map/dot_general | solution.py:282
  89.4 2.9 %collective-permute-done.21 = bf16[104,1216]{1,0:T(8,128)(2,1)S(1)} collective-permute-done((bf16[104,1216]{1,0:T(8,128)(2,1)S(1)}, bf16[104,1216]{1,0:T(8,128)(2,1)S(1)}, u32[]{:S(2)}, u32[]{:S(2)}) %collective-permute-start.21) | collective-permute-done | bytes 252960 | tf_op jit(solution)/shard_map/ppermute | solution.py:205
  92.3 0.1 maximum_maximum_fusion
  92.4 3.0 %select_convert_fusion = bf16[512,2496]{0,1:T(8,128)(2,1)} fusion(f32[512,2496]{0,1:T(8,128)S(1)} %convolution_add_fusion, bf16[312,512]{1,0:T(8,128)(2,1)S(1)} %bitcast.29, bf16[312,2496]{1,0:T(8,128)(2,1)S(1)} %maximum_maximum_fusion, pred[512]{0:T(512)(128)(4,1)S(1)} %fusion.8), kind=kOutput, calls=%fused_computation | convolution fusion | flops 801275904 | bytes 9545216 | tf_op jit(solution)/shard_map/dot_general | solution.py:282
  (36 shorter events, 0.2 us)
Async XLA Ops:
  0.0 17.4 %collective-permute-start.1 = (bf16[104,2496]{1,0:T(8,128)(2,1)}, bf16[104,2496]{1,0:T(8,128)(2,1)}, u32[]{:S(2)}, u32[]{:S(2)}) collective-permute-start(bf16[104,2496]{1,0:T(8,128)(2,1)} %param.16), channel_id=1, source_target_pairs={{0,8},{2,10},{4,12},{6,14},{8,24},{10,26},{12,28},{14,30},{16,0},{... | collective-permute-start | bytes 1557512 | tf_op jit(solution)/shard_map/ppermute | solution.py:193
  3.0 14.4 %collective-permute-start.2 = (bf16[104,2496]{1,0:T(8,128)(2,1)}, bf16[104,2496]{1,0:T(8,128)(2,1)}, u32[]{:S(2)}, u32[]{:S(2)}) collective-permute-start(bf16[104,2496]{1,0:T(8,128)(2,1)} %param.16), channel_id=1, source_target_pairs={{0,2},{2,0},{4,6},{6,4},{8,10},{10,8},{12,14},{14,12},{16,18},{18,... | collective-permute-start | bytes 1557512 | tf_op jit(solution)/shard_map/ppermute | solution.py:201
  4.5 13.6 %collective-permute-start.3 = (bf16[104,2496]{1,0:T(8,128)(2,1)}, bf16[104,2496]{1,0:T(8,128)(2,1)}, u32[]{:S(2)}, u32[]{:S(2)}) collective-permute-start(bf16[104,2496]{1,0:T(8,128)(2,1)} %param.16), channel_id=1, source_target_pairs={{0,4},{2,6},{4,0},{6,2},{8,12},{10,14},{12,8},{14,10},{16,20},{18,... | collective-permute-start | bytes 1557512 | tf_op jit(solution)/shard_map/ppermute | solution.py:201
  6.0 1.1 %copy-start.2 = (bf16[448,832]{1,0:T(8,128)(2,1)S(1)}, bf16[448,832]{1,0:T(8,128)(2,1)}, u32[]{:S(2)}) copy-start(bf16[448,832]{1,0:T(8,128)(2,1)} %patches_ref.1) | copy-start | bytes 2236420
  7.9 2.4 %collective-permute-start = (f32[4,112,256]{2,1,0:T(8,128)S(1)}, f32[4,112,256]{2,1,0:T(8,128)S(1)}, u32[]{:S(2)}, u32[]{:S(2)}) collective-permute-start(f32[4,112,256]{2,1,0:T(8,128)S(1)} %get-tuple-element.53.refs_0_), channel_id=1, source_target_pairs={{0,1},{1,0},{2,3},{3,2},{4,5},{5,4},{6,7},{7,6},{8,9},{9,8},{10,11... | collective-permute-start | bytes 1376264 | tf_op jit(solution)/shard_map/ppermute | solution.py:26
  10.3 4.1 %copy-start = (bf16[4,832,1664]{2,1,0:T(8,128)(2,1)S(1)}, bf16[4,832,1664]{2,1,0:T(8,128)(2,1)}, u32[]{:S(2)}) copy-start(bf16[4,832,1664]{2,1,0:T(8,128)(2,1)} %refs_2_.1) | copy-start | bytes 33226756
  14.5 9.2 %copy-start.1 = (bf16[512,832]{0,1:T(8,128)(2,1)S(1)}, bf16[512,832]{0,1:T(8,128)(2,1)}, u32[]{:S(2)}) copy-start(bf16[512,832]{0,1:T(8,128)(2,1)} %param.14) | copy-start | bytes 2555908
  19.0 4.9 %collective-permute-start.7 = (f32[112,832]{1,0:T(8,128)}, f32[112,832]{1,0:T(8,128)S(1)}, u32[]{:S(2)}, u32[]{:S(2)}) collective-permute-start(f32[112,832]{1,0:T(8,128)} %constant_dynamic-slice_fusion), channel_id=1, source_target_pairs={{0,1},{1,0},{2,3},{3,2},{4,5},{5,4},{6,7},{7,6},{8,9},{9,8},{10,11... | collective-permute-start | bytes 1118216 | tf_op jit(solution)/shard_map/ppermute | solution.py:26
  19.0 29.4 %collective-permute-start.4 = (bf16[104,2496]{1,0:T(8,128)(2,1)}, bf16[104,2496]{1,0:T(8,128)(2,1)}, u32[]{:S(2)}, u32[]{:S(2)}) collective-permute-start(bf16[104,2496]{1,0:T(8,128)(2,1)} %collective-permute-done.1), channel_id=1, source_target_pairs={{0,8},{2,10},{4,12},{6,14},{8,24},{10,26},{12,28},{14,30},{16,0},{... | collective-permute-start | bytes 1557512 | tf_op jit(solution)/shard_map/ppermute | solution.py:193
  21.6 26.8 %collective-permute-start.5 = (bf16[104,2496]{1,0:T(8,128)(2,1)}, bf16[104,2496]{1,0:T(8,128)(2,1)}, u32[]{:S(2)}, u32[]{:S(2)}) collective-permute-start(bf16[104,2496]{1,0:T(8,128)(2,1)} %collective-permute-done.1), channel_id=1, source_target_pairs={{0,2},{2,0},{4,6},{6,4},{8,10},{10,8},{12,14},{14,12},{16,18},{18,... | collective-permute-start | bytes 1557512 | tf_op jit(solution)/shard_map/ppermute | solution.py:201
  22.2 27.2 %collective-permute-start.6 = (bf16[104,2496]{1,0:T(8,128)(2,1)}, bf16[104,2496]{1,0:T(8,128)(2,1)}, u32[]{:S(2)}, u32[]{:S(2)}) collective-permute-start(bf16[104,2496]{1,0:T(8,128)(2,1)} %collective-permute-done.1), channel_id=1, source_target_pairs={{0,4},{2,6},{4,0},{6,2},{8,12},{10,14},{12,8},{14,10},{16,20},{18,... | collective-permute-start | bytes 1557512 | tf_op jit(solution)/shard_map/ppermute | solution.py:201
  23.7 47.8 %collective-permute-start.16 = (bf16[832,512]{1,0:T(8,128)(2,1)S(1)}, bf16[832,512]{1,0:T(8,128)(2,1)S(1)}, u32[]{:S(2)}, u32[]{:S(2)}) collective-permute-start(bf16[832,512]{1,0:T(8,128)(2,1)S(1)} %bitcast.27), channel_id=1, source_target_pairs={{0,1},{1,0},{2,3},{3,2},{4,5},{5,4},{6,7},{7,6},{8,9},{9,8},{10,11... | collective-permute-start | bytes 2555912 | tf_op jit(solution)/shard_map/ppermute | solution.py:26
  23.9 30.1 %copy-start.5 = (s32[2]{0:T(128)S(1)}, s32[2]{0:T(128)}, u32[]{:S(2)}) copy-start(s32[2]{0:T(128)} %param.18) | copy-start | bytes 28
  23.9 30.9 %copy-start.4 = (bf16[1664]{0:T(1024)(128)(2,1)S(1)}, bf16[1664]{0:T(1024)(128)(2,1)}, u32[]{:S(2)}) copy-start(bf16[1664]{0:T(1024)(128)(2,1)} %param.15) | copy-start | bytes 9988
  23.9 31.7 %collective-permute-start.10 = (bf16[104,2496]{1,0:T(8,128)(2,1)}, bf16[104,2496]{1,0:T(8,128)(2,1)}, u32[]{:S(2)}, u32[]{:S(2)}) collective-permute-start(bf16[104,2496]{1,0:T(8,128)(2,1)} %param.16), channel_id=1, source_target_pairs={{8,0},{10,2},{12,4},{14,6},{24,8},{26,10},{28,12},{30,14},{0,16},{... | collective-permute-start | bytes 1557512 | tf_op jit(solution)/shard_map/ppermute | solution.py:197
  28.2 34.4 %all-to-all-start = ((bf16[16,16,896]{2,1,0:T(8,128)(2,1)}), bf16[16,16,896]{2,1,0:T(8,128)(2,1)S(1)}, u32[]{:S(2)}, u32[]{:S(2)}) async-start(bf16[16,16,896]{2,1,0:T(8,128)(2,1)} %bitcast.5), calls=%async_computation | async-start | bytes 917504 | tf_op jit(solution)/shard_map/all_to_all | solution.py:246
  48.4 10.9 %collective-permute-start.8 = (bf16[104,1280]{1,0:T(8,128)(2,1)S(1)}, bf16[104,1280]{1,0:T(8,128)(2,1)}, u32[]{:S(2)}, u32[]{:S(2)}) collective-permute-start(bf16[104,1280]{1,0:T(8,128)(2,1)S(1)} %slice.33), channel_id=1, source_target_pairs={{0,2},{2,0},{4,6},{6,4},{8,10},{10,8},{12,14},{14,12},{16,18},{18,... | collective-permute-start | bytes 798728 | tf_op jit(solution)/shard_map/ppermute | solution.py:204
  48.4 10.9 %collective-permute-start.9 = (bf16[104,1216]{1,0:T(8,128)(2,1)}, bf16[104,1216]{1,0:T(8,128)(2,1)}, u32[]{:S(2)}, u32[]{:S(2)}) collective-permute-start(bf16[104,1216]{1,0:T(8,128)(2,1)} %slice.34), channel_id=1, source_target_pairs={{0,4},{2,6},{4,0},{6,2},{8,12},{10,14},{12,8},{14,10},{16,20},{18,... | collective-permute-start | bytes 758792 | tf_op jit(solution)/shard_map/ppermute | solution.py:205
  49.3 15.0 %collective-permute-start.11 = (bf16[104,2496]{1,0:T(8,128)(2,1)}, bf16[104,2496]{1,0:T(8,128)(2,1)S(1)}, u32[]{:S(2)}, u32[]{:S(2)}) collective-permute-start(bf16[104,2496]{1,0:T(8,128)(2,1)} %collective-permute-done.4), channel_id=1, source_target_pairs={{0,2},{2,0},{4,6},{6,4},{8,10},{10,8},{12,14},{14,12},{16,18},{18,... | collective-permute-start | bytes 1557512 | tf_op jit(solution)/shard_map/ppermute | solution.py:201
  55.6 10.6 %collective-permute-start.12 = (bf16[104,2496]{1,0:T(8,128)(2,1)}, bf16[104,2496]{1,0:T(8,128)(2,1)}, u32[]{:S(2)}, u32[]{:S(2)}) collective-permute-start(bf16[104,2496]{1,0:T(8,128)(2,1)} %collective-permute-done.4), channel_id=1, source_target_pairs={{0,4},{2,6},{4,0},{6,2},{8,12},{10,14},{12,8},{14,10},{16,20},{18,... | collective-permute-start | bytes 1557512 | tf_op jit(solution)/shard_map/ppermute | solution.py:201
  62.7 10.1 %collective-permute-start.17 = (bf16[256,896]{1,0:T(8,128)(2,1)S(1)}, bf16[256,896]{1,0:T(8,128)(2,1)S(1)}, u32[]{:S(2)}, u32[]{:S(2)}) collective-permute-start(bf16[256,896]{1,0:T(8,128)(2,1)S(1)} %bitcast.25), channel_id=1, source_target_pairs={{0,1},{1,0},{2,3},{3,2},{4,5},{5,4},{6,7},{7,6},{8,9},{9,8},{10,11... | collective-permute-start | bytes 1376264 | tf_op jit(solution)/shard_map/ppermute | solution.py:26
  66.2 15.2 %collective-permute-start.18 = (bf16[104,2496]{1,0:T(8,128)(2,1)}, bf16[104,2496]{1,0:T(8,128)(2,1)S(1)}, u32[]{:S(2)}, u32[]{:S(2)}) collective-permute-start(bf16[104,2496]{1,0:T(8,128)(2,1)} %collective-permute-done.10), channel_id=1, source_target_pairs={{0,2},{2,0},{4,6},{6,4},{8,10},{10,8},{12,14},{14,12},{16,18},{18,... | collective-permute-start | bytes 1557512 | tf_op jit(solution)/shard_map/ppermute | solution.py:201
  67.0 15.2 %collective-permute-start.19 = (bf16[104,2496]{1,0:T(8,128)(2,1)}, bf16[104,2496]{1,0:T(8,128)(2,1)S(1)}, u32[]{:S(2)}, u32[]{:S(2)}) collective-permute-start(bf16[104,2496]{1,0:T(8,128)(2,1)} %collective-permute-done.10), channel_id=1, source_target_pairs={{0,4},{2,6},{4,0},{6,2},{8,12},{10,14},{12,8},{14,10},{16,20},{18,... | collective-permute-start | bytes 1557512 | tf_op jit(solution)/shard_map/ppermute | solution.py:201
  68.1 21.3 %collective-permute-start.15 = (bf16[104,1216]{1,0:T(8,128)(2,1)S(1)}, bf16[104,1216]{1,0:T(8,128)(2,1)S(1)}, u32[]{:S(2)}, u32[]{:S(2)}) collective-permute-start(bf16[104,1216]{1,0:T(8,128)(2,1)S(1)} %slice.36), channel_id=1, source_target_pairs={{0,4},{2,6},{4,0},{6,2},{8,12},{10,14},{12,8},{14,10},{16,20},{18,... | collective-permute-start | bytes 758792 | tf_op jit(solution)/shard_map/ppermute | solution.py:205
  71.5 17.9 %collective-permute-start.14 = (bf16[104,1280]{1,0:T(8,128)(2,1)S(1)}, bf16[104,1280]{1,0:T(8,128)(2,1)S(1)}, u32[]{:S(2)}, u32[]{:S(2)}) collective-permute-start(bf16[104,1280]{1,0:T(8,128)(2,1)S(1)} %slice.35), channel_id=1, source_target_pairs={{0,2},{2,0},{4,6},{6,4},{8,10},{10,8},{12,14},{14,12},{16,18},{18,... | collective-permute-start | bytes 798728 | tf_op jit(solution)/shard_map/ppermute | solution.py:204
  72.7 16.7 %collective-permute-start.13 = (bf16[104,2496]{1,0:T(8,128)(2,1)}, bf16[104,2496]{1,0:T(8,128)(2,1)S(1)}, u32[]{:S(2)}, u32[]{:S(2)}) collective-permute-start(bf16[104,2496]{1,0:T(8,128)(2,1)} %constant_dynamic-update-slice_fusion), channel_id=1, source_target_pairs={{0,8},{2,10},{4,12},{6,14},{8,24},{10,26},{12,28},{14,30},{16,0},{... | collective-permute-start | bytes 1557512 | tf_op jit(solution)/shard_map/ppermute | solution.py:193
  74.7 1.6 %copy-start.3 = (bf16[312,2496]{1,0:T(8,128)(2,1)S(1)}, bf16[312,2496]{1,0:T(8,128)(2,1)}, u32[]{:S(2)}) copy-start(bf16[312,2496]{1,0:T(8,128)(2,1)} %pad_maximum_fusion.1) | copy-start | bytes 4672516
  82.3 10.0 %collective-permute-start.21 = (bf16[104,1216]{1,0:T(8,128)(2,1)S(1)}, bf16[104,1216]{1,0:T(8,128)(2,1)S(1)}, u32[]{:S(2)}, u32[]{:S(2)}) collective-permute-start(bf16[104,1216]{1,0:T(8,128)(2,1)S(1)} %slice.40), channel_id=1, source_target_pairs={{0,4},{2,6},{4,0},{6,2},{8,12},{10,14},{12,8},{14,10},{16,20},{18,... | collective-permute-start | bytes 758792 | tf_op jit(solution)/shard_map/ppermute | solution.py:205
  83.4 8.9 %collective-permute-start.20 = (bf16[104,1280]{1,0:T(8,128)(2,1)S(1)}, bf16[104,1280]{1,0:T(8,128)(2,1)S(1)}, u32[]{:S(2)}, u32[]{:S(2)}) collective-permute-start(bf16[104,1280]{1,0:T(8,128)(2,1)S(1)} %slice.39), channel_id=1, source_target_pairs={{0,2},{2,0},{4,6},{6,4},{8,10},{10,8},{12,14},{14,12},{16,18},{18,... | collective-permute-start | bytes 798728 | tf_op jit(solution)/shard_map/ppermute | solution.py:204

commit v22 on v19

--- a/solution.py
+++ b/solution.py
@@ -41,9 +41,8 @@
     order = folded_ring(lines)
     following = {order[i]: order[(i + 1) % lines] for i in range(lines)}
     line_perm = [(z * 4 + p, following[z] * 4 + p) for z in range(lines) for p in range(4)]
-    arrivals = [(0, flip) for flip in range(4)]
-    arrivals += [(step, flip) for step in range(1, lines) for flip in range(3)]
-    arrivals += [(step, 3) for step in range(1, lines)]
+    arrivals = [(step, flip) for step in range(lines) for flip in range(3)]
+    arrivals += [(step, 3) for step in range(lines)]
     table = np.zeros((n_req, n_req), np.int32)
     for index in range(n_req):
         for place, (step, flip) in enumerate(arrivals):
@@ -241,15 +240,17 @@
         outgoing.reshape(n_req, IMG_CAP, -1), "req", split_axis=0, concat_axis=0
     ).reshape(slot_count, -1)
 
+    held.append(along_line(held[2]))
     held[2], sides[1], norm_gain, me = tie(held[2], sides[1], norm_gain, me)
     gain_column = norm_gain.reshape(n_req, rows, 1)
     order = lax.dynamic_slice_in_dim(jnp.asarray(table), me, 1, 0).reshape(-1)
-    held.append(along_line(held[2]))
     sides.append(to_sides(held[2]))
     images = [arrived] + [tp_shift(arrived, n_tp, d) for d in range(1, n_tp)]
     blocks = combine(tp_index, order, texts, images, gain_column)
 
-    held[3], sides[2], halves = tie(held[3], sides[2], halves)
+    first = jnp.concatenate([held[0], *sides[0]], axis=0)
+    second = jnp.concatenate([held[1], *sides[1]], axis=0)
+    held[3], sides[2], halves, first, second = tie(held[3], sides[2], halves, first, second)
     sides.append(to_sides(held[3]))
     corners = [jnp.concatenate(halves, axis=1)]
     corners.append(along_line(corners[0]))
@@ -273,15 +274,15 @@
         )
         return part if total is None else total + part
 
-    total = add_product(None, 0, [held[0], *sides[0], corners[0]])
-    total = add_product(total, 4, [held[1], *sides[1]])
+    total = add_product(None, 0, [first])
+    total = add_product(total, 3, [second])
 
     total, sides[-1] = tie(total, sides[-1])
     corners.append(jnp.concatenate(to_corner(*sides[-1]), axis=1))
     for step in range(2, lines - 1):
-        total = add_product(total, step * 3 + 1, [held[step], *sides[step]])
+        total = add_product(total, step * 3, [held[step], *sides[step]])
     total, late = tie(total, [held[-1], *sides[-1]])
-    total = add_product(total, lines * 3 - 2, late)
+    total = add_product(total, lines * 3 - 3, late)
 
     position = me * row_count + jnp.arange(row_count, dtype=jnp.int32)
     request_ids = jnp.arange(text_len.shape[0], dtype=jnp.int32)
@@ -292,7 +293,7 @@
         axis=1,
     )
     keep = lax.rem(position, SEQ) < limits
-    total = add_product(total, lines * 3 + 1, corners[1:])
+    total = add_product(total, lines * 3, corners)
     return jnp.where(keep[:, None], total, 0.0).astype(jnp.bfloat16)
 
 

time: 92.2 us -> 98.5 us (1.068)
  other arithmetic: 9.61 us -> 15.5 us
  starting transfers between devices: 29 us -> 26.9 us
  waiting for transfers between devices: 19.4 us -> 20.8 us
  local copies, waits for them, and re-layouts: 17.3 us -> 18.3 us
    concatenate x0 -> x2, other arithmetic: none -> 3.95 us  [the longest x1 2.63 us: shards(): second = jnp.concatenate([held[1], *sides[1]], axis=0)]
    ppermute x4, waiting for transfers between devices: 2.06 us -> 4.3 us  [to_sides(): lax.ppermute(block, 'req', x_perm)]
    concatenate x5 -> x3, other arithmetic: 8.44 us -> 10.3 us  [add_product(): weight = jnp.concatenate(weights, axis=0)]
    ppermute x3, starting transfers between devices: 3.63 us -> 2.6 us  [to_corner(): right = lax.ppermute(by_x[:, cut:], 'req', y_perm)]
  transfers between devices with their start and end apart: 23 -> 23, of which waited for: 6 -> 9; matrix products, arithmetic and copies ran while one was open for 30% -> 28% of each run, Pallas kernels for 6% -> 6%
where the time goes in v22:
time: 98.5 us; the launch traced here: 97.8 us
  starting transfers between devices  26.9 us (27%)
  waiting for transfers between devices  20.8 us (21%)
  local copies, waits for them, and re-layouts  18.3 us (19%)
  other arithmetic  15.5 us (16%)
  matrix products  10.5 us (11%)
  Pallas kernels  5.52 us (6%)
    ppermute x4, waiting for transfers between devices, along_line(): return lax.ppermute(block, 'req', line_perm)  10.7 us
    concatenate x3, other arithmetic, add_product(): weight = jnp.concatenate(weights, axis=0)  10.3 us
    dot_general x5, matrix products, add_product(): lax.dot_general(source, weight, (((0,), (0,)), ((), ())), preferred_eleme...  9.47 us
    unnamed x21, local copies, waits for them, and re-layouts  7.37 us
    ppermute x4, starting transfers between devices, along_line(): return lax.ppermute(block, 'req', line_perm)  6.65 us
    ppermute x4, starting transfers between devices, to_sides(): lax.ppermute(block, 'req', y_perm)  6.31 us
    ppermute x4, starting transfers between devices, to_sides(): lax.ppermute(block, 'req', x_perm)  4.63 us
    ppermute x4, waiting for transfers between devices, to_sides(): lax.ppermute(block, 'req', x_perm)  4.3 us
  transfers between devices with their start and end apart: 23, of which 9 were waited for; matrix products, arithmetic and copies ran while one was open for 28% of the time, Pallas kernels for 6%

profile of v22, /device:TPU:0, one launch (start us, length us, event | category | flops | bytes accessed | tf_op | source)
XLA Modules:
  0.0 97.8 jit_solution(5380526513483858627)
XLA Ops:
  0.0 3.0 %collective-permute-start.1 = (bf16[104,2496]{1,0:T(8,128)(2,1)}, bf16[104,2496]{1,0:T(8,128)(2,1)}, u32[]{:S(2)}, u32[]{:S(2)}) collective-permute-start(bf16[104,2496]{1,0:T(8,128)(2,1)} %param.16), channel_id=1, source_target_pairs={{0,8},{2,10},{4,12},{6,14},{8,24},{10,26},{12,28},{14,30},{16,0},{... | collective-permute-start | bytes 1557512 | tf_op jit(solution)/shard_map/ppermute | solution.py:192
  3.0 1.5 %collective-permute-start.2 = (bf16[104,2496]{1,0:T(8,128)(2,1)}, bf16[104,2496]{1,0:T(8,128)(2,1)S(1)}, u32[]{:S(2)}, u32[]{:S(2)}) collective-permute-start(bf16[104,2496]{1,0:T(8,128)(2,1)} %param.16), channel_id=1, source_target_pairs={{0,2},{2,0},{4,6},{6,4},{8,10},{10,8},{12,14},{14,12},{16,18},{18,... | collective-permute-start | bytes 1557512 | tf_op jit(solution)/shard_map/ppermute | solution.py:195
  4.5 1.5 %collective-permute-start.3 = (bf16[104,2496]{1,0:T(8,128)(2,1)}, bf16[104,2496]{1,0:T(8,128)(2,1)S(1)}, u32[]{:S(2)}, u32[]{:S(2)}) collective-permute-start(bf16[104,2496]{1,0:T(8,128)(2,1)} %param.16), channel_id=1, source_target_pairs={{0,4},{2,6},{4,0},{6,2},{8,12},{10,14},{12,8},{14,10},{16,20},{18,... | collective-permute-start | bytes 1557512 | tf_op jit(solution)/shard_map/ppermute | solution.py:195
  6.0 1.1 %copy-done.3 = bf16[448,832]{1,0:T(8,128)(2,1)S(1)} copy-done((bf16[448,832]{1,0:T(8,128)(2,1)S(1)}, bf16[448,832]{1,0:T(8,128)(2,1)}, u32[]{:S(2)}) %copy-start.3) | copy-done | bytes 745496
  7.2 0.8 shard_map.118
  8.0 0.7 convert_bitcast_fusion.1
  8.7 0.7 stack.22
  9.4 0.7 stack.21
  10.1 0.2 convert_reduce_fusion
  10.3 4.1 %copy-done = bf16[4,832,1664]{2,1,0:T(8,128)(2,1)S(1)} copy-done((bf16[4,832,1664]{2,1,0:T(8,128)(2,1)S(1)}, bf16[4,832,1664]{2,1,0:T(8,128)(2,1)}, u32[]{:S(2)}) %copy-start) | copy-done | bytes 11075608
  14.5 2.9 %shard_map.119 = f32[112,1664]{1,0:T(8,128)S(1)} custom-call(bf16[4,112,832]{2,1,0:T(8,128)(2,1)S(1)} %get-tuple-element.49.picked_ref, bf16[2,832]{1,0:T(2,128)(2,1)S(1)} %pad_maximum_fusion.4.gain_bias_ref, f32[4,112,256]{2,1,0:T(8,128)S(1)} %get-tuple-element.50.refs_0_, f32[4,112,256]{2,1,0:T(8,128)S(1)} %collective-permute-done.refs_1_, ...), custom_call_target="tpu_custom_call" | custom-call | flops 1000 | bytes 1000 | tf_op jit(solution)/shard_map/pallas_call | solution.py:116
  17.4 0.6 collective-permute-done.3
  18.0 0.9 constant_dynamic-slice_fusion
  18.9 0.1 pad.14.clone
  19.0 2.6 %collective-permute-start.4 = (bf16[104,2496]{1,0:T(8,128)(2,1)}, bf16[104,2496]{1,0:T(8,128)(2,1)}, u32[]{:S(2)}, u32[]{:S(2)}) collective-permute-start(bf16[104,2496]{1,0:T(8,128)(2,1)} %collective-permute-done.1), channel_id=1, source_target_pairs={{0,8},{2,10},{4,12},{6,14},{8,24},{10,26},{12,28},{14,30},{16,0},{... | collective-permute-start | bytes 1557512 | tf_op jit(solution)/shard_map/ppermute | solution.py:192
  21.6 0.5 collective-permute-start.5
  22.1 1.5 %collective-permute-start.6 = (bf16[104,2496]{1,0:T(8,128)(2,1)}, bf16[104,2496]{1,0:T(8,128)(2,1)}, u32[]{:S(2)}, u32[]{:S(2)}) collective-permute-start(bf16[104,2496]{1,0:T(8,128)(2,1)} %collective-permute-done.1), channel_id=1, source_target_pairs={{0,4},{2,6},{4,0},{6,2},{8,12},{10,14},{12,8},{14,10},{16,20},{18,... | collective-permute-start | bytes 1557512 | tf_op jit(solution)/shard_map/ppermute | solution.py:195
  23.7 0.1 copy.18
  23.8 0.2 add_convert_fusion
  24.0 0.7 slice.33
  24.7 1.5 %collective-permute-start.11 = (bf16[104,1280]{1,0:T(8,128)(2,1)}, bf16[104,1280]{1,0:T(8,128)(2,1)}, u32[]{:S(2)}, u32[]{:S(2)}) collective-permute-start(bf16[104,1280]{1,0:T(8,128)(2,1)} %slice.33), channel_id=1, source_target_pairs={{0,2},{2,0},{4,6},{6,4},{8,10},{10,8},{12,14},{14,12},{16,18},{18,... | collective-permute-start | bytes 798728 | tf_op jit(solution)/shard_map/ppermute | solution.py:198
  26.2 0.7 slice.34
  26.9 0.5 collective-permute-start.12
  27.4 1.1 %convolution_convert_fusion = bf16[256,896]{1,0:T(8,128)(2,1)} fusion(bf16[112,2]{1,0:T(8,128)(2,1)S(1)} %copy.18, bf16[112,832]{1,0:T(8,128)(2,1)S(1)} %add_convert_fusion, bf16[896]{0:T(1024)(128)(2,1)S(1)} %pad.14.clone, s32[112]{0:T(128)S(1)} %multiply_add_fusion), kind=kOutput, calls=%fused_computation.9 | convolution fusion | flops 52240384 | bytes 647808 | tf_op jit(solution)/shard_map/dot_general | solution.py:238
  28.5 3.6 %all-to-all-start = ((bf16[16,16,896]{2,1,0:T(8,128)(2,1)}), bf16[16,16,896]{2,1,0:T(8,128)(2,1)S(1)}, u32[]{:S(2)}, u32[]{:S(2)}) async-start(bf16[16,16,896]{2,1,0:T(8,128)(2,1)} %bitcast.5), calls=%async_computation | async-start | bytes 917504 | tf_op jit(solution)/shard_map/all_to_all | solution.py:239
  32.1 1.3 %pad_maximum_fusion = bf16[312,2496]{1,0:T(8,128)(2,1)} fusion(bf16[104,2496]{1,0:T(8,128)(2,1)S(1)} %collective-permute-done.3, bf16[104,2496]{1,0:T(8,128)(2,1)S(1)} %collective-permute-done.2, bf16[104,2496]{1,0:T(8,128)(2,1)S(1)} %copy-done.7), kind=kLoop, calls=%fused_computation.5 | loop fusion | flops 4672512 | bytes 3115008 | tf_op jit(solution)/shard_map/concatenate | solution.py:251
  33.4 1.4 %collective-permute-done.4 = bf16[104,2496]{1,0:T(8,128)(2,1)} collective-permute-done((bf16[104,2496]{1,0:T(8,128)(2,1)}, bf16[104,2496]{1,0:T(8,128)(2,1)}, u32[]{:S(2)}, u32[]{:S(2)}) %collective-permute-start.4) | collective-permute-done | bytes 519200 | tf_op jit(solution)/shard_map/ppermute | solution.py:192
  34.8 2.6 %collective-permute-done.5 = bf16[104,2496]{1,0:T(8,128)(2,1)} collective-permute-done((bf16[104,2496]{1,0:T(8,128)(2,1)}, bf16[104,2496]{1,0:T(8,128)(2,1)}, u32[]{:S(2)}, u32[]{:S(2)}) %collective-permute-start.5) | collective-permute-done | bytes 519200 | tf_op jit(solution)/shard_map/ppermute | solution.py:195
  37.5 2.2 %collective-permute-done.6 = bf16[104,2496]{1,0:T(8,128)(2,1)} collective-permute-done((bf16[104,2496]{1,0:T(8,128)(2,1)}, bf16[104,2496]{1,0:T(8,128)(2,1)}, u32[]{:S(2)}, u32[]{:S(2)}) %collective-permute-start.6) | collective-permute-done | bytes 519200 | tf_op jit(solution)/shard_map/ppermute | solution.py:195
  39.7 1.1 %collective-permute-start.8 = (bf16[104,2496]{1,0:T(8,128)(2,1)}, bf16[104,2496]{1,0:T(8,128)(2,1)S(1)}, u32[]{:S(2)}, u32[]{:S(2)}) collective-permute-start(bf16[104,2496]{1,0:T(8,128)(2,1)} %collective-permute-done.4), channel_id=1, source_target_pairs={{0,2},{2,0},{4,6},{6,4},{8,10},{10,8},{12,14},{14,12},{16,18},{18,... | collective-permute-start | bytes 1557512 | tf_op jit(solution)/shard_map/ppermute | solution.py:195
  40.8 1.8 %collective-permute-start.9 = (bf16[104,2496]{1,0:T(8,128)(2,1)}, bf16[104,2496]{1,0:T(8,128)(2,1)}, u32[]{:S(2)}, u32[]{:S(2)}) collective-permute-start(bf16[104,2496]{1,0:T(8,128)(2,1)} %collective-permute-done.4), channel_id=1, source_target_pairs={{0,4},{2,6},{4,0},{6,2},{8,12},{10,14},{12,8},{14,10},{16,20},{18,... | collective-permute-start | bytes 1557512 | tf_op jit(solution)/shard_map/ppermute | solution.py:195
  42.5 2.6 %pad_maximum_fusion.1 = bf16[312,2496]{1,0:T(8,128)(2,1)} fusion(bf16[104,2496]{1,0:T(8,128)(2,1)} %collective-permute-done.6, bf16[104,2496]{1,0:T(8,128)(2,1)} %collective-permute-done.5, bf16[104,2496]{1,0:T(8,128)(2,1)} %collective-permute-done.1), kind=kLoop, calls=%fused_computation.6 | loop fusion | flops 4672512 | bytes 3115008 | tf_op jit(solution)/shard_map/concatenate | solution.py:252
  45.2 0.1 fusion.7
  45.3 0.7 fusion.10.order_ref
  46.0 0.8 reshape.62.gain_ref
  46.8 0.3 collective-permute-done.12
  47.1 9.3 %collective-permute-done.7 = bf16[104,2496]{1,0:T(8,128)(2,1)} collective-permute-done((bf16[104,2496]{1,0:T(8,128)(2,1)}, bf16[104,2496]{1,0:T(8,128)(2,1)}, u32[]{:S(2)}, u32[]{:S(2)}) %collective-permute-start.7) | collective-permute-done | bytes 519200 | tf_op jit(solution)/shard_map/ppermute | solution.py:192
  56.4 1.7 %collective-permute-done.8 = bf16[104,2496]{1,0:T(8,128)(2,1)S(1)} collective-permute-done((bf16[104,2496]{1,0:T(8,128)(2,1)}, bf16[104,2496]{1,0:T(8,128)(2,1)S(1)}, u32[]{:S(2)}, u32[]{:S(2)}) %collective-permute-start.8) | collective-permute-done | bytes 519200 | tf_op jit(solution)/shard_map/ppermute | solution.py:195
  58.1 0.4 collective-permute-done.9
  58.4 1.5 %collective-permute-start.18 = (bf16[104,2496]{1,0:T(8,128)(2,1)}, bf16[104,2496]{1,0:T(8,128)(2,1)}, u32[]{:S(2)}, u32[]{:S(2)}) collective-permute-start(bf16[104,2496]{1,0:T(8,128)(2,1)} %collective-permute-done.7), channel_id=1, source_target_pairs={{0,2},{2,0},{4,6},{6,4},{8,10},{10,8},{12,14},{14,12},{16,18},{18,... | collective-permute-start | bytes 1557512 | tf_op jit(solution)/shard_map/ppermute | solution.py:195
  59.9 1.5 %collective-permute-start.19 = (bf16[104,2496]{1,0:T(8,128)(2,1)}, bf16[104,2496]{1,0:T(8,128)(2,1)}, u32[]{:S(2)}, u32[]{:S(2)}) collective-permute-start(bf16[104,2496]{1,0:T(8,128)(2,1)} %collective-permute-done.7), channel_id=1, source_target_pairs={{0,4},{2,6},{4,0},{6,2},{8,12},{10,14},{12,8},{14,10},{16,20},{18,... | collective-permute-start | bytes 1557512 | tf_op jit(solution)/shard_map/ppermute | solution.py:195
  61.4 0.7 slice.36
  62.2 0.5 collective-permute-start.15
  62.7 1.7 %constant_dynamic-update-slice_fusion.1 = bf16[104,2496]{1,0:T(8,128)(2,1)} fusion(bf16[104,1280]{1,0:T(8,128)(2,1)} %collective-permute-done.11), kind=kLoop, calls=%fused_computation.23 | loop fusion | bytes 532480
  64.4 1.7 %constant_dynamic-update-slice_fusion = bf16[104,2496]{1,0:T(8,128)(2,1)} fusion(bf16[104,2496]{1,0:T(8,128)(2,1)} %constant_dynamic-update-slice_fusion.1, bf16[104,1216]{1,0:T(8,128)(2,1)} %collective-permute-done.12), kind=kLoop, calls=%fused_computation.22 | loop fusion | bytes 532480 | tf_op jit(solution)/shard_map/concatenate | solution.py:255
  66.0 1.0 %slice.35 = bf16[104,1280]{1,0:T(8,128)(2,1)S(1)} slice(bf16[104,2496]{1,0:T(8,128)(2,1)} %collective-permute-done.9), slice={[0:104], [0:1280]} | slice | bytes 532480 | tf_op jit(solution)/shard_map/slice | solution.py:198
  67.1 1.3 %pad_maximum_fusion.2 = bf16[312,2496]{1,0:T(8,128)(2,1)S(1)} fusion(bf16[104,2496]{1,0:T(8,128)(2,1)} %collective-permute-done.9, bf16[104,2496]{1,0:T(8,128)(2,1)S(1)} %collective-permute-done.8, bf16[104,2496]{1,0:T(8,128)(2,1)} %collective-permute-done.4), kind=kLoop, calls=%fused_computation.7 | loop fusion | flops 4672512 | bytes 3115008 | tf_op jit(solution)/shard_map/concatenate | solution.py:265
  68.4 0.6 collective-permute-start.14
  69.0 1.0 %collective-permute-start.13 = (bf16[104,2496]{1,0:T(8,128)(2,1)S(1)}, bf16[104,2496]{1,0:T(8,128)(2,1)S(1)}, u32[]{:S(2)}, u32[]{:S(2)}) collective-permute-start(bf16[104,2496]{1,0:T(8,128)(2,1)S(1)} %copy-done.6), channel_id=1, source_target_pairs={{0,8},{2,10},{4,12},{6,14},{8,24},{10,26},{12,28},{14,30},{16,0},{... | collective-permute-start | bytes 1557512 | tf_op jit(solution)/shard_map/ppermute | solution.py:192
  70.0 1.9 %shard_map.120 = bf16[16,104,512]{2,1,0:T(8,128)(2,1)S(1)} custom-call(s32[1]{0:T(128)} %bitcast.2.index_ref, s32[16]{0:T(128)S(1)} %fusion.10.order_ref, bf16[16,104,1]{2,1,0:T(8,128)(2,1)S(1)} %reshape.62.gain_ref, bf16[832,512]{1,0:T(8,128)(2,1)S(1)} %bitcast.29, bf16[832,512]{1,0:T(8,128)(2,1)S(1)} %collective-permute-done.16.refs_1_, ...), custom_call_target="tpu_custom_call" | custom-call | flops 1000 | bytes 1000 | tf_op jit(solution)/shard_map/pallas_call | solution.py:167
  71.9 0.1 fusion.14
  72.0 1.5 %fusion.15 = f32[512,2496]{0,1:T(8,128)S(1)} fusion(bf16[312,512]{1,0:T(8,128)(2,1)S(1)} %bitcast.30, bf16[312,2496]{1,0:T(8,128)(2,1)S(1)} %copy-done.5), kind=kOutput, calls=%fused_computation.48 | convolution fusion | flops 797442048 | bytes 6988800 | tf_op jit(solution)/shard_map/dot_general | solution.py:272
  73.6 0.4 copy-done.4
  74.0 1.5 %convolution_add_fusion.2 = f32[512,2496]{0,1:T(8,128)S(1)} fusion(f32[512,2496]{0,1:T(8,128)S(1)} %fusion.15, bf16[312,512]{1,0:T(8,128)(2,1)S(1)} %bitcast.33, bf16[312,2496]{1,0:T(8,128)(2,1)S(1)} %copy-done.4), kind=kOutput, calls=%fused_computation.3 | convolution fusion | flops 798720000 | bytes 12100608 | tf_op jit(solution)/shard_map/dot_general | solution.py:272
  75.5 1.0 slice.40
  76.5 1.6 %collective-permute-start.21 = (bf16[104,1216]{1,0:T(8,128)(2,1)S(1)}, bf16[104,1216]{1,0:T(8,128)(2,1)S(1)}, u32[]{:S(2)}, u32[]{:S(2)}) collective-permute-start(bf16[104,1216]{1,0:T(8,128)(2,1)S(1)} %slice.40), channel_id=1, source_target_pairs={{0,4},{2,6},{4,0},{6,2},{8,12},{10,14},{12,8},{14,10},{16,20},{18,... | collective-permute-start | bytes 758792 | tf_op jit(solution)/shard_map/ppermute | solution.py:199
  78.1 1.0 slice.39
  79.1 1.0 collective-permute-start.20
  80.0 1.6 %convolution_add_fusion.1 = f32[512,2496]{0,1:T(8,128)S(1)} fusion(f32[512,2496]{0,1:T(8,128)S(1)} %convolution_add_fusion.2, bf16[312,512]{1,0:T(8,128)(2,1)S(1)} %bitcast.32, bf16[312,2496]{1,0:T(8,128)(2,1)S(1)} %pad_maximum_fusion.2), kind=kOutput, calls=%fused_computation.2 | convolution fusion | flops 798720000 | bytes 12100608 | tf_op jit(solution)/shard_map/dot_general | solution.py:272
  81.7 1.5 %pad_maximum_fusion.3 = bf16[312,2496]{1,0:T(8,128)(2,1)S(1)} fusion(bf16[104,2496]{1,0:T(8,128)(2,1)} %collective-permute-done.19, bf16[104,2496]{1,0:T(8,128)(2,1)} %collective-permute-done.18, bf16[104,2496]{1,0:T(8,128)(2,1)} %collective-permute-done.7), kind=kLoop, calls=%fused_computation.8 | loop fusion | flops 4672512 | bytes 3115008 | tf_op jit(solution)/shard_map/concatenate | solution.py:265
  83.2 1.6 %convolution_add_fusion = f32[512,2496]{0,1:T(8,128)S(1)} fusion(f32[512,2496]{0,1:T(8,128)S(1)} %convolution_add_fusion.1, bf16[312,512]{1,0:T(8,128)(2,1)S(1)} %bitcast.31, bf16[312,2496]{1,0:T(8,128)(2,1)S(1)} %pad_maximum_fusion.3), kind=kOutput, calls=%fused_computation.1 | convolution fusion | flops 798720000 | bytes 12100608 | tf_op jit(solution)/shard_map/dot_general | solution.py:272
  84.8 2.3 %collective-permute-done.20 = bf16[104,1280]{1,0:T(8,128)(2,1)S(1)} collective-permute-done((bf16[104,1280]{1,0:T(8,128)(2,1)S(1)}, bf16[104,1280]{1,0:T(8,128)(2,1)S(1)}, u32[]{:S(2)}, u32[]{:S(2)}) %collective-permute-start.20) | collective-permute-done | bytes 266272 | tf_op jit(solution)/shard_map/ppermute | solution.py:198
  87.1 7.5 %maximum_maximum_fusion = bf16[416,2496]{1,0:T(8,128)(2,1)S(1)} fusion(bf16[104,1216]{1,0:T(8,128)(2,1)S(1)} %collective-permute-done.21, bf16[104,1280]{1,0:T(8,128)(2,1)S(1)} %collective-permute-done.20, bf16[104,1216]{1,0:T(8,128)(2,1)S(1)} %collective-permute-done.15, bf16[104,1280]{1,0:T(8,128)(2,1)S(1)} %collective-permute-done.14, ...), kind=kLoop, calls=%fused_computation.4 | loop fusion | flops 12460032 | bytes 4153344 | tf_op jit(solution)/shard_map/concatenate | solution.py:265
  94.6 3.2 %select_convert_fusion = bf16[512,2496]{0,1:T(8,128)(2,1)} fusion(f32[512,2496]{0,1:T(8,128)S(1)} %convolution_add_fusion, bf16[416,512]{1,0:T(8,128)(2,1)S(1)} %bitcast.25, bf16[416,2496]{1,0:T(8,128)(2,1)S(1)} %maximum_maximum_fusion, pred[512]{0:T(512)(128)(4,1)S(1)} %fusion.8), kind=kOutput, calls=%fused_computation | convolution fusion | flops 1067089920 | bytes 10170880 | tf_op jit(solution)/shard_map/dot_general | solution.py:272
  (45 shorter events, 0.2 us)
Async XLA Ops:
  0.0 17.4 %collective-permute-start.1 = (bf16[104,2496]{1,0:T(8,128)(2,1)}, bf16[104,2496]{1,0:T(8,128)(2,1)}, u32[]{:S(2)}, u32[]{:S(2)}) collective-permute-start(bf16[104,2496]{1,0:T(8,128)(2,1)} %param.16), channel_id=1, source_target_pairs={{0,8},{2,10},{4,12},{6,14},{8,24},{10,26},{12,28},{14,30},{16,0},{... | collective-permute-start | bytes 1557512 | tf_op jit(solution)/shard_map/ppermute | solution.py:192
  3.0 14.4 %collective-permute-start.2 = (bf16[104,2496]{1,0:T(8,128)(2,1)}, bf16[104,2496]{1,0:T(8,128)(2,1)S(1)}, u32[]{:S(2)}, u32[]{:S(2)}) collective-permute-start(bf16[104,2496]{1,0:T(8,128)(2,1)} %param.16), channel_id=1, source_target_pairs={{0,2},{2,0},{4,6},{6,4},{8,10},{10,8},{12,14},{14,12},{16,18},{18,... | collective-permute-start | bytes 1557512 | tf_op jit(solution)/shard_map/ppermute | solution.py:195
  4.5 13.5 %collective-permute-start.3 = (bf16[104,2496]{1,0:T(8,128)(2,1)}, bf16[104,2496]{1,0:T(8,128)(2,1)S(1)}, u32[]{:S(2)}, u32[]{:S(2)}) collective-permute-start(bf16[104,2496]{1,0:T(8,128)(2,1)} %param.16), channel_id=1, source_target_pairs={{0,4},{2,6},{4,0},{6,2},{8,12},{10,14},{12,8},{14,10},{16,20},{18,... | collective-permute-start | bytes 1557512 | tf_op jit(solution)/shard_map/ppermute | solution.py:195
  6.0 1.1 %copy-start.3 = (bf16[448,832]{1,0:T(8,128)(2,1)S(1)}, bf16[448,832]{1,0:T(8,128)(2,1)}, u32[]{:S(2)}) copy-start(bf16[448,832]{1,0:T(8,128)(2,1)} %patches_ref.1) | copy-start | bytes 2236420
  7.9 2.4 %collective-permute-start = (f32[4,112,256]{2,1,0:T(8,128)S(1)}, f32[4,112,256]{2,1,0:T(8,128)S(1)}, u32[]{:S(2)}, u32[]{:S(2)}) collective-permute-start(f32[4,112,256]{2,1,0:T(8,128)S(1)} %get-tuple-element.50.refs_0_), channel_id=1, source_target_pairs={{0,1},{1,0},{2,3},{3,2},{4,5},{5,4},{6,7},{7,6},{8,9},{9,8},{10,11... | collective-permute-start | bytes 1376264 | tf_op jit(solution)/shard_map/ppermute | solution.py:26
  10.3 4.1 %copy-start = (bf16[4,832,1664]{2,1,0:T(8,128)(2,1)S(1)}, bf16[4,832,1664]{2,1,0:T(8,128)(2,1)}, u32[]{:S(2)}) copy-start(bf16[4,832,1664]{2,1,0:T(8,128)(2,1)} %refs_2_.1) | copy-start | bytes 33226756
  17.4 14.7 %copy-start.7 = (bf16[104,2496]{1,0:T(8,128)(2,1)S(1)}, bf16[104,2496]{1,0:T(8,128)(2,1)}, u32[]{:S(2)}) copy-start(bf16[104,2496]{1,0:T(8,128)(2,1)} %param.16) | copy-start | bytes 1557508
  18.9 4.9 %collective-permute-start.10 = (f32[112,832]{1,0:T(8,128)}, f32[112,832]{1,0:T(8,128)S(1)}, u32[]{:S(2)}, u32[]{:S(2)}) collective-permute-start(f32[112,832]{1,0:T(8,128)} %constant_dynamic-slice_fusion), channel_id=1, source_target_pairs={{0,1},{1,0},{2,3},{3,2},{4,5},{5,4},{6,7},{7,6},{8,9},{9,8},{10,11... | collective-permute-start | bytes 1118216 | tf_op jit(solution)/shard_map/ppermute | solution.py:26
  19.0 15.8 %collective-permute-start.4 = (bf16[104,2496]{1,0:T(8,128)(2,1)}, bf16[104,2496]{1,0:T(8,128)(2,1)}, u32[]{:S(2)}, u32[]{:S(2)}) collective-permute-start(bf16[104,2496]{1,0:T(8,128)(2,1)} %collective-permute-done.1), channel_id=1, source_target_pairs={{0,8},{2,10},{4,12},{6,14},{8,24},{10,26},{12,28},{14,30},{16,0},{... | collective-permute-start | bytes 1557512 | tf_op jit(solution)/shard_map/ppermute | solution.py:192
  21.6 15.9 %collective-permute-start.5 = (bf16[104,2496]{1,0:T(8,128)(2,1)}, bf16[104,2496]{1,0:T(8,128)(2,1)}, u32[]{:S(2)}, u32[]{:S(2)}) collective-permute-start(bf16[104,2496]{1,0:T(8,128)(2,1)} %collective-permute-done.1), channel_id=1, source_target_pairs={{0,2},{2,0},{4,6},{6,4},{8,10},{10,8},{12,14},{14,12},{16,18},{18,... | collective-permute-start | bytes 1557512 | tf_op jit(solution)/shard_map/ppermute | solution.py:195
  22.1 17.5 %collective-permute-start.6 = (bf16[104,2496]{1,0:T(8,128)(2,1)}, bf16[104,2496]{1,0:T(8,128)(2,1)}, u32[]{:S(2)}, u32[]{:S(2)}) collective-permute-start(bf16[104,2496]{1,0:T(8,128)(2,1)} %collective-permute-done.1), channel_id=1, source_target_pairs={{0,4},{2,6},{4,0},{6,2},{8,12},{10,14},{12,8},{14,10},{16,20},{18,... | collective-permute-start | bytes 1557512 | tf_op jit(solution)/shard_map/ppermute | solution.py:195
  24.7 22.4 %collective-permute-start.11 = (bf16[104,1280]{1,0:T(8,128)(2,1)}, bf16[104,1280]{1,0:T(8,128)(2,1)}, u32[]{:S(2)}, u32[]{:S(2)}) collective-permute-start(bf16[104,1280]{1,0:T(8,128)(2,1)} %slice.33), channel_id=1, source_target_pairs={{0,2},{2,0},{4,6},{6,4},{8,10},{10,8},{12,14},{14,12},{16,18},{18,... | collective-permute-start | bytes 798728 | tf_op jit(solution)/shard_map/ppermute | solution.py:198
  26.9 20.2 %collective-permute-start.12 = (bf16[104,1216]{1,0:T(8,128)(2,1)}, bf16[104,1216]{1,0:T(8,128)(2,1)}, u32[]{:S(2)}, u32[]{:S(2)}) collective-permute-start(bf16[104,1216]{1,0:T(8,128)(2,1)} %slice.34), channel_id=1, source_target_pairs={{0,4},{2,6},{4,0},{6,2},{8,12},{10,14},{12,8},{14,10},{16,20},{18,... | collective-permute-start | bytes 758792 | tf_op jit(solution)/shard_map/ppermute | solution.py:199
  28.5 35.9 %all-to-all-start = ((bf16[16,16,896]{2,1,0:T(8,128)(2,1)}), bf16[16,16,896]{2,1,0:T(8,128)(2,1)S(1)}, u32[]{:S(2)}, u32[]{:S(2)}) async-start(bf16[16,16,896]{2,1,0:T(8,128)(2,1)} %bitcast.5), calls=%async_computation | async-start | bytes 917504 | tf_op jit(solution)/shard_map/all_to_all | solution.py:239
  32.1 13.1 %copy-start.9 = (s32[2]{0:T(128)S(1)}, s32[2]{0:T(128)}, u32[]{:S(2)}) copy-start(s32[2]{0:T(128)} %param.18) | copy-start | bytes 28
  32.1 13.9 %copy-start.8 = (bf16[1664]{0:T(1024)(128)(2,1)S(1)}, bf16[1664]{0:T(1024)(128)(2,1)}, u32[]{:S(2)}) copy-start(bf16[1664]{0:T(1024)(128)(2,1)} %param.15) | copy-start | bytes 9988
  32.1 15.0 %copy-start.2 = (bf16[512,832]{0,1:T(8,128)(2,1)S(1)}, bf16[512,832]{0,1:T(8,128)(2,1)}, u32[]{:S(2)}) copy-start(bf16[512,832]{0,1:T(8,128)(2,1)} %param.14) | copy-start | bytes 2555908
  39.7 18.4 %collective-permute-start.8 = (bf16[104,2496]{1,0:T(8,128)(2,1)}, bf16[104,2496]{1,0:T(8,128)(2,1)S(1)}, u32[]{:S(2)}, u32[]{:S(2)}) collective-permute-start(bf16[104,2496]{1,0:T(8,128)(2,1)} %collective-permute-done.4), channel_id=1, source_target_pairs={{0,2},{2,0},{4,6},{6,4},{8,10},{10,8},{12,14},{14,12},{16,18},{18,... | collective-permute-start | bytes 1557512 | tf_op jit(solution)/shard_map/ppermute | solution.py:195
  40.8 17.6 %collective-permute-start.9 = (bf16[104,2496]{1,0:T(8,128)(2,1)}, bf16[104,2496]{1,0:T(8,128)(2,1)}, u32[]{:S(2)}, u32[]{:S(2)}) collective-permute-start(bf16[104,2496]{1,0:T(8,128)(2,1)} %collective-permute-done.4), channel_id=1, source_target_pairs={{0,4},{2,6},{4,0},{6,2},{8,12},{10,14},{12,8},{14,10},{16,20},{18,... | collective-permute-start | bytes 1557512 | tf_op jit(solution)/shard_map/ppermute | solution.py:195
  45.2 11.2 %collective-permute-start.7 = (bf16[104,2496]{1,0:T(8,128)(2,1)}, bf16[104,2496]{1,0:T(8,128)(2,1)}, u32[]{:S(2)}, u32[]{:S(2)}) collective-permute-start(bf16[104,2496]{1,0:T(8,128)(2,1)} %collective-permute-done.4), channel_id=1, source_target_pairs={{0,8},{2,10},{4,12},{6,14},{8,24},{10,26},{12,28},{14,30},{16,0},{... | collective-permute-start | bytes 1557512 | tf_op jit(solution)/shard_map/ppermute | solution.py:192
  47.1 21.3 %collective-permute-start.16 = (bf16[832,512]{1,0:T(8,128)(2,1)S(1)}, bf16[832,512]{1,0:T(8,128)(2,1)S(1)}, u32[]{:S(2)}, u32[]{:S(2)}) collective-permute-start(bf16[832,512]{1,0:T(8,128)(2,1)S(1)} %bitcast.28), channel_id=1, source_target_pairs={{0,1},{1,0},{2,3},{3,2},{4,5},{5,4},{6,7},{7,6},{8,9},{9,8},{10,11... | collective-permute-start | bytes 2555912 | tf_op jit(solution)/shard_map/ppermute | solution.py:26
  58.4 17.1 %collective-permute-start.18 = (bf16[104,2496]{1,0:T(8,128)(2,1)}, bf16[104,2496]{1,0:T(8,128)(2,1)}, u32[]{:S(2)}, u32[]{:S(2)}) collective-permute-start(bf16[104,2496]{1,0:T(8,128)(2,1)} %collective-permute-done.7), channel_id=1, source_target_pairs={{0,2},{2,0},{4,6},{6,4},{8,10},{10,8},{12,14},{14,12},{16,18},{18,... | collective-permute-start | bytes 1557512 | tf_op jit(solution)/shard_map/ppermute | solution.py:195
  59.9 15.6 %collective-permute-start.19 = (bf16[104,2496]{1,0:T(8,128)(2,1)}, bf16[104,2496]{1,0:T(8,128)(2,1)}, u32[]{:S(2)}, u32[]{:S(2)}) collective-permute-start(bf16[104,2496]{1,0:T(8,128)(2,1)} %collective-permute-done.7), channel_id=1, source_target_pairs={{0,4},{2,6},{4,0},{6,2},{8,12},{10,14},{12,8},{14,10},{16,20},{18,... | collective-permute-start | bytes 1557512 | tf_op jit(solution)/shard_map/ppermute | solution.py:195
  62.2 22.6 %collective-permute-start.15 = (bf16[104,1216]{1,0:T(8,128)(2,1)}, bf16[104,1216]{1,0:T(8,128)(2,1)S(1)}, u32[]{:S(2)}, u32[]{:S(2)}) collective-permute-start(bf16[104,1216]{1,0:T(8,128)(2,1)} %slice.36), channel_id=1, source_target_pairs={{0,4},{2,6},{4,0},{6,2},{8,12},{10,14},{12,8},{14,10},{16,20},{18,... | collective-permute-start | bytes 758792 | tf_op jit(solution)/shard_map/ppermute | solution.py:199
  64.3 4.7 %collective-permute-start.17 = (bf16[256,896]{1,0:T(8,128)(2,1)S(1)}, bf16[256,896]{1,0:T(8,128)(2,1)S(1)}, u32[]{:S(2)}, u32[]{:S(2)}) collective-permute-start(bf16[256,896]{1,0:T(8,128)(2,1)S(1)} %bitcast.26), channel_id=1, source_target_pairs={{0,1},{1,0},{2,3},{3,2},{4,5},{5,4},{6,7},{7,6},{8,9},{9,8},{10,11... | collective-permute-start | bytes 1376264 | tf_op jit(solution)/shard_map/ppermute | solution.py:26
  66.0 3.0 %copy-start.6 = (bf16[104,2496]{1,0:T(8,128)(2,1)S(1)}, bf16[104,2496]{1,0:T(8,128)(2,1)}, u32[]{:S(2)}) copy-start(bf16[104,2496]{1,0:T(8,128)(2,1)} %constant_dynamic-update-slice_fusion) | copy-start | bytes 1557508
  68.4 16.4 %collective-permute-start.14 = (bf16[104,1280]{1,0:T(8,128)(2,1)S(1)}, bf16[104,1280]{1,0:T(8,128)(2,1)S(1)}, u32[]{:S(2)}, u32[]{:S(2)}) collective-permute-start(bf16[104,1280]{1,0:T(8,128)(2,1)S(1)} %slice.35), channel_id=1, source_target_pairs={{0,2},{2,0},{4,6},{6,4},{8,10},{10,8},{12,14},{14,12},{16,18},{18,... | collective-permute-start | bytes 798728 | tf_op jit(solution)/shard_map/ppermute | solution.py:198
  69.0 15.8 %collective-permute-start.13 = (bf16[104,2496]{1,0:T(8,128)(2,1)S(1)}, bf16[104,2496]{1,0:T(8,128)(2,1)S(1)}, u32[]{:S(2)}, u32[]{:S(2)}) collective-permute-start(bf16[104,2496]{1,0:T(8,128)(2,1)S(1)} %copy-done.6), channel_id=1, source_target_pairs={{0,8},{2,10},{4,12},{6,14},{8,24},{10,26},{12,28},{14,30},{16,0},{... | collective-permute-start | bytes 1557512 | tf_op jit(solution)/shard_map/ppermute | solution.py:192
  70.0 2.0 %copy-start.5 = (bf16[312,2496]{1,0:T(8,128)(2,1)S(1)}, bf16[312,2496]{1,0:T(8,128)(2,1)}, u32[]{:S(2)}) copy-start(bf16[312,2496]{1,0:T(8,128)(2,1)} %pad_maximum_fusion) | copy-start | bytes 4672516
  71.9 12.9 %copy-start.1 = (bf16[16,104,512]{2,1,0:T(8,128)(2,1)}, bf16[16,104,512]{2,1,0:T(8,128)(2,1)S(1)}, u32[]{:S(2)}) copy-start(bf16[16,104,512]{2,1,0:T(8,128)(2,1)S(1)} %shard_map.120) | copy-start | bytes 5111812
  72.0 1.9 %copy-start.4 = (bf16[312,2496]{1,0:T(8,128)(2,1)S(1)}, bf16[312,2496]{1,0:T(8,128)(2,1)}, u32[]{:S(2)}) copy-start(bf16[312,2496]{1,0:T(8,128)(2,1)} %pad_maximum_fusion.1) | copy-start | bytes 4672516
  76.5 8.3 %collective-permute-start.21 = (bf16[104,1216]{1,0:T(8,128)(2,1)S(1)}, bf16[104,1216]{1,0:T(8,128)(2,1)S(1)}, u32[]{:S(2)}, u32[]{:S(2)}) collective-permute-start(bf16[104,1216]{1,0:T(8,128)(2,1)S(1)} %slice.40), channel_id=1, source_target_pairs={{0,4},{2,6},{4,0},{6,2},{8,12},{10,14},{12,8},{14,10},{16,20},{18,... | collective-permute-start | bytes 758792 | tf_op jit(solution)/shard_map/ppermute | solution.py:199
  79.1 8.0 %collective-permute-start.20 = (bf16[104,1280]{1,0:T(8,128)(2,1)S(1)}, bf16[104,1280]{1,0:T(8,128)(2,1)S(1)}, u32[]{:S(2)}, u32[]{:S(2)}) collective-permute-start(bf16[104,1280]{1,0:T(8,128)(2,1)S(1)} %slice.39), channel_id=1, source_target_pairs={{0,2},{2,0},{4,6},{6,4},{8,10},{10,8},{12,14},{14,12},{16,18},{18,... | collective-permute-start | bytes 798728 | tf_op jit(solution)/shard_map/ppermute | solution.py:198
  84.8 9.8 %slice-start = ((bf16[16,104,512]{2,1,0:T(8,128)(2,1)}), bf16[4,104,512]{2,1,0:T(8,128)(2,1)S(1)}, s32[]{:S(2)}) async-start(bf16[16,104,512]{2,1,0:T(8,128)(2,1)} %copy-done.1), calls=%async_computation.1 | async-start | bytes 851968 | tf_op jit(solution)/shard_map/slice | solution.py:267

commit v23 on v20

--- a/solution.py
+++ b/solution.py
@@ -24,16 +24,6 @@
 
 def tp_shift(value, n_tp, distance):
     return lax.ppermute(value, "tp", [(i, (i + distance) % n_tp) for i in range(n_tp)])
-
-
-def tp_scatter_sum(value, n_tp, axis):
-    me = lax.axis_index("tp")
-    width = value.shape[axis] // n_tp
-    total = lax.dynamic_slice_in_dim(value, me * width, width, axis)
-    for distance in range(1, n_tp):
-        block = lax.dynamic_slice_in_dim(value, (me + distance) % n_tp * width, width, axis)
-        total = total + tp_shift(block, n_tp, distance)
-    return total
 
 
 def ring_tables(n_req):
@@ -86,17 +76,18 @@
     )(patches)
 
 
-def merge(picked, stats, gain_bias, merge_weight):
+def merge(tp_index, picked, stats, gain_bias, merge_weight):
     window, tokens, width = picked.shape
     features = merge_weight.shape[2]
     count = len(stats)
-
-    def body(picked_ref, gain_bias_ref, *refs):
-        stats_refs, (weight_ref, out_ref) = refs[:count], refs[count:]
+    share = features // count
+
+    def body(index_ref, picked_ref, gain_bias_ref, *refs):
+        stats_refs, (weight_ref, *out_refs, total_ref) = refs[:count], refs[count:]
 
         @pl.when(pl.program_id(0) == 0)
         def _():
-            out_ref[...] = jnp.zeros_like(out_ref)
+            total_ref[...] = jnp.zeros_like(total_ref)
 
         sums = sum(ref[0] for ref in stats_refs) / DV
         row_mean = sums[:, 0:1]
@@ -106,7 +97,15 @@
             (picked_ref[0].astype(jnp.float32) - row_mean) * row_scale * gain_bias[0:1]
             + gain_bias[1:2]
         ).astype(jnp.bfloat16)
-        out_ref[...] += jnp.dot(normed, weight_ref[0], preferred_element_type=jnp.float32)
+        total_ref[...] += jnp.dot(normed, weight_ref[0], preferred_element_type=jnp.float32)
+
+        for index in range(count):
+
+            @pl.when((pl.program_id(0) == window - 1) & (index_ref[0] == index))
+            def _():
+                for distance, out_ref in enumerate(out_refs):
+                    first = (index + distance) % count * share
+                    out_ref[...] = total_ref[:, first : first + share]
 
     def by_slot(*shape):
         return pl.BlockSpec((1, *shape), lambda i: (i, 0, 0))
@@ -116,15 +115,17 @@
 
     return pl.pallas_call(
         body,
-        out_shape=jax.ShapeDtypeStruct((tokens, features), jnp.float32),
+        out_shape=[jax.ShapeDtypeStruct((tokens, share), jnp.float32)] * count,
         grid=(window,),
-        in_specs=[by_slot(tokens, width), whole((2, width))]
+        in_specs=[pl.BlockSpec(memory_space=pltpu.SMEM)]
+        + [by_slot(tokens, width), whole((2, width))]
         + [by_slot(tokens, 256)] * count
         + [by_slot(width, features)],
-        out_specs=whole((tokens, features)),
+        out_specs=[whole((tokens, share))] * count,
+        scratch_shapes=[pltpu.VMEM((tokens, features), jnp.float32)],
         compiler_params=pltpu.CompilerParams(vmem_limit_bytes=VMEM),
         cost_estimate=LIGHT,
-    )(picked, gain_bias, *stats, merge_weight)
+    )(tp_index, picked, gain_bias, *stats, merge_weight)
 
 
 def combine(tp_index, order, texts, images, gain_column):
@@ -219,14 +220,17 @@
     code = lax.rem(token_pos, row_count) + 1
     code_cols = jnp.stack([lax.div(code, 256), lax.rem(code, 256)], axis=1).astype(jnp.bfloat16)
 
-    partial_value = merge(picked, stats, gain_bias, merge_weight)
+    partial_value = merge(tp_index, picked, stats, gain_bias, merge_weight)
 
     partial_value, held[1], sides[0], slot, code_cols = tie(
         partial_value, held[1], sides[0], slot, code_cols
     )
     held.append(along_line(held[1]))
     sides.append(to_sides(held[1]))
-    merged = tp_scatter_sum(partial_value, n_tp, 1).astype(jnp.bfloat16)
+    merged = partial_value[0]
+    for distance in range(1, n_tp):
+        merged = merged + tp_shift(partial_value[distance], n_tp, distance)
+    merged = merged.astype(jnp.bfloat16)
     merged, sides[0] = tie(merged, sides[0])
     halves = to_corner(*sides[0])
     padding = (-width - 2) % 128

time: 88.7 us -> 87.7 us (0.989)
  local copies, waits for them, and re-layouts: 16.2 us -> 15.3 us
    dynamic_slice x1 -> x0, local copies, waits for them, and re-layouts: 0.92 us -> none  [tp_scatter_sum(): lax.dynamic_slice_in_dim(value, (me + distance) % n_tp * width, width, axis)]
  transfers between devices with their start and end apart: 23 -> 23, of which waited for: 10 -> 9; matrix products, arithmetic and copies ran while one was open for 29% -> 29% of each run, Pallas kernels for 6% -> 7%
where the time goes in v23:
time: 87.7 us; the launch traced here: 87.1 us
  starting transfers between devices  28.5 us (32%)
  waiting for transfers between devices  19 us (22%)
  local copies, waits for them, and re-layouts  15.3 us (17%)
  matrix products  10.4 us (12%)
  other arithmetic  7.98 us (9%)
  Pallas kernels  5.72 us (7%)
    dot_general x5, matrix products, add_product(): lax.dot_general(source, weight, (((0,), (0,)), ((), ())), preferred_eleme...  9.31 us
    ppermute x4, waiting for transfers between devices, along_line(): return lax.ppermute(block, 'req', line_perm)  8.71 us
    ppermute x4, starting transfers between devices, along_line(): return lax.ppermute(block, 'req', line_perm)  8.25 us
    ppermute x4, starting transfers between devices, to_sides(): lax.ppermute(block, 'req', y_perm)  6.06 us
    unnamed x13, local copies, waits for them, and re-layouts  6.03 us
    ppermute x4, starting transfers between devices, to_sides(): lax.ppermute(block, 'req', x_perm)  3.75 us
    ppermute x3, starting transfers between devices, to_corner(): right = lax.ppermute(by_x[:, cut:], 'req', y_perm)  3.68 us
    all_to_all x1, starting transfers between devices, shards(): lax.all_to_all(outgoing.reshape(n_req, IMG_CAP, -1), 'req', split_axis=0,...  3.56 us
  transfers between devices with their start and end apart: 23, of which 9 were waited for; matrix products, arithmetic and copies ran while one was open for 29% of the time, Pallas kernels for 7%

profile of v23, /device:TPU:0, one launch (start us, length us, event | category | flops | bytes accessed | tf_op | source)
XLA Modules:
  0.0 87.1 jit_solution(15638780726807201249)
XLA Ops:
  0.0 3.0 %collective-permute-start.1 = (bf16[104,2496]{1,0:T(8,128)(2,1)}, bf16[104,2496]{1,0:T(8,128)(2,1)}, u32[]{:S(2)}, u32[]{:S(2)}) collective-permute-start(bf16[104,2496]{1,0:T(8,128)(2,1)} %param.16), channel_id=1, source_target_pairs={{0,8},{2,10},{4,12},{6,14},{8,24},{10,26},{12,28},{14,30},{16,0},{... | collective-permute-start | bytes 1557512 | tf_op jit(solution)/shard_map/ppermute | solution.py:194
  3.0 1.5 %collective-permute-start.2 = (bf16[104,2496]{1,0:T(8,128)(2,1)}, bf16[104,2496]{1,0:T(8,128)(2,1)}, u32[]{:S(2)}, u32[]{:S(2)}) collective-permute-start(bf16[104,2496]{1,0:T(8,128)(2,1)} %param.16), channel_id=1, source_target_pairs={{0,2},{2,0},{4,6},{6,4},{8,10},{10,8},{12,14},{14,12},{16,18},{18,... | collective-permute-start | bytes 1557512 | tf_op jit(solution)/shard_map/ppermute | solution.py:197
  4.5 1.5 %collective-permute-start.3 = (bf16[104,2496]{1,0:T(8,128)(2,1)}, bf16[104,2496]{1,0:T(8,128)(2,1)}, u32[]{:S(2)}, u32[]{:S(2)}) collective-permute-start(bf16[104,2496]{1,0:T(8,128)(2,1)} %param.16), channel_id=1, source_target_pairs={{0,4},{2,6},{4,0},{6,2},{8,12},{10,14},{12,8},{14,10},{16,20},{18,... | collective-permute-start | bytes 1557512 | tf_op jit(solution)/shard_map/ppermute | solution.py:197
  6.0 1.1 %copy-done.2 = bf16[448,832]{1,0:T(8,128)(2,1)S(1)} copy-done((bf16[448,832]{1,0:T(8,128)(2,1)S(1)}, bf16[448,832]{1,0:T(8,128)(2,1)}, u32[]{:S(2)}) %copy-start.2) | copy-done | bytes 745496
  7.2 0.8 shard_map.118
  7.9 0.1 collective-permute-start
  8.0 0.7 convert_bitcast_fusion.1
  8.7 0.7 stack.22
  9.4 0.7 stack.21
  10.1 0.2 convert_reduce_fusion
  10.3 4.1 %copy-done = bf16[4,832,1664]{2,1,0:T(8,128)(2,1)S(1)} copy-done((bf16[4,832,1664]{2,1,0:T(8,128)(2,1)S(1)}, bf16[4,832,1664]{2,1,0:T(8,128)(2,1)}, u32[]{:S(2)}) %copy-start) | copy-done | bytes 11075608
  14.5 3.1 %shard_map.119 = (f32[112,832]{1,0:T(8,128)S(1)}, f32[112,832]{1,0:T(8,128)S(1)}) custom-call(s32[1]{0:T(128)} %bitcast.index_ref, bf16[4,112,832]{2,1,0:T(8,128)(2,1)S(1)} %get-tuple-element.51.picked_ref, bf16[2,832]{1,0:T(2,128)(2,1)S(1)} %pad_maximum_fusion.4.gain_bias_ref, f32[4,112,256]{2,1,0:T(8,128)S(1)} %get-tuple-element.52.refs_0_, ...), custom_call_target="tpu_custom_call" | custom-call | flops 1000 | bytes 1000 | tf_op jit(solution)/shard_map/pallas_call | solution.py:116
  17.6 0.5 collective-permute-done.3
  18.1 0.1 collective-permute-start.10
  18.2 2.6 %collective-permute-start.4 = (bf16[104,2496]{1,0:T(8,128)(2,1)}, bf16[104,2496]{1,0:T(8,128)(2,1)}, u32[]{:S(2)}, u32[]{:S(2)}) collective-permute-start(bf16[104,2496]{1,0:T(8,128)(2,1)} %collective-permute-done.1), channel_id=1, source_target_pairs={{0,8},{2,10},{4,12},{6,14},{8,24},{10,26},{12,28},{14,30},{16,0},{... | collective-permute-start | bytes 1557512 | tf_op jit(solution)/shard_map/ppermute | solution.py:194
  20.8 0.5 collective-permute-start.5
  21.3 1.5 %collective-permute-start.6 = (bf16[104,2496]{1,0:T(8,128)(2,1)}, bf16[104,2496]{1,0:T(8,128)(2,1)}, u32[]{:S(2)}, u32[]{:S(2)}) collective-permute-start(bf16[104,2496]{1,0:T(8,128)(2,1)} %collective-permute-done.1), channel_id=1, source_target_pairs={{0,4},{2,6},{4,0},{6,2},{8,12},{10,14},{12,8},{14,10},{16,20},{18,... | collective-permute-start | bytes 1557512 | tf_op jit(solution)/shard_map/ppermute | solution.py:197
  22.8 0.1 pad.13.clone
  22.8 0.1 copy.18
  23.0 0.1 add_convert_fusion
  23.1 0.0 copy-start.4
  23.1 1.7 %slice.33 = bf16[104,1280]{1,0:T(8,128)(2,1)} slice(bf16[104,2496]{1,0:T(8,128)(2,1)} %collective-permute-done.3), slice={[0:104], [0:1280]} | slice | bytes 532480 | tf_op jit(solution)/shard_map/slice | solution.py:200
  24.7 1.5 %collective-permute-start.11 = (bf16[104,1280]{1,0:T(8,128)(2,1)}, bf16[104,1280]{1,0:T(8,128)(2,1)S(1)}, u32[]{:S(2)}, u32[]{:S(2)}) collective-permute-start(bf16[104,1280]{1,0:T(8,128)(2,1)} %slice.33), channel_id=1, source_target_pairs={{0,2},{2,0},{4,6},{6,4},{8,10},{10,8},{12,14},{14,12},{16,18},{18,... | collective-permute-start | bytes 798728 | tf_op jit(solution)/shard_map/ppermute | solution.py:200
  26.2 1.7 %slice.34 = bf16[104,1216]{1,0:T(8,128)(2,1)} slice(bf16[104,2496]{1,0:T(8,128)(2,1)} %collective-permute-done.2), slice={[0:104], [1280:2496]} | slice | bytes 505856 | tf_op jit(solution)/shard_map/slice | solution.py:201
  27.9 1.1 %convolution_convert_fusion = bf16[256,896]{1,0:T(8,128)(2,1)} fusion(bf16[112,2]{1,0:T(8,128)(2,1)S(1)} %copy.18, bf16[112,832]{1,0:T(8,128)(2,1)S(1)} %add_convert_fusion, bf16[896]{0:T(1024)(128)(2,1)S(1)} %pad.13.clone, s32[112]{0:T(128)S(1)} %multiply_add_fusion), kind=kOutput, calls=%fused_computation.9 | convolution fusion | flops 52240384 | bytes 647808 | tf_op jit(solution)/shard_map/dot_general | solution.py:243
  29.0 3.6 %all-to-all-start = ((bf16[16,16,896]{2,1,0:T(8,128)(2,1)}), bf16[16,16,896]{2,1,0:T(8,128)(2,1)S(1)}, u32[]{:S(2)}, u32[]{:S(2)}) async-start(bf16[16,16,896]{2,1,0:T(8,128)(2,1)} %bitcast.5), calls=%async_computation | async-start | bytes 917504 | tf_op jit(solution)/shard_map/all_to_all | solution.py:244
  32.5 1.3 %collective-permute-done.4 = bf16[104,2496]{1,0:T(8,128)(2,1)} collective-permute-done((bf16[104,2496]{1,0:T(8,128)(2,1)}, bf16[104,2496]{1,0:T(8,128)(2,1)}, u32[]{:S(2)}, u32[]{:S(2)}) %collective-permute-start.4) | collective-permute-done | bytes 519200 | tf_op jit(solution)/shard_map/ppermute | solution.py:194
  33.8 1.5 %collective-permute-start.12 = (bf16[104,1216]{1,0:T(8,128)(2,1)}, bf16[104,1216]{1,0:T(8,128)(2,1)}, u32[]{:S(2)}, u32[]{:S(2)}) collective-permute-start(bf16[104,1216]{1,0:T(8,128)(2,1)} %slice.34), channel_id=1, source_target_pairs={{0,4},{2,6},{4,0},{6,2},{8,12},{10,14},{12,8},{14,10},{16,20},{18,... | collective-permute-start | bytes 758792 | tf_op jit(solution)/shard_map/ppermute | solution.py:201
  35.4 0.7 collective-permute-done.5
  36.0 1.0 %collective-permute-start.7 = (bf16[104,2496]{1,0:T(8,128)(2,1)}, bf16[104,2496]{1,0:T(8,128)(2,1)}, u32[]{:S(2)}, u32[]{:S(2)}) collective-permute-start(bf16[104,2496]{1,0:T(8,128)(2,1)} %collective-permute-done.4), channel_id=1, source_target_pairs={{0,8},{2,10},{4,12},{6,14},{8,24},{10,26},{12,28},{14,30},{16,0},{... | collective-permute-start | bytes 1557512 | tf_op jit(solution)/shard_map/ppermute | solution.py:194
  37.1 0.5 collective-permute-start.8
  37.6 2.6 %pad_maximum_fusion.1 = bf16[312,2496]{1,0:T(8,128)(2,1)} fusion(bf16[104,2496]{1,0:T(8,128)(2,1)} %collective-permute-done.6, bf16[104,2496]{1,0:T(8,128)(2,1)} %collective-permute-done.5, bf16[104,2496]{1,0:T(8,128)(2,1)} %collective-permute-done.1), kind=kLoop, calls=%fused_computation.5 | loop fusion | flops 4672512 | bytes 3115008 | tf_op jit(solution)/shard_map/concatenate | solution.py:258
  40.2 0.1 fusion.7
  40.3 0.7 dynamic-slice_bitcast_fusion.order_ref
  41.0 0.8 reshape.62.gain_ref
  41.8 2.7 %collective-permute-done.11 = bf16[104,1280]{1,0:T(8,128)(2,1)S(1)} collective-permute-done((bf16[104,1280]{1,0:T(8,128)(2,1)}, bf16[104,1280]{1,0:T(8,128)(2,1)S(1)}, u32[]{:S(2)}, u32[]{:S(2)}) %collective-permute-start.11) | collective-permute-done | bytes 266272 | tf_op jit(solution)/shard_map/ppermute | solution.py:200
  44.5 1.6 %collective-permute-start.9 = (bf16[104,2496]{1,0:T(8,128)(2,1)}, bf16[104,2496]{1,0:T(8,128)(2,1)}, u32[]{:S(2)}, u32[]{:S(2)}) collective-permute-start(bf16[104,2496]{1,0:T(8,128)(2,1)} %collective-permute-done.4), channel_id=1, source_target_pairs={{0,4},{2,6},{4,0},{6,2},{8,12},{10,14},{12,8},{14,10},{16,20},{18,... | collective-permute-start | bytes 1557512 | tf_op jit(solution)/shard_map/ppermute | solution.py:197
  46.1 0.7 constant_dynamic-update-slice_fusion.1
  46.9 1.7 %constant_dynamic-update-slice_fusion = bf16[104,2496]{1,0:T(8,128)(2,1)} fusion(bf16[104,2496]{1,0:T(8,128)(2,1)} %constant_dynamic-update-slice_fusion.1, bf16[104,1216]{1,0:T(8,128)(2,1)} %collective-permute-done.12), kind=kLoop, calls=%fused_computation.22 | loop fusion | bytes 532480 | tf_op jit(solution)/shard_map/concatenate | solution.py:256
  48.5 1.7 %pad_maximum_fusion = bf16[416,2496]{1,0:T(8,128)(2,1)S(1)} fusion(bf16[104,2496]{1,0:T(8,128)(2,1)} %constant_dynamic-update-slice_fusion, bf16[104,2496]{1,0:T(8,128)(2,1)} %collective-permute-done.3, bf16[104,2496]{1,0:T(8,128)(2,1)} %collective-permute-done.2, bf16[104,2496]{1,0:T(8,128)(2,1)} %param.16), kind=kLoop, calls=%fused_computation.4 | loop fusion | flops 8306688 | bytes 4153344 | tf_op jit(solution)/shard_map/concatenate | solution.py:257
  50.2 7.4 %collective-permute-done.7 = bf16[104,2496]{1,0:T(8,128)(2,1)} collective-permute-done((bf16[104,2496]{1,0:T(8,128)(2,1)}, bf16[104,2496]{1,0:T(8,128)(2,1)}, u32[]{:S(2)}, u32[]{:S(2)}) %collective-permute-start.7) | collective-permute-done | bytes 519200 | tf_op jit(solution)/shard_map/ppermute | solution.py:194
  57.6 0.3 collective-permute-done.9
  57.9 1.2 %collective-permute-start.18 = (bf16[104,2496]{1,0:T(8,128)(2,1)}, bf16[104,2496]{1,0:T(8,128)(2,1)S(1)}, u32[]{:S(2)}, u32[]{:S(2)}) collective-permute-start(bf16[104,2496]{1,0:T(8,128)(2,1)} %collective-permute-done.7), channel_id=1, source_target_pairs={{0,2},{2,0},{4,6},{6,4},{8,10},{10,8},{12,14},{14,12},{16,18},{18,... | collective-permute-start | bytes 1557512 | tf_op jit(solution)/shard_map/ppermute | solution.py:197
  59.1 1.5 %collective-permute-start.19 = (bf16[104,2496]{1,0:T(8,128)(2,1)}, bf16[104,2496]{1,0:T(8,128)(2,1)S(1)}, u32[]{:S(2)}, u32[]{:S(2)}) collective-permute-start(bf16[104,2496]{1,0:T(8,128)(2,1)} %collective-permute-done.7), channel_id=1, source_target_pairs={{0,4},{2,6},{4,0},{6,2},{8,12},{10,14},{12,8},{14,10},{16,20},{18,... | collective-permute-start | bytes 1557512 | tf_op jit(solution)/shard_map/ppermute | solution.py:197
  60.6 0.6 collective-permute-start.15
  61.2 1.0 %slice.35 = bf16[104,1280]{1,0:T(8,128)(2,1)S(1)} slice(bf16[104,2496]{1,0:T(8,128)(2,1)} %collective-permute-done.9), slice={[0:104], [0:1280]} | slice | bytes 532480 | tf_op jit(solution)/shard_map/slice | solution.py:200
  62.2 1.3 %pad_maximum_fusion.2 = bf16[312,2496]{1,0:T(8,128)(2,1)S(1)} fusion(bf16[104,2496]{1,0:T(8,128)(2,1)} %collective-permute-done.9, bf16[104,2496]{1,0:T(8,128)(2,1)S(1)} %collective-permute-done.8, bf16[104,2496]{1,0:T(8,128)(2,1)} %collective-permute-done.4), kind=kLoop, calls=%fused_computation.7 | loop fusion | flops 4672512 | bytes 3115008 | tf_op jit(solution)/shard_map/concatenate | solution.py:272
  63.5 0.9 %collective-permute-start.14 = (bf16[104,1280]{1,0:T(8,128)(2,1)S(1)}, bf16[104,1280]{1,0:T(8,128)(2,1)S(1)}, u32[]{:S(2)}, u32[]{:S(2)}) collective-permute-start(bf16[104,1280]{1,0:T(8,128)(2,1)S(1)} %slice.35), channel_id=1, source_target_pairs={{0,2},{2,0},{4,6},{6,4},{8,10},{10,8},{12,14},{14,12},{16,18},{18,... | collective-permute-start | bytes 798728 | tf_op jit(solution)/shard_map/ppermute | solution.py:200
  64.4 1.6 %collective-permute-start.13 = (bf16[104,2496]{1,0:T(8,128)(2,1)}, bf16[104,2496]{1,0:T(8,128)(2,1)S(1)}, u32[]{:S(2)}, u32[]{:S(2)}) collective-permute-start(bf16[104,2496]{1,0:T(8,128)(2,1)} %constant_dynamic-update-slice_fusion), channel_id=1, source_target_pairs={{0,8},{2,10},{4,12},{6,14},{8,24},{10,26},{12,28},{14,30},{16,0},{... | collective-permute-start | bytes 1557512 | tf_op jit(solution)/shard_map/ppermute | solution.py:194
  66.0 1.8 %shard_map.120 = bf16[16,104,512]{2,1,0:T(8,128)(2,1)S(1)} custom-call(s32[1]{0:T(128)} %bitcast.index_ref, s32[16]{0:T(128)S(1)} %dynamic-slice_bitcast_fusion.order_ref, bf16[16,104,1]{2,1,0:T(8,128)(2,1)S(1)} %reshape.62.gain_ref, bf16[832,512]{1,0:T(8,128)(2,1)S(1)} %bitcast.28, bf16[832,512]{1,0:T(8,128)(2,1)S(1)} %collective-permute-done.16.refs_1_, ...), custom_call_target="tpu_custom_call" | custom-call | flops 1000 | bytes 1000 | tf_op jit(solution)/shard_map/pallas_call | solution.py:169
  67.9 0.1 fusion.13
  68.0 0.0 copy-start.3
  68.0 1.5 %fusion.14 = f32[512,2496]{0,1:T(8,128)S(1)} fusion(bf16[416,512]{1,0:T(8,128)(2,1)S(1)} %bitcast.30, bf16[416,2496]{1,0:T(8,128)(2,1)S(1)} %pad_maximum_fusion), kind=kOutput, calls=%fused_computation.46 | convolution fusion | flops 1063256064 | bytes 7614464 | tf_op jit(solution)/shard_map/dot_general | solution.py:279
  69.6 1.6 %convolution_add_fusion.2 = f32[512,2496]{0,1:T(8,128)S(1)} fusion(f32[512,2496]{0,1:T(8,128)S(1)} %fusion.14, bf16[312,512]{1,0:T(8,128)(2,1)S(1)} %bitcast.33, bf16[312,2496]{1,0:T(8,128)(2,1)S(1)} %copy-done.3), kind=kOutput, calls=%fused_computation.3 | convolution fusion | flops 798720000 | bytes 12100608 | tf_op jit(solution)/shard_map/dot_general | solution.py:279
  71.2 2.0 %collective-permute-done.18 = bf16[104,2496]{1,0:T(8,128)(2,1)S(1)} collective-permute-done((bf16[104,2496]{1,0:T(8,128)(2,1)}, bf16[104,2496]{1,0:T(8,128)(2,1)S(1)}, u32[]{:S(2)}, u32[]{:S(2)}) %collective-permute-start.18) | collective-permute-done | bytes 519200 | tf_op jit(solution)/shard_map/ppermute | solution.py:197
  73.2 1.2 %collective-permute-done.19 = bf16[104,2496]{1,0:T(8,128)(2,1)S(1)} collective-permute-done((bf16[104,2496]{1,0:T(8,128)(2,1)}, bf16[104,2496]{1,0:T(8,128)(2,1)S(1)}, u32[]{:S(2)}, u32[]{:S(2)}) %collective-permute-start.19) | collective-permute-done | bytes 519200 | tf_op jit(solution)/shard_map/ppermute | solution.py:197
  74.4 1.5 %collective-permute-start.21 = (bf16[104,1216]{1,0:T(8,128)(2,1)S(1)}, bf16[104,1216]{1,0:T(8,128)(2,1)S(1)}, u32[]{:S(2)}, u32[]{:S(2)}) collective-permute-start(bf16[104,1216]{1,0:T(8,128)(2,1)S(1)} %slice.40), channel_id=1, source_target_pairs={{0,4},{2,6},{4,0},{6,2},{8,12},{10,14},{12,8},{14,10},{16,20},{18,... | collective-permute-start | bytes 758792 | tf_op jit(solution)/shard_map/ppermute | solution.py:201
  75.9 0.6 collective-permute-start.20
  76.6 1.5 %convolution_add_fusion.1 = f32[512,2496]{0,1:T(8,128)S(1)} fusion(f32[512,2496]{0,1:T(8,128)S(1)} %convolution_add_fusion.2, bf16[312,512]{1,0:T(8,128)(2,1)S(1)} %bitcast.32, bf16[312,2496]{1,0:T(8,128)(2,1)S(1)} %pad_maximum_fusion.2), kind=kOutput, calls=%fused_computation.2 | convolution fusion | flops 798720000 | bytes 12100608 | tf_op jit(solution)/shard_map/dot_general | solution.py:279
  78.1 1.2 %pad_maximum_fusion.3 = bf16[312,2496]{1,0:T(8,128)(2,1)S(1)} fusion(bf16[104,2496]{1,0:T(8,128)(2,1)S(1)} %collective-permute-done.19, bf16[104,2496]{1,0:T(8,128)(2,1)S(1)} %collective-permute-done.18, bf16[104,2496]{1,0:T(8,128)(2,1)} %collective-permute-done.7), kind=kLoop, calls=%fused_computation.8 | loop fusion | flops 4672512 | bytes 3115008 | tf_op jit(solution)/shard_map/concatenate | solution.py:272
  79.3 1.6 %convolution_add_fusion = f32[512,2496]{0,1:T(8,128)S(1)} fusion(f32[512,2496]{0,1:T(8,128)S(1)} %convolution_add_fusion.1, bf16[312,512]{1,0:T(8,128)(2,1)S(1)} %bitcast.31, bf16[312,2496]{1,0:T(8,128)(2,1)S(1)} %pad_maximum_fusion.3), kind=kOutput, calls=%fused_computation.1 | convolution fusion | flops 798720000 | bytes 12100608 | tf_op jit(solution)/shard_map/dot_general | solution.py:279
  81.0 2.9 %collective-permute-done.21 = bf16[104,1216]{1,0:T(8,128)(2,1)S(1)} collective-permute-done((bf16[104,1216]{1,0:T(8,128)(2,1)S(1)}, bf16[104,1216]{1,0:T(8,128)(2,1)S(1)}, u32[]{:S(2)}, u32[]{:S(2)}) %collective-permute-start.21) | collective-permute-done | bytes 252960 | tf_op jit(solution)/shard_map/ppermute | solution.py:201
  83.9 0.1 maximum_maximum_fusion
  84.0 3.1 %select_convert_fusion = bf16[512,2496]{0,1:T(8,128)(2,1)} fusion(f32[512,2496]{0,1:T(8,128)S(1)} %convolution_add_fusion, bf16[312,512]{1,0:T(8,128)(2,1)S(1)} %bitcast.29, bf16[312,2496]{1,0:T(8,128)(2,1)S(1)} %maximum_maximum_fusion, pred[512]{0:T(512)(128)(4,1)S(1)} %fusion.8), kind=kOutput, calls=%fused_computation | convolution fusion | flops 801275904 | bytes 9545216 | tf_op jit(solution)/shard_map/dot_general | solution.py:279
  (35 shorter events, 0.2 us)
Async XLA Ops:
  0.0 17.6 %collective-permute-start.1 = (bf16[104,2496]{1,0:T(8,128)(2,1)}, bf16[104,2496]{1,0:T(8,128)(2,1)}, u32[]{:S(2)}, u32[]{:S(2)}) collective-permute-start(bf16[104,2496]{1,0:T(8,128)(2,1)} %param.16), channel_id=1, source_target_pairs={{0,8},{2,10},{4,12},{6,14},{8,24},{10,26},{12,28},{14,30},{16,0},{... | collective-permute-start | bytes 1557512 | tf_op jit(solution)/shard_map/ppermute | solution.py:194
  3.0 14.6 %collective-permute-start.2 = (bf16[104,2496]{1,0:T(8,128)(2,1)}, bf16[104,2496]{1,0:T(8,128)(2,1)}, u32[]{:S(2)}, u32[]{:S(2)}) collective-permute-start(bf16[104,2496]{1,0:T(8,128)(2,1)} %param.16), channel_id=1, source_target_pairs={{0,2},{2,0},{4,6},{6,4},{8,10},{10,8},{12,14},{14,12},{16,18},{18,... | collective-permute-start | bytes 1557512 | tf_op jit(solution)/shard_map/ppermute | solution.py:197
  4.5 13.6 %collective-permute-start.3 = (bf16[104,2496]{1,0:T(8,128)(2,1)}, bf16[104,2496]{1,0:T(8,128)(2,1)}, u32[]{:S(2)}, u32[]{:S(2)}) collective-permute-start(bf16[104,2496]{1,0:T(8,128)(2,1)} %param.16), channel_id=1, source_target_pairs={{0,4},{2,6},{4,0},{6,2},{8,12},{10,14},{12,8},{14,10},{16,20},{18,... | collective-permute-start | bytes 1557512 | tf_op jit(solution)/shard_map/ppermute | solution.py:197
  6.0 1.1 %copy-start.2 = (bf16[448,832]{1,0:T(8,128)(2,1)S(1)}, bf16[448,832]{1,0:T(8,128)(2,1)}, u32[]{:S(2)}) copy-start(bf16[448,832]{1,0:T(8,128)(2,1)} %patches_ref.1) | copy-start | bytes 2236420
  7.9 2.4 %collective-permute-start = (f32[4,112,256]{2,1,0:T(8,128)S(1)}, f32[4,112,256]{2,1,0:T(8,128)S(1)}, u32[]{:S(2)}, u32[]{:S(2)}) collective-permute-start(f32[4,112,256]{2,1,0:T(8,128)S(1)} %get-tuple-element.52.refs_0_), channel_id=1, source_target_pairs={{0,1},{1,0},{2,3},{3,2},{4,5},{5,4},{6,7},{7,6},{8,9},{9,8},{10,11... | collective-permute-start | bytes 1376264 | tf_op jit(solution)/shard_map/ppermute | solution.py:26
  10.3 4.1 %copy-start = (bf16[4,832,1664]{2,1,0:T(8,128)(2,1)S(1)}, bf16[4,832,1664]{2,1,0:T(8,128)(2,1)}, u32[]{:S(2)}) copy-start(bf16[4,832,1664]{2,1,0:T(8,128)(2,1)} %refs_2_.1) | copy-start | bytes 33226756
  14.5 8.3 %copy-start.1 = (bf16[512,832]{0,1:T(8,128)(2,1)S(1)}, bf16[512,832]{0,1:T(8,128)(2,1)}, u32[]{:S(2)}) copy-start(bf16[512,832]{0,1:T(8,128)(2,1)} %param.14) | copy-start | bytes 2555908
  18.1 4.9 %collective-permute-start.10 = (f32[112,832]{1,0:T(8,128)S(1)}, f32[112,832]{1,0:T(8,128)S(1)}, u32[]{:S(2)}, u32[]{:S(2)}) collective-permute-start(f32[112,832]{1,0:T(8,128)S(1)} %get-tuple-element.59), channel_id=1, source_target_pairs={{0,1},{1,0},{2,3},{3,2},{4,5},{5,4},{6,7},{7,6},{8,9},{9,8},{10,11... | collective-permute-start | bytes 1118216 | tf_op jit(solution)/shard_map/ppermute | solution.py:26
  18.2 15.7 %collective-permute-start.4 = (bf16[104,2496]{1,0:T(8,128)(2,1)}, bf16[104,2496]{1,0:T(8,128)(2,1)}, u32[]{:S(2)}, u32[]{:S(2)}) collective-permute-start(bf16[104,2496]{1,0:T(8,128)(2,1)} %collective-permute-done.1), channel_id=1, source_target_pairs={{0,8},{2,10},{4,12},{6,14},{8,24},{10,26},{12,28},{14,30},{16,0},{... | collective-permute-start | bytes 1557512 | tf_op jit(solution)/shard_map/ppermute | solution.py:194
  20.8 15.3 %collective-permute-start.5 = (bf16[104,2496]{1,0:T(8,128)(2,1)}, bf16[104,2496]{1,0:T(8,128)(2,1)}, u32[]{:S(2)}, u32[]{:S(2)}) collective-permute-start(bf16[104,2496]{1,0:T(8,128)(2,1)} %collective-permute-done.1), channel_id=1, source_target_pairs={{0,2},{2,0},{4,6},{6,4},{8,10},{10,8},{12,14},{14,12},{16,18},{18,... | collective-permute-start | bytes 1557512 | tf_op jit(solution)/shard_map/ppermute | solution.py:197
  21.3 14.7 %collective-permute-start.6 = (bf16[104,2496]{1,0:T(8,128)(2,1)}, bf16[104,2496]{1,0:T(8,128)(2,1)}, u32[]{:S(2)}, u32[]{:S(2)}) collective-permute-start(bf16[104,2496]{1,0:T(8,128)(2,1)} %collective-permute-done.1), channel_id=1, source_target_pairs={{0,4},{2,6},{4,0},{6,2},{8,12},{10,14},{12,8},{14,10},{16,20},{18,... | collective-permute-start | bytes 1557512 | tf_op jit(solution)/shard_map/ppermute | solution.py:197
  22.8 40.8 %collective-permute-start.16 = (bf16[832,512]{1,0:T(8,128)(2,1)S(1)}, bf16[832,512]{1,0:T(8,128)(2,1)S(1)}, u32[]{:S(2)}, u32[]{:S(2)}) collective-permute-start(bf16[832,512]{1,0:T(8,128)(2,1)S(1)} %bitcast.27), channel_id=1, source_target_pairs={{0,1},{1,0},{2,3},{3,2},{4,5},{5,4},{6,7},{7,6},{8,9},{9,8},{10,11... | collective-permute-start | bytes 2555912 | tf_op jit(solution)/shard_map/ppermute | solution.py:26
  23.0 17.3 %copy-start.5 = (s32[2]{0:T(128)S(1)}, s32[2]{0:T(128)}, u32[]{:S(2)}) copy-start(s32[2]{0:T(128)} %param.18) | copy-start | bytes 28
  23.1 18.0 %copy-start.4 = (bf16[1664]{0:T(1024)(128)(2,1)S(1)}, bf16[1664]{0:T(1024)(128)(2,1)}, u32[]{:S(2)}) copy-start(bf16[1664]{0:T(1024)(128)(2,1)} %param.15) | copy-start | bytes 9988
  24.7 19.8 %collective-permute-start.11 = (bf16[104,1280]{1,0:T(8,128)(2,1)}, bf16[104,1280]{1,0:T(8,128)(2,1)S(1)}, u32[]{:S(2)}, u32[]{:S(2)}) collective-permute-start(bf16[104,1280]{1,0:T(8,128)(2,1)} %slice.33), channel_id=1, source_target_pairs={{0,2},{2,0},{4,6},{6,4},{8,10},{10,8},{12,14},{14,12},{16,18},{18,... | collective-permute-start | bytes 798728 | tf_op jit(solution)/shard_map/ppermute | solution.py:200
  29.0 19.6 %all-to-all-start = ((bf16[16,16,896]{2,1,0:T(8,128)(2,1)}), bf16[16,16,896]{2,1,0:T(8,128)(2,1)S(1)}, u32[]{:S(2)}, u32[]{:S(2)}) async-start(bf16[16,16,896]{2,1,0:T(8,128)(2,1)} %bitcast.5), calls=%async_computation | async-start | bytes 917504 | tf_op jit(solution)/shard_map/all_to_all | solution.py:244
  33.8 13.0 %collective-permute-start.12 = (bf16[104,1216]{1,0:T(8,128)(2,1)}, bf16[104,1216]{1,0:T(8,128)(2,1)}, u32[]{:S(2)}, u32[]{:S(2)}) collective-permute-start(bf16[104,1216]{1,0:T(8,128)(2,1)} %slice.34), channel_id=1, source_target_pairs={{0,4},{2,6},{4,0},{6,2},{8,12},{10,14},{12,8},{14,10},{16,20},{18,... | collective-permute-start | bytes 758792 | tf_op jit(solution)/shard_map/ppermute | solution.py:201
  36.0 21.6 %collective-permute-start.7 = (bf16[104,2496]{1,0:T(8,128)(2,1)}, bf16[104,2496]{1,0:T(8,128)(2,1)}, u32[]{:S(2)}, u32[]{:S(2)}) collective-permute-start(bf16[104,2496]{1,0:T(8,128)(2,1)} %collective-permute-done.4), channel_id=1, source_target_pairs={{0,8},{2,10},{4,12},{6,14},{8,24},{10,26},{12,28},{14,30},{16,0},{... | collective-permute-start | bytes 1557512 | tf_op jit(solution)/shard_map/ppermute | solution.py:194
  37.1 20.6 %collective-permute-start.8 = (bf16[104,2496]{1,0:T(8,128)(2,1)}, bf16[104,2496]{1,0:T(8,128)(2,1)S(1)}, u32[]{:S(2)}, u32[]{:S(2)}) collective-permute-start(bf16[104,2496]{1,0:T(8,128)(2,1)} %collective-permute-done.4), channel_id=1, source_target_pairs={{0,2},{2,0},{4,6},{6,4},{8,10},{10,8},{12,14},{14,12},{16,18},{18,... | collective-permute-start | bytes 1557512 | tf_op jit(solution)/shard_map/ppermute | solution.py:197
  44.5 13.4 %collective-permute-start.9 = (bf16[104,2496]{1,0:T(8,128)(2,1)}, bf16[104,2496]{1,0:T(8,128)(2,1)}, u32[]{:S(2)}, u32[]{:S(2)}) collective-permute-start(bf16[104,2496]{1,0:T(8,128)(2,1)} %collective-permute-done.4), channel_id=1, source_target_pairs={{0,4},{2,6},{4,0},{6,2},{8,12},{10,14},{12,8},{14,10},{16,20},{18,... | collective-permute-start | bytes 1557512 | tf_op jit(solution)/shard_map/ppermute | solution.py:197
  48.5 15.9 %collective-permute-start.17 = (bf16[256,896]{1,0:T(8,128)(2,1)S(1)}, bf16[256,896]{1,0:T(8,128)(2,1)S(1)}, u32[]{:S(2)}, u32[]{:S(2)}) collective-permute-start(bf16[256,896]{1,0:T(8,128)(2,1)S(1)} %bitcast.25), channel_id=1, source_target_pairs={{0,1},{1,0},{2,3},{3,2},{4,5},{5,4},{6,7},{7,6},{8,9},{9,8},{10,11... | collective-permute-start | bytes 1376264 | tf_op jit(solution)/shard_map/ppermute | solution.py:26
  57.9 15.3 %collective-permute-start.18 = (bf16[104,2496]{1,0:T(8,128)(2,1)}, bf16[104,2496]{1,0:T(8,128)(2,1)S(1)}, u32[]{:S(2)}, u32[]{:S(2)}) collective-permute-start(bf16[104,2496]{1,0:T(8,128)(2,1)} %collective-permute-done.7), channel_id=1, source_target_pairs={{0,2},{2,0},{4,6},{6,4},{8,10},{10,8},{12,14},{14,12},{16,18},{18,... | collective-permute-start | bytes 1557512 | tf_op jit(solution)/shard_map/ppermute | solution.py:197
  59.1 15.2 %collective-permute-start.19 = (bf16[104,2496]{1,0:T(8,128)(2,1)}, bf16[104,2496]{1,0:T(8,128)(2,1)S(1)}, u32[]{:S(2)}, u32[]{:S(2)}) collective-permute-start(bf16[104,2496]{1,0:T(8,128)(2,1)} %collective-permute-done.7), channel_id=1, source_target_pairs={{0,4},{2,6},{4,0},{6,2},{8,12},{10,14},{12,8},{14,10},{16,20},{18,... | collective-permute-start | bytes 1557512 | tf_op jit(solution)/shard_map/ppermute | solution.py:197
  60.6 20.3 %collective-permute-start.15 = (bf16[104,1216]{1,0:T(8,128)(2,1)S(1)}, bf16[104,1216]{1,0:T(8,128)(2,1)S(1)}, u32[]{:S(2)}, u32[]{:S(2)}) collective-permute-start(bf16[104,1216]{1,0:T(8,128)(2,1)S(1)} %slice.36), channel_id=1, source_target_pairs={{0,4},{2,6},{4,0},{6,2},{8,12},{10,14},{12,8},{14,10},{16,20},{18,... | collective-permute-start | bytes 758792 | tf_op jit(solution)/shard_map/ppermute | solution.py:201
  63.5 17.4 %collective-permute-start.14 = (bf16[104,1280]{1,0:T(8,128)(2,1)S(1)}, bf16[104,1280]{1,0:T(8,128)(2,1)S(1)}, u32[]{:S(2)}, u32[]{:S(2)}) collective-permute-start(bf16[104,1280]{1,0:T(8,128)(2,1)S(1)} %slice.35), channel_id=1, source_target_pairs={{0,2},{2,0},{4,6},{6,4},{8,10},{10,8},{12,14},{14,12},{16,18},{18,... | collective-permute-start | bytes 798728 | tf_op jit(solution)/shard_map/ppermute | solution.py:200
  64.4 16.5 %collective-permute-start.13 = (bf16[104,2496]{1,0:T(8,128)(2,1)}, bf16[104,2496]{1,0:T(8,128)(2,1)S(1)}, u32[]{:S(2)}, u32[]{:S(2)}) collective-permute-start(bf16[104,2496]{1,0:T(8,128)(2,1)} %constant_dynamic-update-slice_fusion), channel_id=1, source_target_pairs={{0,8},{2,10},{4,12},{6,14},{8,24},{10,26},{12,28},{14,30},{16,0},{... | collective-permute-start | bytes 1557512 | tf_op jit(solution)/shard_map/ppermute | solution.py:194
  68.0 1.6 %copy-start.3 = (bf16[312,2496]{1,0:T(8,128)(2,1)S(1)}, bf16[312,2496]{1,0:T(8,128)(2,1)}, u32[]{:S(2)}) copy-start(bf16[312,2496]{1,0:T(8,128)(2,1)} %pad_maximum_fusion.1) | copy-start | bytes 4672516
  74.4 9.5 %collective-permute-start.21 = (bf16[104,1216]{1,0:T(8,128)(2,1)S(1)}, bf16[104,1216]{1,0:T(8,128)(2,1)S(1)}, u32[]{:S(2)}, u32[]{:S(2)}) collective-permute-start(bf16[104,1216]{1,0:T(8,128)(2,1)S(1)} %slice.40), channel_id=1, source_target_pairs={{0,4},{2,6},{4,0},{6,2},{8,12},{10,14},{12,8},{14,10},{16,20},{18,... | collective-permute-start | bytes 758792 | tf_op jit(solution)/shard_map/ppermute | solution.py:201
  75.9 7.9 %collective-permute-start.20 = (bf16[104,1280]{1,0:T(8,128)(2,1)S(1)}, bf16[104,1280]{1,0:T(8,128)(2,1)S(1)}, u32[]{:S(2)}, u32[]{:S(2)}) collective-permute-start(bf16[104,1280]{1,0:T(8,128)(2,1)S(1)} %slice.39), channel_id=1, source_target_pairs={{0,2},{2,0},{4,6},{6,4},{8,10},{10,8},{12,14},{14,12},{16,18},{18,... | collective-permute-start | bytes 798728 | tf_op jit(solution)/shard_map/ppermute | solution.py:200

commit v24 on v23

--- a/solution.py
+++ b/solution.py
@@ -31,8 +31,8 @@
     order = folded_ring(lines)
     following = {order[i]: order[(i + 1) % lines] for i in range(lines)}
     line_perm = [(z * 4 + p, following[z] * 4 + p) for z in range(lines) for p in range(4)]
-    arrivals = [(0, flip) for flip in range(4)]
-    arrivals += [(step, flip) for step in range(1, lines) for flip in range(3)]
+    arrivals = [(0, 0), (0, 1), (0, 2), (1, 0), (1, 1), (1, 2), (0, 3)]
+    arrivals += [(step, flip) for step in range(2, lines) for flip in range(3)]
     arrivals += [(step, 3) for step in range(1, lines)]
     table = np.zeros((n_req, n_req), np.int32)
     for index in range(n_req):
@@ -253,20 +253,19 @@
     images = [arrived] + [tp_shift(arrived, n_tp, d) for d in range(1, n_tp)]
     blocks = combine(tp_index, order, texts, images, gain_column)
 
+    first = jnp.concatenate([held[0], *sides[0]], axis=0)
+    last_sides = sides[2]
+    held[3], sides[2], halves, first = tie(held[3], sides[2], halves, first)
+    sides.append(to_sides(held[3]))
     corners = [jnp.concatenate(halves, axis=1)]
-    first = jnp.concatenate([held[0], *sides[0], corners[0]], axis=0)
-    second = jnp.concatenate([held[1], *sides[1]], axis=0)
-    held[3], sides[2], corners[0], first, second = tie(
-        held[3], sides[2], corners[0], first, second
-    )
-    sides.append(to_sides(held[3]))
+    second = jnp.concatenate([held[1], *sides[1], corners[0]], axis=0)
     corners.append(along_line(corners[0]))
     for step in range(4, lines):
         held.append(along_line(held[step - 1]))
         sides.append(to_sides(held[step]))
     for step in range(2, lines - 2):
         corners.append(along_line(corners[step - 1]))
-    corners.append(jnp.concatenate(to_corner(*sides[-2]), axis=1))
+    corners.append(jnp.concatenate(to_corner(*(last_sides if lines == 4 else sides[-2])), axis=1))
 
     def add_product(total, first, weights):
         weight = jnp.concatenate(weights, axis=0)
@@ -282,7 +281,7 @@
         return part if total is None else total + part
 
     total = add_product(None, 0, [first])
-    total = add_product(total, 4, [second])
+    total = add_product(total, 3, [second])
 
     total, sides[-1] = tie(total, sides[-1])
     corners.append(jnp.concatenate(to_corner(*sides[-1]), axis=1))

time: 87.7 us -> 92.3 us (1.052)
  waiting for transfers between devices: 19 us -> 21.7 us
  other arithmetic: 7.98 us -> 9.22 us
    ppermute x4, waiting for transfers between devices: 8.71 us -> 1.67 us  [along_line(): return lax.ppermute(block, 'req', line_perm)]
    ppermute x4, waiting for transfers between devices: 2.68 us -> 9.37 us  [to_sides(): lax.ppermute(block, 'req', x_perm)]
    ppermute x3, waiting for transfers between devices: 2.92 us -> 6.97 us  [to_corner(): right = lax.ppermute(by_x[:, cut:], 'req', y_perm)]
    ppermute x3, waiting for transfers between devices: 2.68 us -> 0.01 us  [to_corner(): left = lax.ppermute(by_y[:, :cut], 'req', x_perm)]
    ppermute x4, starting transfers between devices: 8.25 us -> 6.07 us  [along_line(): return lax.ppermute(block, 'req', line_perm)]
    ppermute x4, waiting for transfers between devices: 1.98 us -> 3.67 us  [to_sides(): lax.ppermute(block, 'req', y_perm)]
    slice x3, local copies, waits for them, and re-layouts: 1.71 us -> 0.06 us  [to_corner(): right = lax.ppermute(by_x[:, cut:], 'req', y_perm)]
    concatenate x3, other arithmetic: 2.61 us -> 4.03 us  [add_product(): weight = jnp.concatenate(weights, axis=0)]
  transfers between devices with their start and end apart: 23 -> 23, of which waited for: 9 -> 7; matrix products, arithmetic and copies ran while one was open for 29% -> 27% of each run, Pallas kernels for 7% -> 6%
where the time goes in v24:
time: 92.3 us; the launch traced here: 91.6 us
  starting transfers between devices  28.5 us (31%)
  waiting for transfers between devices  21.7 us (24%)
  local copies, waits for them, and re-layouts  15.8 us (17%)
  matrix products  10.3 us (11%)
  other arithmetic  9.22 us (10%)
  Pallas kernels  5.72 us (6%)
    ppermute x4, waiting for transfers between devices, to_sides(): lax.ppermute(block, 'req', x_perm)  9.37 us
    dot_general x5, matrix products, add_product(): lax.dot_general(source, weight, (((0,), (0,)), ((), ())), preferred_eleme...  9.27 us
    unnamed x19, local copies, waits for them, and re-layouts  7.21 us
    ppermute x3, waiting for transfers between devices, to_corner(): right = lax.ppermute(by_x[:, cut:], 'req', y_perm)  6.97 us
    ppermute x4, starting transfers between devices, to_sides(): lax.ppermute(block, 'req', y_perm)  6.61 us
    ppermute x4, starting transfers between devices, along_line(): return lax.ppermute(block, 'req', line_perm)  6.07 us
    ppermute x4, starting transfers between devices, to_sides(): lax.ppermute(block, 'req', x_perm)  4.65 us
    concatenate x3, other arithmetic, add_product(): weight = jnp.concatenate(weights, axis=0)  4.03 us
  transfers between devices with their start and end apart: 23, of which 7 were waited for; matrix products, arithmetic and copies ran while one was open for 27% of the time, Pallas kernels for 6%

profile of v24, /device:TPU:0, one launch (start us, length us, event | category | flops | bytes accessed | tf_op | source)
XLA Modules:
  0.0 91.6 jit_solution(4359471717358514210)
XLA Ops:
  0.0 3.0 %collective-permute-start.1 = (bf16[104,2496]{1,0:T(8,128)(2,1)}, bf16[104,2496]{1,0:T(8,128)(2,1)}, u32[]{:S(2)}, u32[]{:S(2)}) collective-permute-start(bf16[104,2496]{1,0:T(8,128)(2,1)} %param.16), channel_id=1, source_target_pairs={{0,8},{2,10},{4,12},{6,14},{8,24},{10,26},{12,28},{14,30},{16,0},{... | collective-permute-start | bytes 1557512 | tf_op jit(solution)/shard_map/ppermute | solution.py:194
  3.0 1.5 %collective-permute-start.2 = (bf16[104,2496]{1,0:T(8,128)(2,1)}, bf16[104,2496]{1,0:T(8,128)(2,1)S(1)}, u32[]{:S(2)}, u32[]{:S(2)}) collective-permute-start(bf16[104,2496]{1,0:T(8,128)(2,1)} %param.16), channel_id=1, source_target_pairs={{0,2},{2,0},{4,6},{6,4},{8,10},{10,8},{12,14},{14,12},{16,18},{18,... | collective-permute-start | bytes 1557512 | tf_op jit(solution)/shard_map/ppermute | solution.py:197
  4.5 1.5 %collective-permute-start.3 = (bf16[104,2496]{1,0:T(8,128)(2,1)}, bf16[104,2496]{1,0:T(8,128)(2,1)}, u32[]{:S(2)}, u32[]{:S(2)}) collective-permute-start(bf16[104,2496]{1,0:T(8,128)(2,1)} %param.16), channel_id=1, source_target_pairs={{0,4},{2,6},{4,0},{6,2},{8,12},{10,14},{12,8},{14,10},{16,20},{18,... | collective-permute-start | bytes 1557512 | tf_op jit(solution)/shard_map/ppermute | solution.py:197
  6.0 1.1 %copy-done.2 = bf16[448,832]{1,0:T(8,128)(2,1)S(1)} copy-done((bf16[448,832]{1,0:T(8,128)(2,1)S(1)}, bf16[448,832]{1,0:T(8,128)(2,1)}, u32[]{:S(2)}) %copy-start.2) | copy-done | bytes 745496
  7.2 0.8 shard_map.118
  7.9 0.1 collective-permute-start
  8.0 0.7 convert_bitcast_fusion.1
  8.7 0.7 stack.21
  9.4 0.7 stack.22
  10.1 0.2 convert_reduce_fusion
  10.3 0.0 copy-start
  10.3 4.1 %copy-done = bf16[4,832,1664]{2,1,0:T(8,128)(2,1)S(1)} copy-done((bf16[4,832,1664]{2,1,0:T(8,128)(2,1)S(1)}, bf16[4,832,1664]{2,1,0:T(8,128)(2,1)}, u32[]{:S(2)}) %copy-start) | copy-done | bytes 11075608
  14.5 3.1 %shard_map.119 = (f32[112,832]{1,0:T(8,128)S(1)}, f32[112,832]{1,0:T(8,128)S(1)}) custom-call(s32[1]{0:T(128)} %bitcast.index_ref, bf16[4,112,832]{2,1,0:T(8,128)(2,1)S(1)} %get-tuple-element.51.picked_ref, bf16[2,832]{1,0:T(2,128)(2,1)S(1)} %pad_maximum_fusion.4.gain_bias_ref, f32[4,112,256]{2,1,0:T(8,128)S(1)} %get-tuple-element.52.refs_0_, ...), custom_call_target="tpu_custom_call" | custom-call | flops 1000 | bytes 1000 | tf_op jit(solution)/shard_map/pallas_call | solution.py:116
  17.6 0.5 collective-permute-done.3
  18.1 0.0 collective-permute-start.10
  18.2 0.1 pad.13.clone
  18.2 2.6 %collective-permute-start.4 = (bf16[104,2496]{1,0:T(8,128)(2,1)}, bf16[104,2496]{1,0:T(8,128)(2,1)}, u32[]{:S(2)}, u32[]{:S(2)}) collective-permute-start(bf16[104,2496]{1,0:T(8,128)(2,1)} %collective-permute-done.1), channel_id=1, source_target_pairs={{0,8},{2,10},{4,12},{6,14},{8,24},{10,26},{12,28},{14,30},{16,0},{... | collective-permute-start | bytes 1557512 | tf_op jit(solution)/shard_map/ppermute | solution.py:194
  20.8 0.5 collective-permute-start.5
  21.4 1.5 %collective-permute-start.6 = (bf16[104,2496]{1,0:T(8,128)(2,1)}, bf16[104,2496]{1,0:T(8,128)(2,1)}, u32[]{:S(2)}, u32[]{:S(2)}) collective-permute-start(bf16[104,2496]{1,0:T(8,128)(2,1)} %collective-permute-done.1), channel_id=1, source_target_pairs={{0,4},{2,6},{4,0},{6,2},{8,12},{10,14},{12,8},{14,10},{16,20},{18,... | collective-permute-start | bytes 1557512 | tf_op jit(solution)/shard_map/ppermute | solution.py:197
  22.8 0.1 copy.18
  23.0 0.0 copy-start.7
  23.0 0.0 copy-start.1
  23.1 1.0 %convolution_convert_fusion = bf16[256,896]{1,0:T(8,128)(2,1)} fusion(bf16[112,2]{1,0:T(8,128)(2,1)S(1)} %copy.18, bf16[112,832]{1,0:T(8,128)(2,1)S(1)} %add_convert_fusion, bf16[896]{0:T(1024)(128)(2,1)S(1)} %pad.13.clone, s32[112]{0:T(128)S(1)} %multiply_add_fusion), kind=kOutput, calls=%fused_computation.9 | convolution fusion | flops 52240384 | bytes 647808 | tf_op jit(solution)/shard_map/dot_general | solution.py:243
  24.1 3.6 %all-to-all-start = ((bf16[16,16,896]{2,1,0:T(8,128)(2,1)}), bf16[16,16,896]{2,1,0:T(8,128)(2,1)S(1)}, u32[]{:S(2)}, u32[]{:S(2)}) async-start(bf16[16,16,896]{2,1,0:T(8,128)(2,1)} %bitcast.5), calls=%async_computation | async-start | bytes 917504 | tf_op jit(solution)/shard_map/all_to_all | solution.py:244
  27.7 1.7 %slice.33 = bf16[104,1280]{1,0:T(8,128)(2,1)} slice(bf16[104,2496]{1,0:T(8,128)(2,1)} %collective-permute-done.3), slice={[0:104], [0:1280]} | slice | bytes 532480 | tf_op jit(solution)/shard_map/slice | solution.py:200
  29.3 1.8 %collective-permute-start.11 = (bf16[104,1280]{1,0:T(8,128)(2,1)}, bf16[104,1280]{1,0:T(8,128)(2,1)S(1)}, u32[]{:S(2)}, u32[]{:S(2)}) collective-permute-start(bf16[104,1280]{1,0:T(8,128)(2,1)} %slice.33), channel_id=1, source_target_pairs={{0,2},{2,0},{4,6},{6,4},{8,10},{10,8},{12,14},{14,12},{16,18},{18,... | collective-permute-start | bytes 798728 | tf_op jit(solution)/shard_map/ppermute | solution.py:200
  31.2 1.5 %collective-permute-start.12 = (bf16[104,1216]{1,0:T(8,128)(2,1)S(1)}, bf16[104,1216]{1,0:T(8,128)(2,1)S(1)}, u32[]{:S(2)}, u32[]{:S(2)}) collective-permute-start(bf16[104,1216]{1,0:T(8,128)(2,1)S(1)} %slice.34), channel_id=1, source_target_pairs={{0,4},{2,6},{4,0},{6,2},{8,12},{10,14},{12,8},{14,10},{16,20},{18,... | collective-permute-start | bytes 758792 | tf_op jit(solution)/shard_map/ppermute | solution.py:201
  32.7 2.5 %pad_maximum_fusion.1 = bf16[312,2496]{1,0:T(8,128)(2,1)} fusion(bf16[104,2496]{1,0:T(8,128)(2,1)} %collective-permute-done.3, bf16[104,2496]{1,0:T(8,128)(2,1)S(1)} %collective-permute-done.2, bf16[104,2496]{1,0:T(8,128)(2,1)} %param.16), kind=kLoop, calls=%fused_computation.5 | loop fusion | flops 4672512 | bytes 3115008 | tf_op jit(solution)/shard_map/concatenate | solution.py:256
  35.2 1.7 %collective-permute-done.4 = bf16[104,2496]{1,0:T(8,128)(2,1)} collective-permute-done((bf16[104,2496]{1,0:T(8,128)(2,1)}, bf16[104,2496]{1,0:T(8,128)(2,1)}, u32[]{:S(2)}, u32[]{:S(2)}) %collective-permute-start.4) | collective-permute-done | bytes 519200 | tf_op jit(solution)/shard_map/ppermute | solution.py:194
  36.9 2.8 %collective-permute-done.6 = bf16[104,2496]{1,0:T(8,128)(2,1)} collective-permute-done((bf16[104,2496]{1,0:T(8,128)(2,1)}, bf16[104,2496]{1,0:T(8,128)(2,1)}, u32[]{:S(2)}, u32[]{:S(2)}) %collective-permute-start.6) | collective-permute-done | bytes 519200 | tf_op jit(solution)/shard_map/ppermute | solution.py:197
  39.6 1.6 %collective-permute-start.8 = (bf16[104,2496]{1,0:T(8,128)(2,1)}, bf16[104,2496]{1,0:T(8,128)(2,1)S(1)}, u32[]{:S(2)}, u32[]{:S(2)}) collective-permute-start(bf16[104,2496]{1,0:T(8,128)(2,1)} %collective-permute-done.4), channel_id=1, source_target_pairs={{0,2},{2,0},{4,6},{6,4},{8,10},{10,8},{12,14},{14,12},{16,18},{18,... | collective-permute-start | bytes 1557512 | tf_op jit(solution)/shard_map/ppermute | solution.py:197
  41.2 2.1 %collective-permute-start.9 = (bf16[104,2496]{1,0:T(8,128)(2,1)}, bf16[104,2496]{1,0:T(8,128)(2,1)}, u32[]{:S(2)}, u32[]{:S(2)}) collective-permute-start(bf16[104,2496]{1,0:T(8,128)(2,1)} %collective-permute-done.4), channel_id=1, source_target_pairs={{0,4},{2,6},{4,0},{6,2},{8,12},{10,14},{12,8},{14,10},{16,20},{18,... | collective-permute-start | bytes 1557512 | tf_op jit(solution)/shard_map/ppermute | solution.py:197
  43.3 0.1 fusion.7
  43.4 0.7 dynamic-slice_bitcast_fusion.order_ref
  44.1 0.8 reshape.62.gain_ref
  44.9 2.2 %collective-permute-done.12 = bf16[104,1216]{1,0:T(8,128)(2,1)S(1)} collective-permute-done((bf16[104,1216]{1,0:T(8,128)(2,1)S(1)}, bf16[104,1216]{1,0:T(8,128)(2,1)S(1)}, u32[]{:S(2)}, u32[]{:S(2)}) %collective-permute-start.12) | collective-permute-done | bytes 252960 | tf_op jit(solution)/shard_map/ppermute | solution.py:201
  47.2 0.7 copy-done.6
  47.9 9.4 %collective-permute-done.8 = bf16[104,2496]{1,0:T(8,128)(2,1)S(1)} collective-permute-done((bf16[104,2496]{1,0:T(8,128)(2,1)}, bf16[104,2496]{1,0:T(8,128)(2,1)S(1)}, u32[]{:S(2)}, u32[]{:S(2)}) %collective-permute-start.8) | collective-permute-done | bytes 519200 | tf_op jit(solution)/shard_map/ppermute | solution.py:197
  57.3 0.4 collective-permute-done.9
  57.6 0.4 copy-done.4
  58.1 1.1 %collective-permute-start.18 = (bf16[104,2496]{1,0:T(8,128)(2,1)}, bf16[104,2496]{1,0:T(8,128)(2,1)S(1)}, u32[]{:S(2)}, u32[]{:S(2)}) collective-permute-start(bf16[104,2496]{1,0:T(8,128)(2,1)} %collective-permute-done.7), channel_id=1, source_target_pairs={{0,2},{2,0},{4,6},{6,4},{8,10},{10,8},{12,14},{14,12},{16,18},{18,... | collective-permute-start | bytes 1557512 | tf_op jit(solution)/shard_map/ppermute | solution.py:197
  59.1 1.5 %collective-permute-start.19 = (bf16[104,2496]{1,0:T(8,128)(2,1)}, bf16[104,2496]{1,0:T(8,128)(2,1)}, u32[]{:S(2)}, u32[]{:S(2)}) collective-permute-start(bf16[104,2496]{1,0:T(8,128)(2,1)} %collective-permute-done.7), channel_id=1, source_target_pairs={{0,4},{2,6},{4,0},{6,2},{8,12},{10,14},{12,8},{14,10},{16,20},{18,... | collective-permute-start | bytes 1557512 | tf_op jit(solution)/shard_map/ppermute | solution.py:197
  60.6 0.8 constant_dynamic-update-slice_fusion.1
  61.4 1.7 %constant_dynamic-update-slice_fusion = bf16[104,2496]{1,0:T(8,128)(2,1)} fusion(bf16[104,2496]{1,0:T(8,128)(2,1)} %constant_dynamic-update-slice_fusion.1, bf16[104,1216]{1,0:T(8,128)(2,1)} %copy-done.6), kind=kLoop, calls=%fused_computation.22 | loop fusion | bytes 532480 | tf_op jit(solution)/shard_map/concatenate | solution.py:260
  63.1 0.5 collective-permute-start.13
  63.6 1.5 %pad_maximum_fusion.2 = bf16[312,2496]{1,0:T(8,128)(2,1)S(1)} fusion(bf16[104,2496]{1,0:T(8,128)(2,1)} %collective-permute-done.9, bf16[104,2496]{1,0:T(8,128)(2,1)} %copy-done.4, bf16[104,2496]{1,0:T(8,128)(2,1)} %collective-permute-done.4), kind=kLoop, calls=%fused_computation.7 | loop fusion | flops 4672512 | bytes 3115008 | tf_op jit(solution)/shard_map/concatenate | solution.py:271
  65.1 1.0 %slice.44 = bf16[104,1280]{1,0:T(8,128)(2,1)S(1)} slice(bf16[104,2496]{1,0:T(8,128)(2,1)} %collective-permute-done.9), slice={[0:104], [0:1280]} | slice | bytes 532480 | tf_op jit(solution)/shard_map/slice | solution.py:200
  66.1 1.7 %pad_maximum_fusion = bf16[416,2496]{1,0:T(8,128)(2,1)S(1)} fusion(bf16[104,2496]{1,0:T(8,128)(2,1)} %constant_dynamic-update-slice_fusion, bf16[104,2496]{1,0:T(8,128)(2,1)} %collective-permute-done.6, bf16[104,2496]{1,0:T(8,128)(2,1)} %collective-permute-done.5, bf16[104,2496]{1,0:T(8,128)(2,1)} %collective-permute-done.1), kind=kLoop, calls=%fused_computation.4 | loop fusion | flops 8306688 | bytes 4153344 | tf_op jit(solution)/shard_map/concatenate | solution.py:261
  67.8 0.0 copy-start.3
  67.8 1.1 %collective-permute-start.14 = (bf16[104,1280]{1,0:T(8,128)(2,1)S(1)}, bf16[104,1280]{1,0:T(8,128)(2,1)S(1)}, u32[]{:S(2)}, u32[]{:S(2)}) collective-permute-start(bf16[104,1280]{1,0:T(8,128)(2,1)S(1)} %slice.44), channel_id=1, source_target_pairs={{0,2},{2,0},{4,6},{6,4},{8,10},{10,8},{12,14},{14,12},{16,18},{18,... | collective-permute-start | bytes 798728 | tf_op jit(solution)/shard_map/ppermute | solution.py:200
  68.9 0.5 collective-permute-start.15
  69.4 1.9 %shard_map.120 = bf16[16,104,512]{2,1,0:T(8,128)(2,1)S(1)} custom-call(s32[1]{0:T(128)} %bitcast.index_ref, s32[16]{0:T(128)S(1)} %dynamic-slice_bitcast_fusion.order_ref, bf16[16,104,1]{2,1,0:T(8,128)(2,1)S(1)} %reshape.62.gain_ref, bf16[832,512]{1,0:T(8,128)(2,1)S(1)} %bitcast.28, bf16[832,512]{1,0:T(8,128)(2,1)S(1)} %collective-permute-done.16.refs_1_, ...), custom_call_target="tpu_custom_call" | custom-call | flops 1000 | bytes 1000 | tf_op jit(solution)/shard_map/pallas_call | solution.py:169
  71.3 0.1 fusion.13
  71.5 1.5 %fusion.14 = f32[512,2496]{0,1:T(8,128)S(1)} fusion(bf16[312,512]{1,0:T(8,128)(2,1)S(1)} %bitcast.31, bf16[312,2496]{1,0:T(8,128)(2,1)S(1)} %copy-done.3), kind=kOutput, calls=%fused_computation.46 | convolution fusion | flops 797442048 | bytes 6988800 | tf_op jit(solution)/shard_map/dot_general | solution.py:278
  73.0 1.5 %convolution_add_fusion.2 = f32[512,2496]{0,1:T(8,128)S(1)} fusion(f32[512,2496]{0,1:T(8,128)S(1)} %fusion.14, bf16[416,512]{1,0:T(8,128)(2,1)S(1)} %bitcast.30, bf16[416,2496]{1,0:T(8,128)(2,1)S(1)} %pad_maximum_fusion), kind=kOutput, calls=%fused_computation.3 | convolution fusion | flops 1064534016 | bytes 12726272 | tf_op jit(solution)/shard_map/dot_general | solution.py:278
  74.6 1.0 %slice.39 = bf16[104,1280]{1,0:T(8,128)(2,1)S(1)} slice(bf16[104,2496]{1,0:T(8,128)(2,1)} %collective-permute-done.19), slice={[0:104], [0:1280]} | slice | bytes 532480 | tf_op jit(solution)/shard_map/slice | solution.py:200
  75.6 1.5 %convolution_add_fusion.1 = f32[512,2496]{0,1:T(8,128)S(1)} fusion(f32[512,2496]{0,1:T(8,128)S(1)} %convolution_add_fusion.2, bf16[312,512]{1,0:T(8,128)(2,1)S(1)} %bitcast.33, bf16[312,2496]{1,0:T(8,128)(2,1)S(1)} %pad_maximum_fusion.2), kind=kOutput, calls=%fused_computation.2 | convolution fusion | flops 798720000 | bytes 12100608 | tf_op jit(solution)/shard_map/dot_general | solution.py:278
  77.1 1.3 %pad_maximum_fusion.3 = bf16[312,2496]{1,0:T(8,128)(2,1)S(1)} fusion(bf16[104,2496]{1,0:T(8,128)(2,1)} %collective-permute-done.19, bf16[104,2496]{1,0:T(8,128)(2,1)S(1)} %collective-permute-done.18, bf16[104,2496]{1,0:T(8,128)(2,1)} %collective-permute-done.7), kind=kLoop, calls=%fused_computation.8 | loop fusion | flops 4672512 | bytes 3115008 | tf_op jit(solution)/shard_map/concatenate | solution.py:271
  78.4 1.1 %collective-permute-start.20 = (bf16[104,1280]{1,0:T(8,128)(2,1)S(1)}, bf16[104,1280]{1,0:T(8,128)(2,1)S(1)}, u32[]{:S(2)}, u32[]{:S(2)}) collective-permute-start(bf16[104,1280]{1,0:T(8,128)(2,1)S(1)} %slice.39), channel_id=1, source_target_pairs={{0,2},{2,0},{4,6},{6,4},{8,10},{10,8},{12,14},{14,12},{16,18},{18,... | collective-permute-start | bytes 798728 | tf_op jit(solution)/shard_map/ppermute | solution.py:200
  79.5 1.5 %collective-permute-start.21 = (bf16[104,1216]{1,0:T(8,128)(2,1)S(1)}, bf16[104,1216]{1,0:T(8,128)(2,1)S(1)}, u32[]{:S(2)}, u32[]{:S(2)}) collective-permute-start(bf16[104,1216]{1,0:T(8,128)(2,1)S(1)} %slice.40), channel_id=1, source_target_pairs={{0,4},{2,6},{4,0},{6,2},{8,12},{10,14},{12,8},{14,10},{16,20},{18,... | collective-permute-start | bytes 758792 | tf_op jit(solution)/shard_map/ppermute | solution.py:201
  81.0 1.6 %convolution_add_fusion = f32[512,2496]{0,1:T(8,128)S(1)} fusion(f32[512,2496]{0,1:T(8,128)S(1)} %convolution_add_fusion.1, bf16[312,512]{1,0:T(8,128)(2,1)S(1)} %bitcast.32, bf16[312,2496]{1,0:T(8,128)(2,1)S(1)} %pad_maximum_fusion.3), kind=kOutput, calls=%fused_computation.1 | convolution fusion | flops 798720000 | bytes 12100608 | tf_op jit(solution)/shard_map/dot_general | solution.py:278
  82.7 4.7 %collective-permute-done.21 = bf16[104,1216]{1,0:T(8,128)(2,1)S(1)} collective-permute-done((bf16[104,1216]{1,0:T(8,128)(2,1)S(1)}, bf16[104,1216]{1,0:T(8,128)(2,1)S(1)}, u32[]{:S(2)}, u32[]{:S(2)}) %collective-permute-start.21) | collective-permute-done | bytes 252960 | tf_op jit(solution)/shard_map/ppermute | solution.py:201
  87.4 1.2 %maximum_maximum_fusion = bf16[312,2496]{1,0:T(8,128)(2,1)S(1)} fusion(bf16[104,1216]{1,0:T(8,128)(2,1)S(1)} %collective-permute-done.21, bf16[104,1280]{1,0:T(8,128)(2,1)S(1)} %collective-permute-done.20, bf16[104,1216]{1,0:T(8,128)(2,1)S(1)} %collective-permute-done.15, bf16[104,1280]{1,0:T(8,128)(2,1)S(1)} %collective-permute-done.14, ...), kind=kLoop, calls=%fused_computation.6 | loop fusion | flops 7787520 | bytes 3115008 | tf_op jit(solution)/shard_map/concatenate | solution.py:271
  88.6 3.1 %select_convert_fusion = bf16[512,2496]{0,1:T(8,128)(2,1)} fusion(f32[512,2496]{0,1:T(8,128)S(1)} %convolution_add_fusion, bf16[312,512]{1,0:T(8,128)(2,1)S(1)} %bitcast.29, bf16[312,2496]{1,0:T(8,128)(2,1)S(1)} %maximum_maximum_fusion, pred[512]{0:T(512)(128)(4,1)S(1)} %fusion.8), kind=kOutput, calls=%fused_computation | convolution fusion | flops 801275904 | bytes 9545216 | tf_op jit(solution)/shard_map/dot_general | solution.py:278
  (41 shorter events, 0.3 us)
Async XLA Ops:
  0.0 17.6 %collective-permute-start.1 = (bf16[104,2496]{1,0:T(8,128)(2,1)}, bf16[104,2496]{1,0:T(8,128)(2,1)}, u32[]{:S(2)}, u32[]{:S(2)}) collective-permute-start(bf16[104,2496]{1,0:T(8,128)(2,1)} %param.16), channel_id=1, source_target_pairs={{0,8},{2,10},{4,12},{6,14},{8,24},{10,26},{12,28},{14,30},{16,0},{... | collective-permute-start | bytes 1557512 | tf_op jit(solution)/shard_map/ppermute | solution.py:194
  3.0 14.6 %collective-permute-start.2 = (bf16[104,2496]{1,0:T(8,128)(2,1)}, bf16[104,2496]{1,0:T(8,128)(2,1)S(1)}, u32[]{:S(2)}, u32[]{:S(2)}) collective-permute-start(bf16[104,2496]{1,0:T(8,128)(2,1)} %param.16), channel_id=1, source_target_pairs={{0,2},{2,0},{4,6},{6,4},{8,10},{10,8},{12,14},{14,12},{16,18},{18,... | collective-permute-start | bytes 1557512 | tf_op jit(solution)/shard_map/ppermute | solution.py:197
  4.5 13.6 %collective-permute-start.3 = (bf16[104,2496]{1,0:T(8,128)(2,1)}, bf16[104,2496]{1,0:T(8,128)(2,1)}, u32[]{:S(2)}, u32[]{:S(2)}) collective-permute-start(bf16[104,2496]{1,0:T(8,128)(2,1)} %param.16), channel_id=1, source_target_pairs={{0,4},{2,6},{4,0},{6,2},{8,12},{10,14},{12,8},{14,10},{16,20},{18,... | collective-permute-start | bytes 1557512 | tf_op jit(solution)/shard_map/ppermute | solution.py:197
  6.0 1.1 %copy-start.2 = (bf16[448,832]{1,0:T(8,128)(2,1)S(1)}, bf16[448,832]{1,0:T(8,128)(2,1)}, u32[]{:S(2)}) copy-start(bf16[448,832]{1,0:T(8,128)(2,1)} %patches_ref.1) | copy-start | bytes 2236420
  7.9 2.4 %collective-permute-start = (f32[4,112,256]{2,1,0:T(8,128)S(1)}, f32[4,112,256]{2,1,0:T(8,128)S(1)}, u32[]{:S(2)}, u32[]{:S(2)}) collective-permute-start(f32[4,112,256]{2,1,0:T(8,128)S(1)} %get-tuple-element.52.refs_0_), channel_id=1, source_target_pairs={{0,1},{1,0},{2,3},{3,2},{4,5},{5,4},{6,7},{7,6},{8,9},{9,8},{10,11... | collective-permute-start | bytes 1376264 | tf_op jit(solution)/shard_map/ppermute | solution.py:26
  10.3 4.1 %copy-start = (bf16[4,832,1664]{2,1,0:T(8,128)(2,1)S(1)}, bf16[4,832,1664]{2,1,0:T(8,128)(2,1)}, u32[]{:S(2)}) copy-start(bf16[4,832,1664]{2,1,0:T(8,128)(2,1)} %refs_2_.1) | copy-start | bytes 33226756
  18.1 4.9 %collective-permute-start.10 = (f32[112,832]{1,0:T(8,128)S(1)}, f32[112,832]{1,0:T(8,128)S(1)}, u32[]{:S(2)}, u32[]{:S(2)}) collective-permute-start(f32[112,832]{1,0:T(8,128)S(1)} %get-tuple-element.59), channel_id=1, source_target_pairs={{0,1},{1,0},{2,3},{3,2},{4,5},{5,4},{6,7},{7,6},{8,9},{9,8},{10,11... | collective-permute-start | bytes 1118216 | tf_op jit(solution)/shard_map/ppermute | solution.py:26
  18.2 18.6 %collective-permute-start.4 = (bf16[104,2496]{1,0:T(8,128)(2,1)}, bf16[104,2496]{1,0:T(8,128)(2,1)}, u32[]{:S(2)}, u32[]{:S(2)}) collective-permute-start(bf16[104,2496]{1,0:T(8,128)(2,1)} %collective-permute-done.1), channel_id=1, source_target_pairs={{0,8},{2,10},{4,12},{6,14},{8,24},{10,26},{12,28},{14,30},{16,0},{... | collective-permute-start | bytes 1557512 | tf_op jit(solution)/shard_map/ppermute | solution.py:194
  20.8 16.0 %collective-permute-start.5 = (bf16[104,2496]{1,0:T(8,128)(2,1)}, bf16[104,2496]{1,0:T(8,128)(2,1)}, u32[]{:S(2)}, u32[]{:S(2)}) collective-permute-start(bf16[104,2496]{1,0:T(8,128)(2,1)} %collective-permute-done.1), channel_id=1, source_target_pairs={{0,2},{2,0},{4,6},{6,4},{8,10},{10,8},{12,14},{14,12},{16,18},{18,... | collective-permute-start | bytes 1557512 | tf_op jit(solution)/shard_map/ppermute | solution.py:197
  21.4 18.3 %collective-permute-start.6 = (bf16[104,2496]{1,0:T(8,128)(2,1)}, bf16[104,2496]{1,0:T(8,128)(2,1)}, u32[]{:S(2)}, u32[]{:S(2)}) collective-permute-start(bf16[104,2496]{1,0:T(8,128)(2,1)} %collective-permute-done.1), channel_id=1, source_target_pairs={{0,4},{2,6},{4,0},{6,2},{8,12},{10,14},{12,8},{14,10},{16,20},{18,... | collective-permute-start | bytes 1557512 | tf_op jit(solution)/shard_map/ppermute | solution.py:197
  23.0 20.4 %copy-start.8 = (s32[2]{0:T(128)S(1)}, s32[2]{0:T(128)}, u32[]{:S(2)}) copy-start(s32[2]{0:T(128)} %param.18) | copy-start | bytes 28
  23.0 21.1 %copy-start.7 = (bf16[1664]{0:T(1024)(128)(2,1)S(1)}, bf16[1664]{0:T(1024)(128)(2,1)}, u32[]{:S(2)}) copy-start(bf16[1664]{0:T(1024)(128)(2,1)} %param.15) | copy-start | bytes 9988
  23.0 24.8 %copy-start.1 = (bf16[512,832]{0,1:T(8,128)(2,1)S(1)}, bf16[512,832]{0,1:T(8,128)(2,1)}, u32[]{:S(2)}) copy-start(bf16[512,832]{0,1:T(8,128)(2,1)} %param.14) | copy-start | bytes 2555908
  24.1 39.5 %all-to-all-start = ((bf16[16,16,896]{2,1,0:T(8,128)(2,1)}), bf16[16,16,896]{2,1,0:T(8,128)(2,1)S(1)}, u32[]{:S(2)}, u32[]{:S(2)}) async-start(bf16[16,16,896]{2,1,0:T(8,128)(2,1)} %bitcast.5), calls=%async_computation | async-start | bytes 917504 | tf_op jit(solution)/shard_map/all_to_all | solution.py:244
  29.3 18.5 %collective-permute-start.11 = (bf16[104,1280]{1,0:T(8,128)(2,1)}, bf16[104,1280]{1,0:T(8,128)(2,1)S(1)}, u32[]{:S(2)}, u32[]{:S(2)}) collective-permute-start(bf16[104,1280]{1,0:T(8,128)(2,1)} %slice.33), channel_id=1, source_target_pairs={{0,2},{2,0},{4,6},{6,4},{8,10},{10,8},{12,14},{14,12},{16,18},{18,... | collective-permute-start | bytes 798728 | tf_op jit(solution)/shard_map/ppermute | solution.py:200
  31.2 16.0 %collective-permute-start.12 = (bf16[104,1216]{1,0:T(8,128)(2,1)S(1)}, bf16[104,1216]{1,0:T(8,128)(2,1)S(1)}, u32[]{:S(2)}, u32[]{:S(2)}) collective-permute-start(bf16[104,1216]{1,0:T(8,128)(2,1)S(1)} %slice.34), channel_id=1, source_target_pairs={{0,4},{2,6},{4,0},{6,2},{8,12},{10,14},{12,8},{14,10},{16,20},{18,... | collective-permute-start | bytes 758792 | tf_op jit(solution)/shard_map/ppermute | solution.py:201
  39.6 17.6 %collective-permute-start.8 = (bf16[104,2496]{1,0:T(8,128)(2,1)}, bf16[104,2496]{1,0:T(8,128)(2,1)S(1)}, u32[]{:S(2)}, u32[]{:S(2)}) collective-permute-start(bf16[104,2496]{1,0:T(8,128)(2,1)} %collective-permute-done.4), channel_id=1, source_target_pairs={{0,2},{2,0},{4,6},{6,4},{8,10},{10,8},{12,14},{14,12},{16,18},{18,... | collective-permute-start | bytes 1557512 | tf_op jit(solution)/shard_map/ppermute | solution.py:197
  41.2 16.4 %collective-permute-start.9 = (bf16[104,2496]{1,0:T(8,128)(2,1)}, bf16[104,2496]{1,0:T(8,128)(2,1)}, u32[]{:S(2)}, u32[]{:S(2)}) collective-permute-start(bf16[104,2496]{1,0:T(8,128)(2,1)} %collective-permute-done.4), channel_id=1, source_target_pairs={{0,4},{2,6},{4,0},{6,2},{8,12},{10,14},{12,8},{14,10},{16,20},{18,... | collective-permute-start | bytes 1557512 | tf_op jit(solution)/shard_map/ppermute | solution.py:197
  43.3 14.8 %collective-permute-start.7 = (bf16[104,2496]{1,0:T(8,128)(2,1)}, bf16[104,2496]{1,0:T(8,128)(2,1)}, u32[]{:S(2)}, u32[]{:S(2)}) collective-permute-start(bf16[104,2496]{1,0:T(8,128)(2,1)} %collective-permute-done.4), channel_id=1, source_target_pairs={{0,8},{2,10},{4,12},{6,14},{8,24},{10,26},{12,28},{14,30},{16,0},{... | collective-permute-start | bytes 1557512 | tf_op jit(solution)/shard_map/ppermute | solution.py:194
  47.2 0.7 copy-start.6
  47.9 19.9 %collective-permute-start.16 = (bf16[832,512]{1,0:T(8,128)(2,1)S(1)}, bf16[832,512]{1,0:T(8,128)(2,1)S(1)}, u32[]{:S(2)}, u32[]{:S(2)}) collective-permute-start(bf16[832,512]{1,0:T(8,128)(2,1)S(1)} %bitcast.27), channel_id=1, source_target_pairs={{0,1},{1,0},{2,3},{3,2},{4,5},{5,4},{6,7},{7,6},{8,9},{9,8},{10,11... | collective-permute-start | bytes 2555912 | tf_op jit(solution)/shard_map/ppermute | solution.py:26
  57.3 0.8 copy-start.4
  58.1 16.5 %collective-permute-start.18 = (bf16[104,2496]{1,0:T(8,128)(2,1)}, bf16[104,2496]{1,0:T(8,128)(2,1)S(1)}, u32[]{:S(2)}, u32[]{:S(2)}) collective-permute-start(bf16[104,2496]{1,0:T(8,128)(2,1)} %collective-permute-done.7), channel_id=1, source_target_pairs={{0,2},{2,0},{4,6},{6,4},{8,10},{10,8},{12,14},{14,12},{16,18},{18,... | collective-permute-start | bytes 1557512 | tf_op jit(solution)/shard_map/ppermute | solution.py:197
  59.1 15.4 %collective-permute-start.19 = (bf16[104,2496]{1,0:T(8,128)(2,1)}, bf16[104,2496]{1,0:T(8,128)(2,1)}, u32[]{:S(2)}, u32[]{:S(2)}) collective-permute-start(bf16[104,2496]{1,0:T(8,128)(2,1)} %collective-permute-done.7), channel_id=1, source_target_pairs={{0,4},{2,6},{4,0},{6,2},{8,12},{10,14},{12,8},{14,10},{16,20},{18,... | collective-permute-start | bytes 1557512 | tf_op jit(solution)/shard_map/ppermute | solution.py:197
  63.1 19.6 %collective-permute-start.13 = (bf16[104,2496]{1,0:T(8,128)(2,1)}, bf16[104,2496]{1,0:T(8,128)(2,1)}, u32[]{:S(2)}, u32[]{:S(2)}) collective-permute-start(bf16[104,2496]{1,0:T(8,128)(2,1)} %constant_dynamic-update-slice_fusion), channel_id=1, source_target_pairs={{0,8},{2,10},{4,12},{6,14},{8,24},{10,26},{12,28},{14,30},{16,0},{... | collective-permute-start | bytes 1557512 | tf_op jit(solution)/shard_map/ppermute | solution.py:194
  63.5 2.5 %copy-start.5 = (bf16[104,2496]{1,0:T(8,128)(2,1)S(1)}, bf16[104,2496]{1,0:T(8,128)(2,1)}, u32[]{:S(2)}) copy-start(bf16[104,2496]{1,0:T(8,128)(2,1)} %copy-done.4) | copy-start | bytes 1557508
  63.6 5.4 %collective-permute-start.17 = (bf16[256,896]{1,0:T(8,128)(2,1)S(1)}, bf16[256,896]{1,0:T(8,128)(2,1)S(1)}, u32[]{:S(2)}, u32[]{:S(2)}) collective-permute-start(bf16[256,896]{1,0:T(8,128)(2,1)S(1)} %bitcast.25), channel_id=1, source_target_pairs={{0,1},{1,0},{2,3},{3,2},{4,5},{5,4},{6,7},{7,6},{8,9},{9,8},{10,11... | collective-permute-start | bytes 1376264 | tf_op jit(solution)/shard_map/ppermute | solution.py:26
  67.8 3.6 %copy-start.3 = (bf16[312,2496]{1,0:T(8,128)(2,1)S(1)}, bf16[312,2496]{1,0:T(8,128)(2,1)}, u32[]{:S(2)}) copy-start(bf16[312,2496]{1,0:T(8,128)(2,1)} %pad_maximum_fusion.1) | copy-start | bytes 4672516
  67.8 14.8 %collective-permute-start.14 = (bf16[104,1280]{1,0:T(8,128)(2,1)S(1)}, bf16[104,1280]{1,0:T(8,128)(2,1)S(1)}, u32[]{:S(2)}, u32[]{:S(2)}) collective-permute-start(bf16[104,1280]{1,0:T(8,128)(2,1)S(1)} %slice.44), channel_id=1, source_target_pairs={{0,2},{2,0},{4,6},{6,4},{8,10},{10,8},{12,14},{14,12},{16,18},{18,... | collective-permute-start | bytes 798728 | tf_op jit(solution)/shard_map/ppermute | solution.py:200
  68.9 13.7 %collective-permute-start.15 = (bf16[104,1216]{1,0:T(8,128)(2,1)S(1)}, bf16[104,1216]{1,0:T(8,128)(2,1)S(1)}, u32[]{:S(2)}, u32[]{:S(2)}) collective-permute-start(bf16[104,1216]{1,0:T(8,128)(2,1)S(1)} %slice.45), channel_id=1, source_target_pairs={{0,4},{2,6},{4,0},{6,2},{8,12},{10,14},{12,8},{14,10},{16,20},{18,... | collective-permute-start | bytes 758792 | tf_op jit(solution)/shard_map/ppermute | solution.py:201
  78.4 9.0 %collective-permute-start.20 = (bf16[104,1280]{1,0:T(8,128)(2,1)S(1)}, bf16[104,1280]{1,0:T(8,128)(2,1)S(1)}, u32[]{:S(2)}, u32[]{:S(2)}) collective-permute-start(bf16[104,1280]{1,0:T(8,128)(2,1)S(1)} %slice.39), channel_id=1, source_target_pairs={{0,2},{2,0},{4,6},{6,4},{8,10},{10,8},{12,14},{14,12},{16,18},{18,... | collective-permute-start | bytes 798728 | tf_op jit(solution)/shard_map/ppermute | solution.py:200
  79.5 7.9 %collective-permute-start.21 = (bf16[104,1216]{1,0:T(8,128)(2,1)S(1)}, bf16[104,1216]{1,0:T(8,128)(2,1)S(1)}, u32[]{:S(2)}, u32[]{:S(2)}) collective-permute-start(bf16[104,1216]{1,0:T(8,128)(2,1)S(1)} %slice.40), channel_id=1, source_target_pairs={{0,4},{2,6},{4,0},{6,2},{8,12},{10,14},{12,8},{14,10},{16,20},{18,... | collective-permute-start | bytes 758792 | tf_op jit(solution)/shard_map/ppermute | solution.py:201

commit v25 on v23

--- a/solution.py
+++ b/solution.py
@@ -210,6 +210,9 @@
     text_turned = text_rows.T
     texts = [text_turned] + [tp_shift(text_turned, n_tp, d) for d in range(1, n_tp)]
 
+    partial_value = merge(tp_index, picked, stats, gain_bias, merge_weight)
+
+    partial_value, held[1], token_pos = tie(partial_value, held[1], token_pos)
     token_count = token_pos.shape[0]
     target = lax.div(token_pos, row_count)
     same = target[:, None] == target[None, :]
@@ -219,12 +222,6 @@
     slot_count = n_req * IMG_CAP
     code = lax.rem(token_pos, row_count) + 1
     code_cols = jnp.stack([lax.div(code, 256), lax.rem(code, 256)], axis=1).astype(jnp.bfloat16)
-
-    partial_value = merge(tp_index, picked, stats, gain_bias, merge_weight)
-
-    partial_value, held[1], sides[0], slot, code_cols = tie(
-        partial_value, held[1], sides[0], slot, code_cols
-    )
     held.append(along_line(held[1]))
     sides.append(to_sides(held[1]))
     merged = partial_value[0]

time: 87.7 us -> 87.7 us (level)
  starting transfers between devices: 28.5 us -> 32.4 us
  waiting for transfers between devices: 19 us -> 15.5 us
    ppermute x4, starting transfers between devices: 8.25 us -> 11.2 us  [along_line(): return lax.ppermute(block, 'req', line_perm)]
    ppermute x3, waiting for transfers between devices: 2.68 us -> 0.01 us  [to_corner(): left = lax.ppermute(by_y[:, :cut], 'req', x_perm)]
    ppermute x4, waiting for transfers between devices: 8.71 us -> 6.49 us  [along_line(): return lax.ppermute(block, 'req', line_perm)]
    ppermute x4, waiting for transfers between devices: 0.01 us -> 1.53 us  [tp_shift(): lax.ppermute(value, 'tp', [(i, (i + distance) % n_tp) for i in range(n_tp)])]
    ppermute x4, waiting for transfers between devices: 1.98 us -> 3.31 us  [to_sides(): lax.ppermute(block, 'req', y_perm)]
    ppermute x4, waiting for transfers between devices: 2.68 us -> 1.5 us  [to_sides(): lax.ppermute(block, 'req', x_perm)]
    unnamed x13 -> x15, local copies, waits for them, and re-layouts: 6.03 us -> 6.05 us
  transfers between devices with their start and end apart: 23 -> 23, of which waited for: 9 -> 7; matrix products, arithmetic and copies ran while one was open for 29% -> 28% of each run, Pallas kernels for 7% -> 7%
where the time goes in v25:
time: 87.7 us; the launch traced here: 87.1 us
  starting transfers between devices  32.4 us (37%)
  waiting for transfers between devices  15.5 us (18%)
  local copies, waits for them, and re-layouts  15.4 us (18%)
  matrix products  10.4 us (12%)
  other arithmetic  7.29 us (8%)
  Pallas kernels  5.77 us (7%)
    ppermute x4, starting transfers between devices, along_line(): return lax.ppermute(block, 'req', line_perm)  11.2 us
    dot_general x5, matrix products, add_product(): lax.dot_general(source, weight, (((0,), (0,)), ((), ())), preferred_eleme...  9.31 us
    ppermute x4, waiting for transfers between devices, along_line(): return lax.ppermute(block, 'req', line_perm)  6.49 us
    ppermute x4, starting transfers between devices, to_sides(): lax.ppermute(block, 'req', y_perm)  6.19 us
    unnamed x15, local copies, waits for them, and re-layouts  6.05 us
    all_to_all x1, starting transfers between devices, shards(): lax.all_to_all(outgoing.reshape(n_req, IMG_CAP, -1), 'req', split_axis=0,...  4.43 us
    ppermute x3, starting transfers between devices, to_corner(): right = lax.ppermute(by_x[:, cut:], 'req', y_perm)  4.14 us
    ppermute x4, starting transfers between devices, to_sides(): lax.ppermute(block, 'req', x_perm)  3.59 us
  transfers between devices with their start and end apart: 23, of which 7 were waited for; matrix products, arithmetic and copies ran while one was open for 28% of the time, Pallas kernels for 7%

profile of v25, /device:TPU:0, one launch (start us, length us, event | category | flops | bytes accessed | tf_op | source)
XLA Modules:
  0.0 87.1 jit_solution(8466774238237504048)
XLA Ops:
  0.0 3.0 %collective-permute-start.1 = (bf16[104,2496]{1,0:T(8,128)(2,1)}, bf16[104,2496]{1,0:T(8,128)(2,1)}, u32[]{:S(2)}, u32[]{:S(2)}) collective-permute-start(bf16[104,2496]{1,0:T(8,128)(2,1)} %param.16), channel_id=1, source_target_pairs={{0,8},{2,10},{4,12},{6,14},{8,24},{10,26},{12,28},{14,30},{16,0},{... | collective-permute-start | bytes 1557512 | tf_op jit(solution)/shard_map/ppermute | solution.py:194
  3.0 1.1 %copy-done.2 = bf16[448,832]{1,0:T(8,128)(2,1)S(1)} copy-done((bf16[448,832]{1,0:T(8,128)(2,1)S(1)}, bf16[448,832]{1,0:T(8,128)(2,1)}, u32[]{:S(2)}) %copy-start.2) | copy-done | bytes 745496
  4.2 0.8 shard_map.100
  4.9 0.1 collective-permute-start
  5.0 1.6 %collective-permute-start.9 = (bf16[104,2496]{1,0:T(8,128)(2,1)}, bf16[104,2496]{1,0:T(8,128)(2,1)}, u32[]{:S(2)}, u32[]{:S(2)}) collective-permute-start(bf16[104,2496]{1,0:T(8,128)(2,1)} %param.16), channel_id=1, source_target_pairs={{0,2},{2,0},{4,6},{6,4},{8,10},{10,8},{12,14},{14,12},{16,18},{18,... | collective-permute-start | bytes 1557512 | tf_op jit(solution)/shard_map/ppermute | solution.py:197
  6.6 1.5 %collective-permute-start.10 = (bf16[104,2496]{1,0:T(8,128)(2,1)}, bf16[104,2496]{1,0:T(8,128)(2,1)}, u32[]{:S(2)}, u32[]{:S(2)}) collective-permute-start(bf16[104,2496]{1,0:T(8,128)(2,1)} %param.16), channel_id=1, source_target_pairs={{0,4},{2,6},{4,0},{6,2},{8,12},{10,14},{12,8},{14,10},{16,20},{18,... | collective-permute-start | bytes 1557512 | tf_op jit(solution)/shard_map/ppermute | solution.py:197
  8.1 0.7 stack.20
  8.8 0.7 stack.19
  9.5 0.1 pad.14.clone
  9.6 0.0 copy-start
  9.6 4.1 %copy-done = bf16[4,832,1664]{2,1,0:T(8,128)(2,1)S(1)} copy-done((bf16[4,832,1664]{2,1,0:T(8,128)(2,1)S(1)}, bf16[4,832,1664]{2,1,0:T(8,128)(2,1)}, u32[]{:S(2)}) %copy-start) | copy-done | bytes 11075608
  13.7 3.2 %shard_map.101 = (f32[112,832]{1,0:T(8,128)S(1)}, f32[112,832]{1,0:T(8,128)S(1)}) custom-call(s32[1]{0:T(128)} %bitcast.index_ref, bf16[4,112,832]{2,1,0:T(8,128)(2,1)S(1)} %get-tuple-element.48.picked_ref, bf16[2,832]{1,0:T(2,128)(2,1)S(1)} %pad_maximum_fusion.4.gain_bias_ref, f32[4,112,256]{2,1,0:T(8,128)S(1)} %get-tuple-element.49.refs_0_, ...), custom_call_target="tpu_custom_call" | custom-call | flops 1000 | bytes 1000 | tf_op jit(solution)/shard_map/pallas_call | solution.py:116
  16.9 2.7 %collective-permute-start.2 = (bf16[104,2496]{1,0:T(8,128)(2,1)}, bf16[104,2496]{1,0:T(8,128)(2,1)}, u32[]{:S(2)}, u32[]{:S(2)}) collective-permute-start(bf16[104,2496]{1,0:T(8,128)(2,1)} %collective-permute-done.1), channel_id=1, source_target_pairs={{0,8},{2,10},{4,12},{6,14},{8,24},{10,26},{12,28},{14,30},{16,0},{... | collective-permute-start | bytes 1557512 | tf_op jit(solution)/shard_map/ppermute | solution.py:194
  19.6 0.5 collective-permute-start.3
  20.1 0.0 collective-permute-start.8
  20.1 0.2 convert_reduce_fusion
  20.3 1.5 %collective-permute-done.8 = f32[112,832]{1,0:T(8,128)S(1)} collective-permute-done((f32[112,832]{1,0:T(8,128)S(1)}, f32[112,832]{1,0:T(8,128)S(1)}, u32[]{:S(2)}, u32[]{:S(2)}) %collective-permute-start.8) | collective-permute-done | bytes 372768 | tf_op jit(solution)/shard_map/ppermute | solution.py:26
  21.8 0.5 collective-permute-start.4
  22.3 0.1 copy.17
  22.5 0.1 copy.16
  22.6 0.0 copy-start.5
  22.7 0.0 copy-start.4
  22.7 0.1 collective-permute-start.16
  22.8 0.0 collective-permute-done.10
  22.8 1.7 %slice.33 = bf16[104,1280]{1,0:T(8,128)(2,1)} slice(bf16[104,2496]{1,0:T(8,128)(2,1)} %collective-permute-done.10), slice={[0:104], [0:1280]} | slice | bytes 532480 | tf_op jit(solution)/shard_map/slice | solution.py:200
  24.5 1.5 %collective-permute-start.11 = (bf16[104,1280]{1,0:T(8,128)(2,1)}, bf16[104,1280]{1,0:T(8,128)(2,1)S(1)}, u32[]{:S(2)}, u32[]{:S(2)}) collective-permute-start(bf16[104,1280]{1,0:T(8,128)(2,1)} %slice.33), channel_id=1, source_target_pairs={{0,2},{2,0},{4,6},{6,4},{8,10},{10,8},{12,14},{14,12},{16,18},{18,... | collective-permute-start | bytes 798728 | tf_op jit(solution)/shard_map/ppermute | solution.py:200
  26.0 1.7 %slice.34 = bf16[104,1216]{1,0:T(8,128)(2,1)} slice(bf16[104,2496]{1,0:T(8,128)(2,1)} %collective-permute-done.9), slice={[0:104], [1280:2496]} | slice | bytes 505856 | tf_op jit(solution)/shard_map/slice | solution.py:201
  27.6 1.1 %convolution_convert_fusion = bf16[256,896]{1,0:T(8,128)(2,1)} fusion(bf16[112,1]{1,0:T(8,128)(2,1)S(1)} %copy.17, bf16[112,1]{1,0:T(8,128)(2,1)S(1)} %copy.16, bf16[112,832]{1,0:T(8,128)(2,1)S(1)} %add_convert_fusion, bf16[896]{0:T(1024)(128)(2,1)S(1)} %pad.14.clone, s32[112]{0:T(128)S(1)} %multiply_add_fusion), kind=kOutput, calls=%fused_computation.9 | convolution fusion | flops 52441088 | bytes 647808 | tf_op jit(solution)/shard_map/dot_general | solution.py:240
  28.7 4.4 %all-to-all-start = ((bf16[16,16,896]{2,1,0:T(8,128)(2,1)}), bf16[16,16,896]{2,1,0:T(8,128)(2,1)S(1)}, u32[]{:S(2)}, u32[]{:S(2)}) async-start(bf16[16,16,896]{2,1,0:T(8,128)(2,1)} %bitcast.5), calls=%async_computation | async-start | bytes 917504 | tf_op jit(solution)/shard_map/all_to_all | solution.py:241
  33.1 2.0 %collective-permute-start.12 = (bf16[104,1216]{1,0:T(8,128)(2,1)}, bf16[104,1216]{1,0:T(8,128)(2,1)}, u32[]{:S(2)}, u32[]{:S(2)}) collective-permute-start(bf16[104,1216]{1,0:T(8,128)(2,1)} %slice.34), channel_id=1, source_target_pairs={{0,4},{2,6},{4,0},{6,2},{8,12},{10,14},{12,8},{14,10},{16,20},{18,... | collective-permute-start | bytes 758792 | tf_op jit(solution)/shard_map/ppermute | solution.py:201
  35.1 1.5 %collective-permute-done.4 = bf16[104,2496]{1,0:T(8,128)(2,1)} collective-permute-done((bf16[104,2496]{1,0:T(8,128)(2,1)}, bf16[104,2496]{1,0:T(8,128)(2,1)}, u32[]{:S(2)}, u32[]{:S(2)}) %collective-permute-start.4) | collective-permute-done | bytes 519200 | tf_op jit(solution)/shard_map/ppermute | solution.py:197
  36.6 3.5 %collective-permute-start.5 = (bf16[104,2496]{1,0:T(8,128)(2,1)}, bf16[104,2496]{1,0:T(8,128)(2,1)}, u32[]{:S(2)}, u32[]{:S(2)}) collective-permute-start(bf16[104,2496]{1,0:T(8,128)(2,1)} %collective-permute-done.2), channel_id=1, source_target_pairs={{0,8},{2,10},{4,12},{6,14},{8,24},{10,26},{12,28},{14,30},{16,0},{... | collective-permute-start | bytes 1557512 | tf_op jit(solution)/shard_map/ppermute | solution.py:194
  40.1 2.6 %pad_maximum_fusion.1 = bf16[312,2496]{1,0:T(8,128)(2,1)} fusion(bf16[104,2496]{1,0:T(8,128)(2,1)} %collective-permute-done.4, bf16[104,2496]{1,0:T(8,128)(2,1)} %collective-permute-done.3, bf16[104,2496]{1,0:T(8,128)(2,1)} %collective-permute-done.1), kind=kLoop, calls=%fused_computation.5 | loop fusion | flops 4672512 | bytes 3115008 | tf_op jit(solution)/shard_map/concatenate | solution.py:255
  42.7 0.1 fusion.9
  42.8 0.7 dynamic-slice_bitcast_fusion.order_ref
  43.5 0.8 reshape.62.gain_ref
  44.3 3.0 %collective-permute-start.7 = (bf16[104,2496]{1,0:T(8,128)(2,1)}, bf16[104,2496]{1,0:T(8,128)(2,1)}, u32[]{:S(2)}, u32[]{:S(2)}) collective-permute-start(bf16[104,2496]{1,0:T(8,128)(2,1)} %collective-permute-done.2), channel_id=1, source_target_pairs={{0,4},{2,6},{4,0},{6,2},{8,12},{10,14},{12,8},{14,10},{16,20},{18,... | collective-permute-start | bytes 1557512 | tf_op jit(solution)/shard_map/ppermute | solution.py:197
  47.4 0.7 constant_dynamic-update-slice_fusion.1
  48.1 1.7 %constant_dynamic-update-slice_fusion = bf16[104,2496]{1,0:T(8,128)(2,1)} fusion(bf16[104,2496]{1,0:T(8,128)(2,1)} %constant_dynamic-update-slice_fusion.1, bf16[104,1216]{1,0:T(8,128)(2,1)} %collective-permute-done.12), kind=kLoop, calls=%fused_computation.24 | loop fusion | bytes 532480 | tf_op jit(solution)/shard_map/concatenate | solution.py:253
  49.8 1.7 %pad_maximum_fusion = bf16[416,2496]{1,0:T(8,128)(2,1)S(1)} fusion(bf16[104,2496]{1,0:T(8,128)(2,1)} %constant_dynamic-update-slice_fusion, bf16[104,2496]{1,0:T(8,128)(2,1)} %collective-permute-done.10, bf16[104,2496]{1,0:T(8,128)(2,1)} %collective-permute-done.9, bf16[104,2496]{1,0:T(8,128)(2,1)} %param.16), kind=kLoop, calls=%fused_computation.4 | loop fusion | flops 8306688 | bytes 4153344 | tf_op jit(solution)/shard_map/concatenate | solution.py:254
  51.5 6.5 %collective-permute-done.5 = bf16[104,2496]{1,0:T(8,128)(2,1)} collective-permute-done((bf16[104,2496]{1,0:T(8,128)(2,1)}, bf16[104,2496]{1,0:T(8,128)(2,1)}, u32[]{:S(2)}, u32[]{:S(2)}) %collective-permute-start.5) | collective-permute-done | bytes 519200 | tf_op jit(solution)/shard_map/ppermute | solution.py:194
  58.0 0.3 collective-permute-done.7
  58.3 1.5 %collective-permute-start.18 = (bf16[104,2496]{1,0:T(8,128)(2,1)}, bf16[104,2496]{1,0:T(8,128)(2,1)S(1)}, u32[]{:S(2)}, u32[]{:S(2)}) collective-permute-start(bf16[104,2496]{1,0:T(8,128)(2,1)} %collective-permute-done.5), channel_id=1, source_target_pairs={{0,2},{2,0},{4,6},{6,4},{8,10},{10,8},{12,14},{14,12},{16,18},{18,... | collective-permute-start | bytes 1557512 | tf_op jit(solution)/shard_map/ppermute | solution.py:197
  59.8 1.1 %collective-permute-start.19 = (bf16[104,2496]{1,0:T(8,128)(2,1)}, bf16[104,2496]{1,0:T(8,128)(2,1)S(1)}, u32[]{:S(2)}, u32[]{:S(2)}) collective-permute-start(bf16[104,2496]{1,0:T(8,128)(2,1)} %collective-permute-done.5), channel_id=1, source_target_pairs={{0,4},{2,6},{4,0},{6,2},{8,12},{10,14},{12,8},{14,10},{16,20},{18,... | collective-permute-start | bytes 1557512 | tf_op jit(solution)/shard_map/ppermute | solution.py:197
  61.0 1.0 %collective-permute-start.15 = (bf16[104,1216]{1,0:T(8,128)(2,1)S(1)}, bf16[104,1216]{1,0:T(8,128)(2,1)S(1)}, u32[]{:S(2)}, u32[]{:S(2)}) collective-permute-start(bf16[104,1216]{1,0:T(8,128)(2,1)S(1)} %slice.36), channel_id=1, source_target_pairs={{0,4},{2,6},{4,0},{6,2},{8,12},{10,14},{12,8},{14,10},{16,20},{18,... | collective-permute-start | bytes 758792 | tf_op jit(solution)/shard_map/ppermute | solution.py:201
  61.9 1.0 %slice.35 = bf16[104,1280]{1,0:T(8,128)(2,1)S(1)} slice(bf16[104,2496]{1,0:T(8,128)(2,1)} %collective-permute-done.7), slice={[0:104], [0:1280]} | slice | bytes 532480 | tf_op jit(solution)/shard_map/slice | solution.py:200
  62.9 1.3 %pad_maximum_fusion.2 = bf16[312,2496]{1,0:T(8,128)(2,1)S(1)} fusion(bf16[104,2496]{1,0:T(8,128)(2,1)} %collective-permute-done.7, bf16[104,2496]{1,0:T(8,128)(2,1)S(1)} %collective-permute-done.6, bf16[104,2496]{1,0:T(8,128)(2,1)} %collective-permute-done.2), kind=kLoop, calls=%fused_computation.7 | loop fusion | flops 4672512 | bytes 3115008 | tf_op jit(solution)/shard_map/concatenate | solution.py:269
  64.3 0.6 collective-permute-start.14
  64.8 2.1 %collective-permute-start.13 = (bf16[104,2496]{1,0:T(8,128)(2,1)}, bf16[104,2496]{1,0:T(8,128)(2,1)S(1)}, u32[]{:S(2)}, u32[]{:S(2)}) collective-permute-start(bf16[104,2496]{1,0:T(8,128)(2,1)} %constant_dynamic-update-slice_fusion), channel_id=1, source_target_pairs={{0,8},{2,10},{4,12},{6,14},{8,24},{10,26},{12,28},{14,30},{16,0},{... | collective-permute-start | bytes 1557512 | tf_op jit(solution)/shard_map/ppermute | solution.py:194
  66.9 1.8 %shard_map.102 = bf16[16,104,512]{2,1,0:T(8,128)(2,1)S(1)} custom-call(s32[1]{0:T(128)} %bitcast.index_ref, s32[16]{0:T(128)S(1)} %dynamic-slice_bitcast_fusion.order_ref, bf16[16,104,1]{2,1,0:T(8,128)(2,1)S(1)} %reshape.62.gain_ref, bf16[832,512]{1,0:T(8,128)(2,1)S(1)} %bitcast.28, bf16[832,512]{1,0:T(8,128)(2,1)S(1)} %collective-permute-done.16.refs_1_, ...), custom_call_target="tpu_custom_call" | custom-call | flops 1000 | bytes 1000 | tf_op jit(solution)/shard_map/pallas_call | solution.py:169
  68.8 0.1 fusion.15
  68.9 0.0 copy-start.3
  68.9 1.5 %fusion.16 = f32[512,2496]{0,1:T(8,128)S(1)} fusion(bf16[416,512]{1,0:T(8,128)(2,1)S(1)} %bitcast.30, bf16[416,2496]{1,0:T(8,128)(2,1)S(1)} %pad_maximum_fusion), kind=kOutput, calls=%fused_computation.47 | convolution fusion | flops 1063256064 | bytes 7614464 | tf_op jit(solution)/shard_map/dot_general | solution.py:276
  70.5 1.6 %convolution_add_fusion.2 = f32[512,2496]{0,1:T(8,128)S(1)} fusion(f32[512,2496]{0,1:T(8,128)S(1)} %fusion.16, bf16[312,512]{1,0:T(8,128)(2,1)S(1)} %bitcast.33, bf16[312,2496]{1,0:T(8,128)(2,1)S(1)} %copy-done.3), kind=kOutput, calls=%fused_computation.3 | convolution fusion | flops 798720000 | bytes 12100608 | tf_op jit(solution)/shard_map/dot_general | solution.py:276
  72.1 1.5 %collective-permute-done.18 = bf16[104,2496]{1,0:T(8,128)(2,1)S(1)} collective-permute-done((bf16[104,2496]{1,0:T(8,128)(2,1)}, bf16[104,2496]{1,0:T(8,128)(2,1)S(1)}, u32[]{:S(2)}, u32[]{:S(2)}) %collective-permute-start.18) | collective-permute-done | bytes 519200 | tf_op jit(solution)/shard_map/ppermute | solution.py:197
  73.6 1.5 %collective-permute-done.19 = bf16[104,2496]{1,0:T(8,128)(2,1)S(1)} collective-permute-done((bf16[104,2496]{1,0:T(8,128)(2,1)}, bf16[104,2496]{1,0:T(8,128)(2,1)S(1)}, u32[]{:S(2)}, u32[]{:S(2)}) %collective-permute-start.19) | collective-permute-done | bytes 519200 | tf_op jit(solution)/shard_map/ppermute | solution.py:197
  75.1 1.2 %collective-permute-start.21 = (bf16[104,1216]{1,0:T(8,128)(2,1)S(1)}, bf16[104,1216]{1,0:T(8,128)(2,1)S(1)}, u32[]{:S(2)}, u32[]{:S(2)}) collective-permute-start(bf16[104,1216]{1,0:T(8,128)(2,1)S(1)} %slice.40), channel_id=1, source_target_pairs={{0,4},{2,6},{4,0},{6,2},{8,12},{10,14},{12,8},{14,10},{16,20},{18,... | collective-permute-start | bytes 758792 | tf_op jit(solution)/shard_map/ppermute | solution.py:201
  76.3 0.6 collective-permute-start.20
  76.9 1.6 %convolution_add_fusion.1 = f32[512,2496]{0,1:T(8,128)S(1)} fusion(f32[512,2496]{0,1:T(8,128)S(1)} %convolution_add_fusion.2, bf16[312,512]{1,0:T(8,128)(2,1)S(1)} %bitcast.32, bf16[312,2496]{1,0:T(8,128)(2,1)S(1)} %pad_maximum_fusion.2), kind=kOutput, calls=%fused_computation.2 | convolution fusion | flops 798720000 | bytes 12100608 | tf_op jit(solution)/shard_map/dot_general | solution.py:276
  78.6 1.2 %pad_maximum_fusion.3 = bf16[312,2496]{1,0:T(8,128)(2,1)S(1)} fusion(bf16[104,2496]{1,0:T(8,128)(2,1)S(1)} %collective-permute-done.19, bf16[104,2496]{1,0:T(8,128)(2,1)S(1)} %collective-permute-done.18, bf16[104,2496]{1,0:T(8,128)(2,1)} %collective-permute-done.5), kind=kLoop, calls=%fused_computation.8 | loop fusion | flops 4672512 | bytes 3115008 | tf_op jit(solution)/shard_map/concatenate | solution.py:269
  79.7 1.5 %convolution_add_fusion = f32[512,2496]{0,1:T(8,128)S(1)} fusion(f32[512,2496]{0,1:T(8,128)S(1)} %convolution_add_fusion.1, bf16[312,512]{1,0:T(8,128)(2,1)S(1)} %bitcast.31, bf16[312,2496]{1,0:T(8,128)(2,1)S(1)} %pad_maximum_fusion.3), kind=kOutput, calls=%fused_computation.1 | convolution fusion | flops 798720000 | bytes 12100608 | tf_op jit(solution)/shard_map/dot_general | solution.py:276
  81.3 2.6 %collective-permute-done.21 = bf16[104,1216]{1,0:T(8,128)(2,1)S(1)} collective-permute-done((bf16[104,1216]{1,0:T(8,128)(2,1)S(1)}, bf16[104,1216]{1,0:T(8,128)(2,1)S(1)}, u32[]{:S(2)}, u32[]{:S(2)}) %collective-permute-start.21) | collective-permute-done | bytes 252960 | tf_op jit(solution)/shard_map/ppermute | solution.py:201
  83.9 0.1 maximum_maximum_fusion
  84.1 3.0 %select_convert_fusion = bf16[512,2496]{0,1:T(8,128)(2,1)} fusion(f32[512,2496]{0,1:T(8,128)S(1)} %convolution_add_fusion, bf16[312,512]{1,0:T(8,128)(2,1)S(1)} %bitcast.29, bf16[312,2496]{1,0:T(8,128)(2,1)S(1)} %maximum_maximum_fusion, pred[512]{0:T(512)(128)(4,1)S(1)} %fusion.10), kind=kOutput, calls=%fused_computation | convolution fusion | flops 801275904 | bytes 9545216 | tf_op jit(solution)/shard_map/dot_general | solution.py:276
  (37 shorter events, 0.3 us)
Async XLA Ops:
  0.0 16.9 %collective-permute-start.1 = (bf16[104,2496]{1,0:T(8,128)(2,1)}, bf16[104,2496]{1,0:T(8,128)(2,1)}, u32[]{:S(2)}, u32[]{:S(2)}) collective-permute-start(bf16[104,2496]{1,0:T(8,128)(2,1)} %param.16), channel_id=1, source_target_pairs={{0,8},{2,10},{4,12},{6,14},{8,24},{10,26},{12,28},{14,30},{16,0},{... | collective-permute-start | bytes 1557512 | tf_op jit(solution)/shard_map/ppermute | solution.py:194
  3.0 1.1 %copy-start.2 = (bf16[448,832]{1,0:T(8,128)(2,1)S(1)}, bf16[448,832]{1,0:T(8,128)(2,1)}, u32[]{:S(2)}) copy-start(bf16[448,832]{1,0:T(8,128)(2,1)} %patches_ref.1) | copy-start | bytes 2236420
  4.9 4.6 %collective-permute-start = (f32[4,112,256]{2,1,0:T(8,128)S(1)}, f32[4,112,256]{2,1,0:T(8,128)S(1)}, u32[]{:S(2)}, u32[]{:S(2)}) collective-permute-start(f32[4,112,256]{2,1,0:T(8,128)S(1)} %get-tuple-element.49.refs_0_), channel_id=1, source_target_pairs={{0,1},{1,0},{2,3},{3,2},{4,5},{5,4},{6,7},{7,6},{8,9},{9,8},{10,11... | collective-permute-start | bytes 1376264 | tf_op jit(solution)/shard_map/ppermute | solution.py:26
  5.0 17.7 %collective-permute-start.9 = (bf16[104,2496]{1,0:T(8,128)(2,1)}, bf16[104,2496]{1,0:T(8,128)(2,1)}, u32[]{:S(2)}, u32[]{:S(2)}) collective-permute-start(bf16[104,2496]{1,0:T(8,128)(2,1)} %param.16), channel_id=1, source_target_pairs={{0,2},{2,0},{4,6},{6,4},{8,10},{10,8},{12,14},{14,12},{16,18},{18,... | collective-permute-start | bytes 1557512 | tf_op jit(solution)/shard_map/ppermute | solution.py:197
  6.6 16.2 %collective-permute-start.10 = (bf16[104,2496]{1,0:T(8,128)(2,1)}, bf16[104,2496]{1,0:T(8,128)(2,1)}, u32[]{:S(2)}, u32[]{:S(2)}) collective-permute-start(bf16[104,2496]{1,0:T(8,128)(2,1)} %param.16), channel_id=1, source_target_pairs={{0,4},{2,6},{4,0},{6,2},{8,12},{10,14},{12,8},{14,10},{16,20},{18,... | collective-permute-start | bytes 1557512 | tf_op jit(solution)/shard_map/ppermute | solution.py:197
  9.6 4.1 %copy-start = (bf16[4,832,1664]{2,1,0:T(8,128)(2,1)S(1)}, bf16[4,832,1664]{2,1,0:T(8,128)(2,1)}, u32[]{:S(2)}) copy-start(bf16[4,832,1664]{2,1,0:T(8,128)(2,1)} %refs_2_.1) | copy-start | bytes 33226756
  13.7 6.4 %copy-start.6 = (s32[112]{0:T(128)S(1)}, s32[112]{0:T(128)}, u32[]{:S(2)}) copy-start(s32[112]{0:T(128)} %param.17) | copy-start | bytes 1348
  13.7 9.0 %copy-start.1 = (bf16[512,832]{0,1:T(8,128)(2,1)S(1)}, bf16[512,832]{0,1:T(8,128)(2,1)}, u32[]{:S(2)}) copy-start(bf16[512,832]{0,1:T(8,128)(2,1)} %param.14) | copy-start | bytes 2555908
  16.9 16.2 %collective-permute-start.2 = (bf16[104,2496]{1,0:T(8,128)(2,1)}, bf16[104,2496]{1,0:T(8,128)(2,1)}, u32[]{:S(2)}, u32[]{:S(2)}) collective-permute-start(bf16[104,2496]{1,0:T(8,128)(2,1)} %collective-permute-done.1), channel_id=1, source_target_pairs={{0,8},{2,10},{4,12},{6,14},{8,24},{10,26},{12,28},{14,30},{16,0},{... | collective-permute-start | bytes 1557512 | tf_op jit(solution)/shard_map/ppermute | solution.py:194
  19.6 15.6 %collective-permute-start.3 = (bf16[104,2496]{1,0:T(8,128)(2,1)}, bf16[104,2496]{1,0:T(8,128)(2,1)}, u32[]{:S(2)}, u32[]{:S(2)}) collective-permute-start(bf16[104,2496]{1,0:T(8,128)(2,1)} %collective-permute-done.1), channel_id=1, source_target_pairs={{0,2},{2,0},{4,6},{6,4},{8,10},{10,8},{12,14},{14,12},{16,18},{18,... | collective-permute-start | bytes 1557512 | tf_op jit(solution)/shard_map/ppermute | solution.py:197
  20.1 1.7 %collective-permute-start.8 = (f32[112,832]{1,0:T(8,128)S(1)}, f32[112,832]{1,0:T(8,128)S(1)}, u32[]{:S(2)}, u32[]{:S(2)}) collective-permute-start(f32[112,832]{1,0:T(8,128)S(1)} %get-tuple-element.56), channel_id=1, source_target_pairs={{0,1},{1,0},{2,3},{3,2},{4,5},{5,4},{6,7},{7,6},{8,9},{9,8},{10,11... | collective-permute-start | bytes 1118216 | tf_op jit(solution)/shard_map/ppermute | solution.py:26
  21.8 14.8 %collective-permute-start.4 = (bf16[104,2496]{1,0:T(8,128)(2,1)}, bf16[104,2496]{1,0:T(8,128)(2,1)}, u32[]{:S(2)}, u32[]{:S(2)}) collective-permute-start(bf16[104,2496]{1,0:T(8,128)(2,1)} %collective-permute-done.1), channel_id=1, source_target_pairs={{0,4},{2,6},{4,0},{6,2},{8,12},{10,14},{12,8},{14,10},{16,20},{18,... | collective-permute-start | bytes 1557512 | tf_op jit(solution)/shard_map/ppermute | solution.py:197
  22.6 20.1 %copy-start.5 = (s32[2]{0:T(128)S(1)}, s32[2]{0:T(128)}, u32[]{:S(2)}) copy-start(s32[2]{0:T(128)} %param.18) | copy-start | bytes 28
  22.7 20.9 %copy-start.4 = (bf16[1664]{0:T(1024)(128)(2,1)S(1)}, bf16[1664]{0:T(1024)(128)(2,1)}, u32[]{:S(2)}) copy-start(bf16[1664]{0:T(1024)(128)(2,1)} %param.15) | copy-start | bytes 9988
  22.7 41.6 %collective-permute-start.16 = (bf16[832,512]{1,0:T(8,128)(2,1)S(1)}, bf16[832,512]{1,0:T(8,128)(2,1)S(1)}, u32[]{:S(2)}, u32[]{:S(2)}) collective-permute-start(bf16[832,512]{1,0:T(8,128)(2,1)S(1)} %bitcast.27), channel_id=1, source_target_pairs={{0,1},{1,0},{2,3},{3,2},{4,5},{5,4},{6,7},{7,6},{8,9},{9,8},{10,11... | collective-permute-start | bytes 2555912 | tf_op jit(solution)/shard_map/ppermute | solution.py:26
  24.5 19.9 %collective-permute-start.11 = (bf16[104,1280]{1,0:T(8,128)(2,1)}, bf16[104,1280]{1,0:T(8,128)(2,1)S(1)}, u32[]{:S(2)}, u32[]{:S(2)}) collective-permute-start(bf16[104,1280]{1,0:T(8,128)(2,1)} %slice.33), channel_id=1, source_target_pairs={{0,2},{2,0},{4,6},{6,4},{8,10},{10,8},{12,14},{14,12},{16,18},{18,... | collective-permute-start | bytes 798728 | tf_op jit(solution)/shard_map/ppermute | solution.py:200
  28.7 21.1 %all-to-all-start = ((bf16[16,16,896]{2,1,0:T(8,128)(2,1)}), bf16[16,16,896]{2,1,0:T(8,128)(2,1)S(1)}, u32[]{:S(2)}, u32[]{:S(2)}) async-start(bf16[16,16,896]{2,1,0:T(8,128)(2,1)} %bitcast.5), calls=%async_computation | async-start | bytes 917504 | tf_op jit(solution)/shard_map/all_to_all | solution.py:241
  33.1 15.0 %collective-permute-start.12 = (bf16[104,1216]{1,0:T(8,128)(2,1)}, bf16[104,1216]{1,0:T(8,128)(2,1)}, u32[]{:S(2)}, u32[]{:S(2)}) collective-permute-start(bf16[104,1216]{1,0:T(8,128)(2,1)} %slice.34), channel_id=1, source_target_pairs={{0,4},{2,6},{4,0},{6,2},{8,12},{10,14},{12,8},{14,10},{16,20},{18,... | collective-permute-start | bytes 758792 | tf_op jit(solution)/shard_map/ppermute | solution.py:201
  36.6 21.4 %collective-permute-start.5 = (bf16[104,2496]{1,0:T(8,128)(2,1)}, bf16[104,2496]{1,0:T(8,128)(2,1)}, u32[]{:S(2)}, u32[]{:S(2)}) collective-permute-start(bf16[104,2496]{1,0:T(8,128)(2,1)} %collective-permute-done.2), channel_id=1, source_target_pairs={{0,8},{2,10},{4,12},{6,14},{8,24},{10,26},{12,28},{14,30},{16,0},{... | collective-permute-start | bytes 1557512 | tf_op jit(solution)/shard_map/ppermute | solution.py:194
  40.1 17.9 %collective-permute-start.6 = (bf16[104,2496]{1,0:T(8,128)(2,1)}, bf16[104,2496]{1,0:T(8,128)(2,1)S(1)}, u32[]{:S(2)}, u32[]{:S(2)}) collective-permute-start(bf16[104,2496]{1,0:T(8,128)(2,1)} %collective-permute-done.2), channel_id=1, source_target_pairs={{0,2},{2,0},{4,6},{6,4},{8,10},{10,8},{12,14},{14,12},{16,18},{18,... | collective-permute-start | bytes 1557512 | tf_op jit(solution)/shard_map/ppermute | solution.py:197
  44.3 14.0 %collective-permute-start.7 = (bf16[104,2496]{1,0:T(8,128)(2,1)}, bf16[104,2496]{1,0:T(8,128)(2,1)}, u32[]{:S(2)}, u32[]{:S(2)}) collective-permute-start(bf16[104,2496]{1,0:T(8,128)(2,1)} %collective-permute-done.2), channel_id=1, source_target_pairs={{0,4},{2,6},{4,0},{6,2},{8,12},{10,14},{12,8},{14,10},{16,20},{18,... | collective-permute-start | bytes 1557512 | tf_op jit(solution)/shard_map/ppermute | solution.py:197
  49.8 15.0 %collective-permute-start.17 = (bf16[256,896]{1,0:T(8,128)(2,1)S(1)}, bf16[256,896]{1,0:T(8,128)(2,1)S(1)}, u32[]{:S(2)}, u32[]{:S(2)}) collective-permute-start(bf16[256,896]{1,0:T(8,128)(2,1)S(1)} %bitcast.25), channel_id=1, source_target_pairs={{0,1},{1,0},{2,3},{3,2},{4,5},{5,4},{6,7},{7,6},{8,9},{9,8},{10,11... | collective-permute-start | bytes 1376264 | tf_op jit(solution)/shard_map/ppermute | solution.py:26
  58.3 15.2 %collective-permute-start.18 = (bf16[104,2496]{1,0:T(8,128)(2,1)}, bf16[104,2496]{1,0:T(8,128)(2,1)S(1)}, u32[]{:S(2)}, u32[]{:S(2)}) collective-permute-start(bf16[104,2496]{1,0:T(8,128)(2,1)} %collective-permute-done.5), channel_id=1, source_target_pairs={{0,2},{2,0},{4,6},{6,4},{8,10},{10,8},{12,14},{14,12},{16,18},{18,... | collective-permute-start | bytes 1557512 | tf_op jit(solution)/shard_map/ppermute | solution.py:197
  59.8 15.2 %collective-permute-start.19 = (bf16[104,2496]{1,0:T(8,128)(2,1)}, bf16[104,2496]{1,0:T(8,128)(2,1)S(1)}, u32[]{:S(2)}, u32[]{:S(2)}) collective-permute-start(bf16[104,2496]{1,0:T(8,128)(2,1)} %collective-permute-done.5), channel_id=1, source_target_pairs={{0,4},{2,6},{4,0},{6,2},{8,12},{10,14},{12,8},{14,10},{16,20},{18,... | collective-permute-start | bytes 1557512 | tf_op jit(solution)/shard_map/ppermute | solution.py:197
  61.0 20.3 %collective-permute-start.15 = (bf16[104,1216]{1,0:T(8,128)(2,1)S(1)}, bf16[104,1216]{1,0:T(8,128)(2,1)S(1)}, u32[]{:S(2)}, u32[]{:S(2)}) collective-permute-start(bf16[104,1216]{1,0:T(8,128)(2,1)S(1)} %slice.36), channel_id=1, source_target_pairs={{0,4},{2,6},{4,0},{6,2},{8,12},{10,14},{12,8},{14,10},{16,20},{18,... | collective-permute-start | bytes 758792 | tf_op jit(solution)/shard_map/ppermute | solution.py:201
  64.3 17.0 %collective-permute-start.14 = (bf16[104,1280]{1,0:T(8,128)(2,1)S(1)}, bf16[104,1280]{1,0:T(8,128)(2,1)S(1)}, u32[]{:S(2)}, u32[]{:S(2)}) collective-permute-start(bf16[104,1280]{1,0:T(8,128)(2,1)S(1)} %slice.35), channel_id=1, source_target_pairs={{0,2},{2,0},{4,6},{6,4},{8,10},{10,8},{12,14},{14,12},{16,18},{18,... | collective-permute-start | bytes 798728 | tf_op jit(solution)/shard_map/ppermute | solution.py:200
  64.8 16.5 %collective-permute-start.13 = (bf16[104,2496]{1,0:T(8,128)(2,1)}, bf16[104,2496]{1,0:T(8,128)(2,1)S(1)}, u32[]{:S(2)}, u32[]{:S(2)}) collective-permute-start(bf16[104,2496]{1,0:T(8,128)(2,1)} %constant_dynamic-update-slice_fusion), channel_id=1, source_target_pairs={{0,8},{2,10},{4,12},{6,14},{8,24},{10,26},{12,28},{14,30},{16,0},{... | collective-permute-start | bytes 1557512 | tf_op jit(solution)/shard_map/ppermute | solution.py:194
  68.9 1.6 %copy-start.3 = (bf16[312,2496]{1,0:T(8,128)(2,1)S(1)}, bf16[312,2496]{1,0:T(8,128)(2,1)}, u32[]{:S(2)}) copy-start(bf16[312,2496]{1,0:T(8,128)(2,1)} %pad_maximum_fusion.1) | copy-start | bytes 4672516
  75.1 8.8 %collective-permute-start.21 = (bf16[104,1216]{1,0:T(8,128)(2,1)S(1)}, bf16[104,1216]{1,0:T(8,128)(2,1)S(1)}, u32[]{:S(2)}, u32[]{:S(2)}) collective-permute-start(bf16[104,1216]{1,0:T(8,128)(2,1)S(1)} %slice.40), channel_id=1, source_target_pairs={{0,4},{2,6},{4,0},{6,2},{8,12},{10,14},{12,8},{14,10},{16,20},{18,... | collective-permute-start | bytes 758792 | tf_op jit(solution)/shard_map/ppermute | solution.py:201
  76.3 7.6 %collective-permute-start.20 = (bf16[104,1280]{1,0:T(8,128)(2,1)S(1)}, bf16[104,1280]{1,0:T(8,128)(2,1)S(1)}, u32[]{:S(2)}, u32[]{:S(2)}) collective-permute-start(bf16[104,1280]{1,0:T(8,128)(2,1)S(1)} %slice.39), channel_id=1, source_target_pairs={{0,2},{2,0},{4,6},{6,4},{8,10},{10,8},{12,14},{14,12},{16,18},{18,... | collective-permute-start | bytes 798728 | tf_op jit(solution)/shard_map/ppermute | solution.py:200

commit v26 on v25

--- a/solution.py
+++ b/solution.py
@@ -242,7 +242,7 @@
         outgoing.reshape(n_req, IMG_CAP, -1), "req", split_axis=0, concat_axis=0
     ).reshape(slot_count, -1)
 
-    held[2], sides[1], norm_gain, me = tie(held[2], sides[1], norm_gain, me)
+    held[2], norm_gain, me = tie(held[2], norm_gain, me)
     gain_column = norm_gain.reshape(n_req, rows, 1)
     order = lax.dynamic_slice_in_dim(jnp.asarray(table), me, 1, 0).reshape(-1)
     held.append(along_line(held[2]))

time: 87.7 us -> 87.4 us (level)
  starting transfers between devices: 32.4 us -> 31.1 us
  waiting for transfers between devices: 15.5 us -> 16.6 us
    ppermute x3, waiting for transfers between devices: 0.01 us -> 3.57 us  [to_corner(): left = lax.ppermute(by_y[:, :cut], 'req', x_perm)]
    ppermute x4, starting transfers between devices: 11.2 us -> 9.18 us  [along_line(): return lax.ppermute(block, 'req', line_perm)]
    ppermute x4, waiting for transfers between devices: 3.31 us -> 1.43 us  [to_sides(): lax.ppermute(block, 'req', y_perm)]
    ppermute x3, starting transfers between devices: 2.71 us -> 4.1 us  [to_corner(): left = lax.ppermute(by_y[:, :cut], 'req', x_perm)]
    ppermute x4, waiting for transfers between devices: 1.5 us -> 2.55 us  [to_sides(): lax.ppermute(block, 'req', x_perm)]
    ppermute x4, starting transfers between devices: 6.19 us -> 5.18 us  [to_sides(): lax.ppermute(block, 'req', y_perm)]
    ppermute x3, waiting for transfers between devices: 2.63 us -> 1.71 us  [to_corner(): right = lax.ppermute(by_x[:, cut:], 'req', y_perm)]
  transfers between devices with their start and end apart: 23 -> 23, of which waited for: 7 -> 9; matrix products, arithmetic and copies ran while one was open for 28% -> 28% of each run, Pallas kernels for 7% -> 7%
where the time goes in v26:
time: 87.4 us; the launch traced here: 86.8 us
  starting transfers between devices  31.1 us (36%)
  waiting for transfers between devices  16.6 us (19%)
  local copies, waits for them, and re-layouts  15.4 us (18%)
  matrix products  10.4 us (12%)
  other arithmetic  7.3 us (8%)
  Pallas kernels  5.72 us (7%)
    dot_general x5, matrix products, add_product(): lax.dot_general(source, weight, (((0,), (0,)), ((), ())), preferred_eleme...  9.32 us
    ppermute x4, starting transfers between devices, along_line(): return lax.ppermute(block, 'req', line_perm)  9.18 us
    ppermute x4, waiting for transfers between devices, along_line(): return lax.ppermute(block, 'req', line_perm)  6.09 us
    unnamed x15, local copies, waits for them, and re-layouts  6.05 us
    ppermute x4, starting transfers between devices, to_sides(): lax.ppermute(block, 'req', y_perm)  5.18 us
    all_to_all x1, starting transfers between devices, shards(): lax.all_to_all(outgoing.reshape(n_req, IMG_CAP, -1), 'req', split_axis=0,...  4.49 us
    ppermute x3, starting transfers between devices, to_corner(): right = lax.ppermute(by_x[:, cut:], 'req', y_perm)  4.14 us
    ppermute x3, starting transfers between devices, to_corner(): left = lax.ppermute(by_y[:, :cut], 'req', x_perm)  4.1 us
  transfers between devices with their start and end apart: 23, of which 9 were waited for; matrix products, arithmetic and copies ran while one was open for 28% of the time, Pallas kernels for 7%

profile of v26, /device:TPU:0, one launch (start us, length us, event | category | flops | bytes accessed | tf_op | source)
XLA Modules:
  0.0 86.8 jit_solution(10298344691042266306)
XLA Ops:
  0.0 3.0 %collective-permute-start.1 = (bf16[104,2496]{1,0:T(8,128)(2,1)}, bf16[104,2496]{1,0:T(8,128)(2,1)}, u32[]{:S(2)}, u32[]{:S(2)}) collective-permute-start(bf16[104,2496]{1,0:T(8,128)(2,1)} %param.16), channel_id=1, source_target_pairs={{0,8},{2,10},{4,12},{6,14},{8,24},{10,26},{12,28},{14,30},{16,0},{... | collective-permute-start | bytes 1557512 | tf_op jit(solution)/shard_map/ppermute | solution.py:194
  3.0 1.1 %copy-done.2 = bf16[448,832]{1,0:T(8,128)(2,1)S(1)} copy-done((bf16[448,832]{1,0:T(8,128)(2,1)S(1)}, bf16[448,832]{1,0:T(8,128)(2,1)}, u32[]{:S(2)}) %copy-start.2) | copy-done | bytes 745496
  4.2 0.8 shard_map.100
  4.9 0.1 collective-permute-start
  5.0 1.6 %collective-permute-start.7 = (bf16[104,2496]{1,0:T(8,128)(2,1)}, bf16[104,2496]{1,0:T(8,128)(2,1)}, u32[]{:S(2)}, u32[]{:S(2)}) collective-permute-start(bf16[104,2496]{1,0:T(8,128)(2,1)} %param.16), channel_id=1, source_target_pairs={{0,2},{2,0},{4,6},{6,4},{8,10},{10,8},{12,14},{14,12},{16,18},{18,... | collective-permute-start | bytes 1557512 | tf_op jit(solution)/shard_map/ppermute | solution.py:197
  6.6 1.5 %collective-permute-start.8 = (bf16[104,2496]{1,0:T(8,128)(2,1)}, bf16[104,2496]{1,0:T(8,128)(2,1)}, u32[]{:S(2)}, u32[]{:S(2)}) collective-permute-start(bf16[104,2496]{1,0:T(8,128)(2,1)} %param.16), channel_id=1, source_target_pairs={{0,4},{2,6},{4,0},{6,2},{8,12},{10,14},{12,8},{14,10},{16,20},{18,... | collective-permute-start | bytes 1557512 | tf_op jit(solution)/shard_map/ppermute | solution.py:197
  8.1 0.7 stack.20
  8.8 0.7 stack.19
  9.5 0.1 pad.14.clone
  9.6 4.1 %copy-done = bf16[4,832,1664]{2,1,0:T(8,128)(2,1)S(1)} copy-done((bf16[4,832,1664]{2,1,0:T(8,128)(2,1)S(1)}, bf16[4,832,1664]{2,1,0:T(8,128)(2,1)}, u32[]{:S(2)}) %copy-start) | copy-done | bytes 11075608
  13.7 3.1 %shard_map.101 = (f32[112,832]{1,0:T(8,128)S(1)}, f32[112,832]{1,0:T(8,128)S(1)}) custom-call(s32[1]{0:T(128)} %bitcast.index_ref, bf16[4,112,832]{2,1,0:T(8,128)(2,1)S(1)} %get-tuple-element.46.picked_ref, bf16[2,832]{1,0:T(2,128)(2,1)S(1)} %pad_maximum_fusion.4.gain_bias_ref, f32[4,112,256]{2,1,0:T(8,128)S(1)} %get-tuple-element.47.refs_0_, ...), custom_call_target="tpu_custom_call" | custom-call | flops 1000 | bytes 1000 | tf_op jit(solution)/shard_map/pallas_call | solution.py:116
  16.9 2.6 %collective-permute-start.2 = (bf16[104,2496]{1,0:T(8,128)(2,1)}, bf16[104,2496]{1,0:T(8,128)(2,1)}, u32[]{:S(2)}, u32[]{:S(2)}) collective-permute-start(bf16[104,2496]{1,0:T(8,128)(2,1)} %collective-permute-done.1), channel_id=1, source_target_pairs={{0,8},{2,10},{4,12},{6,14},{8,24},{10,26},{12,28},{14,30},{16,0},{... | collective-permute-start | bytes 1557512 | tf_op jit(solution)/shard_map/ppermute | solution.py:194
  19.5 0.5 collective-permute-start.12
  20.0 0.2 convert_reduce_fusion
  20.2 0.1 copy.17
  20.4 0.1 copy.16
  20.5 1.3 %collective-permute-done.6 = f32[112,832]{1,0:T(8,128)S(1)} collective-permute-done((f32[112,832]{1,0:T(8,128)S(1)}, f32[112,832]{1,0:T(8,128)S(1)}, u32[]{:S(2)}, u32[]{:S(2)}) %collective-permute-start.6) | collective-permute-done | bytes 372768 | tf_op jit(solution)/shard_map/ppermute | solution.py:26
  21.7 0.5 collective-permute-start.11
  22.3 0.1 add_convert_fusion
  22.4 0.0 copy-start.4
  22.4 0.1 collective-permute-start.16
  22.5 1.7 %slice.33 = bf16[104,1280]{1,0:T(8,128)(2,1)} slice(bf16[104,2496]{1,0:T(8,128)(2,1)} %collective-permute-done.8), slice={[0:104], [0:1280]} | slice | bytes 532480 | tf_op jit(solution)/shard_map/slice | solution.py:200
  24.1 1.5 %collective-permute-start.9 = (bf16[104,1280]{1,0:T(8,128)(2,1)}, bf16[104,1280]{1,0:T(8,128)(2,1)S(1)}, u32[]{:S(2)}, u32[]{:S(2)}) collective-permute-start(bf16[104,1280]{1,0:T(8,128)(2,1)} %slice.33), channel_id=1, source_target_pairs={{0,2},{2,0},{4,6},{6,4},{8,10},{10,8},{12,14},{14,12},{16,18},{18,... | collective-permute-start | bytes 798728 | tf_op jit(solution)/shard_map/ppermute | solution.py:200
  25.6 1.7 %slice.34 = bf16[104,1216]{1,0:T(8,128)(2,1)} slice(bf16[104,2496]{1,0:T(8,128)(2,1)} %collective-permute-done.7), slice={[0:104], [1280:2496]} | slice | bytes 505856 | tf_op jit(solution)/shard_map/slice | solution.py:201
  27.3 1.1 %convolution_convert_fusion = bf16[256,896]{1,0:T(8,128)(2,1)} fusion(bf16[112,1]{1,0:T(8,128)(2,1)S(1)} %copy.17, bf16[112,1]{1,0:T(8,128)(2,1)S(1)} %copy.16, bf16[112,832]{1,0:T(8,128)(2,1)S(1)} %add_convert_fusion, bf16[896]{0:T(1024)(128)(2,1)S(1)} %pad.14.clone, s32[112]{0:T(128)S(1)} %multiply_add_fusion), kind=kOutput, calls=%fused_computation.9 | convolution fusion | flops 52441088 | bytes 647808 | tf_op jit(solution)/shard_map/dot_general | solution.py:240
  28.4 4.5 %all-to-all-start = ((bf16[16,16,896]{2,1,0:T(8,128)(2,1)}), bf16[16,16,896]{2,1,0:T(8,128)(2,1)S(1)}, u32[]{:S(2)}, u32[]{:S(2)}) async-start(bf16[16,16,896]{2,1,0:T(8,128)(2,1)} %bitcast.5), calls=%async_computation | async-start | bytes 917504 | tf_op jit(solution)/shard_map/all_to_all | solution.py:241
  32.9 2.0 %collective-permute-start.10 = (bf16[104,1216]{1,0:T(8,128)(2,1)}, bf16[104,1216]{1,0:T(8,128)(2,1)}, u32[]{:S(2)}, u32[]{:S(2)}) collective-permute-start(bf16[104,1216]{1,0:T(8,128)(2,1)} %slice.34), channel_id=1, source_target_pairs={{0,4},{2,6},{4,0},{6,2},{8,12},{10,14},{12,8},{14,10},{16,20},{18,... | collective-permute-start | bytes 758792 | tf_op jit(solution)/shard_map/ppermute | solution.py:201
  34.9 1.5 %collective-permute-start.3 = (bf16[104,2496]{1,0:T(8,128)(2,1)}, bf16[104,2496]{1,0:T(8,128)(2,1)}, u32[]{:S(2)}, u32[]{:S(2)}) collective-permute-start(bf16[104,2496]{1,0:T(8,128)(2,1)} %collective-permute-done.2), channel_id=1, source_target_pairs={{0,8},{2,10},{4,12},{6,14},{8,24},{10,26},{12,28},{14,30},{16,0},{... | collective-permute-start | bytes 1557512 | tf_op jit(solution)/shard_map/ppermute | solution.py:194
  36.4 0.6 collective-permute-done.11
  37.0 0.9 collective-permute-start.4
  37.9 2.6 %pad_maximum_fusion.1 = bf16[312,2496]{1,0:T(8,128)(2,1)} fusion(bf16[104,2496]{1,0:T(8,128)(2,1)} %collective-permute-done.12, bf16[104,2496]{1,0:T(8,128)(2,1)} %collective-permute-done.11, bf16[104,2496]{1,0:T(8,128)(2,1)} %collective-permute-done.1), kind=kLoop, calls=%fused_computation.5 | loop fusion | flops 4672512 | bytes 3115008 | tf_op jit(solution)/shard_map/concatenate | solution.py:255
  40.5 0.1 fusion.9
  40.6 0.7 dynamic-slice_bitcast_fusion.order_ref
  41.3 0.8 reshape.62.gain_ref
  42.1 3.6 %collective-permute-done.9 = bf16[104,1280]{1,0:T(8,128)(2,1)S(1)} collective-permute-done((bf16[104,1280]{1,0:T(8,128)(2,1)}, bf16[104,1280]{1,0:T(8,128)(2,1)S(1)}, u32[]{:S(2)}, u32[]{:S(2)}) %collective-permute-start.9) | collective-permute-done | bytes 266272 | tf_op jit(solution)/shard_map/ppermute | solution.py:200
  45.7 1.9 %collective-permute-start.5 = (bf16[104,2496]{1,0:T(8,128)(2,1)}, bf16[104,2496]{1,0:T(8,128)(2,1)}, u32[]{:S(2)}, u32[]{:S(2)}) collective-permute-start(bf16[104,2496]{1,0:T(8,128)(2,1)} %collective-permute-done.2), channel_id=1, source_target_pairs={{0,4},{2,6},{4,0},{6,2},{8,12},{10,14},{12,8},{14,10},{16,20},{18,... | collective-permute-start | bytes 1557512 | tf_op jit(solution)/shard_map/ppermute | solution.py:197
  47.5 0.7 constant_dynamic-update-slice_fusion.1
  48.3 1.7 %constant_dynamic-update-slice_fusion = bf16[104,2496]{1,0:T(8,128)(2,1)} fusion(bf16[104,2496]{1,0:T(8,128)(2,1)} %constant_dynamic-update-slice_fusion.1, bf16[104,1216]{1,0:T(8,128)(2,1)} %collective-permute-done.10), kind=kLoop, calls=%fused_computation.24 | loop fusion | bytes 532480 | tf_op jit(solution)/shard_map/concatenate | solution.py:253
  50.0 1.7 %pad_maximum_fusion = bf16[416,2496]{1,0:T(8,128)(2,1)S(1)} fusion(bf16[104,2496]{1,0:T(8,128)(2,1)} %constant_dynamic-update-slice_fusion, bf16[104,2496]{1,0:T(8,128)(2,1)} %collective-permute-done.8, bf16[104,2496]{1,0:T(8,128)(2,1)} %collective-permute-done.7, bf16[104,2496]{1,0:T(8,128)(2,1)} %param.16), kind=kLoop, calls=%fused_computation.4 | loop fusion | flops 8306688 | bytes 4153344 | tf_op jit(solution)/shard_map/concatenate | solution.py:254
  51.7 6.1 %collective-permute-done.3 = bf16[104,2496]{1,0:T(8,128)(2,1)} collective-permute-done((bf16[104,2496]{1,0:T(8,128)(2,1)}, bf16[104,2496]{1,0:T(8,128)(2,1)}, u32[]{:S(2)}, u32[]{:S(2)}) %collective-permute-start.3) | collective-permute-done | bytes 519200 | tf_op jit(solution)/shard_map/ppermute | solution.py:194
  57.7 0.4 collective-permute-done.4
  58.1 0.6 collective-permute-done.5
  58.7 0.9 collective-permute-start.18
  59.5 1.3 %collective-permute-start.19 = (bf16[104,2496]{1,0:T(8,128)(2,1)}, bf16[104,2496]{1,0:T(8,128)(2,1)S(1)}, u32[]{:S(2)}, u32[]{:S(2)}) collective-permute-start(bf16[104,2496]{1,0:T(8,128)(2,1)} %collective-permute-done.3), channel_id=1, source_target_pairs={{0,4},{2,6},{4,0},{6,2},{8,12},{10,14},{12,8},{14,10},{16,20},{18,... | collective-permute-start | bytes 1557512 | tf_op jit(solution)/shard_map/ppermute | solution.py:197
  60.9 0.8 collective-permute-start.15
  61.7 1.0 %slice.35 = bf16[104,1280]{1,0:T(8,128)(2,1)S(1)} slice(bf16[104,2496]{1,0:T(8,128)(2,1)} %collective-permute-done.5), slice={[0:104], [0:1280]} | slice | bytes 532480 | tf_op jit(solution)/shard_map/slice | solution.py:200
  62.6 1.3 %pad_maximum_fusion.2 = bf16[312,2496]{1,0:T(8,128)(2,1)S(1)} fusion(bf16[104,2496]{1,0:T(8,128)(2,1)} %collective-permute-done.5, bf16[104,2496]{1,0:T(8,128)(2,1)S(1)} %collective-permute-done.4, bf16[104,2496]{1,0:T(8,128)(2,1)} %collective-permute-done.2), kind=kLoop, calls=%fused_computation.7 | loop fusion | flops 4672512 | bytes 3115008 | tf_op jit(solution)/shard_map/concatenate | solution.py:269
  64.0 1.2 %collective-permute-start.14 = (bf16[104,1280]{1,0:T(8,128)(2,1)S(1)}, bf16[104,1280]{1,0:T(8,128)(2,1)S(1)}, u32[]{:S(2)}, u32[]{:S(2)}) collective-permute-start(bf16[104,1280]{1,0:T(8,128)(2,1)S(1)} %slice.35), channel_id=1, source_target_pairs={{0,2},{2,0},{4,6},{6,4},{8,10},{10,8},{12,14},{14,12},{16,18},{18,... | collective-permute-start | bytes 798728 | tf_op jit(solution)/shard_map/ppermute | solution.py:200
  65.2 2.0 %collective-permute-start.13 = (bf16[104,2496]{1,0:T(8,128)(2,1)}, bf16[104,2496]{1,0:T(8,128)(2,1)S(1)}, u32[]{:S(2)}, u32[]{:S(2)}) collective-permute-start(bf16[104,2496]{1,0:T(8,128)(2,1)} %constant_dynamic-update-slice_fusion), channel_id=1, source_target_pairs={{0,8},{2,10},{4,12},{6,14},{8,24},{10,26},{12,28},{14,30},{16,0},{... | collective-permute-start | bytes 1557512 | tf_op jit(solution)/shard_map/ppermute | solution.py:194
  67.2 1.8 %shard_map.102 = bf16[16,104,512]{2,1,0:T(8,128)(2,1)S(1)} custom-call(s32[1]{0:T(128)} %bitcast.index_ref, s32[16]{0:T(128)S(1)} %dynamic-slice_bitcast_fusion.order_ref, bf16[16,104,1]{2,1,0:T(8,128)(2,1)S(1)} %reshape.62.gain_ref, bf16[832,512]{1,0:T(8,128)(2,1)S(1)} %bitcast.28, bf16[832,512]{1,0:T(8,128)(2,1)S(1)} %collective-permute-done.16.refs_1_, ...), custom_call_target="tpu_custom_call" | custom-call | flops 1000 | bytes 1000 | tf_op jit(solution)/shard_map/pallas_call | solution.py:169
  69.1 0.1 fusion.15
  69.2 0.0 copy-start.3
  69.2 1.6 %fusion.16 = f32[512,2496]{0,1:T(8,128)S(1)} fusion(bf16[416,512]{1,0:T(8,128)(2,1)S(1)} %bitcast.30, bf16[416,2496]{1,0:T(8,128)(2,1)S(1)} %pad_maximum_fusion), kind=kOutput, calls=%fused_computation.47 | convolution fusion | flops 1063256064 | bytes 7614464 | tf_op jit(solution)/shard_map/dot_general | solution.py:276
  70.8 1.6 %convolution_add_fusion.2 = f32[512,2496]{0,1:T(8,128)S(1)} fusion(f32[512,2496]{0,1:T(8,128)S(1)} %fusion.16, bf16[312,512]{1,0:T(8,128)(2,1)S(1)} %bitcast.33, bf16[312,2496]{1,0:T(8,128)(2,1)S(1)} %copy-done.3), kind=kOutput, calls=%fused_computation.3 | convolution fusion | flops 798720000 | bytes 12100608 | tf_op jit(solution)/shard_map/dot_general | solution.py:276
  72.4 1.6 %collective-permute-done.18 = bf16[104,2496]{1,0:T(8,128)(2,1)S(1)} collective-permute-done((bf16[104,2496]{1,0:T(8,128)(2,1)}, bf16[104,2496]{1,0:T(8,128)(2,1)S(1)}, u32[]{:S(2)}, u32[]{:S(2)}) %collective-permute-start.18) | collective-permute-done | bytes 519200 | tf_op jit(solution)/shard_map/ppermute | solution.py:197
  73.9 0.9 collective-permute-done.19
  74.8 1.4 %collective-permute-start.21 = (bf16[104,1216]{1,0:T(8,128)(2,1)S(1)}, bf16[104,1216]{1,0:T(8,128)(2,1)S(1)}, u32[]{:S(2)}, u32[]{:S(2)}) collective-permute-start(bf16[104,1216]{1,0:T(8,128)(2,1)S(1)} %slice.40), channel_id=1, source_target_pairs={{0,4},{2,6},{4,0},{6,2},{8,12},{10,14},{12,8},{14,10},{16,20},{18,... | collective-permute-start | bytes 758792 | tf_op jit(solution)/shard_map/ppermute | solution.py:201
  76.2 1.4 %collective-permute-start.20 = (bf16[104,1280]{1,0:T(8,128)(2,1)S(1)}, bf16[104,1280]{1,0:T(8,128)(2,1)S(1)}, u32[]{:S(2)}, u32[]{:S(2)}) collective-permute-start(bf16[104,1280]{1,0:T(8,128)(2,1)S(1)} %slice.39), channel_id=1, source_target_pairs={{0,2},{2,0},{4,6},{6,4},{8,10},{10,8},{12,14},{14,12},{16,18},{18,... | collective-permute-start | bytes 798728 | tf_op jit(solution)/shard_map/ppermute | solution.py:200
  77.6 1.6 %convolution_add_fusion.1 = f32[512,2496]{0,1:T(8,128)S(1)} fusion(f32[512,2496]{0,1:T(8,128)S(1)} %convolution_add_fusion.2, bf16[312,512]{1,0:T(8,128)(2,1)S(1)} %bitcast.32, bf16[312,2496]{1,0:T(8,128)(2,1)S(1)} %pad_maximum_fusion.2), kind=kOutput, calls=%fused_computation.2 | convolution fusion | flops 798720000 | bytes 12100608 | tf_op jit(solution)/shard_map/dot_general | solution.py:276
  79.2 1.2 %pad_maximum_fusion.3 = bf16[312,2496]{1,0:T(8,128)(2,1)S(1)} fusion(bf16[104,2496]{1,0:T(8,128)(2,1)S(1)} %collective-permute-done.19, bf16[104,2496]{1,0:T(8,128)(2,1)S(1)} %collective-permute-done.18, bf16[104,2496]{1,0:T(8,128)(2,1)} %collective-permute-done.3), kind=kLoop, calls=%fused_computation.8 | loop fusion | flops 4672512 | bytes 3115008 | tf_op jit(solution)/shard_map/concatenate | solution.py:269
  80.4 1.5 %convolution_add_fusion = f32[512,2496]{0,1:T(8,128)S(1)} fusion(f32[512,2496]{0,1:T(8,128)S(1)} %convolution_add_fusion.1, bf16[312,512]{1,0:T(8,128)(2,1)S(1)} %bitcast.31, bf16[312,2496]{1,0:T(8,128)(2,1)S(1)} %pad_maximum_fusion.3), kind=kOutput, calls=%fused_computation.1 | convolution fusion | flops 798720000 | bytes 12100608 | tf_op jit(solution)/shard_map/dot_general | solution.py:276
  82.0 1.7 %collective-permute-done.21 = bf16[104,1216]{1,0:T(8,128)(2,1)S(1)} collective-permute-done((bf16[104,1216]{1,0:T(8,128)(2,1)S(1)}, bf16[104,1216]{1,0:T(8,128)(2,1)S(1)}, u32[]{:S(2)}, u32[]{:S(2)}) %collective-permute-start.21) | collective-permute-done | bytes 252960 | tf_op jit(solution)/shard_map/ppermute | solution.py:201
  83.7 0.1 maximum_maximum_fusion
  83.8 3.0 %select_convert_fusion = bf16[512,2496]{0,1:T(8,128)(2,1)} fusion(f32[512,2496]{0,1:T(8,128)S(1)} %convolution_add_fusion, bf16[312,512]{1,0:T(8,128)(2,1)S(1)} %bitcast.29, bf16[312,2496]{1,0:T(8,128)(2,1)S(1)} %maximum_maximum_fusion, pred[512]{0:T(512)(128)(4,1)S(1)} %fusion.10), kind=kOutput, calls=%fused_computation | convolution fusion | flops 801275904 | bytes 9545216 | tf_op jit(solution)/shard_map/dot_general | solution.py:276
  (37 shorter events, 0.2 us)
Async XLA Ops:
  0.0 16.8 %collective-permute-start.1 = (bf16[104,2496]{1,0:T(8,128)(2,1)}, bf16[104,2496]{1,0:T(8,128)(2,1)}, u32[]{:S(2)}, u32[]{:S(2)}) collective-permute-start(bf16[104,2496]{1,0:T(8,128)(2,1)} %param.16), channel_id=1, source_target_pairs={{0,8},{2,10},{4,12},{6,14},{8,24},{10,26},{12,28},{14,30},{16,0},{... | collective-permute-start | bytes 1557512 | tf_op jit(solution)/shard_map/ppermute | solution.py:194
  3.0 1.1 %copy-start.2 = (bf16[448,832]{1,0:T(8,128)(2,1)S(1)}, bf16[448,832]{1,0:T(8,128)(2,1)}, u32[]{:S(2)}) copy-start(bf16[448,832]{1,0:T(8,128)(2,1)} %patches_ref.1) | copy-start | bytes 2236420
  4.9 4.6 %collective-permute-start = (f32[4,112,256]{2,1,0:T(8,128)S(1)}, f32[4,112,256]{2,1,0:T(8,128)S(1)}, u32[]{:S(2)}, u32[]{:S(2)}) collective-permute-start(f32[4,112,256]{2,1,0:T(8,128)S(1)} %get-tuple-element.47.refs_0_), channel_id=1, source_target_pairs={{0,1},{1,0},{2,3},{3,2},{4,5},{5,4},{6,7},{7,6},{8,9},{9,8},{10,11... | collective-permute-start | bytes 1376264 | tf_op jit(solution)/shard_map/ppermute | solution.py:26
  5.0 17.4 %collective-permute-start.7 = (bf16[104,2496]{1,0:T(8,128)(2,1)}, bf16[104,2496]{1,0:T(8,128)(2,1)}, u32[]{:S(2)}, u32[]{:S(2)}) collective-permute-start(bf16[104,2496]{1,0:T(8,128)(2,1)} %param.16), channel_id=1, source_target_pairs={{0,2},{2,0},{4,6},{6,4},{8,10},{10,8},{12,14},{14,12},{16,18},{18,... | collective-permute-start | bytes 1557512 | tf_op jit(solution)/shard_map/ppermute | solution.py:197
  6.6 15.9 %collective-permute-start.8 = (bf16[104,2496]{1,0:T(8,128)(2,1)}, bf16[104,2496]{1,0:T(8,128)(2,1)}, u32[]{:S(2)}, u32[]{:S(2)}) collective-permute-start(bf16[104,2496]{1,0:T(8,128)(2,1)} %param.16), channel_id=1, source_target_pairs={{0,4},{2,6},{4,0},{6,2},{8,12},{10,14},{12,8},{14,10},{16,20},{18,... | collective-permute-start | bytes 1557512 | tf_op jit(solution)/shard_map/ppermute | solution.py:197
  9.6 4.1 %copy-start = (bf16[4,832,1664]{2,1,0:T(8,128)(2,1)S(1)}, bf16[4,832,1664]{2,1,0:T(8,128)(2,1)}, u32[]{:S(2)}) copy-start(bf16[4,832,1664]{2,1,0:T(8,128)(2,1)} %refs_2_.1) | copy-start | bytes 33226756
  13.7 6.3 %copy-start.6 = (s32[112]{0:T(128)S(1)}, s32[112]{0:T(128)}, u32[]{:S(2)}) copy-start(s32[112]{0:T(128)} %param.17) | copy-start | bytes 1348
  13.7 8.7 %copy-start.1 = (bf16[512,832]{0,1:T(8,128)(2,1)S(1)}, bf16[512,832]{0,1:T(8,128)(2,1)}, u32[]{:S(2)}) copy-start(bf16[512,832]{0,1:T(8,128)(2,1)} %param.14) | copy-start | bytes 2555908
  16.9 16.0 %collective-permute-start.2 = (bf16[104,2496]{1,0:T(8,128)(2,1)}, bf16[104,2496]{1,0:T(8,128)(2,1)}, u32[]{:S(2)}, u32[]{:S(2)}) collective-permute-start(bf16[104,2496]{1,0:T(8,128)(2,1)} %collective-permute-done.1), channel_id=1, source_target_pairs={{0,8},{2,10},{4,12},{6,14},{8,24},{10,26},{12,28},{14,30},{16,0},{... | collective-permute-start | bytes 1557512 | tf_op jit(solution)/shard_map/ppermute | solution.py:194
  19.5 15.4 %collective-permute-start.12 = (bf16[104,2496]{1,0:T(8,128)(2,1)}, bf16[104,2496]{1,0:T(8,128)(2,1)}, u32[]{:S(2)}, u32[]{:S(2)}) collective-permute-start(bf16[104,2496]{1,0:T(8,128)(2,1)} %collective-permute-done.1), channel_id=1, source_target_pairs={{0,4},{2,6},{4,0},{6,2},{8,12},{10,14},{12,8},{14,10},{16,20},{18,... | collective-permute-start | bytes 1557512 | tf_op jit(solution)/shard_map/ppermute | solution.py:197
  20.0 1.7 %collective-permute-start.6 = (f32[112,832]{1,0:T(8,128)S(1)}, f32[112,832]{1,0:T(8,128)S(1)}, u32[]{:S(2)}, u32[]{:S(2)}) collective-permute-start(f32[112,832]{1,0:T(8,128)S(1)} %get-tuple-element.54), channel_id=1, source_target_pairs={{0,1},{1,0},{2,3},{3,2},{4,5},{5,4},{6,7},{7,6},{8,9},{9,8},{10,11... | collective-permute-start | bytes 1118216 | tf_op jit(solution)/shard_map/ppermute | solution.py:26
  21.7 15.3 %collective-permute-start.11 = (bf16[104,2496]{1,0:T(8,128)(2,1)}, bf16[104,2496]{1,0:T(8,128)(2,1)}, u32[]{:S(2)}, u32[]{:S(2)}) collective-permute-start(bf16[104,2496]{1,0:T(8,128)(2,1)} %collective-permute-done.1), channel_id=1, source_target_pairs={{0,2},{2,0},{4,6},{6,4},{8,10},{10,8},{12,14},{14,12},{16,18},{18,... | collective-permute-start | bytes 1557512 | tf_op jit(solution)/shard_map/ppermute | solution.py:197
  22.3 18.2 %copy-start.5 = (s32[2]{0:T(128)S(1)}, s32[2]{0:T(128)}, u32[]{:S(2)}) copy-start(s32[2]{0:T(128)} %param.18) | copy-start | bytes 28
  22.4 18.9 %copy-start.4 = (bf16[1664]{0:T(1024)(128)(2,1)S(1)}, bf16[1664]{0:T(1024)(128)(2,1)}, u32[]{:S(2)}) copy-start(bf16[1664]{0:T(1024)(128)(2,1)} %param.15) | copy-start | bytes 9988
  22.4 41.6 %collective-permute-start.16 = (bf16[832,512]{1,0:T(8,128)(2,1)S(1)}, bf16[832,512]{1,0:T(8,128)(2,1)S(1)}, u32[]{:S(2)}, u32[]{:S(2)}) collective-permute-start(bf16[832,512]{1,0:T(8,128)(2,1)S(1)} %bitcast.27), channel_id=1, source_target_pairs={{0,1},{1,0},{2,3},{3,2},{4,5},{5,4},{6,7},{7,6},{8,9},{9,8},{10,11... | collective-permute-start | bytes 2555912 | tf_op jit(solution)/shard_map/ppermute | solution.py:26
  24.1 21.5 %collective-permute-start.9 = (bf16[104,1280]{1,0:T(8,128)(2,1)}, bf16[104,1280]{1,0:T(8,128)(2,1)S(1)}, u32[]{:S(2)}, u32[]{:S(2)}) collective-permute-start(bf16[104,1280]{1,0:T(8,128)(2,1)} %slice.33), channel_id=1, source_target_pairs={{0,2},{2,0},{4,6},{6,4},{8,10},{10,8},{12,14},{14,12},{16,18},{18,... | collective-permute-start | bytes 798728 | tf_op jit(solution)/shard_map/ppermute | solution.py:200
  28.4 21.6 %all-to-all-start = ((bf16[16,16,896]{2,1,0:T(8,128)(2,1)}), bf16[16,16,896]{2,1,0:T(8,128)(2,1)S(1)}, u32[]{:S(2)}, u32[]{:S(2)}) async-start(bf16[16,16,896]{2,1,0:T(8,128)(2,1)} %bitcast.5), calls=%async_computation | async-start | bytes 917504 | tf_op jit(solution)/shard_map/all_to_all | solution.py:241
  32.9 15.4 %collective-permute-start.10 = (bf16[104,1216]{1,0:T(8,128)(2,1)}, bf16[104,1216]{1,0:T(8,128)(2,1)}, u32[]{:S(2)}, u32[]{:S(2)}) collective-permute-start(bf16[104,1216]{1,0:T(8,128)(2,1)} %slice.34), channel_id=1, source_target_pairs={{0,4},{2,6},{4,0},{6,2},{8,12},{10,14},{12,8},{14,10},{16,20},{18,... | collective-permute-start | bytes 758792 | tf_op jit(solution)/shard_map/ppermute | solution.py:201
  34.9 22.9 %collective-permute-start.3 = (bf16[104,2496]{1,0:T(8,128)(2,1)}, bf16[104,2496]{1,0:T(8,128)(2,1)}, u32[]{:S(2)}, u32[]{:S(2)}) collective-permute-start(bf16[104,2496]{1,0:T(8,128)(2,1)} %collective-permute-done.2), channel_id=1, source_target_pairs={{0,8},{2,10},{4,12},{6,14},{8,24},{10,26},{12,28},{14,30},{16,0},{... | collective-permute-start | bytes 1557512 | tf_op jit(solution)/shard_map/ppermute | solution.py:194
  37.0 21.1 %collective-permute-start.4 = (bf16[104,2496]{1,0:T(8,128)(2,1)}, bf16[104,2496]{1,0:T(8,128)(2,1)S(1)}, u32[]{:S(2)}, u32[]{:S(2)}) collective-permute-start(bf16[104,2496]{1,0:T(8,128)(2,1)} %collective-permute-done.2), channel_id=1, source_target_pairs={{0,2},{2,0},{4,6},{6,4},{8,10},{10,8},{12,14},{14,12},{16,18},{18,... | collective-permute-start | bytes 1557512 | tf_op jit(solution)/shard_map/ppermute | solution.py:197
  45.7 13.0 %collective-permute-start.5 = (bf16[104,2496]{1,0:T(8,128)(2,1)}, bf16[104,2496]{1,0:T(8,128)(2,1)}, u32[]{:S(2)}, u32[]{:S(2)}) collective-permute-start(bf16[104,2496]{1,0:T(8,128)(2,1)} %collective-permute-done.2), channel_id=1, source_target_pairs={{0,4},{2,6},{4,0},{6,2},{8,12},{10,14},{12,8},{14,10},{16,20},{18,... | collective-permute-start | bytes 1557512 | tf_op jit(solution)/shard_map/ppermute | solution.py:197
  50.0 15.2 %collective-permute-start.17 = (bf16[256,896]{1,0:T(8,128)(2,1)S(1)}, bf16[256,896]{1,0:T(8,128)(2,1)S(1)}, u32[]{:S(2)}, u32[]{:S(2)}) collective-permute-start(bf16[256,896]{1,0:T(8,128)(2,1)S(1)} %bitcast.25), channel_id=1, source_target_pairs={{0,1},{1,0},{2,3},{3,2},{4,5},{5,4},{6,7},{7,6},{8,9},{9,8},{10,11... | collective-permute-start | bytes 1376264 | tf_op jit(solution)/shard_map/ppermute | solution.py:26
  58.7 15.2 %collective-permute-start.18 = (bf16[104,2496]{1,0:T(8,128)(2,1)}, bf16[104,2496]{1,0:T(8,128)(2,1)S(1)}, u32[]{:S(2)}, u32[]{:S(2)}) collective-permute-start(bf16[104,2496]{1,0:T(8,128)(2,1)} %collective-permute-done.3), channel_id=1, source_target_pairs={{0,2},{2,0},{4,6},{6,4},{8,10},{10,8},{12,14},{14,12},{16,18},{18,... | collective-permute-start | bytes 1557512 | tf_op jit(solution)/shard_map/ppermute | solution.py:197
  59.5 15.2 %collective-permute-start.19 = (bf16[104,2496]{1,0:T(8,128)(2,1)}, bf16[104,2496]{1,0:T(8,128)(2,1)S(1)}, u32[]{:S(2)}, u32[]{:S(2)}) collective-permute-start(bf16[104,2496]{1,0:T(8,128)(2,1)} %collective-permute-done.3), channel_id=1, source_target_pairs={{0,4},{2,6},{4,0},{6,2},{8,12},{10,14},{12,8},{14,10},{16,20},{18,... | collective-permute-start | bytes 1557512 | tf_op jit(solution)/shard_map/ppermute | solution.py:197
  60.9 21.1 %collective-permute-start.15 = (bf16[104,1216]{1,0:T(8,128)(2,1)S(1)}, bf16[104,1216]{1,0:T(8,128)(2,1)S(1)}, u32[]{:S(2)}, u32[]{:S(2)}) collective-permute-start(bf16[104,1216]{1,0:T(8,128)(2,1)S(1)} %slice.36), channel_id=1, source_target_pairs={{0,4},{2,6},{4,0},{6,2},{8,12},{10,14},{12,8},{14,10},{16,20},{18,... | collective-permute-start | bytes 758792 | tf_op jit(solution)/shard_map/ppermute | solution.py:201
  64.0 18.0 %collective-permute-start.14 = (bf16[104,1280]{1,0:T(8,128)(2,1)S(1)}, bf16[104,1280]{1,0:T(8,128)(2,1)S(1)}, u32[]{:S(2)}, u32[]{:S(2)}) collective-permute-start(bf16[104,1280]{1,0:T(8,128)(2,1)S(1)} %slice.35), channel_id=1, source_target_pairs={{0,2},{2,0},{4,6},{6,4},{8,10},{10,8},{12,14},{14,12},{16,18},{18,... | collective-permute-start | bytes 798728 | tf_op jit(solution)/shard_map/ppermute | solution.py:200
  65.2 16.7 %collective-permute-start.13 = (bf16[104,2496]{1,0:T(8,128)(2,1)}, bf16[104,2496]{1,0:T(8,128)(2,1)S(1)}, u32[]{:S(2)}, u32[]{:S(2)}) collective-permute-start(bf16[104,2496]{1,0:T(8,128)(2,1)} %constant_dynamic-update-slice_fusion), channel_id=1, source_target_pairs={{0,8},{2,10},{4,12},{6,14},{8,24},{10,26},{12,28},{14,30},{16,0},{... | collective-permute-start | bytes 1557512 | tf_op jit(solution)/shard_map/ppermute | solution.py:194
  69.2 1.6 %copy-start.3 = (bf16[312,2496]{1,0:T(8,128)(2,1)S(1)}, bf16[312,2496]{1,0:T(8,128)(2,1)}, u32[]{:S(2)}) copy-start(bf16[312,2496]{1,0:T(8,128)(2,1)} %pad_maximum_fusion.1) | copy-start | bytes 4672516
  74.8 8.8 %collective-permute-start.21 = (bf16[104,1216]{1,0:T(8,128)(2,1)S(1)}, bf16[104,1216]{1,0:T(8,128)(2,1)S(1)}, u32[]{:S(2)}, u32[]{:S(2)}) collective-permute-start(bf16[104,1216]{1,0:T(8,128)(2,1)S(1)} %slice.40), channel_id=1, source_target_pairs={{0,4},{2,6},{4,0},{6,2},{8,12},{10,14},{12,8},{14,10},{16,20},{18,... | collective-permute-start | bytes 758792 | tf_op jit(solution)/shard_map/ppermute | solution.py:201
  76.2 7.5 %collective-permute-start.20 = (bf16[104,1280]{1,0:T(8,128)(2,1)S(1)}, bf16[104,1280]{1,0:T(8,128)(2,1)S(1)}, u32[]{:S(2)}, u32[]{:S(2)}) collective-permute-start(bf16[104,1280]{1,0:T(8,128)(2,1)S(1)} %slice.39), channel_id=1, source_target_pairs={{0,2},{2,0},{4,6},{6,4},{8,10},{10,8},{12,14},{14,12},{16,18},{18,... | collective-permute-start | bytes 798728 | tf_op jit(solution)/shard_map/ppermute | solution.py:200
